TPU v7x, 32 devices: a whole 2x2x4 slice. The times are simulated.
32 devices in a mesh: groups: 2 (over x), blk: 16 (over z, y, core).
Axes of the slice: x: 2, y: 2, z: 4, core: 2. Of those that a mesh axis runs over, the one named last changes fastest.
Arguments:
- moe_input: bfloat16 [4096, 2048], P(('groups', 'blk')), parts along dimension 0, may hold values from -6 to 6
- moe_grad: bfloat16 [4096, 2048], P(('groups', 'blk')), parts along dimension 0, may hold values from -6 to 6
- routes: int32 [4096, 2], P(('groups', 'blk')), parts along dimension 0, may hold values from 0 to 7, all different within a row; in each aligned block of 128 rows (0 to 127, 128 to 255, ...) at most 48 rows name the same one
- route_weight: float32 [4096, 2], P(('groups', 'blk')), parts along dimension 0, may hold values from 0.1 to 1
- w_gate: bfloat16 [2048, 6144], P(None, 'blk'), may hold values from -0.125 to 0.125
- w_up: bfloat16 [2048, 6144], P(None, 'blk'), may hold values from -0.125 to 0.125
- w_down: bfloat16 [6144, 2048], P('blk'), may hold values from -0.21875 to 0.21875
- w_out: bfloat16 [2048, 4096], P('blk'), may hold values from -0.125 to 0.125
- queries: bfloat16 [4096, 4096], P(('groups', 'blk')), parts along dimension 0, may hold values from -200 to 200
- key_heads: bfloat16 [4096, 256], P(('groups', 'blk')), parts along dimension 0, may hold values from -6 to 6
- value_heads: bfloat16 [4096, 256], P(('groups', 'blk')), parts along dimension 0, may hold values from -6 to 6
- segments: int32 [4096], P(('groups', 'blk')), parts along dimension 0, may hold values from 0 to 15, never falling along the last dimension, each value on 1 to 384 neighbouring positions
Outputs:
- moe_input_grad: bfloat16 [4096, 2048], P(('groups', 'blk')), parts along dimension 0
- query_grad: bfloat16 [4096, 4096], P(('groups', 'blk')), parts along dimension 0
- key_grad: float32 [4096, 256], P(('groups', 'blk')), parts along dimension 0
- value_grad: float32 [4096, 256], P(('groups', 'blk')), parts along dimension 0
There are 2 independent parts, one for each index of `groups`. A program takes and returns all parts, laid end to end along the dimension named above; an argument that names none is the same for every part. Nothing has to cross between parts.
Inputs may be any that keep to these rules, and one draw needn't show every extreme that they name: `routes`: each row names 2 different experts; within each aligned block of 128 rows (the tokens of one device) no expert is named more than 48 times, a bound that some block reaches.
All inputs are finite; a program needn't handle non-finite values.
Results may differ from a plain program's by a relative error of at most 0.014.
Values may be sent and summed in bfloat16 or wider, within the bound.
No kernel may reach another device: no remote copies, remote signals or barrier semaphores. Data moves between devices by JAX's collectives and lax.ppermute only.
A program may use at most 128 MiB of HBM per device.

v0:
```python
import jax
import jax.numpy as jnp
from jax import lax
from jax.sharding import PartitionSpec as P

H = 32
KVH = 2
HD = 128
GROUP = 16


floor_score = -1e30


def from_behind(array, axis, by):
    count = lax.axis_size(axis)
    pairs = [(i, i + by) for i in range(count) if 0 <= i + by < count]
    return lax.ppermute(array, axis, pairs)


def expert_terms(rows_in, grads_in, gate_cols, up_cols, down_rows):
    half_units = gate_cols.shape[1]
    both_cols = jnp.concatenate([gate_cols, up_cols], axis=1)
    both_pre = jnp.dot(rows_in, both_cols, preferred_element_type=jnp.float32)
    gate_pre = both_pre[:, :half_units]
    up_pre = both_pre[:, half_units:]
    down_grad = lax.dot_general(
        grads_in, down_rows, (((1,), (1,)), ((), ())), preferred_element_type=jnp.float32
    )
    sigmoid_gate = jax.nn.sigmoid(gate_pre)
    gate_grad = (
        down_grad * up_pre * sigmoid_gate * (1.0 + gate_pre * (1.0 - sigmoid_gate))
    ).astype(jnp.bfloat16)
    up_grad = (down_grad * gate_pre * sigmoid_gate).astype(jnp.bfloat16)
    both_grad = jnp.concatenate([gate_grad, up_grad], axis=1)
    return lax.dot_general(
        both_grad, both_cols, (((1,), (1,)), ((), ())), preferred_element_type=jnp.float32
    )


def attend(q_rows, grad_rows, key_all, value_all, visible):
    row_count = q_rows.shape[0]
    span_count = key_all.shape[0]
    score_scale = HD ** (-0.5)
    query_split = q_rows.reshape(row_count, KVH, GROUP, HD)
    grad_split = grad_rows.reshape(row_count, KVH, GROUP, HD)
    grad_wide = grad_rows.astype(jnp.float32).reshape(row_count, KVH, GROUP, HD)
    key_split = key_all.reshape(span_count, KVH, HD)
    value_split = value_all.reshape(span_count, KVH, HD)
    scores = (
        jnp.einsum("tgih,sgh->gits", query_split, key_split, preferred_element_type=jnp.float32)
        * score_scale
    )
    masked = jnp.where(visible[None, None], scores, floor_score)
    row_peak = jnp.max(masked, axis=-1, keepdims=True)
    raised = jnp.where(visible[None, None], jnp.exp(masked - row_peak), 0.0)
    shares = raised / jnp.sum(raised, axis=-1, keepdims=True)
    shares_low = shares.astype(jnp.bfloat16)
    attn_out = jnp.einsum(
        "gits,sgh->tgih", shares_low, value_split, preferred_element_type=jnp.float32
    )
    row_dot = jnp.transpose(jnp.sum(attn_out * grad_wide, axis=-1), (1, 2, 0))
    prob_grad = jnp.einsum(
        "tgih,sgh->gits", grad_split, value_split, preferred_element_type=jnp.float32
    )
    score_grad = (shares * (prob_grad - row_dot[..., None]) * score_scale).astype(jnp.bfloat16)
    query_part = jnp.einsum(
        "gits,sgh->tgih", score_grad, key_split, preferred_element_type=jnp.float32
    )
    query_part = query_part.reshape(row_count, H * HD).astype(jnp.bfloat16)
    key_part = jnp.einsum(
        "gits,tgih->sgh", score_grad, query_split, preferred_element_type=jnp.float32
    ).reshape(span_count, KVH * HD)
    value_part = jnp.einsum(
        "gits,tgih->sgh", shares_low, grad_split, preferred_element_type=jnp.float32
    ).reshape(span_count, KVH * HD)
    return (query_part, key_part, value_part)


def local(
    moe_input,
    moe_grad,
    routes,
    route_weight,
    w_gate,
    w_up,
    w_down,
    w_out,
    queries,
    key_heads,
    value_heads,
    segments,
):
    axis_count = lax.axis_size("blk")
    tok_rows = moe_input.shape[0]
    fanout = routes.shape[1]
    model_width = moe_input.shape[1]
    owners = axis_count // 2
    slot_depth = 2 * max(1, 3 * tok_rows * fanout // (2 * axis_count))
    flat_expert = routes.reshape(-1)
    row_total = flat_expert.shape[0]
    expert_hits = (flat_expert[:, None] == jnp.arange(owners, dtype=jnp.int32)[None, :]).astype(
        jnp.int32
    )
    placed = jnp.sum((jnp.cumsum(expert_hits, axis=0) - 1) * expert_hits, axis=1)
    slot_index = flat_expert * slot_depth + placed
    matches = slot_index[None, :] == jnp.arange(owners * slot_depth, dtype=jnp.int32)[:, None]
    source = (
        jnp.sum(jnp.where(matches, jnp.arange(row_total, dtype=jnp.int32)[None, :] + 1, 0), axis=1)
        - 1
    )
    filled = source >= 0
    safe_row = jnp.maximum(source, 0)
    token_of = safe_row // fanout
    picked_in = jnp.take(moe_input, token_of, axis=0)
    inputs_out = jnp.where(filled[:, None], picked_in, jnp.zeros_like(picked_in))
    weight_of = jnp.take(route_weight.reshape(-1), safe_row)
    scaled = (weight_of[:, None] * jnp.take(moe_grad, token_of, axis=0).astype(jnp.float32)).astype(
        jnp.bfloat16
    )
    scaled = jnp.where(filled[:, None], scaled, jnp.zeros_like(scaled))
    inputs_grid = inputs_out.reshape(owners, slot_depth, model_width)
    scaled_grid = scaled.reshape(owners, slot_depth, model_width)
    doubled_in = jnp.repeat(inputs_grid, 2, axis=0)
    doubled_grad = jnp.repeat(scaled_grid, 2, axis=0)
    rows_in = lax.all_to_all(doubled_in, "blk", split_axis=0, concat_axis=0, tiled=True)
    grads_in = lax.all_to_all(doubled_grad, "blk", split_axis=0, concat_axis=0, tiled=True)
    partial_value = expert_terms(
        rows_in.reshape(-1, model_width), grads_in.reshape(-1, model_width), w_gate, w_up, w_down
    )
    returned = lax.all_to_all(
        partial_value.reshape(rows_in.shape).astype(jnp.bfloat16),
        "blk",
        split_axis=0,
        concat_axis=0,
        tiled=True,
    ).astype(jnp.float32)
    combined = jnp.sum(returned.reshape(owners, 2, slot_depth, model_width), axis=1)
    per_route = jnp.take(combined.reshape(owners * slot_depth, model_width), slot_index, axis=0)
    moe_input_grad = jnp.sum(per_route.reshape(tok_rows, fanout, model_width), axis=1).astype(
        jnp.bfloat16
    )
    stream_grad = (moe_grad.astype(jnp.float32) + moe_input_grad.astype(jnp.float32)).astype(
        jnp.bfloat16
    )
    head_grad = jnp.dot(
        stream_grad,
        lax.all_gather(w_out, "blk", axis=0, tiled=True),
        preferred_element_type=jnp.float32,
    ).astype(jnp.bfloat16)
    prev_key, prev_value, prev_segment = from_behind((key_heads, value_heads, segments), "blk", 1)
    position = jnp.arange(tok_rows)
    own_visible = (position[None, :] <= position[:, None]) & (
        segments[None, :] == segments[:, None]
    )
    prev_visible = (prev_segment[None, :] == segments[:, None]) & (lax.axis_index("blk") >= 1)
    visible = jnp.concatenate([prev_visible, own_visible], axis=1)
    key_all = jnp.concatenate([prev_key, key_heads], axis=0)
    value_all = jnp.concatenate([prev_value, value_heads], axis=0)
    query_grad, key_part, value_part = attend(queries, head_grad, key_all, value_all, visible)
    later_key, later_value = (
        from_behind(key_part[:tok_rows].astype(jnp.bfloat16), "blk", -1).astype(jnp.float32),
        from_behind(value_part[:tok_rows].astype(jnp.bfloat16), "blk", -1).astype(jnp.float32),
    )
    key_grad = key_part[tok_rows:] + later_key
    value_grad = value_part[tok_rows:] + later_value
    return (moe_input_grad, query_grad, key_grad, value_grad)


def solution(mesh):
    return jax.shard_map(
        local,
        mesh=mesh,
        in_specs=(
            P(("groups", "blk"), None),
            P(("groups", "blk"), None),
            P(("groups", "blk"), None),
            P(("groups", "blk"), None),
            P(None, "blk"),
            P(None, "blk"),
            P("blk", None),
            P("blk", None),
            P(("groups", "blk"), None),
            P(("groups", "blk"), None),
            P(("groups", "blk"), None),
            P(("groups", "blk")),
        ),
        out_specs=(
            P(("groups", "blk"), None),
            P(("groups", "blk"), None),
            P(("groups", "blk"), None),
            P(("groups", "blk"), None),
        ),
        check_vma=False,
    )
```

profile of v0, /device:TPU:13, one launch (start us, length us, event | category | flops | bytes accessed | tf_op | source)
XLA Modules:
  0.0 414.4 jit_solution(6300679727363325759)
XLA Ops:
  11.1 3.1 gather_fusion.2
  14.2 3.1 gather_fusion.3
  17.4 2.8 gather_fusion
  20.2 2.7 select_select_fusion
  23.3 150.8 %all_to_all.15 = bf16[16,48,2048]{2,1,0:T(8,128)(2,1)} all-to-all(bf16[16,48,2048]{2,1,0:T(8,128)(2,1)S(1)} %bitcast.102), channel_id=1, replica_groups=mesh['groups'=2,'blk'=16] {'blk'}, dimensions={0} | all-to-all | bytes 6291456 | tf_op jit(solution)/shard_map/all_to_all | solution.py:126
  176.2 4.4 %all-to-all-start = ((bf16[16,48,2048]{2,1,0:T(8,128)(2,1)}), bf16[16,48,2048]{2,1,0:T(8,128)(2,1)}, u32[]{:S(2)}, u32[]{:S(2)}) async-start(bf16[16,48,2048]{2,1,0:T(8,128)(2,1)} %bitcast.101), calls=%async_computation | async-start | bytes 6291456 | tf_op jit(solution)/shard_map/all_to_all | solution.py:127
  185.8 4.2 %fusion.28 = f32[768,768]{0,1:T(8,128)} fusion(bf16[768,2048]{1,0:T(8,128)(2,1)S(1)} %bitcast.111, bf16[2048,768]{1,0:T(8,128)(2,1)S(1)} %constant_dynamic-update-slice_fusion), kind=kOutput, calls=%fused_computation.83 | convolution fusion | flops 2415919104 | bytes 8650752 | tf_op jit(solution)/shard_map/dot_general | solution.py:24
  190.0 71.8 %all-to-all-done = bf16[16,48,2048]{2,1,0:T(8,128)(2,1)} async-done(((bf16[16,48,2048]{2,1,0:T(8,128)(2,1)}), bf16[16,48,2048]{2,1,0:T(8,128)(2,1)}, u32[]{:S(2)}, u32[]{:S(2)}) %all-to-all-start) | async-done | bytes 3145760 | tf_op jit(solution)/shard_map/all_to_all | solution.py:127
  261.8 4.4 %fusion.14 = (bf16[768,384]{0,1:T(8,128)(2,1)S(1)}, bf16[768,384]{0,1:T(8,128)(2,1)S(1)}) fusion(f32[768,768]{0,1:T(8,128)} %fusion.28, bf16[768,2048]{1,0:T(8,128)(2,1)} %bitcast.4, bf16[384,2048]{1,0:T(8,128)(2,1)S(1)} %copy-done), kind=kOutput, calls=%fused_computation.31 | convolution fusion | flops 1211793408 | bytes 8257536 | tf_op jit(solution)/shard_map/dot_general | solution.py:27
  266.2 4.1 %convolution_convert_fusion.1 = bf16[768,2048]{1,0:T(8,128)(2,1)} fusion(bf16[2048,768]{1,0:T(8,128)(2,1)S(1)} %copy-done.13, bf16[768,384]{0,1:T(8,128)(2,1)S(1)} %get-tuple-element.24, bf16[768,384]{0,1:T(8,128)(2,1)S(1)} %get-tuple-element.23), kind=kOutput, calls=%fused_computation.13 | convolution fusion | flops 2419851264 | bytes 7471104 | tf_op jit(solution)/shard_map/dot_general | solution.py:36
  270.4 4.5 %all-to-all-start.2 = ((bf16[16,48,2048]{2,1,0:T(8,128)(2,1)}), bf16[16,48,2048]{2,1,0:T(8,128)(2,1)}, u32[]{:S(2)}, u32[]{:S(2)}) async-start(bf16[16,48,2048]{2,1,0:T(8,128)(2,1)} %bitcast.110), calls=%async_computation.2 | async-start | bytes 6291456 | tf_op jit(solution)/shard_map/all_to_all | solution.py:131
  275.0 3.2 collective-permute-start
  280.4 3.5 collective-permute-start.2
  285.3 58.3 %collective-permute-done.1 = s32[128]{0:T(128)S(1)} collective-permute-done((s32[128]{0:T(128)S(1)}, s32[128]{0:T(128)S(1)}, u32[]{:S(2)}, u32[]{:S(2)}) %collective-permute-start.1) | collective-permute-done | bytes 544 | tf_op jit(solution)/shard_map/ppermute | solution.py:18
  343.8 3.6 fusion.27
  347.4 4.0 fusion.9
  351.5 4.6 %copy.101 = bf16[2,16,128,256]{3,1,0,2:T(8,128)(2,1)} copy(bf16[2,16,128,256]{2,3,1,0:T(8,128)(2,1)} %fusion.9) | data formatting | bytes 4194304 | tf_op jit(solution)/shard_map/convert_element_type | solution.py:58
  356.8 4.6 %convert_reduce_fusion = f32[8,48,2048]{2,1,0:T(8,128)} fusion(bf16[16,48,2048]{2,1,0:T(8,128)(2,1)} %all-to-all-done.2), kind=kLoop, calls=%fused_computation.5 | loop fusion | flops 2359296 | bytes 6291456 | tf_op jit(solution)/shard_map/reduce_sum | solution.py:138
  361.4 5.5 %gather_fusion.1 = f32[256,2048]{1,0:T(8,128)} fusion(f32[384,2048]{1,0:T(8,128)} %bitcast.100, s32[1024]{0:T(1024)S(1)} %pad_clamp_fusion), kind=kCustom, calls=%fused_computation.3 | custom fusion | bytes 4195328 | tf_op jit(solution)/shard_map/jit(_take)/gather | solution.py:139
  366.9 3.5 gather.15
  370.4 4.9 %select_reduce_fusion = bf16[128,2048]{1,0:T(8,128)(2,1)S(1)} fusion(f32[128,2,2048]{2,1,0:T(2,128)} %gather.15, pred[128,2]{1,0:T(8,128)(4,1)S(1)} %copy.83), kind=kLoop, calls=%fused_computation.21 | loop fusion | flops 786432 | bytes 2621696 | tf_op jit(solution)/shard_map/reduce_sum | solution.py:140
  375.3 8.3 %fusion.11 = bf16[16,8,32,128]{3,1,2,0:T(8,128)(2,1)S(1)} fusion(bf16[2048,4096]{1,0:T(8,128)(2,1)} %all-gather.2.cloned.1.call-done, bf16[128,2048]{1,0:T(8,128)(2,1)S(1)} %select_reduce_fusion, bf16[128,2048]{1,0:T(8,128)(2,1)S(1)} %copy-done.2), kind=kOutput, calls=%fused_computation.27 | convolution fusion | flops 2149056512 | bytes 18874368 | tf_op jit(solution)/shard_map/dot_general | solution.py:146
  394.0 3.2 fusion.3
  404.4 2.5 collective-permute-done.3
  (103 shorter events, 34.0 us)
Async XLA Ops:
  7.2 254.6 %copy-start = (bf16[384,2048]{1,0:T(8,128)(2,1)S(1)}, bf16[384,2048]{1,0:T(8,128)(2,1)}, u32[]{:S(2)}) copy-start(bf16[384,2048]{1,0:T(8,128)(2,1)} %param.20) | copy-start | bytes 4718596
  7.2 3.9 copy-start.2
  7.2 368.1 %all-gather.2.cloned.1.call-start = ((), (), s32[]{:S(2)}) async-start(), calls=%async_computation.3 | async-start | bytes 17825792 | tf_op jit(solution)/shard_map/all_gather | solution.py:148
  11.1 3.1 copy-start.3
  176.2 85.6 %all-to-all-start = ((bf16[16,48,2048]{2,1,0:T(8,128)(2,1)}), bf16[16,48,2048]{2,1,0:T(8,128)(2,1)}, u32[]{:S(2)}, u32[]{:S(2)}) async-start(bf16[16,48,2048]{2,1,0:T(8,128)(2,1)} %bitcast.101), calls=%async_computation | async-start | bytes 6291456 | tf_op jit(solution)/shard_map/all_to_all | solution.py:127
  182.8 3.0 copy-start.8
  261.8 4.4 %copy-start.13 = (bf16[2048,768]{1,0:T(8,128)(2,1)S(1)}, bf16[2048,768]{1,0:T(8,128)(2,1)}, u32[]{:S(2)}) copy-start(bf16[2048,768]{1,0:T(8,128)(2,1)} %copy-done.12) | copy-start | bytes 9437188
  270.4 4.6 %copy-start.15 = (bf16[128,256]{1,0:T(8,128)(2,1)S(1)}, bf16[128,256]{1,0:T(8,128)(2,1)}, u32[]{:S(2)}) copy-start(bf16[128,256]{1,0:T(8,128)(2,1)} %param.23) | copy-start | bytes 196612
  270.4 7.9 %copy-start.18 = (s32[128]{0:T(128)S(1)}, s32[128]{0:T(128)}, u32[]{:S(2)}) copy-start(s32[128]{0:T(128)} %param.25) | copy-start | bytes 1540
  270.4 10.0 %copy-start.16 = (bf16[128,256]{1,0:T(8,128)(2,1)S(1)}, bf16[128,256]{1,0:T(8,128)(2,1)}, u32[]{:S(2)}) copy-start(bf16[128,256]{1,0:T(8,128)(2,1)} %param.24) | copy-start | bytes 196612
  270.4 13.8 %copy-start.17 = (s32[128,2]{0,1:T(2,128)S(1)}, s32[128,2]{0,1:T(2,128)}, u32[]{:S(2)}) copy-start(s32[128,2]{0,1:T(2,128)} %param.16) | copy-start | bytes 3076
  270.4 14.3 %copy-start.11 = (bf16[128,4096]{1,0:T(8,128)(2,1)S(1)}, bf16[128,4096]{1,0:T(8,128)(2,1)}, u32[]{:S(2)}) copy-start(bf16[128,4096]{1,0:T(8,128)(2,1)} %param.22) | copy-start | bytes 3145732
  270.4 86.4 %all-to-all-start.2 = ((bf16[16,48,2048]{2,1,0:T(8,128)(2,1)}), bf16[16,48,2048]{2,1,0:T(8,128)(2,1)}, u32[]{:S(2)}, u32[]{:S(2)}) async-start(bf16[16,48,2048]{2,1,0:T(8,128)(2,1)} %bitcast.110), calls=%async_computation.2 | async-start | bytes 6291456 | tf_op jit(solution)/shard_map/all_to_all | solution.py:131
  275.0 68.8 %collective-permute-start = (bf16[128,256]{0,1:T(8,128)(2,1)S(1)}, bf16[128,256]{0,1:T(8,128)(2,1)S(1)}, u32[]{:S(2)}, u32[]{:S(2)}) collective-permute-start(bf16[128,256]{0,1:T(8,128)(2,1)S(1)} %copy.86), channel_id=1, source_target_pairs={{0,1},{1,2},{2,3},{3,4},{4,5},{5,6},{6,7},{7,8},{8,9},{9,10},{10,1... | collective-permute-start | bytes 196616 | tf_op jit(solution)/shard_map/ppermute | solution.py:18
  278.3 65.4 %collective-permute-start.1 = (s32[128]{0:T(128)S(1)}, s32[128]{0:T(128)S(1)}, u32[]{:S(2)}, u32[]{:S(2)}) collective-permute-start(s32[128]{0:T(128)S(1)} %copy-done.18), channel_id=1, source_target_pairs={{0,1},{1,2},{2,3},{3,4},{4,5},{5,6},{6,7},{7,8},{8,9},{9,10},{10,1... | collective-permute-start | bytes 1544 | tf_op jit(solution)/shard_map/ppermute | solution.py:18
  280.4 75.6 %collective-permute-start.2 = (bf16[128,256]{0,1:T(8,128)(2,1)S(1)}, bf16[128,256]{0,1:T(8,128)(2,1)S(1)}, u32[]{:S(2)}, u32[]{:S(2)}) collective-permute-start(bf16[128,256]{0,1:T(8,128)(2,1)S(1)} %copy.90), channel_id=1, source_target_pairs={{0,1},{1,2},{2,3},{3,4},{4,5},{5,6},{6,7},{7,8},{8,9},{9,10},{10,1... | collective-permute-start | bytes 196616 | tf_op jit(solution)/shard_map/ppermute | solution.py:18
  285.3 62.1 %copy-start.6 = (bf16[128,4096]{0,1:T(8,128)(2,1)}, bf16[128,4096]{0,1:T(8,128)(2,1)S(1)}, u32[]{:S(2)}) copy-start(bf16[128,4096]{0,1:T(8,128)(2,1)S(1)} %copy.117) | copy-start | bytes 3145732
  375.3 8.4 %copy-start.9 = (bf16[128,2048]{1,0:T(8,128)(2,1)}, bf16[128,2048]{1,0:T(8,128)(2,1)S(1)}, u32[]{:S(2)}) copy-start(bf16[128,2048]{1,0:T(8,128)(2,1)S(1)} %select_reduce_fusion) | copy-start | bytes 1572868
  385.6 6.6 %copy-start.4 = (bf16[2,16,128,256]{2,3,1,0:T(8,128)(2,1)S(1)}, bf16[2,16,128,256]{2,3,1,0:T(8,128)(2,1)}, u32[]{:S(2)}) copy-start(bf16[2,16,128,256]{2,3,1,0:T(8,128)(2,1)} %fusion.9) | copy-start | bytes 6291460
  387.9 6.1 %copy-start.5 = (bf16[128,2,16,128]{0,3,2,1:T(8,128)(2,1)S(1)}, bf16[128,2,16,128]{0,3,2,1:T(8,128)(2,1)}, u32[]{:S(2)}) copy-start(bf16[128,2,16,128]{0,3,2,1:T(8,128)(2,1)} %copy.95) | copy-start | bytes 3145732
  390.1 3.9 copy-start.14
  390.1 12.7 %collective-permute-start.4 = (bf16[128,256]{1,0:T(8,128)(2,1)}, bf16[128,256]{1,0:T(8,128)(2,1)}, u32[]{:S(2)}, u32[]{:S(2)}) collective-permute-start(bf16[128,256]{1,0:T(8,128)(2,1)} %copy.102), channel_id=1, source_target_pairs={{1,0},{2,1},{3,2},{4,3},{5,4},{6,5},{7,6},{8,7},{9,8},{10,9},{11,1... | collective-permute-start | bytes 196616 | tf_op jit(solution)/shard_map/ppermute | solution.py:18
  398.4 9.1 %copy-start.1 = (bf16[384,2048]{1,0:T(8,128)(2,1)S(1)}, bf16[384,2048]{1,0:T(8,128)(2,1)}, u32[]{:S(2)}) copy-start(bf16[384,2048]{1,0:T(8,128)(2,1)} %param.20) | copy-start | bytes 4718596
  399.6 7.3 %collective-permute-start.3 = (bf16[128,256]{1,0:T(8,128)(2,1)S(1)}, bf16[128,256]{1,0:T(8,128)(2,1)S(1)}, u32[]{:S(2)}, u32[]{:S(2)}) collective-permute-start(bf16[128,256]{1,0:T(8,128)(2,1)S(1)} %copy.99), channel_id=1, source_target_pairs={{1,0},{2,1},{3,2},{4,3},{5,4},{6,5},{7,6},{8,7},{9,8},{10,9},{11,1... | collective-permute-start | bytes 196616 | tf_op jit(solution)/shard_map/ppermute | solution.py:18
  (3 other events, 5.0 us)
Sparse Core Ops, SparseCore 0:
  10.2 203.7 all-gather.1
where the time goes:
time: 416 us; the launch traced here: 414 us
  blocking collectives  151 us (36%)
  waiting for transfers between devices  133 us (32%)
  local copies, waits for them, and re-layouts  40.6 us (10%)
  matrix products  33.2 us (8%)
  starting transfers between devices  21.7 us (5%)
  other arithmetic  20.2 us (5%)
  between operations  14.6 us (4%)
    all_to_all x1, blocking collectives, local(): lax.all_to_all(doubled_in, 'blk', split_axis=0, concat_axis=0, tiled=True)  151 us
    all_to_all x1, waiting for transfers between devices, local(): lax.all_to_all(doubled_grad, 'blk', split_axis=0, concat_axis=0, tiled=True)  71.8 us
    ppermute x5, waiting for transfers between devices, from_behind(): return lax.ppermute(array, axis, pairs)  60.8 us
    ppermute x5, starting transfers between devices, from_behind(): return lax.ppermute(array, axis, pairs)  12.7 us
    unnamed x45, local copies, waits for them, and re-layouts  9.01 us
    gather x2, local copies, waits for them, and re-layouts, local(): jnp.take(combined.reshape(owners * slot_depth, model_width), slot_index,...  8.97 us
  transfers between devices with their start and end apart: 8, of which 3 were waited for; matrix products, arithmetic and copies ran while one was open for 18% of the time, Pallas kernels for 0%

commit v1 on v0

v1 whole, which is shorter than its diff:
```python
import functools

import jax
import jax.numpy as jnp
from jax import lax
from jax.experimental import pallas as pl
from jax.experimental.pallas import tpu as pltpu
from jax.sharding import PartitionSpec as P

KVH = 2
GROUP = 16
HD = 128
FLOOR = -1e30
MIB = 1 << 20

NT = (((1,), (1,)), ((), ()))
TN = (((0,), (0,)), ((), ()))


def dot(a, b, dims=(((1,), (0,)), ((), ()))):
    return lax.dot_general(a, b, dims, preferred_element_type=jnp.float32)


def params(mib):
    return pltpu.CompilerParams(vmem_limit_bytes=mib * MIB)


def pick_kernel(owners, depth, routes_ref, weight_ref, input_ref, grad_ref, rows_ref, place_ref):
    tokens = input_ref.shape[0]
    slots = owners * depth
    first = routes_ref[0:1, :]
    second = routes_ref[1:2, :]
    expert = lax.broadcasted_iota(jnp.int32, (owners, tokens), 0)
    is_first = first == expert
    is_second = second == expert
    member = jnp.where(is_first | is_second, 1.0, 0.0)
    before = lax.broadcasted_iota(jnp.int32, (tokens, tokens), 0) < lax.broadcasted_iota(
        jnp.int32, (tokens, tokens), 1
    )
    rank = dot(member.astype(jnp.bfloat16), jnp.where(before, 1.0, 0.0).astype(jnp.bfloat16))
    spot = (expert * depth).astype(jnp.float32) + rank
    slot_first = jnp.sum(jnp.where(is_first, spot, 0.0), axis=0, keepdims=True).astype(jnp.int32)
    slot_second = jnp.sum(jnp.where(is_second, spot, 0.0), axis=0, keepdims=True).astype(jnp.int32)
    slot = lax.broadcasted_iota(jnp.int32, (slots, tokens), 0)
    at_first = slot == slot_first
    at_second = slot == slot_second
    place = jnp.where(at_first | at_second, 1.0, 0.0).astype(jnp.bfloat16)
    place_ref[...] = place
    scale = jnp.sum(
        jnp.where(at_first, weight_ref[0:1, :], 0.0) + jnp.where(at_second, weight_ref[1:2, :], 0.0),
        axis=1,
        keepdims=True,
    )
    width = input_ref.shape[1]
    rows_ref[:, :width] = dot(place, input_ref[...]).astype(jnp.bfloat16)
    rows_ref[:, width:] = (scale * dot(place, grad_ref[...])).astype(jnp.bfloat16)


def pick(routes, route_weight, moe_input, moe_grad, owners, depth):
    tokens, width = moe_input.shape
    slots = owners * depth
    return pl.pallas_call(
        functools.partial(pick_kernel, owners, depth),
        out_shape=(
            jax.ShapeDtypeStruct((slots, 2 * width), jnp.bfloat16),
            jax.ShapeDtypeStruct((slots, tokens), jnp.bfloat16),
        ),
        compiler_params=params(32),
        cost_estimate=pl.CostEstimate(
            flops=4 * slots * tokens * width, bytes_accessed=8 * MIB, transcendentals=0
        ),
        name="pick_rows",
    )(routes.T, route_weight.T, moe_input, moe_grad)


def expert_kernel(rows_ref, *refs):
    own, other, out_ref, total = refs[:3], refs[3:6], refs[6], refs[7]
    step = pl.program_id(0)
    width = rows_ref.shape[1] // 2
    inputs = rows_ref[:, :width]
    grads = rows_ref[:, width:]
    part = None
    for gate_ref, up_ref, down_ref in (own, other):
        gate_cols = gate_ref[...]
        up_cols = up_ref[...]
        gate_pre = dot(inputs, gate_cols)
        up_pre = dot(inputs, up_cols)
        down_grad = dot(grads, down_ref[...], NT)
        sig = jax.nn.sigmoid(gate_pre)
        gate_grad = (down_grad * up_pre * sig * (1.0 + gate_pre * (1.0 - sig))).astype(jnp.bfloat16)
        up_grad = (down_grad * gate_pre * sig).astype(jnp.bfloat16)
        term = dot(gate_grad, gate_cols, NT) + dot(up_grad, up_cols, NT)
        part = term if part is None else part + term

    @pl.when(step == 0)
    def _():
        total[...] = part

    @pl.when(step > 0)
    def _():
        total[...] += part

    @pl.when(step == pl.num_programs(0) - 1)
    def _():
        out_ref[...] = total[...].astype(jnp.bfloat16)


def experts(rows, own, other):
    count, twice = rows.shape
    width = twice // 2
    half = own[0].shape[1]
    tile = 128
    cols = pl.BlockSpec((width, tile), lambda i: (0, i))
    down = pl.BlockSpec((tile, width), lambda i: (i, 0))
    return pl.pallas_call(
        expert_kernel,
        grid=(half // tile,),
        in_specs=[pl.BlockSpec((count, twice), lambda i: (0, 0))] + [cols, cols, down] * 2,
        out_specs=pl.BlockSpec((count, width), lambda i: (0, 0)),
        out_shape=jax.ShapeDtypeStruct((count, width), jnp.bfloat16),
        scratch_shapes=[pltpu.VMEM((count, width), jnp.float32)],
        compiler_params=params(48),
        cost_estimate=pl.CostEstimate(
            flops=2 * count * width * half * 10, bytes_accessed=12 * width * half + 6 * count * width,
            transcendentals=2 * count * half,
        ),
        name="expert_terms",
    )(rows, *own, *other)


def shares_kernel(q_ref, key_ref, seen_ref, out_ref):
    seen = seen_ref[...] > 0.5
    keys = key_ref[...]
    for head in range(GROUP):
        query = q_ref[:, head * HD : (head + 1) * HD]
        scores = dot(query, keys, NT) * (HD**-0.5)
        masked = jnp.where(seen, scores, FLOOR)
        raised = jnp.where(seen, jnp.exp(masked - jnp.max(masked, axis=1, keepdims=True)), 0.0)
        shares = raised / jnp.sum(raised, axis=1, keepdims=True)
        out_ref[:, head * 2 * HD : (head + 1) * 2 * HD] = shares.astype(jnp.bfloat16)


def attention_shares(queries, key_all, seen):
    tokens, width = queries.shape
    span = key_all.shape[0]
    per = GROUP * HD
    return pl.pallas_call(
        shares_kernel,
        grid=(KVH,),
        in_specs=[
            pl.BlockSpec((tokens, per), lambda i: (0, i)),
            pl.BlockSpec((span, HD), lambda i: (0, i)),
            pl.BlockSpec((tokens, span), lambda i: (0, 0)),
        ],
        out_specs=pl.BlockSpec((tokens, GROUP * span), lambda i: (0, i)),
        out_shape=jax.ShapeDtypeStruct((tokens, KVH * GROUP * span), jnp.bfloat16),
        compiler_params=params(32),
        cost_estimate=pl.CostEstimate(
            flops=2 * tokens * width * span, bytes_accessed=4 * MIB,
            transcendentals=tokens * span * KVH * GROUP,
        ),
        name="attention_shares",
    )(queries, key_all, seen)


def tail_kernel(
    per_step, back_ref, place_ref, grad_ref, w_ref, share_ref, q_ref, key_ref, value_ref,
    moe_ref, query_out, key_out, value_out, stream,
):
    group = pl.program_id(0)
    step = pl.program_id(1)
    span = key_ref.shape[0]

    @pl.when((group == 0) & (step == 0))
    def _():
        moe = dot(place_ref[...], back_ref[...], TN).astype(jnp.bfloat16)
        moe_ref[...] = moe
        stream[...] = (grad_ref[...].astype(jnp.float32) + moe.astype(jnp.float32)).astype(jnp.bfloat16)

    head_grad = dot(stream[...], w_ref[...]).astype(jnp.bfloat16)
    keys = key_ref[...]
    values = value_ref[...]
    key_part = None
    value_part = None
    for head in range(per_step):
        cols = slice(head * HD, (head + 1) * HD)
        grad = head_grad[:, cols]
        low = share_ref[:, head * span : (head + 1) * span]
        shares = low.astype(jnp.float32)
        prob_grad = dot(grad, values, NT)
        row_dot = jnp.sum(shares * prob_grad, axis=1, keepdims=True)
        score_grad = (shares * (prob_grad - row_dot) * (HD**-0.5)).astype(jnp.bfloat16)
        query_out[:, cols] = dot(score_grad, keys).astype(jnp.bfloat16)
        key_term = dot(score_grad, q_ref[:, cols], TN)
        value_term = dot(low, grad, TN)
        key_part = key_term if key_part is None else key_part + key_term
        value_part = value_term if value_part is None else value_part + value_term

    @pl.when(step == 0)
    def _():
        key_out[...] = key_part
        value_out[...] = value_part

    @pl.when(step > 0)
    def _():
        key_out[...] += key_part
        value_out[...] += value_part


def tail(back, place, moe_grad, w_all, shares, queries, key_all, value_all):
    tokens, width = moe_grad.shape
    slots = back.shape[0]
    span = key_all.shape[0]
    per_step = 4
    steps = GROUP // per_step
    tile = per_step * HD
    whole = lambda shape: pl.BlockSpec(shape, lambda g, i: (0, 0))
    kv = pl.BlockSpec((span, HD), lambda g, i: (0, g))
    heads = pl.BlockSpec((tokens, tile), lambda g, i: (0, g * steps + i))
    return pl.pallas_call(
        functools.partial(tail_kernel, per_step),
        grid=(KVH, steps),
        in_specs=[
            whole((slots, width)),
            whole((slots, tokens)),
            whole((tokens, width)),
            pl.BlockSpec((None, width, tile), lambda g, i: (g, 0, i)),
            pl.BlockSpec((tokens, per_step * span), lambda g, i: (0, g * steps + i)),
            heads,
            kv,
            kv,
        ],
        out_specs=[whole((tokens, width)), heads, kv, kv],
        out_shape=(
            jax.ShapeDtypeStruct((tokens, width), jnp.bfloat16),
            jax.ShapeDtypeStruct(queries.shape, jnp.bfloat16),
            jax.ShapeDtypeStruct((span, KVH * HD), jnp.float32),
            jax.ShapeDtypeStruct((span, KVH * HD), jnp.float32),
        ),
        scratch_shapes=[pltpu.VMEM((tokens, width), jnp.bfloat16)],
        compiler_params=params(48),
        cost_estimate=pl.CostEstimate(
            flops=2 * tokens * width * KVH * GROUP * HD, bytes_accessed=22 * MIB, transcendentals=0
        ),
        name="tail_attention",
    )(back, place, moe_grad, w_all, shares, queries, key_all, value_all)


def local(
    moe_input,
    moe_grad,
    routes,
    route_weight,
    w_gate,
    w_up,
    w_down,
    w_out,
    queries,
    key_heads,
    value_heads,
    segments,
):
    count = lax.axis_size("blk")
    parts = lax.axis_size("groups")
    tokens, width = moe_input.shape
    owners = count // 2
    depth = 2 * max(1, 3 * tokens * routes.shape[1] // (2 * count))
    same_core = [[2 * chip + core for chip in range(owners)] for core in range(2)]
    partner = [(i, i ^ 1) for i in range(count)]
    onward = [(i, i + 1) for i in range(count - 1)]
    backward = [(i + 1, i) for i in range(count - 1)]

    share_cols = w_out.shape[1] // parts
    w_share = lax.dynamic_slice_in_dim(w_out, lax.axis_index("groups") * share_cols, share_cols, 1)
    w_all = lax.all_gather(w_share, ("groups", "blk"), axis=0, tiled=True)
    w_all = w_all.reshape(parts, width, share_cols)

    rows, place = pick(routes, route_weight, moe_input, moe_grad, owners, depth)
    rows_in = lax.all_to_all(
        rows.reshape(owners, depth, 2 * width), "blk", 0, 0, axis_index_groups=same_core, tiled=True
    )
    own = (w_gate, w_up, w_down)
    other = tuple(lax.ppermute(w, "blk", partner) for w in own)

    kv = jnp.concatenate([key_heads, value_heads], axis=1)
    prev_kv, prev_segment = lax.ppermute((kv, segments), "blk", onward)
    key_all = jnp.concatenate([prev_kv[:, : KVH * HD], key_heads], axis=0)
    value_all = jnp.concatenate([prev_kv[:, KVH * HD :], value_heads], axis=0)
    position = jnp.arange(tokens)
    own_seen = (position[None, :] <= position[:, None]) & (segments[None, :] == segments[:, None])
    prev_seen = (prev_segment[None, :] == segments[:, None]) & (lax.axis_index("blk") >= 1)
    seen = jnp.concatenate([prev_seen, own_seen], axis=1).astype(jnp.float32)
    shares = attention_shares(queries, key_all, seen)

    terms = experts(rows_in.reshape(owners * depth, 2 * width), own, other)
    back = lax.all_to_all(
        terms.reshape(owners, depth, width), "blk", 0, 0, axis_index_groups=same_core, tiled=True
    )
    moe_input_grad, query_grad, key_part, value_part = tail(
        back.reshape(owners * depth, width), place, moe_grad, w_all, shares, queries, key_all, value_all
    )
    sent = jnp.concatenate([key_part[:tokens], value_part[:tokens]], axis=1).astype(jnp.bfloat16)
    later = lax.ppermute(sent, "blk", backward).astype(jnp.float32)
    key_grad = key_part[tokens:] + later[:, : KVH * HD]
    value_grad = value_part[tokens:] + later[:, KVH * HD :]
    return (moe_input_grad, query_grad, key_grad, value_grad)


def solution(mesh):
    by_tokens = P(("groups", "blk"), None)
    return jax.shard_map(
        local,
        mesh=mesh,
        in_specs=(
            by_tokens,
            by_tokens,
            by_tokens,
            by_tokens,
            P(None, "blk"),
            P(None, "blk"),
            P("blk", None),
            P("blk", None),
            by_tokens,
            by_tokens,
            by_tokens,
            P(("groups", "blk")),
        ),
        out_specs=(by_tokens,) * 4,
        check_vma=False,
    )
```

time: 416 us -> 244 us (0.59)
  blocking collectives: 151 us -> 0 us
  Pallas kernels: 0 us -> 45.5 us
  matrix products: 33.2 us -> 0 us
  local copies, waits for them, and re-layouts: 40.6 us -> 11 us
  other arithmetic: 20.2 us -> 0.9 us
  waiting for transfers between devices: 133 us -> 148 us
    all_to_all x1 -> x0, blocking collectives: 151 us -> none  [local(): lax.all_to_all(doubled_in, 'blk', split_axis=0, concat_axis=0, tiled=True)]
    pallas_call x0 -> x4, Pallas kernels: none -> 45.5 us  [the longest x1 25.8 us: experts(): pl.pallas_call(expert_kernel, grid=(half // tile,), in_specs=[pl.BlockSpe...]
    dot_general x9 -> x0, matrix products: 29.6 us -> none  [the longest x1 8.31 us: local(): jnp.dot(stream_grad, lax.all_gather(w_out, 'blk', axis=0, tiled=True), pr...]
    all_to_all x2, waiting for transfers between devices: 71.8 us -> 91.8 us  [the longest x1 91.7 us: local(): lax.all_to_all(rows.reshape(owners, depth, 2 * width), 'blk', 0, 0, axis_...]
    gather x5 -> x0, local copies, waits for them, and re-layouts: 18 us -> none  [the longest x2 8.97 us: local(): jnp.take(combined.reshape(owners * slot_depth, model_width), slot_index,...]
    reduce_sum x4 -> x0, other arithmetic: 9.78 us -> none  [the longest x1 4.92 us: local(): jnp.sum(per_route.reshape(tok_rows, fanout, model_width), axis=1)]
    convert_element_type x3 -> x0, local copies, waits for them, and re-layouts: 6.27 us -> none  [the longest x1 4.6 us: attend(): shares_low = shares.astype(jnp.bfloat16)]
    all_to_all x2, starting transfers between devices: 8.92 us -> 13.3 us  [the longest x1 7.54 us: local(): lax.all_to_all(terms.reshape(owners, depth, width), 'blk', 0, 0, axis_ind...]
  transfers between devices with their start and end apart: 8 -> 9, of which waited for: 3 -> 6; matrix products, arithmetic and copies ran while one was open for 18% -> 0% of each run, Pallas kernels for 0% -> 12%
where the time goes in v1:
time: 244 us; the launch traced here: 243 us
  waiting for transfers between devices  148 us (61%)
  Pallas kernels  45.5 us (19%)
  starting transfers between devices  23 us (9%)
  between operations  14.3 us (6%)
  local copies, waits for them, and re-layouts  11 us (5%)
    all_to_all x1, waiting for transfers between devices, local(): lax.all_to_all(rows.reshape(owners, depth, 2 * width), 'blk', 0, 0, axis_...  91.7 us
    ppermute x2, waiting for transfers between devices, local(): prev_kv, prev_segment = lax.ppermute((kv, segments), 'blk', onward)  44.7 us
    pallas_call x1, Pallas kernels, experts(): pl.pallas_call(expert_kernel, grid=(half // tile,), in_specs=[pl.BlockSpe...  25.8 us
    pallas_call x1, Pallas kernels, tail(): pl.pallas_call(functools.partial(tail_kernel, per_step), grid=(KVH, steps...  16.3 us
    unnamed x32, local copies, waits for them, and re-layouts  10.1 us
    all_to_all x1, starting transfers between devices, local(): lax.all_to_all(terms.reshape(owners, depth, width), 'blk', 0, 0, axis_ind...  7.54 us
    ppermute x1, waiting for transfers between devices, local(): later = lax.ppermute(sent, 'blk', backward).astype(jnp.float32)  5.99 us
    ppermute x2, starting transfers between devices, local(): prev_kv, prev_segment = lax.ppermute((kv, segments), 'blk', onward)  5.97 us
  transfers between devices with their start and end apart: 9, of which 6 were waited for; matrix products, arithmetic and copies ran while one was open for 0% of the time, Pallas kernels for 12%

profile of v1, /device:TPU:13, one launch (start us, length us, event | category | flops | bytes accessed | tf_op | source)
XLA Modules:
  0.0 243.1 jit_solution(1017574670350876220)
XLA Ops:
  7.3 1.1 copy-done
  9.3 1.1 pick_rows.1
  10.4 1.7 copy-done.3
  12.1 5.8 %all-to-all-start = ((bf16[8,48,4096]{2,1,0:T(8,128)(2,1)}), bf16[8,48,4096]{2,1,0:T(8,128)(2,1)}, u32[]{:S(2)}, u32[]{:S(2)}) async-start(bf16[8,48,4096]{2,1,0:T(8,128)(2,1)} %bitcast.7), calls=%async_computation | async-start | bytes 6291456 | tf_op jit(solution)/shard_map/all_to_all | solution.py:279
  17.9 1.2 collective-permute-start
  19.7 4.1 %collective-permute-done.refs_3_ = bf16[2048,384]{1,0:T(8,128)(2,1)S(1)} collective-permute-done((bf16[2048,384]{1,0:T(8,128)(2,1)S(1)}, bf16[2048,384]{1,0:T(8,128)(2,1)S(1)}, u32[]{:S(2)}, u32[]{:S(2)}) %collective-permute-start) | collective-permute-done | bytes 1572896 | tf_op jit(solution)/shard_map/ppermute | solution.py:283
  23.7 1.1 copy-done.14
  24.9 1.9 collective-permute-done.1.refs_4_
  26.8 1.2 copy-done.15
  28.0 91.7 %all-to-all-done = bf16[8,48,4096]{2,1,0:T(8,128)(2,1)} async-done(((bf16[8,48,4096]{2,1,0:T(8,128)(2,1)}), bf16[8,48,4096]{2,1,0:T(8,128)(2,1)}, u32[]{:S(2)}, u32[]{:S(2)}) %all-to-all-start) | async-done | bytes 3145760 | tf_op jit(solution)/shard_map/all_to_all | solution.py:279
  119.8 1.4 copy-done.7
  121.2 25.8 %expert_terms.1 = bf16[384,2048]{1,0:T(8,128)(2,1)} custom-call(bf16[384,4096]{1,0:T(8,128)(2,1)} %bitcast.3.rows_ref, bf16[2048,384]{1,0:T(8,128)(2,1)S(1)} %copy-done.6, bf16[2048,384]{1,0:T(8,128)(2,1)S(1)} %copy-done.7, bf16[384,2048]{1,0:T(8,128)(2,1)} %refs_2_.1, bf16[2048,384]{1,0:T(8,128)(2,1)} %copy-done.14, bf16[2048,384]{1,0:T(8,128)(2,1)} %copy-done.15, ...), custom_call_target="tpu_custom_call" | custom-call | flops 6039797760 | bytes 14155776 | tf_op jit(solution)/shard_map/expert_terms/pallas_call | solution.py:115
  147.0 7.5 %all-to-all-start.1 = ((bf16[8,48,2048]{2,1,0:T(8,128)(2,1)}), bf16[8,48,2048]{2,1,0:T(8,128)(2,1)}, u32[]{:S(2)}, u32[]{:S(2)}) async-start(bf16[8,48,2048]{2,1,0:T(8,128)(2,1)} %bitcast.4), calls=%async_computation.1 | async-start | bytes 3145728 | tf_op jit(solution)/shard_map/all_to_all | solution.py:296
  154.5 4.0 %collective-permute-start.4 = (s32[128]{0:T(128)S(1)}, s32[128]{0:T(128)S(1)}, u32[]{:S(2)}, u32[]{:S(2)}) collective-permute-start(s32[128]{0:T(128)S(1)} %copy-done.13), channel_id=1, source_target_pairs={{0,1},{1,2},{2,3},{3,4},{4,5},{5,6},{6,7},{7,8},{8,9},{9,10},{10,1... | collective-permute-start | bytes 1544 | tf_op jit(solution)/shard_map/ppermute | solution.py:286
  158.6 1.9 collective-permute-start.3
  160.5 43.5 %collective-permute-done.4 = s32[128]{0:T(128)S(1)} collective-permute-done((s32[128]{0:T(128)S(1)}, s32[128]{0:T(128)S(1)}, u32[]{:S(2)}, u32[]{:S(2)}) %collective-permute-start.4) | collective-permute-done | bytes 544 | tf_op jit(solution)/shard_map/ppermute | solution.py:286
  204.1 1.2 collective-permute-done.3
  205.4 1.2 copy-done.1
  206.6 2.3 attention_shares.1.share_ref
  209.0 1.2 copy-done.2
  210.2 1.0 copy-done.5
  211.2 16.3 %tail_attention.1 = (bf16[128,2048]{1,0:T(8,128)(2,1)}, bf16[128,4096]{1,0:T(8,128)(2,1)}, f32[256,256]{1,0:T(8,128)S(1)}, f32[256,256]{1,0:T(8,128)S(1)}) custom-call(bf16[384,2048]{1,0:T(8,128)(2,1)} %bitcast.5.back_ref, bf16[384,128]{1,0:T(8,128)(2,1)S(1)} %get-tuple-element.11.place_ref, bf16[128,2048]{1,0:T(8,128)(2,1)S(1)} %copy-done.5, ...), custom_call_target="tpu_custom_call" | custom-call | flops 2147483648 | bytes 23068672 | tf_op jit(solution)/shard_map/tail_attention/pallas_call | solution.py:220
  227.6 1.9 collective-permute-start.5
  229.5 6.0 %collective-permute-done.5 = bf16[128,512]{1,0:T(8,128)(2,1)S(1)} collective-permute-done((bf16[128,512]{1,0:T(8,128)(2,1)S(1)}, bf16[128,512]{1,0:T(8,128)(2,1)S(1)}, u32[]{:S(2)}, u32[]{:S(2)}) %collective-permute-start.5) | collective-permute-done | bytes 131104 | tf_op jit(solution)/shard_map/ppermute | solution.py:303
  (42 shorter events, 2.4 us)
Async XLA Ops:
  7.2 1.2 copy-start
  7.2 2.1 copy-start.9
  7.2 2.1 copy-start.10
  7.2 2.1 copy-start.8
  7.2 2.1 copy-start.4
  7.2 201.7 %all-gather.2.cloned.1.call-start = ((), (), s32[]{:S(2)}) async-start(), calls=%async_computation.2 | async-start | bytes 17301504 | tf_op jit(solution)/shard_map/all_gather | solution.py:275
  10.4 1.7 copy-start.3
  12.1 5.8 %copy-start.6 = (bf16[2048,384]{1,0:T(8,128)(2,1)S(1)}, bf16[2048,384]{1,0:T(8,128)(2,1)}, u32[]{:S(2)}) copy-start(bf16[2048,384]{1,0:T(8,128)(2,1)} %refs_0_.1) | copy-start | bytes 4718596
  12.1 107.6 %all-to-all-start = ((bf16[8,48,4096]{2,1,0:T(8,128)(2,1)}), bf16[8,48,4096]{2,1,0:T(8,128)(2,1)}, u32[]{:S(2)}, u32[]{:S(2)}) async-start(bf16[8,48,4096]{2,1,0:T(8,128)(2,1)} %bitcast.7), calls=%async_computation | async-start | bytes 6291456 | tf_op jit(solution)/shard_map/all_to_all | solution.py:279
  17.9 5.8 %collective-permute-start = (bf16[2048,384]{1,0:T(8,128)(2,1)S(1)}, bf16[2048,384]{1,0:T(8,128)(2,1)S(1)}, u32[]{:S(2)}, u32[]{:S(2)}) collective-permute-start(bf16[2048,384]{1,0:T(8,128)(2,1)S(1)} %copy-done.6), channel_id=1, source_target_pairs={{0,1},{1,0},{2,3},{3,2},{4,5},{5,4},{6,7},{7,6},{8,9},{9,8},{10,11... | collective-permute-start | bytes 4718600 | tf_op jit(solution)/shard_map/ppermute | solution.py:283
  19.2 7.6 %collective-permute-start.1 = (bf16[2048,384]{1,0:T(8,128)(2,1)}, bf16[2048,384]{1,0:T(8,128)(2,1)S(1)}, u32[]{:S(2)}, u32[]{:S(2)}) collective-permute-start(bf16[2048,384]{1,0:T(8,128)(2,1)} %refs_1_.1), channel_id=1, source_target_pairs={{0,1},{1,0},{2,3},{3,2},{4,5},{5,4},{6,7},{7,6},{8,9},{9,8},{10,11... | collective-permute-start | bytes 4718600 | tf_op jit(solution)/shard_map/ppermute | solution.py:283
  19.2 8.8 %collective-permute-start.2 = (bf16[384,2048]{1,0:T(8,128)(2,1)}, bf16[384,2048]{1,0:T(8,128)(2,1)}, u32[]{:S(2)}, u32[]{:S(2)}) collective-permute-start(bf16[384,2048]{1,0:T(8,128)(2,1)} %refs_2_.1), channel_id=1, source_target_pairs={{0,1},{1,0},{2,3},{3,2},{4,5},{5,4},{6,7},{7,6},{8,9},{9,8},{10,11... | collective-permute-start | bytes 4718600 | tf_op jit(solution)/shard_map/ppermute | solution.py:283
  23.7 1.1 copy-start.14
  26.8 1.2 copy-start.15
  119.8 1.4 copy-start.7
  146.9 7.6 %copy-start.13 = (s32[128]{0:T(128)S(1)}, s32[128]{0:T(128)}, u32[]{:S(2)}) copy-start(s32[128]{0:T(128)} %param.23) | copy-start | bytes 1540
  146.9 11.6 %copy-start.11 = (bf16[128,256]{1,0:T(8,128)(2,1)S(1)}, bf16[128,256]{1,0:T(8,128)(2,1)}, u32[]{:S(2)}) copy-start(bf16[128,256]{1,0:T(8,128)(2,1)} %param.21) | copy-start | bytes 196612
  146.9 11.6 %copy-start.12 = (bf16[128,256]{1,0:T(8,128)(2,1)S(1)}, bf16[128,256]{1,0:T(8,128)(2,1)}, u32[]{:S(2)}) copy-start(bf16[128,256]{1,0:T(8,128)(2,1)} %param.22) | copy-start | bytes 196612
  147.0 62.0 %all-to-all-start.1 = ((bf16[8,48,2048]{2,1,0:T(8,128)(2,1)}), bf16[8,48,2048]{2,1,0:T(8,128)(2,1)}, u32[]{:S(2)}, u32[]{:S(2)}) async-start(bf16[8,48,2048]{2,1,0:T(8,128)(2,1)} %bitcast.4), calls=%async_computation.1 | async-start | bytes 3145728 | tf_op jit(solution)/shard_map/all_to_all | solution.py:296
  154.5 49.5 %collective-permute-start.4 = (s32[128]{0:T(128)S(1)}, s32[128]{0:T(128)S(1)}, u32[]{:S(2)}, u32[]{:S(2)}) collective-permute-start(s32[128]{0:T(128)S(1)} %copy-done.13), channel_id=1, source_target_pairs={{0,1},{1,2},{2,3},{3,4},{4,5},{5,6},{6,7},{7,8},{8,9},{9,10},{10,1... | collective-permute-start | bytes 1544 | tf_op jit(solution)/shard_map/ppermute | solution.py:286
  158.6 46.7 %collective-permute-start.3 = (bf16[128,512]{1,0:T(8,128)(2,1)S(1)}, bf16[128,512]{1,0:T(8,128)(2,1)S(1)}, u32[]{:S(2)}, u32[]{:S(2)}) collective-permute-start(bf16[128,512]{1,0:T(8,128)(2,1)S(1)} %pad_maximum_fusion), channel_id=1, source_target_pairs={{0,1},{1,2},{2,3},{3,4},{4,5},{5,6},{6,7},{7,8},{8,9},{9,10},{10,1... | collective-permute-start | bytes 393224 | tf_op jit(solution)/shard_map/ppermute | solution.py:286
  205.4 1.2 copy-start.1
  209.0 1.2 copy-start.2
  227.6 7.9 %collective-permute-start.5 = (bf16[128,512]{1,0:T(8,128)(2,1)S(1)}, bf16[128,512]{1,0:T(8,128)(2,1)S(1)}, u32[]{:S(2)}, u32[]{:S(2)}) collective-permute-start(bf16[128,512]{1,0:T(8,128)(2,1)S(1)} %pad_maximum_fusion.3), channel_id=1, source_target_pairs={{1,0},{2,1},{3,2},{4,3},{5,4},{6,5},{7,6},{8,7},{9,8},{10,9},{11,1... | collective-permute-start | bytes 393224 | tf_op jit(solution)/shard_map/ppermute | solution.py:303
  (1 other events, 1.0 us)
Sparse Core Ops, SparseCore 0:
  11.5 178.9 all-gather.1

commit v2 on v1

--- a/solution.py
+++ b/solution.py
@@ -73,59 +73,95 @@
     )(routes.T, route_weight.T, moe_input, moe_grad)
 
 
-def expert_kernel(rows_ref, *refs):
-    own, other, out_ref, total = refs[:3], refs[3:6], refs[6], refs[7]
+def weights_kernel(*refs):
+    own, other, (cols_ref, down_ref, rows_ref) = refs[:3], refs[3:6], refs[6:]
+    tile = own[0].shape[1]
+    for place, (gate_ref, up_ref, low_ref) in enumerate((own, other)):
+        for kind, ref in enumerate((gate_ref, up_ref)):
+            spot = slice((2 * kind + place) * tile, (2 * kind + place + 1) * tile)
+            cols_ref[0, :, spot] = ref[...]
+            rows_ref[0, spot, :] = ref[...].T
+        down_ref[0, :, place * tile : (place + 1) * tile] = low_ref[...].T
+
+
+def prepare_weights(own, other):
+    width, half = own[0].shape
+    tile = 128
+    steps = half // tile
+    cols = pl.BlockSpec((width, tile), lambda i: (0, i))
+    down = pl.BlockSpec((tile, width), lambda i: (i, 0))
+    return pl.pallas_call(
+        weights_kernel,
+        grid=(steps,),
+        in_specs=[cols, cols, down] * 2,
+        out_specs=[
+            pl.BlockSpec((1, width, 4 * tile), lambda i: (i, 0, 0)),
+            pl.BlockSpec((1, width, 2 * tile), lambda i: (i, 0, 0)),
+            pl.BlockSpec((1, 4 * tile, width), lambda i: (i, 0, 0)),
+        ],
+        out_shape=(
+            jax.ShapeDtypeStruct((steps, width, 4 * tile), jnp.bfloat16),
+            jax.ShapeDtypeStruct((steps, width, 2 * tile), jnp.bfloat16),
+            jax.ShapeDtypeStruct((steps, 4 * tile, width), jnp.bfloat16),
+        ),
+        compiler_params=params(48),
+        cost_estimate=pl.CostEstimate(
+            flops=0, bytes_accessed=32 * width * half, transcendentals=0
+        ),
+        name="prepare_weights",
+    )(*own, *other)
+
+
+def expert_kernel(steps, rows_ref, cols_ref, down_ref, back_ref, out_ref, hidden):
     step = pl.program_id(0)
     width = rows_ref.shape[1] // 2
-    inputs = rows_ref[:, :width]
-    grads = rows_ref[:, width:]
-    part = None
-    for gate_ref, up_ref, down_ref in (own, other):
-        gate_cols = gate_ref[...]
-        up_cols = up_ref[...]
-        gate_pre = dot(inputs, gate_cols)
-        up_pre = dot(inputs, up_cols)
-        down_grad = dot(grads, down_ref[...], NT)
+    pair = down_ref.shape[2]
+
+    @pl.when(step < steps)
+    def _():
+        both_pre = dot(rows_ref[:, :width], cols_ref[0])
+        gate_pre = both_pre[:, :pair]
+        up_pre = both_pre[:, pair:]
+        down_grad = dot(rows_ref[:, width:], down_ref[0])
         sig = jax.nn.sigmoid(gate_pre)
-        gate_grad = (down_grad * up_pre * sig * (1.0 + gate_pre * (1.0 - sig))).astype(jnp.bfloat16)
-        up_grad = (down_grad * gate_pre * sig).astype(jnp.bfloat16)
-        term = dot(gate_grad, gate_cols, NT) + dot(up_grad, up_cols, NT)
-        part = term if part is None else part + term
-
-    @pl.when(step == 0)
-    def _():
-        total[...] = part
-
-    @pl.when(step > 0)
-    def _():
-        total[...] += part
-
-    @pl.when(step == pl.num_programs(0) - 1)
-    def _():
-        out_ref[...] = total[...].astype(jnp.bfloat16)
-
-
-def experts(rows, own, other):
+        hidden[step, :, :pair] = (
+            down_grad * up_pre * sig * (1.0 + gate_pre * (1.0 - sig))
+        ).astype(jnp.bfloat16)
+        hidden[step, :, pair:] = (down_grad * gate_pre * sig).astype(jnp.bfloat16)
+
+    @pl.when(step >= steps)
+    def _():
+        total = dot(hidden[0], back_ref[0])
+        for i in range(1, steps):
+            total += dot(hidden[i], back_ref[i])
+        out_ref[...] = total.astype(jnp.bfloat16)
+
+
+def experts(rows, cols, down, back):
     count, twice = rows.shape
-    width = twice // 2
-    half = own[0].shape[1]
-    tile = 128
-    cols = pl.BlockSpec((width, tile), lambda i: (0, i))
-    down = pl.BlockSpec((tile, width), lambda i: (i, 0))
-    return pl.pallas_call(
-        expert_kernel,
-        grid=(half // tile,),
-        in_specs=[pl.BlockSpec((count, twice), lambda i: (0, 0))] + [cols, cols, down] * 2,
-        out_specs=pl.BlockSpec((count, width), lambda i: (0, 0)),
+    steps, width, quad = cols.shape
+    tile = 512
+    last = steps - 1
+    turn = lambda i: jnp.maximum(i - steps, 0)
+    return pl.pallas_call(
+        functools.partial(expert_kernel, steps),
+        grid=(steps + width // tile,),
+        in_specs=[
+            pl.BlockSpec((count, twice), lambda i: (0, 0)),
+            pl.BlockSpec((1, width, quad), lambda i: (jnp.minimum(i, last), 0, 0)),
+            pl.BlockSpec((1, width, quad // 2), lambda i: (jnp.minimum(i, last), 0, 0)),
+            pl.BlockSpec((steps, quad, tile), lambda i: (0, 0, turn(i))),
+        ],
+        out_specs=pl.BlockSpec((count, tile), lambda i: (0, turn(i))),
         out_shape=jax.ShapeDtypeStruct((count, width), jnp.bfloat16),
-        scratch_shapes=[pltpu.VMEM((count, width), jnp.float32)],
+        scratch_shapes=[pltpu.VMEM((steps, count, quad), jnp.bfloat16)],
         compiler_params=params(48),
         cost_estimate=pl.CostEstimate(
-            flops=2 * count * width * half * 10, bytes_accessed=12 * width * half + 6 * count * width,
-            transcendentals=2 * count * half,
+            flops=5 * count * width * steps * quad, bytes_accessed=20 * MIB,
+            transcendentals=count * steps * quad,
         ),
         name="expert_terms",
-    )(rows, *own, *other)
+    )(rows, cols, down, back)
 
 
 def shares_kernel(q_ref, key_ref, seen_ref, out_ref):
@@ -164,7 +200,7 @@
 
 
 def tail_kernel(
-    per_step, back_ref, place_ref, grad_ref, w_ref, share_ref, q_ref, key_ref, value_ref,
+    per_step, order, back_ref, place_ref, grad_ref, w_ref, share_ref, q_ref, key_ref, value_ref,
     moe_ref, query_out, key_out, value_out, stream,
 ):
     group = pl.program_id(0)
@@ -175,7 +211,10 @@
     def _():
         moe = dot(place_ref[...], back_ref[...], TN).astype(jnp.bfloat16)
         moe_ref[...] = moe
-        stream[...] = (grad_ref[...].astype(jnp.float32) + moe.astype(jnp.float32)).astype(jnp.bfloat16)
+        added = (grad_ref[...].astype(jnp.float32) + moe.astype(jnp.float32)).astype(jnp.bfloat16)
+        size = added.shape[1] // len(order)
+        for to, source in enumerate(order):
+            stream[:, to * size : (to + 1) * size] = added[:, source * size : (source + 1) * size]
 
     head_grad = dot(stream[...], w_ref[...]).astype(jnp.bfloat16)
     keys = key_ref[...]
@@ -207,7 +246,7 @@
         value_out[...] += value_part
 
 
-def tail(back, place, moe_grad, w_all, shares, queries, key_all, value_all):
+def tail(order, back, place, moe_grad, w_all, shares, queries, key_all, value_all):
     tokens, width = moe_grad.shape
     slots = back.shape[0]
     span = key_all.shape[0]
@@ -218,7 +257,7 @@
     kv = pl.BlockSpec((span, HD), lambda g, i: (0, g))
     heads = pl.BlockSpec((tokens, tile), lambda g, i: (0, g * steps + i))
     return pl.pallas_call(
-        functools.partial(tail_kernel, per_step),
+        functools.partial(tail_kernel, per_step, order),
         grid=(KVH, steps),
         in_specs=[
             whole((slots, width)),
@@ -246,6 +285,14 @@
     )(back, place, moe_grad, w_all, shares, queries, key_all, value_all)
 
 
+def far_first(share):
+    for axis in ("far", "near"):
+        moved = lax.ppermute(share, axis, [(0, 1), (1, 0)])
+        mine = lax.axis_index(axis) == 0
+        share = jnp.where(mine, jnp.stack([share, moved]), jnp.stack([moved, share]))
+    return share
+
+
 def local(
     moe_input,
     moe_grad,
@@ -260,70 +307,86 @@
     value_heads,
     segments,
 ):
-    count = lax.axis_size("blk")
+    chips = ("far", "near", "low")
+    blk = chips + ("core",)
+    low = lax.axis_size("low")
+    owners = 4 * low
+    count = 2 * owners
     parts = lax.axis_size("groups")
     tokens, width = moe_input.shape
-    owners = count // 2
     depth = 2 * max(1, 3 * tokens * routes.shape[1] // (2 * count))
-    same_core = [[2 * chip + core for chip in range(owners)] for core in range(2)]
-    partner = [(i, i ^ 1) for i in range(count)]
     onward = [(i, i + 1) for i in range(count - 1)]
     backward = [(i + 1, i) for i in range(count - 1)]
 
     share_cols = w_out.shape[1] // parts
     w_share = lax.dynamic_slice_in_dim(w_out, lax.axis_index("groups") * share_cols, share_cols, 1)
-    w_all = lax.all_gather(w_share, ("groups", "blk"), axis=0, tiled=True)
+    w_plane = far_first(w_share)
+    w_all = lax.all_gather(w_plane, ("groups", "low", "core"), axis=0, tiled=False)
+    block = w_out.shape[0]
+    w_all = w_all.reshape(parts, 2 * low, 2, 2, block, share_cols)
+    order = tuple(
+        (2 * far + near) * 2 * low + rest
+        for rest in range(2 * low)
+        for near in range(2)
+        for far in range(2)
+    )
+    if block % 128:
+        w_all = w_all.transpose(0, 3, 2, 1, 4, 5)
+        order = (0,)
     w_all = w_all.reshape(parts, width, share_cols)
 
     rows, place = pick(routes, route_weight, moe_input, moe_grad, owners, depth)
-    rows_in = lax.all_to_all(
-        rows.reshape(owners, depth, 2 * width), "blk", 0, 0, axis_index_groups=same_core, tiled=True
-    )
+    rows_in = lax.all_to_all(rows.reshape(owners, depth, 2 * width), chips, 0, 0, tiled=True)
     own = (w_gate, w_up, w_down)
-    other = tuple(lax.ppermute(w, "blk", partner) for w in own)
+    other = tuple(lax.ppermute(w, "core", [(0, 1), (1, 0)]) for w in own)
+    prepared = prepare_weights(own, other)
 
     kv = jnp.concatenate([key_heads, value_heads], axis=1)
-    prev_kv, prev_segment = lax.ppermute((kv, segments), "blk", onward)
+    prev_kv, prev_segment = lax.ppermute((kv, segments), blk, onward)
     key_all = jnp.concatenate([prev_kv[:, : KVH * HD], key_heads], axis=0)
     value_all = jnp.concatenate([prev_kv[:, KVH * HD :], value_heads], axis=0)
     position = jnp.arange(tokens)
     own_seen = (position[None, :] <= position[:, None]) & (segments[None, :] == segments[:, None])
-    prev_seen = (prev_segment[None, :] == segments[:, None]) & (lax.axis_index("blk") >= 1)
+    prev_seen = (prev_segment[None, :] == segments[:, None]) & (lax.axis_index(blk) >= 1)
     seen = jnp.concatenate([prev_seen, own_seen], axis=1).astype(jnp.float32)
     shares = attention_shares(queries, key_all, seen)
 
-    terms = experts(rows_in.reshape(owners * depth, 2 * width), own, other)
-    back = lax.all_to_all(
-        terms.reshape(owners, depth, width), "blk", 0, 0, axis_index_groups=same_core, tiled=True
-    )
+    prepared, shares, rows_in = lax.optimization_barrier((prepared, shares, rows_in))
+    terms = experts(rows_in.reshape(owners * depth, 2 * width), *prepared)
+    back = lax.all_to_all(terms.reshape(owners, depth, width), chips, 0, 0, tiled=True)
     moe_input_grad, query_grad, key_part, value_part = tail(
-        back.reshape(owners * depth, width), place, moe_grad, w_all, shares, queries, key_all, value_all
+        order, back.reshape(owners * depth, width), place, moe_grad, w_all, shares, queries,
+        key_all, value_all,
     )
     sent = jnp.concatenate([key_part[:tokens], value_part[:tokens]], axis=1).astype(jnp.bfloat16)
-    later = lax.ppermute(sent, "blk", backward).astype(jnp.float32)
+    later = lax.ppermute(sent, blk, backward).astype(jnp.float32)
     key_grad = key_part[tokens:] + later[:, : KVH * HD]
     value_grad = value_part[tokens:] + later[:, KVH * HD :]
     return (moe_input_grad, query_grad, key_grad, value_grad)
 
 
 def solution(mesh):
-    by_tokens = P(("groups", "blk"), None)
+    names = ("groups", "far", "near", "low", "core")
+    shape = (mesh.shape["groups"], 2, 2, mesh.shape["blk"] // 8, 2)
+    fine = jax.sharding.Mesh(mesh.devices.reshape(shape), names)
+    blk = names[1:]
+    by_tokens = P(names, None)
     return jax.shard_map(
         local,
-        mesh=mesh,
+        mesh=fine,
         in_specs=(
             by_tokens,
             by_tokens,
             by_tokens,
             by_tokens,
-            P(None, "blk"),
-            P(None, "blk"),
-            P("blk", None),
-            P("blk", None),
-            by_tokens,
-            by_tokens,
-            by_tokens,
-            P(("groups", "blk")),
+            P(None, blk),
+            P(None, blk),
+            P(blk, None),
+            P(blk, None),
+            by_tokens,
+            by_tokens,
+            by_tokens,
+            P(names),
         ),
         out_specs=(by_tokens,) * 4,
         check_vma=False,

time: 244 us -> 244 us (level); the launches traced: 243 us -> 241 us
  other arithmetic: 0.9 us -> 3.82 us
  local copies, waits for them, and re-layouts: 11 us -> 8.16 us
    all_to_all x2, waiting for transfers between devices: 91.8 us -> 33.8 us  [the longest x1 33.8 us: local(): lax.all_to_all(terms.reshape(owners, depth, width), chips, 0, 0, tiled=True)]
    ppermute x6 -> x8, waiting for transfers between devices: 56.6 us -> 113 us  [the longest x2 61.7 us: local(): prev_kv, prev_segment = lax.ppermute((kv, segments), blk, onward)]
    ppermute x6 -> x8, starting transfers between devices: 9.63 us -> 12.6 us  [the longest x2 5.38 us: local(): prev_kv, prev_segment = lax.ppermute((kv, segments), blk, onward)]
    select_n x0 -> x2, other arithmetic: none -> 2.74 us  [far_first(): jnp.where(mine, jnp.stack([share, moved]), jnp.stack([moved, share]))]
    unnamed x32, local copies, waits for them, and re-layouts: 10.1 us -> 7.4 us
    pallas_call x2 -> x3, Pallas kernels: 42.1 us -> 40.1 us  [the longest x1 16.4 us: tail(): pl.pallas_call(functools.partial(tail_kernel, per_step, order), grid=(KVH...]
  transfers between devices with their start and end apart: 9 -> 11, of which waited for: 6 -> 6; matrix products, arithmetic and copies ran while one was open for 0% -> 0% of each run, Pallas kernels for 12% -> 11%
where the time goes in v2:
time: 244 us; the launch traced here: 241 us
  waiting for transfers between devices  147 us (60%)
  Pallas kernels  43.6 us (18%)
  starting transfers between devices  23.6 us (10%)
  between operations  14.3 us (6%)
  local copies, waits for them, and re-layouts  8.16 us (3%)
  other arithmetic  3.82 us (2%)
    ppermute x2, waiting for transfers between devices, local(): prev_kv, prev_segment = lax.ppermute((kv, segments), blk, onward)  61.7 us
    ppermute x2, waiting for transfers between devices, far_first(): moved = lax.ppermute(share, axis, [(0, 1), (1, 0)])  46.9 us
    all_to_all x1, waiting for transfers between devices, local(): lax.all_to_all(terms.reshape(owners, depth, width), chips, 0, 0, tiled=True)  33.8 us
    pallas_call x1, Pallas kernels, tail(): pl.pallas_call(functools.partial(tail_kernel, per_step, order), grid=(KVH...  16.4 us
    pallas_call x1, Pallas kernels, experts(): pl.pallas_call(functools.partial(expert_kernel, steps), grid=(steps + wid...  13.1 us
    pallas_call x1, Pallas kernels, prepare_weights(): pl.pallas_call(weights_kernel, grid=(steps,), in_specs=[cols, cols, down]...  10.6 us
    unnamed x32, local copies, waits for them, and re-layouts  7.4 us
    all_to_all x1, starting transfers between devices, local(): lax.all_to_all(rows.reshape(owners, depth, 2 * width), chips, 0, 0, tiled...  6.61 us
  transfers between devices with their start and end apart: 11, of which 6 were waited for; matrix products, arithmetic and copies ran while one was open for 0% of the time, Pallas kernels for 11%

profile of v2, /device:TPU:13, one launch (start us, length us, event | category | flops | bytes accessed | tf_op | source)
XLA Modules:
  0.0 240.7 jit_solution(6652232584815678342)
XLA Ops:
  7.2 1.2 copy-done
  8.4 2.4 collective-permute-start.5
  10.8 22.7 %collective-permute-done.5 = bf16[128,2048]{1,0:T(8,128)(2,1)S(1)} collective-permute-done((bf16[128,2048]{1,0:T(8,128)(2,1)S(1)}, bf16[128,2048]{1,0:T(8,128)(2,1)S(1)}, u32[]{:S(2)}, u32[]{:S(2)}) %collective-permute-start.5) | collective-permute-done | bytes 524320 | tf_op jit(solution)/shard_map/ppermute | solution.py:290
  33.6 1.1 maximum_select_fusion.2
  35.0 24.2 %collective-permute-done.6 = bf16[2,128,2048]{2,1,0:T(8,128)(2,1)S(1)} collective-permute-done((bf16[2,128,2048]{2,1,0:T(8,128)(2,1)}, bf16[2,128,2048]{2,1,0:T(8,128)(2,1)S(1)}, u32[]{:S(2)}, u32[]{:S(2)}) %collective-permute-start.6) | collective-permute-done | bytes 1048608 | tf_op jit(solution)/shard_map/ppermute | solution.py:290
  59.2 1.6 maximum_select_fusion
  62.0 1.1 pick_rows.1
  63.1 1.6 copy-done.4
  64.7 6.6 %all-to-all-start = ((bf16[8,48,4096]{2,1,0:T(8,128)(2,1)}), bf16[8,48,4096]{2,1,0:T(8,128)(2,1)}, u32[]{:S(2)}, u32[]{:S(2)}) async-start(bf16[8,48,4096]{2,1,0:T(8,128)(2,1)} %bitcast.16), calls=%async_computation | async-start | bytes 6291456 | tf_op jit(solution)/shard_map/all_to_all | solution.py:339
  71.3 1.9 collective-permute-start
  73.8 3.0 %collective-permute-start.4 = (s32[128]{0:T(128)S(1)}, s32[128]{0:T(128)S(1)}, u32[]{:S(2)}, u32[]{:S(2)}) collective-permute-start(s32[128]{0:T(128)S(1)} %copy-done.15), channel_id=1, source_target_pairs={{0,1},{1,2},{2,3},{3,4},{4,5},{5,6},{6,7},{7,8},{8,9},{9,10},{10,1... | collective-permute-start | bytes 1544 | tf_op jit(solution)/shard_map/ppermute | solution.py:345
  76.8 2.4 %collective-permute-start.3 = (bf16[128,512]{1,0:T(8,128)(2,1)S(1)}, bf16[128,512]{1,0:T(8,128)(2,1)S(1)}, u32[]{:S(2)}, u32[]{:S(2)}) collective-permute-start(bf16[128,512]{1,0:T(8,128)(2,1)S(1)} %pad_maximum_fusion), channel_id=1, source_target_pairs={{0,1},{1,2},{2,3},{3,4},{4,5},{5,6},{6,7},{7,8},{8,9},{9,10},{10,1... | collective-permute-start | bytes 393224 | tf_op jit(solution)/shard_map/ppermute | solution.py:345
  79.2 60.4 %collective-permute-done.4 = s32[128]{0:T(128)S(1)} collective-permute-done((s32[128]{0:T(128)S(1)}, s32[128]{0:T(128)S(1)}, u32[]{:S(2)}, u32[]{:S(2)}) %collective-permute-start.4) | collective-permute-done | bytes 544 | tf_op jit(solution)/shard_map/ppermute | solution.py:345
  139.7 1.3 collective-permute-done.3
  141.7 2.3 attention_shares.1.share_ref
  144.0 10.6 %prepare_weights.1 = (bf16[3,2048,512]{2,1,0:T(8,128)(2,1)}, bf16[3,2048,256]{2,1,0:T(8,128)(2,1)}, bf16[3,512,2048]{2,1,0:T(8,128)(2,1)}) custom-call(bf16[2048,384]{1,0:T(8,128)(2,1)} %refs_0_.1, bf16[2048,384]{1,0:T(8,128)(2,1)} %refs_1_.1, bf16[384,2048]{1,0:T(8,128)(2,1)} %refs_2_.1, bf16[2048,384]{1,0:T(8,128)(2,1)} %collective-permute-done.refs_3_, ...), custom_call_target="tpu_custom_call" | custom-call | bytes 25165824 | tf_op jit(solution)/shard_map/prepare_weights/pallas_call | solution.py:93
  154.6 13.1 %expert_terms.1 = bf16[384,2048]{1,0:T(8,128)(2,1)S(1)} custom-call(bf16[384,4096]{1,0:T(8,128)(2,1)} %bitcast.3.rows_ref, bf16[3,2048,512]{2,1,0:T(8,128)(2,1)} %get-tuple-element.23.cols_ref, bf16[3,2048,256]{2,1,0:T(8,128)(2,1)} %get-tuple-element.24.down_ref, bf16[3,512,2048]{2,1,0:T(8,128)(2,1)} %get-tuple-element.25.back_ref), custom_call_target="tpu_custom_call" | custom-call | flops 6039797760 | bytes 20971520 | tf_op jit(solution)/shard_map/expert_terms/pallas_call | solution.py:146
  167.8 1.1 copy-done.5
  168.9 4.4 %all-to-all-start.1 = ((bf16[8,48,2048]{2,1,0:T(8,128)(2,1)}), bf16[8,48,2048]{2,1,0:T(8,128)(2,1)}, u32[]{:S(2)}, u32[]{:S(2)}) async-start(bf16[8,48,2048]{2,1,0:T(8,128)(2,1)} %bitcast.17), calls=%async_computation.1 | async-start | bytes 3145728 | tf_op jit(solution)/shard_map/all_to_all | solution.py:356
  173.3 33.8 %all-to-all-done.1 = bf16[8,48,2048]{2,1,0:T(8,128)(2,1)} async-done(((bf16[8,48,2048]{2,1,0:T(8,128)(2,1)}), bf16[8,48,2048]{2,1,0:T(8,128)(2,1)}, u32[]{:S(2)}, u32[]{:S(2)}) %all-to-all-start.1) | async-done | bytes 1572896 | tf_op jit(solution)/shard_map/all_to_all | solution.py:356
  207.2 1.2 copy-done.3
  209.4 16.4 %tail_attention.1 = (bf16[128,2048]{1,0:T(8,128)(2,1)}, bf16[128,4096]{1,0:T(8,128)(2,1)}, f32[256,256]{1,0:T(8,128)S(1)}, f32[256,256]{1,0:T(8,128)S(1)}) custom-call(bf16[384,2048]{1,0:T(8,128)(2,1)} %bitcast.5.back_ref, bf16[384,128]{1,0:T(8,128)(2,1)S(1)} %get-tuple-element.26.place_ref, bf16[128,2048]{1,0:T(8,128)(2,1)S(1)} %copy-done.7, ...), custom_call_target="tpu_custom_call" | custom-call | flops 2147483648 | bytes 23068672 | tf_op jit(solution)/shard_map/tail_attention/pallas_call | solution.py:259
  225.9 2.4 collective-permute-start.7
  228.3 4.8 %collective-permute-done.7 = bf16[128,512]{1,0:T(8,128)(2,1)S(1)} collective-permute-done((bf16[128,512]{1,0:T(8,128)(2,1)S(1)}, bf16[128,512]{1,0:T(8,128)(2,1)S(1)}, u32[]{:S(2)}, u32[]{:S(2)}) %collective-permute-start.7) | collective-permute-done | bytes 131104 | tf_op jit(solution)/shard_map/ppermute | solution.py:362
  (53 shorter events, 4.7 us)
Async XLA Ops:
  7.2 1.2 copy-start
  7.2 200.0 %all-gather.2.cloned.1.call-start = ((), (), s32[]{:S(2)}) async-start(), calls=%async_computation.2 | async-start | bytes 18874368 | tf_op jit(solution)/shard_map/all_gather | solution.py:324
  8.4 25.1 %collective-permute-start.5 = (bf16[128,2048]{1,0:T(8,128)(2,1)S(1)}, bf16[128,2048]{1,0:T(8,128)(2,1)S(1)}, u32[]{:S(2)}, u32[]{:S(2)}) collective-permute-start(bf16[128,2048]{1,0:T(8,128)(2,1)S(1)} %constant_dynamic-slice_fusion), channel_id=1, source_target_pairs={{0,8},{8,0},{1,9},{9,1},{2,10},{10,2},{3,11},{11,3},{4,12},{12,4},... | collective-permute-start | bytes 1572872 | tf_op jit(solution)/shard_map/ppermute | solution.py:290
  34.7 24.4 %collective-permute-start.6 = (bf16[2,128,2048]{2,1,0:T(8,128)(2,1)}, bf16[2,128,2048]{2,1,0:T(8,128)(2,1)S(1)}, u32[]{:S(2)}, u32[]{:S(2)}) collective-permute-start(bf16[2,128,2048]{2,1,0:T(8,128)(2,1)} %maximum_select_fusion.2), channel_id=1, source_target_pairs={{0,4},{4,0},{1,5},{5,1},{2,6},{6,2},{3,7},{7,3},{8,12},{12,8},{9,1... | collective-permute-start | bytes 3145736 | tf_op jit(solution)/shard_map/ppermute | solution.py:290
  60.8 1.2 copy-start.8
  60.8 1.2 copy-start.9
  60.8 1.2 copy-start.10
  63.1 1.6 copy-start.4
  64.7 9.0 %copy-start.15 = (s32[128]{0:T(128)S(1)}, s32[128]{0:T(128)}, u32[]{:S(2)}) copy-start(s32[128]{0:T(128)} %param.23) | copy-start | bytes 1540
  64.7 12.0 %copy-start.11 = (bf16[128,256]{1,0:T(8,128)(2,1)S(1)}, bf16[128,256]{1,0:T(8,128)(2,1)}, u32[]{:S(2)}) copy-start(bf16[128,256]{1,0:T(8,128)(2,1)} %param.21) | copy-start | bytes 196612
  64.7 12.0 %copy-start.12 = (bf16[128,256]{1,0:T(8,128)(2,1)S(1)}, bf16[128,256]{1,0:T(8,128)(2,1)}, u32[]{:S(2)}) copy-start(bf16[128,256]{1,0:T(8,128)(2,1)} %param.22) | copy-start | bytes 196612
  64.7 76.9 %copy-start.2 = (bf16[128,4096]{1,0:T(8,128)(2,1)S(1)}, bf16[128,4096]{1,0:T(8,128)(2,1)}, u32[]{:S(2)}) copy-start(bf16[128,4096]{1,0:T(8,128)(2,1)} %q_ref.3) | copy-start | bytes 3145732
  64.7 89.9 %all-to-all-start = ((bf16[8,48,4096]{2,1,0:T(8,128)(2,1)}), bf16[8,48,4096]{2,1,0:T(8,128)(2,1)}, u32[]{:S(2)}, u32[]{:S(2)}) async-start(bf16[8,48,4096]{2,1,0:T(8,128)(2,1)} %bitcast.16), calls=%async_computation | async-start | bytes 6291456 | tf_op jit(solution)/shard_map/all_to_all | solution.py:339
  71.3 72.7 %collective-permute-start = (bf16[2048,384]{1,0:T(8,128)(2,1)}, bf16[2048,384]{1,0:T(8,128)(2,1)}, u32[]{:S(2)}, u32[]{:S(2)}) collective-permute-start(bf16[2048,384]{1,0:T(8,128)(2,1)} %refs_0_.1), channel_id=1, source_target_pairs={{0,1},{1,0},{2,3},{3,2},{4,5},{5,4},{6,7},{7,6},{8,9},{9,8},{10,11... | collective-permute-start | bytes 4718600 | tf_op jit(solution)/shard_map/ppermute | solution.py:341
  73.2 70.8 %collective-permute-start.1 = (bf16[2048,384]{1,0:T(8,128)(2,1)}, bf16[2048,384]{1,0:T(8,128)(2,1)}, u32[]{:S(2)}, u32[]{:S(2)}) collective-permute-start(bf16[2048,384]{1,0:T(8,128)(2,1)} %refs_1_.1), channel_id=1, source_target_pairs={{0,1},{1,0},{2,3},{3,2},{4,5},{5,4},{6,7},{7,6},{8,9},{9,8},{10,11... | collective-permute-start | bytes 4718600 | tf_op jit(solution)/shard_map/ppermute | solution.py:341
  73.2 70.8 %collective-permute-start.2 = (bf16[384,2048]{1,0:T(8,128)(2,1)}, bf16[384,2048]{1,0:T(8,128)(2,1)}, u32[]{:S(2)}, u32[]{:S(2)}) collective-permute-start(bf16[384,2048]{1,0:T(8,128)(2,1)} %refs_2_.1), channel_id=1, source_target_pairs={{0,1},{1,0},{2,3},{3,2},{4,5},{5,4},{6,7},{7,6},{8,9},{9,8},{10,11... | collective-permute-start | bytes 4718600 | tf_op jit(solution)/shard_map/ppermute | solution.py:341
  73.8 65.8 %collective-permute-start.4 = (s32[128]{0:T(128)S(1)}, s32[128]{0:T(128)S(1)}, u32[]{:S(2)}, u32[]{:S(2)}) collective-permute-start(s32[128]{0:T(128)S(1)} %copy-done.15), channel_id=1, source_target_pairs={{0,1},{1,2},{2,3},{3,4},{4,5},{5,6},{6,7},{7,8},{8,9},{9,10},{10,1... | collective-permute-start | bytes 1544 | tf_op jit(solution)/shard_map/ppermute | solution.py:345
  76.8 64.3 %collective-permute-start.3 = (bf16[128,512]{1,0:T(8,128)(2,1)S(1)}, bf16[128,512]{1,0:T(8,128)(2,1)S(1)}, u32[]{:S(2)}, u32[]{:S(2)}) collective-permute-start(bf16[128,512]{1,0:T(8,128)(2,1)S(1)} %pad_maximum_fusion), channel_id=1, source_target_pairs={{0,1},{1,2},{2,3},{3,4},{4,5},{5,6},{6,7},{7,8},{8,9},{9,10},{10,1... | collective-permute-start | bytes 393224 | tf_op jit(solution)/shard_map/ppermute | solution.py:345
  168.9 4.4 %copy-start.13 = (bf16[128,256]{1,0:T(8,128)(2,1)S(1)}, bf16[128,256]{1,0:T(8,128)(2,1)}, u32[]{:S(2)}) copy-start(bf16[128,256]{1,0:T(8,128)(2,1)} %param.22) | copy-start | bytes 196612
  168.9 4.4 %copy-start.14 = (bf16[128,256]{1,0:T(8,128)(2,1)S(1)}, bf16[128,256]{1,0:T(8,128)(2,1)}, u32[]{:S(2)}) copy-start(bf16[128,256]{1,0:T(8,128)(2,1)} %get-tuple-element.34) | copy-start | bytes 196612
  168.9 38.2 %all-to-all-start.1 = ((bf16[8,48,2048]{2,1,0:T(8,128)(2,1)}), bf16[8,48,2048]{2,1,0:T(8,128)(2,1)}, u32[]{:S(2)}, u32[]{:S(2)}) async-start(bf16[8,48,2048]{2,1,0:T(8,128)(2,1)} %bitcast.17), calls=%async_computation.1 | async-start | bytes 3145728 | tf_op jit(solution)/shard_map/all_to_all | solution.py:356
  207.2 1.2 copy-start.3
  209.4 24.4 %copy-start.1 = (bf16[128,4096]{1,0:T(8,128)(2,1)S(1)}, bf16[128,4096]{1,0:T(8,128)(2,1)}, u32[]{:S(2)}) copy-start(bf16[128,4096]{1,0:T(8,128)(2,1)} %param.19) | copy-start | bytes 3145732
  225.9 7.2 %collective-permute-start.7 = (bf16[128,512]{1,0:T(8,128)(2,1)S(1)}, bf16[128,512]{1,0:T(8,128)(2,1)S(1)}, u32[]{:S(2)}, u32[]{:S(2)}) collective-permute-start(bf16[128,512]{1,0:T(8,128)(2,1)S(1)} %pad_maximum_fusion.3), channel_id=1, source_target_pairs={{1,0},{2,1},{3,2},{4,3},{5,4},{6,5},{7,6},{8,7},{9,8},{10,9},{11,1... | collective-permute-start | bytes 393224 | tf_op jit(solution)/shard_map/ppermute | solution.py:362
  (3 other events, 3.2 us)
Sparse Core Ops, SparseCore 0:
  60.9 141.8 all-gather.1

commit v3 on v2

v3 whole, which is shorter than its diff:
```python
import functools

import jax
import jax.numpy as jnp
from jax import lax
from jax.experimental import pallas as pl
from jax.experimental.pallas import tpu as pltpu
from jax.sharding import PartitionSpec as P

KVH = 2
GROUP = 16
HD = 128
FLOOR = -1e30
MIB = 1 << 20

NT = (((1,), (1,)), ((), ()))
TN = (((0,), (0,)), ((), ()))


def dot(a, b, dims=(((1,), (0,)), ((), ()))):
    return lax.dot_general(a, b, dims, preferred_element_type=jnp.float32)


def params(mib):
    return pltpu.CompilerParams(vmem_limit_bytes=mib * MIB)


def pick_kernel(owners, depth, routes_ref, weight_ref, input_ref, grad_ref, rows_ref, back_ref, place, scale):
    tokens = input_ref.shape[0]
    slots = owners * depth
    step = pl.program_id(0)
    half = pl.num_programs(0) // 2

    @pl.when(step == 0)
    def _():
        first = routes_ref[0:1, :]
        second = routes_ref[1:2, :]
        expert = lax.broadcasted_iota(jnp.int32, (owners, tokens), 0)
        is_first = first == expert
        is_second = second == expert
        member = jnp.where(is_first | is_second, 1.0, 0.0)
        before = lax.broadcasted_iota(jnp.int32, (tokens, tokens), 0) < lax.broadcasted_iota(
            jnp.int32, (tokens, tokens), 1
        )
        rank = dot(member.astype(jnp.bfloat16), jnp.where(before, 1.0, 0.0).astype(jnp.bfloat16))
        spot = (expert * depth).astype(jnp.float32) + rank
        slot_first = jnp.sum(jnp.where(is_first, spot, 0.0), axis=0, keepdims=True).astype(jnp.int32)
        slot_second = jnp.sum(jnp.where(is_second, spot, 0.0), axis=0, keepdims=True).astype(jnp.int32)
        slot = lax.broadcasted_iota(jnp.int32, (slots, tokens), 0)
        at_first = slot == slot_first
        at_second = slot == slot_second
        chosen = jnp.where(at_first | at_second, 1.0, 0.0).astype(jnp.bfloat16)
        place[...] = chosen
        back_ref[...] = chosen.T
        scale[...] = jnp.sum(
            jnp.where(at_first, weight_ref[0:1, :], 0.0) + jnp.where(at_second, weight_ref[1:2, :], 0.0),
            axis=1,
            keepdims=True,
        )

    @pl.when(step < half)
    def _():
        rows_ref[...] = dot(place[...], input_ref[...]).astype(jnp.bfloat16)

    @pl.when(step >= half)
    def _():
        rows_ref[...] = (scale[...] * dot(place[...], grad_ref[...])).astype(jnp.bfloat16)


def pick(routes, route_weight, moe_input, moe_grad, owners, depth):
    tokens, width = moe_input.shape
    slots = owners * depth
    tile = 1024
    half = width // tile
    return pl.pallas_call(
        functools.partial(pick_kernel, owners, depth),
        grid=(2 * half,),
        in_specs=[
            pl.BlockSpec((2, tokens), lambda i: (0, 0)),
            pl.BlockSpec((2, tokens), lambda i: (0, 0)),
            pl.BlockSpec((tokens, tile), lambda i: (0, jnp.minimum(i, half - 1))),
            pl.BlockSpec((tokens, tile), lambda i: (0, jnp.maximum(i - half, 0))),
        ],
        out_specs=[
            pl.BlockSpec((slots, tile), lambda i: (0, i)),
            pl.BlockSpec((tokens, slots), lambda i: (0, 0)),
        ],
        out_shape=(
            jax.ShapeDtypeStruct((slots, 2 * width), jnp.bfloat16),
            jax.ShapeDtypeStruct((tokens, slots), jnp.bfloat16),
        ),
        scratch_shapes=[pltpu.VMEM((slots, tokens), jnp.bfloat16), pltpu.VMEM((slots, 1), jnp.float32)],
        compiler_params=params(60),
        cost_estimate=pl.CostEstimate(
            flops=4 * slots * tokens * width, bytes_accessed=8 * MIB, transcendentals=0
        ),
        name="pick_rows",
    )(routes.T, route_weight.T, moe_input, moe_grad)


def weights_kernel(*refs):
    own, other, (cols_ref, down_ref, rows_ref) = refs[:3], refs[3:6], refs[6:]
    tile = own[0].shape[1]
    for place, (gate_ref, up_ref, low_ref) in enumerate((own, other)):
        for kind, ref in enumerate((gate_ref, up_ref)):
            spot = slice((2 * kind + place) * tile, (2 * kind + place + 1) * tile)
            cols_ref[0, :, spot] = ref[...]
            rows_ref[0, spot, :] = ref[...].T
        down_ref[0, :, place * tile : (place + 1) * tile] = low_ref[...].T


def prepare_weights(own, other):
    width, half = own[0].shape
    tile = 128
    steps = half // tile
    cols = pl.BlockSpec((width, tile), lambda i: (0, i))
    down = pl.BlockSpec((tile, width), lambda i: (i, 0))
    return pl.pallas_call(
        weights_kernel,
        grid=(steps,),
        in_specs=[cols, cols, down] * 2,
        out_specs=[
            pl.BlockSpec((1, width, 4 * tile), lambda i: (i, 0, 0)),
            pl.BlockSpec((1, width, 2 * tile), lambda i: (i, 0, 0)),
            pl.BlockSpec((1, 4 * tile, width), lambda i: (i, 0, 0)),
        ],
        out_shape=(
            jax.ShapeDtypeStruct((steps, width, 4 * tile), jnp.bfloat16),
            jax.ShapeDtypeStruct((steps, width, 2 * tile), jnp.bfloat16),
            jax.ShapeDtypeStruct((steps, 4 * tile, width), jnp.bfloat16),
        ),
        compiler_params=params(48),
        cost_estimate=pl.CostEstimate(
            flops=0, bytes_accessed=32 * width * half, transcendentals=0
        ),
        name="prepare_weights",
    )(*own, *other)


def expert_kernel(steps, rows_ref, cols_ref, down_ref, back_ref, out_ref, hidden):
    step = pl.program_id(0)
    width = rows_ref.shape[1] // 2
    pair = down_ref.shape[2]

    @pl.when(step < steps)
    def _():
        both_pre = dot(rows_ref[:, :width], cols_ref[0])
        gate_pre = both_pre[:, :pair]
        up_pre = both_pre[:, pair:]
        down_grad = dot(rows_ref[:, width:], down_ref[0])
        sig = jax.nn.sigmoid(gate_pre)
        hidden[step, :, :pair] = (
            down_grad * up_pre * sig * (1.0 + gate_pre * (1.0 - sig))
        ).astype(jnp.bfloat16)
        hidden[step, :, pair:] = (down_grad * gate_pre * sig).astype(jnp.bfloat16)

    @pl.when(step >= steps)
    def _():
        total = dot(hidden[0], back_ref[0])
        for i in range(1, steps):
            total += dot(hidden[i], back_ref[i])
        out_ref[...] = total.astype(jnp.bfloat16)


def experts(rows, cols, down, back):
    count, twice = rows.shape
    steps, width, quad = cols.shape
    tile = 512
    last = steps - 1
    turn = lambda i: jnp.maximum(i - steps, 0)
    return pl.pallas_call(
        functools.partial(expert_kernel, steps),
        grid=(steps + width // tile,),
        in_specs=[
            pl.BlockSpec((count, twice), lambda i: (0, 0)),
            pl.BlockSpec((1, width, quad), lambda i: (jnp.minimum(i, last), 0, 0)),
            pl.BlockSpec((1, width, quad // 2), lambda i: (jnp.minimum(i, last), 0, 0)),
            pl.BlockSpec((steps, quad, tile), lambda i: (0, 0, turn(i))),
        ],
        out_specs=pl.BlockSpec((count, tile), lambda i: (0, turn(i))),
        out_shape=jax.ShapeDtypeStruct((count, width), jnp.bfloat16),
        scratch_shapes=[pltpu.VMEM((steps, count, quad), jnp.bfloat16)],
        compiler_params=params(48),
        cost_estimate=pl.CostEstimate(
            flops=5 * count * width * steps * quad, bytes_accessed=20 * MIB,
            transcendentals=count * steps * quad,
        ),
        name="expert_terms",
    )(rows, cols, down, back)


def shares_kernel(
    q_ref, key_ref, value_ref, prev_key_ref, prev_value_ref, prev_seg_ref, seg_row_ref, seg_col_ref,
    low_ref, turned_ref, query_ref, key_out, value_out,
):
    tokens = q_ref.shape[0]
    seg_col = seg_col_ref[...]
    row = lax.broadcasted_iota(jnp.int32, (tokens, tokens), 0)
    col = lax.broadcasted_iota(jnp.int32, (tokens, tokens), 1)
    own_seen = jnp.where((col <= row) & (seg_row_ref[...] == seg_col), 1.0, 0.0)
    prev_seg = prev_seg_ref[tokens : tokens + 16, :].astype(jnp.float32)[0:1, :]
    prev_seen = jnp.where(prev_seg == seg_col, 1.0, 0.0)
    seen = jnp.concatenate([prev_seen, own_seen], axis=1) > 0.5
    keys = jnp.concatenate([prev_key_ref[:tokens, :], key_ref[...]], axis=0)
    values = jnp.concatenate([prev_value_ref[:tokens, :], value_ref[...]], axis=0)
    key_out[0] = keys
    value_out[0] = values.T
    for head in range(GROUP):
        rows = slice(head * tokens, (head + 1) * tokens)
        query = q_ref[:, head * HD : (head + 1) * HD]
        scores = dot(query, keys, NT) * (HD**-0.5)
        masked = jnp.where(seen, scores, FLOOR)
        raised = jnp.where(seen, jnp.exp(masked - jnp.max(masked, axis=1, keepdims=True)), 0.0)
        shares = raised / jnp.sum(raised, axis=1, keepdims=True)
        low = shares.astype(jnp.bfloat16)
        low_ref[0, rows, :] = low
        turned_ref[0, :, rows] = low.T
        query_ref[0, rows, :] = query


def attention_shares(queries, key_heads, value_heads, prev, segs):
    tokens, width = queries.shape
    span = 2 * tokens
    stack = GROUP * tokens
    high = prev.shape[0]
    own = pl.BlockSpec((tokens, HD), lambda g: (0, g))
    group = lambda shape: pl.BlockSpec((1,) + shape, lambda g: (g, 0, 0))
    made = lambda shape: jax.ShapeDtypeStruct((KVH,) + shape, jnp.bfloat16)
    shapes = ((stack, span), (span, stack), (stack, HD), (span, HD), (HD, span))
    return pl.pallas_call(
        shares_kernel,
        grid=(KVH,),
        in_specs=[
            pl.BlockSpec((tokens, GROUP * HD), lambda g: (0, g)),
            own,
            own,
            pl.BlockSpec((high, HD), lambda g: (0, g)),
            pl.BlockSpec((high, HD), lambda g: (0, KVH + g)),
            pl.BlockSpec((high, HD), lambda g: (0, 0)),
            pl.BlockSpec((1, tokens), lambda g: (0, 0)),
            pl.BlockSpec((tokens, 1), lambda g: (0, 0)),
        ],
        out_specs=[group(shape) for shape in shapes],
        out_shape=[made(shape) for shape in shapes],
        compiler_params=params(32),
        cost_estimate=pl.CostEstimate(
            flops=2 * tokens * width * span, bytes_accessed=8 * MIB,
            transcendentals=tokens * span * KVH * GROUP,
        ),
        name="attention_shares",
    )(queries, key_heads, value_heads, prev, prev, prev, segs[None, :], segs[:, None])


def tail_kernel(plan, *refs):
    order, first, last, heads, tiles = plan
    refs = list(refs)
    take = lambda n: [refs.pop(0) for _ in range(n)]
    step = pl.program_id(0)
    if first:
        back_ref, place_ref, grad_ref = take(3)
    else:
        stream_in, sums_in, _ = take(3)
    w_ref, low_ref, turned_ref, q_ref, key_ref, value_ref = take(6)
    if first:
        moe_ref, stream = take(2)
    else:
        stream = stream_in
    (query_out,) = take(1)
    if last:
        key_out, value_out, sent_out = take(3)
    else:
        (sums_out,) = take(1)
    held, sums = take(2)
    tokens = query_out.shape[0]

    @pl.when(step == 0)
    def _():
        if first:
            moe = dot(place_ref[...], back_ref[...]).astype(jnp.bfloat16)
            moe_ref[...] = moe
            added = (grad_ref[...].astype(jnp.float32) + moe.astype(jnp.float32)).astype(jnp.bfloat16)
            size = added.shape[1] // len(order)
            for to, source in enumerate(order):
                stream[:, to * size : (to + 1) * size] = added[:, source * size : (source + 1) * size]
        held[...] = jnp.zeros_like(held)

    @pl.when((step == 0) | ((step > 1) & ((step - 1) % tiles == 0)))
    def _():
        if first:
            sums[...] = jnp.zeros_like(sums)
        else:
            sums[...] = sums_in[...]

    grads = held[...]
    head_grad = dot(stream[...], w_ref[0]).astype(jnp.bfloat16)
    low = low_ref[0].astype(jnp.float32)
    prob_grad = dot(grads, value_ref[0])
    row_dot = jnp.sum(low * prob_grad, axis=1, keepdims=True)
    score_grad = (low * (prob_grad - row_dot) * (HD**-0.5)).astype(jnp.bfloat16)
    query_grad = dot(score_grad, key_ref[0]).astype(jnp.bfloat16)
    sums[0] += dot(score_grad, q_ref[0], TN)
    sums[1] += dot(turned_ref[0], grads)
    for head in range(heads):
        cols = slice(head * HD, (head + 1) * HD)
        rows = slice(head * tokens, (head + 1) * tokens)
        query_out[:, cols] = query_grad[rows, :]
        held[rows, :] = head_grad[:, cols]

    @pl.when((step > 0) & (step % tiles == 0))
    def _():
        if last:
            key_out[...] = sums[0, tokens:, :]
            value_out[...] = sums[1, tokens:, :]
            sent_out[...] = sums[:, :tokens, :].astype(jnp.bfloat16)
        else:
            sums_out[...] = sums[...]


def tail(chunk, chunks, order, carried, w_part, low, turned, query, keys, values):
    first, last = chunk == 0, chunk == chunks - 1
    width, cols = w_part.shape[1:]
    span = keys.shape[1]
    tokens = span // 2
    heads = 4
    tile = heads * HD
    tiles = cols // tile
    steps = KVH * tiles
    per_group = tiles * chunks
    now = lambda i: jnp.minimum(i, steps - 1)
    was = lambda i: jnp.maximum(i - 1, 0)
    spot = lambda i: chunk * tiles + was(i) % tiles
    whole = lambda shape: pl.BlockSpec(shape, lambda i: (0,) * len(shape))
    group = lambda shape: pl.BlockSpec((1,) + shape, lambda i: (was(i) // tiles, 0, 0))
    rows = lambda shape: pl.BlockSpec((1,) + shape, lambda i: (was(i) // tiles, spot(i), 0))
    sums = pl.BlockSpec((2, span, HD), lambda i: (0, 0, was(i) // tiles))
    if first:
        in_specs = [whole(array.shape) for array in carried]
        out_specs = [whole((tokens, width)), whole((tokens, width))]
        out_shape = [jax.ShapeDtypeStruct((tokens, width), jnp.bfloat16)] * 2
    else:
        in_specs = [whole((tokens, width)), sums, pl.BlockSpec(memory_space=pl.ANY)]
        out_specs, out_shape = [], []
    in_specs += [
        pl.BlockSpec((1, width, tile), lambda i: (now(i) // tiles, 0, now(i) % tiles)),
        rows((heads * tokens, span)),
        pl.BlockSpec((1, span, heads * tokens), lambda i: (was(i) // tiles, 0, spot(i))),
        rows((heads * tokens, HD)),
        group((span, HD)),
        group((HD, span)),
    ]
    out_specs.append(
        pl.BlockSpec((tokens, tile), lambda i: (0, (was(i) // tiles) * per_group + spot(i)))
    )
    out_shape.append(jax.ShapeDtypeStruct((tokens, KVH * chunks * cols), jnp.bfloat16))
    if last:
        half = pl.BlockSpec((tokens, HD), lambda i: (0, was(i) // tiles))
        out_specs += [half, half, pl.BlockSpec((2, tokens, HD), lambda i: (0, 0, was(i) // tiles))]
        out_shape += [jax.ShapeDtypeStruct((tokens, KVH * HD), jnp.float32)] * 2
        out_shape.append(jax.ShapeDtypeStruct((2, tokens, KVH * HD), jnp.bfloat16))
    else:
        out_specs.append(sums)
        out_shape.append(jax.ShapeDtypeStruct((2, span, KVH * HD), jnp.float32))
    return pl.pallas_call(
        functools.partial(tail_kernel, (order, first, last, heads, tiles)),
        grid=(steps + 1,),
        in_specs=in_specs,
        out_specs=out_specs,
        out_shape=out_shape,
        scratch_shapes=[
            pltpu.VMEM((heads * tokens, HD), jnp.bfloat16),
            pltpu.VMEM((2, span, HD), jnp.float32),
        ],
        input_output_aliases={} if first else {2: 0},
        compiler_params=params(60),
        cost_estimate=pl.CostEstimate(
            flops=2 * tokens * width * KVH * cols, bytes_accessed=22 * MIB // chunks, transcendentals=0
        ),
        name="tail_attention",
    )(*carried, w_part, low, turned, query, keys, values)


def far_first(share):
    for axis in ("far", "near"):
        moved = lax.ppermute(share, axis, [(0, 1), (1, 0)])
        mine = lax.axis_index(axis) == 0
        share = jnp.where(mine, jnp.stack([share, moved]), jnp.stack([moved, share]))
    return share


def local(
    moe_input,
    moe_grad,
    routes,
    route_weight,
    w_gate,
    w_up,
    w_down,
    w_out,
    queries,
    key_heads,
    value_heads,
    segments,
):
    chips = ("far", "near", "low")
    blk = chips + ("core",)
    low = lax.axis_size("low")
    owners = 4 * low
    count = 2 * owners
    parts = lax.axis_size("groups")
    tokens, width = moe_input.shape
    depth = 2 * max(1, 3 * tokens * routes.shape[1] // (2 * count))
    onward = [(i, i + 1) for i in range(count - 1)]
    backward = [(i + 1, i) for i in range(count - 1)]

    kv = jnp.concatenate([key_heads, value_heads], axis=1)
    segs = (segments + 1).astype(jnp.float32)
    seg_rows = jnp.zeros((16, kv.shape[1]), jnp.bfloat16).at[0, :tokens].set(segs.astype(jnp.bfloat16))
    prev = lax.ppermute(jnp.concatenate([kv, seg_rows], axis=0), blk, onward)
    rows, place = pick(routes, route_weight, moe_input, moe_grad, owners, depth)
    rows, prev, w_out = lax.optimization_barrier((rows, prev, w_out))
    rows_in = lax.all_to_all(rows.reshape(owners, depth, 2 * width), chips, 0, 0, tiled=True)

    chunks = 2
    block = w_out.shape[0]
    share_cols = w_out.shape[1] // parts
    cols = share_cols // chunks
    order = tuple(
        (2 * far + near) * 2 * low + rest
        for rest in range(2 * low)
        for near in range(2)
        for far in range(2)
    )
    w_parts = []
    for chunk in range(chunks):
        start = lax.axis_index("groups") * share_cols + chunk * cols
        w_plane = far_first(lax.dynamic_slice_in_dim(w_out, start, cols, 1))
        w_part = lax.all_gather(w_plane, ("groups", "low", "core"), axis=0, tiled=False)
        w_part = w_part.reshape(parts, 2 * low, 2, 2, block, cols)
        if block % 128:
            w_part = w_part.transpose(0, 3, 2, 1, 4, 5)
        w_parts.append(w_part.reshape(parts, width, cols))
    if block % 128:
        order = (0,)

    own = (w_gate, w_up, w_down)
    other = tuple(lax.ppermute(w, "core", [(0, 1), (1, 0)]) for w in own)
    prepared = prepare_weights(own, other)
    attention = attention_shares(queries, key_heads, value_heads, prev, segs)

    prepared, attention, rows_in = lax.optimization_barrier((prepared, attention, rows_in))
    terms = experts(rows_in.reshape(owners * depth, 2 * width), *prepared)
    back = lax.all_to_all(terms.reshape(owners, depth, width), chips, 0, 0, tiled=True)

    carried = (back.reshape(owners * depth, width), place, moe_grad)
    for chunk in range(chunks):
        outs = tail(chunk, chunks, order, carried, w_parts[chunk], *attention)
        if chunk == 0:
            moe_input_grad, stream = outs[:2]
            outs = outs[2:]
        carried = (stream, outs[1], outs[0])
    query_grad, key_part, value_part, sent = outs
    later = lax.ppermute(sent, blk, backward).astype(jnp.float32)
    return (moe_input_grad, query_grad, key_part + later[0], value_part + later[1])


def solution(mesh):
    names = ("groups", "far", "near", "low", "core")
    shape = (mesh.shape["groups"], 2, 2, mesh.shape["blk"] // 8, 2)
    fine = jax.sharding.Mesh(mesh.devices.reshape(shape), names)
    blk = names[1:]
    by_tokens = P(names, None)
    return jax.shard_map(
        local,
        mesh=fine,
        in_specs=(
            by_tokens,
            by_tokens,
            by_tokens,
            by_tokens,
            P(None, blk),
            P(None, blk),
            P(blk, None),
            P(blk, None),
            by_tokens,
            by_tokens,
            by_tokens,
            P(names),
        ),
        out_specs=(by_tokens,) * 4,
        check_vma=False,
    )
```

time: 244 us -> 241 us (0.988)
  waiting for transfers between devices: 147 us -> 93.1 us
  blocking collectives: 0 us -> 40.2 us
  Pallas kernels: 43.6 us -> 49.3 us
    ppermute x2 -> x1, waiting for transfers between devices: 61.7 us -> 0.01 us  [local(): prev = lax.ppermute(jnp.concatenate([kv, seg_rows], axis=0), blk, onward)]
    all_to_all x1, waiting for transfers between devices: 0.01 us -> 44.2 us  [local(): lax.all_to_all(rows.reshape(owners, depth, 2 * width), chips, 0, 0, tiled...]
    all_to_all x0 -> x1, blocking collectives: none -> 40.2 us  [local(): lax.all_to_all(terms.reshape(owners, depth, width), chips, 0, 0, tiled=True)]
    all_to_all x1 -> x0, waiting for transfers between devices: 33.8 us -> none  [local(): lax.all_to_all(terms.reshape(owners, depth, width), chips, 0, 0, tiled=True)]
    pallas_call x2 -> x3, Pallas kernels: 17.6 us -> 25.2 us  [the longest x2 20.1 us: tail(): pl.pallas_call(functools.partial(tail_kernel, (order, first, last, heads,...]
    ppermute x2 -> x4, starting transfers between devices: 2.42 us -> 9.65 us  [far_first(): moved = lax.ppermute(share, axis, [(0, 1), (1, 0)])]
    all_to_all x1 -> x0, starting transfers between devices: 4.37 us -> none  [local(): lax.all_to_all(terms.reshape(owners, depth, width), chips, 0, 0, tiled=True)]
    ppermute x2 -> x4, waiting for transfers between devices: 46.9 us -> 44.5 us  [far_first(): moved = lax.ppermute(share, axis, [(0, 1), (1, 0)])]
  transfers between devices with their start and end apart: 11 -> 12, of which waited for: 6 -> 6; matrix products, arithmetic and copies ran while one was open for 0% -> 1% of each run, Pallas kernels for 11% -> 17%
where the time goes in v3:
time: 241 us; the launch traced here: 238 us
  waiting for transfers between devices  93.1 us (39%)
  Pallas kernels  49.3 us (20%)
  blocking collectives  40.2 us (17%)
  starting transfers between devices  25.7 us (11%)
  between operations  14.2 us (6%)
  local copies, waits for them, and re-layouts  9.25 us (4%)
  other arithmetic  5.91 us (2%)
    ppermute x4, waiting for transfers between devices, far_first(): moved = lax.ppermute(share, axis, [(0, 1), (1, 0)])  44.5 us
    all_to_all x1, waiting for transfers between devices, local(): lax.all_to_all(rows.reshape(owners, depth, 2 * width), chips, 0, 0, tiled...  44.2 us
    all_to_all x1, blocking collectives, local(): lax.all_to_all(terms.reshape(owners, depth, width), chips, 0, 0, tiled=True)  40.2 us
    pallas_call x2, Pallas kernels, tail(): pl.pallas_call(functools.partial(tail_kernel, (order, first, last, heads,...  20.1 us
    pallas_call x1, Pallas kernels, experts(): pl.pallas_call(functools.partial(expert_kernel, steps), grid=(steps + wid...  11.8 us
    ppermute x4, starting transfers between devices, far_first(): moved = lax.ppermute(share, axis, [(0, 1), (1, 0)])  9.65 us
    unnamed x24, local copies, waits for them, and re-layouts  9.1 us
    pallas_call x1, Pallas kernels, prepare_weights(): pl.pallas_call(weights_kernel, grid=(steps,), in_specs=[cols, cols, down]...  8.75 us
  transfers between devices with their start and end apart: 12, of which 6 were waited for; matrix products, arithmetic and copies ran while one was open for 1% of the time, Pallas kernels for 17%

profile of v3, /device:TPU:13, one launch (start us, length us, event | category | flops | bytes accessed | tf_op | source)
XLA Modules:
  0.0 237.7 jit_solution(14378271926227758602)
XLA Ops:
  8.8 3.7 %collective-permute-start.3 = (bf16[144,512]{1,0:T(8,128)(2,1)S(1)}, bf16[144,512]{1,0:T(8,128)(2,1)S(1)}, u32[]{:S(2)}, u32[]{:S(2)}) collective-permute-start(bf16[144,512]{1,0:T(8,128)(2,1)S(1)} %fusion.3), channel_id=1, source_target_pairs={{0,1},{1,2},{2,3},{3,4},{4,5},{5,6},{6,7},{7,8},{8,9},{9,10},{10,1... | collective-permute-start | bytes 442376 | tf_op jit(solution)/shard_map/ppermute | solution.py:418
  12.6 5.1 %pick_rows.1 = (bf16[384,4096]{1,0:T(8,128)(2,1)}, bf16[128,384]{1,0:T(8,128)(2,1)}) custom-call(s32[2,128]{1,0:T(2,128)} %bitcast.52, f32[2,128]{1,0:T(2,128)} %bitcast.53, bf16[128,2048]{1,0:T(8,128)(2,1)} %input_ref.1, bf16[128,2048]{1,0:T(8,128)(2,1)} %refs_2_.3), custom_call_target="tpu_custom_call" | custom-call | flops 402653184 | bytes 8388608 | tf_op jit(solution)/shard_map/pick_rows/pallas_call | solution.py:75
  17.8 10.0 %collective-permute-done.4 = bf16[128,1024]{1,0:T(8,128)(2,1)S(1)} collective-permute-done((bf16[128,1024]{1,0:T(8,128)(2,1)S(1)}, bf16[128,1024]{1,0:T(8,128)(2,1)S(1)}, u32[]{:S(2)}, u32[]{:S(2)}) %collective-permute-start.4) | collective-permute-done | bytes 262176 | tf_op jit(solution)/shard_map/ppermute | solution.py:384
  27.9 4.1 %collective-permute-start.5 = (bf16[2,128,1024]{2,1,0:T(8,128)(2,1)S(1)}, bf16[2,128,1024]{2,1,0:T(8,128)(2,1)S(1)}, u32[]{:S(2)}, u32[]{:S(2)}) collective-permute-start(bf16[2,128,1024]{2,1,0:T(8,128)(2,1)S(1)} %maximum_select_fusion.3), channel_id=1, source_target_pairs={{0,4},{4,0},{1,5},{5,1},{2,6},{6,2},{3,7},{7,3},{8,12},{12,8},{9,1... | collective-permute-start | bytes 1572872 | tf_op jit(solution)/shard_map/ppermute | solution.py:384
  32.1 12.1 %collective-permute-done.5 = bf16[2,128,1024]{2,1,0:T(8,128)(2,1)S(1)} collective-permute-done((bf16[2,128,1024]{2,1,0:T(8,128)(2,1)S(1)}, bf16[2,128,1024]{2,1,0:T(8,128)(2,1)S(1)}, u32[]{:S(2)}, u32[]{:S(2)}) %collective-permute-start.5) | collective-permute-done | bytes 524320 | tf_op jit(solution)/shard_map/ppermute | solution.py:384
  45.5 10.6 %collective-permute-done.6 = bf16[128,1024]{1,0:T(8,128)(2,1)S(1)} collective-permute-done((bf16[128,1024]{1,0:T(8,128)(2,1)S(1)}, bf16[128,1024]{1,0:T(8,128)(2,1)S(1)}, u32[]{:S(2)}, u32[]{:S(2)}) %collective-permute-start.6) | collective-permute-done | bytes 262176 | tf_op jit(solution)/shard_map/ppermute | solution.py:384
  56.2 5.4 %collective-permute-start.7 = (bf16[2,128,1024]{2,1,0:T(8,128)(2,1)S(1)}, bf16[2,128,1024]{2,1,0:T(8,128)(2,1)S(1)}, u32[]{:S(2)}, u32[]{:S(2)}) collective-permute-start(bf16[2,128,1024]{2,1,0:T(8,128)(2,1)S(1)} %maximum_select_fusion.5), channel_id=1, source_target_pairs={{0,4},{4,0},{1,5},{5,1},{2,6},{6,2},{3,7},{7,3},{8,12},{12,8},{9,1... | collective-permute-start | bytes 1572872 | tf_op jit(solution)/shard_map/ppermute | solution.py:384
  61.7 11.8 %collective-permute-done.7 = bf16[2,128,1024]{2,1,0:T(8,128)(2,1)S(1)} collective-permute-done((bf16[2,128,1024]{2,1,0:T(8,128)(2,1)S(1)}, bf16[2,128,1024]{2,1,0:T(8,128)(2,1)S(1)}, u32[]{:S(2)}, u32[]{:S(2)}) %collective-permute-start.7) | collective-permute-done | bytes 524320 | tf_op jit(solution)/shard_map/ppermute | solution.py:384
  74.6 5.9 %all-to-all-start = ((bf16[8,48,4096]{2,1,0:T(8,128)(2,1)}), bf16[8,48,4096]{2,1,0:T(8,128)(2,1)S(1)}, u32[]{:S(2)}, u32[]{:S(2)}) async-start(bf16[8,48,4096]{2,1,0:T(8,128)(2,1)} %bitcast.41), calls=%async_computation | async-start | bytes 6291456 | tf_op jit(solution)/shard_map/all_to_all | solution.py:421
  80.5 2.0 collective-permute-start
  83.1 1.4 copy-done.10
  84.5 3.5 %attention_shares.1 = (bf16[2,2048,256]{2,1,0:T(8,128)(2,1)S(1)}, bf16[2,256,2048]{2,1,0:T(8,128)(2,1)S(1)}, bf16[2,2048,128]{2,1,0:T(8,128)(2,1)S(1)}, bf16[2,2...) custom-call(bf16[128,4096]{1,0:T(8,128)(2,1)S(1)} %copy-done.10, bf16[128,256]{1,0:T(8,128)(2,1)S(1)} %copy-done.8, ...), custom_call_target="tpu_custom_call" | custom-call | flops 268435456 | bytes 8388608 | tf_op jit(solution)/shard_map/attention_shares/pallas_call | solution.py:230
  88.0 1.3 copy-done
  93.0 1.4 copy-done.4
  94.4 1.4 copy-done.5
  95.8 8.8 %prepare_weights.1 = (bf16[3,2048,512]{2,1,0:T(8,128)(2,1)}, bf16[3,2048,256]{2,1,0:T(8,128)(2,1)}, bf16[3,512,2048]{2,1,0:T(8,128)(2,1)}) custom-call(bf16[2048,384]{1,0:T(8,128)(2,1)S(1)} %copy-done.3, bf16[2048,384]{1,0:T(8,128)(2,1)S(1)} %copy-done.4, bf16[384,2048]{1,0:T(8,128)(2,1)S(1)} %copy-done.5, bf16[2048,384]{1,0:T(8,128)(2,1)} %collective-permute-done.refs_3_, ...), custom_call_target="tpu_custom_call" | custom-call | bytes 25165824 | tf_op jit(solution)/shard_map/prepare_weights/pallas_call | solution.py:118
  104.5 44.2 %all-to-all-done = bf16[8,48,4096]{2,1,0:T(8,128)(2,1)S(1)} async-done(((bf16[8,48,4096]{2,1,0:T(8,128)(2,1)}), bf16[8,48,4096]{2,1,0:T(8,128)(2,1)S(1)}, u32[]{:S(2)}, u32[]{:S(2)}) %all-to-all-start) | async-done | bytes 3145760 | tf_op jit(solution)/shard_map/all_to_all | solution.py:421
  148.7 11.8 %expert_terms.1 = bf16[384,2048]{1,0:T(8,128)(2,1)S(1)} custom-call(bf16[384,4096]{1,0:T(8,128)(2,1)S(1)} %bitcast.36, bf16[3,2048,512]{2,1,0:T(8,128)(2,1)} %get-tuple-element.58.cols_ref, bf16[3,2048,256]{2,1,0:T(8,128)(2,1)} %get-tuple-element.59.down_ref, bf16[3,512,2048]{2,1,0:T(8,128)(2,1)} %get-tuple-element.60.back_ref), custom_call_target="tpu_custom_call" | custom-call | flops 6039797760 | bytes 20971520 | tf_op jit(solution)/shard_map/expert_terms/pallas_call | solution.py:171
  160.5 40.2 %all_to_all.10 = bf16[8,48,2048]{2,1,0:T(8,128)(2,1)} all-to-all(bf16[8,48,2048]{2,1,0:T(8,128)(2,1)S(1)} %bitcast.37), channel_id=1, replica_groups=mesh['groups'=2,'far'=2,'near'=2,'low'=2,'core'=2] {'far','near','low'}, dimensions={0} | all-to-all | bytes 3145728 | tf_op jit(solution)/shard_map/all_to_all | solution.py:452
  200.7 10.5 %tail_attention.2 = (bf16[128,2048]{1,0:T(8,128)(2,1)}, bf16[128,2048]{1,0:T(8,128)(2,1)}, bf16[128,4096]{1,0:T(8,128)(2,1)}, f32[2,256,256]{2,1,0:T(8,128)}) custom-call(bf16[384,2048]{1,0:T(8,128)(2,1)} %bitcast.40, bf16[128,384]{1,0:T(8,128)(2,1)} %get-tuple-element.61.refs_1_, bf16[128,2048]{1,0:T(8,128)(2,1)} %refs_2_.3, ...), custom_call_target="tpu_custom_call" | custom-call | flops 1073741824 | bytes 11534336 | tf_op jit(solution)/shard_map/tail_attention/pallas_call | solution.py:363
  211.2 9.7 %tail_attention.3 = (bf16[128,4096]{1,0:T(8,128)(2,1)}, f32[128,256]{1,0:T(8,128)}, f32[128,256]{1,0:T(8,128)}, bf16[2,128,256]{2,1,0:T(8,128)(2,1)}) custom-call(bf16[128,2048]{1,0:T(8,128)(2,1)} %get-tuple-element.69.refs_0_, f32[2,256,256]{2,1,0:T(8,128)} %get-tuple-element.70.refs_1_, ...), custom_call_target="tpu_custom_call", output_to_operand_aliasing={{0}: (2, {})} | custom-call | flops 1073741824 | bytes 11534336 | tf_op jit(solution)/shard_map/tail_attention/pallas_call | solution.py:363
  220.8 3.9 %collective-permute-start.8 = (bf16[2,128,256]{2,1,0:T(8,128)(2,1)}, bf16[2,128,256]{2,1,0:T(8,128)(2,1)S(1)}, u32[]{:S(2)}, u32[]{:S(2)}) collective-permute-start(bf16[2,128,256]{2,1,0:T(8,128)(2,1)} %get-tuple-element.74), channel_id=1, source_target_pairs={{1,0},{2,1},{3,2},{4,3},{5,4},{6,5},{7,6},{8,7},{9,8},{10,9},{11,1... | collective-permute-start | bytes 393224 | tf_op jit(solution)/shard_map/ppermute | solution.py:462
  224.8 4.3 %collective-permute-done.8 = bf16[2,128,256]{2,1,0:T(8,128)(2,1)S(1)} collective-permute-done((bf16[2,128,256]{2,1,0:T(8,128)(2,1)}, bf16[2,128,256]{2,1,0:T(8,128)(2,1)S(1)}, u32[]{:S(2)}, u32[]{:S(2)}) %collective-permute-start.8) | collective-permute-done | bytes 131104 | tf_op jit(solution)/shard_map/ppermute | solution.py:462
  229.1 1.7 fusion.4
  (45 shorter events, 8.8 us)
Async XLA Ops:
  7.2 10.5 %copy-start.11 = (bf16[128,4096]{1,0:T(8,128)(2,1)S(1)}, bf16[128,4096]{1,0:T(8,128)(2,1)}, u32[]{:S(2)}) copy-start(bf16[128,4096]{1,0:T(8,128)(2,1)} %param.21) | copy-start | bytes 3145732
  7.2 193.5 %all-gather.3.cloned.1.call-start = ((), (), s32[]{:S(2)}) async-start(), calls=%async_computation.2 | async-start | bytes 9437184 | tf_op jit(solution)/shard_map/all_gather | solution.py:437
  8.8 8.8 %collective-permute-start.3 = (bf16[144,512]{1,0:T(8,128)(2,1)S(1)}, bf16[144,512]{1,0:T(8,128)(2,1)S(1)}, u32[]{:S(2)}, u32[]{:S(2)}) collective-permute-start(bf16[144,512]{1,0:T(8,128)(2,1)S(1)} %fusion.3), channel_id=1, source_target_pairs={{0,1},{1,2},{2,3},{3,4},{4,5},{5,6},{6,7},{7,8},{8,9},{9,10},{10,1... | collective-permute-start | bytes 442376 | tf_op jit(solution)/shard_map/ppermute | solution.py:418
  17.7 10.1 %collective-permute-start.4 = (bf16[128,1024]{1,0:T(8,128)(2,1)S(1)}, bf16[128,1024]{1,0:T(8,128)(2,1)S(1)}, u32[]{:S(2)}, u32[]{:S(2)}) collective-permute-start(bf16[128,1024]{1,0:T(8,128)(2,1)S(1)} %get-tuple-element.77), channel_id=1, source_target_pairs={{0,8},{8,0},{1,9},{9,1},{2,10},{10,2},{3,11},{11,3},{4,12},{12,4},... | collective-permute-start | bytes 786440 | tf_op jit(solution)/shard_map/ppermute | solution.py:384
  27.9 16.3 %collective-permute-start.5 = (bf16[2,128,1024]{2,1,0:T(8,128)(2,1)S(1)}, bf16[2,128,1024]{2,1,0:T(8,128)(2,1)S(1)}, u32[]{:S(2)}, u32[]{:S(2)}) collective-permute-start(bf16[2,128,1024]{2,1,0:T(8,128)(2,1)S(1)} %maximum_select_fusion.3), channel_id=1, source_target_pairs={{0,4},{4,0},{1,5},{5,1},{2,6},{6,2},{3,7},{7,3},{8,12},{12,8},{9,1... | collective-permute-start | bytes 1572872 | tf_op jit(solution)/shard_map/ppermute | solution.py:384
  45.4 165.8 %all-gather.5.cloned.1.call-start = ((), (), s32[]{:S(2)}) async-start(), calls=%async_computation.3 | async-start | bytes 9437184 | tf_op jit(solution)/shard_map/all_gather | solution.py:437
  45.4 10.7 %collective-permute-start.6 = (bf16[128,1024]{1,0:T(8,128)(2,1)S(1)}, bf16[128,1024]{1,0:T(8,128)(2,1)S(1)}, u32[]{:S(2)}, u32[]{:S(2)}) collective-permute-start(bf16[128,1024]{1,0:T(8,128)(2,1)S(1)} %get-tuple-element.76), channel_id=1, source_target_pairs={{0,8},{8,0},{1,9},{9,1},{2,10},{10,2},{3,11},{11,3},{4,12},{12,4},... | collective-permute-start | bytes 786440 | tf_op jit(solution)/shard_map/ppermute | solution.py:384
  56.2 17.3 %collective-permute-start.7 = (bf16[2,128,1024]{2,1,0:T(8,128)(2,1)S(1)}, bf16[2,128,1024]{2,1,0:T(8,128)(2,1)S(1)}, u32[]{:S(2)}, u32[]{:S(2)}) collective-permute-start(bf16[2,128,1024]{2,1,0:T(8,128)(2,1)S(1)} %maximum_select_fusion.5), channel_id=1, source_target_pairs={{0,4},{4,0},{1,5},{5,1},{2,6},{6,2},{3,7},{7,3},{8,12},{12,8},{9,1... | collective-permute-start | bytes 1572872 | tf_op jit(solution)/shard_map/ppermute | solution.py:384
  74.6 8.5 %copy-start.8 = (bf16[128,256]{1,0:T(8,128)(2,1)S(1)}, bf16[128,256]{1,0:T(8,128)(2,1)}, u32[]{:S(2)}) copy-start(bf16[128,256]{1,0:T(8,128)(2,1)} %key_ref.1) | copy-start | bytes 196612
  74.6 8.5 %copy-start.9 = (bf16[128,256]{1,0:T(8,128)(2,1)S(1)}, bf16[128,256]{1,0:T(8,128)(2,1)}, u32[]{:S(2)}) copy-start(bf16[128,256]{1,0:T(8,128)(2,1)} %value_ref.1) | copy-start | bytes 196612
  74.6 74.1 %all-to-all-start = ((bf16[8,48,4096]{2,1,0:T(8,128)(2,1)}), bf16[8,48,4096]{2,1,0:T(8,128)(2,1)S(1)}, u32[]{:S(2)}, u32[]{:S(2)}) async-start(bf16[8,48,4096]{2,1,0:T(8,128)(2,1)} %bitcast.41), calls=%async_computation | async-start | bytes 6291456 | tf_op jit(solution)/shard_map/all_to_all | solution.py:421
  80.5 12.4 %collective-permute-start = (bf16[2048,384]{1,0:T(8,128)(2,1)}, bf16[2048,384]{1,0:T(8,128)(2,1)}, u32[]{:S(2)}, u32[]{:S(2)}) collective-permute-start(bf16[2048,384]{1,0:T(8,128)(2,1)} %refs_0_.1), channel_id=1, source_target_pairs={{0,1},{1,0},{2,3},{3,2},{4,5},{5,4},{6,7},{7,6},{8,9},{9,8},{10,11... | collective-permute-start | bytes 4718600 | tf_op jit(solution)/shard_map/ppermute | solution.py:446
  82.5 10.5 %collective-permute-start.1 = (bf16[2048,384]{1,0:T(8,128)(2,1)}, bf16[2048,384]{1,0:T(8,128)(2,1)}, u32[]{:S(2)}, u32[]{:S(2)}) collective-permute-start(bf16[2048,384]{1,0:T(8,128)(2,1)} %refs_1_.1), channel_id=1, source_target_pairs={{0,1},{1,0},{2,3},{3,2},{4,5},{5,4},{6,7},{7,6},{8,9},{9,8},{10,11... | collective-permute-start | bytes 4718600 | tf_op jit(solution)/shard_map/ppermute | solution.py:446
  82.5 10.5 %collective-permute-start.2 = (bf16[384,2048]{1,0:T(8,128)(2,1)}, bf16[384,2048]{1,0:T(8,128)(2,1)}, u32[]{:S(2)}, u32[]{:S(2)}) collective-permute-start(bf16[384,2048]{1,0:T(8,128)(2,1)} %refs_2_.2), channel_id=1, source_target_pairs={{0,1},{1,0},{2,3},{3,2},{4,5},{5,4},{6,7},{7,6},{8,9},{9,8},{10,11... | collective-permute-start | bytes 4718600 | tf_op jit(solution)/shard_map/ppermute | solution.py:446
  83.1 9.9 %copy-start.3 = (bf16[2048,384]{1,0:T(8,128)(2,1)S(1)}, bf16[2048,384]{1,0:T(8,128)(2,1)}, u32[]{:S(2)}) copy-start(bf16[2048,384]{1,0:T(8,128)(2,1)} %refs_0_.1) | copy-start | bytes 4718596
  83.1 1.4 copy-start.10
  88.0 1.3 copy-start
  89.4 1.3 copy-start.1
  90.7 1.0 copy-start.2
  91.6 0.7 copy-start.6
  92.3 0.7 copy-start.7
  92.9 1.4 copy-start.4
  94.4 1.4 copy-start.5
  220.8 8.3 %collective-permute-start.8 = (bf16[2,128,256]{2,1,0:T(8,128)(2,1)}, bf16[2,128,256]{2,1,0:T(8,128)(2,1)S(1)}, u32[]{:S(2)}, u32[]{:S(2)}) collective-permute-start(bf16[2,128,256]{2,1,0:T(8,128)(2,1)} %get-tuple-element.74), channel_id=1, source_target_pairs={{1,0},{2,1},{3,2},{4,3},{5,4},{6,5},{7,6},{8,7},{9,8},{10,9},{11,1... | collective-permute-start | bytes 393224 | tf_op jit(solution)/shard_map/ppermute | solution.py:462
Sparse Core Ops, SparseCore 0:
  45.5 89.4 all-gather.2
  136.9 71.2 all-gather.4

commit v4 on v2

v4 whole, which is shorter than its diff:
```python
import functools

import jax
import jax.numpy as jnp
from jax import lax
from jax.experimental import pallas as pl
from jax.experimental.pallas import tpu as pltpu
from jax.sharding import PartitionSpec as P

KVH = 2
GROUP = 16
HD = 128
FLOOR = -1e30
MIB = 1 << 20

NT = (((1,), (1,)), ((), ()))
TN = (((0,), (0,)), ((), ()))


def dot(a, b, dims=(((1,), (0,)), ((), ()))):
    return lax.dot_general(a, b, dims, preferred_element_type=jnp.float32)


def params(mib):
    return pltpu.CompilerParams(vmem_limit_bytes=mib * MIB)


def pick_kernel(owners, depth, routes_ref, weight_ref, input_ref, grad_ref, rows_ref, back_ref):
    tokens = input_ref.shape[0]
    slots = owners * depth
    first = routes_ref[0:1, :]
    second = routes_ref[1:2, :]
    expert = lax.broadcasted_iota(jnp.int32, (owners, tokens), 0)
    is_first = first == expert
    is_second = second == expert
    member = jnp.where(is_first | is_second, 1.0, 0.0)
    before = lax.broadcasted_iota(jnp.int32, (tokens, tokens), 0) < lax.broadcasted_iota(
        jnp.int32, (tokens, tokens), 1
    )
    rank = dot(member.astype(jnp.bfloat16), jnp.where(before, 1.0, 0.0).astype(jnp.bfloat16))
    spot = (expert * depth).astype(jnp.float32) + rank
    slot_first = jnp.sum(jnp.where(is_first, spot, 0.0), axis=0, keepdims=True).astype(jnp.int32)
    slot_second = jnp.sum(jnp.where(is_second, spot, 0.0), axis=0, keepdims=True).astype(jnp.int32)
    slot = lax.broadcasted_iota(jnp.int32, (slots, tokens), 0)
    at_first = slot == slot_first
    at_second = slot == slot_second
    place = jnp.where(at_first | at_second, 1.0, 0.0).astype(jnp.bfloat16)
    back_ref[...] = place.T
    scale = jnp.sum(
        jnp.where(at_first, weight_ref[0:1, :], 0.0) + jnp.where(at_second, weight_ref[1:2, :], 0.0),
        axis=1,
        keepdims=True,
    )
    width = input_ref.shape[1]
    rows_ref[:, :width] = dot(place, input_ref[...]).astype(jnp.bfloat16)
    rows_ref[:, width:] = (scale * dot(place, grad_ref[...])).astype(jnp.bfloat16)


def pick(routes, route_weight, moe_input, moe_grad, owners, depth):
    tokens, width = moe_input.shape
    slots = owners * depth
    return pl.pallas_call(
        functools.partial(pick_kernel, owners, depth),
        out_shape=(
            jax.ShapeDtypeStruct((slots, 2 * width), jnp.bfloat16),
            jax.ShapeDtypeStruct((tokens, slots), jnp.bfloat16),
        ),
        compiler_params=params(32),
        cost_estimate=pl.CostEstimate(
            flops=4 * slots * tokens * width, bytes_accessed=8 * MIB, transcendentals=0
        ),
        name="pick_rows",
    )(routes.T, route_weight.T, moe_input, moe_grad)


def weights_kernel(*refs):
    own, other, (cols_ref, down_ref, rows_ref) = refs[:3], refs[3:6], refs[6:]
    tile = own[0].shape[1]
    for place, (gate_ref, up_ref, low_ref) in enumerate((own, other)):
        for kind, ref in enumerate((gate_ref, up_ref)):
            spot = slice((2 * kind + place) * tile, (2 * kind + place + 1) * tile)
            cols_ref[0, :, spot] = ref[...]
            rows_ref[0, spot, :] = ref[...].T
        down_ref[0, :, place * tile : (place + 1) * tile] = low_ref[...].T


def prepare_weights(own, other):
    width, half = own[0].shape
    tile = 128
    steps = half // tile
    cols = pl.BlockSpec((width, tile), lambda i: (0, i))
    down = pl.BlockSpec((tile, width), lambda i: (i, 0))
    return pl.pallas_call(
        weights_kernel,
        grid=(steps,),
        in_specs=[cols, cols, down] * 2,
        out_specs=[
            pl.BlockSpec((1, width, 4 * tile), lambda i: (i, 0, 0)),
            pl.BlockSpec((1, width, 2 * tile), lambda i: (i, 0, 0)),
            pl.BlockSpec((1, 4 * tile, width), lambda i: (i, 0, 0)),
        ],
        out_shape=(
            jax.ShapeDtypeStruct((steps, width, 4 * tile), jnp.bfloat16),
            jax.ShapeDtypeStruct((steps, width, 2 * tile), jnp.bfloat16),
            jax.ShapeDtypeStruct((steps, 4 * tile, width), jnp.bfloat16),
        ),
        compiler_params=params(48),
        cost_estimate=pl.CostEstimate(
            flops=0, bytes_accessed=32 * width * half, transcendentals=0
        ),
        name="prepare_weights",
    )(*own, *other)


def expert_kernel(steps, rows_ref, cols_ref, down_ref, back_ref, out_ref, hidden):
    step = pl.program_id(0)
    width = rows_ref.shape[1] // 2
    pair = down_ref.shape[2]

    @pl.when(step < steps)
    def _():
        both_pre = dot(rows_ref[:, :width], cols_ref[0])
        gate_pre = both_pre[:, :pair]
        up_pre = both_pre[:, pair:]
        down_grad = dot(rows_ref[:, width:], down_ref[0])
        sig = jax.nn.sigmoid(gate_pre)
        hidden[step, :, :pair] = (
            down_grad * up_pre * sig * (1.0 + gate_pre * (1.0 - sig))
        ).astype(jnp.bfloat16)
        hidden[step, :, pair:] = (down_grad * gate_pre * sig).astype(jnp.bfloat16)

    @pl.when(step >= steps)
    def _():
        total = dot(hidden[0], back_ref[0])
        for i in range(1, steps):
            total += dot(hidden[i], back_ref[i])
        out_ref[...] = total.astype(jnp.bfloat16)


def experts(rows, cols, down, back):
    count, twice = rows.shape
    steps, width, quad = cols.shape
    tile = 512
    last = steps - 1
    turn = lambda i: jnp.maximum(i - steps, 0)
    return pl.pallas_call(
        functools.partial(expert_kernel, steps),
        grid=(steps + width // tile,),
        in_specs=[
            pl.BlockSpec((count, twice), lambda i: (0, 0)),
            pl.BlockSpec((1, width, quad), lambda i: (jnp.minimum(i, last), 0, 0)),
            pl.BlockSpec((1, width, quad // 2), lambda i: (jnp.minimum(i, last), 0, 0)),
            pl.BlockSpec((steps, quad, tile), lambda i: (0, 0, turn(i))),
        ],
        out_specs=pl.BlockSpec((count, tile), lambda i: (0, turn(i))),
        out_shape=jax.ShapeDtypeStruct((count, width), jnp.bfloat16),
        scratch_shapes=[pltpu.VMEM((steps, count, quad), jnp.bfloat16)],
        compiler_params=params(48),
        cost_estimate=pl.CostEstimate(
            flops=100 * count * width * steps * quad, bytes_accessed=20 * MIB,
            transcendentals=count * steps * quad,
        ),
        name="expert_terms",
    )(rows, cols, down, back)


def shares_kernel(
    q_ref, key_ref, value_ref, prev_key_ref, prev_value_ref, prev_seg_ref, seg_row_ref, seg_col_ref,
    low_ref, turned_ref, query_ref, key_out, value_out,
):
    tokens = q_ref.shape[0]
    seg_col = seg_col_ref[...]
    row = lax.broadcasted_iota(jnp.int32, (tokens, tokens), 0)
    col = lax.broadcasted_iota(jnp.int32, (tokens, tokens), 1)
    own_seen = jnp.where((col <= row) & (seg_row_ref[...] == seg_col), 1.0, 0.0)
    prev_seg = prev_seg_ref[tokens : tokens + 16, :].astype(jnp.float32)[0:1, :]
    prev_seen = jnp.where(prev_seg == seg_col, 1.0, 0.0)
    seen = jnp.concatenate([prev_seen, own_seen], axis=1) > 0.5
    keys = jnp.concatenate([prev_key_ref[:tokens, :], key_ref[...]], axis=0)
    values = jnp.concatenate([prev_value_ref[:tokens, :], value_ref[...]], axis=0)
    key_out[0] = keys
    value_out[0] = values.T
    for head in range(GROUP):
        rows = slice(head * tokens, (head + 1) * tokens)
        query = q_ref[:, head * HD : (head + 1) * HD]
        scores = dot(query, keys, NT) * (HD**-0.5)
        masked = jnp.where(seen, scores, FLOOR)
        raised = jnp.where(seen, jnp.exp(masked - jnp.max(masked, axis=1, keepdims=True)), 0.0)
        shares = raised / jnp.sum(raised, axis=1, keepdims=True)
        low = shares.astype(jnp.bfloat16)
        low_ref[0, rows, :] = low
        turned_ref[0, :, rows] = low.T
        query_ref[0, rows, :] = query


def attention_shares(queries, key_heads, value_heads, prev, segs):
    tokens, width = queries.shape
    span = 2 * tokens
    stack = GROUP * tokens
    high = prev.shape[0]
    own = pl.BlockSpec((tokens, HD), lambda g: (0, g))
    group = lambda shape: pl.BlockSpec((1,) + shape, lambda g: (g, 0, 0))
    made = lambda shape: jax.ShapeDtypeStruct((KVH,) + shape, jnp.bfloat16)
    shapes = ((stack, span), (span, stack), (stack, HD), (span, HD), (HD, span))
    return pl.pallas_call(
        shares_kernel,
        grid=(KVH,),
        in_specs=[
            pl.BlockSpec((tokens, GROUP * HD), lambda g: (0, g)),
            own,
            own,
            pl.BlockSpec((high, HD), lambda g: (0, g)),
            pl.BlockSpec((high, HD), lambda g: (0, KVH + g)),
            pl.BlockSpec((high, HD), lambda g: (0, 0)),
            pl.BlockSpec((1, tokens), lambda g: (0, 0)),
            pl.BlockSpec((tokens, 1), lambda g: (0, 0)),
        ],
        out_specs=[group(shape) for shape in shapes],
        out_shape=[made(shape) for shape in shapes],
        compiler_params=params(32),
        cost_estimate=pl.CostEstimate(
            flops=2 * tokens * width * span, bytes_accessed=8 * MIB,
            transcendentals=tokens * span * KVH * GROUP,
        ),
        name="attention_shares",
    )(queries, key_heads, value_heads, prev, prev, prev, segs[None, :], segs[:, None])


def tail_kernel(
    plan, back_ref, place_ref, grad_ref, own_ref, other_ref, low_ref, turned_ref, q_ref, key_ref, value_ref,
    moe_ref, query_out, key_out, value_out, sent_out, stream, held, sums,
):
    orders, heads, tiles = plan
    step = pl.program_id(0)
    tokens = query_out.shape[0]
    half = own_ref.shape[1]

    @pl.when(step == 0)
    def _():
        moe = dot(place_ref[...], back_ref[...]).astype(jnp.bfloat16)
        moe_ref[...] = moe
        added = (grad_ref[...].astype(jnp.float32) + moe.astype(jnp.float32)).astype(jnp.bfloat16)
        size = added.shape[1] // len(orders[0])
        for core, order in enumerate(orders):

            @pl.when(lax.axis_index("core") == core)
            def _():
                for to, source in enumerate(order):
                    stream[:, to * size : (to + 1) * size] = added[:, source * size : (source + 1) * size]

        held[...] = jnp.zeros_like(held)

    @pl.when((step == 0) | ((step > 1) & ((step - 1) % tiles == 0)))
    def _():
        sums[...] = jnp.zeros_like(sums)

    grads = held[...]
    head_grad = (dot(stream[:, :half], own_ref[0]) + dot(stream[:, half:], other_ref[0])).astype(jnp.bfloat16)
    low = low_ref[0].astype(jnp.float32)
    prob_grad = dot(grads, value_ref[0])
    row_dot = jnp.sum(low * prob_grad, axis=1, keepdims=True)
    score_grad = (low * (prob_grad - row_dot) * (HD**-0.5)).astype(jnp.bfloat16)
    query_grad = dot(score_grad, key_ref[0]).astype(jnp.bfloat16)
    sums[0] += dot(score_grad, q_ref[0], TN)
    sums[1] += dot(turned_ref[0], grads)
    for head in range(heads):
        cols = slice(head * HD, (head + 1) * HD)
        rows = slice(head * tokens, (head + 1) * tokens)
        query_out[:, cols] = query_grad[rows, :]
        held[rows, :] = head_grad[:, cols]

    @pl.when((step > 0) & (step % tiles == 0))
    def _():
        key_out[...] = sums[0, tokens:, :]
        value_out[...] = sums[1, tokens:, :]
        sent_out[...] = sums[:, :tokens, :].astype(jnp.bfloat16)


def tail(orders, back, place, moe_grad, w_own, w_other, low, turned, query, keys, values):
    tokens, width = moe_grad.shape
    half, cols = w_own.shape[1:]
    span = keys.shape[1]
    heads = 4
    tile = heads * HD
    tiles = cols // tile
    steps = KVH * tiles
    now = lambda i: jnp.minimum(i, steps - 1)
    was = lambda i: jnp.maximum(i - 1, 0)
    whole = lambda shape: pl.BlockSpec(shape, lambda i: (0,) * len(shape))
    group = lambda shape: pl.BlockSpec((1,) + shape, lambda i: (was(i) // tiles, 0, 0))
    rows = lambda shape: pl.BlockSpec((1,) + shape, lambda i: (was(i) // tiles, was(i) % tiles, 0))
    w_spec = pl.BlockSpec((1, half, tile), lambda i: (now(i) // tiles, 0, now(i) % tiles))
    kv = pl.BlockSpec((tokens, HD), lambda i: (0, was(i) // tiles))
    return pl.pallas_call(
        functools.partial(tail_kernel, (orders, heads, tiles)),
        grid=(steps + 1,),
        in_specs=[
            whole(back.shape),
            whole(place.shape),
            whole(moe_grad.shape),
            w_spec,
            w_spec,
            rows((heads * tokens, span)),
            pl.BlockSpec((1, span, heads * tokens), lambda i: (was(i) // tiles, 0, was(i) % tiles)),
            rows((heads * tokens, HD)),
            group((span, HD)),
            group((HD, span)),
        ],
        out_specs=[
            whole((tokens, width)),
            pl.BlockSpec((tokens, tile), lambda i: (0, was(i))),
            kv,
            kv,
            pl.BlockSpec((2, tokens, HD), lambda i: (0, 0, was(i) // tiles)),
        ],
        out_shape=(
            jax.ShapeDtypeStruct((tokens, width), jnp.bfloat16),
            jax.ShapeDtypeStruct((tokens, KVH * cols), jnp.bfloat16),
            jax.ShapeDtypeStruct((tokens, KVH * HD), jnp.float32),
            jax.ShapeDtypeStruct((tokens, KVH * HD), jnp.float32),
            jax.ShapeDtypeStruct((2, tokens, KVH * HD), jnp.bfloat16),
        ),
        scratch_shapes=[
            pltpu.VMEM((tokens, width), jnp.bfloat16),
            pltpu.VMEM((heads * tokens, HD), jnp.bfloat16),
            pltpu.VMEM((2, span, HD), jnp.float32),
        ],
        compiler_params=params(56),
        cost_estimate=pl.CostEstimate(
            flops=2 * tokens * width * KVH * cols, bytes_accessed=22 * MIB, transcendentals=0
        ),
        name="tail_attention",
    )(back, place, moe_grad, w_own, w_other, low, turned, query, keys, values)


def local(
    moe_input,
    moe_grad,
    routes,
    route_weight,
    w_gate,
    w_up,
    w_down,
    w_out,
    queries,
    key_heads,
    value_heads,
    segments,
):
    chips = ("far", "near", "low")
    blk = chips + ("core",)
    low = lax.axis_size("low")
    owners = 4 * low
    count = 2 * owners
    parts = lax.axis_size("groups")
    tokens, width = moe_input.shape
    depth = 2 * max(1, 3 * tokens * routes.shape[1] // (2 * count))
    swap = [(0, 1), (1, 0)]
    onward = [(i, i + 1) for i in range(count - 1)]
    backward = [(i + 1, i) for i in range(count - 1)]

    rows, place = pick(routes, route_weight, moe_input, moe_grad, owners, depth)
    rows, w_out = lax.optimization_barrier((rows, w_out))
    rows_in = lax.all_to_all(rows.reshape(owners, depth, 2 * width), chips, 0, 0, tiled=True)

    block = w_out.shape[0]
    share_cols = w_out.shape[1] // parts
    w_share = lax.dynamic_slice_in_dim(w_out, lax.axis_index("groups") * share_cols, share_cols, 1)
    w_line = lax.all_gather(w_share, ("far", "near"), axis=0, tiled=True)
    w_own = lax.all_gather(w_line, ("groups", "low"), axis=0, tiled=False)
    w_own = w_own.reshape(parts, low, 4, block, share_cols)
    if block % 128:
        w_own = w_own.transpose(0, 2, 1, 3, 4)
    w_own = w_own.reshape(parts, width // 2, share_cols)
    w_other = lax.ppermute(w_own, "core", swap)
    orders = tuple(
        tuple(
            (z * low + rest) * 2 + (core ^ flip)
            for flip in range(2)
            for z, rest in (
                [(z, rest) for rest in range(low) for z in range(4)]
                if block % 128 == 0
                else [(z, rest) for z in range(4) for rest in range(low)]
            )
        )
        for core in range(2)
    )

    own = (w_gate, w_up, w_down)
    other = tuple(lax.ppermute(w, "core", swap) for w in own)
    prepared = prepare_weights(own, other)

    kv = jnp.concatenate([key_heads, value_heads], axis=1)
    segs = (segments + 1).astype(jnp.float32)
    seg_rows = jnp.zeros((16, kv.shape[1]), jnp.bfloat16).at[0, :tokens].set(segs.astype(jnp.bfloat16))
    prev = lax.ppermute(jnp.concatenate([kv, seg_rows], axis=0), blk, onward)

    prepared, prev, rows_in = lax.optimization_barrier((prepared, prev, rows_in))
    terms = experts(rows_in.reshape(owners * depth, 2 * width), *prepared)
    prev, terms = lax.optimization_barrier((prev, terms))
    back = lax.all_to_all(terms.reshape(owners, depth, width), chips, 0, 0, tiled=True)
    attention = attention_shares(queries, key_heads, value_heads, prev, segs)

    moe_input_grad, query_grad, key_part, value_part, sent = tail(
        orders, back.reshape(owners * depth, width), place, moe_grad, w_own, w_other, *attention
    )
    later = lax.ppermute(sent, blk, backward).astype(jnp.float32)
    return (moe_input_grad, query_grad, key_part + later[0], value_part + later[1])


def solution(mesh):
    names = ("groups", "far", "near", "low", "core")
    shape = (mesh.shape["groups"], 2, 2, mesh.shape["blk"] // 8, 2)
    fine = jax.sharding.Mesh(mesh.devices.reshape(shape), names)
    blk = names[1:]
    by_tokens = P(names, None)
    return jax.shard_map(
        local,
        mesh=fine,
        in_specs=(
            by_tokens,
            by_tokens,
            by_tokens,
            by_tokens,
            P(None, blk),
            P(None, blk),
            P(blk, None),
            P(blk, None),
            by_tokens,
            by_tokens,
            by_tokens,
            P(names),
        ),
        out_specs=(by_tokens,) * 4,
        check_vma=False,
    )
```

time: 244 us -> 271 us (1.11)
  waiting for transfers between devices: 147 us -> 172 us
  local copies, waits for them, and re-layouts: 8.16 us -> 15.8 us
  starting transfers between devices: 23.6 us -> 19.9 us
    all_gather x1 -> x2, waiting for transfers between devices: 0.01 us -> 88.5 us  [the longest x1 45.3 us: local(): w_line = lax.all_gather(w_share, ('far', 'near'), axis=0, tiled=True)]
    ppermute x7 -> x5, waiting for transfers between devices: 109 us -> 52.5 us  [the longest x1 48.3 us: local(): prev = lax.ppermute(jnp.concatenate([kv, seg_rows], axis=0), blk, onward)]
    all_to_all x1, waiting for transfers between devices: 33.8 us -> 25.8 us  [local(): lax.all_to_all(terms.reshape(owners, depth, width), chips, 0, 0, tiled=True)]
    unnamed x32 -> x44, local copies, waits for them, and re-layouts: 7.4 us -> 14.8 us
    ppermute x7 -> x5, starting transfers between devices: 10.2 us -> 5.19 us  [the longest x1 3.05 us: local(): prev = lax.ppermute(jnp.concatenate([kv, seg_rows], axis=0), blk, onward)]
    select_n x2 -> x0, other arithmetic: 2.74 us -> none  [far_first(): jnp.where(mine, jnp.stack([share, moved]), jnp.stack([moved, share]))]
  transfers between devices with their start and end apart: 11 -> 10, of which waited for: 6 -> 8; matrix products, arithmetic and copies ran while one was open for 0% -> 0% of each run, Pallas kernels for 11% -> 10%
where the time goes in v4:
time: 271 us; the launch traced here: 267 us
  waiting for transfers between devices  172 us (63%)
  Pallas kernels  43.6 us (16%)
  starting transfers between devices  19.9 us (7%)
  local copies, waits for them, and re-layouts  15.8 us (6%)
  between operations  14.2 us (5%)
    ppermute x1, waiting for transfers between devices, local(): prev = lax.ppermute(jnp.concatenate([kv, seg_rows], axis=0), blk, onward)  48.3 us
    all_gather x1, waiting for transfers between devices, local(): w_line = lax.all_gather(w_share, ('far', 'near'), axis=0, tiled=True)  45.3 us
    all_gather x1, waiting for transfers between devices, local(): w_own = lax.all_gather(w_line, ('groups', 'low'), axis=0, tiled=False)  43.2 us
    all_to_all x1, waiting for transfers between devices, local(): lax.all_to_all(terms.reshape(owners, depth, width), chips, 0, 0, tiled=True)  25.8 us
    pallas_call x1, Pallas kernels, tail(): pl.pallas_call(functools.partial(tail_kernel, (orders, heads, tiles)), gr...  16.2 us
    unnamed x44, local copies, waits for them, and re-layouts  14.8 us
    pallas_call x1, Pallas kernels, experts(): pl.pallas_call(functools.partial(expert_kernel, steps), grid=(steps + wid...  13.9 us
    pallas_call x1, Pallas kernels, prepare_weights(): pl.pallas_call(weights_kernel, grid=(steps,), in_specs=[cols, cols, down]...  8.76 us
  transfers between devices with their start and end apart: 10, of which 8 were waited for; matrix products, arithmetic and copies ran while one was open for 0% of the time, Pallas kernels for 10%

profile of v4, /device:TPU:13, one launch (start us, length us, event | category | flops | bytes accessed | tf_op | source)
XLA Modules:
  0.0 266.9 jit_solution(5467508895809567857)
XLA Ops:
  7.2 1.1 copy-done.8
  8.4 1.0 copy-done.15
  10.8 1.2 pick_rows.1
  11.9 1.6 copy-done.1
  15.1 45.3 %all-gather.4.cloned.1.call-done = bf16[512,2048]{1,0:T(8,128)(2,1)} async-done(((bf16[128,2048]{1,0:T(8,128)(2,1)}), bf16[512,2048]{1,0:T(8,128)(2,1)}) %all-gather.4.cloned.1.call-update) | async-done | bytes 2097168 | tf_op jit(solution)/shard_map/all_gather | solution.py:369
  60.5 6.6 %all-to-all-start = ((bf16[8,48,4096]{2,1,0:T(8,128)(2,1)}), bf16[8,48,4096]{2,1,0:T(8,128)(2,1)}, u32[]{:S(2)}, u32[]{:S(2)}) async-start(bf16[8,48,4096]{2,1,0:T(8,128)(2,1)} %bitcast.21), calls=%async_computation | async-start | bytes 6291456 | tf_op jit(solution)/shard_map/all_to_all | solution.py:364
  68.6 3.1 %collective-permute-start.3 = (bf16[144,512]{1,0:T(8,128)(2,1)S(1)}, bf16[144,512]{1,0:T(8,128)(2,1)S(1)}, u32[]{:S(2)}, u32[]{:S(2)}) collective-permute-start(bf16[144,512]{1,0:T(8,128)(2,1)S(1)} %fusion.1), channel_id=1, source_target_pairs={{0,1},{1,2},{2,3},{3,4},{4,5},{5,6},{6,7},{7,8},{8,9},{9,10},{10,1... | collective-permute-start | bytes 442376 | tf_op jit(solution)/shard_map/ppermute | solution.py:396
  73.5 2.3 collective-permute-done.2.refs_5_
  75.9 1.2 copy-done.20
  77.1 1.4 copy-done.5
  78.5 1.4 copy-done.6
  79.9 8.8 %prepare_weights.1 = (bf16[3,2048,512]{2,1,0:T(8,128)(2,1)}, bf16[3,2048,256]{2,1,0:T(8,128)(2,1)}, bf16[3,512,2048]{2,1,0:T(8,128)(2,1)}) custom-call(bf16[2048,384]{1,0:T(8,128)(2,1)S(1)} %copy-done.4, bf16[2048,384]{1,0:T(8,128)(2,1)S(1)} %copy-done.5, bf16[384,2048]{1,0:T(8,128)(2,1)S(1)} %copy-done.6, bf16[2048,384]{1,0:T(8,128)(2,1)} %copy-done.18, ...), custom_call_target="tpu_custom_call" | custom-call | bytes 25165824 | tf_op jit(solution)/shard_map/prepare_weights/pallas_call | solution.py:93
  88.6 48.3 %collective-permute-done.3.prev_key_ref.prev_value_ref.prev_seg_ref = bf16[144,512]{1,0:T(8,128)(2,1)S(1)} collective-permute-done((bf16[144,512]{1,0:T(8,128)(2,1)S(1)}, bf16[144,512]{1,0:T(8,128)(2,1)S(1)}, u32[]{:S(2)}, u32[]{:S(2)}) %collective-permute-start.3) | collective-permute-done | bytes 147488 | tf_op jit(solution)/shard_map/ppermute | solution.py:396
  136.9 43.2 %all-gather.6.cloned.1.call-done = bf16[2048,2048]{1,0:T(8,128)(2,1)} async-done(((bf16[512,2048]{1,0:T(8,128)(2,1)}), bf16[2048,2048]{1,0:T(8,128)(2,1)}) %all-gather.6.cloned.1.call-update) | async-done | bytes 8388624 | tf_op jit(solution)/shard_map/all_gather | solution.py:370
  180.8 13.9 %expert_terms.1 = bf16[384,2048]{1,0:T(8,128)(2,1)} custom-call(bf16[384,4096]{1,0:T(8,128)(2,1)} %bitcast.4.rows_ref, bf16[3,2048,512]{2,1,0:T(8,128)(2,1)} %get-tuple-element.47.cols_ref, bf16[3,2048,256]{2,1,0:T(8,128)(2,1)} %get-tuple-element.48.down_ref, bf16[3,512,2048]{2,1,0:T(8,128)(2,1)} %get-tuple-element.49.back_ref), custom_call_target="tpu_custom_call" | custom-call | flops 120795955200 | bytes 20971520 | tf_op jit(solution)/shard_map/expert_terms/pallas_call | solution.py:146
  194.6 5.6 %all-to-all-start.1 = ((bf16[8,48,2048]{2,1,0:T(8,128)(2,1)}), bf16[8,48,2048]{2,1,0:T(8,128)(2,1)}, u32[]{:S(2)}, u32[]{:S(2)}) async-start(bf16[8,48,2048]{2,1,0:T(8,128)(2,1)} %bitcast.5), calls=%async_computation.1 | async-start | bytes 3145728 | tf_op jit(solution)/shard_map/all_to_all | solution.py:401
  200.4 3.5 %attention_shares.1 = (bf16[2,2048,256]{2,1,0:T(8,128)(2,1)S(1)}, bf16[2,256,2048]{2,1,0:T(8,128)(2,1)S(1)}, bf16[2,2048,128]{2,1,0:T(8,128)(2,1)S(1)}, bf16[2,2...) custom-call(bf16[128,4096]{1,0:T(8,128)(2,1)S(1)} %copy-done.14, bf16[128,256]{1,0:T(8,128)(2,1)S(1)} %copy-done.12, ...), custom_call_target="tpu_custom_call" | custom-call | flops 268435456 | bytes 8388608 | tf_op jit(solution)/shard_map/attention_shares/pallas_call | solution.py:205
  203.9 1.4 copy-done.2
  205.3 1.3 copy-done.3
  208.9 25.8 %all-to-all-done.1 = bf16[8,48,2048]{2,1,0:T(8,128)(2,1)} async-done(((bf16[8,48,2048]{2,1,0:T(8,128)(2,1)}), bf16[8,48,2048]{2,1,0:T(8,128)(2,1)}, u32[]{:S(2)}, u32[]{:S(2)}) %all-to-all-start.1) | async-done | bytes 1572896 | tf_op jit(solution)/shard_map/all_to_all | solution.py:401
  234.8 16.2 %tail_attention.1 = (bf16[128,2048]{1,0:T(8,128)(2,1)}, bf16[128,4096]{1,0:T(8,128)(2,1)}, f32[128,256]{1,0:T(8,128)}, f32[128,256]{1,0:T(8,128)}, bf16[2,128,256]{2,1,0:T(8,128)(2,1)}) custom-call(bf16[384,2048]{1,0:T(8,128)(2,1)} %bitcast.6.back_ref, bf16[128,384]{1,0:T(8,128)(2,1)} %copy-done.11, bf16[128,2048]{1,0:T(8,128)(2,1)} %grad_ref.3, ...), custom_call_target="tpu_custom_call" | custom-call | flops 2147483648 | bytes 23068672 | tf_op jit(solution)/shard_map/tail_attention/pallas_call | solution.py:294
  251.0 2.4 collective-permute-start.5
  253.4 5.0 %collective-permute-done.5 = bf16[2,128,256]{2,1,0:T(8,128)(2,1)S(1)} collective-permute-done((bf16[2,128,256]{2,1,0:T(8,128)(2,1)}, bf16[2,128,256]{2,1,0:T(8,128)(2,1)S(1)}, u32[]{:S(2)}, u32[]{:S(2)}) %collective-permute-start.5) | collective-permute-done | bytes 131104 | tf_op jit(solution)/shard_map/ppermute | solution.py:407
  258.4 1.7 fusion.2
  (53 shorter events, 9.5 us)
Async XLA Ops:
  7.2 7.0 %copy-start = (bf16[128,4096]{1,0:T(8,128)(2,1)S(1)}, bf16[128,4096]{1,0:T(8,128)(2,1)}, u32[]{:S(2)}) copy-start(bf16[128,4096]{1,0:T(8,128)(2,1)} %param.21) | copy-start | bytes 3145732
  7.2 53.2 %all-gather.4.cloned.1.call-start = ((), (), s32[]{:S(2)}) async-start(), calls=%async_computation.2 | async-start | bytes 2621440 | tf_op jit(solution)/shard_map/all_gather | solution.py:369
  11.9 1.6 copy-start.1
  15.1 165.0 %all-gather.6.cloned.1.call-start = ((), (), s32[]{:S(2)}) async-start(), calls=%async_computation.3 | async-start | bytes 10485760 | tf_op jit(solution)/shard_map/all_gather | solution.py:370
  60.4 6.7 %copy-start.4 = (bf16[2048,384]{1,0:T(8,128)(2,1)S(1)}, bf16[2048,384]{1,0:T(8,128)(2,1)}, u32[]{:S(2)}) copy-start(bf16[2048,384]{1,0:T(8,128)(2,1)} %refs_0_.1) | copy-start | bytes 4718596
  60.4 8.1 %copy-start.21 = (s32[128]{0:T(128)S(1)}, s32[128]{0:T(128)}, u32[]{:S(2)}) copy-start(s32[128]{0:T(128)} %param.25) | copy-start | bytes 1540
  60.5 8.1 %copy-start.12 = (bf16[128,256]{1,0:T(8,128)(2,1)S(1)}, bf16[128,256]{1,0:T(8,128)(2,1)}, u32[]{:S(2)}) copy-start(bf16[128,256]{1,0:T(8,128)(2,1)} %key_ref.1) | copy-start | bytes 196612
  60.5 8.1 %copy-start.13 = (bf16[128,256]{1,0:T(8,128)(2,1)S(1)}, bf16[128,256]{1,0:T(8,128)(2,1)}, u32[]{:S(2)}) copy-start(bf16[128,256]{1,0:T(8,128)(2,1)} %value_ref.1) | copy-start | bytes 196612
  60.5 76.4 %all-to-all-start = ((bf16[8,48,4096]{2,1,0:T(8,128)(2,1)}), bf16[8,48,4096]{2,1,0:T(8,128)(2,1)}, u32[]{:S(2)}, u32[]{:S(2)}) async-start(bf16[8,48,4096]{2,1,0:T(8,128)(2,1)} %bitcast.21), calls=%async_computation | async-start | bytes 6291456 | tf_op jit(solution)/shard_map/all_to_all | solution.py:364
  67.1 5.5 %collective-permute-start = (bf16[2048,384]{1,0:T(8,128)(2,1)S(1)}, bf16[2048,384]{1,0:T(8,128)(2,1)S(1)}, u32[]{:S(2)}, u32[]{:S(2)}) collective-permute-start(bf16[2048,384]{1,0:T(8,128)(2,1)S(1)} %copy-done.4), channel_id=1, source_target_pairs={{0,1},{1,0},{2,3},{3,2},{4,5},{5,4},{6,7},{7,6},{8,9},{9,8},{10,11... | collective-permute-start | bytes 4718600 | tf_op jit(solution)/shard_map/ppermute | solution.py:390
  68.0 5.5 %collective-permute-start.1 = (bf16[2048,384]{1,0:T(8,128)(2,1)}, bf16[2048,384]{1,0:T(8,128)(2,1)S(1)}, u32[]{:S(2)}, u32[]{:S(2)}) collective-permute-start(bf16[2048,384]{1,0:T(8,128)(2,1)} %refs_1_.1), channel_id=1, source_target_pairs={{0,1},{1,0},{2,3},{3,2},{4,5},{5,4},{6,7},{7,6},{8,9},{9,8},{10,11... | collective-permute-start | bytes 4718600 | tf_op jit(solution)/shard_map/ppermute | solution.py:390
  68.1 7.8 %collective-permute-start.2 = (bf16[384,2048]{1,0:T(8,128)(2,1)}, bf16[384,2048]{1,0:T(8,128)(2,1)S(1)}, u32[]{:S(2)}, u32[]{:S(2)}) collective-permute-start(bf16[384,2048]{1,0:T(8,128)(2,1)} %refs_2_.1), channel_id=1, source_target_pairs={{0,1},{1,0},{2,3},{3,2},{4,5},{5,4},{6,7},{7,6},{8,9},{9,8},{10,11... | collective-permute-start | bytes 4718600 | tf_op jit(solution)/shard_map/ppermute | solution.py:390
  68.6 68.3 %collective-permute-start.3 = (bf16[144,512]{1,0:T(8,128)(2,1)S(1)}, bf16[144,512]{1,0:T(8,128)(2,1)S(1)}, u32[]{:S(2)}, u32[]{:S(2)}) collective-permute-start(bf16[144,512]{1,0:T(8,128)(2,1)S(1)} %fusion.1), channel_id=1, source_target_pairs={{0,1},{1,2},{2,3},{3,4},{4,5},{5,6},{6,7},{7,8},{8,9},{9,10},{10,1... | collective-permute-start | bytes 442376 | tf_op jit(solution)/shard_map/ppermute | solution.py:396
  72.6 3.3 %copy-start.18 = (bf16[2048,384]{1,0:T(8,128)(2,1)}, bf16[2048,384]{1,0:T(8,128)(2,1)S(1)}, u32[]{:S(2)}) copy-start(bf16[2048,384]{1,0:T(8,128)(2,1)S(1)} %collective-permute-done.refs_3_) | copy-start | bytes 4718596
  73.5 2.3 copy-start.19
  75.9 1.2 copy-start.20
  77.1 1.4 copy-start.5
  78.5 1.4 copy-start.6
  180.1 54.7 %collective-permute-start.4 = (bf16[2,1024,2048]{2,1,0:T(8,128)(2,1)}, bf16[2,1024,2048]{2,1,0:T(8,128)(2,1)}, u32[]{:S(2)}, u32[]{:S(2)}) collective-permute-start(bf16[2,1024,2048]{2,1,0:T(8,128)(2,1)} %bitcast.24), channel_id=1, source_target_pairs={{0,1},{1,0},{2,3},{3,2},{4,5},{5,4},{6,7},{7,6},{8,9},{9,8},{10,11... | collective-permute-start | bytes 25165832 | tf_op jit(solution)/shard_map/ppermute | solution.py:375
  194.6 5.7 %copy-start.14 = (bf16[128,4096]{1,0:T(8,128)(2,1)S(1)}, bf16[128,4096]{1,0:T(8,128)(2,1)}, u32[]{:S(2)}) copy-start(bf16[128,4096]{1,0:T(8,128)(2,1)} %q_ref.1) | copy-start | bytes 3145732
  194.6 40.1 %all-to-all-start.1 = ((bf16[8,48,2048]{2,1,0:T(8,128)(2,1)}), bf16[8,48,2048]{2,1,0:T(8,128)(2,1)}, u32[]{:S(2)}, u32[]{:S(2)}) async-start(bf16[8,48,2048]{2,1,0:T(8,128)(2,1)} %bitcast.5), calls=%async_computation.1 | async-start | bytes 3145728 | tf_op jit(solution)/shard_map/all_to_all | solution.py:401
  203.9 1.4 copy-start.2
  205.3 1.3 copy-start.3
  251.0 7.4 %collective-permute-start.5 = (bf16[2,128,256]{2,1,0:T(8,128)(2,1)}, bf16[2,128,256]{2,1,0:T(8,128)(2,1)S(1)}, u32[]{:S(2)}, u32[]{:S(2)}) collective-permute-start(bf16[2,128,256]{2,1,0:T(8,128)(2,1)} %get-tuple-element.62), channel_id=1, source_target_pairs={{1,0},{2,1},{3,2},{4,3},{5,4},{6,5},{7,6},{8,7},{9,8},{10,9},{11,1... | collective-permute-start | bytes 393224 | tf_op jit(solution)/shard_map/ppermute | solution.py:407
  (8 other events, 6.5 us)
Sparse Core Ops, SparseCore 0:
  15.2 45.1 all-gather.3
  62.3 117.7 all-gather.5

commit v5 on v4

--- a/solution.py
+++ b/solution.py
@@ -157,7 +157,7 @@
         scratch_shapes=[pltpu.VMEM((steps, count, quad), jnp.bfloat16)],
         compiler_params=params(48),
         cost_estimate=pl.CostEstimate(
-            flops=100 * count * width * steps * quad, bytes_accessed=20 * MIB,
+            flops=5 * count * width * steps * quad, bytes_accessed=20 * MIB,
             transcendentals=count * steps * quad,
         ),
         name="expert_terms",
@@ -230,7 +230,7 @@
     plan, back_ref, place_ref, grad_ref, own_ref, other_ref, low_ref, turned_ref, q_ref, key_ref, value_ref,
     moe_ref, query_out, key_out, value_out, sent_out, stream, held, sums,
 ):
-    orders, heads, tiles = plan
+    heads, tiles = plan
     step = pl.program_id(0)
     tokens = query_out.shape[0]
     half = own_ref.shape[1]
@@ -240,14 +240,9 @@
         moe = dot(place_ref[...], back_ref[...]).astype(jnp.bfloat16)
         moe_ref[...] = moe
         added = (grad_ref[...].astype(jnp.float32) + moe.astype(jnp.float32)).astype(jnp.bfloat16)
-        size = added.shape[1] // len(orders[0])
-        for core, order in enumerate(orders):
-
-            @pl.when(lax.axis_index("core") == core)
-            def _():
-                for to, source in enumerate(order):
-                    stream[:, to * size : (to + 1) * size] = added[:, source * size : (source + 1) * size]
-
+        low_half = lax.axis_index("far") == 0
+        stream[:, :half] = jnp.where(low_half, added[:, :half], added[:, half:])
+        stream[:, half:] = jnp.where(low_half, added[:, half:], added[:, :half])
         held[...] = jnp.zeros_like(held)
 
     @pl.when((step == 0) | ((step > 1) & ((step - 1) % tiles == 0)))
@@ -276,7 +271,7 @@
         sent_out[...] = sums[:, :tokens, :].astype(jnp.bfloat16)
 
 
-def tail(orders, back, place, moe_grad, w_own, w_other, low, turned, query, keys, values):
+def tail(back, place, moe_grad, w_own, w_other, low, turned, query, keys, values):
     tokens, width = moe_grad.shape
     half, cols = w_own.shape[1:]
     span = keys.shape[1]
@@ -292,7 +287,7 @@
     w_spec = pl.BlockSpec((1, half, tile), lambda i: (now(i) // tiles, 0, now(i) % tiles))
     kv = pl.BlockSpec((tokens, HD), lambda i: (0, was(i) // tiles))
     return pl.pallas_call(
-        functools.partial(tail_kernel, (orders, heads, tiles)),
+        functools.partial(tail_kernel, (heads, tiles)),
         grid=(steps + 1,),
         in_specs=[
             whole(back.shape),
@@ -360,32 +355,11 @@
     backward = [(i + 1, i) for i in range(count - 1)]
 
     rows, place = pick(routes, route_weight, moe_input, moe_grad, owners, depth)
-    rows, w_out = lax.optimization_barrier((rows, w_out))
     rows_in = lax.all_to_all(rows.reshape(owners, depth, 2 * width), chips, 0, 0, tiled=True)
 
-    block = w_out.shape[0]
     share_cols = w_out.shape[1] // parts
     w_share = lax.dynamic_slice_in_dim(w_out, lax.axis_index("groups") * share_cols, share_cols, 1)
-    w_line = lax.all_gather(w_share, ("far", "near"), axis=0, tiled=True)
-    w_own = lax.all_gather(w_line, ("groups", "low"), axis=0, tiled=False)
-    w_own = w_own.reshape(parts, low, 4, block, share_cols)
-    if block % 128:
-        w_own = w_own.transpose(0, 2, 1, 3, 4)
-    w_own = w_own.reshape(parts, width // 2, share_cols)
-    w_other = lax.ppermute(w_own, "core", swap)
-    orders = tuple(
-        tuple(
-            (z * low + rest) * 2 + (core ^ flip)
-            for flip in range(2)
-            for z, rest in (
-                [(z, rest) for rest in range(low) for z in range(4)]
-                if block % 128 == 0
-                else [(z, rest) for z in range(4) for rest in range(low)]
-            )
-        )
-        for core in range(2)
-    )
-
+    w_mirror = lax.ppermute(w_share, "far", swap)
     own = (w_gate, w_up, w_down)
     other = tuple(lax.ppermute(w, "core", swap) for w in own)
     prepared = prepare_weights(own, other)
@@ -395,14 +369,21 @@
     seg_rows = jnp.zeros((16, kv.shape[1]), jnp.bfloat16).at[0, :tokens].set(segs.astype(jnp.bfloat16))
     prev = lax.ppermute(jnp.concatenate([kv, seg_rows], axis=0), blk, onward)
 
-    prepared, prev, rows_in = lax.optimization_barrier((prepared, prev, rows_in))
+    w_mirror, prepared, prev, rows_in = lax.optimization_barrier((w_mirror, prepared, prev, rows_in))
+    w_own, w_other = (
+        lax.all_gather(part, ("groups", "near", "low", "core"), axis=0, tiled=True).reshape(
+            parts, width // 2, share_cols
+        )
+        for part in (w_share, w_mirror)
+    )
+
     terms = experts(rows_in.reshape(owners * depth, 2 * width), *prepared)
     prev, terms = lax.optimization_barrier((prev, terms))
     back = lax.all_to_all(terms.reshape(owners, depth, width), chips, 0, 0, tiled=True)
     attention = attention_shares(queries, key_heads, value_heads, prev, segs)
 
     moe_input_grad, query_grad, key_part, value_part, sent = tail(
-        orders, back.reshape(owners * depth, width), place, moe_grad, w_own, w_other, *attention
+        back.reshape(owners * depth, width), place, moe_grad, w_own, w_other, *attention
     )
     later = lax.ppermute(sent, blk, backward).astype(jnp.float32)
     return (moe_input_grad, query_grad, key_part + later[0], value_part + later[1])

time: 271 us -> 233 us (0.86)
  waiting for transfers between devices: 172 us -> 130 us
  starting transfers between devices: 19.9 us -> 25.2 us
    all_gather x2, waiting for transfers between devices: 88.5 us -> 18.1 us  [local(): lax.all_gather(part, ('groups', 'near', 'low', 'core'), axis=0, tiled=True)]
    ppermute x1, waiting for transfers between devices: 48.3 us -> 66.4 us  [local(): prev = lax.ppermute(jnp.concatenate([kv, seg_rows], axis=0), blk, onward)]
    all_to_all x1, waiting for transfers between devices: 25.8 us -> 33.8 us  [local(): lax.all_to_all(terms.reshape(owners, depth, width), chips, 0, 0, tiled=True)]
    all_to_all x1, starting transfers between devices: 5.61 us -> 11.4 us  [local(): lax.all_to_all(terms.reshape(owners, depth, width), chips, 0, 0, tiled=True)]
    unnamed x44 -> x46, local copies, waits for them, and re-layouts: 14.8 us -> 15.8 us
  transfers between devices with their start and end apart: 10 -> 10, of which waited for: 8 -> 7; matrix products, arithmetic and copies ran while one was open for 0% -> 0% of each run, Pallas kernels for 10% -> 12%
where the time goes in v5:
time: 233 us; the launch traced here: 231 us
  waiting for transfers between devices  130 us (56%)
  Pallas kernels  43.6 us (19%)
  starting transfers between devices  25.2 us (11%)
  local copies, waits for them, and re-layouts  16.8 us (7%)
  between operations  14.2 us (6%)
    ppermute x1, waiting for transfers between devices, local(): prev = lax.ppermute(jnp.concatenate([kv, seg_rows], axis=0), blk, onward)  66.4 us
    all_to_all x1, waiting for transfers between devices, local(): lax.all_to_all(terms.reshape(owners, depth, width), chips, 0, 0, tiled=True)  33.8 us
    all_gather x2, waiting for transfers between devices, local(): lax.all_gather(part, ('groups', 'near', 'low', 'core'), axis=0, tiled=True)  18.1 us
    pallas_call x1, Pallas kernels, tail(): pl.pallas_call(functools.partial(tail_kernel, (heads, tiles)), grid=(step...  16.1 us
    unnamed x46, local copies, waits for them, and re-layouts  15.8 us
    pallas_call x1, Pallas kernels, experts(): pl.pallas_call(functools.partial(expert_kernel, steps), grid=(steps + wid...  14 us
    all_to_all x1, starting transfers between devices, local(): lax.all_to_all(terms.reshape(owners, depth, width), chips, 0, 0, tiled=True)  11.4 us
    pallas_call x1, Pallas kernels, prepare_weights(): pl.pallas_call(weights_kernel, grid=(steps,), in_specs=[cols, cols, down]...  8.75 us
  transfers between devices with their start and end apart: 10, of which 7 were waited for; matrix products, arithmetic and copies ran while one was open for 0% of the time, Pallas kernels for 12%

profile of v5, /device:TPU:13, one launch (start us, length us, event | category | flops | bytes accessed | tf_op | source)
XLA Modules:
  0.0 231.4 jit_solution(17785304065543877170)
XLA Ops:
  7.2 1.2 copy-done
  13.9 1.6 copy-done.1
  16.2 5.8 %all-to-all-start = ((bf16[8,48,4096]{2,1,0:T(8,128)(2,1)}), bf16[8,48,4096]{2,1,0:T(8,128)(2,1)}, u32[]{:S(2)}, u32[]{:S(2)}) async-start(bf16[8,48,4096]{2,1,0:T(8,128)(2,1)} %bitcast.22), calls=%async_computation | async-start | bytes 6291456 | tf_op jit(solution)/shard_map/all_to_all | solution.py:358
  22.0 1.3 collective-permute-start.1
  23.8 2.1 collective-permute-start
  25.9 1.9 collective-permute-start.4
  27.9 1.3 collective-permute-done.2.refs_4_
  29.2 2.4 %collective-permute-done.3.refs_5_ = bf16[384,2048]{1,0:T(8,128)(2,1)S(1)} collective-permute-done((bf16[384,2048]{1,0:T(8,128)(2,1)}, bf16[384,2048]{1,0:T(8,128)(2,1)S(1)}, u32[]{:S(2)}, u32[]{:S(2)}) %collective-permute-start.3) | collective-permute-done | bytes 1572896 | tf_op jit(solution)/shard_map/ppermute | solution.py:364
  32.7 1.4 copy-done.5
  34.1 1.4 copy-done.6
  35.6 8.8 %prepare_weights.1 = (bf16[3,2048,512]{2,1,0:T(8,128)(2,1)}, bf16[3,2048,256]{2,1,0:T(8,128)(2,1)}, bf16[3,512,2048]{2,1,0:T(8,128)(2,1)}) custom-call(bf16[2048,384]{1,0:T(8,128)(2,1)S(1)} %copy-done.4, bf16[2048,384]{1,0:T(8,128)(2,1)S(1)} %copy-done.5, bf16[384,2048]{1,0:T(8,128)(2,1)S(1)} %copy-done.6, bf16[2048,384]{1,0:T(8,128)(2,1)} %copy-done.19, ...), custom_call_target="tpu_custom_call" | custom-call | bytes 25165824 | tf_op jit(solution)/shard_map/prepare_weights/pallas_call | solution.py:93
  44.3 66.4 %collective-permute-done.4.prev_key_ref.prev_value_ref.prev_seg_ref = bf16[144,512]{1,0:T(8,128)(2,1)S(1)} collective-permute-done((bf16[144,512]{1,0:T(8,128)(2,1)S(1)}, bf16[144,512]{1,0:T(8,128)(2,1)S(1)}, u32[]{:S(2)}, u32[]{:S(2)}) %collective-permute-start.4) | collective-permute-done | bytes 147488 | tf_op jit(solution)/shard_map/ppermute | solution.py:370
  110.7 2.6 %collective-permute-done = bf16[128,2048]{1,0:T(8,128)(2,1)} collective-permute-done((bf16[128,2048]{1,0:T(8,128)(2,1)S(1)}, bf16[128,2048]{1,0:T(8,128)(2,1)}, u32[]{:S(2)}, u32[]{:S(2)}) %collective-permute-start) | collective-permute-done | bytes 524320 | tf_op jit(solution)/shard_map/ppermute | solution.py:362
  113.4 14.0 %expert_terms.1 = bf16[384,2048]{1,0:T(8,128)(2,1)} custom-call(bf16[384,4096]{1,0:T(8,128)(2,1)} %bitcast.4.rows_ref, bf16[3,2048,512]{2,1,0:T(8,128)(2,1)} %get-tuple-element.45.cols_ref, bf16[3,2048,256]{2,1,0:T(8,128)(2,1)} %get-tuple-element.46.down_ref, bf16[3,512,2048]{2,1,0:T(8,128)(2,1)} %get-tuple-element.47.back_ref), custom_call_target="tpu_custom_call" | custom-call | flops 6039797760 | bytes 20971520 | tf_op jit(solution)/shard_map/expert_terms/pallas_call | solution.py:146
  127.4 11.4 %all-to-all-start.1 = ((bf16[8,48,2048]{2,1,0:T(8,128)(2,1)}), bf16[8,48,2048]{2,1,0:T(8,128)(2,1)}, u32[]{:S(2)}, u32[]{:S(2)}) async-start(bf16[8,48,2048]{2,1,0:T(8,128)(2,1)} %bitcast.5), calls=%async_computation.1 | async-start | bytes 3145728 | tf_op jit(solution)/shard_map/all_to_all | solution.py:382
  138.9 3.5 %attention_shares.1 = (bf16[2,2048,256]{2,1,0:T(8,128)(2,1)S(1)}, bf16[2,256,2048]{2,1,0:T(8,128)(2,1)S(1)}, bf16[2,2048,128]{2,1,0:T(8,128)(2,1)S(1)}, bf16[2,2...) custom-call(bf16[128,4096]{1,0:T(8,128)(2,1)S(1)} %copy-done.14, bf16[128,256]{1,0:T(8,128)(2,1)S(1)} %copy-done.12, ...), custom_call_target="tpu_custom_call" | custom-call | flops 268435456 | bytes 8388608 | tf_op jit(solution)/shard_map/attention_shares/pallas_call | solution.py:205
  142.4 1.3 copy-done.2
  143.8 1.3 copy-done.3
  147.4 33.8 %all-to-all-done.1 = bf16[8,48,2048]{2,1,0:T(8,128)(2,1)} async-done(((bf16[8,48,2048]{2,1,0:T(8,128)(2,1)}), bf16[8,48,2048]{2,1,0:T(8,128)(2,1)}, u32[]{:S(2)}, u32[]{:S(2)}) %all-to-all-start.1) | async-done | bytes 1572896 | tf_op jit(solution)/shard_map/all_to_all | solution.py:382
  181.2 18.1 %all-gather.5.cloned.1.call-done = bf16[2048,2048]{1,0:T(8,128)(2,1)} async-done(((bf16[128,2048]{1,0:T(8,128)(2,1)}), bf16[2048,2048]{1,0:T(8,128)(2,1)}) %all-gather.5.cloned.1.call-update) | async-done | bytes 8388624 | tf_op jit(solution)/shard_map/all_gather | solution.py:374
  199.3 16.1 %tail_attention.1 = (bf16[128,2048]{1,0:T(8,128)(2,1)}, bf16[128,4096]{1,0:T(8,128)(2,1)}, f32[128,256]{1,0:T(8,128)}, f32[128,256]{1,0:T(8,128)}, bf16[2,128,256]{2,1,0:T(8,128)(2,1)}) custom-call(bf16[384,2048]{1,0:T(8,128)(2,1)} %bitcast.6.back_ref, bf16[128,384]{1,0:T(8,128)(2,1)} %copy-done.11, bf16[128,2048]{1,0:T(8,128)(2,1)} %grad_ref.3, ...), custom_call_target="tpu_custom_call" | custom-call | flops 2147483648 | bytes 23068672 | tf_op jit(solution)/shard_map/tail_attention/pallas_call | solution.py:289
  215.5 2.1 collective-permute-start.5
  217.6 5.2 %collective-permute-done.5 = bf16[2,128,256]{2,1,0:T(8,128)(2,1)S(1)} collective-permute-done((bf16[2,128,256]{2,1,0:T(8,128)(2,1)}, bf16[2,128,256]{2,1,0:T(8,128)(2,1)S(1)}, u32[]{:S(2)}, u32[]{:S(2)}) %collective-permute-start.5) | collective-permute-done | bytes 131104 | tf_op jit(solution)/shard_map/ppermute | solution.py:388
  222.9 1.7 fusion.2
  (55 shorter events, 10.3 us)
Async XLA Ops:
  7.2 1.2 copy-start
  7.2 174.1 %all-gather.3.cloned.1.call-start = ((), (), s32[]{:S(2)}) async-start(), calls=%async_computation.2 | async-start | bytes 8912896 | tf_op jit(solution)/shard_map/all_gather | solution.py:374
  13.9 1.6 copy-start.1
  16.1 5.8 %copy-start.4 = (bf16[2048,384]{1,0:T(8,128)(2,1)S(1)}, bf16[2048,384]{1,0:T(8,128)(2,1)}, u32[]{:S(2)}) copy-start(bf16[2048,384]{1,0:T(8,128)(2,1)} %refs_0_.1) | copy-start | bytes 4718596
  16.1 7.7 %copy-start.18 = (bf16[128,2048]{1,0:T(8,128)(2,1)S(1)}, bf16[128,2048]{1,0:T(8,128)(2,1)}, u32[]{:S(2)}) copy-start(bf16[128,2048]{1,0:T(8,128)(2,1)} %constant_dynamic-slice_fusion) | copy-start | bytes 1572868
  16.1 9.8 %copy-start.22 = (s32[128]{0:T(128)S(1)}, s32[128]{0:T(128)}, u32[]{:S(2)}) copy-start(s32[128]{0:T(128)} %param.25) | copy-start | bytes 1540
  16.1 9.8 %copy-start.12 = (bf16[128,256]{1,0:T(8,128)(2,1)S(1)}, bf16[128,256]{1,0:T(8,128)(2,1)}, u32[]{:S(2)}) copy-start(bf16[128,256]{1,0:T(8,128)(2,1)} %key_ref.1) | copy-start | bytes 196612
  16.2 9.8 %copy-start.13 = (bf16[128,256]{1,0:T(8,128)(2,1)S(1)}, bf16[128,256]{1,0:T(8,128)(2,1)}, u32[]{:S(2)}) copy-start(bf16[128,256]{1,0:T(8,128)(2,1)} %value_ref.1) | copy-start | bytes 196612
  16.2 97.2 %all-to-all-start = ((bf16[8,48,4096]{2,1,0:T(8,128)(2,1)}), bf16[8,48,4096]{2,1,0:T(8,128)(2,1)}, u32[]{:S(2)}, u32[]{:S(2)}) async-start(bf16[8,48,4096]{2,1,0:T(8,128)(2,1)} %bitcast.22), calls=%async_computation | async-start | bytes 6291456 | tf_op jit(solution)/shard_map/all_to_all | solution.py:358
  22.0 177.4 %all-gather.5.cloned.1.call-start = ((), (), s32[]{:S(2)}) async-start(), calls=%async_computation.3 | async-start | bytes 8912896 | tf_op jit(solution)/shard_map/all_gather | solution.py:374
  22.0 5.9 %collective-permute-start.1 = (bf16[2048,384]{1,0:T(8,128)(2,1)S(1)}, bf16[2048,384]{1,0:T(8,128)(2,1)S(1)}, u32[]{:S(2)}, u32[]{:S(2)}) collective-permute-start(bf16[2048,384]{1,0:T(8,128)(2,1)S(1)} %copy-done.4), channel_id=1, source_target_pairs={{0,1},{1,0},{2,3},{3,2},{4,5},{5,4},{6,7},{7,6},{8,9},{9,8},{10,11... | collective-permute-start | bytes 4718600 | tf_op jit(solution)/shard_map/ppermute | solution.py:364
  23.3 5.9 %collective-permute-start.2 = (bf16[2048,384]{1,0:T(8,128)(2,1)}, bf16[2048,384]{1,0:T(8,128)(2,1)S(1)}, u32[]{:S(2)}, u32[]{:S(2)}) collective-permute-start(bf16[2048,384]{1,0:T(8,128)(2,1)} %refs_1_.1), channel_id=1, source_target_pairs={{0,1},{1,0},{2,3},{3,2},{4,5},{5,4},{6,7},{7,6},{8,9},{9,8},{10,11... | collective-permute-start | bytes 4718600 | tf_op jit(solution)/shard_map/ppermute | solution.py:364
  23.4 8.2 %collective-permute-start.3 = (bf16[384,2048]{1,0:T(8,128)(2,1)}, bf16[384,2048]{1,0:T(8,128)(2,1)S(1)}, u32[]{:S(2)}, u32[]{:S(2)}) collective-permute-start(bf16[384,2048]{1,0:T(8,128)(2,1)} %refs_2_.1), channel_id=1, source_target_pairs={{0,1},{1,0},{2,3},{3,2},{4,5},{5,4},{6,7},{7,6},{8,9},{9,8},{10,11... | collective-permute-start | bytes 4718600 | tf_op jit(solution)/shard_map/ppermute | solution.py:364
  23.8 89.5 %collective-permute-start = (bf16[128,2048]{1,0:T(8,128)(2,1)S(1)}, bf16[128,2048]{1,0:T(8,128)(2,1)}, u32[]{:S(2)}, u32[]{:S(2)}) collective-permute-start(bf16[128,2048]{1,0:T(8,128)(2,1)S(1)} %copy-done.18), channel_id=1, source_target_pairs={{0,8},{8,0},{1,9},{9,1},{2,10},{10,2},{3,11},{11,3},{4,12},{12,4},... | collective-permute-start | bytes 1572872 | tf_op jit(solution)/shard_map/ppermute | solution.py:362
  25.9 84.8 %collective-permute-start.4 = (bf16[144,512]{1,0:T(8,128)(2,1)S(1)}, bf16[144,512]{1,0:T(8,128)(2,1)S(1)}, u32[]{:S(2)}, u32[]{:S(2)}) collective-permute-start(bf16[144,512]{1,0:T(8,128)(2,1)S(1)} %fusion.1), channel_id=1, source_target_pairs={{0,1},{1,2},{2,3},{3,4},{4,5},{5,6},{6,7},{7,8},{8,9},{9,10},{10,1... | collective-permute-start | bytes 442376 | tf_op jit(solution)/shard_map/ppermute | solution.py:370
  27.9 3.7 %copy-start.19 = (bf16[2048,384]{1,0:T(8,128)(2,1)}, bf16[2048,384]{1,0:T(8,128)(2,1)S(1)}, u32[]{:S(2)}) copy-start(bf16[2048,384]{1,0:T(8,128)(2,1)S(1)} %collective-permute-done.1.refs_3_) | copy-start | bytes 4718596
  29.2 2.4 %copy-start.20 = (bf16[2048,384]{1,0:T(8,128)(2,1)}, bf16[2048,384]{1,0:T(8,128)(2,1)S(1)}, u32[]{:S(2)}) copy-start(bf16[2048,384]{1,0:T(8,128)(2,1)S(1)} %collective-permute-done.2.refs_4_) | copy-start | bytes 4718596
  32.7 1.4 copy-start.5
  34.1 1.4 copy-start.6
  127.4 11.5 %copy-start.14 = (bf16[128,4096]{1,0:T(8,128)(2,1)S(1)}, bf16[128,4096]{1,0:T(8,128)(2,1)}, u32[]{:S(2)}) copy-start(bf16[128,4096]{1,0:T(8,128)(2,1)} %q_ref.1) | copy-start | bytes 3145732
  127.4 53.8 %all-to-all-start.1 = ((bf16[8,48,2048]{2,1,0:T(8,128)(2,1)}), bf16[8,48,2048]{2,1,0:T(8,128)(2,1)}, u32[]{:S(2)}, u32[]{:S(2)}) async-start(bf16[8,48,2048]{2,1,0:T(8,128)(2,1)} %bitcast.5), calls=%async_computation.1 | async-start | bytes 3145728 | tf_op jit(solution)/shard_map/all_to_all | solution.py:382
  142.4 1.4 copy-start.2
  143.8 1.3 copy-start.3
  215.5 7.4 %collective-permute-start.5 = (bf16[2,128,256]{2,1,0:T(8,128)(2,1)}, bf16[2,128,256]{2,1,0:T(8,128)(2,1)S(1)}, u32[]{:S(2)}, u32[]{:S(2)}) collective-permute-start(bf16[2,128,256]{2,1,0:T(8,128)(2,1)} %get-tuple-element.60), channel_id=1, source_target_pairs={{1,0},{2,1},{3,2},{4,3},{5,4},{6,5},{7,6},{8,7},{9,8},{10,9},{11,1... | collective-permute-start | bytes 393224 | tf_op jit(solution)/shard_map/ppermute | solution.py:388
  (9 other events, 7.5 us)
Sparse Core Ops, SparseCore 0:
  10.2 113.3 all-gather.2
  125.2 74.1 all-gather.4

commit v6 on v5

--- a/solution.py
+++ b/solution.py
@@ -227,42 +227,62 @@
 
 
 def tail_kernel(
-    plan, back_ref, place_ref, grad_ref, own_ref, other_ref, low_ref, turned_ref, q_ref, key_ref, value_ref,
-    moe_ref, query_out, key_out, value_out, sent_out, stream, held, sums,
+    plan, place_info, back_ref, place_ref, grad_ref, *refs
 ):
-    heads, tiles = plan
+    heads, tiles, blocks = plan
+    own_refs, other_refs, refs = refs[:4], refs[4:8], refs[8:]
+    low_ref, turned_ref, q_ref, key_ref, value_ref, *refs = refs
+    moe_ref, query_out, key_out, value_out, sent_out, stream, held, sums = refs
     step = pl.program_id(0)
     tokens = query_out.shape[0]
-    half = own_ref.shape[1]
 
     @pl.when(step == 0)
     def _():
         moe = dot(place_ref[...], back_ref[...]).astype(jnp.bfloat16)
         moe_ref[...] = moe
         added = (grad_ref[...].astype(jnp.float32) + moe.astype(jnp.float32)).astype(jnp.bfloat16)
-        low_half = lax.axis_index("far") == 0
-        stream[:, :half] = jnp.where(low_half, added[:, :half], added[:, half:])
-        stream[:, half:] = jnp.where(low_half, added[:, half:], added[:, :half])
+        size = added.shape[1] // (4 * blocks)
+        for far in range(2):
+            for core in range(2):
+                for rest in range(blocks):
+                    source = (far * blocks + rest) * 2 + core
+                    stream[2 * far + core, :, rest * size : (rest + 1) * size] = added[
+                        :, source * size : (source + 1) * size
+                    ]
         held[...] = jnp.zeros_like(held)
 
     @pl.when((step == 0) | ((step > 1) & ((step - 1) % tiles == 0)))
     def _():
         sums[...] = jnp.zeros_like(sums)
 
-    grads = held[...]
-    head_grad = (dot(stream[:, :half], own_ref[0]) + dot(stream[:, half:], other_ref[0])).astype(jnp.bfloat16)
-    low = low_ref[0].astype(jnp.float32)
-    prob_grad = dot(grads, value_ref[0])
-    row_dot = jnp.sum(low * prob_grad, axis=1, keepdims=True)
-    score_grad = (low * (prob_grad - row_dot) * (HD**-0.5)).astype(jnp.bfloat16)
-    query_grad = dot(score_grad, key_ref[0]).astype(jnp.bfloat16)
-    sums[0] += dot(score_grad, q_ref[0], TN)
-    sums[1] += dot(turned_ref[0], grads)
-    for head in range(heads):
-        cols = slice(head * HD, (head + 1) * HD)
-        rows = slice(head * tokens, (head + 1) * tokens)
-        query_out[:, cols] = query_grad[rows, :]
-        held[rows, :] = head_grad[:, cols]
+    def advance(w_refs):
+        far, core = place_info[1], place_info[2]
+        grads = held[...]
+        head_grad = None
+        for k, w_ref in enumerate(w_refs):
+            part = dot(stream[2 * (far ^ (k // 2)) + (core ^ (k % 2))], w_ref[...])
+            head_grad = part if head_grad is None else head_grad + part
+        head_grad = head_grad.astype(jnp.bfloat16)
+        low = low_ref[0].astype(jnp.float32)
+        prob_grad = dot(grads, value_ref[0])
+        row_dot = jnp.sum(low * prob_grad, axis=1, keepdims=True)
+        score_grad = (low * (prob_grad - row_dot) * (HD**-0.5)).astype(jnp.bfloat16)
+        query_grad = dot(score_grad, key_ref[0]).astype(jnp.bfloat16)
+        sums[0] += dot(score_grad, q_ref[0], TN)
+        sums[1] += dot(turned_ref[0], grads)
+        for head in range(heads):
+            cols = slice(head * HD, (head + 1) * HD)
+            rows = slice(head * tokens, (head + 1) * tokens)
+            query_out[:, cols] = query_grad[rows, :]
+            held[rows, :] = head_grad[:, cols]
+
+    @pl.when(step < tiles)
+    def _():
+        advance(own_refs)
+
+    @pl.when(step >= tiles)
+    def _():
+        advance(other_refs)
 
     @pl.when((step > 0) & (step % tiles == 0))
     def _():
@@ -271,43 +291,56 @@
         sent_out[...] = sums[:, :tokens, :].astype(jnp.bfloat16)
 
 
-def tail(back, place, moe_grad, w_own, w_other, low, turned, query, keys, values):
+def tail(place_info, blocks, back, place, moe_grad, w_own, w_other, low, turned, query, keys, values):
     tokens, width = moe_grad.shape
-    half, cols = w_own.shape[1:]
+    quarter, cols = w_own[0].shape
     span = keys.shape[1]
     heads = 4
     tile = heads * HD
     tiles = cols // tile
     steps = KVH * tiles
-    now = lambda i: jnp.minimum(i, steps - 1)
     was = lambda i: jnp.maximum(i - 1, 0)
-    whole = lambda shape: pl.BlockSpec(shape, lambda i: (0,) * len(shape))
-    group = lambda shape: pl.BlockSpec((1,) + shape, lambda i: (was(i) // tiles, 0, 0))
-    rows = lambda shape: pl.BlockSpec((1,) + shape, lambda i: (was(i) // tiles, was(i) % tiles, 0))
-    w_spec = pl.BlockSpec((1, half, tile), lambda i: (now(i) // tiles, 0, now(i) % tiles))
-    kv = pl.BlockSpec((tokens, HD), lambda i: (0, was(i) // tiles))
+    kv_group = lambda i, info: (was(i) // tiles) ^ info[0]
+    whole = lambda shape: pl.BlockSpec(shape, lambda i, info: (0,) * len(shape))
+    group = lambda shape: pl.BlockSpec((1,) + shape, lambda i, info: (kv_group(i, info), 0, 0))
+    rows = lambda shape: pl.BlockSpec((1,) + shape, lambda i, info: (kv_group(i, info), was(i) % tiles, 0))
+    own_spec = pl.BlockSpec((quarter, tile), lambda i, info: (0, jnp.minimum(i, tiles - 1)))
+    other_spec = pl.BlockSpec(
+        (quarter, tile), lambda i, info: (0, jnp.minimum(jnp.maximum(i - tiles, 0), tiles - 1))
+    )
+    kv = pl.BlockSpec((tokens, HD), lambda i, info: (0, kv_group(i, info)))
     return pl.pallas_call(
-        functools.partial(tail_kernel, (heads, tiles)),
-        grid=(steps + 1,),
-        in_specs=[
-            whole(back.shape),
-            whole(place.shape),
-            whole(moe_grad.shape),
-            w_spec,
-            w_spec,
-            rows((heads * tokens, span)),
-            pl.BlockSpec((1, span, heads * tokens), lambda i: (was(i) // tiles, 0, was(i) % tiles)),
-            rows((heads * tokens, HD)),
-            group((span, HD)),
-            group((HD, span)),
-        ],
-        out_specs=[
-            whole((tokens, width)),
-            pl.BlockSpec((tokens, tile), lambda i: (0, was(i))),
-            kv,
-            kv,
-            pl.BlockSpec((2, tokens, HD), lambda i: (0, 0, was(i) // tiles)),
-        ],
+        functools.partial(tail_kernel, (heads, tiles, blocks)),
+        grid_spec=pltpu.PrefetchScalarGridSpec(
+            num_scalar_prefetch=1,
+            grid=(steps + 1,),
+            in_specs=[whole(back.shape), whole(place.shape), whole(moe_grad.shape)]
+            + [own_spec] * 4
+            + [other_spec] * 4
+            + [
+                rows((heads * tokens, span)),
+                pl.BlockSpec(
+                    (1, span, heads * tokens), lambda i, info: (kv_group(i, info), 0, was(i) % tiles)
+                ),
+                rows((heads * tokens, HD)),
+                group((span, HD)),
+                group((HD, span)),
+            ],
+            out_specs=[
+                whole((tokens, width)),
+                pl.BlockSpec(
+                    (tokens, tile), lambda i, info: (0, kv_group(i, info) * tiles + was(i) % tiles)
+                ),
+                kv,
+                kv,
+                pl.BlockSpec((2, tokens, HD), lambda i, info: (0, 0, kv_group(i, info))),
+            ],
+            scratch_shapes=[
+                pltpu.VMEM((4, tokens, quarter), jnp.bfloat16),
+                pltpu.VMEM((heads * tokens, HD), jnp.bfloat16),
+                pltpu.VMEM((2, span, HD), jnp.float32),
+            ],
+        ),
         out_shape=(
             jax.ShapeDtypeStruct((tokens, width), jnp.bfloat16),
             jax.ShapeDtypeStruct((tokens, KVH * cols), jnp.bfloat16),
@@ -315,17 +348,12 @@
             jax.ShapeDtypeStruct((tokens, KVH * HD), jnp.float32),
             jax.ShapeDtypeStruct((2, tokens, KVH * HD), jnp.bfloat16),
         ),
-        scratch_shapes=[
-            pltpu.VMEM((tokens, width), jnp.bfloat16),
-            pltpu.VMEM((heads * tokens, HD), jnp.bfloat16),
-            pltpu.VMEM((2, span, HD), jnp.float32),
-        ],
         compiler_params=params(56),
         cost_estimate=pl.CostEstimate(
             flops=2 * tokens * width * KVH * cols, bytes_accessed=22 * MIB, transcendentals=0
         ),
         name="tail_attention",
-    )(back, place, moe_grad, w_own, w_other, low, turned, query, keys, values)
+    )(place_info, back, place, moe_grad, *w_own, *w_other, low, turned, query, keys, values)
 
 
 def local(
@@ -354,12 +382,17 @@
     onward = [(i, i + 1) for i in range(count - 1)]
     backward = [(i + 1, i) for i in range(count - 1)]
 
-    rows, place = pick(routes, route_weight, moe_input, moe_grad, owners, depth)
-    rows_in = lax.all_to_all(rows.reshape(owners, depth, 2 * width), chips, 0, 0, tiled=True)
-
     share_cols = w_out.shape[1] // parts
     w_share = lax.dynamic_slice_in_dim(w_out, lax.axis_index("groups") * share_cols, share_cols, 1)
     w_mirror = lax.ppermute(w_share, "far", swap)
+    w_near, w_far = (
+        lax.all_gather(part, ("near", "low"), axis=0, tiled=True) for part in (w_share, w_mirror)
+    )
+
+    rows, place = pick(routes, route_weight, moe_input, moe_grad, owners, depth)
+    rows_in = lax.all_to_all(rows.reshape(owners, depth, 2 * width), chips, 0, 0, tiled=True)
+    x_near = lax.ppermute(w_near, "groups", swap)
+
     own = (w_gate, w_up, w_down)
     other = tuple(lax.ppermute(w, "core", swap) for w in own)
     prepared = prepare_weights(own, other)
@@ -369,21 +402,20 @@
     seg_rows = jnp.zeros((16, kv.shape[1]), jnp.bfloat16).at[0, :tokens].set(segs.astype(jnp.bfloat16))
     prev = lax.ppermute(jnp.concatenate([kv, seg_rows], axis=0), blk, onward)
 
-    w_mirror, prepared, prev, rows_in = lax.optimization_barrier((w_mirror, prepared, prev, rows_in))
-    w_own, w_other = (
-        lax.all_gather(part, ("groups", "near", "low", "core"), axis=0, tiled=True).reshape(
-            parts, width // 2, share_cols
-        )
-        for part in (w_share, w_mirror)
-    )
-
+    rows_in, prepared, prev, w_near, w_far, x_near = lax.optimization_barrier(
+        (rows_in, prepared, prev, w_near, w_far, x_near)
+    )
+    x_far = lax.ppermute(w_far, "groups", swap)
     terms = experts(rows_in.reshape(owners * depth, 2 * width), *prepared)
     prev, terms = lax.optimization_barrier((prev, terms))
     back = lax.all_to_all(terms.reshape(owners, depth, width), chips, 0, 0, tiled=True)
     attention = attention_shares(queries, key_heads, value_heads, prev, segs)
+    both_cores = lambda *pieces: [w for piece in pieces for w in (piece, lax.ppermute(piece, "core", swap))]
 
     moe_input_grad, query_grad, key_part, value_part, sent = tail(
-        back.reshape(owners * depth, width), place, moe_grad, w_own, w_other, *attention
+        jnp.stack([lax.axis_index(axis) for axis in ("groups", "far", "core")]).astype(jnp.int32),
+        2 * low, back.reshape(owners * depth, width), place, moe_grad,
+        both_cores(w_near, w_far), both_cores(x_near, x_far), *attention,
     )
     later = lax.ppermute(sent, blk, backward).astype(jnp.float32)
     return (moe_input_grad, query_grad, key_part + later[0], value_part + later[1])

time: 233 us -> 254 us (1.090)
  waiting for transfers between devices: 130 us -> 142 us
  starting transfers between devices: 25.2 us -> 31.1 us
    ppermute x1, waiting for transfers between devices: 2.6 us -> 88.4 us  [local(): w_mirror = lax.ppermute(w_share, 'far', swap)]
    ppermute x1, waiting for transfers between devices: 66.4 us -> 0.01 us  [local(): prev = lax.ppermute(jnp.concatenate([kv, seg_rows], axis=0), blk, onward)]
    all_to_all x1, waiting for transfers between devices: 33.8 us -> 0.01 us  [local(): lax.all_to_all(terms.reshape(owners, depth, width), chips, 0, 0, tiled=True)]
    ppermute x0 -> x6, waiting for transfers between devices: none -> 21.1 us  [the longest x1 21.1 us: local(): x_far = lax.ppermute(w_far, 'groups', swap)]
    ppermute x0 -> x6, starting transfers between devices: none -> 7.08 us  [the longest x4 5.45 us: local(): lax.ppermute(piece, 'core', swap)]
    all_gather x2, waiting for transfers between devices: 18.1 us -> 24.4 us  [local(): lax.all_gather(part, ('near', 'low'), axis=0, tiled=True)]
    all_to_all x1, starting transfers between devices: 11.4 us -> 7.24 us  [local(): lax.all_to_all(terms.reshape(owners, depth, width), chips, 0, 0, tiled=True)]
    ppermute x1, starting transfers between devices: 1.92 us -> 4.65 us  [local(): prev = lax.ppermute(jnp.concatenate([kv, seg_rows], axis=0), blk, onward)]
  transfers between devices with their start and end apart: 10 -> 16, of which waited for: 7 -> 6; matrix products, arithmetic and copies ran while one was open for 0% -> 0% of each run, Pallas kernels for 12% -> 11%
where the time goes in v6:
time: 254 us; the launch traced here: 251 us
  waiting for transfers between devices  142 us (56%)
  Pallas kernels  44.8 us (18%)
  starting transfers between devices  31.1 us (12%)
  local copies, waits for them, and re-layouts  16.9 us (7%)
  between operations  14.2 us (6%)
    ppermute x1, waiting for transfers between devices, local(): w_mirror = lax.ppermute(w_share, 'far', swap)  88.4 us
    all_gather x2, waiting for transfers between devices, local(): lax.all_gather(part, ('near', 'low'), axis=0, tiled=True)  24.4 us
    ppermute x1, waiting for transfers between devices, local(): x_far = lax.ppermute(w_far, 'groups', swap)  21.1 us
    pallas_call x1, Pallas kernels, tail(): pl.pallas_call(functools.partial(tail_kernel, (heads, tiles, blocks)), gr...  17.4 us
    unnamed x46, local copies, waits for them, and re-layouts  16 us
    pallas_call x1, Pallas kernels, experts(): pl.pallas_call(functools.partial(expert_kernel, steps), grid=(steps + wid...  13.9 us
    pallas_call x1, Pallas kernels, prepare_weights(): pl.pallas_call(weights_kernel, grid=(steps,), in_specs=[cols, cols, down]...  8.77 us
    all_to_all x1, starting transfers between devices, local(): lax.all_to_all(terms.reshape(owners, depth, width), chips, 0, 0, tiled=True)  7.24 us
  transfers between devices with their start and end apart: 16, of which 6 were waited for; matrix products, arithmetic and copies ran while one was open for 0% of the time, Pallas kernels for 11%

profile of v6, /device:TPU:13, one launch (start us, length us, event | category | flops | bytes accessed | tf_op | source)
XLA Modules:
  0.0 251.4 jit_solution(11197244677097003969)
XLA Ops:
  7.2 1.2 copy-done
  13.9 1.7 copy-done.1
  16.2 5.8 %all-to-all-start = ((bf16[8,48,4096]{2,1,0:T(8,128)(2,1)}), bf16[8,48,4096]{2,1,0:T(8,128)(2,1)}, u32[]{:S(2)}, u32[]{:S(2)}) async-start(bf16[8,48,4096]{2,1,0:T(8,128)(2,1)} %bitcast.23), calls=%async_computation | async-start | bytes 6291456 | tf_op jit(solution)/shard_map/all_to_all | solution.py:393
  22.0 2.1 collective-permute-start.4
  24.2 88.4 %collective-permute-done.4 = bf16[128,2048]{1,0:T(8,128)(2,1)} collective-permute-done((bf16[128,2048]{1,0:T(8,128)(2,1)S(1)}, bf16[128,2048]{1,0:T(8,128)(2,1)}, u32[]{:S(2)}, u32[]{:S(2)}) %collective-permute-start.4) | collective-permute-done | bytes 524320 | tf_op jit(solution)/shard_map/ppermute | solution.py:387
  113.6 1.7 collective-permute-start
  115.8 4.6 %collective-permute-start.3 = (bf16[144,512]{1,0:T(8,128)(2,1)S(1)}, bf16[144,512]{1,0:T(8,128)(2,1)S(1)}, u32[]{:S(2)}, u32[]{:S(2)}) collective-permute-start(bf16[144,512]{1,0:T(8,128)(2,1)S(1)} %fusion.1), channel_id=1, source_target_pairs={{0,1},{1,2},{2,3},{3,4},{4,5},{5,6},{6,7},{7,8},{8,9},{9,10},{10,1... | collective-permute-start | bytes 442376 | tf_op jit(solution)/shard_map/ppermute | solution.py:403
  120.8 2.3 collective-permute-done.2.refs_5_
  124.3 1.4 copy-done.5
  125.7 1.4 copy-done.6
  127.1 8.8 %prepare_weights.1 = (bf16[3,2048,512]{2,1,0:T(8,128)(2,1)}, bf16[3,2048,256]{2,1,0:T(8,128)(2,1)}, bf16[3,512,2048]{2,1,0:T(8,128)(2,1)}) custom-call(bf16[2048,384]{1,0:T(8,128)(2,1)S(1)} %copy-done.4, bf16[2048,384]{1,0:T(8,128)(2,1)S(1)} %copy-done.5, bf16[384,2048]{1,0:T(8,128)(2,1)S(1)} %copy-done.6, bf16[2048,384]{1,0:T(8,128)(2,1)} %copy-done.19, ...), custom_call_target="tpu_custom_call" | custom-call | bytes 25165824 | tf_op jit(solution)/shard_map/prepare_weights/pallas_call | solution.py:93
  135.9 24.3 %all-gather.5.cloned.1.call-done.refs_2_ = bf16[512,2048]{1,0:T(8,128)(2,1)} async-done(((bf16[128,2048]{1,0:T(8,128)(2,1)}), bf16[512,2048]{1,0:T(8,128)(2,1)}) %all-gather.5.cloned.1.call-update) | async-done | bytes 2097168 | tf_op jit(solution)/shard_map/all_gather | solution.py:389
  160.9 13.9 %expert_terms.1 = bf16[384,2048]{1,0:T(8,128)(2,1)} custom-call(bf16[384,4096]{1,0:T(8,128)(2,1)} %bitcast.7.rows_ref, bf16[3,2048,512]{2,1,0:T(8,128)(2,1)} %get-tuple-element.47.cols_ref, bf16[3,2048,256]{2,1,0:T(8,128)(2,1)} %get-tuple-element.48.down_ref, bf16[3,512,2048]{2,1,0:T(8,128)(2,1)} %get-tuple-element.49.back_ref), custom_call_target="tpu_custom_call" | custom-call | flops 6039797760 | bytes 20971520 | tf_op jit(solution)/shard_map/expert_terms/pallas_call | solution.py:146
  174.8 7.2 %all-to-all-start.1 = ((bf16[8,48,2048]{2,1,0:T(8,128)(2,1)}), bf16[8,48,2048]{2,1,0:T(8,128)(2,1)}, u32[]{:S(2)}, u32[]{:S(2)}) async-start(bf16[8,48,2048]{2,1,0:T(8,128)(2,1)} %bitcast.8), calls=%async_computation.1 | async-start | bytes 3145728 | tf_op jit(solution)/shard_map/all_to_all | solution.py:411
  182.0 3.2 %collective-permute-start.7 = (bf16[512,2048]{1,0:T(8,128)(2,1)}, bf16[512,2048]{1,0:T(8,128)(2,1)}, u32[]{:S(2)}, u32[]{:S(2)}) collective-permute-start(bf16[512,2048]{1,0:T(8,128)(2,1)} %all-gather.5.cloned.1.call-done.refs_2_), channel_id=1, source_target_pairs={{0,1},{1,0},{2,3},{3,2},{4,5},{5,4},{6,7},{7,6},{8,9},{9,8},{10,11... | collective-permute-start | bytes 6291464 | tf_op jit(solution)/shard_map/ppermute | solution.py:413
  185.8 21.1 %collective-permute-done.9.refs_6_ = bf16[512,2048]{1,0:T(8,128)(2,1)} collective-permute-done((bf16[512,2048]{1,0:T(8,128)(2,1)}, bf16[512,2048]{1,0:T(8,128)(2,1)}, u32[]{:S(2)}, u32[]{:S(2)}) %collective-permute-start.9) | collective-permute-done | bytes 2097184 | tf_op jit(solution)/shard_map/ppermute | solution.py:408
  206.9 1.7 collective-permute-start.10
  209.4 3.5 %attention_shares.1 = (bf16[2,2048,256]{2,1,0:T(8,128)(2,1)S(1)}, bf16[2,256,2048]{2,1,0:T(8,128)(2,1)S(1)}, bf16[2,2048,128]{2,1,0:T(8,128)(2,1)S(1)}, bf16[2,2...) custom-call(bf16[128,4096]{1,0:T(8,128)(2,1)S(1)} %copy-done.14, bf16[128,256]{1,0:T(8,128)(2,1)S(1)} %copy-done.12, ...), custom_call_target="tpu_custom_call" | custom-call | flops 268435456 | bytes 8388608 | tf_op jit(solution)/shard_map/attention_shares/pallas_call | solution.py:205
  212.9 1.3 copy-done.2
  214.3 1.4 copy-done.3
  218.0 17.4 %tail_attention.1 = (bf16[128,2048]{1,0:T(8,128)(2,1)}, bf16[128,4096]{1,0:T(8,128)(2,1)}, f32[128,256]{1,0:T(8,128)}, f32[128,256]{1,0:T(8,128)}, bf16[2,128,256]{2,1,0:T(8,128)(2,1)}) custom-call(s32[3]{0:T(128)} %pad_add_fusion.place_info, bf16[384,2048]{1,0:T(8,128)(2,1)} %bitcast.9.back_ref, bf16[128,384]{1,0:T(8,128)(2,1)} %copy-done.11, ...), custom_call_target="tpu_custom_call" | custom-call | flops 2147483648 | bytes 23068672 | tf_op jit(solution)/shard_map/tail_attention/pallas_call | solution.py:312
  235.4 1.9 collective-permute-start.11
  237.3 5.5 %collective-permute-done.11 = bf16[2,128,256]{2,1,0:T(8,128)(2,1)S(1)} collective-permute-done((bf16[2,128,256]{2,1,0:T(8,128)(2,1)}, bf16[2,128,256]{2,1,0:T(8,128)(2,1)S(1)}, u32[]{:S(2)}, u32[]{:S(2)}) %collective-permute-start.11) | collective-permute-done | bytes 131104 | tf_op jit(solution)/shard_map/ppermute | solution.py:420
  242.8 1.7 fusion.2
  (68 shorter events, 13.4 us)
Async XLA Ops:
  7.2 105.4 %all-gather.3.cloned.1.call-start = ((), (), s32[]{:S(2)}) async-start(), calls=%async_computation.2 | async-start | bytes 2621440 | tf_op jit(solution)/shard_map/all_gather | solution.py:389
  16.2 5.8 %copy-start.18 = (bf16[128,2048]{1,0:T(8,128)(2,1)S(1)}, bf16[128,2048]{1,0:T(8,128)(2,1)}, u32[]{:S(2)}) copy-start(bf16[128,2048]{1,0:T(8,128)(2,1)} %constant_dynamic-slice_fusion) | copy-start | bytes 1572868
  16.2 97.4 %copy-start.4 = (bf16[2048,384]{1,0:T(8,128)(2,1)S(1)}, bf16[2048,384]{1,0:T(8,128)(2,1)}, u32[]{:S(2)}) copy-start(bf16[2048,384]{1,0:T(8,128)(2,1)} %refs_0_.1) | copy-start | bytes 4718596
  16.2 99.6 %copy-start.22 = (s32[128]{0:T(128)S(1)}, s32[128]{0:T(128)}, u32[]{:S(2)}) copy-start(s32[128]{0:T(128)} %param.25) | copy-start | bytes 1540
  16.2 99.6 %copy-start.12 = (bf16[128,256]{1,0:T(8,128)(2,1)S(1)}, bf16[128,256]{1,0:T(8,128)(2,1)}, u32[]{:S(2)}) copy-start(bf16[128,256]{1,0:T(8,128)(2,1)} %key_ref.1) | copy-start | bytes 196612
  16.2 99.6 %copy-start.13 = (bf16[128,256]{1,0:T(8,128)(2,1)S(1)}, bf16[128,256]{1,0:T(8,128)(2,1)}, u32[]{:S(2)}) copy-start(bf16[128,256]{1,0:T(8,128)(2,1)} %value_ref.1) | copy-start | bytes 196612
  16.2 144.0 %all-to-all-start = ((bf16[8,48,4096]{2,1,0:T(8,128)(2,1)}), bf16[8,48,4096]{2,1,0:T(8,128)(2,1)}, u32[]{:S(2)}, u32[]{:S(2)}) async-start(bf16[8,48,4096]{2,1,0:T(8,128)(2,1)} %bitcast.23), calls=%async_computation | async-start | bytes 6291456 | tf_op jit(solution)/shard_map/all_to_all | solution.py:393
  22.0 138.2 %all-gather.5.cloned.1.call-start = ((), (), s32[]{:S(2)}) async-start(), calls=%async_computation.3 | async-start | bytes 2621440 | tf_op jit(solution)/shard_map/all_gather | solution.py:389
  22.0 90.6 %collective-permute-start.4 = (bf16[128,2048]{1,0:T(8,128)(2,1)S(1)}, bf16[128,2048]{1,0:T(8,128)(2,1)}, u32[]{:S(2)}, u32[]{:S(2)}) collective-permute-start(bf16[128,2048]{1,0:T(8,128)(2,1)S(1)} %copy-done.18), channel_id=1, source_target_pairs={{0,8},{8,0},{1,9},{9,1},{2,10},{10,2},{3,11},{11,3},{4,12},{12,4},... | collective-permute-start | bytes 1572872 | tf_op jit(solution)/shard_map/ppermute | solution.py:387
  112.6 47.6 %collective-permute-start.5 = (bf16[512,2048]{1,0:T(8,128)(2,1)}, bf16[512,2048]{1,0:T(8,128)(2,1)}, u32[]{:S(2)}, u32[]{:S(2)}) collective-permute-start(bf16[512,2048]{1,0:T(8,128)(2,1)} %all-gather.3.cloned.1.call-done.refs_0_), channel_id=1, source_target_pairs={{0,16},{16,0},{1,17},{17,1},{2,18},{18,2},{3,19},{19,3},{4,20},{20... | collective-permute-start | bytes 6291464 | tf_op jit(solution)/shard_map/ppermute | solution.py:394
  113.6 6.9 %collective-permute-start = (bf16[2048,384]{1,0:T(8,128)(2,1)S(1)}, bf16[2048,384]{1,0:T(8,128)(2,1)S(1)}, u32[]{:S(2)}, u32[]{:S(2)}) collective-permute-start(bf16[2048,384]{1,0:T(8,128)(2,1)S(1)} %copy-done.4), channel_id=1, source_target_pairs={{0,1},{1,0},{2,3},{3,2},{4,5},{5,4},{6,7},{7,6},{8,9},{9,8},{10,11... | collective-permute-start | bytes 4718600 | tf_op jit(solution)/shard_map/ppermute | solution.py:397
  115.3 5.5 %collective-permute-start.1 = (bf16[2048,384]{1,0:T(8,128)(2,1)}, bf16[2048,384]{1,0:T(8,128)(2,1)S(1)}, u32[]{:S(2)}, u32[]{:S(2)}) collective-permute-start(bf16[2048,384]{1,0:T(8,128)(2,1)} %refs_1_.1), channel_id=1, source_target_pairs={{0,1},{1,0},{2,3},{3,2},{4,5},{5,4},{6,7},{7,6},{8,9},{9,8},{10,11... | collective-permute-start | bytes 4718600 | tf_op jit(solution)/shard_map/ppermute | solution.py:397
  115.3 7.8 %collective-permute-start.2 = (bf16[384,2048]{1,0:T(8,128)(2,1)}, bf16[384,2048]{1,0:T(8,128)(2,1)S(1)}, u32[]{:S(2)}, u32[]{:S(2)}) collective-permute-start(bf16[384,2048]{1,0:T(8,128)(2,1)} %refs_2_.1), channel_id=1, source_target_pairs={{0,1},{1,0},{2,3},{3,2},{4,5},{5,4},{6,7},{7,6},{8,9},{9,8},{10,11... | collective-permute-start | bytes 4718600 | tf_op jit(solution)/shard_map/ppermute | solution.py:397
  115.8 20.1 %collective-permute-start.3 = (bf16[144,512]{1,0:T(8,128)(2,1)S(1)}, bf16[144,512]{1,0:T(8,128)(2,1)S(1)}, u32[]{:S(2)}, u32[]{:S(2)}) collective-permute-start(bf16[144,512]{1,0:T(8,128)(2,1)S(1)} %fusion.1), channel_id=1, source_target_pairs={{0,1},{1,2},{2,3},{3,4},{4,5},{5,6},{6,7},{7,8},{8,9},{9,10},{10,1... | collective-permute-start | bytes 442376 | tf_op jit(solution)/shard_map/ppermute | solution.py:403
  120.5 2.6 %copy-start.19 = (bf16[2048,384]{1,0:T(8,128)(2,1)}, bf16[2048,384]{1,0:T(8,128)(2,1)S(1)}, u32[]{:S(2)}) copy-start(bf16[2048,384]{1,0:T(8,128)(2,1)S(1)} %collective-permute-done.refs_3_) | copy-start | bytes 4718596
  120.8 2.3 copy-start.20
  160.2 46.6 %collective-permute-start.9 = (bf16[512,2048]{1,0:T(8,128)(2,1)}, bf16[512,2048]{1,0:T(8,128)(2,1)}, u32[]{:S(2)}, u32[]{:S(2)}) collective-permute-start(bf16[512,2048]{1,0:T(8,128)(2,1)} %all-gather.5.cloned.1.call-done.refs_2_), channel_id=1, source_target_pairs={{0,16},{16,0},{1,17},{17,1},{2,18},{18,2},{3,19},{19,3},{4,20},{20... | collective-permute-start | bytes 6291464 | tf_op jit(solution)/shard_map/ppermute | solution.py:408
  174.8 34.6 %copy-start.14 = (bf16[128,4096]{1,0:T(8,128)(2,1)S(1)}, bf16[128,4096]{1,0:T(8,128)(2,1)}, u32[]{:S(2)}) copy-start(bf16[128,4096]{1,0:T(8,128)(2,1)} %q_ref.1) | copy-start | bytes 3145732
  174.8 43.2 %all-to-all-start.1 = ((bf16[8,48,2048]{2,1,0:T(8,128)(2,1)}), bf16[8,48,2048]{2,1,0:T(8,128)(2,1)}, u32[]{:S(2)}, u32[]{:S(2)}) async-start(bf16[8,48,2048]{2,1,0:T(8,128)(2,1)} %bitcast.8), calls=%async_computation.1 | async-start | bytes 3145728 | tf_op jit(solution)/shard_map/all_to_all | solution.py:411
  182.0 35.9 %collective-permute-start.7 = (bf16[512,2048]{1,0:T(8,128)(2,1)}, bf16[512,2048]{1,0:T(8,128)(2,1)}, u32[]{:S(2)}, u32[]{:S(2)}) collective-permute-start(bf16[512,2048]{1,0:T(8,128)(2,1)} %all-gather.5.cloned.1.call-done.refs_2_), channel_id=1, source_target_pairs={{0,1},{1,0},{2,3},{3,2},{4,5},{5,4},{6,7},{7,6},{8,9},{9,8},{10,11... | collective-permute-start | bytes 6291464 | tf_op jit(solution)/shard_map/ppermute | solution.py:413
  185.3 32.7 %collective-permute-start.6 = (bf16[512,2048]{1,0:T(8,128)(2,1)}, bf16[512,2048]{1,0:T(8,128)(2,1)}, u32[]{:S(2)}, u32[]{:S(2)}) collective-permute-start(bf16[512,2048]{1,0:T(8,128)(2,1)} %all-gather.3.cloned.1.call-done.refs_0_), channel_id=1, source_target_pairs={{0,1},{1,0},{2,3},{3,2},{4,5},{5,4},{6,7},{7,6},{8,9},{9,8},{10,11... | collective-permute-start | bytes 6291464 | tf_op jit(solution)/shard_map/ppermute | solution.py:413
  185.3 32.7 %collective-permute-start.8 = (bf16[512,2048]{1,0:T(8,128)(2,1)}, bf16[512,2048]{1,0:T(8,128)(2,1)}, u32[]{:S(2)}, u32[]{:S(2)}) collective-permute-start(bf16[512,2048]{1,0:T(8,128)(2,1)} %collective-permute-done.5.refs_4_), channel_id=1, source_target_pairs={{0,1},{1,0},{2,3},{3,2},{4,5},{5,4},{6,7},{7,6},{8,9},{9,8},{10,11... | collective-permute-start | bytes 6291464 | tf_op jit(solution)/shard_map/ppermute | solution.py:413
  206.9 11.1 %collective-permute-start.10 = (bf16[512,2048]{1,0:T(8,128)(2,1)}, bf16[512,2048]{1,0:T(8,128)(2,1)}, u32[]{:S(2)}, u32[]{:S(2)}) collective-permute-start(bf16[512,2048]{1,0:T(8,128)(2,1)} %collective-permute-done.9.refs_6_), channel_id=1, source_target_pairs={{0,1},{1,0},{2,3},{3,2},{4,5},{5,4},{6,7},{7,6},{8,9},{9,8},{10,11... | collective-permute-start | bytes 6291464 | tf_op jit(solution)/shard_map/ppermute | solution.py:413
  235.4 7.4 %collective-permute-start.11 = (bf16[2,128,256]{2,1,0:T(8,128)(2,1)}, bf16[2,128,256]{2,1,0:T(8,128)(2,1)S(1)}, u32[]{:S(2)}, u32[]{:S(2)}) collective-permute-start(bf16[2,128,256]{2,1,0:T(8,128)(2,1)} %get-tuple-element.64), channel_id=1, source_target_pairs={{1,0},{2,1},{3,2},{4,3},{5,4},{6,5},{7,6},{8,7},{9,8},{10,9},{11,1... | collective-permute-start | bytes 393224 | tf_op jit(solution)/shard_map/ppermute | solution.py:420
  (15 other events, 16.0 us)
Sparse Core Ops, SparseCore 0:
  10.1 78.9 all-gather.2
  112.7 47.4 all-gather.4

commit v7 on v5

--- a/solution.py
+++ b/solution.py
@@ -12,6 +12,7 @@
 HD = 128
 FLOOR = -1e30
 MIB = 1 << 20
+LIGHT = pl.CostEstimate(flops=0, bytes_accessed=0, transcendentals=0)
 
 NT = (((1,), (1,)), ((), ()))
 TN = (((0,), (0,)), ((), ()))
@@ -105,9 +106,7 @@
             jax.ShapeDtypeStruct((steps, 4 * tile, width), jnp.bfloat16),
         ),
         compiler_params=params(48),
-        cost_estimate=pl.CostEstimate(
-            flops=0, bytes_accessed=32 * width * half, transcendentals=0
-        ),
+        cost_estimate=LIGHT,
         name="prepare_weights",
     )(*own, *other)
 
@@ -156,10 +155,7 @@
         out_shape=jax.ShapeDtypeStruct((count, width), jnp.bfloat16),
         scratch_shapes=[pltpu.VMEM((steps, count, quad), jnp.bfloat16)],
         compiler_params=params(48),
-        cost_estimate=pl.CostEstimate(
-            flops=5 * count * width * steps * quad, bytes_accessed=20 * MIB,
-            transcendentals=count * steps * quad,
-        ),
+        cost_estimate=LIGHT,
         name="expert_terms",
     )(rows, cols, down, back)
 
@@ -218,31 +214,29 @@
         out_specs=[group(shape) for shape in shapes],
         out_shape=[made(shape) for shape in shapes],
         compiler_params=params(32),
-        cost_estimate=pl.CostEstimate(
-            flops=2 * tokens * width * span, bytes_accessed=8 * MIB,
-            transcendentals=tokens * span * KVH * GROUP,
-        ),
+        cost_estimate=LIGHT,
         name="attention_shares",
     )(queries, key_heads, value_heads, prev, prev, prev, segs[None, :], segs[:, None])
 
 
 def tail_kernel(
-    plan, back_ref, place_ref, grad_ref, own_ref, other_ref, low_ref, turned_ref, q_ref, key_ref, value_ref,
+    plan, back_ref, place_ref, grad_ref, own_ref, pair_ref, last_ref, low_ref, turned_ref, q_ref, key_ref, value_ref,
     moe_ref, query_out, key_out, value_out, sent_out, stream, held, sums,
 ):
     heads, tiles = plan
     step = pl.program_id(0)
     tokens = query_out.shape[0]
-    half = own_ref.shape[1]
+    spread, size = last_ref.shape[1:3]
 
     @pl.when(step == 0)
     def _():
         moe = dot(place_ref[...], back_ref[...]).astype(jnp.bfloat16)
         moe_ref[...] = moe
         added = (grad_ref[...].astype(jnp.float32) + moe.astype(jnp.float32)).astype(jnp.bfloat16)
-        low_half = lax.axis_index("far") == 0
-        stream[:, :half] = jnp.where(low_half, added[:, :half], added[:, half:])
-        stream[:, half:] = jnp.where(low_half, added[:, half:], added[:, :half])
+        for z in range(4):
+            for rest in range(spread):
+                source = z * spread + rest
+                stream[z, :, rest * size : (rest + 1) * size] = added[:, source * size : (source + 1) * size]
         held[...] = jnp.zeros_like(held)
 
     @pl.when((step == 0) | ((step > 1) & ((step - 1) % tiles == 0)))
@@ -250,7 +244,13 @@
         sums[...] = jnp.zeros_like(sums)
 
     grads = held[...]
-    head_grad = (dot(stream[:, :half], own_ref[0]) + dot(stream[:, half:], other_ref[0])).astype(jnp.bfloat16)
+    here = 2 * lax.axis_index("far") + lax.axis_index("near")
+    tile = last_ref.shape[3]
+    head_grad = dot(stream[here], own_ref[0].reshape(spread * size, tile))
+    for turn in range(2):
+        head_grad += dot(stream[here ^ (turn + 1)], pair_ref[0, :, turn].reshape(spread * size, tile))
+    head_grad += dot(stream[3 - here], last_ref[0].reshape(spread * size, tile))
+    head_grad = head_grad.astype(jnp.bfloat16)
     low = low_ref[0].astype(jnp.float32)
     prob_grad = dot(grads, value_ref[0])
     row_dot = jnp.sum(low * prob_grad, axis=1, keepdims=True)
@@ -271,9 +271,9 @@
         sent_out[...] = sums[:, :tokens, :].astype(jnp.bfloat16)
 
 
-def tail(back, place, moe_grad, w_own, w_other, low, turned, query, keys, values):
+def tail(back, place, moe_grad, w_own, w_pair, w_last, low, turned, query, keys, values):
     tokens, width = moe_grad.shape
-    half, cols = w_own.shape[1:]
+    spread, size, cols = w_last.shape[1:]
     span = keys.shape[1]
     heads = 4
     tile = heads * HD
@@ -284,7 +284,10 @@
     whole = lambda shape: pl.BlockSpec(shape, lambda i: (0,) * len(shape))
     group = lambda shape: pl.BlockSpec((1,) + shape, lambda i: (was(i) // tiles, 0, 0))
     rows = lambda shape: pl.BlockSpec((1,) + shape, lambda i: (was(i) // tiles, was(i) % tiles, 0))
-    w_spec = pl.BlockSpec((1, half, tile), lambda i: (now(i) // tiles, 0, now(i) % tiles))
+    pair_spec = pl.BlockSpec(
+        (1, spread, 2, size, tile), lambda i: (now(i) // tiles, 0, 0, 0, now(i) % tiles)
+    )
+    one_spec = pl.BlockSpec((1, spread, size, tile), lambda i: (now(i) // tiles, 0, 0, now(i) % tiles))
     kv = pl.BlockSpec((tokens, HD), lambda i: (0, was(i) // tiles))
     return pl.pallas_call(
         functools.partial(tail_kernel, (heads, tiles)),
@@ -293,8 +296,9 @@
             whole(back.shape),
             whole(place.shape),
             whole(moe_grad.shape),
-            w_spec,
-            w_spec,
+            one_spec,
+            pair_spec,
+            one_spec,
             rows((heads * tokens, span)),
             pl.BlockSpec((1, span, heads * tokens), lambda i: (was(i) // tiles, 0, was(i) % tiles)),
             rows((heads * tokens, HD)),
@@ -316,7 +320,7 @@
             jax.ShapeDtypeStruct((2, tokens, KVH * HD), jnp.bfloat16),
         ),
         scratch_shapes=[
-            pltpu.VMEM((tokens, width), jnp.bfloat16),
+            pltpu.VMEM((4, tokens, width // 4), jnp.bfloat16),
             pltpu.VMEM((heads * tokens, HD), jnp.bfloat16),
             pltpu.VMEM((2, span, HD), jnp.float32),
         ],
@@ -325,7 +329,7 @@
             flops=2 * tokens * width * KVH * cols, bytes_accessed=22 * MIB, transcendentals=0
         ),
         name="tail_attention",
-    )(back, place, moe_grad, w_own, w_other, low, turned, query, keys, values)
+    )(back, place, moe_grad, w_own, w_pair, w_last, low, turned, query, keys, values)
 
 
 def local(
@@ -354,36 +358,39 @@
     onward = [(i, i + 1) for i in range(count - 1)]
     backward = [(i + 1, i) for i in range(count - 1)]
 
-    rows, place = pick(routes, route_weight, moe_input, moe_grad, owners, depth)
-    rows_in = lax.all_to_all(rows.reshape(owners, depth, 2 * width), chips, 0, 0, tiled=True)
-
     share_cols = w_out.shape[1] // parts
     w_share = lax.dynamic_slice_in_dim(w_out, lax.axis_index("groups") * share_cols, share_cols, 1)
-    w_mirror = lax.ppermute(w_share, "far", swap)
-    own = (w_gate, w_up, w_down)
-    other = tuple(lax.ppermute(w, "core", swap) for w in own)
-    prepared = prepare_weights(own, other)
+    w_near = lax.ppermute(w_share, "near", swap)
+    w_far = lax.ppermute(w_share, "far", swap)
 
     kv = jnp.concatenate([key_heads, value_heads], axis=1)
     segs = (segments + 1).astype(jnp.float32)
     seg_rows = jnp.zeros((16, kv.shape[1]), jnp.bfloat16).at[0, :tokens].set(segs.astype(jnp.bfloat16))
     prev = lax.ppermute(jnp.concatenate([kv, seg_rows], axis=0), blk, onward)
 
-    w_mirror, prepared, prev, rows_in = lax.optimization_barrier((w_mirror, prepared, prev, rows_in))
-    w_own, w_other = (
-        lax.all_gather(part, ("groups", "near", "low", "core"), axis=0, tiled=True).reshape(
-            parts, width // 2, share_cols
-        )
-        for part in (w_share, w_mirror)
-    )
-
+    own = (w_gate, w_up, w_down)
+    other = tuple(lax.ppermute(w, "core", swap) for w in own)
+    rows, place = pick(routes, route_weight, moe_input, moe_grad, owners, depth)
+    rows, w_near, w_far, prev, other = lax.optimization_barrier((rows, w_near, w_far, prev, other))
+
+    rows_in = lax.all_to_all(rows.reshape(owners, depth, 2 * width), chips, 0, 0, tiled=True)
+    plane = ("groups", "low", "core")
+    w_own = lax.all_gather(w_share, plane, axis=0, tiled=False)
+    w_pair = lax.all_gather(jnp.stack([w_near, w_far]), plane, axis=0, tiled=False)
+    w_last = lax.ppermute(w_far, "near", swap)
+    prepared = prepare_weights(own, other)
+    attention = attention_shares(queries, key_heads, value_heads, prev, segs)
+
+    rows_in, prepared, attention, w_last = lax.optimization_barrier((rows_in, prepared, attention, w_last))
+    w_last = lax.all_gather(w_last, plane, axis=0, tiled=False)
+    split = lambda w: w.reshape((parts, 2 * low) + w.shape[1:])
     terms = experts(rows_in.reshape(owners * depth, 2 * width), *prepared)
-    prev, terms = lax.optimization_barrier((prev, terms))
+    terms, w_pair = lax.optimization_barrier((terms, w_pair))
     back = lax.all_to_all(terms.reshape(owners, depth, width), chips, 0, 0, tiled=True)
-    attention = attention_shares(queries, key_heads, value_heads, prev, segs)
 
     moe_input_grad, query_grad, key_part, value_part, sent = tail(
-        back.reshape(owners * depth, width), place, moe_grad, w_own, w_other, *attention
+        back.reshape(owners * depth, width), place, moe_grad,
+        split(w_own), split(w_pair), split(w_last), *attention,
     )
     later = lax.ppermute(sent, blk, backward).astype(jnp.float32)
     return (moe_input_grad, query_grad, key_part + later[0], value_part + later[1])

time: 233 us -> 254 us (1.090)
  waiting for transfers between devices: 130 us -> 156 us
  starting transfers between devices: 25.2 us -> 18.8 us
  other arithmetic: 1.74 us -> 4.32 us
    all_gather x2 -> x3, waiting for transfers between devices: 18.1 us -> 85.2 us  [the longest x1 46.5 us: local(): w_own = lax.all_gather(w_share, plane, axis=0, tiled=False)]
    ppermute x1, waiting for transfers between devices: 66.4 us -> 1.76 us  [local(): prev = lax.ppermute(jnp.concatenate([kv, seg_rows], axis=0), blk, onward)]
    ppermute x1 -> x3, waiting for transfers between devices: 2.6 us -> 54.7 us  [the longest x1 38.3 us: local(): w_last = lax.ppermute(w_far, 'near', swap)]
    all_to_all x1, waiting for transfers between devices: 33.8 us -> 0.01 us  [local(): lax.all_to_all(terms.reshape(owners, depth, width), chips, 0, 0, tiled=True)]
    all_to_all x1, waiting for transfers between devices: 0.01 us -> 8.77 us  [local(): lax.all_to_all(rows.reshape(owners, depth, 2 * width), chips, 0, 0, tiled...]
    all_to_all x1, starting transfers between devices: 11.4 us -> 6.71 us  [local(): lax.all_to_all(terms.reshape(owners, depth, width), chips, 0, 0, tiled=True)]
    ppermute x3, waiting for transfers between devices: 3.69 us -> 0.01 us  [local(): other = tuple((lax.ppermute(w, 'core', swap) for w in own))]
  transfers between devices with their start and end apart: 10 -> 13, of which waited for: 7 -> 8; matrix products, arithmetic and copies ran while one was open for 0% -> 1% of each run, Pallas kernels for 12% -> 11%
where the time goes in v7:
time: 254 us; the launch traced here: 253 us
  waiting for transfers between devices  156 us (61%)
  Pallas kernels  44.1 us (17%)
  starting transfers between devices  18.8 us (7%)
  local copies, waits for them, and re-layouts  15.6 us (6%)
  between operations  13.9 us (5%)
  other arithmetic  4.32 us (2%)
    all_gather x1, waiting for transfers between devices, local(): w_own = lax.all_gather(w_share, plane, axis=0, tiled=False)  46.5 us
    all_gather x1, waiting for transfers between devices, local(): w_last = lax.all_gather(w_last, plane, axis=0, tiled=False)  38.6 us
    ppermute x1, waiting for transfers between devices, local(): w_last = lax.ppermute(w_far, 'near', swap)  38.3 us
    pallas_call x1, Pallas kernels, tail(): pl.pallas_call(functools.partial(tail_kernel, (heads, tiles)), grid=(step...  16.2 us
    unnamed x46, local copies, waits for them, and re-layouts  15.4 us
    pallas_call x1, Pallas kernels, experts(): pl.pallas_call(functools.partial(expert_kernel, steps), grid=(steps + wid...  14 us
    ppermute x1, waiting for transfers between devices, local(): w_near = lax.ppermute(w_share, 'near', swap)  12.2 us
    pallas_call x1, Pallas kernels, prepare_weights(): pl.pallas_call(weights_kernel, grid=(steps,), in_specs=[cols, cols, down]...  9.11 us
  transfers between devices with their start and end apart: 13, of which 8 were waited for; matrix products, arithmetic and copies ran while one was open for 1% of the time, Pallas kernels for 11%

profile of v7, /device:TPU:13, one launch (start us, length us, event | category | flops | bytes accessed | tf_op | source)
XLA Modules:
  0.0 253.1 jit_solution(16553448286368887273)
XLA Ops:
  10.0 3.1 %collective-permute-start.2 = (bf16[144,512]{1,0:T(8,128)(2,1)S(1)}, bf16[144,512]{1,0:T(8,128)(2,1)S(1)}, u32[]{:S(2)}, u32[]{:S(2)}) collective-permute-start(bf16[144,512]{1,0:T(8,128)(2,1)S(1)} %fusion.1), channel_id=1, source_target_pairs={{0,1},{1,2},{2,3},{3,4},{4,5},{5,6},{6,7},{7,8},{8,9},{9,10},{10,1... | collective-permute-start | bytes 442376 | tf_op jit(solution)/shard_map/ppermute | solution.py:369
  13.5 1.8 collective-permute-done.2.prev_key_ref.prev_value_ref.prev_seg_ref
  19.3 1.2 pick_rows.1
  20.5 1.6 copy-done.1
  22.7 12.2 %collective-permute-done = bf16[128,2048]{1,0:T(8,128)(2,1)S(1)} collective-permute-done((bf16[128,2048]{1,0:T(8,128)(2,1)S(1)}, bf16[128,2048]{1,0:T(8,128)(2,1)S(1)}, u32[]{:S(2)}, u32[]{:S(2)}) %collective-permute-start) | collective-permute-done | bytes 524320 | tf_op jit(solution)/shard_map/ppermute | solution.py:363
  34.9 4.1 %collective-permute-done.1 = bf16[128,2048]{1,0:T(8,128)(2,1)S(1)} collective-permute-done((bf16[128,2048]{1,0:T(8,128)(2,1)S(1)}, bf16[128,2048]{1,0:T(8,128)(2,1)S(1)}, u32[]{:S(2)}, u32[]{:S(2)}) %collective-permute-start.1) | collective-permute-done | bytes 524320 | tf_op jit(solution)/shard_map/ppermute | solution.py:364
  41.7 4.5 %all-to-all-start = ((bf16[8,48,4096]{2,1,0:T(8,128)(2,1)}), bf16[8,48,4096]{2,1,0:T(8,128)(2,1)}, u32[]{:S(2)}, u32[]{:S(2)}) async-start(bf16[8,48,4096]{2,1,0:T(8,128)(2,1)} %bitcast.26), calls=%async_computation | async-start | bytes 6291456 | tf_op jit(solution)/shard_map/all_to_all | solution.py:376
  46.5 1.4 copy-done.5
  47.9 1.4 copy-done.6
  49.3 9.1 %prepare_weights.1 = (bf16[3,2048,512]{2,1,0:T(8,128)(2,1)}, bf16[3,2048,256]{2,1,0:T(8,128)(2,1)}, bf16[3,512,2048]{2,1,0:T(8,128)(2,1)}) custom-call(bf16[2048,384]{1,0:T(8,128)(2,1)S(1)} %copy-done.4, bf16[2048,384]{1,0:T(8,128)(2,1)S(1)} %copy-done.5, bf16[384,2048]{1,0:T(8,128)(2,1)S(1)} %copy-done.6, bf16[2048,384]{1,0:T(8,128)(2,1)} %copy-done.20, ...), custom_call_target="tpu_custom_call" | custom-call | tf_op jit(solution)/shard_map/prepare_weights/pallas_call | solution.py:94
  58.5 3.6 %attention_shares.1 = (bf16[2,2048,256]{2,1,0:T(8,128)(2,1)S(1)}, bf16[2,256,2048]{2,1,0:T(8,128)(2,1)S(1)}, bf16[2,2048,128]{2,1,0:T(8,128)(2,1)S(1)}, bf16[2,2...) custom-call(bf16[128,4096]{1,0:T(8,128)(2,1)S(1)} %copy-done.8, bf16[128,256]{1,0:T(8,128)(2,1)S(1)} %copy-done.10, ...), custom_call_target="tpu_custom_call" | custom-call | tf_op jit(solution)/shard_map/attention_shares/pallas_call | solution.py:201
  62.0 1.4 copy-done.2
  63.4 1.3 copy-done.3
  67.0 38.3 %collective-permute-done.6 = bf16[128,2048]{1,0:T(8,128)(2,1)S(1)} collective-permute-done((bf16[128,2048]{1,0:T(8,128)(2,1)}, bf16[128,2048]{1,0:T(8,128)(2,1)S(1)}, u32[]{:S(2)}, u32[]{:S(2)}) %collective-permute-start.6) | collective-permute-done | bytes 524320 | tf_op jit(solution)/shard_map/ppermute | solution.py:380
  105.3 8.8 %all-to-all-done = bf16[8,48,4096]{2,1,0:T(8,128)(2,1)} async-done(((bf16[8,48,4096]{2,1,0:T(8,128)(2,1)}), bf16[8,48,4096]{2,1,0:T(8,128)(2,1)}, u32[]{:S(2)}, u32[]{:S(2)}) %all-to-all-start) | async-done | bytes 3145760 | tf_op jit(solution)/shard_map/all_to_all | solution.py:376
  114.1 14.0 %expert_terms.1 = bf16[384,2048]{1,0:T(8,128)(2,1)} custom-call(bf16[384,4096]{1,0:T(8,128)(2,1)} %bitcast.6.rows_ref, bf16[3,2048,512]{2,1,0:T(8,128)(2,1)} %get-tuple-element.66.cols_ref, bf16[3,2048,256]{2,1,0:T(8,128)(2,1)} %get-tuple-element.67.down_ref, bf16[3,512,2048]{2,1,0:T(8,128)(2,1)} %get-tuple-element.68.back_ref), custom_call_target="tpu_custom_call" | custom-call | tf_op jit(solution)/shard_map/expert_terms/pallas_call | solution.py:145
  128.2 6.7 %all-to-all-start.1 = ((bf16[8,48,2048]{2,1,0:T(8,128)(2,1)}), bf16[8,48,2048]{2,1,0:T(8,128)(2,1)S(1)}, u32[]{:S(2)}, u32[]{:S(2)}) async-start(bf16[8,48,2048]{2,1,0:T(8,128)(2,1)} %bitcast.10), calls=%async_computation.1 | async-start | bytes 3145728 | tf_op jit(solution)/shard_map/all_to_all | solution.py:389
  134.9 46.5 %all-gather.9.cloned.1.call-done = bf16[1024,2048]{1,0:T(8,128)(2,1)} async-done(((bf16[128,2048]{1,0:T(8,128)(2,1)}), bf16[1024,2048]{1,0:T(8,128)(2,1)}) %all-gather.9.cloned.1.call-update) | async-done | bytes 4194320 | tf_op jit(solution)/shard_map/all_gather | solution.py:378
  181.4 38.6 %all-gather.11.cloned.1.call-done = bf16[1024,2048]{1,0:T(8,128)(2,1)} async-done(((bf16[128,2048]{1,0:T(8,128)(2,1)}), bf16[1024,2048]{1,0:T(8,128)(2,1)}) %all-gather.11.cloned.1.call-update) | async-done | bytes 4194320 | tf_op jit(solution)/shard_map/all_gather | solution.py:385
  220.1 1.1 copy-done.18
  221.2 16.2 %tail_attention.1 = (bf16[128,2048]{1,0:T(8,128)(2,1)}, bf16[128,4096]{1,0:T(8,128)(2,1)}, f32[128,256]{1,0:T(8,128)}, f32[128,256]{1,0:T(8,128)}, bf16[2,128,256]{2,1,0:T(8,128)(2,1)}) custom-call(bf16[384,2048]{1,0:T(8,128)(2,1)} %bitcast.30, bf16[128,384]{1,0:T(8,128)(2,1)} %copy-done.14, bf16[128,2048]{1,0:T(8,128)(2,1)} %grad_ref.3, ...), custom_call_target="tpu_custom_call" | custom-call | flops 2147483648 | bytes 23068672 | tf_op jit(solution)/shard_map/tail_attention/pallas_call | solution.py:292
  237.4 2.2 collective-permute-start.7
  239.6 5.2 %collective-permute-done.7 = bf16[2,128,256]{2,1,0:T(8,128)(2,1)S(1)} collective-permute-done((bf16[2,128,256]{2,1,0:T(8,128)(2,1)}, bf16[2,128,256]{2,1,0:T(8,128)(2,1)S(1)}, u32[]{:S(2)}, u32[]{:S(2)}) %collective-permute-start.7) | collective-permute-done | bytes 131104 | tf_op jit(solution)/shard_map/ppermute | solution.py:395
  244.9 1.7 fusion.2
  (63 shorter events, 13.0 us)
Async XLA Ops:
  7.2 6.0 %copy-start = (bf16[128,4096]{1,0:T(8,128)(2,1)S(1)}, bf16[128,4096]{1,0:T(8,128)(2,1)}, u32[]{:S(2)}) copy-start(bf16[128,4096]{1,0:T(8,128)(2,1)} %param.21) | copy-start | bytes 3145732
  7.2 121.0 %all-gather.7.cloned.1.call-start = ((), (), s32[]{:S(2)}) async-start(), calls=%async_computation.2 | async-start | bytes 9437184 | tf_op jit(solution)/shard_map/all_gather | solution.py:379
  7.2 31.8 %collective-permute-start.3 = (bf16[2048,384]{1,0:T(8,128)(2,1)}, bf16[2048,384]{1,0:T(8,128)(2,1)S(1)}, u32[]{:S(2)}, u32[]{:S(2)}) collective-permute-start(bf16[2048,384]{1,0:T(8,128)(2,1)} %refs_0_.1), channel_id=1, source_target_pairs={{0,1},{1,0},{2,3},{3,2},{4,5},{5,4},{6,7},{7,6},{8,9},{9,8},{10,11... | collective-permute-start | bytes 4718600 | tf_op jit(solution)/shard_map/ppermute | solution.py:372
  8.0 31.1 %collective-permute-start.4 = (bf16[2048,384]{1,0:T(8,128)(2,1)}, bf16[2048,384]{1,0:T(8,128)(2,1)}, u32[]{:S(2)}, u32[]{:S(2)}) collective-permute-start(bf16[2048,384]{1,0:T(8,128)(2,1)} %refs_1_.1), channel_id=1, source_target_pairs={{0,1},{1,0},{2,3},{3,2},{4,5},{5,4},{6,7},{7,6},{8,9},{9,8},{10,11... | collective-permute-start | bytes 4718600 | tf_op jit(solution)/shard_map/ppermute | solution.py:372
  8.0 31.0 %collective-permute-start.5 = (bf16[384,2048]{1,0:T(8,128)(2,1)}, bf16[384,2048]{1,0:T(8,128)(2,1)}, u32[]{:S(2)}, u32[]{:S(2)}) collective-permute-start(bf16[384,2048]{1,0:T(8,128)(2,1)} %refs_2_.1), channel_id=1, source_target_pairs={{0,1},{1,0},{2,3},{3,2},{4,5},{5,4},{6,7},{7,6},{8,9},{9,8},{10,11... | collective-permute-start | bytes 4718600 | tf_op jit(solution)/shard_map/ppermute | solution.py:372
  10.0 5.2 %collective-permute-start.2 = (bf16[144,512]{1,0:T(8,128)(2,1)S(1)}, bf16[144,512]{1,0:T(8,128)(2,1)S(1)}, u32[]{:S(2)}, u32[]{:S(2)}) collective-permute-start(bf16[144,512]{1,0:T(8,128)(2,1)S(1)} %fusion.1), channel_id=1, source_target_pairs={{0,1},{1,2},{2,3},{3,4},{4,5},{5,6},{6,7},{7,8},{8,9},{9,10},{10,1... | collective-permute-start | bytes 442376 | tf_op jit(solution)/shard_map/ppermute | solution.py:369
  13.2 27.7 %copy-start.19 = (bf16[128,2048]{1,0:T(8,128)(2,1)}, bf16[128,2048]{1,0:T(8,128)(2,1)S(1)}, u32[]{:S(2)}) copy-start(bf16[128,2048]{1,0:T(8,128)(2,1)S(1)} %constant_dynamic-slice_fusion) | copy-start | bytes 1572868
  13.2 21.7 %collective-permute-start = (bf16[128,2048]{1,0:T(8,128)(2,1)S(1)}, bf16[128,2048]{1,0:T(8,128)(2,1)S(1)}, u32[]{:S(2)}, u32[]{:S(2)}) collective-permute-start(bf16[128,2048]{1,0:T(8,128)(2,1)S(1)} %constant_dynamic-slice_fusion), channel_id=1, source_target_pairs={{0,4},{4,0},{1,5},{5,1},{2,6},{6,2},{3,7},{7,3},{8,12},{12,8},{9,1... | collective-permute-start | bytes 1572872 | tf_op jit(solution)/shard_map/ppermute | solution.py:363
  15.2 23.8 %collective-permute-start.1 = (bf16[128,2048]{1,0:T(8,128)(2,1)S(1)}, bf16[128,2048]{1,0:T(8,128)(2,1)S(1)}, u32[]{:S(2)}, u32[]{:S(2)}) collective-permute-start(bf16[128,2048]{1,0:T(8,128)(2,1)S(1)} %constant_dynamic-slice_fusion), channel_id=1, source_target_pairs={{0,8},{8,0},{1,9},{9,1},{2,10},{10,2},{3,11},{11,3},{4,12},{12,4},... | collective-permute-start | bytes 1572872 | tf_op jit(solution)/shard_map/ppermute | solution.py:364
  20.5 1.6 copy-start.1
  39.1 2.6 %copy-start.20 = (bf16[2048,384]{1,0:T(8,128)(2,1)}, bf16[2048,384]{1,0:T(8,128)(2,1)S(1)}, u32[]{:S(2)}) copy-start(bf16[2048,384]{1,0:T(8,128)(2,1)S(1)} %collective-permute-done.3.refs_3_) | copy-start | bytes 4718596
  41.0 140.5 %all-gather.9.cloned.1.call-start = ((), (), s32[]{:S(2)}) async-start(), calls=%async_computation.3 | async-start | bytes 4718592 | tf_op jit(solution)/shard_map/all_gather | solution.py:378
  41.7 4.8 %copy-start.4 = (bf16[2048,384]{1,0:T(8,128)(2,1)S(1)}, bf16[2048,384]{1,0:T(8,128)(2,1)}, u32[]{:S(2)}) copy-start(bf16[2048,384]{1,0:T(8,128)(2,1)} %refs_0_.1) | copy-start | bytes 4718596
  41.7 72.4 %all-to-all-start = ((bf16[8,48,4096]{2,1,0:T(8,128)(2,1)}), bf16[8,48,4096]{2,1,0:T(8,128)(2,1)}, u32[]{:S(2)}, u32[]{:S(2)}) async-start(bf16[8,48,4096]{2,1,0:T(8,128)(2,1)} %bitcast.26), calls=%async_computation | async-start | bytes 6291456 | tf_op jit(solution)/shard_map/all_to_all | solution.py:376
  46.3 173.8 %all-gather.11.cloned.1.call-start = ((), (), s32[]{:S(2)}) async-start(), calls=%async_computation.4 | async-start | bytes 4718592 | tf_op jit(solution)/shard_map/all_gather | solution.py:385
  46.3 59.0 %collective-permute-start.6 = (bf16[128,2048]{1,0:T(8,128)(2,1)}, bf16[128,2048]{1,0:T(8,128)(2,1)S(1)}, u32[]{:S(2)}, u32[]{:S(2)}) collective-permute-start(bf16[128,2048]{1,0:T(8,128)(2,1)} %copy-done.22), channel_id=1, source_target_pairs={{0,4},{4,0},{1,5},{5,1},{2,6},{6,2},{3,7},{7,3},{8,12},{12,8},{9,1... | collective-permute-start | bytes 1572872 | tf_op jit(solution)/shard_map/ppermute | solution.py:380
  46.5 1.4 copy-start.5
  47.9 1.4 copy-start.6
  49.3 9.1 %copy-start.8 = (bf16[128,4096]{1,0:T(8,128)(2,1)S(1)}, bf16[128,4096]{1,0:T(8,128)(2,1)}, u32[]{:S(2)}) copy-start(bf16[128,4096]{1,0:T(8,128)(2,1)} %q_ref.1) | copy-start | bytes 3145732
  49.3 9.1 %copy-start.10 = (bf16[128,256]{1,0:T(8,128)(2,1)S(1)}, bf16[128,256]{1,0:T(8,128)(2,1)}, u32[]{:S(2)}) copy-start(bf16[128,256]{1,0:T(8,128)(2,1)} %key_ref.1) | copy-start | bytes 196612
  49.3 9.1 %copy-start.11 = (bf16[128,256]{1,0:T(8,128)(2,1)S(1)}, bf16[128,256]{1,0:T(8,128)(2,1)}, u32[]{:S(2)}) copy-start(bf16[128,256]{1,0:T(8,128)(2,1)} %value_ref.1) | copy-start | bytes 196612
  105.3 8.8 %copy-start.21 = (bf16[128,2048]{1,0:T(8,128)(2,1)}, bf16[128,2048]{1,0:T(8,128)(2,1)S(1)}, u32[]{:S(2)}) copy-start(bf16[128,2048]{1,0:T(8,128)(2,1)S(1)} %collective-permute-done.6) | copy-start | bytes 1572868
  128.2 91.9 %all-to-all-start.1 = ((bf16[8,48,2048]{2,1,0:T(8,128)(2,1)}), bf16[8,48,2048]{2,1,0:T(8,128)(2,1)S(1)}, u32[]{:S(2)}, u32[]{:S(2)}) async-start(bf16[8,48,2048]{2,1,0:T(8,128)(2,1)} %bitcast.10), calls=%async_computation.1 | async-start | bytes 3145728 | tf_op jit(solution)/shard_map/all_to_all | solution.py:389
  237.4 7.4 %collective-permute-start.7 = (bf16[2,128,256]{2,1,0:T(8,128)(2,1)}, bf16[2,128,256]{2,1,0:T(8,128)(2,1)S(1)}, u32[]{:S(2)}, u32[]{:S(2)}) collective-permute-start(bf16[2,128,256]{2,1,0:T(8,128)(2,1)} %get-tuple-element.82), channel_id=1, source_target_pairs={{1,0},{2,1},{3,2},{4,3},{5,4},{6,5},{7,6},{8,7},{9,8},{10,9},{11,1... | collective-permute-start | bytes 393224 | tf_op jit(solution)/shard_map/ppermute | solution.py:395
  (12 other events, 11.0 us)
Sparse Core Ops, SparseCore 0:
  41.1 85.2 all-gather.6
  128.8 52.5 all-gather.8
  183.3 36.7 all-gather.10

commit v8 on v5

--- a/solution.py
+++ b/solution.py
@@ -12,6 +12,7 @@
 HD = 128
 FLOOR = -1e30
 MIB = 1 << 20
+LIGHT = pl.CostEstimate(flops=0, bytes_accessed=0, transcendentals=0)
 
 NT = (((1,), (1,)), ((), ()))
 TN = (((0,), (0,)), ((), ()))
@@ -105,9 +106,7 @@
             jax.ShapeDtypeStruct((steps, 4 * tile, width), jnp.bfloat16),
         ),
         compiler_params=params(48),
-        cost_estimate=pl.CostEstimate(
-            flops=0, bytes_accessed=32 * width * half, transcendentals=0
-        ),
+        cost_estimate=LIGHT,
         name="prepare_weights",
     )(*own, *other)
 
@@ -156,10 +155,7 @@
         out_shape=jax.ShapeDtypeStruct((count, width), jnp.bfloat16),
         scratch_shapes=[pltpu.VMEM((steps, count, quad), jnp.bfloat16)],
         compiler_params=params(48),
-        cost_estimate=pl.CostEstimate(
-            flops=5 * count * width * steps * quad, bytes_accessed=20 * MIB,
-            transcendentals=count * steps * quad,
-        ),
+        cost_estimate=LIGHT,
         name="expert_terms",
     )(rows, cols, down, back)
 
@@ -218,31 +214,24 @@
         out_specs=[group(shape) for shape in shapes],
         out_shape=[made(shape) for shape in shapes],
         compiler_params=params(32),
-        cost_estimate=pl.CostEstimate(
-            flops=2 * tokens * width * span, bytes_accessed=8 * MIB,
-            transcendentals=tokens * span * KVH * GROUP,
-        ),
+        cost_estimate=LIGHT,
         name="attention_shares",
     )(queries, key_heads, value_heads, prev, prev, prev, segs[None, :], segs[:, None])
 
 
 def tail_kernel(
-    plan, back_ref, place_ref, grad_ref, own_ref, other_ref, low_ref, turned_ref, q_ref, key_ref, value_ref,
+    plan, back_ref, place_ref, grad_ref, w_ref, low_ref, turned_ref, q_ref, key_ref, value_ref,
     moe_ref, query_out, key_out, value_out, sent_out, stream, held, sums,
 ):
     heads, tiles = plan
     step = pl.program_id(0)
     tokens = query_out.shape[0]
-    half = own_ref.shape[1]
 
     @pl.when(step == 0)
     def _():
         moe = dot(place_ref[...], back_ref[...]).astype(jnp.bfloat16)
         moe_ref[...] = moe
-        added = (grad_ref[...].astype(jnp.float32) + moe.astype(jnp.float32)).astype(jnp.bfloat16)
-        low_half = lax.axis_index("far") == 0
-        stream[:, :half] = jnp.where(low_half, added[:, :half], added[:, half:])
-        stream[:, half:] = jnp.where(low_half, added[:, half:], added[:, :half])
+        stream[...] = (grad_ref[...].astype(jnp.float32) + moe.astype(jnp.float32)).astype(jnp.bfloat16)
         held[...] = jnp.zeros_like(held)
 
     @pl.when((step == 0) | ((step > 1) & ((step - 1) % tiles == 0)))
@@ -250,7 +239,7 @@
         sums[...] = jnp.zeros_like(sums)
 
     grads = held[...]
-    head_grad = (dot(stream[:, :half], own_ref[0]) + dot(stream[:, half:], other_ref[0])).astype(jnp.bfloat16)
+    head_grad = dot(stream[...], w_ref[0]).astype(jnp.bfloat16)
     low = low_ref[0].astype(jnp.float32)
     prob_grad = dot(grads, value_ref[0])
     row_dot = jnp.sum(low * prob_grad, axis=1, keepdims=True)
@@ -271,9 +260,9 @@
         sent_out[...] = sums[:, :tokens, :].astype(jnp.bfloat16)
 
 
-def tail(back, place, moe_grad, w_own, w_other, low, turned, query, keys, values):
+def tail(back, place, moe_grad, w_all, low, turned, query, keys, values):
     tokens, width = moe_grad.shape
-    half, cols = w_own.shape[1:]
+    cols = w_all.shape[2]
     span = keys.shape[1]
     heads = 4
     tile = heads * HD
@@ -284,7 +273,7 @@
     whole = lambda shape: pl.BlockSpec(shape, lambda i: (0,) * len(shape))
     group = lambda shape: pl.BlockSpec((1,) + shape, lambda i: (was(i) // tiles, 0, 0))
     rows = lambda shape: pl.BlockSpec((1,) + shape, lambda i: (was(i) // tiles, was(i) % tiles, 0))
-    w_spec = pl.BlockSpec((1, half, tile), lambda i: (now(i) // tiles, 0, now(i) % tiles))
+    w_spec = pl.BlockSpec((1, width, tile), lambda i: (now(i) // tiles, 0, now(i) % tiles))
     kv = pl.BlockSpec((tokens, HD), lambda i: (0, was(i) // tiles))
     return pl.pallas_call(
         functools.partial(tail_kernel, (heads, tiles)),
@@ -294,7 +283,6 @@
             whole(place.shape),
             whole(moe_grad.shape),
             w_spec,
-            w_spec,
             rows((heads * tokens, span)),
             pl.BlockSpec((1, span, heads * tokens), lambda i: (was(i) // tiles, 0, was(i) % tiles)),
             rows((heads * tokens, HD)),
@@ -325,7 +313,7 @@
             flops=2 * tokens * width * KVH * cols, bytes_accessed=22 * MIB, transcendentals=0
         ),
         name="tail_attention",
-    )(back, place, moe_grad, w_own, w_other, low, turned, query, keys, values)
+    )(back, place, moe_grad, w_all, low, turned, query, keys, values)
 
 
 def local(
@@ -354,36 +342,28 @@
     onward = [(i, i + 1) for i in range(count - 1)]
     backward = [(i + 1, i) for i in range(count - 1)]
 
+    share_cols = w_out.shape[1] // parts
+    w_share = lax.dynamic_slice_in_dim(w_out, lax.axis_index("groups") * share_cols, share_cols, 1)
+    w_all = lax.all_gather(w_share, ("groups",) + blk, axis=0, tiled=True).reshape(parts, width, share_cols)
     rows, place = pick(routes, route_weight, moe_input, moe_grad, owners, depth)
     rows_in = lax.all_to_all(rows.reshape(owners, depth, 2 * width), chips, 0, 0, tiled=True)
-
-    share_cols = w_out.shape[1] // parts
-    w_share = lax.dynamic_slice_in_dim(w_out, lax.axis_index("groups") * share_cols, share_cols, 1)
-    w_mirror = lax.ppermute(w_share, "far", swap)
-    own = (w_gate, w_up, w_down)
-    other = tuple(lax.ppermute(w, "core", swap) for w in own)
-    prepared = prepare_weights(own, other)
 
     kv = jnp.concatenate([key_heads, value_heads], axis=1)
     segs = (segments + 1).astype(jnp.float32)
     seg_rows = jnp.zeros((16, kv.shape[1]), jnp.bfloat16).at[0, :tokens].set(segs.astype(jnp.bfloat16))
     prev = lax.ppermute(jnp.concatenate([kv, seg_rows], axis=0), blk, onward)
 
-    w_mirror, prepared, prev, rows_in = lax.optimization_barrier((w_mirror, prepared, prev, rows_in))
-    w_own, w_other = (
-        lax.all_gather(part, ("groups", "near", "low", "core"), axis=0, tiled=True).reshape(
-            parts, width // 2, share_cols
-        )
-        for part in (w_share, w_mirror)
-    )
-
+    own = (w_gate, w_up, w_down)
+    other = tuple(lax.ppermute(w, "core", swap) for w in own)
+    prepared = prepare_weights(own, other)
+    rows_in, prepared, prev = lax.optimization_barrier((rows_in, prepared, prev))
     terms = experts(rows_in.reshape(owners * depth, 2 * width), *prepared)
-    prev, terms = lax.optimization_barrier((prev, terms))
+    terms, prev = lax.optimization_barrier((terms, prev))
     back = lax.all_to_all(terms.reshape(owners, depth, width), chips, 0, 0, tiled=True)
     attention = attention_shares(queries, key_heads, value_heads, prev, segs)
 
     moe_input_grad, query_grad, key_part, value_part, sent = tail(
-        back.reshape(owners * depth, width), place, moe_grad, w_own, w_other, *attention
+        back.reshape(owners * depth, width), place, moe_grad, w_all, *attention
     )
     later = lax.ppermute(sent, blk, backward).astype(jnp.float32)
     return (moe_input_grad, query_grad, key_part + later[0], value_part + later[1])

time: 233 us -> 242 us (1.039)
  waiting for transfers between devices: 130 us -> 141 us
  starting transfers between devices: 25.2 us -> 19.7 us
    all_gather x2 -> x1, waiting for transfers between devices: 18.1 us -> 0.01 us  [local(): lax.all_gather(w_share, ('groups',) + blk, axis=0, tiled=True)]
    all_to_all x1, waiting for transfers between devices: 33.8 us -> 50.4 us  [local(): lax.all_to_all(terms.reshape(owners, depth, width), chips, 0, 0, tiled=True)]
    ppermute x1, waiting for transfers between devices: 66.4 us -> 81.5 us  [local(): prev = lax.ppermute(jnp.concatenate([kv, seg_rows], axis=0), blk, onward)]
    all_to_all x1, starting transfers between devices: 11.4 us -> 6.66 us  [local(): lax.all_to_all(terms.reshape(owners, depth, width), chips, 0, 0, tiled=True)]
    ppermute x1 -> x0, waiting for transfers between devices: 2.6 us -> none  [local(): w_mirror = lax.ppermute(w_share, 'far', swap)]
    unnamed x46 -> x44, local copies, waits for them, and re-layouts: 15.8 us -> 15.9 us
  transfers between devices with their start and end apart: 10 -> 8, of which waited for: 7 -> 6; matrix products, arithmetic and copies ran while one was open for 0% -> 0% of each run, Pallas kernels for 12% -> 12%
where the time goes in v8:
time: 242 us; the launch traced here: 238 us
  waiting for transfers between devices  141 us (58%)
  Pallas kernels  44.8 us (19%)
  starting transfers between devices  19.7 us (8%)
  local copies, waits for them, and re-layouts  16.8 us (7%)
  between operations  14.1 us (6%)
    ppermute x1, waiting for transfers between devices, local(): prev = lax.ppermute(jnp.concatenate([kv, seg_rows], axis=0), blk, onward)  81.5 us
    all_to_all x1, waiting for transfers between devices, local(): lax.all_to_all(terms.reshape(owners, depth, width), chips, 0, 0, tiled=True)  50.4 us
    pallas_call x1, Pallas kernels, tail(): pl.pallas_call(functools.partial(tail_kernel, (heads, tiles)), grid=(step...  16.1 us
    unnamed x44, local copies, waits for them, and re-layouts  15.9 us
    pallas_call x1, Pallas kernels, experts(): pl.pallas_call(functools.partial(expert_kernel, steps), grid=(steps + wid...  15.2 us
    pallas_call x1, Pallas kernels, prepare_weights(): pl.pallas_call(weights_kernel, grid=(steps,), in_specs=[cols, cols, down]...  8.79 us
    all_to_all x1, starting transfers between devices, local(): lax.all_to_all(terms.reshape(owners, depth, width), chips, 0, 0, tiled=True)  6.66 us
    all_to_all x1, starting transfers between devices, local(): lax.all_to_all(rows.reshape(owners, depth, 2 * width), chips, 0, 0, tiled...  5.8 us
  transfers between devices with their start and end apart: 8, of which 6 were waited for; matrix products, arithmetic and copies ran while one was open for 0% of the time, Pallas kernels for 12%

profile of v8, /device:TPU:13, one launch (start us, length us, event | category | flops | bytes accessed | tf_op | source)
XLA Modules:
  0.0 238.3 jit_solution(8886841045155147789)
XLA Ops:
  7.2 1.2 copy-done
  9.3 1.0 copy-done.9
  10.3 1.0 copy-done.15
  12.7 1.2 pick_rows.1
  13.9 1.6 copy-done.1
  16.2 5.8 %all-to-all-start = ((bf16[8,48,4096]{2,1,0:T(8,128)(2,1)}), bf16[8,48,4096]{2,1,0:T(8,128)(2,1)}, u32[]{:S(2)}, u32[]{:S(2)}) async-start(bf16[8,48,4096]{2,1,0:T(8,128)(2,1)} %bitcast.21), calls=%async_computation | async-start | bytes 6291456 | tf_op jit(solution)/shard_map/all_to_all | solution.py:349
  22.0 1.2 collective-permute-start
  23.8 3.0 %collective-permute-start.3 = (bf16[144,512]{1,0:T(8,128)(2,1)S(1)}, bf16[144,512]{1,0:T(8,128)(2,1)S(1)}, u32[]{:S(2)}, u32[]{:S(2)}) collective-permute-start(bf16[144,512]{1,0:T(8,128)(2,1)S(1)} %fusion.1), channel_id=1, source_target_pairs={{0,1},{1,2},{2,3},{3,4},{4,5},{5,6},{6,7},{7,8},{8,9},{9,10},{10,1... | collective-permute-start | bytes 442376 | tf_op jit(solution)/shard_map/ppermute | solution.py:354
  28.7 2.3 collective-permute-done.2.refs_5_
  31.0 1.2 copy-done.20
  32.2 1.4 copy-done.5
  33.6 1.4 copy-done.6
  35.0 8.8 %prepare_weights.1 = (bf16[3,2048,512]{2,1,0:T(8,128)(2,1)}, bf16[3,2048,256]{2,1,0:T(8,128)(2,1)}, bf16[3,512,2048]{2,1,0:T(8,128)(2,1)}) custom-call(bf16[2048,384]{1,0:T(8,128)(2,1)S(1)} %copy-done.4, bf16[2048,384]{1,0:T(8,128)(2,1)S(1)} %copy-done.5, bf16[384,2048]{1,0:T(8,128)(2,1)S(1)} %copy-done.6, bf16[2048,384]{1,0:T(8,128)(2,1)} %copy-done.18, ...), custom_call_target="tpu_custom_call" | custom-call | tf_op jit(solution)/shard_map/prepare_weights/pallas_call | solution.py:94
  43.8 81.5 %collective-permute-done.3.prev_key_ref.prev_value_ref.prev_seg_ref = bf16[144,512]{1,0:T(8,128)(2,1)S(1)} collective-permute-done((bf16[144,512]{1,0:T(8,128)(2,1)S(1)}, bf16[144,512]{1,0:T(8,128)(2,1)S(1)}, u32[]{:S(2)}, u32[]{:S(2)}) %collective-permute-start.3) | collective-permute-done | bytes 147488 | tf_op jit(solution)/shard_map/ppermute | solution.py:354
  125.4 15.2 %expert_terms.1 = bf16[384,2048]{1,0:T(8,128)(2,1)} custom-call(bf16[384,4096]{1,0:T(8,128)(2,1)} %bitcast.4.rows_ref, bf16[3,2048,512]{2,1,0:T(8,128)(2,1)} %get-tuple-element.43.cols_ref, bf16[3,2048,256]{2,1,0:T(8,128)(2,1)} %get-tuple-element.44.down_ref, bf16[3,512,2048]{2,1,0:T(8,128)(2,1)} %get-tuple-element.45.back_ref), custom_call_target="tpu_custom_call" | custom-call | tf_op jit(solution)/shard_map/expert_terms/pallas_call | solution.py:145
  140.6 6.7 %all-to-all-start.1 = ((bf16[8,48,2048]{2,1,0:T(8,128)(2,1)}), bf16[8,48,2048]{2,1,0:T(8,128)(2,1)}, u32[]{:S(2)}, u32[]{:S(2)}) async-start(bf16[8,48,2048]{2,1,0:T(8,128)(2,1)} %bitcast.5), calls=%async_computation.1 | async-start | bytes 3145728 | tf_op jit(solution)/shard_map/all_to_all | solution.py:362
  147.4 3.5 %attention_shares.1 = (bf16[2,2048,256]{2,1,0:T(8,128)(2,1)S(1)}, bf16[2,256,2048]{2,1,0:T(8,128)(2,1)S(1)}, bf16[2,2048,128]{2,1,0:T(8,128)(2,1)S(1)}, bf16[2,2...) custom-call(bf16[128,4096]{1,0:T(8,128)(2,1)S(1)} %copy-done.8, bf16[128,256]{1,0:T(8,128)(2,1)S(1)} %copy-done.10, ...), custom_call_target="tpu_custom_call" | custom-call | tf_op jit(solution)/shard_map/attention_shares/pallas_call | solution.py:201
  150.9 1.4 copy-done.2
  152.3 1.3 copy-done.3
  155.9 50.4 %all-to-all-done.1 = bf16[8,48,2048]{2,1,0:T(8,128)(2,1)} async-done(((bf16[8,48,2048]{2,1,0:T(8,128)(2,1)}), bf16[8,48,2048]{2,1,0:T(8,128)(2,1)}, u32[]{:S(2)}, u32[]{:S(2)}) %all-to-all-start.1) | async-done | bytes 1572896 | tf_op jit(solution)/shard_map/all_to_all | solution.py:362
  206.3 16.1 %tail_attention.1 = (bf16[128,2048]{1,0:T(8,128)(2,1)}, bf16[128,4096]{1,0:T(8,128)(2,1)}, f32[128,256]{1,0:T(8,128)}, f32[128,256]{1,0:T(8,128)}, bf16[2,128,256]{2,1,0:T(8,128)(2,1)}) custom-call(bf16[384,2048]{1,0:T(8,128)(2,1)} %bitcast.6.back_ref, bf16[128,384]{1,0:T(8,128)(2,1)} %copy-done.14, bf16[128,2048]{1,0:T(8,128)(2,1)} %grad_ref.3, ...), custom_call_target="tpu_custom_call" | custom-call | flops 2147483648 | bytes 23068672 | tf_op jit(solution)/shard_map/tail_attention/pallas_call | solution.py:278
  222.4 2.4 collective-permute-start.4
  224.7 5.0 %collective-permute-done.4 = bf16[2,128,256]{2,1,0:T(8,128)(2,1)S(1)} collective-permute-done((bf16[2,128,256]{2,1,0:T(8,128)(2,1)}, bf16[2,128,256]{2,1,0:T(8,128)(2,1)S(1)}, u32[]{:S(2)}, u32[]{:S(2)}) %collective-permute-start.4) | collective-permute-done | bytes 131104 | tf_op jit(solution)/shard_map/ppermute | solution.py:368
  229.8 1.7 fusion.2
  (48 shorter events, 7.8 us)
Async XLA Ops:
  7.2 1.2 copy-start
  7.2 199.1 %all-gather.2.cloned.1.call-start = ((), (), s32[]{:S(2)}) async-start(), calls=%async_computation.2 | async-start | bytes 17301504 | tf_op jit(solution)/shard_map/all_gather | solution.py:347
  9.3 1.0 copy-start.9
  10.3 1.0 copy-start.15
  13.9 1.6 copy-start.1
  16.1 5.8 %copy-start.4 = (bf16[2048,384]{1,0:T(8,128)(2,1)S(1)}, bf16[2048,384]{1,0:T(8,128)(2,1)}, u32[]{:S(2)}) copy-start(bf16[2048,384]{1,0:T(8,128)(2,1)} %refs_0_.1) | copy-start | bytes 4718596
  16.1 7.6 %copy-start.21 = (s32[128]{0:T(128)S(1)}, s32[128]{0:T(128)}, u32[]{:S(2)}) copy-start(s32[128]{0:T(128)} %param.25) | copy-start | bytes 1540
  16.1 7.6 %copy-start.10 = (bf16[128,256]{1,0:T(8,128)(2,1)S(1)}, bf16[128,256]{1,0:T(8,128)(2,1)}, u32[]{:S(2)}) copy-start(bf16[128,256]{1,0:T(8,128)(2,1)} %key_ref.1) | copy-start | bytes 196612
  16.1 7.6 %copy-start.11 = (bf16[128,256]{1,0:T(8,128)(2,1)S(1)}, bf16[128,256]{1,0:T(8,128)(2,1)}, u32[]{:S(2)}) copy-start(bf16[128,256]{1,0:T(8,128)(2,1)} %value_ref.1) | copy-start | bytes 196612
  16.2 109.2 %all-to-all-start = ((bf16[8,48,4096]{2,1,0:T(8,128)(2,1)}), bf16[8,48,4096]{2,1,0:T(8,128)(2,1)}, u32[]{:S(2)}, u32[]{:S(2)}) async-start(bf16[8,48,4096]{2,1,0:T(8,128)(2,1)} %bitcast.21), calls=%async_computation | async-start | bytes 6291456 | tf_op jit(solution)/shard_map/all_to_all | solution.py:349
  22.0 5.8 %collective-permute-start = (bf16[2048,384]{1,0:T(8,128)(2,1)S(1)}, bf16[2048,384]{1,0:T(8,128)(2,1)S(1)}, u32[]{:S(2)}, u32[]{:S(2)}) collective-permute-start(bf16[2048,384]{1,0:T(8,128)(2,1)S(1)} %copy-done.4), channel_id=1, source_target_pairs={{0,1},{1,0},{2,3},{3,2},{4,5},{5,4},{6,7},{7,6},{8,9},{9,8},{10,11... | collective-permute-start | bytes 4718600 | tf_op jit(solution)/shard_map/ppermute | solution.py:357
  23.2 5.5 %collective-permute-start.1 = (bf16[2048,384]{1,0:T(8,128)(2,1)}, bf16[2048,384]{1,0:T(8,128)(2,1)S(1)}, u32[]{:S(2)}, u32[]{:S(2)}) collective-permute-start(bf16[2048,384]{1,0:T(8,128)(2,1)} %refs_1_.1), channel_id=1, source_target_pairs={{0,1},{1,0},{2,3},{3,2},{4,5},{5,4},{6,7},{7,6},{8,9},{9,8},{10,11... | collective-permute-start | bytes 4718600 | tf_op jit(solution)/shard_map/ppermute | solution.py:357
  23.3 7.8 %collective-permute-start.2 = (bf16[384,2048]{1,0:T(8,128)(2,1)}, bf16[384,2048]{1,0:T(8,128)(2,1)S(1)}, u32[]{:S(2)}, u32[]{:S(2)}) collective-permute-start(bf16[384,2048]{1,0:T(8,128)(2,1)} %refs_2_.1), channel_id=1, source_target_pairs={{0,1},{1,0},{2,3},{3,2},{4,5},{5,4},{6,7},{7,6},{8,9},{9,8},{10,11... | collective-permute-start | bytes 4718600 | tf_op jit(solution)/shard_map/ppermute | solution.py:357
  23.8 101.6 %collective-permute-start.3 = (bf16[144,512]{1,0:T(8,128)(2,1)S(1)}, bf16[144,512]{1,0:T(8,128)(2,1)S(1)}, u32[]{:S(2)}, u32[]{:S(2)}) collective-permute-start(bf16[144,512]{1,0:T(8,128)(2,1)S(1)} %fusion.1), channel_id=1, source_target_pairs={{0,1},{1,2},{2,3},{3,4},{4,5},{5,6},{6,7},{7,8},{8,9},{9,10},{10,1... | collective-permute-start | bytes 442376 | tf_op jit(solution)/shard_map/ppermute | solution.py:354
  27.8 3.3 %copy-start.18 = (bf16[2048,384]{1,0:T(8,128)(2,1)}, bf16[2048,384]{1,0:T(8,128)(2,1)S(1)}, u32[]{:S(2)}) copy-start(bf16[2048,384]{1,0:T(8,128)(2,1)S(1)} %collective-permute-done.refs_3_) | copy-start | bytes 4718596
  28.7 2.3 copy-start.19
  31.0 1.2 copy-start.20
  32.2 1.4 copy-start.5
  33.6 1.4 copy-start.6
  140.6 6.8 %copy-start.8 = (bf16[128,4096]{1,0:T(8,128)(2,1)S(1)}, bf16[128,4096]{1,0:T(8,128)(2,1)}, u32[]{:S(2)}) copy-start(bf16[128,4096]{1,0:T(8,128)(2,1)} %q_ref.1) | copy-start | bytes 3145732
  140.6 65.7 %all-to-all-start.1 = ((bf16[8,48,2048]{2,1,0:T(8,128)(2,1)}), bf16[8,48,2048]{2,1,0:T(8,128)(2,1)}, u32[]{:S(2)}, u32[]{:S(2)}) async-start(bf16[8,48,2048]{2,1,0:T(8,128)(2,1)} %bitcast.5), calls=%async_computation.1 | async-start | bytes 3145728 | tf_op jit(solution)/shard_map/all_to_all | solution.py:362
  150.9 1.4 copy-start.2
  152.3 1.3 copy-start.3
  222.4 7.4 %collective-permute-start.4 = (bf16[2,128,256]{2,1,0:T(8,128)(2,1)}, bf16[2,128,256]{2,1,0:T(8,128)(2,1)S(1)}, u32[]{:S(2)}, u32[]{:S(2)}) collective-permute-start(bf16[2,128,256]{2,1,0:T(8,128)(2,1)} %get-tuple-element.58), channel_id=1, source_target_pairs={{1,0},{2,1},{3,2},{4,3},{5,4},{6,5},{7,6},{8,7},{9,8},{10,9},{11,1... | collective-permute-start | bytes 393224 | tf_op jit(solution)/shard_map/ppermute | solution.py:368
  (6 other events, 4.3 us)
Sparse Core Ops, SparseCore 0:
  11.5 190.9 all-gather.1

commit v9 on v6

--- a/solution.py
+++ b/solution.py
@@ -12,6 +12,7 @@
 HD = 128
 FLOOR = -1e30
 MIB = 1 << 20
+LIGHT = pl.CostEstimate(flops=0, bytes_accessed=0, transcendentals=0)
 
 NT = (((1,), (1,)), ((), ()))
 TN = (((0,), (0,)), ((), ()))
@@ -105,9 +106,7 @@
             jax.ShapeDtypeStruct((steps, 4 * tile, width), jnp.bfloat16),
         ),
         compiler_params=params(48),
-        cost_estimate=pl.CostEstimate(
-            flops=0, bytes_accessed=32 * width * half, transcendentals=0
-        ),
+        cost_estimate=LIGHT,
         name="prepare_weights",
     )(*own, *other)
 
@@ -156,10 +155,7 @@
         out_shape=jax.ShapeDtypeStruct((count, width), jnp.bfloat16),
         scratch_shapes=[pltpu.VMEM((steps, count, quad), jnp.bfloat16)],
         compiler_params=params(48),
-        cost_estimate=pl.CostEstimate(
-            flops=5 * count * width * steps * quad, bytes_accessed=20 * MIB,
-            transcendentals=count * steps * quad,
-        ),
+        cost_estimate=LIGHT,
         name="expert_terms",
     )(rows, cols, down, back)
 
@@ -218,10 +214,7 @@
         out_specs=[group(shape) for shape in shapes],
         out_shape=[made(shape) for shape in shapes],
         compiler_params=params(32),
-        cost_estimate=pl.CostEstimate(
-            flops=2 * tokens * width * span, bytes_accessed=8 * MIB,
-            transcendentals=tokens * span * KVH * GROUP,
-        ),
+        cost_estimate=LIGHT,
         name="attention_shares",
     )(queries, key_heads, value_heads, prev, prev, prev, segs[None, :], segs[:, None])
 
@@ -229,38 +222,34 @@
 def tail_kernel(
     plan, place_info, back_ref, place_ref, grad_ref, *refs
 ):
-    heads, tiles, blocks = plan
-    own_refs, other_refs, refs = refs[:4], refs[4:8], refs[8:]
-    low_ref, turned_ref, q_ref, key_ref, value_ref, *refs = refs
+    heads, tiles = plan
+    own_ref, pair_ref, own_across, own_swapped, pair_across, pair_swapped, last_ref, low_ref, turned_ref, q_ref, key_ref, value_ref, *refs = refs
     moe_ref, query_out, key_out, value_out, sent_out, stream, held, sums = refs
     step = pl.program_id(0)
     tokens = query_out.shape[0]
+    part_size = stream.shape[2]
+    half = last_ref.shape[1] // 2
+    here, core = place_info[1], place_info[2]
 
     @pl.when(step == 0)
     def _():
         moe = dot(place_ref[...], back_ref[...]).astype(jnp.bfloat16)
         moe_ref[...] = moe
         added = (grad_ref[...].astype(jnp.float32) + moe.astype(jnp.float32)).astype(jnp.bfloat16)
-        size = added.shape[1] // (4 * blocks)
-        for far in range(2):
-            for core in range(2):
-                for rest in range(blocks):
-                    source = (far * blocks + rest) * 2 + core
-                    stream[2 * far + core, :, rest * size : (rest + 1) * size] = added[
-                        :, source * size : (source + 1) * size
-                    ]
+        for eighth in range(8):
+            stream[eighth] = added[:, eighth * part_size : (eighth + 1) * part_size]
         held[...] = jnp.zeros_like(held)
 
     @pl.when((step == 0) | ((step > 1) & ((step - 1) % tiles == 0)))
     def _():
         sums[...] = jnp.zeros_like(sums)
 
-    def advance(w_refs):
-        far, core = place_info[1], place_info[2]
+    def advance(pieces):
         grads = held[...]
         head_grad = None
-        for k, w_ref in enumerate(w_refs):
-            part = dot(stream[2 * (far ^ (k // 2)) + (core ^ (k % 2))], w_ref[...])
+        for turn, side, piece in pieces:
+            rows = stream[2 * (here ^ turn) + side]
+            part = dot(rows, piece.reshape(part_size, piece.shape[-1]))
             head_grad = part if head_grad is None else head_grad + part
         head_grad = head_grad.astype(jnp.bfloat16)
         low = low_ref[0].astype(jnp.float32)
@@ -276,13 +265,21 @@
             query_out[:, cols] = query_grad[rows, :]
             held[rows, :] = head_grad[:, cols]
 
+    sides = [(side, slice(side * half, (side + 1) * half)) for side in range(2)]
+    last_pieces = [(3, side, last_ref[0, part]) for side, part in sides]
+
     @pl.when(step < tiles)
     def _():
-        advance(own_refs)
+        pieces = [(0, side, own_ref[part]) for side, part in sides]
+        pieces += [(1 + i, side, pair_ref[part, i]) for i in range(2) for side, part in sides]
+        advance(pieces + last_pieces)
 
     @pl.when(step >= tiles)
     def _():
-        advance(other_refs)
+        pieces = [(0, core, own_across[...]), (0, 1 - core, own_swapped[...])]
+        for i in range(2):
+            pieces += [(1 + i, core, pair_across[:, i]), (1 + i, 1 - core, pair_swapped[:, i])]
+        advance(pieces + last_pieces)
 
     @pl.when((step > 0) & (step % tiles == 0))
     def _():
@@ -291,9 +288,9 @@
         sent_out[...] = sums[:, :tokens, :].astype(jnp.bfloat16)
 
 
-def tail(place_info, blocks, back, place, moe_grad, w_own, w_other, low, turned, query, keys, values):
+def tail(place_info, back, place, moe_grad, pieces, w_last, low, turned, query, keys, values):
     tokens, width = moe_grad.shape
-    quarter, cols = w_own[0].shape
+    spread, size, cols = w_last.shape[1:]
     span = keys.shape[1]
     heads = 4
     tile = heads * HD
@@ -304,19 +301,25 @@
     whole = lambda shape: pl.BlockSpec(shape, lambda i, info: (0,) * len(shape))
     group = lambda shape: pl.BlockSpec((1,) + shape, lambda i, info: (kv_group(i, info), 0, 0))
     rows = lambda shape: pl.BlockSpec((1,) + shape, lambda i, info: (kv_group(i, info), was(i) % tiles, 0))
-    own_spec = pl.BlockSpec((quarter, tile), lambda i, info: (0, jnp.minimum(i, tiles - 1)))
-    other_spec = pl.BlockSpec(
-        (quarter, tile), lambda i, info: (0, jnp.minimum(jnp.maximum(i - tiles, 0), tiles - 1))
-    )
+    now = lambda i: jnp.minimum(i, steps - 1)
+    own_tile = lambda i: jnp.minimum(i, tiles - 1)
+    other_tile = lambda i: jnp.minimum(jnp.maximum(i - tiles, 0), tiles - 1)
+    both_spec = pl.BlockSpec(
+        (1, spread, size, tile), lambda i, info: ((now(i) // tiles) ^ info[0], 0, 0, now(i) % tiles)
+    )
+    one = lambda count, turn: pl.BlockSpec((count, size, tile), lambda i, info: (0, 0, turn(i)))
+    two = lambda count, turn: pl.BlockSpec((count, 2, size, tile), lambda i, info: (0, 0, 0, turn(i)))
     kv = pl.BlockSpec((tokens, HD), lambda i, info: (0, kv_group(i, info)))
     return pl.pallas_call(
-        functools.partial(tail_kernel, (heads, tiles, blocks)),
+        functools.partial(tail_kernel, (heads, tiles)),
         grid_spec=pltpu.PrefetchScalarGridSpec(
             num_scalar_prefetch=1,
             grid=(steps + 1,),
             in_specs=[whole(back.shape), whole(place.shape), whole(moe_grad.shape)]
-            + [own_spec] * 4
-            + [other_spec] * 4
+            + [one(spread, own_tile), two(spread, own_tile)]
+            + [one(spread // 2, other_tile)] * 2
+            + [two(spread // 2, other_tile)] * 2
+            + [both_spec]
             + [
                 rows((heads * tokens, span)),
                 pl.BlockSpec(
@@ -336,7 +339,7 @@
                 pl.BlockSpec((2, tokens, HD), lambda i, info: (0, 0, kv_group(i, info))),
             ],
             scratch_shapes=[
-                pltpu.VMEM((4, tokens, quarter), jnp.bfloat16),
+                pltpu.VMEM((8, tokens, spread * size // 2), jnp.bfloat16),
                 pltpu.VMEM((heads * tokens, HD), jnp.bfloat16),
                 pltpu.VMEM((2, span, HD), jnp.float32),
             ],
@@ -353,7 +356,7 @@
             flops=2 * tokens * width * KVH * cols, bytes_accessed=22 * MIB, transcendentals=0
         ),
         name="tail_attention",
-    )(place_info, back, place, moe_grad, *w_own, *w_other, low, turned, query, keys, values)
+    )(place_info, back, place, moe_grad, *pieces, w_last, low, turned, query, keys, values)
 
 
 def local(
@@ -384,38 +387,46 @@
 
     share_cols = w_out.shape[1] // parts
     w_share = lax.dynamic_slice_in_dim(w_out, lax.axis_index("groups") * share_cols, share_cols, 1)
-    w_mirror = lax.ppermute(w_share, "far", swap)
-    w_near, w_far = (
-        lax.all_gather(part, ("near", "low"), axis=0, tiled=True) for part in (w_share, w_mirror)
-    )
-
-    rows, place = pick(routes, route_weight, moe_input, moe_grad, owners, depth)
-    rows_in = lax.all_to_all(rows.reshape(owners, depth, 2 * width), chips, 0, 0, tiled=True)
-    x_near = lax.ppermute(w_near, "groups", swap)
-
-    own = (w_gate, w_up, w_down)
-    other = tuple(lax.ppermute(w, "core", swap) for w in own)
-    prepared = prepare_weights(own, other)
+    w_near = lax.ppermute(w_share, "near", swap)
+    w_far = lax.ppermute(w_share, "far", swap)
 
     kv = jnp.concatenate([key_heads, value_heads], axis=1)
     segs = (segments + 1).astype(jnp.float32)
     seg_rows = jnp.zeros((16, kv.shape[1]), jnp.bfloat16).at[0, :tokens].set(segs.astype(jnp.bfloat16))
     prev = lax.ppermute(jnp.concatenate([kv, seg_rows], axis=0), blk, onward)
 
-    rows_in, prepared, prev, w_near, w_far, x_near = lax.optimization_barrier(
-        (rows_in, prepared, prev, w_near, w_far, x_near)
-    )
-    x_far = lax.ppermute(w_far, "groups", swap)
+    own = (w_gate, w_up, w_down)
+    other = tuple(lax.ppermute(w, "core", swap) for w in own)
+    rows, place = pick(routes, route_weight, moe_input, moe_grad, owners, depth)
+    plane = ("groups", "low", "core")
+    core = lax.axis_index("core")
+    w_own = lax.all_gather(w_share, plane[1:], axis=0, tiled=False)
+    rows, w_near, w_far, w_own, prev, other = lax.optimization_barrier((rows, w_near, w_far, w_own, prev, other))
+
+    half_of = lambda w: lax.dynamic_slice_in_dim(w, core * low, low, 0)
+    rows_in = lax.all_to_all(rows.reshape(owners, depth, 2 * width), chips, 0, 0, tiled=True)
+    own_across = lax.ppermute(half_of(w_own), "groups", swap)
+    w_pair = lax.all_gather(jnp.stack([w_near, w_far]), plane[1:], axis=0, tiled=False)
+    w_half = half_of(w_pair)
+    w_last = lax.ppermute(w_far, "near", swap)
+    prepared = prepare_weights(own, other)
+    attention = attention_shares(queries, key_heads, value_heads, prev, segs)
+
+    rows_in, prepared, attention, own_across, w_pair, w_half, w_last = lax.optimization_barrier(
+        (rows_in, prepared, attention, own_across, w_pair, w_half, w_last)
+    )
+    own_swapped = lax.ppermute(own_across, "core", swap)
+    pair_across = lax.ppermute(w_half, "groups", swap)
+    pair_swapped = lax.ppermute(pair_across, "core", swap)
+    w_last = lax.all_gather(w_last, plane, axis=0, tiled=False).reshape(parts, 2 * low, *w_share.shape)
     terms = experts(rows_in.reshape(owners * depth, 2 * width), *prepared)
-    prev, terms = lax.optimization_barrier((prev, terms))
     back = lax.all_to_all(terms.reshape(owners, depth, width), chips, 0, 0, tiled=True)
-    attention = attention_shares(queries, key_heads, value_heads, prev, segs)
-    both_cores = lambda *pieces: [w for piece in pieces for w in (piece, lax.ppermute(piece, "core", swap))]
-
+
+    z = 2 * lax.axis_index("far") + lax.axis_index("near")
     moe_input_grad, query_grad, key_part, value_part, sent = tail(
-        jnp.stack([lax.axis_index(axis) for axis in ("groups", "far", "core")]).astype(jnp.int32),
-        2 * low, back.reshape(owners * depth, width), place, moe_grad,
-        both_cores(w_near, w_far), both_cores(x_near, x_far), *attention,
+        jnp.stack([lax.axis_index("groups"), z, core]).astype(jnp.int32),
+        back.reshape(owners * depth, width), place, moe_grad,
+        (w_own, w_pair, own_across, own_swapped, pair_across, pair_swapped), w_last, *attention,
     )
     later = lax.ppermute(sent, blk, backward).astype(jnp.float32)
     return (moe_input_grad, query_grad, key_part + later[0], value_part + later[1])

time: 254 us -> 225 us (0.89)
  waiting for transfers between devices: 142 us -> 111 us
  local copies, waits for them, and re-layouts: 16.9 us -> 26.6 us
  starting transfers between devices: 31.1 us -> 22 us
  other arithmetic: 2.38 us -> 5.99 us
    ppermute x7, waiting for transfers between devices: 110 us -> 64.6 us  [the longest x1 43.3 us: local(): pair_across = lax.ppermute(w_half, 'groups', swap)]
    all_gather x2 -> x3, waiting for transfers between devices: 24.4 us -> 33.3 us  [the longest x1 33.3 us: local(): lax.all_gather(jnp.stack([w_near, w_far]), plane[1:], axis=0, tiled=False)]
    dynamic_slice x0 -> x2, local copies, waits for them, and re-layouts: none -> 5.44 us  [local(): half_of = lambda w: lax.dynamic_slice_in_dim(w, core * low, low, 0)]
    all_to_all x1, waiting for transfers between devices: 0.01 us -> 5.42 us  [local(): lax.all_to_all(rows.reshape(owners, depth, 2 * width), chips, 0, 0, tiled...]
    ppermute x7, starting transfers between devices: 9.23 us -> 4.98 us  [the longest x1 1.34 us: local(): pair_swapped = lax.ppermute(pair_across, 'core', swap)]
    unnamed x46 -> x44, local copies, waits for them, and re-layouts: 16 us -> 20.2 us
    ppermute x3, waiting for transfers between devices: 2.61 us -> 0.01 us  [local(): other = tuple((lax.ppermute(w, 'core', swap) for w in own))]
  transfers between devices with their start and end apart: 16 -> 17, of which waited for: 6 -> 8; matrix products, arithmetic and copies ran while one was open for 0% -> 3% of each run, Pallas kernels for 11% -> 11%
where the time goes in v9:
time: 225 us; the launch traced here: 222 us
  waiting for transfers between devices  111 us (49%)
  Pallas kernels  43.1 us (19%)
  local copies, waits for them, and re-layouts  26.6 us (12%)
  starting transfers between devices  22 us (10%)
  between operations  13.9 us (6%)
  other arithmetic  5.99 us (3%)
    ppermute x1, waiting for transfers between devices, local(): pair_across = lax.ppermute(w_half, 'groups', swap)  43.3 us
    all_gather x1, waiting for transfers between devices, local(): lax.all_gather(jnp.stack([w_near, w_far]), plane[1:], axis=0, tiled=False)  33.3 us
    unnamed x44, local copies, waits for them, and re-layouts  20.2 us
    pallas_call x1, Pallas kernels, tail(): pl.pallas_call(functools.partial(tail_kernel, (heads, tiles)), grid_spec=...  17.7 us
    ppermute x1, waiting for transfers between devices, local(): w_near = lax.ppermute(w_share, 'near', swap)  12.6 us
    pallas_call x1, Pallas kernels, experts(): pl.pallas_call(functools.partial(expert_kernel, steps), grid=(steps + wid...  11.8 us
    pallas_call x1, Pallas kernels, prepare_weights(): pl.pallas_call(weights_kernel, grid=(steps,), in_specs=[cols, cols, down]...  8.87 us
    all_to_all x1, starting transfers between devices, local(): lax.all_to_all(terms.reshape(owners, depth, width), chips, 0, 0, tiled=True)  6.36 us
  transfers between devices with their start and end apart: 17, of which 8 were waited for; matrix products, arithmetic and copies ran while one was open for 3% of the time, Pallas kernels for 11%

profile of v9, /device:TPU:13, one launch (start us, length us, event | category | flops | bytes accessed | tf_op | source)
XLA Modules:
  0.0 222.2 jit_solution(16091195620183445667)
XLA Ops:
  12.1 3.1 %collective-permute-start.2 = (bf16[144,512]{1,0:T(8,128)(2,1)S(1)}, bf16[144,512]{1,0:T(8,128)(2,1)S(1)}, u32[]{:S(2)}, u32[]{:S(2)}) collective-permute-start(bf16[144,512]{1,0:T(8,128)(2,1)S(1)} %fusion.1), channel_id=1, source_target_pairs={{0,1},{1,2},{2,3},{3,4},{4,5},{5,6},{6,7},{7,8},{8,9},{9,10},{10,1... | collective-permute-start | bytes 442376 | tf_op jit(solution)/shard_map/ppermute | solution.py:396
  15.5 1.8 collective-permute-done.2.prev_key_ref.prev_value_ref.prev_seg_ref
  22.6 1.6 copy-done.3
  24.8 12.6 %collective-permute-done = bf16[128,2048]{1,0:T(8,128)(2,1)S(1)} collective-permute-done((bf16[128,2048]{1,0:T(8,128)(2,1)}, bf16[128,2048]{1,0:T(8,128)(2,1)S(1)}, u32[]{:S(2)}, u32[]{:S(2)}) %collective-permute-start) | collective-permute-done | bytes 524320 | tf_op jit(solution)/shard_map/ppermute | solution.py:390
  37.4 3.9 %collective-permute-done.1 = bf16[128,2048]{1,0:T(8,128)(2,1)} collective-permute-done((bf16[128,2048]{1,0:T(8,128)(2,1)}, bf16[128,2048]{1,0:T(8,128)(2,1)}, u32[]{:S(2)}, u32[]{:S(2)}) %collective-permute-start.1) | collective-permute-done | bytes 524320 | tf_op jit(solution)/shard_map/ppermute | solution.py:391
  41.4 2.1 pad_maximum_fusion
  43.5 4.2 %all-to-all-start = ((bf16[8,48,4096]{2,1,0:T(8,128)(2,1)}), bf16[8,48,4096]{2,1,0:T(8,128)(2,1)S(1)}, u32[]{:S(2)}, u32[]{:S(2)}) async-start(bf16[8,48,4096]{2,1,0:T(8,128)(2,1)} %bitcast.30), calls=%async_computation | async-start | bytes 6291456 | tf_op jit(solution)/shard_map/all_to_all | solution.py:407
  47.7 2.3 %constant_dynamic-slice_fusion.1 = bf16[2,128,2048]{2,1,0:T(8,128)(2,1)} fusion(bf16[4,128,2048]{2,1,0:T(8,128)(2,1)} %bitcast.36, s32[]{:T(128)S(6)} %select_n.8), kind=kLoop, calls=%fused_computation.9 | loop fusion | bytes 2097156 | tf_op jit(solution)/shard_map/dynamic_slice | solution.py:406
  51.7 1.5 copy-done.6
  53.2 1.6 copy-done.7
  54.8 1.9 copy-done.8
  56.7 8.9 %prepare_weights.1 = (bf16[3,2048,512]{2,1,0:T(8,128)(2,1)}, bf16[3,2048,256]{2,1,0:T(8,128)(2,1)}, bf16[3,512,2048]{2,1,0:T(8,128)(2,1)}) custom-call(bf16[2048,384]{1,0:T(8,128)(2,1)S(1)} %copy-done.6, bf16[2048,384]{1,0:T(8,128)(2,1)S(1)} %copy-done.7, bf16[384,2048]{1,0:T(8,128)(2,1)S(1)} %copy-done.8, bf16[2048,384]{1,0:T(8,128)(2,1)} %collective-permute-done.3.refs_3_, ...), custom_call_target="tpu_custom_call" | custom-call | tf_op jit(solution)/shard_map/prepare_weights/pallas_call | solution.py:94
  65.6 3.5 %attention_shares.1 = (bf16[2,2048,256]{2,1,0:T(8,128)(2,1)S(1)}, bf16[2,256,2048]{2,1,0:T(8,128)(2,1)S(1)}, bf16[2,2048,128]{2,1,0:T(8,128)(2,1)S(1)}, bf16[2,2...) custom-call(bf16[128,4096]{1,0:T(8,128)(2,1)S(1)} %copy-done.9, bf16[128,256]{1,0:T(8,128)(2,1)S(1)} %copy-done.12, ...), custom_call_target="tpu_custom_call" | custom-call | tf_op jit(solution)/shard_map/attention_shares/pallas_call | solution.py:201
  74.1 33.3 %all-gather.9.cloned.1.call-done = bf16[8,128,2048]{2,1,0:T(8,128)(2,1)} async-done(((bf16[2,128,2048]{2,1,0:T(8,128)(2,1)}), bf16[8,128,2048]{2,1,0:T(8,128)(2,1)}) %all-gather.9.cloned.1.call-update) | async-done | bytes 4194320 | tf_op jit(solution)/shard_map/all_gather | solution.py:409
  107.4 3.1 %constant_dynamic-slice_fusion = bf16[2,2,128,2048]{3,2,1,0:T(8,128)(2,1)} fusion(bf16[4,2,128,2048]{3,2,1,0:T(8,128)(2,1)} %bitcast.33, s32[]{:T(128)S(6)} %select_n.8), kind=kLoop, calls=%fused_computation.8 | loop fusion | bytes 4194308 | tf_op jit(solution)/shard_map/dynamic_slice | solution.py:406
  110.5 5.4 %all-to-all-done = bf16[8,48,4096]{2,1,0:T(8,128)(2,1)S(1)} async-done(((bf16[8,48,4096]{2,1,0:T(8,128)(2,1)}), bf16[8,48,4096]{2,1,0:T(8,128)(2,1)S(1)}, u32[]{:S(2)}, u32[]{:S(2)}) %all-to-all-start) | async-done | bytes 3145760 | tf_op jit(solution)/shard_map/all_to_all | solution.py:407
  117.3 11.8 %expert_terms.1 = bf16[384,2048]{1,0:T(8,128)(2,1)S(1)} custom-call(bf16[384,4096]{1,0:T(8,128)(2,1)S(1)} %bitcast.28, bf16[3,2048,512]{2,1,0:T(8,128)(2,1)} %get-tuple-element.70.cols_ref, bf16[3,2048,256]{2,1,0:T(8,128)(2,1)} %get-tuple-element.71.down_ref, bf16[3,512,2048]{2,1,0:T(8,128)(2,1)} %get-tuple-element.72.back_ref), custom_call_target="tpu_custom_call" | custom-call | tf_op jit(solution)/shard_map/expert_terms/pallas_call | solution.py:145
  130.3 6.4 %all-to-all-start.1 = ((bf16[8,48,2048]{2,1,0:T(8,128)(2,1)}), bf16[8,48,2048]{2,1,0:T(8,128)(2,1)S(1)}, u32[]{:S(2)}, u32[]{:S(2)}) async-start(bf16[8,48,2048]{2,1,0:T(8,128)(2,1)} %bitcast.29), calls=%async_computation.1 | async-start | bytes 3145728 | tf_op jit(solution)/shard_map/all_to_all | solution.py:423
  136.6 43.3 %collective-permute-done.9.refs_4_ = bf16[2,2,128,2048]{3,2,1,0:T(8,128)(2,1)} collective-permute-done((bf16[2,2,128,2048]{3,2,1,0:T(8,128)(2,1)}, bf16[2,2,128,2048]{3,2,1,0:T(8,128)(2,1)}, u32[]{:S(2)}, u32[]{:S(2)}) %collective-permute-start.9) | collective-permute-done | bytes 2097184 | tf_op jit(solution)/shard_map/ppermute | solution.py:419
  181.9 4.7 %collective-permute-done.8.refs_3_ = bf16[2,128,2048]{2,1,0:T(8,128)(2,1)S(1)} collective-permute-done((bf16[2,128,2048]{2,1,0:T(8,128)(2,1)}, bf16[2,128,2048]{2,1,0:T(8,128)(2,1)S(1)}, u32[]{:S(2)}, u32[]{:S(2)}) %collective-permute-start.8) | collective-permute-done | bytes 1048608 | tf_op jit(solution)/shard_map/ppermute | solution.py:418
  188.8 17.7 %tail_attention.1 = (bf16[128,2048]{1,0:T(8,128)(2,1)}, bf16[128,4096]{1,0:T(8,128)(2,1)}, f32[128,256]{1,0:T(8,128)}, f32[128,256]{1,0:T(8,128)}, bf16[2,128,256]{2,1,0:T(8,128)(2,1)}) custom-call(s32[3]{0:T(128)} %pad_add_fusion.place_info, bf16[384,2048]{1,0:T(8,128)(2,1)} %bitcast.35, bf16[128,384]{1,0:T(8,128)(2,1)} %copy-done.16, ...), custom_call_target="tpu_custom_call" | custom-call | flops 2147483648 | bytes 23068672 | tf_op jit(solution)/shard_map/tail_attention/pallas_call | solution.py:313
  206.5 2.0 collective-permute-start.11
  208.6 5.3 %collective-permute-done.11 = bf16[2,128,256]{2,1,0:T(8,128)(2,1)S(1)} collective-permute-done((bf16[2,128,256]{2,1,0:T(8,128)(2,1)}, bf16[2,128,256]{2,1,0:T(8,128)(2,1)S(1)}, u32[]{:S(2)}, u32[]{:S(2)}) %collective-permute-start.11) | collective-permute-done | bytes 131104 | tf_op jit(solution)/shard_map/ppermute | solution.py:431
  213.9 1.7 fusion.2
  (72 shorter events, 24.2 us)
Async XLA Ops:
  7.2 34.2 %all-gather.7.cloned.1.call-start = ((), (), s32[]{:S(2)}) async-start(), calls=%async_computation.2 | async-start | bytes 2621440 | tf_op jit(solution)/shard_map/all_gather | solution.py:403
  9.3 98.1 %all-gather.9.cloned.1.call-start = ((), (), s32[]{:S(2)}) async-start(), calls=%async_computation.3 | async-start | bytes 5242880 | tf_op jit(solution)/shard_map/all_gather | solution.py:409
  9.3 32.1 %collective-permute-start.3 = (bf16[2048,384]{1,0:T(8,128)(2,1)}, bf16[2048,384]{1,0:T(8,128)(2,1)}, u32[]{:S(2)}, u32[]{:S(2)}) collective-permute-start(bf16[2048,384]{1,0:T(8,128)(2,1)} %refs_0_.1), channel_id=1, source_target_pairs={{0,1},{1,0},{2,3},{3,2},{4,5},{5,4},{6,7},{7,6},{8,9},{9,8},{10,11... | collective-permute-start | bytes 4718600 | tf_op jit(solution)/shard_map/ppermute | solution.py:399
  10.0 31.3 %collective-permute-start.4 = (bf16[2048,384]{1,0:T(8,128)(2,1)}, bf16[2048,384]{1,0:T(8,128)(2,1)}, u32[]{:S(2)}, u32[]{:S(2)}) collective-permute-start(bf16[2048,384]{1,0:T(8,128)(2,1)} %refs_1_.1), channel_id=1, source_target_pairs={{0,1},{1,0},{2,3},{3,2},{4,5},{5,4},{6,7},{7,6},{8,9},{9,8},{10,11... | collective-permute-start | bytes 4718600 | tf_op jit(solution)/shard_map/ppermute | solution.py:399
  10.1 31.2 %collective-permute-start.5 = (bf16[384,2048]{1,0:T(8,128)(2,1)}, bf16[384,2048]{1,0:T(8,128)(2,1)}, u32[]{:S(2)}, u32[]{:S(2)}) collective-permute-start(bf16[384,2048]{1,0:T(8,128)(2,1)} %refs_2_.1), channel_id=1, source_target_pairs={{0,1},{1,0},{2,3},{3,2},{4,5},{5,4},{6,7},{7,6},{8,9},{9,8},{10,11... | collective-permute-start | bytes 4718600 | tf_op jit(solution)/shard_map/ppermute | solution.py:399
  12.1 5.2 %collective-permute-start.2 = (bf16[144,512]{1,0:T(8,128)(2,1)S(1)}, bf16[144,512]{1,0:T(8,128)(2,1)S(1)}, u32[]{:S(2)}, u32[]{:S(2)}) collective-permute-start(bf16[144,512]{1,0:T(8,128)(2,1)S(1)} %fusion.1), channel_id=1, source_target_pairs={{0,1},{1,2},{2,3},{3,4},{4,5},{5,6},{6,7},{7,8},{8,9},{9,10},{10,1... | collective-permute-start | bytes 442376 | tf_op jit(solution)/shard_map/ppermute | solution.py:396
  15.2 22.2 %collective-permute-start = (bf16[128,2048]{1,0:T(8,128)(2,1)}, bf16[128,2048]{1,0:T(8,128)(2,1)S(1)}, u32[]{:S(2)}, u32[]{:S(2)}) collective-permute-start(bf16[128,2048]{1,0:T(8,128)(2,1)} %constant_dynamic-slice_fusion.2), channel_id=1, source_target_pairs={{0,4},{4,0},{1,5},{5,1},{2,6},{6,2},{3,7},{7,3},{8,12},{12,8},{9,1... | collective-permute-start | bytes 1572872 | tf_op jit(solution)/shard_map/ppermute | solution.py:390
  17.3 24.1 %collective-permute-start.1 = (bf16[128,2048]{1,0:T(8,128)(2,1)}, bf16[128,2048]{1,0:T(8,128)(2,1)}, u32[]{:S(2)}, u32[]{:S(2)}) collective-permute-start(bf16[128,2048]{1,0:T(8,128)(2,1)} %constant_dynamic-slice_fusion.2), channel_id=1, source_target_pairs={{0,8},{8,0},{1,9},{9,1},{2,10},{10,2},{3,11},{11,3},{4,12},{12,4},... | collective-permute-start | bytes 1572872 | tf_op jit(solution)/shard_map/ppermute | solution.py:391
  22.6 1.6 copy-start.3
  43.5 72.4 %all-to-all-start = ((bf16[8,48,4096]{2,1,0:T(8,128)(2,1)}), bf16[8,48,4096]{2,1,0:T(8,128)(2,1)S(1)}, u32[]{:S(2)}, u32[]{:S(2)}) async-start(bf16[8,48,4096]{2,1,0:T(8,128)(2,1)} %bitcast.30), calls=%async_computation | async-start | bytes 6291456 | tf_op jit(solution)/shard_map/all_to_all | solution.py:407
  47.7 139.9 %all-gather.11.cloned.1.call-start = ((), (), s32[]{:S(2)}) async-start(), calls=%async_computation.4 | async-start | bytes 4718592 | tf_op jit(solution)/shard_map/all_gather | solution.py:421
  50.0 60.5 %collective-permute-start.6 = (bf16[2,128,2048]{2,1,0:T(8,128)(2,1)}, bf16[2,128,2048]{2,1,0:T(8,128)(2,1)}, u32[]{:S(2)}, u32[]{:S(2)}) collective-permute-start(bf16[2,128,2048]{2,1,0:T(8,128)(2,1)} %constant_dynamic-slice_fusion.1), channel_id=1, source_target_pairs={{0,16},{16,0},{1,17},{17,1},{2,18},{18,2},{3,19},{19,3},{4,20},{20... | collective-permute-start | bytes 3145736 | tf_op jit(solution)/shard_map/ppermute | solution.py:408
  51.3 59.3 %collective-permute-start.7 = (bf16[128,2048]{1,0:T(8,128)(2,1)}, bf16[128,2048]{1,0:T(8,128)(2,1)}, u32[]{:S(2)}, u32[]{:S(2)}) collective-permute-start(bf16[128,2048]{1,0:T(8,128)(2,1)} %collective-permute-done.1), channel_id=1, source_target_pairs={{0,4},{4,0},{1,5},{5,1},{2,6},{6,2},{3,7},{7,3},{8,12},{12,8},{9,1... | collective-permute-start | bytes 1572872 | tf_op jit(solution)/shard_map/ppermute | solution.py:411
  53.2 1.6 copy-start.7
  54.8 1.9 copy-start.8
  56.7 8.9 %copy-start.9 = (bf16[128,4096]{1,0:T(8,128)(2,1)S(1)}, bf16[128,4096]{1,0:T(8,128)(2,1)}, u32[]{:S(2)}) copy-start(bf16[128,4096]{1,0:T(8,128)(2,1)} %q_ref.1) | copy-start | bytes 3145732
  56.7 8.9 %copy-start.12 = (bf16[128,256]{1,0:T(8,128)(2,1)S(1)}, bf16[128,256]{1,0:T(8,128)(2,1)}, u32[]{:S(2)}) copy-start(bf16[128,256]{1,0:T(8,128)(2,1)} %key_ref.1) | copy-start | bytes 196612
  56.7 8.9 %copy-start.13 = (bf16[128,256]{1,0:T(8,128)(2,1)S(1)}, bf16[128,256]{1,0:T(8,128)(2,1)}, u32[]{:S(2)}) copy-start(bf16[128,256]{1,0:T(8,128)(2,1)} %value_ref.1) | copy-start | bytes 196612
  116.0 63.9 %collective-permute-start.9 = (bf16[2,2,128,2048]{3,2,1,0:T(8,128)(2,1)}, bf16[2,2,128,2048]{3,2,1,0:T(8,128)(2,1)}, u32[]{:S(2)}, u32[]{:S(2)}) collective-permute-start(bf16[2,2,128,2048]{3,2,1,0:T(8,128)(2,1)} %constant_dynamic-slice_fusion), channel_id=1, source_target_pairs={{0,16},{16,0},{1,17},{17,1},{2,18},{18,2},{3,19},{19,3},{4,20},{20... | collective-permute-start | bytes 6291464 | tf_op jit(solution)/shard_map/ppermute | solution.py:419
  130.3 56.4 %all-to-all-start.1 = ((bf16[8,48,2048]{2,1,0:T(8,128)(2,1)}), bf16[8,48,2048]{2,1,0:T(8,128)(2,1)S(1)}, u32[]{:S(2)}, u32[]{:S(2)}) async-start(bf16[8,48,2048]{2,1,0:T(8,128)(2,1)} %bitcast.29), calls=%async_computation.1 | async-start | bytes 3145728 | tf_op jit(solution)/shard_map/all_to_all | solution.py:423
  179.9 7.7 %collective-permute-start.10 = (bf16[2,2,128,2048]{3,2,1,0:T(8,128)(2,1)}, bf16[2,2,128,2048]{3,2,1,0:T(8,128)(2,1)}, u32[]{:S(2)}, u32[]{:S(2)}) collective-permute-start(bf16[2,2,128,2048]{3,2,1,0:T(8,128)(2,1)} %collective-permute-done.9.refs_4_), channel_id=1, source_target_pairs={{0,1},{1,0},{2,3},{3,2},{4,5},{5,4},{6,7},{7,6},{8,9},{9,8},{10,11... | collective-permute-start | bytes 6291464 | tf_op jit(solution)/shard_map/ppermute | solution.py:420
  181.3 5.4 %collective-permute-start.8 = (bf16[2,128,2048]{2,1,0:T(8,128)(2,1)}, bf16[2,128,2048]{2,1,0:T(8,128)(2,1)S(1)}, u32[]{:S(2)}, u32[]{:S(2)}) collective-permute-start(bf16[2,128,2048]{2,1,0:T(8,128)(2,1)} %collective-permute-done.6.refs_2_), channel_id=1, source_target_pairs={{0,1},{1,0},{2,3},{3,2},{4,5},{5,4},{6,7},{7,6},{8,9},{9,8},{10,11... | collective-permute-start | bytes 3145736 | tf_op jit(solution)/shard_map/ppermute | solution.py:418
  188.8 26.9 %copy-start.1 = (bf16[128,4096]{1,0:T(8,128)(2,1)S(1)}, bf16[128,4096]{1,0:T(8,128)(2,1)}, u32[]{:S(2)}) copy-start(bf16[128,4096]{1,0:T(8,128)(2,1)} %param.21) | copy-start | bytes 3145732
  206.5 7.4 %collective-permute-start.11 = (bf16[2,128,256]{2,1,0:T(8,128)(2,1)}, bf16[2,128,256]{2,1,0:T(8,128)(2,1)S(1)}, u32[]{:S(2)}, u32[]{:S(2)}) collective-permute-start(bf16[2,128,256]{2,1,0:T(8,128)(2,1)} %get-tuple-element.86), channel_id=1, source_target_pairs={{1,0},{2,1},{3,2},{4,3},{5,4},{6,5},{7,6},{8,7},{9,8},{10,9},{11,1... | collective-permute-start | bytes 393224 | tf_op jit(solution)/shard_map/ppermute | solution.py:431
  (15 other events, 15.2 us)
Sparse Core Ops, SparseCore 0:
  10.2 23.1 all-gather.6
  43.7 63.6 all-gather.8
  116.1 55.4 all-gather.10

commit v10 on v9

--- a/solution.py
+++ b/solution.py
@@ -154,7 +154,7 @@
         out_specs=pl.BlockSpec((count, tile), lambda i: (0, turn(i))),
         out_shape=jax.ShapeDtypeStruct((count, width), jnp.bfloat16),
         scratch_shapes=[pltpu.VMEM((steps, count, quad), jnp.bfloat16)],
-        compiler_params=params(48),
+        compiler_params=params(24),
         cost_estimate=LIGHT,
         name="expert_terms",
     )(rows, cols, down, back)
@@ -223,8 +223,9 @@
     plan, place_info, back_ref, place_ref, grad_ref, *refs
 ):
     heads, tiles = plan
-    own_ref, pair_ref, own_across, own_swapped, pair_across, pair_swapped, last_ref, low_ref, turned_ref, q_ref, key_ref, value_ref, *refs = refs
-    moe_ref, query_out, key_out, value_out, sent_out, stream, held, sums = refs
+    mine, across, swapped, refs = refs[:3], refs[3:6], refs[6:9], refs[9:]
+    last_ref, low_ref, turned_ref, q_ref, key_ref, value_ref, *refs = refs
+    moe_ref, query_out, kept_out, sent_out, stream, held, sums = refs
     step = pl.program_id(0)
     tokens = query_out.shape[0]
     part_size = stream.shape[2]
@@ -238,20 +239,25 @@
         added = (grad_ref[...].astype(jnp.float32) + moe.astype(jnp.float32)).astype(jnp.bfloat16)
         for eighth in range(8):
             stream[eighth] = added[:, eighth * part_size : (eighth + 1) * part_size]
-        held[...] = jnp.zeros_like(held)
-
-    @pl.when((step == 0) | ((step > 1) & ((step - 1) % tiles == 0)))
+
+    @pl.when((step > 0) & ((step - 1) % tiles == 0))
     def _():
         sums[...] = jnp.zeros_like(sums)
 
-    def advance(pieces):
-        grads = held[...]
+    def project(pieces):
         head_grad = None
         for turn, side, piece in pieces:
             rows = stream[2 * (here ^ turn) + side]
             part = dot(rows, piece.reshape(part_size, piece.shape[-1]))
             head_grad = part if head_grad is None else head_grad + part
-        head_grad = head_grad.astype(jnp.bfloat16)
+        return head_grad.astype(jnp.bfloat16)
+
+    def hold(head_grad):
+        for head in range(heads):
+            held[head * tokens : (head + 1) * tokens, :] = head_grad[:, head * HD : (head + 1) * HD]
+
+    def attend():
+        grads = held[...]
         low = low_ref[0].astype(jnp.float32)
         prob_grad = dot(grads, value_ref[0])
         row_dot = jnp.sum(low * prob_grad, axis=1, keepdims=True)
@@ -260,31 +266,43 @@
         sums[0] += dot(score_grad, q_ref[0], TN)
         sums[1] += dot(turned_ref[0], grads)
         for head in range(heads):
-            cols = slice(head * HD, (head + 1) * HD)
-            rows = slice(head * tokens, (head + 1) * tokens)
-            query_out[:, cols] = query_grad[rows, :]
-            held[rows, :] = head_grad[:, cols]
+            query_out[:, head * HD : (head + 1) * HD] = query_grad[head * tokens : (head + 1) * tokens, :]
 
     sides = [(side, slice(side * half, (side + 1) * half)) for side in range(2)]
-    last_pieces = [(3, side, last_ref[0, part]) for side, part in sides]
-
-    @pl.when(step < tiles)
-    def _():
-        pieces = [(0, side, own_ref[part]) for side, part in sides]
-        pieces += [(1 + i, side, pair_ref[part, i]) for i in range(2) for side, part in sides]
-        advance(pieces + last_pieces)
-
-    @pl.when(step >= tiles)
-    def _():
-        pieces = [(0, core, own_across[...]), (0, 1 - core, own_swapped[...])]
-        for i in range(2):
-            pieces += [(1 + i, core, pair_across[:, i]), (1 + i, 1 - core, pair_swapped[:, i])]
-        advance(pieces + last_pieces)
+
+    def own_pieces():
+        pieces = [(turn, side, mine[turn][part]) for turn in range(3) for side, part in sides]
+        return pieces + [(3, side, last_ref[0, part]) for side, part in sides]
+
+    def other_pieces():
+        pieces = []
+        for turn in range(3):
+            pieces += [(turn, core, across[turn][...]), (turn, 1 - core, swapped[turn][...])]
+        return pieces + [(3, side, last_ref[0, part]) for side, part in sides]
+
+    @pl.when(step == 0)
+    def _():
+        hold(project(own_pieces()))
+
+    @pl.when((step > 0) & (step < tiles))
+    def _():
+        head_grad = project(own_pieces())
+        attend()
+        hold(head_grad)
+
+    @pl.when((step >= tiles) & (step < 2 * tiles))
+    def _():
+        head_grad = project(other_pieces())
+        attend()
+        hold(head_grad)
+
+    @pl.when(step == 2 * tiles)
+    def _():
+        attend()
 
     @pl.when((step > 0) & (step % tiles == 0))
     def _():
-        key_out[...] = sums[0, tokens:, :]
-        value_out[...] = sums[1, tokens:, :]
+        kept_out[...] = sums[:, tokens:, :]
         sent_out[...] = sums[:, :tokens, :].astype(jnp.bfloat16)
 
 
@@ -308,17 +326,15 @@
         (1, spread, size, tile), lambda i, info: ((now(i) // tiles) ^ info[0], 0, 0, now(i) % tiles)
     )
     one = lambda count, turn: pl.BlockSpec((count, size, tile), lambda i, info: (0, 0, turn(i)))
-    two = lambda count, turn: pl.BlockSpec((count, 2, size, tile), lambda i, info: (0, 0, 0, turn(i)))
-    kv = pl.BlockSpec((tokens, HD), lambda i, info: (0, kv_group(i, info)))
+    kv = pl.BlockSpec((2, tokens, HD), lambda i, info: (0, 0, kv_group(i, info)))
     return pl.pallas_call(
         functools.partial(tail_kernel, (heads, tiles)),
         grid_spec=pltpu.PrefetchScalarGridSpec(
             num_scalar_prefetch=1,
             grid=(steps + 1,),
             in_specs=[whole(back.shape), whole(place.shape), whole(moe_grad.shape)]
-            + [one(spread, own_tile), two(spread, own_tile)]
-            + [one(spread // 2, other_tile)] * 2
-            + [two(spread // 2, other_tile)] * 2
+            + [one(spread, own_tile)] * 3
+            + [one(spread // 2, other_tile)] * 6
             + [both_spec]
             + [
                 rows((heads * tokens, span)),
@@ -336,7 +352,6 @@
                 ),
                 kv,
                 kv,
-                pl.BlockSpec((2, tokens, HD), lambda i, info: (0, 0, kv_group(i, info))),
             ],
             scratch_shapes=[
                 pltpu.VMEM((8, tokens, spread * size // 2), jnp.bfloat16),
@@ -347,16 +362,27 @@
         out_shape=(
             jax.ShapeDtypeStruct((tokens, width), jnp.bfloat16),
             jax.ShapeDtypeStruct((tokens, KVH * cols), jnp.bfloat16),
-            jax.ShapeDtypeStruct((tokens, KVH * HD), jnp.float32),
-            jax.ShapeDtypeStruct((tokens, KVH * HD), jnp.float32),
+            jax.ShapeDtypeStruct((2, tokens, KVH * HD), jnp.float32),
             jax.ShapeDtypeStruct((2, tokens, KVH * HD), jnp.bfloat16),
         ),
-        compiler_params=params(56),
+        compiler_params=params(40),
         cost_estimate=pl.CostEstimate(
             flops=2 * tokens * width * KVH * cols, bytes_accessed=22 * MIB, transcendentals=0
         ),
         name="tail_attention",
     )(place_info, back, place, moe_grad, *pieces, w_last, low, turned, query, keys, values)
+
+
+def finish_kernel(kept_ref, later_ref, key_ref, value_ref):
+    for kind, out_ref in enumerate((key_ref, value_ref)):
+        out_ref[...] = kept_ref[kind] + later_ref[kind].astype(jnp.float32)
+
+
+def finish(kept, later):
+    out = jax.ShapeDtypeStruct(kept.shape[1:], jnp.float32)
+    return pl.pallas_call(
+        finish_kernel, out_shape=(out, out), compiler_params=params(16), cost_estimate=LIGHT, name="finish"
+    )(kept, later)
 
 
 def local(
@@ -390,46 +416,47 @@
     w_near = lax.ppermute(w_share, "near", swap)
     w_far = lax.ppermute(w_share, "far", swap)
 
-    kv = jnp.concatenate([key_heads, value_heads], axis=1)
-    segs = (segments + 1).astype(jnp.float32)
-    seg_rows = jnp.zeros((16, kv.shape[1]), jnp.bfloat16).at[0, :tokens].set(segs.astype(jnp.bfloat16))
-    prev = lax.ppermute(jnp.concatenate([kv, seg_rows], axis=0), blk, onward)
-
     own = (w_gate, w_up, w_down)
     other = tuple(lax.ppermute(w, "core", swap) for w in own)
     rows, place = pick(routes, route_weight, moe_input, moe_grad, owners, depth)
     plane = ("groups", "low", "core")
     core = lax.axis_index("core")
     w_own = lax.all_gather(w_share, plane[1:], axis=0, tiled=False)
-    rows, w_near, w_far, w_own, prev, other = lax.optimization_barrier((rows, w_near, w_far, w_own, prev, other))
+    rows, w_near, w_far, w_own = lax.optimization_barrier((rows, w_near, w_far, w_own))
 
     half_of = lambda w: lax.dynamic_slice_in_dim(w, core * low, low, 0)
     rows_in = lax.all_to_all(rows.reshape(owners, depth, 2 * width), chips, 0, 0, tiled=True)
     own_across = lax.ppermute(half_of(w_own), "groups", swap)
-    w_pair = lax.all_gather(jnp.stack([w_near, w_far]), plane[1:], axis=0, tiled=False)
-    w_half = half_of(w_pair)
+    near_rows = lax.all_gather(w_near, plane[1:], axis=0, tiled=False)
+    near_across = lax.ppermute(half_of(near_rows), "groups", swap)
+    far_rows = lax.all_gather(w_far, plane[1:], axis=0, tiled=False)
+    far_half = half_of(far_rows)
     w_last = lax.ppermute(w_far, "near", swap)
     prepared = prepare_weights(own, other)
-    attention = attention_shares(queries, key_heads, value_heads, prev, segs)
-
-    rows_in, prepared, attention, own_across, w_pair, w_half, w_last = lax.optimization_barrier(
-        (rows_in, prepared, attention, own_across, w_pair, w_half, w_last)
-    )
-    own_swapped = lax.ppermute(own_across, "core", swap)
-    pair_across = lax.ppermute(w_half, "groups", swap)
-    pair_swapped = lax.ppermute(pair_across, "core", swap)
+    kv = jnp.concatenate([key_heads, value_heads], axis=1)
+    segs = (segments + 1).astype(jnp.float32)
+    seg_rows = jnp.zeros((16, kv.shape[1]), jnp.bfloat16).at[0, :tokens].set(segs.astype(jnp.bfloat16))
+    prev = lax.ppermute(jnp.concatenate([kv, seg_rows], axis=0), blk, onward)
+
+    rows_in, prepared, prev, own_across, near_across, far_rows, far_half, w_last = lax.optimization_barrier(
+        (rows_in, prepared, prev, own_across, near_across, far_rows, far_half, w_last)
+    )
+    far_across = lax.ppermute(far_half, "groups", swap)
+    across = (own_across, near_across, far_across)
+    swapped = tuple(lax.ppermute(w, "core", swap) for w in across)
     w_last = lax.all_gather(w_last, plane, axis=0, tiled=False).reshape(parts, 2 * low, *w_share.shape)
     terms = experts(rows_in.reshape(owners * depth, 2 * width), *prepared)
+    terms, prev = lax.optimization_barrier((terms, prev))
     back = lax.all_to_all(terms.reshape(owners, depth, width), chips, 0, 0, tiled=True)
+    attention = attention_shares(queries, key_heads, value_heads, prev, segs)
 
     z = 2 * lax.axis_index("far") + lax.axis_index("near")
-    moe_input_grad, query_grad, key_part, value_part, sent = tail(
+    moe_input_grad, query_grad, kept, sent = tail(
         jnp.stack([lax.axis_index("groups"), z, core]).astype(jnp.int32),
         back.reshape(owners * depth, width), place, moe_grad,
-        (w_own, w_pair, own_across, own_swapped, pair_across, pair_swapped), w_last, *attention,
-    )
-    later = lax.ppermute(sent, blk, backward).astype(jnp.float32)
-    return (moe_input_grad, query_grad, key_part + later[0], value_part + later[1])
+        (w_own, near_rows, far_rows, *across, *swapped), w_last, *attention,
+    )
+    return (moe_input_grad, query_grad, *finish(kept, lax.ppermute(sent, blk, backward)))
 
 
 def solution(mesh):

time: 225 us -> 224 us (level)
  waiting for transfers between devices: 111 us -> 95 us
  starting transfers between devices: 22 us -> 37 us
  local copies, waits for them, and re-layouts: 26.6 us -> 38.6 us
  Pallas kernels: 43.1 us -> 37 us
  other arithmetic: 5.99 us -> 0.76 us
    ppermute x4 -> x6, waiting for transfers between devices: 53.4 us -> 38.3 us  [the longest x1 33 us: local(): far_across = lax.ppermute(far_half, 'groups', swap)]
    unnamed x44 -> x64, local copies, waits for them, and re-layouts: 20.2 us -> 30.5 us
    all_gather x1 -> x2, waiting for transfers between devices: 33.3 us -> 39.8 us  [the longest x1 36.7 us: local(): near_rows = lax.all_gather(w_near, plane[1:], axis=0, tiled=False)]
    ppermute x1, starting transfers between devices: 3.11 us -> 8.88 us  [local(): prev = lax.ppermute(jnp.concatenate([kv, seg_rows], axis=0), blk, onward)]
    all_to_all x1, waiting for transfers between devices: 5.42 us -> 0.01 us  [local(): lax.all_to_all(rows.reshape(owners, depth, 2 * width), chips, 0, 0, tiled...]
    pallas_call x1, Pallas kernels: 11.8 us -> 8.16 us  [experts(): pl.pallas_call(functools.partial(expert_kernel, steps), grid=(steps + wid...]
    pallas_call x1, Pallas kernels: 17.7 us -> 14.6 us  [tail(): pl.pallas_call(functools.partial(tail_kernel, (heads, tiles)), grid_spec=...]
    ppermute x3, starting transfers between devices: 1.25 us -> 4.24 us  [local(): other = tuple((lax.ppermute(w, 'core', swap) for w in own))]
  transfers between devices with their start and end apart: 17 -> 20, of which waited for: 8 -> 6; matrix products, arithmetic and copies ran while one was open for 3% -> 4% of each run, Pallas kernels for 11% -> 10%
where the time goes in v10:
time: 224 us; the launch traced here: 222 us
  waiting for transfers between devices  95 us (42%)
  local copies, waits for them, and re-layouts  38.6 us (17%)
  starting transfers between devices  37 us (17%)
  Pallas kernels  37 us (17%)
  between operations  14 us (6%)
    all_gather x1, waiting for transfers between devices, local(): near_rows = lax.all_gather(w_near, plane[1:], axis=0, tiled=False)  36.7 us
    ppermute x1, waiting for transfers between devices, local(): far_across = lax.ppermute(far_half, 'groups', swap)  33 us
    unnamed x64, local copies, waits for them, and re-layouts  30.5 us
    pallas_call x1, Pallas kernels, tail(): pl.pallas_call(functools.partial(tail_kernel, (heads, tiles)), grid_spec=...  14.6 us
    ppermute x1, waiting for transfers between devices, local(): w_near = lax.ppermute(w_share, 'near', swap)  12.8 us
    all_to_all x1, starting transfers between devices, local(): lax.all_to_all(terms.reshape(owners, depth, width), chips, 0, 0, tiled=True)  9.33 us
    ppermute x1, starting transfers between devices, local(): prev = lax.ppermute(jnp.concatenate([kv, seg_rows], axis=0), blk, onward)  8.88 us
    pallas_call x1, Pallas kernels, prepare_weights(): pl.pallas_call(weights_kernel, grid=(steps,), in_specs=[cols, cols, down]...  8.8 us
  transfers between devices with their start and end apart: 20, of which 6 were waited for; matrix products, arithmetic and copies ran while one was open for 4% of the time, Pallas kernels for 10%

profile of v10, /device:TPU:13, one launch (start us, length us, event | category | flops | bytes accessed | tf_op | source)
XLA Modules:
  0.0 222.4 jit_solution(4928837794617693948)
XLA Ops:
  9.5 2.3 %collective-permute-start.1 = (bf16[128,2048]{1,0:T(8,128)(2,1)}, bf16[128,2048]{1,0:T(8,128)(2,1)}, u32[]{:S(2)}, u32[]{:S(2)}) collective-permute-start(bf16[128,2048]{1,0:T(8,128)(2,1)} %constant_dynamic-slice_fusion.3), channel_id=1, source_target_pairs={{0,8},{8,0},{1,9},{9,1},{2,10},{10,2},{3,11},{11,3},{4,12},{12,4},... | collective-permute-start | bytes 1572872 | tf_op jit(solution)/shard_map/ppermute | solution.py:417
  16.5 1.6 copy-done.8
  18.7 12.8 %collective-permute-done = bf16[128,2048]{1,0:T(8,128)(2,1)S(1)} collective-permute-done((bf16[128,2048]{1,0:T(8,128)(2,1)}, bf16[128,2048]{1,0:T(8,128)(2,1)S(1)}, u32[]{:S(2)}, u32[]{:S(2)}) %collective-permute-start) | collective-permute-done | bytes 524320 | tf_op jit(solution)/shard_map/ppermute | solution.py:416
  31.5 3.2 %collective-permute-done.1 = bf16[128,2048]{1,0:T(8,128)(2,1)} collective-permute-done((bf16[128,2048]{1,0:T(8,128)(2,1)}, bf16[128,2048]{1,0:T(8,128)(2,1)}, u32[]{:S(2)}, u32[]{:S(2)}) %collective-permute-start.1) | collective-permute-done | bytes 524320 | tf_op jit(solution)/shard_map/ppermute | solution.py:417
  34.8 4.2 %all-to-all-start = ((bf16[8,48,4096]{2,1,0:T(8,128)(2,1)}), bf16[8,48,4096]{2,1,0:T(8,128)(2,1)S(1)}, u32[]{:S(2)}, u32[]{:S(2)}) async-start(bf16[8,48,4096]{2,1,0:T(8,128)(2,1)} %bitcast.26), calls=%async_computation | async-start | bytes 6291456 | tf_op jit(solution)/shard_map/all_to_all | solution.py:428
  39.7 3.7 %collective-permute-start.2 = (bf16[2048,384]{1,0:T(8,128)(2,1)}, bf16[2048,384]{1,0:T(8,128)(2,1)}, u32[]{:S(2)}, u32[]{:S(2)}) collective-permute-start(bf16[2048,384]{1,0:T(8,128)(2,1)} %refs_0_.1), channel_id=1, source_target_pairs={{0,1},{1,0},{2,3},{3,2},{4,5},{5,4},{6,7},{7,6},{8,9},{9,8},{10,11... | collective-permute-start | bytes 4718600 | tf_op jit(solution)/shard_map/ppermute | solution.py:420
  44.0 2.4 %constant_dynamic-slice_fusion.2 = bf16[2,128,2048]{2,1,0:T(8,128)(2,1)} fusion(bf16[4,128,2048]{2,1,0:T(8,128)(2,1)} %bitcast.22, s32[]{:T(128)S(6)} %select_n.9), kind=kLoop, calls=%fused_computation.5 | loop fusion | bytes 2097156 | tf_op jit(solution)/shard_map/dynamic_slice | solution.py:427
  47.6 36.7 %all-gather.11.cloned.1.call-done = bf16[512,2048]{1,0:T(8,128)(2,1)} async-done(((bf16[128,2048]{1,0:T(8,128)(2,1)}), bf16[512,2048]{1,0:T(8,128)(2,1)}) %all-gather.11.cloned.1.call-update) | async-done | bytes 2097168 | tf_op jit(solution)/shard_map/all_gather | solution.py:430
  84.3 2.4 %constant_dynamic-slice_fusion.1 = bf16[2,128,2048]{2,1,0:T(8,128)(2,1)} fusion(bf16[4,128,2048]{2,1,0:T(8,128)(2,1)} %bitcast.24, s32[]{:T(128)S(6)} %select_n.9), kind=kLoop, calls=%fused_computation.4 | loop fusion | bytes 2097156 | tf_op jit(solution)/shard_map/dynamic_slice | solution.py:427
  88.6 8.9 %collective-permute-start.5 = (bf16[144,512]{1,0:T(8,128)(2,1)}, bf16[144,512]{1,0:T(8,128)(2,1)S(1)}, u32[]{:S(2)}, u32[]{:S(2)}) collective-permute-start(bf16[144,512]{1,0:T(8,128)(2,1)} %fusion.1), channel_id=1, source_target_pairs={{0,1},{1,2},{2,3},{3,4},{4,5},{5,6},{6,7},{7,8},{8,9},{9,10},{10,1... | collective-permute-start | bytes 442376 | tf_op jit(solution)/shard_map/ppermute | solution.py:439
  100.5 8.8 %prepare_weights.1 = (bf16[3,2048,512]{2,1,0:T(8,128)(2,1)}, bf16[3,2048,256]{2,1,0:T(8,128)(2,1)}, bf16[3,512,2048]{2,1,0:T(8,128)(2,1)}) custom-call(bf16[2048,384]{1,0:T(8,128)(2,1)S(1)} %copy-done.11, bf16[2048,384]{1,0:T(8,128)(2,1)S(1)} %copy-done.12, bf16[384,2048]{1,0:T(8,128)(2,1)S(1)} %copy-done.13, ...), custom_call_target="tpu_custom_call" | custom-call | tf_op jit(solution)/shard_map/prepare_weights/pallas_call | solution.py:94
  109.3 3.2 %all-gather.13.cloned.1.call-done = bf16[512,2048]{1,0:T(8,128)(2,1)} async-done(((bf16[128,2048]{1,0:T(8,128)(2,1)}), bf16[512,2048]{1,0:T(8,128)(2,1)}) %all-gather.13.cloned.1.call-update) | async-done | bytes 2097168 | tf_op jit(solution)/shard_map/all_gather | solution.py:432
  112.5 2.4 %constant_dynamic-slice_fusion = bf16[2,128,2048]{2,1,0:T(8,128)(2,1)} fusion(bf16[4,128,2048]{2,1,0:T(8,128)(2,1)} %bitcast.29, s32[]{:T(128)S(6)} %select_n.9), kind=kLoop, calls=%fused_computation.3 | loop fusion | bytes 2097156 | tf_op jit(solution)/shard_map/dynamic_slice | solution.py:427
  114.9 2.8 %copy-done.3 = bf16[3,2048,512]{2,1,0:T(8,128)(2,1)S(1)} copy-done((bf16[3,2048,512]{2,1,0:T(8,128)(2,1)S(1)}, bf16[3,2048,512]{2,1,0:T(8,128)(2,1)}, u32[]{:S(2)}) %copy-start.3) | copy-done | bytes 6291480
  117.7 2.8 %copy-done.4 = bf16[3,512,2048]{2,1,0:T(8,128)(2,1)S(1)} copy-done((bf16[3,512,2048]{2,1,0:T(8,128)(2,1)S(1)}, bf16[3,512,2048]{2,1,0:T(8,128)(2,1)}, u32[]{:S(2)}) %copy-start.4) | copy-done | bytes 6291480
  120.5 1.9 copy-done.7
  122.4 8.2 %expert_terms.1 = bf16[384,2048]{1,0:T(8,128)(2,1)S(1)} custom-call(bf16[384,4096]{1,0:T(8,128)(2,1)S(1)} %bitcast.19, bf16[3,2048,512]{2,1,0:T(8,128)(2,1)S(1)} %copy-done.3, bf16[3,2048,256]{2,1,0:T(8,128)(2,1)S(1)} %copy-done.7, bf16[3,512,2048]{2,1,0:T(8,128)(2,1)S(1)} %copy-done.4), custom_call_target="tpu_custom_call" | custom-call | tf_op jit(solution)/shard_map/expert_terms/pallas_call | solution.py:145
  131.7 9.3 %all-to-all-start.1 = ((bf16[8,48,2048]{2,1,0:T(8,128)(2,1)}), bf16[8,48,2048]{2,1,0:T(8,128)(2,1)S(1)}, u32[]{:S(2)}, u32[]{:S(2)}) async-start(bf16[8,48,2048]{2,1,0:T(8,128)(2,1)} %bitcast.20), calls=%async_computation.1 | async-start | bytes 3145728 | tf_op jit(solution)/shard_map/all_to_all | solution.py:450
  143.4 33.0 %collective-permute-done.9.refs_5_ = bf16[2,128,2048]{2,1,0:T(8,128)(2,1)} collective-permute-done((bf16[2,128,2048]{2,1,0:T(8,128)(2,1)}, bf16[2,128,2048]{2,1,0:T(8,128)(2,1)}, u32[]{:S(2)}, u32[]{:S(2)}) %collective-permute-start.9) | collective-permute-done | bytes 1048608 | tf_op jit(solution)/shard_map/ppermute | solution.py:444
  177.7 3.5 %attention_shares.1 = (bf16[2,2048,256]{2,1,0:T(8,128)(2,1)S(1)}, bf16[2,256,2048]{2,1,0:T(8,128)(2,1)S(1)}, bf16[2,2048,128]{2,1,0:T(8,128)(2,1)S(1)}, bf16[2,2...) custom-call(bf16[128,4096]{1,0:T(8,128)(2,1)S(1)} %copy-done.14, bf16[128,256]{1,0:T(8,128)(2,1)S(1)} %copy-done.19, ...), custom_call_target="tpu_custom_call" | custom-call | tf_op jit(solution)/shard_map/attention_shares/pallas_call | solution.py:201
  187.8 1.6 copy-done.6
  193.3 14.6 %tail_attention.1 = (bf16[128,2048]{1,0:T(8,128)(2,1)}, bf16[128,4096]{1,0:T(8,128)(2,1)}, f32[2,128,256]{2,1,0:T(8,128)S(1)}, bf16[2,128,256]{2,1,0:T(8,128)(2,1)S(1)}) custom-call(s32[3]{0:T(128)S(1)} %pad_add_fusion.place_info, bf16[384,2048]{1,0:T(8,128)(2,1)S(1)} %bitcast.21, bf16[128,384]{1,0:T(8,128)(2,1)S(1)} %copy-done.26, ...), custom_call_target="tpu_custom_call" | custom-call | flops 2147483648 | bytes 23068672 | tf_op jit(solution)/shard_map/tail_attention/pallas_call | solution.py:330
  208.0 1.9 collective-permute-start.13
  209.9 5.3 %collective-permute-done.13.later_ref = bf16[2,128,256]{2,1,0:T(8,128)(2,1)S(1)} collective-permute-done((bf16[2,128,256]{2,1,0:T(8,128)(2,1)S(1)}, bf16[2,128,256]{2,1,0:T(8,128)(2,1)S(1)}, u32[]{:S(2)}, u32[]{:S(2)}) %collective-permute-start.13) | collective-permute-done | bytes 131104 | tf_op jit(solution)/shard_map/ppermute | solution.py:459
  (98 shorter events, 30.9 us)
Async XLA Ops:
  7.2 27.6 %all-gather.9.cloned.1.call-start = ((), (), s32[]{:S(2)}) async-start(), calls=%async_computation.2 | async-start | bytes 2621440 | tf_op jit(solution)/shard_map/all_gather | solution.py:424
  9.3 75.0 %all-gather.11.cloned.1.call-start = ((), (), s32[]{:S(2)}) async-start(), calls=%async_computation.3 | async-start | bytes 2621440 | tf_op jit(solution)/shard_map/all_gather | solution.py:430
  9.3 22.2 %collective-permute-start = (bf16[128,2048]{1,0:T(8,128)(2,1)}, bf16[128,2048]{1,0:T(8,128)(2,1)S(1)}, u32[]{:S(2)}, u32[]{:S(2)}) collective-permute-start(bf16[128,2048]{1,0:T(8,128)(2,1)} %constant_dynamic-slice_fusion.3), channel_id=1, source_target_pairs={{0,4},{4,0},{1,5},{5,1},{2,6},{6,2},{3,7},{7,3},{8,12},{12,8},{9,1... | collective-permute-start | bytes 1572872 | tf_op jit(solution)/shard_map/ppermute | solution.py:416
  9.5 25.2 %collective-permute-start.1 = (bf16[128,2048]{1,0:T(8,128)(2,1)}, bf16[128,2048]{1,0:T(8,128)(2,1)}, u32[]{:S(2)}, u32[]{:S(2)}) collective-permute-start(bf16[128,2048]{1,0:T(8,128)(2,1)} %constant_dynamic-slice_fusion.3), channel_id=1, source_target_pairs={{0,8},{8,0},{1,9},{9,1},{2,10},{10,2},{3,11},{11,3},{4,12},{12,4},... | collective-permute-start | bytes 1572872 | tf_op jit(solution)/shard_map/ppermute | solution.py:417
  34.8 80.1 %all-to-all-start = ((bf16[8,48,4096]{2,1,0:T(8,128)(2,1)}), bf16[8,48,4096]{2,1,0:T(8,128)(2,1)S(1)}, u32[]{:S(2)}, u32[]{:S(2)}) async-start(bf16[8,48,4096]{2,1,0:T(8,128)(2,1)} %bitcast.26), calls=%async_computation | async-start | bytes 6291456 | tf_op jit(solution)/shard_map/all_to_all | solution.py:428
  39.0 73.5 %all-gather.13.cloned.1.call-start = ((), (), s32[]{:S(2)}) async-start(), calls=%async_computation.4 | async-start | bytes 2621440 | tf_op jit(solution)/shard_map/all_gather | solution.py:432
  39.7 146.5 %all-gather.15.cloned.1.call-start = ((), (), s32[]{:S(2)}) async-start(), calls=%async_computation.5 | async-start | bytes 4718592 | tf_op jit(solution)/shard_map/all_gather | solution.py:447
  39.7 48.2 %collective-permute-start.2 = (bf16[2048,384]{1,0:T(8,128)(2,1)}, bf16[2048,384]{1,0:T(8,128)(2,1)}, u32[]{:S(2)}, u32[]{:S(2)}) collective-permute-start(bf16[2048,384]{1,0:T(8,128)(2,1)} %refs_0_.1), channel_id=1, source_target_pairs={{0,1},{1,0},{2,3},{3,2},{4,5},{5,4},{6,7},{7,6},{8,9},{9,8},{10,11... | collective-permute-start | bytes 4718600 | tf_op jit(solution)/shard_map/ppermute | solution.py:420
  43.5 45.2 %collective-permute-start.3 = (bf16[2048,384]{1,0:T(8,128)(2,1)}, bf16[2048,384]{1,0:T(8,128)(2,1)}, u32[]{:S(2)}, u32[]{:S(2)}) collective-permute-start(bf16[2048,384]{1,0:T(8,128)(2,1)} %refs_1_.1), channel_id=1, source_target_pairs={{0,1},{1,0},{2,3},{3,2},{4,5},{5,4},{6,7},{7,6},{8,9},{9,8},{10,11... | collective-permute-start | bytes 4718600 | tf_op jit(solution)/shard_map/ppermute | solution.py:420
  43.5 54.0 %collective-permute-start.4 = (bf16[384,2048]{1,0:T(8,128)(2,1)}, bf16[384,2048]{1,0:T(8,128)(2,1)}, u32[]{:S(2)}, u32[]{:S(2)}) collective-permute-start(bf16[384,2048]{1,0:T(8,128)(2,1)} %refs_2_.1), channel_id=1, source_target_pairs={{0,1},{1,0},{2,3},{3,2},{4,5},{5,4},{6,7},{7,6},{8,9},{9,8},{10,11... | collective-permute-start | bytes 4718600 | tf_op jit(solution)/shard_map/ppermute | solution.py:420
  44.0 44.0 %copy-start.19 = (bf16[128,256]{1,0:T(8,128)(2,1)S(1)}, bf16[128,256]{1,0:T(8,128)(2,1)}, u32[]{:S(2)}) copy-start(bf16[128,256]{1,0:T(8,128)(2,1)} %key_ref.1) | copy-start | bytes 196612
  44.0 44.0 %copy-start.20 = (bf16[128,256]{1,0:T(8,128)(2,1)S(1)}, bf16[128,256]{1,0:T(8,128)(2,1)}, u32[]{:S(2)}) copy-start(bf16[128,256]{1,0:T(8,128)(2,1)} %value_ref.1) | copy-start | bytes 196612
  46.4 68.5 %collective-permute-start.6 = (bf16[2,128,2048]{2,1,0:T(8,128)(2,1)}, bf16[2,128,2048]{2,1,0:T(8,128)(2,1)}, u32[]{:S(2)}, u32[]{:S(2)}) collective-permute-start(bf16[2,128,2048]{2,1,0:T(8,128)(2,1)} %constant_dynamic-slice_fusion.2), channel_id=1, source_target_pairs={{0,16},{16,0},{1,17},{17,1},{2,18},{18,2},{3,19},{19,3},{4,20},{20... | collective-permute-start | bytes 3145736 | tf_op jit(solution)/shard_map/ppermute | solution.py:429
  86.7 28.2 %collective-permute-start.7 = (bf16[2,128,2048]{2,1,0:T(8,128)(2,1)}, bf16[2,128,2048]{2,1,0:T(8,128)(2,1)}, u32[]{:S(2)}, u32[]{:S(2)}) collective-permute-start(bf16[2,128,2048]{2,1,0:T(8,128)(2,1)} %constant_dynamic-slice_fusion.1), channel_id=1, source_target_pairs={{0,16},{16,0},{1,17},{17,1},{2,18},{18,2},{3,19},{19,3},{4,20},{20... | collective-permute-start | bytes 3145736 | tf_op jit(solution)/shard_map/ppermute | solution.py:431
  87.9 27.0 %collective-permute-start.8 = (bf16[128,2048]{1,0:T(8,128)(2,1)}, bf16[128,2048]{1,0:T(8,128)(2,1)}, u32[]{:S(2)}, u32[]{:S(2)}) collective-permute-start(bf16[128,2048]{1,0:T(8,128)(2,1)} %collective-permute-done.1), channel_id=1, source_target_pairs={{0,4},{4,0},{1,5},{5,1},{2,6},{6,2},{3,7},{7,3},{8,12},{12,8},{9,1... | collective-permute-start | bytes 1572872 | tf_op jit(solution)/shard_map/ppermute | solution.py:434
  88.6 26.2 %collective-permute-start.5 = (bf16[144,512]{1,0:T(8,128)(2,1)}, bf16[144,512]{1,0:T(8,128)(2,1)S(1)}, u32[]{:S(2)}, u32[]{:S(2)}) collective-permute-start(bf16[144,512]{1,0:T(8,128)(2,1)} %fusion.1), channel_id=1, source_target_pairs={{0,1},{1,2},{2,3},{3,4},{4,5},{5,6},{6,7},{7,8},{8,9},{9,10},{10,1... | collective-permute-start | bytes 442376 | tf_op jit(solution)/shard_map/ppermute | solution.py:439
  131.7 46.0 %copy-start.14 = (bf16[128,4096]{1,0:T(8,128)(2,1)S(1)}, bf16[128,4096]{1,0:T(8,128)(2,1)}, u32[]{:S(2)}) copy-start(bf16[128,4096]{1,0:T(8,128)(2,1)} %q_ref.1) | copy-start | bytes 3145732
  131.7 54.5 %copy-start.18 = (bf16[128,2048]{1,0:T(8,128)(2,1)S(1)}, bf16[128,2048]{1,0:T(8,128)(2,1)}, u32[]{:S(2)}) copy-start(bf16[128,2048]{1,0:T(8,128)(2,1)} %grad_ref.3) | copy-start | bytes 1572868
  131.7 54.5 %all-to-all-start.1 = ((bf16[8,48,2048]{2,1,0:T(8,128)(2,1)}), bf16[8,48,2048]{2,1,0:T(8,128)(2,1)S(1)}, u32[]{:S(2)}, u32[]{:S(2)}) async-start(bf16[8,48,2048]{2,1,0:T(8,128)(2,1)} %bitcast.20), calls=%async_computation.1 | async-start | bytes 3145728 | tf_op jit(solution)/shard_map/all_to_all | solution.py:450
  141.0 35.4 %collective-permute-start.9 = (bf16[2,128,2048]{2,1,0:T(8,128)(2,1)}, bf16[2,128,2048]{2,1,0:T(8,128)(2,1)}, u32[]{:S(2)}, u32[]{:S(2)}) collective-permute-start(bf16[2,128,2048]{2,1,0:T(8,128)(2,1)} %constant_dynamic-slice_fusion), channel_id=1, source_target_pairs={{0,16},{16,0},{1,17},{17,1},{2,18},{18,2},{3,19},{19,3},{4,20},{20... | collective-permute-start | bytes 3145736 | tf_op jit(solution)/shard_map/ppermute | solution.py:444
  141.8 44.3 %collective-permute-start.10 = (bf16[2,128,2048]{2,1,0:T(8,128)(2,1)}, bf16[2,128,2048]{2,1,0:T(8,128)(2,1)}, u32[]{:S(2)}, u32[]{:S(2)}) collective-permute-start(bf16[2,128,2048]{2,1,0:T(8,128)(2,1)} %collective-permute-done.6.refs_3_), channel_id=1, source_target_pairs={{0,1},{1,0},{2,3},{3,2},{4,5},{5,4},{6,7},{7,6},{8,9},{9,8},{10,11... | collective-permute-start | bytes 3145736 | tf_op jit(solution)/shard_map/ppermute | solution.py:446
  143.4 42.8 %collective-permute-start.11 = (bf16[2,128,2048]{2,1,0:T(8,128)(2,1)}, bf16[2,128,2048]{2,1,0:T(8,128)(2,1)}, u32[]{:S(2)}, u32[]{:S(2)}) collective-permute-start(bf16[2,128,2048]{2,1,0:T(8,128)(2,1)} %collective-permute-done.7.refs_4_), channel_id=1, source_target_pairs={{0,1},{1,0},{2,3},{3,2},{4,5},{5,4},{6,7},{7,6},{8,9},{9,8},{10,11... | collective-permute-start | bytes 3145736 | tf_op jit(solution)/shard_map/ppermute | solution.py:446
  176.5 9.7 %collective-permute-start.12 = (bf16[2,128,2048]{2,1,0:T(8,128)(2,1)}, bf16[2,128,2048]{2,1,0:T(8,128)(2,1)}, u32[]{:S(2)}, u32[]{:S(2)}) collective-permute-start(bf16[2,128,2048]{2,1,0:T(8,128)(2,1)} %collective-permute-done.9.refs_5_), channel_id=1, source_target_pairs={{0,1},{1,0},{2,3},{3,2},{4,5},{5,4},{6,7},{7,6},{8,9},{9,8},{10,11... | collective-permute-start | bytes 3145736 | tf_op jit(solution)/shard_map/ppermute | solution.py:446
  208.0 7.2 %collective-permute-start.13 = (bf16[2,128,256]{2,1,0:T(8,128)(2,1)S(1)}, bf16[2,128,256]{2,1,0:T(8,128)(2,1)S(1)}, u32[]{:S(2)}, u32[]{:S(2)}) collective-permute-start(bf16[2,128,256]{2,1,0:T(8,128)(2,1)S(1)} %get-tuple-element.77), channel_id=1, source_target_pairs={{1,0},{2,1},{3,2},{4,3},{5,4},{6,5},{7,6},{8,7},{9,8},{10,9},{11,1... | collective-permute-start | bytes 393224 | tf_op jit(solution)/shard_map/ppermute | solution.py:459
  (28 other events, 113.5 us)
Sparse Core Ops, SparseCore 0:
  10.2 23.1 all-gather.8
  34.9 49.3 all-gather.10
  85.8 26.6 all-gather.12
  115.1 57.2 all-gather.14

commit v11 on v10

--- a/solution.py
+++ b/solution.py
@@ -105,7 +105,7 @@
             jax.ShapeDtypeStruct((steps, width, 2 * tile), jnp.bfloat16),
             jax.ShapeDtypeStruct((steps, 4 * tile, width), jnp.bfloat16),
         ),
-        compiler_params=params(48),
+        compiler_params=params(20),
         cost_estimate=LIGHT,
         name="prepare_weights",
     )(*own, *other)
@@ -213,7 +213,7 @@
         ],
         out_specs=[group(shape) for shape in shapes],
         out_shape=[made(shape) for shape in shapes],
-        compiler_params=params(32),
+        compiler_params=params(16),
         cost_estimate=LIGHT,
         name="attention_shares",
     )(queries, key_heads, value_heads, prev, prev, prev, segs[None, :], segs[:, None])
@@ -223,13 +223,14 @@
     plan, place_info, back_ref, place_ref, grad_ref, *refs
 ):
     heads, tiles = plan
-    mine, across, swapped, refs = refs[:3], refs[3:6], refs[6:9], refs[9:]
-    last_ref, low_ref, turned_ref, q_ref, key_ref, value_ref, *refs = refs
+    mine, across, refs = refs[:8], refs[8:16], refs[16:]
+    low_ref, turned_ref, q_ref, key_ref, value_ref, *refs = refs
     moe_ref, query_out, kept_out, sent_out, stream, held, sums = refs
     step = pl.program_id(0)
     tokens = query_out.shape[0]
     part_size = stream.shape[2]
-    half = last_ref.shape[1] // 2
+    size = mine[0].shape[1]
+    spread = part_size // size
     here, core = place_info[1], place_info[2]
 
     @pl.when(step == 0)
@@ -237,8 +238,11 @@
         moe = dot(place_ref[...], back_ref[...]).astype(jnp.bfloat16)
         moe_ref[...] = moe
         added = (grad_ref[...].astype(jnp.float32) + moe.astype(jnp.float32)).astype(jnp.bfloat16)
-        for eighth in range(8):
-            stream[eighth] = added[:, eighth * part_size : (eighth + 1) * part_size]
+        for z in range(4):
+            for rest in range(spread):
+                for side in range(2):
+                    source = ((z * spread + rest) * 2 + side) * size
+                    stream[2 * z + side, :, rest * size : (rest + 1) * size] = added[:, source : source + size]
 
     @pl.when((step > 0) & ((step - 1) % tiles == 0))
     def _():
@@ -246,9 +250,9 @@
 
     def project(pieces):
         head_grad = None
-        for turn, side, piece in pieces:
-            rows = stream[2 * (here ^ turn) + side]
-            part = dot(rows, piece.reshape(part_size, piece.shape[-1]))
+        for i, piece in enumerate(pieces):
+            rows = stream[2 * (here ^ (i // 2)) + (core ^ (i % 2))]
+            part = dot(rows, piece[...].reshape(part_size, piece.shape[-1]))
             head_grad = part if head_grad is None else head_grad + part
         return head_grad.astype(jnp.bfloat16)
 
@@ -268,31 +272,19 @@
         for head in range(heads):
             query_out[:, head * HD : (head + 1) * HD] = query_grad[head * tokens : (head + 1) * tokens, :]
 
-    sides = [(side, slice(side * half, (side + 1) * half)) for side in range(2)]
-
-    def own_pieces():
-        pieces = [(turn, side, mine[turn][part]) for turn in range(3) for side, part in sides]
-        return pieces + [(3, side, last_ref[0, part]) for side, part in sides]
-
-    def other_pieces():
-        pieces = []
-        for turn in range(3):
-            pieces += [(turn, core, across[turn][...]), (turn, 1 - core, swapped[turn][...])]
-        return pieces + [(3, side, last_ref[0, part]) for side, part in sides]
-
     @pl.when(step == 0)
     def _():
-        hold(project(own_pieces()))
+        hold(project(mine))
 
     @pl.when((step > 0) & (step < tiles))
     def _():
-        head_grad = project(own_pieces())
+        head_grad = project(mine)
         attend()
         hold(head_grad)
 
     @pl.when((step >= tiles) & (step < 2 * tiles))
     def _():
-        head_grad = project(other_pieces())
+        head_grad = project(across)
         attend()
         hold(head_grad)
 
@@ -306,9 +298,9 @@
         sent_out[...] = sums[:, :tokens, :].astype(jnp.bfloat16)
 
 
-def tail(place_info, back, place, moe_grad, pieces, w_last, low, turned, query, keys, values):
+def tail(place_info, back, place, moe_grad, pieces, low, turned, query, keys, values):
     tokens, width = moe_grad.shape
-    spread, size, cols = w_last.shape[1:]
+    spread, size, cols = pieces[0].shape
     span = keys.shape[1]
     heads = 4
     tile = heads * HD
@@ -319,13 +311,9 @@
     whole = lambda shape: pl.BlockSpec(shape, lambda i, info: (0,) * len(shape))
     group = lambda shape: pl.BlockSpec((1,) + shape, lambda i, info: (kv_group(i, info), 0, 0))
     rows = lambda shape: pl.BlockSpec((1,) + shape, lambda i, info: (kv_group(i, info), was(i) % tiles, 0))
-    now = lambda i: jnp.minimum(i, steps - 1)
     own_tile = lambda i: jnp.minimum(i, tiles - 1)
     other_tile = lambda i: jnp.minimum(jnp.maximum(i - tiles, 0), tiles - 1)
-    both_spec = pl.BlockSpec(
-        (1, spread, size, tile), lambda i, info: ((now(i) // tiles) ^ info[0], 0, 0, now(i) % tiles)
-    )
-    one = lambda count, turn: pl.BlockSpec((count, size, tile), lambda i, info: (0, 0, turn(i)))
+    piece = lambda turn: pl.BlockSpec((spread, size, tile), lambda i, info: (0, 0, turn(i)))
     kv = pl.BlockSpec((2, tokens, HD), lambda i, info: (0, 0, kv_group(i, info)))
     return pl.pallas_call(
         functools.partial(tail_kernel, (heads, tiles)),
@@ -333,9 +321,8 @@
             num_scalar_prefetch=1,
             grid=(steps + 1,),
             in_specs=[whole(back.shape), whole(place.shape), whole(moe_grad.shape)]
-            + [one(spread, own_tile)] * 3
-            + [one(spread // 2, other_tile)] * 6
-            + [both_spec]
+            + [piece(own_tile)] * 8
+            + [piece(other_tile)] * 8
             + [
                 rows((heads * tokens, span)),
                 pl.BlockSpec(
@@ -354,7 +341,7 @@
                 kv,
             ],
             scratch_shapes=[
-                pltpu.VMEM((8, tokens, spread * size // 2), jnp.bfloat16),
+                pltpu.VMEM((8, tokens, spread * size), jnp.bfloat16),
                 pltpu.VMEM((heads * tokens, HD), jnp.bfloat16),
                 pltpu.VMEM((2, span, HD), jnp.float32),
             ],
@@ -365,12 +352,12 @@
             jax.ShapeDtypeStruct((2, tokens, KVH * HD), jnp.float32),
             jax.ShapeDtypeStruct((2, tokens, KVH * HD), jnp.bfloat16),
         ),
-        compiler_params=params(40),
+        compiler_params=params(56),
         cost_estimate=pl.CostEstimate(
             flops=2 * tokens * width * KVH * cols, bytes_accessed=22 * MIB, transcendentals=0
         ),
         name="tail_attention",
-    )(place_info, back, place, moe_grad, *pieces, w_last, low, turned, query, keys, values)
+    )(place_info, back, place, moe_grad, *pieces, low, turned, query, keys, values)
 
 
 def finish_kernel(kept_ref, later_ref, key_ref, value_ref):
@@ -416,45 +403,42 @@
     w_near = lax.ppermute(w_share, "near", swap)
     w_far = lax.ppermute(w_share, "far", swap)
 
+    rows, place = pick(routes, route_weight, moe_input, moe_grad, owners, depth)
+    line = lambda w: lax.all_gather(w, "low", axis=0, tiled=False)
+    cross = lambda w: lax.ppermute(w, "groups", swap)
+    other_core = lambda w: lax.ppermute(w, "core", swap)
     own = (w_gate, w_up, w_down)
-    other = tuple(lax.ppermute(w, "core", swap) for w in own)
-    rows, place = pick(routes, route_weight, moe_input, moe_grad, owners, depth)
-    plane = ("groups", "low", "core")
-    core = lax.axis_index("core")
-    w_own = lax.all_gather(w_share, plane[1:], axis=0, tiled=False)
-    rows, w_near, w_far, w_own = lax.optimization_barrier((rows, w_near, w_far, w_own))
-
-    half_of = lambda w: lax.dynamic_slice_in_dim(w, core * low, low, 0)
-    rows_in = lax.all_to_all(rows.reshape(owners, depth, 2 * width), chips, 0, 0, tiled=True)
-    own_across = lax.ppermute(half_of(w_own), "groups", swap)
-    near_rows = lax.all_gather(w_near, plane[1:], axis=0, tiled=False)
-    near_across = lax.ppermute(half_of(near_rows), "groups", swap)
-    far_rows = lax.all_gather(w_far, plane[1:], axis=0, tiled=False)
-    far_half = half_of(far_rows)
-    w_last = lax.ppermute(w_far, "near", swap)
-    prepared = prepare_weights(own, other)
+    other = tuple(other_core(w) for w in own)
+
+    key_heads, value_heads, segments, place = lax.optimization_barrier((key_heads, value_heads, segments, place))
     kv = jnp.concatenate([key_heads, value_heads], axis=1)
     segs = (segments + 1).astype(jnp.float32)
     seg_rows = jnp.zeros((16, kv.shape[1]), jnp.bfloat16).at[0, :tokens].set(segs.astype(jnp.bfloat16))
     prev = lax.ppermute(jnp.concatenate([kv, seg_rows], axis=0), blk, onward)
-
-    rows_in, prepared, prev, own_across, near_across, far_rows, far_half, w_last = lax.optimization_barrier(
-        (rows_in, prepared, prev, own_across, near_across, far_rows, far_half, w_last)
+    own_line = line(w_share)
+    rows, w_near, w_far, own_line, prev = lax.optimization_barrier((rows, w_near, w_far, own_line, prev))
+
+    rows_in = lax.all_to_all(rows.reshape(owners, depth, 2 * width), chips, 0, 0, tiled=True)
+    lines = [own_line, line(w_near), line(w_far)]
+    crossed = [cross(w) for w in lines]
+    w_last = lax.ppermute(w_far, "near", swap)
+    prepared = prepare_weights(own, other)
+    attention = attention_shares(queries, key_heads, value_heads, prev, segs)
+    rows_in, prepared, attention, lines, crossed, w_last = lax.optimization_barrier(
+        (rows_in, prepared, attention, lines, crossed, w_last)
     )
-    far_across = lax.ppermute(far_half, "groups", swap)
-    across = (own_across, near_across, far_across)
-    swapped = tuple(lax.ppermute(w, "core", swap) for w in across)
-    w_last = lax.all_gather(w_last, plane, axis=0, tiled=False).reshape(parts, 2 * low, *w_share.shape)
+    last_line = line(w_last)
+    last_crossed = cross(last_line)
     terms = experts(rows_in.reshape(owners * depth, 2 * width), *prepared)
-    terms, prev = lax.optimization_barrier((terms, prev))
+    terms, lines, crossed = lax.optimization_barrier((terms, lines, crossed))
     back = lax.all_to_all(terms.reshape(owners, depth, width), chips, 0, 0, tiled=True)
-    attention = attention_shares(queries, key_heads, value_heads, prev, segs)
+    both = lambda pieces: [w for piece in pieces for w in (piece, other_core(piece))]
 
     z = 2 * lax.axis_index("far") + lax.axis_index("near")
     moe_input_grad, query_grad, kept, sent = tail(
-        jnp.stack([lax.axis_index("groups"), z, core]).astype(jnp.int32),
+        jnp.stack([lax.axis_index("groups"), z, lax.axis_index("core")]).astype(jnp.int32),
         back.reshape(owners * depth, width), place, moe_grad,
-        (w_own, near_rows, far_rows, *across, *swapped), w_last, *attention,
+        both(lines + [last_line]) + both(crossed + [last_crossed]), *attention,
     )
     return (moe_input_grad, query_grad, *finish(kept, lax.ppermute(sent, blk, backward)))
 

time: 224 us -> 237 us (1.058)
  waiting for transfers between devices: 95 us -> 120 us
  local copies, waits for them, and re-layouts: 38.6 us -> 30 us
  starting transfers between devices: 37 us -> 30.4 us
    all_gather x4, waiting for transfers between devices: 39.9 us -> 65.8 us  [local(): line = lambda w: lax.all_gather(w, 'low', axis=0, tiled=False)]
    ppermute x1, waiting for transfers between devices: 0.01 us -> 18.9 us  [local(): prev = lax.ppermute(jnp.concatenate([kv, seg_rows], axis=0), blk, onward)]
    ppermute x1, waiting for transfers between devices: 12.8 us -> 0.01 us  [local(): w_near = lax.ppermute(w_share, 'near', swap)]
    ppermute x9 -> x15, waiting for transfers between devices: 33.1 us -> 23.6 us  [the longest x4 19.6 us: local(): cross = lambda w: lax.ppermute(w, 'groups', swap)]
    dynamic_slice x3 -> x0, local copies, waits for them, and re-layouts: 7.21 us -> none  [local(): half_of = lambda w: lax.dynamic_slice_in_dim(w, core * low, low, 0)]
    all_to_all x1, waiting for transfers between devices: 0.01 us -> 6.06 us  [local(): lax.all_to_all(terms.reshape(owners, depth, width), chips, 0, 0, tiled=True)]
    ppermute x1, starting transfers between devices: 8.88 us -> 3.14 us  [local(): prev = lax.ppermute(jnp.concatenate([kv, seg_rows], axis=0), blk, onward)]
    all_to_all x1, starting transfers between devices: 9.33 us -> 4.08 us  [local(): lax.all_to_all(terms.reshape(owners, depth, width), chips, 0, 0, tiled=True)]
  transfers between devices with their start and end apart: 20 -> 26, of which waited for: 6 -> 9; matrix products, arithmetic and copies ran while one was open for 4% -> 0% of each run, Pallas kernels for 10% -> 9%
where the time goes in v11:
time: 237 us; the launch traced here: 233 us
  waiting for transfers between devices  120 us (51%)
  Pallas kernels  38.1 us (16%)
  starting transfers between devices  30.4 us (13%)
  local copies, waits for them, and re-layouts  30 us (13%)
  between operations  14.1 us (6%)
    all_gather x4, waiting for transfers between devices, local(): line = lambda w: lax.all_gather(w, 'low', axis=0, tiled=False)  65.8 us
    unnamed x60, local copies, waits for them, and re-layouts  29 us
    ppermute x4, waiting for transfers between devices, local(): cross = lambda w: lax.ppermute(w, 'groups', swap)  19.6 us
    ppermute x1, waiting for transfers between devices, local(): prev = lax.ppermute(jnp.concatenate([kv, seg_rows], axis=0), blk, onward)  18.9 us
    pallas_call x1, Pallas kernels, tail(): pl.pallas_call(functools.partial(tail_kernel, (heads, tiles)), grid_spec=...  16.5 us
    pallas_call x1, Pallas kernels, experts(): pl.pallas_call(functools.partial(expert_kernel, steps), grid=(steps + wid...  10.7 us
    ppermute x11, starting transfers between devices, local(): other_core = lambda w: lax.ppermute(w, 'core', swap)  7.22 us
    all_to_all x1, waiting for transfers between devices, local(): lax.all_to_all(terms.reshape(owners, depth, width), chips, 0, 0, tiled=True)  6.06 us
  transfers between devices with their start and end apart: 26, of which 9 were waited for; matrix products, arithmetic and copies ran while one was open for 0% of the time, Pallas kernels for 9%

profile of v11, /device:TPU:13, one launch (start us, length us, event | category | flops | bytes accessed | tf_op | source)
XLA Modules:
  0.0 233.3 jit_solution(766979947726610190)
XLA Ops:
  9.5 2.3 collective-permute-start.1
  14.7 3.1 %collective-permute-start.2 = (bf16[144,512]{1,0:T(8,128)(2,1)S(1)}, bf16[144,512]{1,0:T(8,128)(2,1)S(1)}, u32[]{:S(2)}, u32[]{:S(2)}) collective-permute-start(bf16[144,512]{1,0:T(8,128)(2,1)S(1)} %fusion.1), channel_id=1, source_target_pairs={{0,1},{1,2},{2,3},{3,4},{4,5},{5,6},{6,7},{7,8},{8,9},{9,10},{10,1... | collective-permute-start | bytes 442376 | tf_op jit(solution)/shard_map/ppermute | solution.py:417
  17.8 18.9 %collective-permute-done.2.prev_key_ref.prev_value_ref.prev_seg_ref = bf16[144,512]{1,0:T(8,128)(2,1)S(1)} collective-permute-done((bf16[144,512]{1,0:T(8,128)(2,1)S(1)}, bf16[144,512]{1,0:T(8,128)(2,1)S(1)}, u32[]{:S(2)}, u32[]{:S(2)}) %collective-permute-start.2) | collective-permute-done | bytes 147488 | tf_op jit(solution)/shard_map/ppermute | solution.py:417
  37.7 4.5 %all-to-all-start = ((bf16[8,48,4096]{2,1,0:T(8,128)(2,1)}), bf16[8,48,4096]{2,1,0:T(8,128)(2,1)}, u32[]{:S(2)}, u32[]{:S(2)}) async-start(bf16[8,48,4096]{2,1,0:T(8,128)(2,1)} %bitcast.19), calls=%async_computation | async-start | bytes 6291456 | tf_op jit(solution)/shard_map/all_to_all | solution.py:421
  43.1 2.5 %collective-permute-start.3 = (bf16[2048,384]{1,0:T(8,128)(2,1)S(1)}, bf16[2048,384]{1,0:T(8,128)(2,1)}, u32[]{:S(2)}, u32[]{:S(2)}) collective-permute-start(bf16[2048,384]{1,0:T(8,128)(2,1)S(1)} %copy-done.10), channel_id=1, source_target_pairs={{0,1},{1,0},{2,3},{3,2},{4,5},{5,4},{6,7},{7,6},{8,9},{9,8},{10,11... | collective-permute-start | bytes 4718600 | tf_op jit(solution)/shard_map/ppermute | solution.py:409
  47.5 38.2 %all-gather.11.cloned.1.call-done = bf16[256,2048]{1,0:T(8,128)(2,1)} async-done(((bf16[128,2048]{1,0:T(8,128)(2,1)}), bf16[256,2048]{1,0:T(8,128)(2,1)}) %all-gather.11.cloned.1.call-update) | async-done | bytes 1048592 | tf_op jit(solution)/shard_map/all_gather | solution.py:407
  86.9 27.6 %all-gather.13.cloned.1.call-done = bf16[256,2048]{1,0:T(8,128)(2,1)} async-done(((bf16[128,2048]{1,0:T(8,128)(2,1)}), bf16[256,2048]{1,0:T(8,128)(2,1)}) %all-gather.13.cloned.1.call-update) | async-done | bytes 1048592 | tf_op jit(solution)/shard_map/all_gather | solution.py:407
  115.7 2.6 %collective-permute-start.9 = (bf16[128,2048]{1,0:T(8,128)(2,1)}, bf16[128,2048]{1,0:T(8,128)(2,1)S(1)}, u32[]{:S(2)}, u32[]{:S(2)}) collective-permute-start(bf16[128,2048]{1,0:T(8,128)(2,1)} %copy-done.26), channel_id=1, source_target_pairs={{0,4},{4,0},{1,5},{5,1},{2,6},{6,2},{3,7},{7,3},{8,12},{12,8},{9,1... | collective-permute-start | bytes 1572872 | tf_op jit(solution)/shard_map/ppermute | solution.py:424
  119.7 3.5 %attention_shares.1 = (bf16[2,2048,256]{2,1,0:T(8,128)(2,1)S(1)}, bf16[2,256,2048]{2,1,0:T(8,128)(2,1)S(1)}, bf16[2,2048,128]{2,1,0:T(8,128)(2,1)S(1)}, bf16[2,2...) custom-call(bf16[128,4096]{1,0:T(8,128)(2,1)S(1)} %copy-done.13, bf16[128,256]{1,0:T(8,128)(2,1)S(1)} %copy-done.16, ...), custom_call_target="tpu_custom_call" | custom-call | tf_op jit(solution)/shard_map/attention_shares/pallas_call | solution.py:201
  129.7 5.5 %prepare_weights.1 = (bf16[3,2048,512]{2,1,0:T(8,128)(2,1)S(1)}, bf16[3,2048,256]{2,1,0:T(8,128)(2,1)S(1)}, bf16[3,512,2048]{2,1,0:T(8,128)(2,1)S(1)}) custom-call(bf16[2048,384]{1,0:T(8,128)(2,1)S(1)} %copy-done.10, bf16[2048,384]{1,0:T(8,128)(2,1)S(1)} %copy-done.11, bf16[384,2048]{1,0:T(8,128)(2,1)S(1)} %copy-done.12, ...), custom_call_target="tpu_custom_call" | custom-call | tf_op jit(solution)/shard_map/prepare_weights/pallas_call | solution.py:94
  135.2 2.6 %copy-done.1 = bf16[3,2048,512]{2,1,0:T(8,128)(2,1)} copy-done((bf16[3,2048,512]{2,1,0:T(8,128)(2,1)}, bf16[3,2048,512]{2,1,0:T(8,128)(2,1)S(1)}, u32[]{:S(2)}) %copy-start.1) | copy-done | bytes 6291480
  137.8 2.7 %copy-done.3 = bf16[3,512,2048]{2,1,0:T(8,128)(2,1)} copy-done((bf16[3,512,2048]{2,1,0:T(8,128)(2,1)}, bf16[3,512,2048]{2,1,0:T(8,128)(2,1)S(1)}, u32[]{:S(2)}) %copy-start.3) | copy-done | bytes 6291480
  140.5 1.7 copy-done.5
  143.0 2.8 %copy-done.2 = bf16[3,2048,512]{2,1,0:T(8,128)(2,1)S(1)} copy-done((bf16[3,2048,512]{2,1,0:T(8,128)(2,1)S(1)}, bf16[3,2048,512]{2,1,0:T(8,128)(2,1)}, u32[]{:S(2)}) %copy-start.2) | copy-done | bytes 6291480
  145.8 2.9 %copy-done.4 = bf16[3,512,2048]{2,1,0:T(8,128)(2,1)S(1)} copy-done((bf16[3,512,2048]{2,1,0:T(8,128)(2,1)S(1)}, bf16[3,512,2048]{2,1,0:T(8,128)(2,1)}, u32[]{:S(2)}) %copy-start.4) | copy-done | bytes 6291480
  148.7 2.0 copy-done.6
  150.7 10.7 %expert_terms.1 = bf16[384,2048]{1,0:T(8,128)(2,1)} custom-call(bf16[384,4096]{1,0:T(8,128)(2,1)} %bitcast.12.rows_ref, bf16[3,2048,512]{2,1,0:T(8,128)(2,1)S(1)} %copy-done.2, bf16[3,2048,256]{2,1,0:T(8,128)(2,1)S(1)} %copy-done.6, bf16[3,512,2048]{2,1,0:T(8,128)(2,1)S(1)} %copy-done.4), custom_call_target="tpu_custom_call" | custom-call | tf_op jit(solution)/shard_map/expert_terms/pallas_call | solution.py:145
  161.4 4.1 %all-to-all-start.1 = ((bf16[8,48,2048]{2,1,0:T(8,128)(2,1)}), bf16[8,48,2048]{2,1,0:T(8,128)(2,1)S(1)}, u32[]{:S(2)}, u32[]{:S(2)}) async-start(bf16[8,48,2048]{2,1,0:T(8,128)(2,1)} %bitcast.13), calls=%async_computation.1 | async-start | bytes 3145728 | tf_op jit(solution)/shard_map/all_to_all | solution.py:434
  167.7 1.7 collective-permute-done.10.refs_1_
  172.8 19.6 %collective-permute-done.17.refs_14_ = bf16[2,128,2048]{2,1,0:T(8,128)(2,1)} collective-permute-done((bf16[2,128,2048]{2,1,0:T(8,128)(2,1)}, bf16[2,128,2048]{2,1,0:T(8,128)(2,1)}, u32[]{:S(2)}, u32[]{:S(2)}) %collective-permute-start.17) | collective-permute-done | bytes 1048608 | tf_op jit(solution)/shard_map/ppermute | solution.py:408
  193.9 6.1 %all-to-all-done.1 = bf16[8,48,2048]{2,1,0:T(8,128)(2,1)S(1)} async-done(((bf16[8,48,2048]{2,1,0:T(8,128)(2,1)}), bf16[8,48,2048]{2,1,0:T(8,128)(2,1)S(1)}, u32[]{:S(2)}, u32[]{:S(2)}) %all-to-all-start.1) | async-done | bytes 1572896 | tf_op jit(solution)/shard_map/all_to_all | solution.py:434
  201.1 16.5 %tail_attention.1 = (bf16[128,2048]{1,0:T(8,128)(2,1)}, bf16[128,4096]{1,0:T(8,128)(2,1)}, f32[2,128,256]{2,1,0:T(8,128)}, bf16[2,128,256]{2,1,0:T(8,128)(2,1)}) custom-call(s32[3]{0:T(128)} %pad_add_fusion.place_info, bf16[384,2048]{1,0:T(8,128)(2,1)} %bitcast.22, bf16[128,384]{1,0:T(8,128)(2,1)} %copy-done.21, bf16[128,2048]{1,0:T(8,128)(2,1)} %grad_ref.3, ...), custom_call_target="tpu_custom_call" | custom-call | flops 2147483648 | bytes 23068672 | tf_op jit(solution)/shard_map/tail_attention/pallas_call | solution.py:318
  217.7 2.4 %collective-permute-start.19 = (bf16[2,128,256]{2,1,0:T(8,128)(2,1)}, bf16[2,128,256]{2,1,0:T(8,128)(2,1)S(1)}, u32[]{:S(2)}, u32[]{:S(2)}) collective-permute-start(bf16[2,128,256]{2,1,0:T(8,128)(2,1)} %get-tuple-element.109), channel_id=1, source_target_pairs={{1,0},{2,1},{3,2},{4,3},{5,4},{6,5},{7,6},{8,7},{9,8},{10,9},{11,1... | collective-permute-start | bytes 393224 | tf_op jit(solution)/shard_map/ppermute | solution.py:443
  220.1 5.0 %collective-permute-done.19.later_ref = bf16[2,128,256]{2,1,0:T(8,128)(2,1)S(1)} collective-permute-done((bf16[2,128,256]{2,1,0:T(8,128)(2,1)}, bf16[2,128,256]{2,1,0:T(8,128)(2,1)S(1)}, u32[]{:S(2)}, u32[]{:S(2)}) %collective-permute-start.19) | collective-permute-done | bytes 131104 | tf_op jit(solution)/shard_map/ppermute | solution.py:443
  (103 shorter events, 29.7 us)
Async XLA Ops:
  7.3 29.5 %all-gather.9.cloned.1.call-start = ((), (), s32[]{:S(2)}) async-start(), calls=%async_computation.2 | async-start | bytes 1572864 | tf_op jit(solution)/shard_map/all_gather | solution.py:407
  9.3 27.4 %collective-permute-start = (bf16[128,2048]{1,0:T(8,128)(2,1)}, bf16[128,2048]{1,0:T(8,128)(2,1)S(1)}, u32[]{:S(2)}, u32[]{:S(2)}) collective-permute-start(bf16[128,2048]{1,0:T(8,128)(2,1)} %constant_dynamic-slice_fusion), channel_id=1, source_target_pairs={{0,4},{4,0},{1,5},{5,1},{2,6},{6,2},{3,7},{7,3},{8,12},{12,8},{9,1... | collective-permute-start | bytes 1572872 | tf_op jit(solution)/shard_map/ppermute | solution.py:403
  9.5 27.2 %collective-permute-start.1 = (bf16[128,2048]{1,0:T(8,128)(2,1)}, bf16[128,2048]{1,0:T(8,128)(2,1)S(1)}, u32[]{:S(2)}, u32[]{:S(2)}) collective-permute-start(bf16[128,2048]{1,0:T(8,128)(2,1)} %constant_dynamic-slice_fusion), channel_id=1, source_target_pairs={{0,8},{8,0},{1,9},{9,1},{2,10},{10,2},{3,11},{11,3},{4,12},{12,4},... | collective-permute-start | bytes 1572872 | tf_op jit(solution)/shard_map/ppermute | solution.py:404
  14.7 22.0 %collective-permute-start.2 = (bf16[144,512]{1,0:T(8,128)(2,1)S(1)}, bf16[144,512]{1,0:T(8,128)(2,1)S(1)}, u32[]{:S(2)}, u32[]{:S(2)}) collective-permute-start(bf16[144,512]{1,0:T(8,128)(2,1)S(1)} %fusion.1), channel_id=1, source_target_pairs={{0,1},{1,2},{2,3},{3,4},{4,5},{5,6},{6,7},{7,8},{8,9},{9,10},{10,1... | collective-permute-start | bytes 442376 | tf_op jit(solution)/shard_map/ppermute | solution.py:417
  37.7 104.5 %all-to-all-start = ((bf16[8,48,4096]{2,1,0:T(8,128)(2,1)}), bf16[8,48,4096]{2,1,0:T(8,128)(2,1)}, u32[]{:S(2)}, u32[]{:S(2)}) async-start(bf16[8,48,4096]{2,1,0:T(8,128)(2,1)} %bitcast.19), calls=%async_computation | async-start | bytes 6291456 | tf_op jit(solution)/shard_map/all_to_all | solution.py:421
  42.2 43.4 %all-gather.11.cloned.1.call-start = ((), (), s32[]{:S(2)}) async-start(), calls=%async_computation.3 | async-start | bytes 1572864 | tf_op jit(solution)/shard_map/all_gather | solution.py:407
  43.0 71.5 %all-gather.13.cloned.1.call-start = ((), (), s32[]{:S(2)}) async-start(), calls=%async_computation.4 | async-start | bytes 1572864 | tf_op jit(solution)/shard_map/all_gather | solution.py:407
  43.1 43.8 %collective-permute-start.3 = (bf16[2048,384]{1,0:T(8,128)(2,1)S(1)}, bf16[2048,384]{1,0:T(8,128)(2,1)}, u32[]{:S(2)}, u32[]{:S(2)}) collective-permute-start(bf16[2048,384]{1,0:T(8,128)(2,1)S(1)} %copy-done.10), channel_id=1, source_target_pairs={{0,1},{1,0},{2,3},{3,2},{4,5},{5,4},{6,7},{7,6},{8,9},{9,8},{10,11... | collective-permute-start | bytes 4718600 | tf_op jit(solution)/shard_map/ppermute | solution.py:409
  45.6 70.2 %collective-permute-start.4 = (bf16[2048,384]{1,0:T(8,128)(2,1)}, bf16[2048,384]{1,0:T(8,128)(2,1)}, u32[]{:S(2)}, u32[]{:S(2)}) collective-permute-start(bf16[2048,384]{1,0:T(8,128)(2,1)} %refs_1_.1), channel_id=1, source_target_pairs={{0,1},{1,0},{2,3},{3,2},{4,5},{5,4},{6,7},{7,6},{8,9},{9,8},{10,11... | collective-permute-start | bytes 4718600 | tf_op jit(solution)/shard_map/ppermute | solution.py:409
  45.7 121.7 %all-gather.15.cloned.1.call-start = ((), (), s32[]{:S(2)}) async-start(), calls=%async_computation.5 | async-start | bytes 1572864 | tf_op jit(solution)/shard_map/all_gather | solution.py:407
  45.7 82.6 %collective-permute-start.5 = (bf16[384,2048]{1,0:T(8,128)(2,1)}, bf16[384,2048]{1,0:T(8,128)(2,1)}, u32[]{:S(2)}, u32[]{:S(2)}) collective-permute-start(bf16[384,2048]{1,0:T(8,128)(2,1)} %refs_2_.1), channel_id=1, source_target_pairs={{0,1},{1,0},{2,3},{3,2},{4,5},{5,4},{6,7},{7,6},{8,9},{9,8},{10,11... | collective-permute-start | bytes 4718600 | tf_op jit(solution)/shard_map/ppermute | solution.py:409
  46.3 95.9 %collective-permute-start.6 = (bf16[2,128,2048]{2,1,0:T(8,128)(2,1)}, bf16[2,128,2048]{2,1,0:T(8,128)(2,1)}, u32[]{:S(2)}, u32[]{:S(2)}) collective-permute-start(bf16[2,128,2048]{2,1,0:T(8,128)(2,1)} %bitcast.23), channel_id=1, source_target_pairs={{0,16},{16,0},{1,17},{17,1},{2,18},{18,2},{3,19},{19,3},{4,20},{20... | collective-permute-start | bytes 3145736 | tf_op jit(solution)/shard_map/ppermute | solution.py:408
  85.7 56.5 %collective-permute-start.7 = (bf16[2,128,2048]{2,1,0:T(8,128)(2,1)}, bf16[2,128,2048]{2,1,0:T(8,128)(2,1)}, u32[]{:S(2)}, u32[]{:S(2)}) collective-permute-start(bf16[2,128,2048]{2,1,0:T(8,128)(2,1)} %bitcast.26), channel_id=1, source_target_pairs={{0,16},{16,0},{1,17},{17,1},{2,18},{18,2},{3,19},{19,3},{4,20},{20... | collective-permute-start | bytes 3145736 | tf_op jit(solution)/shard_map/ppermute | solution.py:408
  114.5 27.7 %collective-permute-start.8 = (bf16[2,128,2048]{2,1,0:T(8,128)(2,1)}, bf16[2,128,2048]{2,1,0:T(8,128)(2,1)}, u32[]{:S(2)}, u32[]{:S(2)}) collective-permute-start(bf16[2,128,2048]{2,1,0:T(8,128)(2,1)} %bitcast.29), channel_id=1, source_target_pairs={{0,16},{16,0},{1,17},{17,1},{2,18},{18,2},{3,19},{19,3},{4,20},{20... | collective-permute-start | bytes 3145736 | tf_op jit(solution)/shard_map/ppermute | solution.py:408
  115.7 26.5 %collective-permute-start.9 = (bf16[128,2048]{1,0:T(8,128)(2,1)}, bf16[128,2048]{1,0:T(8,128)(2,1)S(1)}, u32[]{:S(2)}, u32[]{:S(2)}) collective-permute-start(bf16[128,2048]{1,0:T(8,128)(2,1)} %copy-done.26), channel_id=1, source_target_pairs={{0,4},{4,0},{1,5},{5,1},{2,6},{6,2},{3,7},{7,3},{8,12},{12,8},{9,1... | collective-permute-start | bytes 1572872 | tf_op jit(solution)/shard_map/ppermute | solution.py:424
  161.4 38.5 %all-to-all-start.1 = ((bf16[8,48,2048]{2,1,0:T(8,128)(2,1)}), bf16[8,48,2048]{2,1,0:T(8,128)(2,1)S(1)}, u32[]{:S(2)}, u32[]{:S(2)}) async-start(bf16[8,48,2048]{2,1,0:T(8,128)(2,1)} %bitcast.13), calls=%async_computation.1 | async-start | bytes 3145728 | tf_op jit(solution)/shard_map/all_to_all | solution.py:434
  166.8 5.6 %collective-permute-start.12 = (bf16[2,128,2048]{2,1,0:T(8,128)(2,1)}, bf16[2,128,2048]{2,1,0:T(8,128)(2,1)}, u32[]{:S(2)}, u32[]{:S(2)}) collective-permute-start(bf16[2,128,2048]{2,1,0:T(8,128)(2,1)} %bitcast.30), channel_id=1, source_target_pairs={{0,1},{1,0},{2,3},{3,2},{4,5},{5,4},{6,7},{7,6},{8,9},{9,8},{10,11... | collective-permute-start | bytes 3145736 | tf_op jit(solution)/shard_map/ppermute | solution.py:409
  167.4 25.1 %collective-permute-start.17 = (bf16[2,128,2048]{2,1,0:T(8,128)(2,1)}, bf16[2,128,2048]{2,1,0:T(8,128)(2,1)}, u32[]{:S(2)}, u32[]{:S(2)}) collective-permute-start(bf16[2,128,2048]{2,1,0:T(8,128)(2,1)} %bitcast.32), channel_id=1, source_target_pairs={{0,16},{16,0},{1,17},{17,1},{2,18},{18,2},{3,19},{19,3},{4,20},{20... | collective-permute-start | bytes 3145736 | tf_op jit(solution)/shard_map/ppermute | solution.py:408
  167.5 26.4 %collective-permute-start.14 = (bf16[2,128,2048]{2,1,0:T(8,128)(2,1)}, bf16[2,128,2048]{2,1,0:T(8,128)(2,1)}, u32[]{:S(2)}, u32[]{:S(2)}) collective-permute-start(bf16[2,128,2048]{2,1,0:T(8,128)(2,1)} %collective-permute-done.6.refs_8_), channel_id=1, source_target_pairs={{0,1},{1,0},{2,3},{3,2},{4,5},{5,4},{6,7},{7,6},{8,9},{9,8},{10,11... | collective-permute-start | bytes 3145736 | tf_op jit(solution)/shard_map/ppermute | solution.py:409
  169.5 24.4 %collective-permute-start.15 = (bf16[2,128,2048]{2,1,0:T(8,128)(2,1)}, bf16[2,128,2048]{2,1,0:T(8,128)(2,1)}, u32[]{:S(2)}, u32[]{:S(2)}) collective-permute-start(bf16[2,128,2048]{2,1,0:T(8,128)(2,1)} %collective-permute-done.7.refs_10_), channel_id=1, source_target_pairs={{0,1},{1,0},{2,3},{3,2},{4,5},{5,4},{6,7},{7,6},{8,9},{9,8},{10,11... | collective-permute-start | bytes 3145736 | tf_op jit(solution)/shard_map/ppermute | solution.py:409
  171.0 22.9 %collective-permute-start.16 = (bf16[2,128,2048]{2,1,0:T(8,128)(2,1)}, bf16[2,128,2048]{2,1,0:T(8,128)(2,1)}, u32[]{:S(2)}, u32[]{:S(2)}) collective-permute-start(bf16[2,128,2048]{2,1,0:T(8,128)(2,1)} %collective-permute-done.8.refs_12_), channel_id=1, source_target_pairs={{0,1},{1,0},{2,3},{3,2},{4,5},{5,4},{6,7},{7,6},{8,9},{9,8},{10,11... | collective-permute-start | bytes 3145736 | tf_op jit(solution)/shard_map/ppermute | solution.py:409
  172.5 21.4 %collective-permute-start.13 = (bf16[2,128,2048]{2,1,0:T(8,128)(2,1)}, bf16[2,128,2048]{2,1,0:T(8,128)(2,1)}, u32[]{:S(2)}, u32[]{:S(2)}) collective-permute-start(bf16[2,128,2048]{2,1,0:T(8,128)(2,1)} %bitcast.33), channel_id=1, source_target_pairs={{0,1},{1,0},{2,3},{3,2},{4,5},{5,4},{6,7},{7,6},{8,9},{9,8},{10,11... | collective-permute-start | bytes 3145736 | tf_op jit(solution)/shard_map/ppermute | solution.py:409
  192.5 7.5 %collective-permute-start.18 = (bf16[2,128,2048]{2,1,0:T(8,128)(2,1)}, bf16[2,128,2048]{2,1,0:T(8,128)(2,1)}, u32[]{:S(2)}, u32[]{:S(2)}) collective-permute-start(bf16[2,128,2048]{2,1,0:T(8,128)(2,1)} %collective-permute-done.17.refs_14_), channel_id=1, source_target_pairs={{0,1},{1,0},{2,3},{3,2},{4,5},{5,4},{6,7},{7,6},{8,9},{9,8},{10,11... | collective-permute-start | bytes 3145736 | tf_op jit(solution)/shard_map/ppermute | solution.py:409
  217.7 7.4 %collective-permute-start.19 = (bf16[2,128,256]{2,1,0:T(8,128)(2,1)}, bf16[2,128,256]{2,1,0:T(8,128)(2,1)S(1)}, u32[]{:S(2)}, u32[]{:S(2)}) collective-permute-start(bf16[2,128,256]{2,1,0:T(8,128)(2,1)} %get-tuple-element.109), channel_id=1, source_target_pairs={{1,0},{2,1},{3,2},{4,3},{5,4},{6,5},{7,6},{8,7},{9,8},{10,9},{11,1... | collective-permute-start | bytes 393224 | tf_op jit(solution)/shard_map/ppermute | solution.py:443
  (32 other events, 116.5 us)
Sparse Core Ops, SparseCore 0:
  10.2 23.1 all-gather.8
  45.2 40.4 all-gather.10
  87.2 27.2 all-gather.12
  143.1 18.8 all-gather.14

commit v12 on v11

--- a/solution.py
+++ b/solution.py
@@ -105,7 +105,7 @@
             jax.ShapeDtypeStruct((steps, width, 2 * tile), jnp.bfloat16),
             jax.ShapeDtypeStruct((steps, 4 * tile, width), jnp.bfloat16),
         ),
-        compiler_params=params(20),
+        compiler_params=params(48),
         cost_estimate=LIGHT,
         name="prepare_weights",
     )(*own, *other)
@@ -154,7 +154,7 @@
         out_specs=pl.BlockSpec((count, tile), lambda i: (0, turn(i))),
         out_shape=jax.ShapeDtypeStruct((count, width), jnp.bfloat16),
         scratch_shapes=[pltpu.VMEM((steps, count, quad), jnp.bfloat16)],
-        compiler_params=params(24),
+        compiler_params=params(48),
         cost_estimate=LIGHT,
         name="expert_terms",
     )(rows, cols, down, back)
@@ -213,7 +213,7 @@
         ],
         out_specs=[group(shape) for shape in shapes],
         out_shape=[made(shape) for shape in shapes],
-        compiler_params=params(16),
+        compiler_params=params(32),
         cost_estimate=LIGHT,
         name="attention_shares",
     )(queries, key_heads, value_heads, prev, prev, prev, segs[None, :], segs[:, None])
@@ -419,15 +419,18 @@
     rows, w_near, w_far, own_line, prev = lax.optimization_barrier((rows, w_near, w_far, own_line, prev))
 
     rows_in = lax.all_to_all(rows.reshape(owners, depth, 2 * width), chips, 0, 0, tiled=True)
-    lines = [own_line, line(w_near), line(w_far)]
-    crossed = [cross(w) for w in lines]
+    near_line, far_line = line(w_near), line(w_far)
     w_last = lax.ppermute(w_far, "near", swap)
     prepared = prepare_weights(own, other)
     attention = attention_shares(queries, key_heads, value_heads, prev, segs)
-    rows_in, prepared, attention, lines, crossed, w_last = lax.optimization_barrier(
-        (rows_in, prepared, attention, lines, crossed, w_last)
+    near_line, prepared, attention = lax.optimization_barrier((near_line, prepared, attention))
+    crossed = [cross(own_line), cross(near_line)]
+    rows_in, prepared, attention, near_line, far_line, crossed, w_last = lax.optimization_barrier(
+        (rows_in, prepared, attention, near_line, far_line, crossed, w_last)
     )
+    lines = [own_line, near_line, far_line]
     last_line = line(w_last)
+    far_crossed = cross(far_line)
     last_crossed = cross(last_line)
     terms = experts(rows_in.reshape(owners * depth, 2 * width), *prepared)
     terms, lines, crossed = lax.optimization_barrier((terms, lines, crossed))
@@ -438,7 +441,7 @@
     moe_input_grad, query_grad, kept, sent = tail(
         jnp.stack([lax.axis_index("groups"), z, lax.axis_index("core")]).astype(jnp.int32),
         back.reshape(owners * depth, width), place, moe_grad,
-        both(lines + [last_line]) + both(crossed + [last_crossed]), *attention,
+        both(lines + [last_line]) + both(crossed + [far_crossed, last_crossed]), *attention,
     )
     return (moe_input_grad, query_grad, *finish(kept, lax.ppermute(sent, blk, backward)))
 

time: 237 us -> 227 us (0.958); the launches traced: 233 us -> 226 us
  local copies, waits for them, and re-layouts: 30 us -> 13.3 us
  starting transfers between devices: 30.4 us -> 43.6 us
  waiting for transfers between devices: 120 us -> 110 us
  Pallas kernels: 38.1 us -> 45 us
    all_gather x4, waiting for transfers between devices: 65.8 us -> 31.5 us  [local(): line = lambda w: lax.all_gather(w, 'low', axis=0, tiled=False)]
    ppermute x4, waiting for transfers between devices: 19.6 us -> 36.5 us  [local(): cross = lambda w: lax.ppermute(w, 'groups', swap)]
    unnamed x60 -> x52, local copies, waits for them, and re-layouts: 29 us -> 12.4 us
    ppermute x1, waiting for transfers between devices: 0.01 us -> 14.9 us  [local(): w_last = lax.ppermute(w_far, 'near', swap)]
    all_to_all x1, starting transfers between devices: 4.08 us -> 12.6 us  [local(): lax.all_to_all(terms.reshape(owners, depth, width), chips, 0, 0, tiled=True)]
    ppermute x11, starting transfers between devices: 7.22 us -> 14.5 us  [local(): other_core = lambda w: lax.ppermute(w, 'core', swap)]
    all_to_all x1, waiting for transfers between devices: 6.06 us -> 0.01 us  [local(): lax.all_to_all(terms.reshape(owners, depth, width), chips, 0, 0, tiled=True)]
    pallas_call x1, Pallas kernels: 10.7 us -> 14.2 us  [experts(): pl.pallas_call(functools.partial(expert_kernel, steps), grid=(steps + wid...]
  transfers between devices with their start and end apart: 26 -> 26, of which waited for: 9 -> 9; matrix products, arithmetic and copies ran while one was open for 0% -> 0% of each run, Pallas kernels for 9% -> 12%
where the time goes in v12:
time: 227 us; the launch traced here: 226 us
  waiting for transfers between devices  110 us (48%)
  Pallas kernels  45 us (20%)
  starting transfers between devices  43.6 us (19%)
  between operations  14.1 us (6%)
  local copies, waits for them, and re-layouts  13.3 us (6%)
    ppermute x4, waiting for transfers between devices, local(): cross = lambda w: lax.ppermute(w, 'groups', swap)  36.5 us
    all_gather x4, waiting for transfers between devices, local(): line = lambda w: lax.all_gather(w, 'low', axis=0, tiled=False)  31.5 us
    ppermute x1, waiting for transfers between devices, local(): prev = lax.ppermute(jnp.concatenate([kv, seg_rows], axis=0), blk, onward)  18.9 us
    pallas_call x1, Pallas kernels, tail(): pl.pallas_call(functools.partial(tail_kernel, (heads, tiles)), grid_spec=...  16.5 us
    ppermute x1, waiting for transfers between devices, local(): w_last = lax.ppermute(w_far, 'near', swap)  14.9 us
    ppermute x11, starting transfers between devices, local(): other_core = lambda w: lax.ppermute(w, 'core', swap)  14.5 us
    pallas_call x1, Pallas kernels, experts(): pl.pallas_call(functools.partial(expert_kernel, steps), grid=(steps + wid...  14.2 us
    all_to_all x1, starting transfers between devices, local(): lax.all_to_all(terms.reshape(owners, depth, width), chips, 0, 0, tiled=True)  12.6 us
  transfers between devices with their start and end apart: 26, of which 9 were waited for; matrix products, arithmetic and copies ran while one was open for 0% of the time, Pallas kernels for 12%

profile of v12, /device:TPU:13, one launch (start us, length us, event | category | flops | bytes accessed | tf_op | source)
XLA Modules:
  0.0 226.2 jit_solution(8915900025624577587)
XLA Ops:
  9.5 2.3 %collective-permute-start.1 = (bf16[128,2048]{1,0:T(8,128)(2,1)}, bf16[128,2048]{1,0:T(8,128)(2,1)S(1)}, u32[]{:S(2)}, u32[]{:S(2)}) collective-permute-start(bf16[128,2048]{1,0:T(8,128)(2,1)} %constant_dynamic-slice_fusion), channel_id=1, source_target_pairs={{0,8},{8,0},{1,9},{9,1},{2,10},{10,2},{3,11},{11,3},{4,12},{12,4},... | collective-permute-start | bytes 1572872 | tf_op jit(solution)/shard_map/ppermute | solution.py:404
  13.0 1.6 copy-done.1
  14.7 3.1 %collective-permute-start.2 = (bf16[144,512]{1,0:T(8,128)(2,1)S(1)}, bf16[144,512]{1,0:T(8,128)(2,1)S(1)}, u32[]{:S(2)}, u32[]{:S(2)}) collective-permute-start(bf16[144,512]{1,0:T(8,128)(2,1)S(1)} %fusion.1), channel_id=1, source_target_pairs={{0,1},{1,2},{2,3},{3,4},{4,5},{5,6},{6,7},{7,8},{8,9},{9,10},{10,1... | collective-permute-start | bytes 442376 | tf_op jit(solution)/shard_map/ppermute | solution.py:417
  17.8 18.9 %collective-permute-done.2.prev_key_ref.prev_value_ref.prev_seg_ref = bf16[144,512]{1,0:T(8,128)(2,1)S(1)} collective-permute-done((bf16[144,512]{1,0:T(8,128)(2,1)S(1)}, bf16[144,512]{1,0:T(8,128)(2,1)S(1)}, u32[]{:S(2)}, u32[]{:S(2)}) %collective-permute-start.2) | collective-permute-done | bytes 147488 | tf_op jit(solution)/shard_map/ppermute | solution.py:417
  37.7 4.5 %all-to-all-start = ((bf16[8,48,4096]{2,1,0:T(8,128)(2,1)}), bf16[8,48,4096]{2,1,0:T(8,128)(2,1)}, u32[]{:S(2)}, u32[]{:S(2)}) async-start(bf16[8,48,4096]{2,1,0:T(8,128)(2,1)} %bitcast.19), calls=%async_computation | async-start | bytes 6291456 | tf_op jit(solution)/shard_map/all_to_all | solution.py:421
  42.3 2.5 %collective-permute-start.3 = (bf16[2048,384]{1,0:T(8,128)(2,1)S(1)}, bf16[2048,384]{1,0:T(8,128)(2,1)}, u32[]{:S(2)}, u32[]{:S(2)}) collective-permute-start(bf16[2048,384]{1,0:T(8,128)(2,1)S(1)} %copy-done.4), channel_id=1, source_target_pairs={{0,1},{1,0},{2,3},{3,2},{4,5},{5,4},{6,7},{7,6},{8,9},{9,8},{10,11... | collective-permute-start | bytes 4718600 | tf_op jit(solution)/shard_map/ppermute | solution.py:409
  46.8 1.3 copy-done.7
  48.2 3.5 %attention_shares.1 = (bf16[2,2048,256]{2,1,0:T(8,128)(2,1)S(1)}, bf16[2,256,2048]{2,1,0:T(8,128)(2,1)S(1)}, bf16[2,2048,128]{2,1,0:T(8,128)(2,1)S(1)}, bf16[2,2...) custom-call(bf16[128,4096]{1,0:T(8,128)(2,1)S(1)} %copy-done.7, bf16[128,256]{1,0:T(8,128)(2,1)S(1)} %copy-done.10, ...), custom_call_target="tpu_custom_call" | custom-call | tf_op jit(solution)/shard_map/attention_shares/pallas_call | solution.py:201
  51.7 1.3 copy-done.2
  53.0 1.4 copy-done.3
  56.7 1.4 copy-done.6
  58.1 8.8 %prepare_weights.1 = (bf16[3,2048,512]{2,1,0:T(8,128)(2,1)}, bf16[3,2048,256]{2,1,0:T(8,128)(2,1)}, bf16[3,512,2048]{2,1,0:T(8,128)(2,1)}) custom-call(bf16[2048,384]{1,0:T(8,128)(2,1)S(1)} %copy-done.4, bf16[2048,384]{1,0:T(8,128)(2,1)S(1)} %copy-done.5, bf16[384,2048]{1,0:T(8,128)(2,1)S(1)} %copy-done.6, bf16[2048,384]{1,0:T(8,128)(2,1)} %collective-permute-done.3.refs_3_, ...), custom_call_target="tpu_custom_call" | custom-call | tf_op jit(solution)/shard_map/prepare_weights/pallas_call | solution.py:94
  66.9 18.7 %all-gather.11.cloned.1.call-done = bf16[256,2048]{1,0:T(8,128)(2,1)} async-done(((bf16[128,2048]{1,0:T(8,128)(2,1)}), bf16[256,2048]{1,0:T(8,128)(2,1)}) %all-gather.11.cloned.1.call-update) | async-done | bytes 1048592 | tf_op jit(solution)/shard_map/all_gather | solution.py:407
  86.9 14.9 %collective-permute-done.8 = bf16[128,2048]{1,0:T(8,128)(2,1)S(1)} collective-permute-done((bf16[128,2048]{1,0:T(8,128)(2,1)S(1)}, bf16[128,2048]{1,0:T(8,128)(2,1)S(1)}, u32[]{:S(2)}, u32[]{:S(2)}) %collective-permute-start.8) | collective-permute-done | bytes 524320 | tf_op jit(solution)/shard_map/ppermute | solution.py:423
  101.7 12.8 %all-gather.13.cloned.1.call-done = bf16[256,2048]{1,0:T(8,128)(2,1)} async-done(((bf16[128,2048]{1,0:T(8,128)(2,1)}), bf16[256,2048]{1,0:T(8,128)(2,1)}) %all-gather.13.cloned.1.call-update) | async-done | bytes 1048592 | tf_op jit(solution)/shard_map/all_gather | solution.py:407
  114.6 14.2 %expert_terms.1 = bf16[384,2048]{1,0:T(8,128)(2,1)} custom-call(bf16[384,4096]{1,0:T(8,128)(2,1)} %bitcast.12.rows_ref, bf16[3,2048,512]{2,1,0:T(8,128)(2,1)} %get-tuple-element.98.cols_ref, bf16[3,2048,256]{2,1,0:T(8,128)(2,1)} %get-tuple-element.99.down_ref, bf16[3,512,2048]{2,1,0:T(8,128)(2,1)} %get-tuple-element.100.back_ref), custom_call_target="tpu_custom_call" | custom-call | tf_op jit(solution)/shard_map/expert_terms/pallas_call | solution.py:145
  128.8 12.6 %all-to-all-start.1 = ((bf16[8,48,2048]{2,1,0:T(8,128)(2,1)}), bf16[8,48,2048]{2,1,0:T(8,128)(2,1)S(1)}, u32[]{:S(2)}, u32[]{:S(2)}) async-start(bf16[8,48,2048]{2,1,0:T(8,128)(2,1)} %bitcast.13), calls=%async_computation.1 | async-start | bytes 3145728 | tf_op jit(solution)/shard_map/all_to_all | solution.py:437
  145.2 7.3 %collective-permute-start.13 = (bf16[2,128,2048]{2,1,0:T(8,128)(2,1)}, bf16[2,128,2048]{2,1,0:T(8,128)(2,1)}, u32[]{:S(2)}, u32[]{:S(2)}) collective-permute-start(bf16[2,128,2048]{2,1,0:T(8,128)(2,1)} %collective-permute-done.6.refs_8_), channel_id=1, source_target_pairs={{0,1},{1,0},{2,3},{3,2},{4,5},{5,4},{6,7},{7,6},{8,9},{9,8},{10,11... | collective-permute-start | bytes 3145736 | tf_op jit(solution)/shard_map/ppermute | solution.py:409
  153.0 15.2 %collective-permute-done.15.refs_12_ = bf16[2,128,2048]{2,1,0:T(8,128)(2,1)} collective-permute-done((bf16[2,128,2048]{2,1,0:T(8,128)(2,1)}, bf16[2,128,2048]{2,1,0:T(8,128)(2,1)}, u32[]{:S(2)}, u32[]{:S(2)}) %collective-permute-start.15) | collective-permute-done | bytes 1048608 | tf_op jit(solution)/shard_map/ppermute | solution.py:408
  169.4 21.3 %collective-permute-done.17.refs_14_ = bf16[2,128,2048]{2,1,0:T(8,128)(2,1)} collective-permute-done((bf16[2,128,2048]{2,1,0:T(8,128)(2,1)}, bf16[2,128,2048]{2,1,0:T(8,128)(2,1)}, u32[]{:S(2)}, u32[]{:S(2)}) %collective-permute-start.17) | collective-permute-done | bytes 1048608 | tf_op jit(solution)/shard_map/ppermute | solution.py:408
  192.1 1.9 collective-permute-done.18.refs_15_
  194.1 16.5 %tail_attention.1 = (bf16[128,2048]{1,0:T(8,128)(2,1)}, bf16[128,4096]{1,0:T(8,128)(2,1)}, f32[2,128,256]{2,1,0:T(8,128)}, bf16[2,128,256]{2,1,0:T(8,128)(2,1)}) custom-call(s32[3]{0:T(128)} %pad_add_fusion.place_info, bf16[384,2048]{1,0:T(8,128)(2,1)} %bitcast.22, bf16[128,384]{1,0:T(8,128)(2,1)} %copy-done.15, bf16[128,2048]{1,0:T(8,128)(2,1)} %grad_ref.3, ...), custom_call_target="tpu_custom_call" | custom-call | flops 2147483648 | bytes 23068672 | tf_op jit(solution)/shard_map/tail_attention/pallas_call | solution.py:318
  210.6 2.3 %collective-permute-start.19 = (bf16[2,128,256]{2,1,0:T(8,128)(2,1)}, bf16[2,128,256]{2,1,0:T(8,128)(2,1)S(1)}, u32[]{:S(2)}, u32[]{:S(2)}) collective-permute-start(bf16[2,128,256]{2,1,0:T(8,128)(2,1)} %get-tuple-element.121), channel_id=1, source_target_pairs={{1,0},{2,1},{3,2},{4,3},{5,4},{6,5},{7,6},{8,7},{9,8},{10,9},{11,1... | collective-permute-start | bytes 393224 | tf_op jit(solution)/shard_map/ppermute | solution.py:446
  212.9 5.1 %collective-permute-done.19.later_ref = bf16[2,128,256]{2,1,0:T(8,128)(2,1)S(1)} collective-permute-done((bf16[2,128,256]{2,1,0:T(8,128)(2,1)}, bf16[2,128,256]{2,1,0:T(8,128)(2,1)S(1)}, u32[]{:S(2)}, u32[]{:S(2)}) %collective-permute-start.19) | collective-permute-done | bytes 131104 | tf_op jit(solution)/shard_map/ppermute | solution.py:446
  (95 shorter events, 18.7 us)
Async XLA Ops:
  7.3 29.5 %all-gather.9.cloned.1.call-start = ((), (), s32[]{:S(2)}) async-start(), calls=%async_computation.2 | async-start | bytes 1572864 | tf_op jit(solution)/shard_map/all_gather | solution.py:407
  9.3 27.4 %collective-permute-start = (bf16[128,2048]{1,0:T(8,128)(2,1)}, bf16[128,2048]{1,0:T(8,128)(2,1)S(1)}, u32[]{:S(2)}, u32[]{:S(2)}) collective-permute-start(bf16[128,2048]{1,0:T(8,128)(2,1)} %constant_dynamic-slice_fusion), channel_id=1, source_target_pairs={{0,4},{4,0},{1,5},{5,1},{2,6},{6,2},{3,7},{7,3},{8,12},{12,8},{9,1... | collective-permute-start | bytes 1572872 | tf_op jit(solution)/shard_map/ppermute | solution.py:403
  9.5 27.2 %collective-permute-start.1 = (bf16[128,2048]{1,0:T(8,128)(2,1)}, bf16[128,2048]{1,0:T(8,128)(2,1)S(1)}, u32[]{:S(2)}, u32[]{:S(2)}) collective-permute-start(bf16[128,2048]{1,0:T(8,128)(2,1)} %constant_dynamic-slice_fusion), channel_id=1, source_target_pairs={{0,8},{8,0},{1,9},{9,1},{2,10},{10,2},{3,11},{11,3},{4,12},{12,4},... | collective-permute-start | bytes 1572872 | tf_op jit(solution)/shard_map/ppermute | solution.py:404
  14.7 22.0 %collective-permute-start.2 = (bf16[144,512]{1,0:T(8,128)(2,1)S(1)}, bf16[144,512]{1,0:T(8,128)(2,1)S(1)}, u32[]{:S(2)}, u32[]{:S(2)}) collective-permute-start(bf16[144,512]{1,0:T(8,128)(2,1)S(1)} %fusion.1), channel_id=1, source_target_pairs={{0,1},{1,2},{2,3},{3,4},{4,5},{5,6},{6,7},{7,8},{8,9},{9,10},{10,1... | collective-permute-start | bytes 442376 | tf_op jit(solution)/shard_map/ppermute | solution.py:417
  37.7 76.8 %all-to-all-start = ((bf16[8,48,4096]{2,1,0:T(8,128)(2,1)}), bf16[8,48,4096]{2,1,0:T(8,128)(2,1)}, u32[]{:S(2)}, u32[]{:S(2)}) async-start(bf16[8,48,4096]{2,1,0:T(8,128)(2,1)} %bitcast.19), calls=%async_computation | async-start | bytes 6291456 | tf_op jit(solution)/shard_map/all_to_all | solution.py:421
  42.2 43.4 %all-gather.11.cloned.1.call-start = ((), (), s32[]{:S(2)}) async-start(), calls=%async_computation.3 | async-start | bytes 1572864 | tf_op jit(solution)/shard_map/all_gather | solution.py:407
  42.3 14.4 %collective-permute-start.3 = (bf16[2048,384]{1,0:T(8,128)(2,1)S(1)}, bf16[2048,384]{1,0:T(8,128)(2,1)}, u32[]{:S(2)}, u32[]{:S(2)}) collective-permute-start(bf16[2048,384]{1,0:T(8,128)(2,1)S(1)} %copy-done.4), channel_id=1, source_target_pairs={{0,1},{1,0},{2,3},{3,2},{4,5},{5,4},{6,7},{7,6},{8,9},{9,8},{10,11... | collective-permute-start | bytes 4718600 | tf_op jit(solution)/shard_map/ppermute | solution.py:409
  44.8 11.9 %collective-permute-start.4 = (bf16[2048,384]{1,0:T(8,128)(2,1)}, bf16[2048,384]{1,0:T(8,128)(2,1)}, u32[]{:S(2)}, u32[]{:S(2)}) collective-permute-start(bf16[2048,384]{1,0:T(8,128)(2,1)} %refs_1_.1), channel_id=1, source_target_pairs={{0,1},{1,0},{2,3},{3,2},{4,5},{5,4},{6,7},{7,6},{8,9},{9,8},{10,11... | collective-permute-start | bytes 4718600 | tf_op jit(solution)/shard_map/ppermute | solution.py:409
  44.8 11.8 %collective-permute-start.5 = (bf16[384,2048]{1,0:T(8,128)(2,1)}, bf16[384,2048]{1,0:T(8,128)(2,1)}, u32[]{:S(2)}, u32[]{:S(2)}) collective-permute-start(bf16[384,2048]{1,0:T(8,128)(2,1)} %refs_2_.1), channel_id=1, source_target_pairs={{0,1},{1,0},{2,3},{3,2},{4,5},{5,4},{6,7},{7,6},{8,9},{9,8},{10,11... | collective-permute-start | bytes 4718600 | tf_op jit(solution)/shard_map/ppermute | solution.py:409
  45.3 69.2 %all-gather.13.cloned.1.call-start = ((), (), s32[]{:S(2)}) async-start(), calls=%async_computation.4 | async-start | bytes 1572864 | tf_op jit(solution)/shard_map/all_gather | solution.py:407
  45.5 69.1 %collective-permute-start.6 = (bf16[2,128,2048]{2,1,0:T(8,128)(2,1)}, bf16[2,128,2048]{2,1,0:T(8,128)(2,1)}, u32[]{:S(2)}, u32[]{:S(2)}) collective-permute-start(bf16[2,128,2048]{2,1,0:T(8,128)(2,1)} %bitcast.23), channel_id=1, source_target_pairs={{0,16},{16,0},{1,17},{17,1},{2,18},{18,2},{3,19},{19,3},{4,20},{20... | collective-permute-start | bytes 3145736 | tf_op jit(solution)/shard_map/ppermute | solution.py:408
  46.7 97.0 %all-gather.15.cloned.1.call-start = ((), (), s32[]{:S(2)}) async-start(), calls=%async_computation.5 | async-start | bytes 1572864 | tf_op jit(solution)/shard_map/all_gather | solution.py:407
  85.7 28.8 %collective-permute-start.7 = (bf16[2,128,2048]{2,1,0:T(8,128)(2,1)}, bf16[2,128,2048]{2,1,0:T(8,128)(2,1)S(1)}, u32[]{:S(2)}, u32[]{:S(2)}) collective-permute-start(bf16[2,128,2048]{2,1,0:T(8,128)(2,1)} %bitcast.26), channel_id=1, source_target_pairs={{0,16},{16,0},{1,17},{17,1},{2,18},{18,2},{3,19},{19,3},{4,20},{20... | collective-permute-start | bytes 3145736 | tf_op jit(solution)/shard_map/ppermute | solution.py:408
  86.9 14.9 %collective-permute-start.8 = (bf16[128,2048]{1,0:T(8,128)(2,1)S(1)}, bf16[128,2048]{1,0:T(8,128)(2,1)S(1)}, u32[]{:S(2)}, u32[]{:S(2)}) collective-permute-start(bf16[128,2048]{1,0:T(8,128)(2,1)S(1)} %copy-done.22), channel_id=1, source_target_pairs={{0,4},{4,0},{1,5},{5,1},{2,6},{6,2},{3,7},{7,3},{8,12},{12,8},{9,1... | collective-permute-start | bytes 1572872 | tf_op jit(solution)/shard_map/ppermute | solution.py:423
  128.8 63.3 %all-to-all-start.1 = ((bf16[8,48,2048]{2,1,0:T(8,128)(2,1)}), bf16[8,48,2048]{2,1,0:T(8,128)(2,1)S(1)}, u32[]{:S(2)}, u32[]{:S(2)}) async-start(bf16[8,48,2048]{2,1,0:T(8,128)(2,1)} %bitcast.13), calls=%async_computation.1 | async-start | bytes 3145728 | tf_op jit(solution)/shard_map/all_to_all | solution.py:437
  142.6 9.9 %collective-permute-start.10 = (bf16[2,128,2048]{2,1,0:T(8,128)(2,1)}, bf16[2,128,2048]{2,1,0:T(8,128)(2,1)}, u32[]{:S(2)}, u32[]{:S(2)}) collective-permute-start(bf16[2,128,2048]{2,1,0:T(8,128)(2,1)} %bitcast.27), channel_id=1, source_target_pairs={{0,1},{1,0},{2,3},{3,2},{4,5},{5,4},{6,7},{7,6},{8,9},{9,8},{10,11... | collective-permute-start | bytes 3145736 | tf_op jit(solution)/shard_map/ppermute | solution.py:409
  142.6 10.0 %collective-permute-start.11 = (bf16[2,128,2048]{2,1,0:T(8,128)(2,1)}, bf16[2,128,2048]{2,1,0:T(8,128)(2,1)}, u32[]{:S(2)}, u32[]{:S(2)}) collective-permute-start(bf16[2,128,2048]{2,1,0:T(8,128)(2,1)} %bitcast.29), channel_id=1, source_target_pairs={{0,1},{1,0},{2,3},{3,2},{4,5},{5,4},{6,7},{7,6},{8,9},{9,8},{10,11... | collective-permute-start | bytes 3145736 | tf_op jit(solution)/shard_map/ppermute | solution.py:409
  143.1 25.1 %collective-permute-start.15 = (bf16[2,128,2048]{2,1,0:T(8,128)(2,1)}, bf16[2,128,2048]{2,1,0:T(8,128)(2,1)}, u32[]{:S(2)}, u32[]{:S(2)}) collective-permute-start(bf16[2,128,2048]{2,1,0:T(8,128)(2,1)} %bitcast.30), channel_id=1, source_target_pairs={{0,16},{16,0},{1,17},{17,1},{2,18},{18,2},{3,19},{19,3},{4,20},{20... | collective-permute-start | bytes 3145736 | tf_op jit(solution)/shard_map/ppermute | solution.py:408
  143.8 46.9 %collective-permute-start.17 = (bf16[2,128,2048]{2,1,0:T(8,128)(2,1)}, bf16[2,128,2048]{2,1,0:T(8,128)(2,1)}, u32[]{:S(2)}, u32[]{:S(2)}) collective-permute-start(bf16[2,128,2048]{2,1,0:T(8,128)(2,1)} %bitcast.32), channel_id=1, source_target_pairs={{0,16},{16,0},{1,17},{17,1},{2,18},{18,2},{3,19},{19,3},{4,20},{20... | collective-permute-start | bytes 3145736 | tf_op jit(solution)/shard_map/ppermute | solution.py:408
  145.2 46.9 %collective-permute-start.13 = (bf16[2,128,2048]{2,1,0:T(8,128)(2,1)}, bf16[2,128,2048]{2,1,0:T(8,128)(2,1)}, u32[]{:S(2)}, u32[]{:S(2)}) collective-permute-start(bf16[2,128,2048]{2,1,0:T(8,128)(2,1)} %collective-permute-done.6.refs_8_), channel_id=1, source_target_pairs={{0,1},{1,0},{2,3},{3,2},{4,5},{5,4},{6,7},{7,6},{8,9},{9,8},{10,11... | collective-permute-start | bytes 3145736 | tf_op jit(solution)/shard_map/ppermute | solution.py:409
  152.5 39.6 %collective-permute-start.14 = (bf16[2,128,2048]{2,1,0:T(8,128)(2,1)}, bf16[2,128,2048]{2,1,0:T(8,128)(2,1)}, u32[]{:S(2)}, u32[]{:S(2)}) collective-permute-start(bf16[2,128,2048]{2,1,0:T(8,128)(2,1)} %copy-done.20), channel_id=1, source_target_pairs={{0,1},{1,0},{2,3},{3,2},{4,5},{5,4},{6,7},{7,6},{8,9},{9,8},{10,11... | collective-permute-start | bytes 3145736 | tf_op jit(solution)/shard_map/ppermute | solution.py:409
  152.6 39.5 %collective-permute-start.12 = (bf16[2,128,2048]{2,1,0:T(8,128)(2,1)}, bf16[2,128,2048]{2,1,0:T(8,128)(2,1)}, u32[]{:S(2)}, u32[]{:S(2)}) collective-permute-start(bf16[2,128,2048]{2,1,0:T(8,128)(2,1)} %bitcast.33), channel_id=1, source_target_pairs={{0,1},{1,0},{2,3},{3,2},{4,5},{5,4},{6,7},{7,6},{8,9},{9,8},{10,11... | collective-permute-start | bytes 3145736 | tf_op jit(solution)/shard_map/ppermute | solution.py:409
  168.2 23.9 %collective-permute-start.16 = (bf16[2,128,2048]{2,1,0:T(8,128)(2,1)}, bf16[2,128,2048]{2,1,0:T(8,128)(2,1)}, u32[]{:S(2)}, u32[]{:S(2)}) collective-permute-start(bf16[2,128,2048]{2,1,0:T(8,128)(2,1)} %collective-permute-done.15.refs_12_), channel_id=1, source_target_pairs={{0,1},{1,0},{2,3},{3,2},{4,5},{5,4},{6,7},{7,6},{8,9},{9,8},{10,11... | collective-permute-start | bytes 3145736 | tf_op jit(solution)/shard_map/ppermute | solution.py:409
  210.6 7.4 %collective-permute-start.19 = (bf16[2,128,256]{2,1,0:T(8,128)(2,1)}, bf16[2,128,256]{2,1,0:T(8,128)(2,1)S(1)}, u32[]{:S(2)}, u32[]{:S(2)}) collective-permute-start(bf16[2,128,256]{2,1,0:T(8,128)(2,1)} %get-tuple-element.121), channel_id=1, source_target_pairs={{1,0},{2,1},{3,2},{4,3},{5,4},{6,5},{7,6},{8,7},{9,8},{10,9},{11,1... | collective-permute-start | bytes 393224 | tf_op jit(solution)/shard_map/ppermute | solution.py:446
  (28 other events, 155.9 us)
Sparse Core Ops, SparseCore 0:
  10.2 23.1 all-gather.8
  45.4 40.2 all-gather.10
  87.2 27.2 all-gather.12
  116.5 26.2 all-gather.14

commit v13 on v11

--- a/solution.py
+++ b/solution.py
@@ -75,7 +75,8 @@
 
 
 def weights_kernel(*refs):
-    own, other, (cols_ref, down_ref, rows_ref) = refs[:3], refs[3:6], refs[6:]
+    own, other, (cols_ref, down_ref, rows_ref, token_ref) = refs[:3], refs[3:6], refs[6:]
+    token_ref[...] = jnp.zeros_like(token_ref)
     tile = own[0].shape[1]
     for place, (gate_ref, up_ref, low_ref) in enumerate((own, other)):
         for kind, ref in enumerate((gate_ref, up_ref)):
@@ -99,11 +100,13 @@
             pl.BlockSpec((1, width, 4 * tile), lambda i: (i, 0, 0)),
             pl.BlockSpec((1, width, 2 * tile), lambda i: (i, 0, 0)),
             pl.BlockSpec((1, 4 * tile, width), lambda i: (i, 0, 0)),
+            pl.BlockSpec((8, 128), lambda i: (0, 0)),
         ],
         out_shape=(
             jax.ShapeDtypeStruct((steps, width, 4 * tile), jnp.bfloat16),
             jax.ShapeDtypeStruct((steps, width, 2 * tile), jnp.bfloat16),
             jax.ShapeDtypeStruct((steps, 4 * tile, width), jnp.bfloat16),
+            jax.ShapeDtypeStruct((8, 128), jnp.float32),
         ),
         compiler_params=params(20),
         cost_estimate=LIGHT,
@@ -111,7 +114,7 @@
     )(*own, *other)
 
 
-def expert_kernel(steps, rows_ref, cols_ref, down_ref, back_ref, out_ref, hidden):
+def expert_kernel(steps, rows_ref, cols_ref, down_ref, back_ref, token_ref, out_ref, hidden):
     step = pl.program_id(0)
     width = rows_ref.shape[1] // 2
     pair = down_ref.shape[2]
@@ -136,7 +139,7 @@
         out_ref[...] = total.astype(jnp.bfloat16)
 
 
-def experts(rows, cols, down, back):
+def experts(rows, cols, down, back, token):
     count, twice = rows.shape
     steps, width, quad = cols.shape
     tile = 512
@@ -150,6 +153,7 @@
             pl.BlockSpec((1, width, quad), lambda i: (jnp.minimum(i, last), 0, 0)),
             pl.BlockSpec((1, width, quad // 2), lambda i: (jnp.minimum(i, last), 0, 0)),
             pl.BlockSpec((steps, quad, tile), lambda i: (0, 0, turn(i))),
+            pl.BlockSpec((8, 128), lambda i: (0, 0)),
         ],
         out_specs=pl.BlockSpec((count, tile), lambda i: (0, turn(i))),
         out_shape=jax.ShapeDtypeStruct((count, width), jnp.bfloat16),
@@ -157,7 +161,7 @@
         compiler_params=params(24),
         cost_estimate=LIGHT,
         name="expert_terms",
-    )(rows, cols, down, back)
+    )(rows, cols, down, back, token)
 
 
 def shares_kernel(
@@ -223,13 +227,14 @@
     plan, place_info, back_ref, place_ref, grad_ref, *refs
 ):
     heads, tiles = plan
-    mine, across, refs = refs[:8], refs[8:16], refs[16:]
+    mine, across, whole, refs = refs[:4], refs[4:8], refs[8:12], refs[12:]
     low_ref, turned_ref, q_ref, key_ref, value_ref, *refs = refs
     moe_ref, query_out, kept_out, sent_out, stream, held, sums = refs
     step = pl.program_id(0)
     tokens = query_out.shape[0]
     part_size = stream.shape[2]
     size = mine[0].shape[1]
+    mine, across = mine + whole, across + whole
     spread = part_size // size
     here, core = place_info[1], place_info[2]
 
@@ -313,6 +318,10 @@
     rows = lambda shape: pl.BlockSpec((1,) + shape, lambda i, info: (kv_group(i, info), was(i) % tiles, 0))
     own_tile = lambda i: jnp.minimum(i, tiles - 1)
     other_tile = lambda i: jnp.minimum(jnp.maximum(i - tiles, 0), tiles - 1)
+    now = lambda i: jnp.minimum(i, steps - 1)
+    both = pl.BlockSpec(
+        (1, spread, size, tile), lambda i, info: ((now(i) // tiles) ^ info[0], 0, 0, now(i) % tiles)
+    )
     piece = lambda turn: pl.BlockSpec((spread, size, tile), lambda i, info: (0, 0, turn(i)))
     kv = pl.BlockSpec((2, tokens, HD), lambda i, info: (0, 0, kv_group(i, info)))
     return pl.pallas_call(
@@ -321,8 +330,9 @@
             num_scalar_prefetch=1,
             grid=(steps + 1,),
             in_specs=[whole(back.shape), whole(place.shape), whole(moe_grad.shape)]
-            + [piece(own_tile)] * 8
-            + [piece(other_tile)] * 8
+            + [piece(own_tile)] * 4
+            + [piece(other_tile)] * 4
+            + [both] * 4
             + [
                 rows((heads * tokens, span)),
                 pl.BlockSpec(
@@ -419,17 +429,19 @@
     rows, w_near, w_far, own_line, prev = lax.optimization_barrier((rows, w_near, w_far, own_line, prev))
 
     rows_in = lax.all_to_all(rows.reshape(owners, depth, 2 * width), chips, 0, 0, tiled=True)
-    lines = [own_line, line(w_near), line(w_far)]
-    crossed = [cross(w) for w in lines]
+    plane = lambda w: lax.all_gather(w, ("groups", "low"), axis=0, tiled=False).reshape(parts, low, *w.shape)
+    near_line, far_plane = line(w_near), plane(w_far)
     w_last = lax.ppermute(w_far, "near", swap)
-    prepared = prepare_weights(own, other)
+    *prepared, token = prepare_weights(own, other)
     attention = attention_shares(queries, key_heads, value_heads, prev, segs)
-    rows_in, prepared, attention, lines, crossed, w_last = lax.optimization_barrier(
-        (rows_in, prepared, attention, lines, crossed, w_last)
-    )
-    last_line = line(w_last)
-    last_crossed = cross(last_line)
-    terms = experts(rows_in.reshape(owners * depth, 2 * width), *prepared)
+    near_line, token, attention = lax.optimization_barrier((near_line, token, attention))
+    crossed = [cross(own_line), cross(near_line)]
+    rows_in, token, attention, near_line, crossed, w_last = lax.optimization_barrier(
+        (rows_in, token, attention, near_line, crossed, w_last)
+    )
+    lines = [own_line, near_line]
+    last_plane = plane(w_last)
+    terms = experts(rows_in.reshape(owners * depth, 2 * width), *prepared, token)
     terms, lines, crossed = lax.optimization_barrier((terms, lines, crossed))
     back = lax.all_to_all(terms.reshape(owners, depth, width), chips, 0, 0, tiled=True)
     both = lambda pieces: [w for piece in pieces for w in (piece, other_core(piece))]
@@ -438,7 +450,7 @@
     moe_input_grad, query_grad, kept, sent = tail(
         jnp.stack([lax.axis_index("groups"), z, lax.axis_index("core")]).astype(jnp.int32),
         back.reshape(owners * depth, width), place, moe_grad,
-        both(lines + [last_line]) + both(crossed + [last_crossed]), *attention,
+        both(lines) + both(crossed) + both([far_plane, last_plane]), *attention,
     )
     return (moe_input_grad, query_grad, *finish(kept, lax.ppermute(sent, blk, backward)))
 

time: 237 us -> 235 us (level)
  starting transfers between devices: 30.4 us -> 26.2 us
    all_gather x4 -> x2, waiting for transfers between devices: 65.8 us -> 13.1 us  [local(): line = lambda w: lax.all_gather(w, 'low', axis=0, tiled=False)]
    all_gather x0 -> x2, waiting for transfers between devices: none -> 49.5 us  [local(): lax.all_gather(w, ('groups', 'low'), axis=0, tiled=False)]
    ppermute x1, waiting for transfers between devices: 0.01 us -> 14.8 us  [local(): w_last = lax.ppermute(w_far, 'near', swap)]
    ppermute x4 -> x2, waiting for transfers between devices: 19.6 us -> 13.3 us  [local(): cross = lambda w: lax.ppermute(w, 'groups', swap)]
    all_to_all x1, waiting for transfers between devices: 6.06 us -> 0.01 us  [local(): lax.all_to_all(terms.reshape(owners, depth, width), chips, 0, 0, tiled=True)]
    ppermute x11 -> x9, waiting for transfers between devices: 4 us -> 8.47 us  [local(): other_core = lambda w: lax.ppermute(w, 'core', swap)]
    ppermute x1, waiting for transfers between devices: 18.9 us -> 15.4 us  [local(): prev = lax.ppermute(jnp.concatenate([kv, seg_rows], axis=0), blk, onward)]
    ppermute x1, starting transfers between devices: 2.56 us -> 0.01 us  [local(): w_last = lax.ppermute(w_far, 'near', swap)]
  transfers between devices with their start and end apart: 26 -> 22, of which waited for: 9 -> 11; matrix products, arithmetic and copies ran while one was open for 0% -> 0% of each run, Pallas kernels for 9% -> 9%
where the time goes in v13:
time: 235 us; the launch traced here: 233 us
  waiting for transfers between devices  121 us (51%)
  Pallas kernels  38.5 us (16%)
  local copies, waits for them, and re-layouts  32.2 us (14%)
  starting transfers between devices  26.2 us (11%)
  between operations  14 us (6%)
    all_gather x2, waiting for transfers between devices, local(): lax.all_gather(w, ('groups', 'low'), axis=0, tiled=False)  49.5 us
    unnamed x62, local copies, waits for them, and re-layouts  31.2 us
    pallas_call x1, Pallas kernels, tail(): pl.pallas_call(functools.partial(tail_kernel, (heads, tiles)), grid_spec=...  16.6 us
    ppermute x1, waiting for transfers between devices, local(): prev = lax.ppermute(jnp.concatenate([kv, seg_rows], axis=0), blk, onward)  15.4 us
    ppermute x1, waiting for transfers between devices, local(): w_last = lax.ppermute(w_far, 'near', swap)  14.8 us
    ppermute x2, waiting for transfers between devices, local(): cross = lambda w: lax.ppermute(w, 'groups', swap)  13.3 us
    all_gather x2, waiting for transfers between devices, local(): line = lambda w: lax.all_gather(w, 'low', axis=0, tiled=False)  13.1 us
    pallas_call x1, Pallas kernels, experts(): pl.pallas_call(functools.partial(expert_kernel, steps), grid=(steps + wid...  11 us
  transfers between devices with their start and end apart: 22, of which 11 were waited for; matrix products, arithmetic and copies ran while one was open for 0% of the time, Pallas kernels for 9%

profile of v13, /device:TPU:13, one launch (start us, length us, event | category | flops | bytes accessed | tf_op | source)
XLA Modules:
  0.0 232.8 jit_solution(1558302155372010872)
XLA Ops:
  9.5 2.3 collective-permute-start.1
  18.1 3.1 %collective-permute-start.2 = (bf16[144,512]{1,0:T(8,128)(2,1)S(1)}, bf16[144,512]{1,0:T(8,128)(2,1)S(1)}, u32[]{:S(2)}, u32[]{:S(2)}) collective-permute-start(bf16[144,512]{1,0:T(8,128)(2,1)S(1)} %fusion.1), channel_id=1, source_target_pairs={{0,1},{1,2},{2,3},{3,4},{4,5},{5,6},{6,7},{7,8},{8,9},{9,10},{10,1... | collective-permute-start | bytes 442376 | tf_op jit(solution)/shard_map/ppermute | solution.py:427
  21.3 15.4 %collective-permute-done.2.prev_key_ref.prev_value_ref.prev_seg_ref = bf16[144,512]{1,0:T(8,128)(2,1)S(1)} collective-permute-done((bf16[144,512]{1,0:T(8,128)(2,1)S(1)}, bf16[144,512]{1,0:T(8,128)(2,1)S(1)}, u32[]{:S(2)}, u32[]{:S(2)}) %collective-permute-start.2) | collective-permute-done | bytes 147488 | tf_op jit(solution)/shard_map/ppermute | solution.py:427
  37.5 4.4 %all-to-all-start = ((bf16[8,48,4096]{2,1,0:T(8,128)(2,1)}), bf16[8,48,4096]{2,1,0:T(8,128)(2,1)}, u32[]{:S(2)}, u32[]{:S(2)}) async-start(bf16[8,48,4096]{2,1,0:T(8,128)(2,1)} %bitcast.19), calls=%async_computation | async-start | bytes 6291456 | tf_op jit(solution)/shard_map/all_to_all | solution.py:431
  43.5 2.8 %collective-permute-start.3 = (bf16[2048,384]{1,0:T(8,128)(2,1)S(1)}, bf16[2048,384]{1,0:T(8,128)(2,1)}, u32[]{:S(2)}, u32[]{:S(2)}) collective-permute-start(bf16[2048,384]{1,0:T(8,128)(2,1)S(1)} %copy-done.10), channel_id=1, source_target_pairs={{0,1},{1,0},{2,3},{3,2},{4,5},{5,4},{6,7},{7,6},{8,9},{9,8},{10,11... | collective-permute-start | bytes 4718600 | tf_op jit(solution)/shard_map/ppermute | solution.py:419
  49.4 3.5 %attention_shares.1 = (bf16[2,2048,256]{2,1,0:T(8,128)(2,1)S(1)}, bf16[2,256,2048]{2,1,0:T(8,128)(2,1)S(1)}, bf16[2,2048,128]{2,1,0:T(8,128)(2,1)S(1)}, bf16[2,2...) custom-call(bf16[128,4096]{1,0:T(8,128)(2,1)S(1)} %copy-done.13, bf16[128,256]{1,0:T(8,128)(2,1)S(1)} %copy-done.16, ...), custom_call_target="tpu_custom_call" | custom-call | tf_op jit(solution)/shard_map/attention_shares/pallas_call | solution.py:205
  59.4 5.5 %prepare_weights.1 = (bf16[3,2048,512]{2,1,0:T(8,128)(2,1)S(1)}, bf16[3,2048,256]{2,1,0:T(8,128)(2,1)S(1)}, bf16[3,512,2048]{2,1,0:T(8,128)(2,1)S(1)}, f32[8,128]{1,0:T(8,128)S(1)}) custom-call(bf16[2048,384]{1,0:T(8,128)(2,1)S(1)} %copy-done.10, bf16[2048,384]{1,0:T(8,128)(2,1)S(1)} %copy-done.11, bf16[384,2048]{1,0:T(8,128)(2,1)S(1)} %copy-done.12, ...), custom_call_target="tpu_custom_call" | custom-call | tf_op jit(solution)/shard_map/prepare_weights/pallas_call | solution.py:95
  64.9 2.7 %copy-done.1 = bf16[3,2048,512]{2,1,0:T(8,128)(2,1)} copy-done((bf16[3,2048,512]{2,1,0:T(8,128)(2,1)}, bf16[3,2048,512]{2,1,0:T(8,128)(2,1)S(1)}, u32[]{:S(2)}) %copy-start.1) | copy-done | bytes 6291480
  67.6 2.7 %copy-done.3 = bf16[3,512,2048]{2,1,0:T(8,128)(2,1)} copy-done((bf16[3,512,2048]{2,1,0:T(8,128)(2,1)}, bf16[3,512,2048]{2,1,0:T(8,128)(2,1)S(1)}, u32[]{:S(2)}) %copy-start.3) | copy-done | bytes 6291480
  70.3 1.6 copy-done.6
  71.9 13.1 %all-gather.11.cloned.1.call-done = bf16[256,2048]{1,0:T(8,128)(2,1)} async-done(((bf16[128,2048]{1,0:T(8,128)(2,1)}), bf16[256,2048]{1,0:T(8,128)(2,1)}) %all-gather.11.cloned.1.call-update) | async-done | bytes 1048592 | tf_op jit(solution)/shard_map/all_gather | solution.py:417
  86.3 14.8 %collective-permute-done.8 = bf16[128,2048]{1,0:T(8,128)(2,1)S(1)} collective-permute-done((bf16[128,2048]{1,0:T(8,128)(2,1)S(1)}, bf16[128,2048]{1,0:T(8,128)(2,1)S(1)}, u32[]{:S(2)}, u32[]{:S(2)}) %collective-permute-start.8) | collective-permute-done | bytes 524320 | tf_op jit(solution)/shard_map/ppermute | solution.py:434
  101.0 13.3 %collective-permute-done.7.refs_6_ = bf16[2,128,2048]{2,1,0:T(8,128)(2,1)S(1)} collective-permute-done((bf16[2,128,2048]{2,1,0:T(8,128)(2,1)}, bf16[2,128,2048]{2,1,0:T(8,128)(2,1)S(1)}, u32[]{:S(2)}, u32[]{:S(2)}) %collective-permute-start.7) | collective-permute-done | bytes 1048608 | tf_op jit(solution)/shard_map/ppermute | solution.py:418
  114.4 20.6 %all-gather.13.cloned.1.call-done = bf16[512,2048]{1,0:T(8,128)(2,1)} async-done(((bf16[128,2048]{1,0:T(8,128)(2,1)}), bf16[512,2048]{1,0:T(8,128)(2,1)}) %all-gather.13.cloned.1.call-update) | async-done | bytes 2097168 | tf_op jit(solution)/shard_map/all_gather | solution.py:432
  135.7 2.8 %copy-done.2 = bf16[3,2048,512]{2,1,0:T(8,128)(2,1)S(1)} copy-done((bf16[3,2048,512]{2,1,0:T(8,128)(2,1)S(1)}, bf16[3,2048,512]{2,1,0:T(8,128)(2,1)}, u32[]{:S(2)}) %copy-start.2) | copy-done | bytes 6291480
  138.5 2.8 %copy-done.4 = bf16[3,512,2048]{2,1,0:T(8,128)(2,1)S(1)} copy-done((bf16[3,512,2048]{2,1,0:T(8,128)(2,1)S(1)}, bf16[3,512,2048]{2,1,0:T(8,128)(2,1)}, u32[]{:S(2)}) %copy-start.4) | copy-done | bytes 6291480
  141.3 1.9 copy-done.7
  143.2 11.0 %expert_terms.1 = bf16[384,2048]{1,0:T(8,128)(2,1)} custom-call(bf16[384,4096]{1,0:T(8,128)(2,1)} %bitcast.11.rows_ref, bf16[3,2048,512]{2,1,0:T(8,128)(2,1)S(1)} %copy-done.2, bf16[3,2048,256]{2,1,0:T(8,128)(2,1)S(1)} %copy-done.7, bf16[3,512,2048]{2,1,0:T(8,128)(2,1)S(1)} %copy-done.4, f32[8,128]{1,0:T(8,128)S(1)} %get-tuple-element.92.token_ref), custom_call_target="tpu_custom_call" | custom-call | tf_op jit(solution)/shard_map/expert_terms/pallas_call | solution.py:148
  154.2 5.5 %all-to-all-start.1 = ((bf16[8,48,2048]{2,1,0:T(8,128)(2,1)}), bf16[8,48,2048]{2,1,0:T(8,128)(2,1)S(1)}, u32[]{:S(2)}, u32[]{:S(2)}) async-start(bf16[8,48,2048]{2,1,0:T(8,128)(2,1)} %bitcast.12), calls=%async_computation.1 | async-start | bytes 3145728 | tf_op jit(solution)/shard_map/all_to_all | solution.py:446
  159.7 28.9 %all-gather.15.cloned.1.call-done = bf16[512,2048]{1,0:T(8,128)(2,1)} async-done(((bf16[128,2048]{1,0:T(8,128)(2,1)}), bf16[512,2048]{1,0:T(8,128)(2,1)}) %all-gather.15.cloned.1.call-update) | async-done | bytes 2097168 | tf_op jit(solution)/shard_map/all_gather | solution.py:432
  190.9 4.0 %collective-permute-done.9.refs_1_ = bf16[2,128,2048]{2,1,0:T(8,128)(2,1)} collective-permute-done((bf16[2,128,2048]{2,1,0:T(8,128)(2,1)}, bf16[2,128,2048]{2,1,0:T(8,128)(2,1)}, u32[]{:S(2)}, u32[]{:S(2)}) %collective-permute-start.9) | collective-permute-done | bytes 1048608 | tf_op jit(solution)/shard_map/ppermute | solution.py:419
  200.6 16.6 %tail_attention.1 = (bf16[128,2048]{1,0:T(8,128)(2,1)}, bf16[128,4096]{1,0:T(8,128)(2,1)}, f32[2,128,256]{2,1,0:T(8,128)}, bf16[2,128,256]{2,1,0:T(8,128)(2,1)}) custom-call(s32[3]{0:T(128)} %pad_add_fusion.place_info, bf16[384,2048]{1,0:T(8,128)(2,1)} %bitcast.22, bf16[128,384]{1,0:T(8,128)(2,1)} %copy-done.21, bf16[128,2048]{1,0:T(8,128)(2,1)} %grad_ref.3, ...), custom_call_target="tpu_custom_call" | custom-call | flops 2147483648 | bytes 23068672 | tf_op jit(solution)/shard_map/tail_attention/pallas_call | solution.py:327
  217.1 2.3 collective-permute-start.15
  219.5 5.1 %collective-permute-done.15.later_ref = bf16[2,128,256]{2,1,0:T(8,128)(2,1)S(1)} collective-permute-done((bf16[2,128,256]{2,1,0:T(8,128)(2,1)}, bf16[2,128,256]{2,1,0:T(8,128)(2,1)S(1)}, u32[]{:S(2)}, u32[]{:S(2)}) %collective-permute-start.15) | collective-permute-done | bytes 131104 | tf_op jit(solution)/shard_map/ppermute | solution.py:455
  (97 shorter events, 32.0 us)
Async XLA Ops:
  7.2 29.5 %all-gather.9.cloned.1.call-start = ((), (), s32[]{:S(2)}) async-start(), calls=%async_computation.2 | async-start | bytes 1572864 | tf_op jit(solution)/shard_map/all_gather | solution.py:417
  9.3 27.4 %collective-permute-start = (bf16[128,2048]{1,0:T(8,128)(2,1)}, bf16[128,2048]{1,0:T(8,128)(2,1)}, u32[]{:S(2)}, u32[]{:S(2)}) collective-permute-start(bf16[128,2048]{1,0:T(8,128)(2,1)} %constant_dynamic-slice_fusion), channel_id=1, source_target_pairs={{0,4},{4,0},{1,5},{5,1},{2,6},{6,2},{3,7},{7,3},{8,12},{12,8},{9,1... | collective-permute-start | bytes 1572872 | tf_op jit(solution)/shard_map/ppermute | solution.py:413
  9.5 27.2 %collective-permute-start.1 = (bf16[128,2048]{1,0:T(8,128)(2,1)}, bf16[128,2048]{1,0:T(8,128)(2,1)S(1)}, u32[]{:S(2)}, u32[]{:S(2)}) collective-permute-start(bf16[128,2048]{1,0:T(8,128)(2,1)} %constant_dynamic-slice_fusion), channel_id=1, source_target_pairs={{0,8},{8,0},{1,9},{9,1},{2,10},{10,2},{3,11},{11,3},{4,12},{12,4},... | collective-permute-start | bytes 1572872 | tf_op jit(solution)/shard_map/ppermute | solution.py:414
  18.1 18.6 %collective-permute-start.2 = (bf16[144,512]{1,0:T(8,128)(2,1)S(1)}, bf16[144,512]{1,0:T(8,128)(2,1)S(1)}, u32[]{:S(2)}, u32[]{:S(2)}) collective-permute-start(bf16[144,512]{1,0:T(8,128)(2,1)S(1)} %fusion.1), channel_id=1, source_target_pairs={{0,1},{1,2},{2,3},{3,4},{4,5},{5,6},{6,7},{7,8},{8,9},{9,10},{10,1... | collective-permute-start | bytes 442376 | tf_op jit(solution)/shard_map/ppermute | solution.py:427
  37.5 76.9 %all-to-all-start = ((bf16[8,48,4096]{2,1,0:T(8,128)(2,1)}), bf16[8,48,4096]{2,1,0:T(8,128)(2,1)}, u32[]{:S(2)}, u32[]{:S(2)}) async-start(bf16[8,48,4096]{2,1,0:T(8,128)(2,1)} %bitcast.19), calls=%async_computation | async-start | bytes 6291456 | tf_op jit(solution)/shard_map/all_to_all | solution.py:431
  41.9 43.1 %all-gather.11.cloned.1.call-start = ((), (), s32[]{:S(2)}) async-start(), calls=%async_computation.3 | async-start | bytes 1572864 | tf_op jit(solution)/shard_map/all_gather | solution.py:417
  42.7 92.4 %all-gather.13.cloned.1.call-start = ((), (), s32[]{:S(2)}) async-start(), calls=%async_computation.4 | async-start | bytes 2621440 | tf_op jit(solution)/shard_map/all_gather | solution.py:432
  43.4 145.2 %all-gather.15.cloned.1.call-start = ((), (), s32[]{:S(2)}) async-start(), calls=%async_computation.5 | async-start | bytes 2621440 | tf_op jit(solution)/shard_map/all_gather | solution.py:432
  43.5 14.5 %collective-permute-start.3 = (bf16[2048,384]{1,0:T(8,128)(2,1)S(1)}, bf16[2048,384]{1,0:T(8,128)(2,1)}, u32[]{:S(2)}, u32[]{:S(2)}) collective-permute-start(bf16[2048,384]{1,0:T(8,128)(2,1)S(1)} %copy-done.10), channel_id=1, source_target_pairs={{0,1},{1,0},{2,3},{3,2},{4,5},{5,4},{6,7},{7,6},{8,9},{9,8},{10,11... | collective-permute-start | bytes 4718600 | tf_op jit(solution)/shard_map/ppermute | solution.py:419
  46.3 11.7 %collective-permute-start.4 = (bf16[2048,384]{1,0:T(8,128)(2,1)}, bf16[2048,384]{1,0:T(8,128)(2,1)}, u32[]{:S(2)}, u32[]{:S(2)}) collective-permute-start(bf16[2048,384]{1,0:T(8,128)(2,1)} %refs_1_.1), channel_id=1, source_target_pairs={{0,1},{1,0},{2,3},{3,2},{4,5},{5,4},{6,7},{7,6},{8,9},{9,8},{10,11... | collective-permute-start | bytes 4718600 | tf_op jit(solution)/shard_map/ppermute | solution.py:419
  46.3 11.7 %collective-permute-start.5 = (bf16[384,2048]{1,0:T(8,128)(2,1)}, bf16[384,2048]{1,0:T(8,128)(2,1)}, u32[]{:S(2)}, u32[]{:S(2)}) collective-permute-start(bf16[384,2048]{1,0:T(8,128)(2,1)} %refs_2_.1), channel_id=1, source_target_pairs={{0,1},{1,0},{2,3},{3,2},{4,5},{5,4},{6,7},{7,6},{8,9},{9,8},{10,11... | collective-permute-start | bytes 4718600 | tf_op jit(solution)/shard_map/ppermute | solution.py:419
  46.9 54.1 %collective-permute-start.6 = (bf16[2,128,2048]{2,1,0:T(8,128)(2,1)}, bf16[2,128,2048]{2,1,0:T(8,128)(2,1)}, u32[]{:S(2)}, u32[]{:S(2)}) collective-permute-start(bf16[2,128,2048]{2,1,0:T(8,128)(2,1)} %bitcast.27), channel_id=1, source_target_pairs={{0,16},{16,0},{1,17},{17,1},{2,18},{18,2},{3,19},{19,3},{4,20},{20... | collective-permute-start | bytes 3145736 | tf_op jit(solution)/shard_map/ppermute | solution.py:418
  59.4 26.9 %copy-start.28 = (bf16[128,2048]{1,0:T(8,128)(2,1)S(1)}, bf16[128,2048]{1,0:T(8,128)(2,1)}, u32[]{:S(2)}) copy-start(bf16[128,2048]{1,0:T(8,128)(2,1)} %copy-done.27) | copy-start | bytes 1572868
  85.1 29.3 %collective-permute-start.7 = (bf16[2,128,2048]{2,1,0:T(8,128)(2,1)}, bf16[2,128,2048]{2,1,0:T(8,128)(2,1)S(1)}, u32[]{:S(2)}, u32[]{:S(2)}) collective-permute-start(bf16[2,128,2048]{2,1,0:T(8,128)(2,1)} %bitcast.30), channel_id=1, source_target_pairs={{0,16},{16,0},{1,17},{17,1},{2,18},{18,2},{3,19},{19,3},{4,20},{20... | collective-permute-start | bytes 3145736 | tf_op jit(solution)/shard_map/ppermute | solution.py:418
  86.3 14.8 %collective-permute-start.8 = (bf16[128,2048]{1,0:T(8,128)(2,1)S(1)}, bf16[128,2048]{1,0:T(8,128)(2,1)S(1)}, u32[]{:S(2)}, u32[]{:S(2)}) collective-permute-start(bf16[128,2048]{1,0:T(8,128)(2,1)S(1)} %copy-done.28), channel_id=1, source_target_pairs={{0,4},{4,0},{1,5},{5,1},{2,6},{6,2},{3,7},{7,3},{8,12},{12,8},{9,1... | collective-permute-start | bytes 1572872 | tf_op jit(solution)/shard_map/ppermute | solution.py:434
  114.4 39.8 %copy-start.26 = (bf16[2,128,2048]{2,1,0:T(8,128)(2,1)}, bf16[2,128,2048]{2,1,0:T(8,128)(2,1)S(1)}, u32[]{:S(2)}) copy-start(bf16[2,128,2048]{2,1,0:T(8,128)(2,1)S(1)} %collective-permute-done.7.refs_6_) | copy-start | bytes 3145732
  135.0 54.8 %collective-permute-start.13 = (bf16[2,2,128,2048]{3,2,1,0:T(8,128)(2,1)}, bf16[2,2,128,2048]{3,2,1,0:T(8,128)(2,1)}, u32[]{:S(2)}, u32[]{:S(2)}) collective-permute-start(bf16[2,2,128,2048]{3,2,1,0:T(8,128)(2,1)} %bitcast.23), channel_id=1, source_target_pairs={{0,1},{1,0},{2,3},{3,2},{4,5},{5,4},{6,7},{7,6},{8,9},{9,8},{10,11... | collective-permute-start | bytes 6291464 | tf_op jit(solution)/shard_map/ppermute | solution.py:419
  154.2 45.2 %all-to-all-start.1 = ((bf16[8,48,2048]{2,1,0:T(8,128)(2,1)}), bf16[8,48,2048]{2,1,0:T(8,128)(2,1)S(1)}, u32[]{:S(2)}, u32[]{:S(2)}) async-start(bf16[8,48,2048]{2,1,0:T(8,128)(2,1)} %bitcast.12), calls=%async_computation.1 | async-start | bytes 3145728 | tf_op jit(solution)/shard_map/all_to_all | solution.py:446
  188.6 10.8 %collective-permute-start.14 = (bf16[2,2,128,2048]{3,2,1,0:T(8,128)(2,1)}, bf16[2,2,128,2048]{3,2,1,0:T(8,128)(2,1)}, u32[]{:S(2)}, u32[]{:S(2)}) collective-permute-start(bf16[2,2,128,2048]{3,2,1,0:T(8,128)(2,1)} %bitcast.25), channel_id=1, source_target_pairs={{0,1},{1,0},{2,3},{3,2},{4,5},{5,4},{6,7},{7,6},{8,9},{9,8},{10,11... | collective-permute-start | bytes 6291464 | tf_op jit(solution)/shard_map/ppermute | solution.py:419
  189.3 5.6 %collective-permute-start.9 = (bf16[2,128,2048]{2,1,0:T(8,128)(2,1)}, bf16[2,128,2048]{2,1,0:T(8,128)(2,1)}, u32[]{:S(2)}, u32[]{:S(2)}) collective-permute-start(bf16[2,128,2048]{2,1,0:T(8,128)(2,1)} %bitcast.28), channel_id=1, source_target_pairs={{0,1},{1,0},{2,3},{3,2},{4,5},{5,4},{6,7},{7,6},{8,9},{9,8},{10,11... | collective-permute-start | bytes 3145736 | tf_op jit(solution)/shard_map/ppermute | solution.py:419
  189.3 7.1 %collective-permute-start.10 = (bf16[2,128,2048]{2,1,0:T(8,128)(2,1)}, bf16[2,128,2048]{2,1,0:T(8,128)(2,1)}, u32[]{:S(2)}, u32[]{:S(2)}) collective-permute-start(bf16[2,128,2048]{2,1,0:T(8,128)(2,1)} %bitcast.31), channel_id=1, source_target_pairs={{0,1},{1,0},{2,3},{3,2},{4,5},{5,4},{6,7},{7,6},{8,9},{9,8},{10,11... | collective-permute-start | bytes 3145736 | tf_op jit(solution)/shard_map/ppermute | solution.py:419
  189.8 8.1 %collective-permute-start.11 = (bf16[2,128,2048]{2,1,0:T(8,128)(2,1)}, bf16[2,128,2048]{2,1,0:T(8,128)(2,1)}, u32[]{:S(2)}, u32[]{:S(2)}) collective-permute-start(bf16[2,128,2048]{2,1,0:T(8,128)(2,1)} %collective-permute-done.6.refs_4_), channel_id=1, source_target_pairs={{0,1},{1,0},{2,3},{3,2},{4,5},{5,4},{6,7},{7,6},{8,9},{9,8},{10,11... | collective-permute-start | bytes 3145736 | tf_op jit(solution)/shard_map/ppermute | solution.py:419
  189.8 9.6 %collective-permute-start.12 = (bf16[2,128,2048]{2,1,0:T(8,128)(2,1)}, bf16[2,128,2048]{2,1,0:T(8,128)(2,1)}, u32[]{:S(2)}, u32[]{:S(2)}) collective-permute-start(bf16[2,128,2048]{2,1,0:T(8,128)(2,1)} %copy-done.26), channel_id=1, source_target_pairs={{0,1},{1,0},{2,3},{3,2},{4,5},{5,4},{6,7},{7,6},{8,9},{9,8},{10,11... | collective-permute-start | bytes 3145736 | tf_op jit(solution)/shard_map/ppermute | solution.py:419
  217.1 7.4 %collective-permute-start.15 = (bf16[2,128,256]{2,1,0:T(8,128)(2,1)}, bf16[2,128,256]{2,1,0:T(8,128)(2,1)S(1)}, u32[]{:S(2)}, u32[]{:S(2)}) collective-permute-start(bf16[2,128,256]{2,1,0:T(8,128)(2,1)} %get-tuple-element.111), channel_id=1, source_target_pairs={{1,0},{2,1},{3,2},{4,3},{5,4},{6,5},{7,6},{8,7},{9,8},{10,9},{11,1... | collective-permute-start | bytes 393224 | tf_op jit(solution)/shard_map/ppermute | solution.py:455
  (29 other events, 113.8 us)
Sparse Core Ops, SparseCore 0:
  10.2 23.0 all-gather.8
  44.3 40.6 all-gather.10
  87.5 47.5 all-gather.12
  137.3 51.2 all-gather.14

commit v14 on v12

--- a/solution.py
+++ b/solution.py
@@ -225,10 +225,10 @@
     heads, tiles = plan
     mine, across, refs = refs[:8], refs[8:16], refs[16:]
     low_ref, turned_ref, q_ref, key_ref, value_ref, *refs = refs
-    moe_ref, query_out, kept_out, sent_out, stream, held, sums = refs
+    moe_ref, query_out, kept_out, sent_out, by_place, stream, held, sums = refs
     step = pl.program_id(0)
     tokens = query_out.shape[0]
-    part_size = stream.shape[2]
+    part_size = by_place.shape[2]
     size = mine[0].shape[1]
     spread = part_size // size
     here, core = place_info[1], place_info[2]
@@ -242,19 +242,18 @@
             for rest in range(spread):
                 for side in range(2):
                     source = ((z * spread + rest) * 2 + side) * size
-                    stream[2 * z + side, :, rest * size : (rest + 1) * size] = added[:, source : source + size]
+                    by_place[2 * z + side, :, rest * size : (rest + 1) * size] = added[:, source : source + size]
+        for i in range(8):
+            spot = slice(i * part_size, (i + 1) * part_size)
+            stream[:, spot] = by_place[2 * (here ^ (i // 2)) + (core ^ (i % 2))]
 
     @pl.when((step > 0) & ((step - 1) % tiles == 0))
     def _():
         sums[...] = jnp.zeros_like(sums)
 
     def project(pieces):
-        head_grad = None
-        for i, piece in enumerate(pieces):
-            rows = stream[2 * (here ^ (i // 2)) + (core ^ (i % 2))]
-            part = dot(rows, piece[...].reshape(part_size, piece.shape[-1]))
-            head_grad = part if head_grad is None else head_grad + part
-        return head_grad.astype(jnp.bfloat16)
+        columns = jnp.concatenate([piece[...].reshape(part_size, piece.shape[-1]) for piece in pieces], axis=0)
+        return dot(stream[...], columns).astype(jnp.bfloat16)
 
     def hold(head_grad):
         for head in range(heads):
@@ -342,6 +341,7 @@
             ],
             scratch_shapes=[
                 pltpu.VMEM((8, tokens, spread * size), jnp.bfloat16),
+                pltpu.VMEM((tokens, width), jnp.bfloat16),
                 pltpu.VMEM((heads * tokens, HD), jnp.bfloat16),
                 pltpu.VMEM((2, span, HD), jnp.float32),
             ],
@@ -368,7 +368,7 @@
 def finish(kept, later):
     out = jax.ShapeDtypeStruct(kept.shape[1:], jnp.float32)
     return pl.pallas_call(
-        finish_kernel, out_shape=(out, out), compiler_params=params(16), cost_estimate=LIGHT, name="finish"
+        finish_kernel, out_shape=(out, out), compiler_params=params(60), cost_estimate=LIGHT, name="finish"
     )(kept, later)
 
 
@@ -430,10 +430,12 @@
     )
     lines = [own_line, near_line, far_line]
     last_line = line(w_last)
-    far_crossed = cross(far_line)
+    half = low // 2
+    far_first, far_rest = cross(far_line[:half]), cross(far_line[half:])
     last_crossed = cross(last_line)
     terms = experts(rows_in.reshape(owners * depth, 2 * width), *prepared)
-    terms, lines, crossed = lax.optimization_barrier((terms, lines, crossed))
+    terms, lines, crossed, far_first = lax.optimization_barrier((terms, lines, crossed, far_first))
+    far_crossed = jnp.concatenate([far_first, far_rest], axis=0)
     back = lax.all_to_all(terms.reshape(owners, depth, width), chips, 0, 0, tiled=True)
     both = lambda pieces: [w for piece in pieces for w in (piece, other_core(piece))]
 

time: 227 us -> 235 us (1.035)
  local copies, waits for them, and re-layouts: 13.3 us -> 21.5 us
  waiting for transfers between devices: 110 us -> 117 us
  starting transfers between devices: 43.6 us -> 37.3 us
    all_gather x4, waiting for transfers between devices: 31.5 us -> 39.7 us  [local(): line = lambda w: lax.all_gather(w, 'low', axis=0, tiled=False)]
    unnamed x52 -> x55, local copies, waits for them, and re-layouts: 12.4 us -> 17.5 us
    ppermute x11, starting transfers between devices: 14.5 us -> 9.4 us  [local(): other_core = lambda w: lax.ppermute(w, 'core', swap)]
    ppermute x4 -> x5, waiting for transfers between devices: 36.5 us -> 31.8 us  [local(): cross = lambda w: lax.ppermute(w, 'groups', swap)]
    ppermute x11, waiting for transfers between devices: 2.6 us -> 6.1 us  [local(): other_core = lambda w: lax.ppermute(w, 'core', swap)]
    pallas_call x1, Pallas kernels: 14.2 us -> 11.7 us  [experts(): pl.pallas_call(functools.partial(expert_kernel, steps), grid=(steps + wid...]
    ppermute x4 -> x5, starting transfers between devices: 3.95 us -> 5.29 us  [local(): cross = lambda w: lax.ppermute(w, 'groups', swap)]
  transfers between devices with their start and end apart: 26 -> 27, of which waited for: 9 -> 12; matrix products, arithmetic and copies ran while one was open for 0% -> 2% of each run, Pallas kernels for 12% -> 11%
where the time goes in v14:
time: 235 us; the launch traced here: 234 us
  waiting for transfers between devices  117 us (50%)
  Pallas kernels  43.6 us (19%)
  starting transfers between devices  37.3 us (16%)
  local copies, waits for them, and re-layouts  21.5 us (9%)
  between operations  14 us (6%)
    all_gather x4, waiting for transfers between devices, local(): line = lambda w: lax.all_gather(w, 'low', axis=0, tiled=False)  39.7 us
    ppermute x5, waiting for transfers between devices, local(): cross = lambda w: lax.ppermute(w, 'groups', swap)  31.8 us
    ppermute x1, waiting for transfers between devices, local(): prev = lax.ppermute(jnp.concatenate([kv, seg_rows], axis=0), blk, onward)  18.9 us
    unnamed x55, local copies, waits for them, and re-layouts  17.5 us
    pallas_call x1, Pallas kernels, tail(): pl.pallas_call(functools.partial(tail_kernel, (heads, tiles)), grid_spec=...  16.7 us
    ppermute x1, waiting for transfers between devices, local(): w_last = lax.ppermute(w_far, 'near', swap)  14.9 us
    pallas_call x1, Pallas kernels, experts(): pl.pallas_call(functools.partial(expert_kernel, steps), grid=(steps + wid...  11.7 us
    all_to_all x1, starting transfers between devices, local(): lax.all_to_all(terms.reshape(owners, depth, width), chips, 0, 0, tiled=True)  10.9 us
  transfers between devices with their start and end apart: 27, of which 12 were waited for; matrix products, arithmetic and copies ran while one was open for 2% of the time, Pallas kernels for 11%

profile of v14, /device:TPU:13, one launch (start us, length us, event | category | flops | bytes accessed | tf_op | source)
XLA Modules:
  0.0 233.7 jit_solution(13603964280367789118)
XLA Ops:
  9.5 2.3 collective-permute-start.1
  13.0 1.6 copy-done.3
  14.7 3.2 %collective-permute-start.2 = (bf16[144,512]{1,0:T(8,128)(2,1)S(1)}, bf16[144,512]{1,0:T(8,128)(2,1)S(1)}, u32[]{:S(2)}, u32[]{:S(2)}) collective-permute-start(bf16[144,512]{1,0:T(8,128)(2,1)S(1)} %fusion.1), channel_id=1, source_target_pairs={{0,1},{1,2},{2,3},{3,4},{4,5},{5,6},{6,7},{7,8},{8,9},{9,10},{10,1... | collective-permute-start | bytes 442376 | tf_op jit(solution)/shard_map/ppermute | solution.py:417
  17.8 18.9 %collective-permute-done.2.prev_key_ref.prev_value_ref.prev_seg_ref = bf16[144,512]{1,0:T(8,128)(2,1)S(1)} collective-permute-done((bf16[144,512]{1,0:T(8,128)(2,1)S(1)}, bf16[144,512]{1,0:T(8,128)(2,1)S(1)}, u32[]{:S(2)}, u32[]{:S(2)}) %collective-permute-start.2) | collective-permute-done | bytes 147488 | tf_op jit(solution)/shard_map/ppermute | solution.py:417
  37.5 3.6 %all-to-all-start = ((bf16[8,48,4096]{2,1,0:T(8,128)(2,1)}), bf16[8,48,4096]{2,1,0:T(8,128)(2,1)S(1)}, u32[]{:S(2)}, u32[]{:S(2)}) async-start(bf16[8,48,4096]{2,1,0:T(8,128)(2,1)} %bitcast.21), calls=%async_computation | async-start | bytes 6291456 | tf_op jit(solution)/shard_map/all_to_all | solution.py:421
  41.2 3.5 %collective-permute-start.3 = (bf16[2048,384]{1,0:T(8,128)(2,1)}, bf16[2048,384]{1,0:T(8,128)(2,1)}, u32[]{:S(2)}, u32[]{:S(2)}) collective-permute-start(bf16[2048,384]{1,0:T(8,128)(2,1)} %refs_0_.1), channel_id=1, source_target_pairs={{0,1},{1,0},{2,3},{3,2},{4,5},{5,4},{6,7},{7,6},{8,9},{9,8},{10,11... | collective-permute-start | bytes 4718600 | tf_op jit(solution)/shard_map/ppermute | solution.py:409
  48.1 3.5 %attention_shares.1 = (bf16[2,2048,256]{2,1,0:T(8,128)(2,1)S(1)}, bf16[2,256,2048]{2,1,0:T(8,128)(2,1)S(1)}, bf16[2,2048,128]{2,1,0:T(8,128)(2,1)S(1)}, bf16[2,2...) custom-call(bf16[128,4096]{1,0:T(8,128)(2,1)S(1)} %copy-done.9, bf16[128,256]{1,0:T(8,128)(2,1)S(1)} %copy-done.12, ...), custom_call_target="tpu_custom_call" | custom-call | tf_op jit(solution)/shard_map/attention_shares/pallas_call | solution.py:201
  59.5 8.8 %prepare_weights.1 = (bf16[3,2048,512]{2,1,0:T(8,128)(2,1)}, bf16[3,2048,256]{2,1,0:T(8,128)(2,1)}, bf16[3,512,2048]{2,1,0:T(8,128)(2,1)}) custom-call(bf16[2048,384]{1,0:T(8,128)(2,1)S(1)} %copy-done.6, bf16[2048,384]{1,0:T(8,128)(2,1)S(1)} %copy-done.7, bf16[384,2048]{1,0:T(8,128)(2,1)S(1)} %copy-done.8, bf16[2048,384]{1,0:T(8,128)(2,1)} %collective-permute-done.3.refs_3_, ...), custom_call_target="tpu_custom_call" | custom-call | tf_op jit(solution)/shard_map/prepare_weights/pallas_call | solution.py:94
  68.3 16.8 %all-gather.11.cloned.1.call-done = bf16[256,2048]{1,0:T(8,128)(2,1)} async-done(((bf16[128,2048]{1,0:T(8,128)(2,1)}), bf16[256,2048]{1,0:T(8,128)(2,1)}) %all-gather.11.cloned.1.call-update) | async-done | bytes 1048592 | tf_op jit(solution)/shard_map/all_gather | solution.py:407
  86.3 14.9 %collective-permute-done.8 = bf16[128,2048]{1,0:T(8,128)(2,1)} collective-permute-done((bf16[128,2048]{1,0:T(8,128)(2,1)}, bf16[128,2048]{1,0:T(8,128)(2,1)}, u32[]{:S(2)}, u32[]{:S(2)}) %collective-permute-start.8) | collective-permute-done | bytes 524320 | tf_op jit(solution)/shard_map/ppermute | solution.py:423
  101.1 13.2 %all-gather.13.cloned.1.call-done = bf16[256,2048]{1,0:T(8,128)(2,1)} async-done(((bf16[128,2048]{1,0:T(8,128)(2,1)}), bf16[256,2048]{1,0:T(8,128)(2,1)}) %all-gather.13.cloned.1.call-update) | async-done | bytes 1048592 | tf_op jit(solution)/shard_map/all_gather | solution.py:407
  114.3 2.3 fusion.2
  117.8 11.7 %expert_terms.1 = bf16[384,2048]{1,0:T(8,128)(2,1)S(1)} custom-call(bf16[384,4096]{1,0:T(8,128)(2,1)S(1)} %bitcast.19, bf16[3,2048,512]{2,1,0:T(8,128)(2,1)} %get-tuple-element.99.cols_ref, bf16[3,2048,256]{2,1,0:T(8,128)(2,1)} %get-tuple-element.100.down_ref, bf16[3,512,2048]{2,1,0:T(8,128)(2,1)} %get-tuple-element.101.back_ref), custom_call_target="tpu_custom_call" | custom-call | tf_op jit(solution)/shard_map/expert_terms/pallas_call | solution.py:145
  130.8 10.9 %all-to-all-start.1 = ((bf16[8,48,2048]{2,1,0:T(8,128)(2,1)}), bf16[8,48,2048]{2,1,0:T(8,128)(2,1)S(1)}, u32[]{:S(2)}, u32[]{:S(2)}) async-start(bf16[8,48,2048]{2,1,0:T(8,128)(2,1)} %bitcast.20), calls=%async_computation.1 | async-start | bytes 3145728 | tf_op jit(solution)/shard_map/all_to_all | solution.py:439
  141.6 1.8 collective-permute-start.10
  144.0 9.7 %all-gather.15.cloned.1.call-done = bf16[256,2048]{1,0:T(8,128)(2,1)} async-done(((bf16[128,2048]{1,0:T(8,128)(2,1)}), bf16[256,2048]{1,0:T(8,128)(2,1)}) %all-gather.15.cloned.1.call-update) | async-done | bytes 1048592 | tf_op jit(solution)/shard_map/all_gather | solution.py:407
  155.3 1.9 constant_dynamic-update-slice_fusion.1
  157.2 31.6 %collective-permute-done.16 = bf16[1,128,2048]{2,1,0:T(8,128)(2,1)S(1)} collective-permute-done((bf16[1,128,2048]{2,1,0:T(8,128)(2,1)S(1)}, bf16[1,128,2048]{2,1,0:T(8,128)(2,1)S(1)}, u32[]{:S(2)}, u32[]{:S(2)}) %collective-permute-start.16) | collective-permute-done | bytes 524320 | tf_op jit(solution)/shard_map/ppermute | solution.py:408
  188.8 2.0 collective-permute-start.14
  193.5 3.0 %collective-permute-done.15.refs_11_ = bf16[2,128,2048]{2,1,0:T(8,128)(2,1)} collective-permute-done((bf16[2,128,2048]{2,1,0:T(8,128)(2,1)}, bf16[2,128,2048]{2,1,0:T(8,128)(2,1)}, u32[]{:S(2)}, u32[]{:S(2)}) %collective-permute-start.15) | collective-permute-done | bytes 1048608 | tf_op jit(solution)/shard_map/ppermute | solution.py:409
  200.7 16.7 %tail_attention.1 = (bf16[128,2048]{1,0:T(8,128)(2,1)}, bf16[128,4096]{1,0:T(8,128)(2,1)}, f32[2,128,256]{2,1,0:T(8,128)}, bf16[2,128,256]{2,1,0:T(8,128)(2,1)}) custom-call(s32[3]{0:T(128)} %pad_add_fusion.place_info, bf16[384,2048]{1,0:T(8,128)(2,1)} %bitcast.24, bf16[128,384]{1,0:T(8,128)(2,1)} %copy-done.16, bf16[128,2048]{1,0:T(8,128)(2,1)} %grad_ref.3, ...), custom_call_target="tpu_custom_call" | custom-call | flops 2147483648 | bytes 23068672 | tf_op jit(solution)/shard_map/tail_attention/pallas_call | solution.py:317
  217.4 2.3 collective-permute-start.20
  219.7 5.1 %collective-permute-done.20.later_ref = bf16[2,128,256]{2,1,0:T(8,128)(2,1)S(1)} collective-permute-done((bf16[2,128,256]{2,1,0:T(8,128)(2,1)}, bf16[2,128,256]{2,1,0:T(8,128)(2,1)S(1)}, u32[]{:S(2)}, u32[]{:S(2)}) %collective-permute-start.20) | collective-permute-done | bytes 131104 | tf_op jit(solution)/shard_map/ppermute | solution.py:448
  225.4 1.7 finish.1
  (102 shorter events, 28.6 us)
Async XLA Ops:
  7.3 29.5 %all-gather.9.cloned.1.call-start = ((), (), s32[]{:S(2)}) async-start(), calls=%async_computation.2 | async-start | bytes 1572864 | tf_op jit(solution)/shard_map/all_gather | solution.py:407
  9.3 27.4 %collective-permute-start = (bf16[128,2048]{1,0:T(8,128)(2,1)}, bf16[128,2048]{1,0:T(8,128)(2,1)}, u32[]{:S(2)}, u32[]{:S(2)}) collective-permute-start(bf16[128,2048]{1,0:T(8,128)(2,1)} %constant_dynamic-slice_fusion), channel_id=1, source_target_pairs={{0,4},{4,0},{1,5},{5,1},{2,6},{6,2},{3,7},{7,3},{8,12},{12,8},{9,1... | collective-permute-start | bytes 1572872 | tf_op jit(solution)/shard_map/ppermute | solution.py:403
  9.5 27.2 %collective-permute-start.1 = (bf16[128,2048]{1,0:T(8,128)(2,1)}, bf16[128,2048]{1,0:T(8,128)(2,1)S(1)}, u32[]{:S(2)}, u32[]{:S(2)}) collective-permute-start(bf16[128,2048]{1,0:T(8,128)(2,1)} %constant_dynamic-slice_fusion), channel_id=1, source_target_pairs={{0,8},{8,0},{1,9},{9,1},{2,10},{10,2},{3,11},{11,3},{4,12},{12,4},... | collective-permute-start | bytes 1572872 | tf_op jit(solution)/shard_map/ppermute | solution.py:404
  14.7 22.0 %collective-permute-start.2 = (bf16[144,512]{1,0:T(8,128)(2,1)S(1)}, bf16[144,512]{1,0:T(8,128)(2,1)S(1)}, u32[]{:S(2)}, u32[]{:S(2)}) collective-permute-start(bf16[144,512]{1,0:T(8,128)(2,1)S(1)} %fusion.1), channel_id=1, source_target_pairs={{0,1},{1,2},{2,3},{3,4},{4,5},{5,6},{6,7},{7,8},{8,9},{9,10},{10,1... | collective-permute-start | bytes 442376 | tf_op jit(solution)/shard_map/ppermute | solution.py:417
  37.5 76.8 %all-to-all-start = ((bf16[8,48,4096]{2,1,0:T(8,128)(2,1)}), bf16[8,48,4096]{2,1,0:T(8,128)(2,1)S(1)}, u32[]{:S(2)}, u32[]{:S(2)}) async-start(bf16[8,48,4096]{2,1,0:T(8,128)(2,1)} %bitcast.21), calls=%async_computation | async-start | bytes 6291456 | tf_op jit(solution)/shard_map/all_to_all | solution.py:421
  41.1 43.9 %all-gather.11.cloned.1.call-start = ((), (), s32[]{:S(2)}) async-start(), calls=%async_computation.3 | async-start | bytes 1572864 | tf_op jit(solution)/shard_map/all_gather | solution.py:407
  41.2 15.5 %collective-permute-start.3 = (bf16[2048,384]{1,0:T(8,128)(2,1)}, bf16[2048,384]{1,0:T(8,128)(2,1)}, u32[]{:S(2)}, u32[]{:S(2)}) collective-permute-start(bf16[2048,384]{1,0:T(8,128)(2,1)} %refs_0_.1), channel_id=1, source_target_pairs={{0,1},{1,0},{2,3},{3,2},{4,5},{5,4},{6,7},{7,6},{8,9},{9,8},{10,11... | collective-permute-start | bytes 4718600 | tf_op jit(solution)/shard_map/ppermute | solution.py:409
  44.7 11.9 %collective-permute-start.4 = (bf16[2048,384]{1,0:T(8,128)(2,1)}, bf16[2048,384]{1,0:T(8,128)(2,1)}, u32[]{:S(2)}, u32[]{:S(2)}) collective-permute-start(bf16[2048,384]{1,0:T(8,128)(2,1)} %refs_1_.1), channel_id=1, source_target_pairs={{0,1},{1,0},{2,3},{3,2},{4,5},{5,4},{6,7},{7,6},{8,9},{9,8},{10,11... | collective-permute-start | bytes 4718600 | tf_op jit(solution)/shard_map/ppermute | solution.py:409
  44.7 11.9 %collective-permute-start.5 = (bf16[384,2048]{1,0:T(8,128)(2,1)}, bf16[384,2048]{1,0:T(8,128)(2,1)}, u32[]{:S(2)}, u32[]{:S(2)}) collective-permute-start(bf16[384,2048]{1,0:T(8,128)(2,1)} %refs_2_.1), channel_id=1, source_target_pairs={{0,1},{1,0},{2,3},{3,2},{4,5},{5,4},{6,7},{7,6},{8,9},{9,8},{10,11... | collective-permute-start | bytes 4718600 | tf_op jit(solution)/shard_map/ppermute | solution.py:409
  45.2 69.1 %all-gather.13.cloned.1.call-start = ((), (), s32[]{:S(2)}) async-start(), calls=%async_computation.4 | async-start | bytes 1572864 | tf_op jit(solution)/shard_map/all_gather | solution.py:407
  45.4 69.0 %collective-permute-start.6 = (bf16[2,128,2048]{2,1,0:T(8,128)(2,1)}, bf16[2,128,2048]{2,1,0:T(8,128)(2,1)}, u32[]{:S(2)}, u32[]{:S(2)}) collective-permute-start(bf16[2,128,2048]{2,1,0:T(8,128)(2,1)} %bitcast.28), channel_id=1, source_target_pairs={{0,16},{16,0},{1,17},{17,1},{2,18},{18,2},{3,19},{19,3},{4,20},{20... | collective-permute-start | bytes 3145736 | tf_op jit(solution)/shard_map/ppermute | solution.py:408
  46.7 107.0 %all-gather.15.cloned.1.call-start = ((), (), s32[]{:S(2)}) async-start(), calls=%async_computation.5 | async-start | bytes 1572864 | tf_op jit(solution)/shard_map/all_gather | solution.py:407
  85.1 29.3 %collective-permute-start.7 = (bf16[2,128,2048]{2,1,0:T(8,128)(2,1)}, bf16[2,128,2048]{2,1,0:T(8,128)(2,1)}, u32[]{:S(2)}, u32[]{:S(2)}) collective-permute-start(bf16[2,128,2048]{2,1,0:T(8,128)(2,1)} %bitcast.31), channel_id=1, source_target_pairs={{0,16},{16,0},{1,17},{17,1},{2,18},{18,2},{3,19},{19,3},{4,20},{20... | collective-permute-start | bytes 3145736 | tf_op jit(solution)/shard_map/ppermute | solution.py:408
  86.3 14.9 %collective-permute-start.8 = (bf16[128,2048]{1,0:T(8,128)(2,1)}, bf16[128,2048]{1,0:T(8,128)(2,1)}, u32[]{:S(2)}, u32[]{:S(2)}) collective-permute-start(bf16[128,2048]{1,0:T(8,128)(2,1)} %copy-done.23), channel_id=1, source_target_pairs={{0,4},{4,0},{1,5},{5,1},{2,6},{6,2},{3,7},{7,3},{8,12},{12,8},{9,1... | collective-permute-start | bytes 1572872 | tf_op jit(solution)/shard_map/ppermute | solution.py:423
  116.6 13.1 %collective-permute-start.9 = (bf16[1,128,2048]{2,1,0:T(8,128)(2,1)}, bf16[1,128,2048]{2,1,0:T(8,128)(2,1)}, u32[]{:S(2)}, u32[]{:S(2)}) collective-permute-start(bf16[1,128,2048]{2,1,0:T(8,128)(2,1)} %get-tuple-element.127), channel_id=1, source_target_pairs={{0,16},{16,0},{1,17},{17,1},{2,18},{18,2},{3,19},{19,3},{4,20},{20... | collective-permute-start | bytes 1572872 | tf_op jit(solution)/shard_map/ppermute | solution.py:408
  130.8 68.7 %all-to-all-start.1 = ((bf16[8,48,2048]{2,1,0:T(8,128)(2,1)}), bf16[8,48,2048]{2,1,0:T(8,128)(2,1)S(1)}, u32[]{:S(2)}, u32[]{:S(2)}) async-start(bf16[8,48,2048]{2,1,0:T(8,128)(2,1)} %bitcast.20), calls=%async_computation.1 | async-start | bytes 3145728 | tf_op jit(solution)/shard_map/all_to_all | solution.py:439
  141.6 50.1 %collective-permute-start.10 = (bf16[2,128,2048]{2,1,0:T(8,128)(2,1)}, bf16[2,128,2048]{2,1,0:T(8,128)(2,1)}, u32[]{:S(2)}, u32[]{:S(2)}) collective-permute-start(bf16[2,128,2048]{2,1,0:T(8,128)(2,1)} %bitcast.29), channel_id=1, source_target_pairs={{0,1},{1,0},{2,3},{3,2},{4,5},{5,4},{6,7},{7,6},{8,9},{9,8},{10,11... | collective-permute-start | bytes 3145736 | tf_op jit(solution)/shard_map/ppermute | solution.py:409
  143.5 48.2 %collective-permute-start.11 = (bf16[2,128,2048]{2,1,0:T(8,128)(2,1)}, bf16[2,128,2048]{2,1,0:T(8,128)(2,1)}, u32[]{:S(2)}, u32[]{:S(2)}) collective-permute-start(bf16[2,128,2048]{2,1,0:T(8,128)(2,1)} %bitcast.32), channel_id=1, source_target_pairs={{0,1},{1,0},{2,3},{3,2},{4,5},{5,4},{6,7},{7,6},{8,9},{9,8},{10,11... | collective-permute-start | bytes 3145736 | tf_op jit(solution)/shard_map/ppermute | solution.py:409
  143.5 48.7 %collective-permute-start.12 = (bf16[2,128,2048]{2,1,0:T(8,128)(2,1)S(1)}, bf16[2,128,2048]{2,1,0:T(8,128)(2,1)}, u32[]{:S(2)}, u32[]{:S(2)}) collective-permute-start(bf16[2,128,2048]{2,1,0:T(8,128)(2,1)S(1)} %bitcast.27), channel_id=1, source_target_pairs={{0,1},{1,0},{2,3},{3,2},{4,5},{5,4},{6,7},{7,6},{8,9},{9,8},{10,11... | collective-permute-start | bytes 3145736 | tf_op jit(solution)/shard_map/ppermute | solution.py:409
  153.7 38.6 %collective-permute-start.18 = (bf16[2,128,2048]{2,1,0:T(8,128)(2,1)}, bf16[2,128,2048]{2,1,0:T(8,128)(2,1)}, u32[]{:S(2)}, u32[]{:S(2)}) collective-permute-start(bf16[2,128,2048]{2,1,0:T(8,128)(2,1)} %bitcast.15.refs_6_), channel_id=1, source_target_pairs={{0,16},{16,0},{1,17},{17,1},{2,18},{18,2},{3,19},{19,3},{4,20},{20... | collective-permute-start | bytes 3145736 | tf_op jit(solution)/shard_map/ppermute | solution.py:408
  155.3 33.5 %collective-permute-start.16 = (bf16[1,128,2048]{2,1,0:T(8,128)(2,1)S(1)}, bf16[1,128,2048]{2,1,0:T(8,128)(2,1)S(1)}, u32[]{:S(2)}, u32[]{:S(2)}) collective-permute-start(bf16[1,128,2048]{2,1,0:T(8,128)(2,1)S(1)} %copy-done.24), channel_id=1, source_target_pairs={{0,16},{16,0},{1,17},{17,1},{2,18},{18,2},{3,19},{19,3},{4,20},{20... | collective-permute-start | bytes 1572872 | tf_op jit(solution)/shard_map/ppermute | solution.py:408
  191.7 6.3 %collective-permute-start.17 = (bf16[2,128,2048]{2,1,0:T(8,128)(2,1)}, bf16[2,128,2048]{2,1,0:T(8,128)(2,1)}, u32[]{:S(2)}, u32[]{:S(2)}) collective-permute-start(bf16[2,128,2048]{2,1,0:T(8,128)(2,1)} %constant_dynamic-update-slice_fusion.refs_12_), channel_id=1, source_target_pairs={{0,1},{1,0},{2,3},{3,2},{4,5},{5,4},{6,7},{7,6},{8,9},{9,8},{10,11... | collective-permute-start | bytes 3145736 | tf_op jit(solution)/shard_map/ppermute | solution.py:409
  192.3 7.2 %collective-permute-start.19 = (bf16[2,128,2048]{2,1,0:T(8,128)(2,1)}, bf16[2,128,2048]{2,1,0:T(8,128)(2,1)}, u32[]{:S(2)}, u32[]{:S(2)}) collective-permute-start(bf16[2,128,2048]{2,1,0:T(8,128)(2,1)} %collective-permute-done.18.refs_14_), channel_id=1, source_target_pairs={{0,1},{1,0},{2,3},{3,2},{4,5},{5,4},{6,7},{7,6},{8,9},{9,8},{10,11... | collective-permute-start | bytes 3145736 | tf_op jit(solution)/shard_map/ppermute | solution.py:409
  217.4 7.4 %collective-permute-start.20 = (bf16[2,128,256]{2,1,0:T(8,128)(2,1)}, bf16[2,128,256]{2,1,0:T(8,128)(2,1)S(1)}, u32[]{:S(2)}, u32[]{:S(2)}) collective-permute-start(bf16[2,128,256]{2,1,0:T(8,128)(2,1)} %get-tuple-element.123), channel_id=1, source_target_pairs={{1,0},{2,1},{3,2},{4,3},{5,4},{6,5},{7,6},{8,7},{9,8},{10,9},{11,1... | collective-permute-start | bytes 393224 | tf_op jit(solution)/shard_map/ppermute | solution.py:448
  (30 other events, 169.0 us)
Sparse Core Ops, SparseCore 0:
  10.2 23.1 all-gather.8
  45.3 39.6 all-gather.10
  87.2 27.1 all-gather.12
  118.0 35.6 all-gather.14

commit v15 on v14

--- a/solution.py
+++ b/solution.py
@@ -223,13 +223,14 @@
     plan, place_info, back_ref, place_ref, grad_ref, *refs
 ):
     heads, tiles = plan
-    mine, across, refs = refs[:8], refs[8:16], refs[16:]
+    mine, across, last, refs = refs[:6], refs[6:12], refs[12:14], refs[14:]
     low_ref, turned_ref, q_ref, key_ref, value_ref, *refs = refs
     moe_ref, query_out, kept_out, sent_out, by_place, stream, held, sums = refs
     step = pl.program_id(0)
     tokens = query_out.shape[0]
     part_size = by_place.shape[2]
     size = mine[0].shape[1]
+    mine, across = mine + last, across + last
     spread = part_size // size
     here, core = place_info[1], place_info[2]
 
@@ -312,6 +313,8 @@
     rows = lambda shape: pl.BlockSpec((1,) + shape, lambda i, info: (kv_group(i, info), was(i) % tiles, 0))
     own_tile = lambda i: jnp.minimum(i, tiles - 1)
     other_tile = lambda i: jnp.minimum(jnp.maximum(i - tiles, 0), tiles - 1)
+    now = lambda i: jnp.minimum(i, steps - 1)
+    last = pl.BlockSpec((spread, 1, size, tile), lambda i, info: (0, now(i) // tiles, 0, now(i) % tiles))
     piece = lambda turn: pl.BlockSpec((spread, size, tile), lambda i, info: (0, 0, turn(i)))
     kv = pl.BlockSpec((2, tokens, HD), lambda i, info: (0, 0, kv_group(i, info)))
     return pl.pallas_call(
@@ -320,8 +323,9 @@
             num_scalar_prefetch=1,
             grid=(steps + 1,),
             in_specs=[whole(back.shape), whole(place.shape), whole(moe_grad.shape)]
-            + [piece(own_tile)] * 8
-            + [piece(other_tile)] * 8
+            + [piece(own_tile)] * 6
+            + [piece(other_tile)] * 6
+            + [last] * 2
             + [
                 rows((heads * tokens, span)),
                 pl.BlockSpec(
@@ -429,13 +433,11 @@
         (rows_in, prepared, attention, near_line, far_line, crossed, w_last)
     )
     lines = [own_line, near_line, far_line]
-    last_line = line(w_last)
-    half = low // 2
-    far_first, far_rest = cross(far_line[:half]), cross(far_line[half:])
-    last_crossed = cross(last_line)
+    last_crossed = cross(w_last)
     terms = experts(rows_in.reshape(owners * depth, 2 * width), *prepared)
-    terms, lines, crossed, far_first = lax.optimization_barrier((terms, lines, crossed, far_first))
-    far_crossed = jnp.concatenate([far_first, far_rest], axis=0)
+    terms, lines, crossed, last_crossed = lax.optimization_barrier((terms, lines, crossed, last_crossed))
+    last_line = line(jnp.stack([w_last, last_crossed]))
+    far_crossed = cross(lines[2])
     back = lax.all_to_all(terms.reshape(owners, depth, width), chips, 0, 0, tiled=True)
     both = lambda pieces: [w for piece in pieces for w in (piece, other_core(piece))]
 
@@ -443,7 +445,7 @@
     moe_input_grad, query_grad, kept, sent = tail(
         jnp.stack([lax.axis_index("groups"), z, lax.axis_index("core")]).astype(jnp.int32),
         back.reshape(owners * depth, width), place, moe_grad,
-        both(lines + [last_line]) + both(crossed + [far_crossed, last_crossed]), *attention,
+        both(lines) + both(crossed + [far_crossed]) + both([last_line]), *attention,
     )
     return (moe_input_grad, query_grad, *finish(kept, lax.ppermute(sent, blk, backward)))
 

time: 235 us -> 230 us (0.979)
  local copies, waits for them, and re-layouts: 21.5 us -> 17.7 us
  waiting for transfers between devices: 117 us -> 114 us
  starting transfers between devices: 37.3 us -> 34.6 us
    ppermute x5 -> x4, waiting for transfers between devices: 31.8 us -> 0.01 us  [local(): cross = lambda w: lax.ppermute(w, 'groups', swap)]
    all_gather x4, waiting for transfers between devices: 39.7 us -> 70.2 us  [local(): line = lambda w: lax.all_gather(w, 'low', axis=0, tiled=False)]
    ppermute x1, waiting for transfers between devices: 18.9 us -> 15.4 us  [local(): prev = lax.ppermute(jnp.concatenate([kv, seg_rows], axis=0), blk, onward)]
    ppermute x11 -> x10, starting transfers between devices: 9.4 us -> 6.31 us  [local(): other_core = lambda w: lax.ppermute(w, 'core', swap)]
    ppermute x11 -> x10, waiting for transfers between devices: 6.1 us -> 8.5 us  [local(): other_core = lambda w: lax.ppermute(w, 'core', swap)]
    ppermute x5 -> x4, starting transfers between devices: 5.29 us -> 4.46 us  [local(): cross = lambda w: lax.ppermute(w, 'groups', swap)]
    unnamed x55 -> x50, local copies, waits for them, and re-layouts: 17.5 us -> 16.8 us
  transfers between devices with their start and end apart: 27 -> 25, of which waited for: 12 -> 10; matrix products, arithmetic and copies ran while one was open for 2% -> 0% of each run, Pallas kernels for 11% -> 12%
where the time goes in v15:
time: 230 us; the launch traced here: 228 us
  waiting for transfers between devices  114 us (50%)
  Pallas kernels  45.7 us (20%)
  starting transfers between devices  34.6 us (15%)
  local copies, waits for them, and re-layouts  17.7 us (8%)
  between operations  14 us (6%)
    all_gather x4, waiting for transfers between devices, local(): line = lambda w: lax.all_gather(w, 'low', axis=0, tiled=False)  70.2 us
    unnamed x50, local copies, waits for them, and re-layouts  16.8 us
    pallas_call x1, Pallas kernels, tail(): pl.pallas_call(functools.partial(tail_kernel, (heads, tiles)), grid_spec=...  16.6 us
    ppermute x1, waiting for transfers between devices, local(): prev = lax.ppermute(jnp.concatenate([kv, seg_rows], axis=0), blk, onward)  15.4 us
    ppermute x1, waiting for transfers between devices, local(): w_last = lax.ppermute(w_far, 'near', swap)  14.8 us
    pallas_call x1, Pallas kernels, experts(): pl.pallas_call(functools.partial(expert_kernel, steps), grid=(steps + wid...  13.9 us
    all_to_all x1, starting transfers between devices, local(): lax.all_to_all(terms.reshape(owners, depth, width), chips, 0, 0, tiled=True)  11.1 us
    pallas_call x1, Pallas kernels, prepare_weights(): pl.pallas_call(weights_kernel, grid=(steps,), in_specs=[cols, cols, down]...  8.82 us
  transfers between devices with their start and end apart: 25, of which 10 were waited for; matrix products, arithmetic and copies ran while one was open for 0% of the time, Pallas kernels for 12%

profile of v15, /device:TPU:13, one launch (start us, length us, event | category | flops | bytes accessed | tf_op | source)
XLA Modules:
  0.0 227.9 jit_solution(3776612196970511184)
XLA Ops:
  9.5 2.3 %collective-permute-start.1 = (bf16[128,2048]{1,0:T(8,128)(2,1)}, bf16[128,2048]{1,0:T(8,128)(2,1)S(1)}, u32[]{:S(2)}, u32[]{:S(2)}) collective-permute-start(bf16[128,2048]{1,0:T(8,128)(2,1)} %constant_dynamic-slice_fusion), channel_id=1, source_target_pairs={{0,8},{8,0},{1,9},{9,1},{2,10},{10,2},{3,11},{11,3},{4,12},{12,4},... | collective-permute-start | bytes 1572872 | tf_op jit(solution)/shard_map/ppermute | solution.py:408
  16.4 1.6 copy-done.1
  18.1 3.1 %collective-permute-start.2 = (bf16[144,512]{1,0:T(8,128)(2,1)S(1)}, bf16[144,512]{1,0:T(8,128)(2,1)S(1)}, u32[]{:S(2)}, u32[]{:S(2)}) collective-permute-start(bf16[144,512]{1,0:T(8,128)(2,1)S(1)} %fusion.1), channel_id=1, source_target_pairs={{0,1},{1,2},{2,3},{3,4},{4,5},{5,6},{6,7},{7,8},{8,9},{9,10},{10,1... | collective-permute-start | bytes 442376 | tf_op jit(solution)/shard_map/ppermute | solution.py:421
  21.3 15.4 %collective-permute-done.2.prev_key_ref.prev_value_ref.prev_seg_ref = bf16[144,512]{1,0:T(8,128)(2,1)S(1)} collective-permute-done((bf16[144,512]{1,0:T(8,128)(2,1)S(1)}, bf16[144,512]{1,0:T(8,128)(2,1)S(1)}, u32[]{:S(2)}, u32[]{:S(2)}) %collective-permute-start.2) | collective-permute-done | bytes 147488 | tf_op jit(solution)/shard_map/ppermute | solution.py:421
  37.7 4.5 %all-to-all-start = ((bf16[8,48,4096]{2,1,0:T(8,128)(2,1)}), bf16[8,48,4096]{2,1,0:T(8,128)(2,1)}, u32[]{:S(2)}, u32[]{:S(2)}) async-start(bf16[8,48,4096]{2,1,0:T(8,128)(2,1)} %bitcast.21), calls=%async_computation | async-start | bytes 6291456 | tf_op jit(solution)/shard_map/all_to_all | solution.py:425
  42.3 2.5 %collective-permute-start.3 = (bf16[2048,384]{1,0:T(8,128)(2,1)S(1)}, bf16[2048,384]{1,0:T(8,128)(2,1)}, u32[]{:S(2)}, u32[]{:S(2)}) collective-permute-start(bf16[2048,384]{1,0:T(8,128)(2,1)S(1)} %copy-done.4), channel_id=1, source_target_pairs={{0,1},{1,0},{2,3},{3,2},{4,5},{5,4},{6,7},{7,6},{8,9},{9,8},{10,11... | collective-permute-start | bytes 4718600 | tf_op jit(solution)/shard_map/ppermute | solution.py:413
  48.2 3.5 %attention_shares.1 = (bf16[2,2048,256]{2,1,0:T(8,128)(2,1)S(1)}, bf16[2,256,2048]{2,1,0:T(8,128)(2,1)S(1)}, bf16[2,2048,128]{2,1,0:T(8,128)(2,1)S(1)}, bf16[2,2...) custom-call(bf16[128,4096]{1,0:T(8,128)(2,1)S(1)} %copy-done.7, bf16[128,256]{1,0:T(8,128)(2,1)S(1)} %copy-done.10, ...), custom_call_target="tpu_custom_call" | custom-call | tf_op jit(solution)/shard_map/attention_shares/pallas_call | solution.py:201
  56.7 1.4 copy-done.6
  58.1 8.8 %prepare_weights.1 = (bf16[3,2048,512]{2,1,0:T(8,128)(2,1)}, bf16[3,2048,256]{2,1,0:T(8,128)(2,1)}, bf16[3,512,2048]{2,1,0:T(8,128)(2,1)}) custom-call(bf16[2048,384]{1,0:T(8,128)(2,1)S(1)} %copy-done.4, bf16[2048,384]{1,0:T(8,128)(2,1)S(1)} %copy-done.5, bf16[384,2048]{1,0:T(8,128)(2,1)S(1)} %copy-done.6, bf16[2048,384]{1,0:T(8,128)(2,1)} %collective-permute-done.3.refs_3_, ...), custom_call_target="tpu_custom_call" | custom-call | tf_op jit(solution)/shard_map/prepare_weights/pallas_call | solution.py:94
  66.9 18.7 %all-gather.11.cloned.1.call-done = bf16[256,2048]{1,0:T(8,128)(2,1)} async-done(((bf16[128,2048]{1,0:T(8,128)(2,1)}), bf16[256,2048]{1,0:T(8,128)(2,1)}) %all-gather.11.cloned.1.call-update) | async-done | bytes 1048592 | tf_op jit(solution)/shard_map/all_gather | solution.py:411
  86.9 14.8 %collective-permute-done.8 = bf16[128,2048]{1,0:T(8,128)(2,1)S(1)} collective-permute-done((bf16[128,2048]{1,0:T(8,128)(2,1)S(1)}, bf16[128,2048]{1,0:T(8,128)(2,1)S(1)}, u32[]{:S(2)}, u32[]{:S(2)}) %collective-permute-start.8) | collective-permute-done | bytes 524320 | tf_op jit(solution)/shard_map/ppermute | solution.py:427
  101.7 12.8 %all-gather.13.cloned.1.call-done = bf16[256,2048]{1,0:T(8,128)(2,1)} async-done(((bf16[128,2048]{1,0:T(8,128)(2,1)}), bf16[256,2048]{1,0:T(8,128)(2,1)}) %all-gather.13.cloned.1.call-update) | async-done | bytes 1048592 | tf_op jit(solution)/shard_map/all_gather | solution.py:411
  115.8 13.9 %expert_terms.1 = bf16[384,2048]{1,0:T(8,128)(2,1)} custom-call(bf16[384,4096]{1,0:T(8,128)(2,1)} %bitcast.12.rows_ref, bf16[3,2048,512]{2,1,0:T(8,128)(2,1)} %get-tuple-element.99.cols_ref, bf16[3,2048,256]{2,1,0:T(8,128)(2,1)} %get-tuple-element.100.down_ref, bf16[3,512,2048]{2,1,0:T(8,128)(2,1)} %get-tuple-element.101.back_ref), custom_call_target="tpu_custom_call" | custom-call | tf_op jit(solution)/shard_map/expert_terms/pallas_call | solution.py:145
  130.8 11.1 %all-to-all-start.1 = ((bf16[8,48,2048]{2,1,0:T(8,128)(2,1)}), bf16[8,48,2048]{2,1,0:T(8,128)(2,1)S(1)}, u32[]{:S(2)}, u32[]{:S(2)}) async-start(bf16[8,48,2048]{2,1,0:T(8,128)(2,1)} %bitcast.13), calls=%async_computation.1 | async-start | bytes 3145728 | tf_op jit(solution)/shard_map/all_to_all | solution.py:441
  141.9 1.9 collective-permute-start.10
  144.5 38.7 %all-gather.15.cloned.1.call-done = bf16[4,128,2048]{2,1,0:T(8,128)(2,1)} async-done(((bf16[2,128,2048]{2,1,0:T(8,128)(2,1)}), bf16[4,128,2048]{2,1,0:T(8,128)(2,1)}) %all-gather.15.cloned.1.call-update) | async-done | bytes 2097168 | tf_op jit(solution)/shard_map/all_gather | solution.py:411
  185.2 4.0 %collective-permute-done.12.refs_5_ = bf16[2,128,2048]{2,1,0:T(8,128)(2,1)} collective-permute-done((bf16[2,128,2048]{2,1,0:T(8,128)(2,1)}, bf16[2,128,2048]{2,1,0:T(8,128)(2,1)}, u32[]{:S(2)}, u32[]{:S(2)}) %collective-permute-start.12) | collective-permute-done | bytes 1048608 | tf_op jit(solution)/shard_map/ppermute | solution.py:413
  189.2 1.5 collective-permute-done.13.refs_7_
  190.7 1.5 collective-permute-done.14.refs_9_
  192.2 1.5 collective-permute-done.16.refs_11_
  194.9 16.6 %tail_attention.1 = (bf16[128,2048]{1,0:T(8,128)(2,1)}, bf16[128,4096]{1,0:T(8,128)(2,1)}, f32[2,128,256]{2,1,0:T(8,128)}, bf16[2,128,256]{2,1,0:T(8,128)(2,1)}) custom-call(s32[3]{0:T(128)} %pad_add_fusion.place_info, bf16[384,2048]{1,0:T(8,128)(2,1)} %bitcast.24, bf16[128,384]{1,0:T(8,128)(2,1)} %copy-done.14, bf16[128,2048]{1,0:T(8,128)(2,1)} %grad_ref.3, ...), custom_call_target="tpu_custom_call" | custom-call | flops 2147483648 | bytes 23068672 | tf_op jit(solution)/shard_map/tail_attention/pallas_call | solution.py:320
  211.6 2.3 collective-permute-start.18
  213.8 5.1 %collective-permute-done.18.later_ref = bf16[2,128,256]{2,1,0:T(8,128)(2,1)S(1)} collective-permute-done((bf16[2,128,256]{2,1,0:T(8,128)(2,1)}, bf16[2,128,256]{2,1,0:T(8,128)(2,1)S(1)}, u32[]{:S(2)}, u32[]{:S(2)}) %collective-permute-start.18) | collective-permute-done | bytes 131104 | tf_op jit(solution)/shard_map/ppermute | solution.py:450
  219.6 1.7 finish.1
  (92 shorter events, 24.5 us)
Async XLA Ops:
  7.2 29.5 %all-gather.9.cloned.1.call-start = ((), (), s32[]{:S(2)}) async-start(), calls=%async_computation.2 | async-start | bytes 1572864 | tf_op jit(solution)/shard_map/all_gather | solution.py:411
  9.3 27.4 %collective-permute-start = (bf16[128,2048]{1,0:T(8,128)(2,1)}, bf16[128,2048]{1,0:T(8,128)(2,1)S(1)}, u32[]{:S(2)}, u32[]{:S(2)}) collective-permute-start(bf16[128,2048]{1,0:T(8,128)(2,1)} %constant_dynamic-slice_fusion), channel_id=1, source_target_pairs={{0,4},{4,0},{1,5},{5,1},{2,6},{6,2},{3,7},{7,3},{8,12},{12,8},{9,1... | collective-permute-start | bytes 1572872 | tf_op jit(solution)/shard_map/ppermute | solution.py:407
  9.5 27.2 %collective-permute-start.1 = (bf16[128,2048]{1,0:T(8,128)(2,1)}, bf16[128,2048]{1,0:T(8,128)(2,1)S(1)}, u32[]{:S(2)}, u32[]{:S(2)}) collective-permute-start(bf16[128,2048]{1,0:T(8,128)(2,1)} %constant_dynamic-slice_fusion), channel_id=1, source_target_pairs={{0,8},{8,0},{1,9},{9,1},{2,10},{10,2},{3,11},{11,3},{4,12},{12,4},... | collective-permute-start | bytes 1572872 | tf_op jit(solution)/shard_map/ppermute | solution.py:408
  18.1 18.6 %collective-permute-start.2 = (bf16[144,512]{1,0:T(8,128)(2,1)S(1)}, bf16[144,512]{1,0:T(8,128)(2,1)S(1)}, u32[]{:S(2)}, u32[]{:S(2)}) collective-permute-start(bf16[144,512]{1,0:T(8,128)(2,1)S(1)} %fusion.1), channel_id=1, source_target_pairs={{0,1},{1,2},{2,3},{3,4},{4,5},{5,6},{6,7},{7,8},{8,9},{9,10},{10,1... | collective-permute-start | bytes 442376 | tf_op jit(solution)/shard_map/ppermute | solution.py:421
  37.7 76.8 %all-to-all-start = ((bf16[8,48,4096]{2,1,0:T(8,128)(2,1)}), bf16[8,48,4096]{2,1,0:T(8,128)(2,1)}, u32[]{:S(2)}, u32[]{:S(2)}) async-start(bf16[8,48,4096]{2,1,0:T(8,128)(2,1)} %bitcast.21), calls=%async_computation | async-start | bytes 6291456 | tf_op jit(solution)/shard_map/all_to_all | solution.py:425
  42.2 43.4 %all-gather.11.cloned.1.call-start = ((), (), s32[]{:S(2)}) async-start(), calls=%async_computation.3 | async-start | bytes 1572864 | tf_op jit(solution)/shard_map/all_gather | solution.py:411
  42.3 14.4 %collective-permute-start.3 = (bf16[2048,384]{1,0:T(8,128)(2,1)S(1)}, bf16[2048,384]{1,0:T(8,128)(2,1)}, u32[]{:S(2)}, u32[]{:S(2)}) collective-permute-start(bf16[2048,384]{1,0:T(8,128)(2,1)S(1)} %copy-done.4), channel_id=1, source_target_pairs={{0,1},{1,0},{2,3},{3,2},{4,5},{5,4},{6,7},{7,6},{8,9},{9,8},{10,11... | collective-permute-start | bytes 4718600 | tf_op jit(solution)/shard_map/ppermute | solution.py:413
  44.8 11.9 %collective-permute-start.4 = (bf16[2048,384]{1,0:T(8,128)(2,1)}, bf16[2048,384]{1,0:T(8,128)(2,1)}, u32[]{:S(2)}, u32[]{:S(2)}) collective-permute-start(bf16[2048,384]{1,0:T(8,128)(2,1)} %refs_1_.1), channel_id=1, source_target_pairs={{0,1},{1,0},{2,3},{3,2},{4,5},{5,4},{6,7},{7,6},{8,9},{9,8},{10,11... | collective-permute-start | bytes 4718600 | tf_op jit(solution)/shard_map/ppermute | solution.py:413
  44.8 11.8 %collective-permute-start.5 = (bf16[384,2048]{1,0:T(8,128)(2,1)}, bf16[384,2048]{1,0:T(8,128)(2,1)}, u32[]{:S(2)}, u32[]{:S(2)}) collective-permute-start(bf16[384,2048]{1,0:T(8,128)(2,1)} %refs_2_.1), channel_id=1, source_target_pairs={{0,1},{1,0},{2,3},{3,2},{4,5},{5,4},{6,7},{7,6},{8,9},{9,8},{10,11... | collective-permute-start | bytes 4718600 | tf_op jit(solution)/shard_map/ppermute | solution.py:413
  45.3 69.2 %all-gather.13.cloned.1.call-start = ((), (), s32[]{:S(2)}) async-start(), calls=%async_computation.4 | async-start | bytes 1572864 | tf_op jit(solution)/shard_map/all_gather | solution.py:411
  45.5 69.1 %collective-permute-start.6 = (bf16[2,128,2048]{2,1,0:T(8,128)(2,1)}, bf16[2,128,2048]{2,1,0:T(8,128)(2,1)}, u32[]{:S(2)}, u32[]{:S(2)}) collective-permute-start(bf16[2,128,2048]{2,1,0:T(8,128)(2,1)} %bitcast.27), channel_id=1, source_target_pairs={{0,16},{16,0},{1,17},{17,1},{2,18},{18,2},{3,19},{19,3},{4,20},{20... | collective-permute-start | bytes 3145736 | tf_op jit(solution)/shard_map/ppermute | solution.py:412
  46.7 136.4 %all-gather.15.cloned.1.call-start = ((), (), s32[]{:S(2)}) async-start(), calls=%async_computation.5 | async-start | bytes 3145728 | tf_op jit(solution)/shard_map/all_gather | solution.py:411
  85.7 28.8 %collective-permute-start.7 = (bf16[2,128,2048]{2,1,0:T(8,128)(2,1)}, bf16[2,128,2048]{2,1,0:T(8,128)(2,1)S(1)}, u32[]{:S(2)}, u32[]{:S(2)}) collective-permute-start(bf16[2,128,2048]{2,1,0:T(8,128)(2,1)} %bitcast.30), channel_id=1, source_target_pairs={{0,16},{16,0},{1,17},{17,1},{2,18},{18,2},{3,19},{19,3},{4,20},{20... | collective-permute-start | bytes 3145736 | tf_op jit(solution)/shard_map/ppermute | solution.py:412
  86.9 14.8 %collective-permute-start.8 = (bf16[128,2048]{1,0:T(8,128)(2,1)S(1)}, bf16[128,2048]{1,0:T(8,128)(2,1)S(1)}, u32[]{:S(2)}, u32[]{:S(2)}) collective-permute-start(bf16[128,2048]{1,0:T(8,128)(2,1)S(1)} %copy-done.21), channel_id=1, source_target_pairs={{0,4},{4,0},{1,5},{5,1},{2,6},{6,2},{3,7},{7,3},{8,12},{12,8},{9,1... | collective-permute-start | bytes 1572872 | tf_op jit(solution)/shard_map/ppermute | solution.py:427
  114.5 15.1 %collective-permute-start.9 = (bf16[128,2048]{1,0:T(8,128)(2,1)S(1)}, bf16[128,2048]{1,0:T(8,128)(2,1)S(1)}, u32[]{:S(2)}, u32[]{:S(2)}) collective-permute-start(bf16[128,2048]{1,0:T(8,128)(2,1)S(1)} %collective-permute-done.8), channel_id=1, source_target_pairs={{0,16},{16,0},{1,17},{17,1},{2,18},{18,2},{3,19},{19,3},{4,20},{20... | collective-permute-start | bytes 1572872 | tf_op jit(solution)/shard_map/ppermute | solution.py:412
  130.8 63.0 %all-to-all-start.1 = ((bf16[8,48,2048]{2,1,0:T(8,128)(2,1)}), bf16[8,48,2048]{2,1,0:T(8,128)(2,1)S(1)}, u32[]{:S(2)}, u32[]{:S(2)}) async-start(bf16[8,48,2048]{2,1,0:T(8,128)(2,1)} %bitcast.13), calls=%async_computation.1 | async-start | bytes 3145728 | tf_op jit(solution)/shard_map/all_to_all | solution.py:441
  141.9 41.8 %collective-permute-start.10 = (bf16[2,128,2048]{2,1,0:T(8,128)(2,1)}, bf16[2,128,2048]{2,1,0:T(8,128)(2,1)}, u32[]{:S(2)}, u32[]{:S(2)}) collective-permute-start(bf16[2,128,2048]{2,1,0:T(8,128)(2,1)} %bitcast.28), channel_id=1, source_target_pairs={{0,1},{1,0},{2,3},{3,2},{4,5},{5,4},{6,7},{7,6},{8,9},{9,8},{10,11... | collective-permute-start | bytes 3145736 | tf_op jit(solution)/shard_map/ppermute | solution.py:413
  143.8 40.3 %collective-permute-start.11 = (bf16[2,128,2048]{2,1,0:T(8,128)(2,1)}, bf16[2,128,2048]{2,1,0:T(8,128)(2,1)}, u32[]{:S(2)}, u32[]{:S(2)}) collective-permute-start(bf16[2,128,2048]{2,1,0:T(8,128)(2,1)} %bitcast.31), channel_id=1, source_target_pairs={{0,1},{1,0},{2,3},{3,2},{4,5},{5,4},{6,7},{7,6},{8,9},{9,8},{10,11... | collective-permute-start | bytes 3145736 | tf_op jit(solution)/shard_map/ppermute | solution.py:413
  143.8 40.4 %collective-permute-start.15 = (bf16[2,128,2048]{2,1,0:T(8,128)(2,1)}, bf16[2,128,2048]{2,1,0:T(8,128)(2,1)}, u32[]{:S(2)}, u32[]{:S(2)}) collective-permute-start(bf16[2,128,2048]{2,1,0:T(8,128)(2,1)} %bitcast.33), channel_id=1, source_target_pairs={{0,16},{16,0},{1,17},{17,1},{2,18},{18,2},{3,19},{19,3},{4,20},{20... | collective-permute-start | bytes 3145736 | tf_op jit(solution)/shard_map/ppermute | solution.py:412
  183.2 10.6 %collective-permute-start.17 = (bf16[2,2,128,2048]{3,2,1,0:T(8,128)(2,1)}, bf16[2,2,128,2048]{3,2,1,0:T(8,128)(2,1)}, u32[]{:S(2)}, u32[]{:S(2)}) collective-permute-start(bf16[2,2,128,2048]{3,2,1,0:T(8,128)(2,1)} %bitcast.25), channel_id=1, source_target_pairs={{0,1},{1,0},{2,3},{3,2},{4,5},{5,4},{6,7},{7,6},{8,9},{9,8},{10,11... | collective-permute-start | bytes 6291464 | tf_op jit(solution)/shard_map/ppermute | solution.py:413
  183.7 7.1 %collective-permute-start.13 = (bf16[2,128,2048]{2,1,0:T(8,128)(2,1)}, bf16[2,128,2048]{2,1,0:T(8,128)(2,1)}, u32[]{:S(2)}, u32[]{:S(2)}) collective-permute-start(bf16[2,128,2048]{2,1,0:T(8,128)(2,1)} %collective-permute-done.6.refs_6_), channel_id=1, source_target_pairs={{0,1},{1,0},{2,3},{3,2},{4,5},{5,4},{6,7},{7,6},{8,9},{9,8},{10,11... | collective-permute-start | bytes 3145736 | tf_op jit(solution)/shard_map/ppermute | solution.py:413
  184.1 8.1 %collective-permute-start.14 = (bf16[2,128,2048]{2,1,0:T(8,128)(2,1)}, bf16[2,128,2048]{2,1,0:T(8,128)(2,1)}, u32[]{:S(2)}, u32[]{:S(2)}) collective-permute-start(bf16[2,128,2048]{2,1,0:T(8,128)(2,1)} %copy-done.19), channel_id=1, source_target_pairs={{0,1},{1,0},{2,3},{3,2},{4,5},{5,4},{6,7},{7,6},{8,9},{9,8},{10,11... | collective-permute-start | bytes 3145736 | tf_op jit(solution)/shard_map/ppermute | solution.py:413
  184.2 9.5 %collective-permute-start.16 = (bf16[2,128,2048]{2,1,0:T(8,128)(2,1)}, bf16[2,128,2048]{2,1,0:T(8,128)(2,1)}, u32[]{:S(2)}, u32[]{:S(2)}) collective-permute-start(bf16[2,128,2048]{2,1,0:T(8,128)(2,1)} %collective-permute-done.15.refs_10_), channel_id=1, source_target_pairs={{0,1},{1,0},{2,3},{3,2},{4,5},{5,4},{6,7},{7,6},{8,9},{9,8},{10,11... | collective-permute-start | bytes 3145736 | tf_op jit(solution)/shard_map/ppermute | solution.py:413
  211.6 7.4 %collective-permute-start.18 = (bf16[2,128,256]{2,1,0:T(8,128)(2,1)}, bf16[2,128,256]{2,1,0:T(8,128)(2,1)S(1)}, u32[]{:S(2)}, u32[]{:S(2)}) collective-permute-start(bf16[2,128,256]{2,1,0:T(8,128)(2,1)} %get-tuple-element.123), channel_id=1, source_target_pairs={{1,0},{2,1},{3,2},{4,3},{5,4},{6,5},{7,6},{8,7},{9,8},{10,9},{11,1... | collective-permute-start | bytes 393224 | tf_op jit(solution)/shard_map/ppermute | solution.py:450
  (26 other events, 133.2 us)
Sparse Core Ops, SparseCore 0:
  10.2 23.0 all-gather.8
  45.4 40.2 all-gather.10
  87.2 27.2 all-gather.12
  130.9 52.2 all-gather.14

commit v16 on v15

--- a/solution.py
+++ b/solution.py
@@ -223,14 +223,14 @@
     plan, place_info, back_ref, place_ref, grad_ref, *refs
 ):
     heads, tiles = plan
-    mine, across, last, refs = refs[:6], refs[6:12], refs[12:14], refs[14:]
+    own, last, twin, refs = refs[:4], refs[4:8], refs[8:12], refs[12:]
     low_ref, turned_ref, q_ref, key_ref, value_ref, *refs = refs
     moe_ref, query_out, kept_out, sent_out, by_place, stream, held, sums = refs
     step = pl.program_id(0)
     tokens = query_out.shape[0]
     part_size = by_place.shape[2]
-    size = mine[0].shape[1]
-    mine, across = mine + last, across + last
+    size = own[0].shape[1]
+    mine, across = own[:2] + twin + last[:2], own[2:] + twin + last[2:]
     spread = part_size // size
     here, core = place_info[1], place_info[2]
 
@@ -314,7 +314,7 @@
     own_tile = lambda i: jnp.minimum(i, tiles - 1)
     other_tile = lambda i: jnp.minimum(jnp.maximum(i - tiles, 0), tiles - 1)
     now = lambda i: jnp.minimum(i, steps - 1)
-    last = pl.BlockSpec((spread, 1, size, tile), lambda i, info: (0, now(i) // tiles, 0, now(i) % tiles))
+    twin = pl.BlockSpec((spread, 1, size, tile), lambda i, info: (0, now(i) // tiles, 0, now(i) % tiles))
     piece = lambda turn: pl.BlockSpec((spread, size, tile), lambda i, info: (0, 0, turn(i)))
     kv = pl.BlockSpec((2, tokens, HD), lambda i, info: (0, 0, kv_group(i, info)))
     return pl.pallas_call(
@@ -323,9 +323,8 @@
             num_scalar_prefetch=1,
             grid=(steps + 1,),
             in_specs=[whole(back.shape), whole(place.shape), whole(moe_grad.shape)]
-            + [piece(own_tile)] * 6
-            + [piece(other_tile)] * 6
-            + [last] * 2
+            + ([piece(own_tile)] * 2 + [piece(other_tile)] * 2) * 2
+            + [twin] * 4
             + [
                 rows((heads * tokens, span)),
                 pl.BlockSpec(
@@ -423,29 +422,36 @@
     rows, w_near, w_far, own_line, prev = lax.optimization_barrier((rows, w_near, w_far, own_line, prev))
 
     rows_in = lax.all_to_all(rows.reshape(owners, depth, 2 * width), chips, 0, 0, tiled=True)
-    near_line, far_line = line(w_near), line(w_far)
+    near_crossed, far_crossed = cross(w_near), cross(w_far)
+    near_twin = line(jnp.stack([w_near, near_crossed]))
+    far_twin = line(jnp.stack([w_far, far_crossed]))
+    own_line, near_crossed, far_crossed = lax.optimization_barrier((own_line, near_crossed, far_crossed))
+    own_crossed = cross(own_line)
     w_last = lax.ppermute(w_far, "near", swap)
     prepared = prepare_weights(own, other)
     attention = attention_shares(queries, key_heads, value_heads, prev, segs)
-    near_line, prepared, attention = lax.optimization_barrier((near_line, prepared, attention))
-    crossed = [cross(own_line), cross(near_line)]
-    rows_in, prepared, attention, near_line, far_line, crossed, w_last = lax.optimization_barrier(
-        (rows_in, prepared, attention, near_line, far_line, crossed, w_last)
-    )
-    lines = [own_line, near_line, far_line]
-    last_crossed = cross(w_last)
+    rows_in, prepared, attention, own_line, own_crossed, w_last = lax.optimization_barrier(
+        (rows_in, prepared, attention, own_line, own_crossed, w_last)
+    )
+    if low == 2:
+        moved = lax.ppermute(w_last, "low", swap)
+        first = lax.axis_index("low") == 0
+        last_line = jnp.where(first, jnp.stack([w_last, moved]), jnp.stack([moved, w_last]))
+    else:
+        last_line = line(w_last)
     terms = experts(rows_in.reshape(owners * depth, 2 * width), *prepared)
-    terms, lines, crossed, last_crossed = lax.optimization_barrier((terms, lines, crossed, last_crossed))
-    last_line = line(jnp.stack([w_last, last_crossed]))
-    far_crossed = cross(lines[2])
+    terms, own_line, own_crossed, last_line, near_twin, far_twin = lax.optimization_barrier(
+        (terms, own_line, own_crossed, last_line, near_twin, far_twin)
+    )
+    last_crossed = cross(last_line)
     back = lax.all_to_all(terms.reshape(owners, depth, width), chips, 0, 0, tiled=True)
-    both = lambda pieces: [w for piece in pieces for w in (piece, other_core(piece))]
+    both = lambda *pieces: [w for piece in pieces for w in (piece, other_core(piece))]
 
     z = 2 * lax.axis_index("far") + lax.axis_index("near")
     moe_input_grad, query_grad, kept, sent = tail(
         jnp.stack([lax.axis_index("groups"), z, lax.axis_index("core")]).astype(jnp.int32),
         back.reshape(owners * depth, width), place, moe_grad,
-        both(lines) + both(crossed + [far_crossed]) + both([last_line]), *attention,
+        both(own_line, own_crossed, last_line, last_crossed, near_twin, far_twin), *attention,
     )
     return (moe_input_grad, query_grad, *finish(kept, lax.ppermute(sent, blk, backward)))
 

time: 230 us -> 225 us (0.978)
  waiting for transfers between devices: 114 us -> 105 us
  other arithmetic: 1.69 us -> 6.66 us
  starting transfers between devices: 34.6 us -> 31.7 us
    all_gather x4 -> x3, waiting for transfers between devices: 70.2 us -> 17.5 us  [local(): line = lambda w: lax.all_gather(w, 'low', axis=0, tiled=False)]
    ppermute x4, waiting for transfers between devices: 0.01 us -> 36 us  [local(): cross = lambda w: lax.ppermute(w, 'groups', swap)]
    all_to_all x1, waiting for transfers between devices: 0.01 us -> 7.2 us  [local(): lax.all_to_all(rows.reshape(owners, depth, 2 * width), chips, 0, 0, tiled...]
    ppermute x10 -> x9, waiting for transfers between devices: 8.5 us -> 2.46 us  [local(): other_core = lambda w: lax.ppermute(w, 'core', swap)]
    all_to_all x1, waiting for transfers between devices: 0.01 us -> 5.14 us  [local(): lax.all_to_all(terms.reshape(owners, depth, width), chips, 0, 0, tiled=True)]
    all_to_all x1, starting transfers between devices: 11.1 us -> 6.35 us  [local(): lax.all_to_all(terms.reshape(owners, depth, width), chips, 0, 0, tiled=True)]
    ppermute x0 -> x1, waiting for transfers between devices: none -> 3.6 us  [local(): moved = lax.ppermute(w_last, 'low', swap)]
    another operation x1 -> x2, other arithmetic: 1.06 us -> 4.28 us  [the longest x1 2.17 us: local(): far_twin = line(jnp.stack([w_far, far_crossed]))]
  transfers between devices with their start and end apart: 25 -> 24, of which waited for: 10 -> 12; matrix products, arithmetic and copies ran while one was open for 0% -> 3% of each run, Pallas kernels for 12% -> 12%
where the time goes in v16:
time: 225 us; the launch traced here: 221 us
  waiting for transfers between devices  105 us (47%)
  Pallas kernels  44.7 us (20%)
  starting transfers between devices  31.7 us (14%)
  local copies, waits for them, and re-layouts  19.1 us (8%)
  between operations  13.9 us (6%)
  other arithmetic  6.66 us (3%)
    ppermute x4, waiting for transfers between devices, local(): cross = lambda w: lax.ppermute(w, 'groups', swap)  36 us
    unnamed x50, local copies, waits for them, and re-layouts  18.2 us
    all_gather x3, waiting for transfers between devices, local(): line = lambda w: lax.all_gather(w, 'low', axis=0, tiled=False)  17.5 us
    pallas_call x1, Pallas kernels, tail(): pl.pallas_call(functools.partial(tail_kernel, (heads, tiles)), grid_spec=...  16.6 us
    ppermute x1, waiting for transfers between devices, local(): prev = lax.ppermute(jnp.concatenate([kv, seg_rows], axis=0), blk, onward)  15.4 us
    pallas_call x1, Pallas kernels, experts(): pl.pallas_call(functools.partial(expert_kernel, steps), grid=(steps + wid...  13 us
    ppermute x1, waiting for transfers between devices, local(): w_last = lax.ppermute(w_far, 'near', swap)  12.7 us
    pallas_call x1, Pallas kernels, prepare_weights(): pl.pallas_call(weights_kernel, grid=(steps,), in_specs=[cols, cols, down]...  8.79 us
  transfers between devices with their start and end apart: 24, of which 12 were waited for; matrix products, arithmetic and copies ran while one was open for 3% of the time, Pallas kernels for 12%

profile of v16, /device:TPU:13, one launch (start us, length us, event | category | flops | bytes accessed | tf_op | source)
XLA Modules:
  0.0 221.1 jit_solution(8521008735821628585)
XLA Ops:
  9.5 2.3 %collective-permute-start.1 = (bf16[128,2048]{1,0:T(8,128)(2,1)}, bf16[128,2048]{1,0:T(8,128)(2,1)}, u32[]{:S(2)}, u32[]{:S(2)}) collective-permute-start(bf16[128,2048]{1,0:T(8,128)(2,1)} %constant_dynamic-slice_fusion), channel_id=1, source_target_pairs={{0,8},{8,0},{1,9},{9,1},{2,10},{10,2},{3,11},{11,3},{4,12},{12,4},... | collective-permute-start | bytes 1572872 | tf_op jit(solution)/shard_map/ppermute | solution.py:407
  18.1 3.2 %collective-permute-start.2 = (bf16[144,512]{1,0:T(8,128)(2,1)S(1)}, bf16[144,512]{1,0:T(8,128)(2,1)S(1)}, u32[]{:S(2)}, u32[]{:S(2)}) collective-permute-start(bf16[144,512]{1,0:T(8,128)(2,1)S(1)} %fusion.1), channel_id=1, source_target_pairs={{0,1},{1,2},{2,3},{3,4},{4,5},{5,6},{6,7},{7,8},{8,9},{9,10},{10,1... | collective-permute-start | bytes 442376 | tf_op jit(solution)/shard_map/ppermute | solution.py:420
  21.3 15.4 %collective-permute-done.2.prev_key_ref.prev_value_ref.prev_seg_ref = bf16[144,512]{1,0:T(8,128)(2,1)S(1)} collective-permute-done((bf16[144,512]{1,0:T(8,128)(2,1)S(1)}, bf16[144,512]{1,0:T(8,128)(2,1)S(1)}, u32[]{:S(2)}, u32[]{:S(2)}) %collective-permute-start.2) | collective-permute-done | bytes 147488 | tf_op jit(solution)/shard_map/ppermute | solution.py:420
  37.5 3.6 %all-to-all-start = ((bf16[8,48,4096]{2,1,0:T(8,128)(2,1)}), bf16[8,48,4096]{2,1,0:T(8,128)(2,1)S(1)}, u32[]{:S(2)}, u32[]{:S(2)}) async-start(bf16[8,48,4096]{2,1,0:T(8,128)(2,1)} %bitcast.25), calls=%async_computation | async-start | bytes 6291456 | tf_op jit(solution)/shard_map/all_to_all | solution.py:424
  42.5 9.7 %collective-permute-done.6 = bf16[128,2048]{1,0:T(8,128)(2,1)S(1)} collective-permute-done((bf16[128,2048]{1,0:T(8,128)(2,1)}, bf16[128,2048]{1,0:T(8,128)(2,1)S(1)}, u32[]{:S(2)}, u32[]{:S(2)}) %collective-permute-start.6) | collective-permute-done | bytes 524320 | tf_op jit(solution)/shard_map/ppermute | solution.py:411
  52.1 2.1 pad_maximum_fusion
  55.6 3.9 %collective-permute-start.3 = (bf16[2048,384]{1,0:T(8,128)(2,1)}, bf16[2048,384]{1,0:T(8,128)(2,1)}, u32[]{:S(2)}, u32[]{:S(2)}) collective-permute-start(bf16[2048,384]{1,0:T(8,128)(2,1)} %refs_0_.1), channel_id=1, source_target_pairs={{0,1},{1,0},{2,3},{3,2},{4,5},{5,4},{6,7},{7,6},{8,9},{9,8},{10,11... | collective-permute-start | bytes 4718600 | tf_op jit(solution)/shard_map/ppermute | solution.py:412
  60.0 4.3 %collective-permute-done.7 = bf16[128,2048]{1,0:T(8,128)(2,1)S(1)} collective-permute-done((bf16[128,2048]{1,0:T(8,128)(2,1)}, bf16[128,2048]{1,0:T(8,128)(2,1)S(1)}, u32[]{:S(2)}, u32[]{:S(2)}) %collective-permute-start.7) | collective-permute-done | bytes 524320 | tf_op jit(solution)/shard_map/ppermute | solution.py:411
  64.3 2.2 pad_maximum_fusion.1
  69.4 3.5 %attention_shares.1 = (bf16[2,2048,256]{2,1,0:T(8,128)(2,1)S(1)}, bf16[2,256,2048]{2,1,0:T(8,128)(2,1)S(1)}, bf16[2,2048,128]{2,1,0:T(8,128)(2,1)S(1)}, bf16[2,2...) custom-call(bf16[128,4096]{1,0:T(8,128)(2,1)S(1)} %copy-done.8, bf16[128,256]{1,0:T(8,128)(2,1)S(1)} %copy-done.11, ...), custom_call_target="tpu_custom_call" | custom-call | tf_op jit(solution)/shard_map/attention_shares/pallas_call | solution.py:201
  80.8 8.8 %prepare_weights.1 = (bf16[3,2048,512]{2,1,0:T(8,128)(2,1)}, bf16[3,2048,256]{2,1,0:T(8,128)(2,1)}, bf16[3,512,2048]{2,1,0:T(8,128)(2,1)}) custom-call(bf16[2048,384]{1,0:T(8,128)(2,1)S(1)} %copy-done.5, bf16[2048,384]{1,0:T(8,128)(2,1)S(1)} %copy-done.6, bf16[384,2048]{1,0:T(8,128)(2,1)S(1)} %copy-done.7, bf16[2048,384]{1,0:T(8,128)(2,1)} %collective-permute-done.3.refs_3_, ...), custom_call_target="tpu_custom_call" | custom-call | tf_op jit(solution)/shard_map/prepare_weights/pallas_call | solution.py:94
  89.6 12.7 %collective-permute-done.9 = bf16[128,2048]{1,0:T(8,128)(2,1)} collective-permute-done((bf16[128,2048]{1,0:T(8,128)(2,1)}, bf16[128,2048]{1,0:T(8,128)(2,1)}, u32[]{:S(2)}, u32[]{:S(2)}) %collective-permute-start.9) | collective-permute-done | bytes 524320 | tf_op jit(solution)/shard_map/ppermute | solution.py:430
  102.2 7.2 %all-to-all-done = bf16[8,48,4096]{2,1,0:T(8,128)(2,1)S(1)} async-done(((bf16[8,48,4096]{2,1,0:T(8,128)(2,1)}), bf16[8,48,4096]{2,1,0:T(8,128)(2,1)S(1)}, u32[]{:S(2)}, u32[]{:S(2)}) %all-to-all-start) | async-done | bytes 3145760 | tf_op jit(solution)/shard_map/all_to_all | solution.py:424
  110.4 13.0 %expert_terms.1 = bf16[384,2048]{1,0:T(8,128)(2,1)} custom-call(bf16[384,4096]{1,0:T(8,128)(2,1)S(1)} %bitcast.24, bf16[3,2048,512]{2,1,0:T(8,128)(2,1)} %get-tuple-element.80.cols_ref, bf16[3,2048,256]{2,1,0:T(8,128)(2,1)} %get-tuple-element.81.down_ref, bf16[3,512,2048]{2,1,0:T(8,128)(2,1)} %get-tuple-element.82.back_ref), custom_call_target="tpu_custom_call" | custom-call | tf_op jit(solution)/shard_map/expert_terms/pallas_call | solution.py:145
  123.4 3.6 %collective-permute-done.10 = bf16[128,2048]{1,0:T(8,128)(2,1)} collective-permute-done((bf16[128,2048]{1,0:T(8,128)(2,1)}, bf16[128,2048]{1,0:T(8,128)(2,1)}, u32[]{:S(2)}, u32[]{:S(2)}) %collective-permute-start.10) | collective-permute-done | bytes 524320 | tf_op jit(solution)/shard_map/ppermute | solution.py:437
  127.0 1.7 maximum_select_fusion.refs_4_
  128.7 17.5 %all-gather.11.cloned.1.call-done = bf16[4,128,2048]{2,1,0:T(8,128)(2,1)} async-done(((bf16[2,128,2048]{2,1,0:T(8,128)(2,1)}), bf16[4,128,2048]{2,1,0:T(8,128)(2,1)}) %all-gather.11.cloned.1.call-update) | async-done | bytes 2097168 | tf_op jit(solution)/shard_map/all_gather | solution.py:410
  146.2 6.3 %all-to-all-start.1 = ((bf16[8,48,2048]{2,1,0:T(8,128)(2,1)}), bf16[8,48,2048]{2,1,0:T(8,128)(2,1)S(1)}, u32[]{:S(2)}, u32[]{:S(2)}) async-start(bf16[8,48,2048]{2,1,0:T(8,128)(2,1)} %bitcast.19), calls=%async_computation.1 | async-start | bytes 3145728 | tf_op jit(solution)/shard_map/all_to_all | solution.py:447
  156.5 22.0 %collective-permute-done.14.refs_6_ = bf16[2,128,2048]{2,1,0:T(8,128)(2,1)} collective-permute-done((bf16[2,128,2048]{2,1,0:T(8,128)(2,1)S(1)}, bf16[2,128,2048]{2,1,0:T(8,128)(2,1)}, u32[]{:S(2)}, u32[]{:S(2)}) %collective-permute-start.14) | collective-permute-done | bytes 1048608 | tf_op jit(solution)/shard_map/ppermute | solution.py:411
  180.0 2.0 collective-permute-done.15.refs_7_
  181.9 5.1 %all-to-all-done.1 = bf16[8,48,2048]{2,1,0:T(8,128)(2,1)S(1)} async-done(((bf16[8,48,2048]{2,1,0:T(8,128)(2,1)}), bf16[8,48,2048]{2,1,0:T(8,128)(2,1)S(1)}, u32[]{:S(2)}, u32[]{:S(2)}) %all-to-all-start.1) | async-done | bytes 1572896 | tf_op jit(solution)/shard_map/all_to_all | solution.py:447
  188.3 16.6 %tail_attention.1 = (bf16[128,2048]{1,0:T(8,128)(2,1)}, bf16[128,4096]{1,0:T(8,128)(2,1)}, f32[2,128,256]{2,1,0:T(8,128)}, bf16[2,128,256]{2,1,0:T(8,128)(2,1)}) custom-call(s32[3]{0:T(128)} %pad_add_fusion.place_info, bf16[384,2048]{1,0:T(8,128)(2,1)} %bitcast.28, bf16[128,384]{1,0:T(8,128)(2,1)} %copy-done.15, bf16[128,2048]{1,0:T(8,128)(2,1)} %grad_ref.3, ...), custom_call_target="tpu_custom_call" | custom-call | flops 2147483648 | bytes 23068672 | tf_op jit(solution)/shard_map/tail_attention/pallas_call | solution.py:320
  204.9 2.4 %collective-permute-start.18 = (bf16[2,128,256]{2,1,0:T(8,128)(2,1)}, bf16[2,128,256]{2,1,0:T(8,128)(2,1)S(1)}, u32[]{:S(2)}, u32[]{:S(2)}) collective-permute-start(bf16[2,128,256]{2,1,0:T(8,128)(2,1)} %get-tuple-element.101), channel_id=1, source_target_pairs={{1,0},{2,1},{3,2},{4,3},{5,4},{6,5},{7,6},{8,7},{9,8},{10,9},{11,1... | collective-permute-start | bytes 393224 | tf_op jit(solution)/shard_map/ppermute | solution.py:456
  207.3 5.0 %collective-permute-done.18.later_ref = bf16[2,128,256]{2,1,0:T(8,128)(2,1)S(1)} collective-permute-done((bf16[2,128,256]{2,1,0:T(8,128)(2,1)}, bf16[2,128,256]{2,1,0:T(8,128)(2,1)S(1)}, u32[]{:S(2)}, u32[]{:S(2)}) %collective-permute-start.18) | collective-permute-done | bytes 131104 | tf_op jit(solution)/shard_map/ppermute | solution.py:456
  (91 shorter events, 33.1 us)
Async XLA Ops:
  7.2 30.3 %all-gather.7.cloned.1.call-start = ((), (), s32[]{:S(2)}) async-start(), calls=%async_computation.2 | async-start | bytes 1572864 | tf_op jit(solution)/shard_map/all_gather | solution.py:410
  9.3 27.4 %collective-permute-start = (bf16[128,2048]{1,0:T(8,128)(2,1)}, bf16[128,2048]{1,0:T(8,128)(2,1)S(1)}, u32[]{:S(2)}, u32[]{:S(2)}) collective-permute-start(bf16[128,2048]{1,0:T(8,128)(2,1)} %constant_dynamic-slice_fusion), channel_id=1, source_target_pairs={{0,4},{4,0},{1,5},{5,1},{2,6},{6,2},{3,7},{7,3},{8,12},{12,8},{9,1... | collective-permute-start | bytes 1572872 | tf_op jit(solution)/shard_map/ppermute | solution.py:406
  9.5 28.0 %collective-permute-start.1 = (bf16[128,2048]{1,0:T(8,128)(2,1)}, bf16[128,2048]{1,0:T(8,128)(2,1)}, u32[]{:S(2)}, u32[]{:S(2)}) collective-permute-start(bf16[128,2048]{1,0:T(8,128)(2,1)} %constant_dynamic-slice_fusion), channel_id=1, source_target_pairs={{0,8},{8,0},{1,9},{9,1},{2,10},{10,2},{3,11},{11,3},{4,12},{12,4},... | collective-permute-start | bytes 1572872 | tf_op jit(solution)/shard_map/ppermute | solution.py:407
  18.1 18.6 %collective-permute-start.2 = (bf16[144,512]{1,0:T(8,128)(2,1)S(1)}, bf16[144,512]{1,0:T(8,128)(2,1)S(1)}, u32[]{:S(2)}, u32[]{:S(2)}) collective-permute-start(bf16[144,512]{1,0:T(8,128)(2,1)S(1)} %fusion.1), channel_id=1, source_target_pairs={{0,1},{1,2},{2,3},{3,4},{4,5},{5,6},{6,7},{7,8},{8,9},{9,10},{10,1... | collective-permute-start | bytes 442376 | tf_op jit(solution)/shard_map/ppermute | solution.py:420
  37.5 71.9 %all-to-all-start = ((bf16[8,48,4096]{2,1,0:T(8,128)(2,1)}), bf16[8,48,4096]{2,1,0:T(8,128)(2,1)S(1)}, u32[]{:S(2)}, u32[]{:S(2)}) async-start(bf16[8,48,4096]{2,1,0:T(8,128)(2,1)} %bitcast.25), calls=%async_computation | async-start | bytes 6291456 | tf_op jit(solution)/shard_map/all_to_all | solution.py:424
  41.2 87.6 %all-gather.9.cloned.1.call-start = ((), (), s32[]{:S(2)}) async-start(), calls=%async_computation.3 | async-start | bytes 3145728 | tf_op jit(solution)/shard_map/all_gather | solution.py:410
  41.2 10.9 %collective-permute-start.6 = (bf16[128,2048]{1,0:T(8,128)(2,1)}, bf16[128,2048]{1,0:T(8,128)(2,1)S(1)}, u32[]{:S(2)}, u32[]{:S(2)}) collective-permute-start(bf16[128,2048]{1,0:T(8,128)(2,1)} %copy-done.22), channel_id=1, source_target_pairs={{0,16},{16,0},{1,17},{17,1},{2,18},{18,2},{3,19},{19,3},{4,20},{20... | collective-permute-start | bytes 1572872 | tf_op jit(solution)/shard_map/ppermute | solution.py:411
  54.3 92.0 %all-gather.11.cloned.1.call-start = ((), (), s32[]{:S(2)}) async-start(), calls=%async_computation.4 | async-start | bytes 3145728 | tf_op jit(solution)/shard_map/all_gather | solution.py:410
  54.3 10.0 %collective-permute-start.7 = (bf16[128,2048]{1,0:T(8,128)(2,1)}, bf16[128,2048]{1,0:T(8,128)(2,1)S(1)}, u32[]{:S(2)}, u32[]{:S(2)}) collective-permute-start(bf16[128,2048]{1,0:T(8,128)(2,1)} %collective-permute-done.1), channel_id=1, source_target_pairs={{0,16},{16,0},{1,17},{17,1},{2,18},{18,2},{3,19},{19,3},{4,20},{20... | collective-permute-start | bytes 1572872 | tf_op jit(solution)/shard_map/ppermute | solution.py:411
  55.6 22.3 %collective-permute-start.3 = (bf16[2048,384]{1,0:T(8,128)(2,1)}, bf16[2048,384]{1,0:T(8,128)(2,1)}, u32[]{:S(2)}, u32[]{:S(2)}) collective-permute-start(bf16[2048,384]{1,0:T(8,128)(2,1)} %refs_0_.1), channel_id=1, source_target_pairs={{0,1},{1,0},{2,3},{3,2},{4,5},{5,4},{6,7},{7,6},{8,9},{9,8},{10,11... | collective-permute-start | bytes 4718600 | tf_op jit(solution)/shard_map/ppermute | solution.py:412
  59.5 18.4 %collective-permute-start.4 = (bf16[2048,384]{1,0:T(8,128)(2,1)}, bf16[2048,384]{1,0:T(8,128)(2,1)}, u32[]{:S(2)}, u32[]{:S(2)}) collective-permute-start(bf16[2048,384]{1,0:T(8,128)(2,1)} %refs_1_.1), channel_id=1, source_target_pairs={{0,1},{1,0},{2,3},{3,2},{4,5},{5,4},{6,7},{7,6},{8,9},{9,8},{10,11... | collective-permute-start | bytes 4718600 | tf_op jit(solution)/shard_map/ppermute | solution.py:412
  59.5 18.4 %collective-permute-start.5 = (bf16[384,2048]{1,0:T(8,128)(2,1)}, bf16[384,2048]{1,0:T(8,128)(2,1)}, u32[]{:S(2)}, u32[]{:S(2)}) collective-permute-start(bf16[384,2048]{1,0:T(8,128)(2,1)} %refs_2_.1), channel_id=1, source_target_pairs={{0,1},{1,0},{2,3},{3,2},{4,5},{5,4},{6,7},{7,6},{8,9},{9,8},{10,11... | collective-permute-start | bytes 4718600 | tf_op jit(solution)/shard_map/ppermute | solution.py:412
  66.5 35.7 %collective-permute-start.8 = (bf16[2,128,2048]{2,1,0:T(8,128)(2,1)}, bf16[2,128,2048]{2,1,0:T(8,128)(2,1)}, u32[]{:S(2)}, u32[]{:S(2)}) collective-permute-start(bf16[2,128,2048]{2,1,0:T(8,128)(2,1)} %bitcast.33), channel_id=1, source_target_pairs={{0,16},{16,0},{1,17},{17,1},{2,18},{18,2},{3,19},{19,3},{4,20},{20... | collective-permute-start | bytes 3145736 | tf_op jit(solution)/shard_map/ppermute | solution.py:411
  67.8 34.4 %collective-permute-start.9 = (bf16[128,2048]{1,0:T(8,128)(2,1)}, bf16[128,2048]{1,0:T(8,128)(2,1)}, u32[]{:S(2)}, u32[]{:S(2)}) collective-permute-start(bf16[128,2048]{1,0:T(8,128)(2,1)} %collective-permute-done.1), channel_id=1, source_target_pairs={{0,4},{4,0},{1,5},{5,1},{2,6},{6,2},{3,7},{7,3},{8,12},{12,8},{9,1... | collective-permute-start | bytes 1572872 | tf_op jit(solution)/shard_map/ppermute | solution.py:430
  109.4 17.6 %collective-permute-start.10 = (bf16[128,2048]{1,0:T(8,128)(2,1)}, bf16[128,2048]{1,0:T(8,128)(2,1)}, u32[]{:S(2)}, u32[]{:S(2)}) collective-permute-start(bf16[128,2048]{1,0:T(8,128)(2,1)} %collective-permute-done.9), channel_id=1, source_target_pairs={{0,2},{2,0},{1,3},{3,1},{4,6},{6,4},{5,7},{7,5},{8,10},{10,8},{9,1... | collective-permute-start | bytes 1572872 | tf_op jit(solution)/shard_map/ppermute | solution.py:437
  146.2 40.8 %all-to-all-start.1 = ((bf16[8,48,2048]{2,1,0:T(8,128)(2,1)}), bf16[8,48,2048]{2,1,0:T(8,128)(2,1)S(1)}, u32[]{:S(2)}, u32[]{:S(2)}) async-start(bf16[8,48,2048]{2,1,0:T(8,128)(2,1)} %bitcast.19), calls=%async_computation.1 | async-start | bytes 3145728 | tf_op jit(solution)/shard_map/all_to_all | solution.py:447
  152.6 3.5 %collective-permute-start.11 = (bf16[2,128,2048]{2,1,0:T(8,128)(2,1)}, bf16[2,128,2048]{2,1,0:T(8,128)(2,1)S(1)}, u32[]{:S(2)}, u32[]{:S(2)}) collective-permute-start(bf16[2,128,2048]{2,1,0:T(8,128)(2,1)} %bitcast.34), channel_id=1, source_target_pairs={{0,1},{1,0},{2,3},{3,2},{4,5},{5,4},{6,7},{7,6},{8,9},{9,8},{10,11... | collective-permute-start | bytes 3145736 | tf_op jit(solution)/shard_map/ppermute | solution.py:412
  153.6 24.9 %collective-permute-start.14 = (bf16[2,128,2048]{2,1,0:T(8,128)(2,1)S(1)}, bf16[2,128,2048]{2,1,0:T(8,128)(2,1)}, u32[]{:S(2)}, u32[]{:S(2)}) collective-permute-start(bf16[2,128,2048]{2,1,0:T(8,128)(2,1)S(1)} %maximum_select_fusion.refs_4_), channel_id=1, source_target_pairs={{0,16},{16,0},{1,17},{17,1},{2,18},{18,2},{3,19},{19,3},{4,20},{20... | collective-permute-start | bytes 3145736 | tf_op jit(solution)/shard_map/ppermute | solution.py:411
  154.8 27.1 %collective-permute-start.16 = (bf16[2,2,128,2048]{3,2,1,0:T(8,128)(2,1)}, bf16[2,2,128,2048]{3,2,1,0:T(8,128)(2,1)}, u32[]{:S(2)}, u32[]{:S(2)}) collective-permute-start(bf16[2,2,128,2048]{3,2,1,0:T(8,128)(2,1)} %bitcast.29), channel_id=1, source_target_pairs={{0,1},{1,0},{2,3},{3,2},{4,5},{5,4},{6,7},{7,6},{8,9},{9,8},{10,11... | collective-permute-start | bytes 6291464 | tf_op jit(solution)/shard_map/ppermute | solution.py:412
  155.1 26.8 %collective-permute-start.17 = (bf16[2,2,128,2048]{3,2,1,0:T(8,128)(2,1)}, bf16[2,2,128,2048]{3,2,1,0:T(8,128)(2,1)}, u32[]{:S(2)}, u32[]{:S(2)}) collective-permute-start(bf16[2,2,128,2048]{3,2,1,0:T(8,128)(2,1)} %bitcast.31), channel_id=1, source_target_pairs={{0,1},{1,0},{2,3},{3,2},{4,5},{5,4},{6,7},{7,6},{8,9},{9,8},{10,11... | collective-permute-start | bytes 6291464 | tf_op jit(solution)/shard_map/ppermute | solution.py:412
  155.3 24.6 %collective-permute-start.13 = (bf16[2,128,2048]{2,1,0:T(8,128)(2,1)S(1)}, bf16[2,128,2048]{2,1,0:T(8,128)(2,1)}, u32[]{:S(2)}, u32[]{:S(2)}) collective-permute-start(bf16[2,128,2048]{2,1,0:T(8,128)(2,1)S(1)} %maximum_select_fusion.refs_4_), channel_id=1, source_target_pairs={{0,1},{1,0},{2,3},{3,2},{4,5},{5,4},{6,7},{7,6},{8,9},{9,8},{10,11... | collective-permute-start | bytes 3145736 | tf_op jit(solution)/shard_map/ppermute | solution.py:412
  156.1 23.9 %collective-permute-start.12 = (bf16[2,128,2048]{2,1,0:T(8,128)(2,1)}, bf16[2,128,2048]{2,1,0:T(8,128)(2,1)}, u32[]{:S(2)}, u32[]{:S(2)}) collective-permute-start(bf16[2,128,2048]{2,1,0:T(8,128)(2,1)} %collective-permute-done.8.refs_2_), channel_id=1, source_target_pairs={{0,1},{1,0},{2,3},{3,2},{4,5},{5,4},{6,7},{7,6},{8,9},{9,8},{10,11... | collective-permute-start | bytes 3145736 | tf_op jit(solution)/shard_map/ppermute | solution.py:412
  178.5 3.4 %collective-permute-start.15 = (bf16[2,128,2048]{2,1,0:T(8,128)(2,1)}, bf16[2,128,2048]{2,1,0:T(8,128)(2,1)}, u32[]{:S(2)}, u32[]{:S(2)}) collective-permute-start(bf16[2,128,2048]{2,1,0:T(8,128)(2,1)} %collective-permute-done.14.refs_6_), channel_id=1, source_target_pairs={{0,1},{1,0},{2,3},{3,2},{4,5},{5,4},{6,7},{7,6},{8,9},{9,8},{10,11... | collective-permute-start | bytes 3145736 | tf_op jit(solution)/shard_map/ppermute | solution.py:412
  204.9 7.4 %collective-permute-start.18 = (bf16[2,128,256]{2,1,0:T(8,128)(2,1)}, bf16[2,128,256]{2,1,0:T(8,128)(2,1)S(1)}, u32[]{:S(2)}, u32[]{:S(2)}) collective-permute-start(bf16[2,128,256]{2,1,0:T(8,128)(2,1)} %get-tuple-element.101), channel_id=1, source_target_pairs={{1,0},{2,1},{3,2},{4,3},{5,4},{6,5},{7,6},{8,7},{9,8},{10,9},{11,1... | collective-permute-start | bytes 393224 | tf_op jit(solution)/shard_map/ppermute | solution.py:456
  (25 other events, 186.6 us)
Sparse Core Ops, SparseCore 0:
  10.2 23.0 all-gather.6
  54.4 51.7 all-gather.8
  107.7 38.5 all-gather.10

commit v17 on v16

--- a/solution.py
+++ b/solution.py
@@ -223,14 +223,13 @@
     plan, place_info, back_ref, place_ref, grad_ref, *refs
 ):
     heads, tiles = plan
-    own, last, twin, refs = refs[:4], refs[4:8], refs[8:12], refs[12:]
+    mine, across, refs = refs[:8], refs[8:16], refs[16:]
     low_ref, turned_ref, q_ref, key_ref, value_ref, *refs = refs
     moe_ref, query_out, kept_out, sent_out, by_place, stream, held, sums = refs
     step = pl.program_id(0)
     tokens = query_out.shape[0]
     part_size = by_place.shape[2]
-    size = own[0].shape[1]
-    mine, across = own[:2] + twin + last[:2], own[2:] + twin + last[2:]
+    size = mine[0].shape[1]
     spread = part_size // size
     here, core = place_info[1], place_info[2]
 
@@ -313,9 +312,13 @@
     rows = lambda shape: pl.BlockSpec((1,) + shape, lambda i, info: (kv_group(i, info), was(i) % tiles, 0))
     own_tile = lambda i: jnp.minimum(i, tiles - 1)
     other_tile = lambda i: jnp.minimum(jnp.maximum(i - tiles, 0), tiles - 1)
-    now = lambda i: jnp.minimum(i, steps - 1)
-    twin = pl.BlockSpec((spread, 1, size, tile), lambda i, info: (0, now(i) // tiles, 0, now(i) % tiles))
-    piece = lambda turn: pl.BlockSpec((spread, size, tile), lambda i, info: (0, 0, turn(i)))
+    single = lambda turn: pl.BlockSpec((spread, size, tile), lambda i, info: (0, 0, turn(i)))
+    paired = lambda turn, which: pl.BlockSpec(
+        (spread, 1, size, tile), lambda i, info: (0, which, 0, turn(i))
+    )
+    pieces_of = lambda turn: (
+        [single(turn)] * 2 + [paired(turn, 0)] * 2 + [paired(turn, 1)] * 2 + [single(turn)] * 2
+    )
     kv = pl.BlockSpec((2, tokens, HD), lambda i, info: (0, 0, kv_group(i, info)))
     return pl.pallas_call(
         functools.partial(tail_kernel, (heads, tiles)),
@@ -323,8 +326,7 @@
             num_scalar_prefetch=1,
             grid=(steps + 1,),
             in_specs=[whole(back.shape), whole(place.shape), whole(moe_grad.shape)]
-            + ([piece(own_tile)] * 2 + [piece(other_tile)] * 2) * 2
-            + [twin] * 4
+            + [spec for turn in (own_tile, other_tile) for spec in pieces_of(turn)]
             + [
                 rows((heads * tokens, span)),
                 pl.BlockSpec(
@@ -422,14 +424,12 @@
     rows, w_near, w_far, own_line, prev = lax.optimization_barrier((rows, w_near, w_far, own_line, prev))
 
     rows_in = lax.all_to_all(rows.reshape(owners, depth, 2 * width), chips, 0, 0, tiled=True)
-    near_crossed, far_crossed = cross(w_near), cross(w_far)
-    near_twin = line(jnp.stack([w_near, near_crossed]))
-    far_twin = line(jnp.stack([w_far, far_crossed]))
-    own_line, near_crossed, far_crossed = lax.optimization_barrier((own_line, near_crossed, far_crossed))
-    own_crossed = cross(own_line)
+    pair_line = line(jnp.stack([w_near, w_far]))
     w_last = lax.ppermute(w_far, "near", swap)
     prepared = prepare_weights(own, other)
     attention = attention_shares(queries, key_heads, value_heads, prev, segs)
+    pair_line, prepared, attention = lax.optimization_barrier((pair_line, prepared, attention))
+    own_crossed, pair_crossed = cross(own_line), cross(pair_line)
     rows_in, prepared, attention, own_line, own_crossed, w_last = lax.optimization_barrier(
         (rows_in, prepared, attention, own_line, own_crossed, w_last)
     )
@@ -440,18 +440,21 @@
     else:
         last_line = line(w_last)
     terms = experts(rows_in.reshape(owners * depth, 2 * width), *prepared)
-    terms, own_line, own_crossed, last_line, near_twin, far_twin = lax.optimization_barrier(
-        (terms, own_line, own_crossed, last_line, near_twin, far_twin)
+    terms, own_line, own_crossed, last_line, pair_line, pair_crossed = lax.optimization_barrier(
+        (terms, own_line, own_crossed, last_line, pair_line, pair_crossed)
     )
     last_crossed = cross(last_line)
     back = lax.all_to_all(terms.reshape(owners, depth, width), chips, 0, 0, tiled=True)
-    both = lambda *pieces: [w for piece in pieces for w in (piece, other_core(piece))]
+
+    def pieces(own_piece, pair_piece, last_piece):
+        pairs = [(piece, other_core(piece)) for piece in (own_piece, pair_piece, last_piece)]
+        return [*pairs[0], *pairs[1], *pairs[1], *pairs[2]]
 
     z = 2 * lax.axis_index("far") + lax.axis_index("near")
     moe_input_grad, query_grad, kept, sent = tail(
         jnp.stack([lax.axis_index("groups"), z, lax.axis_index("core")]).astype(jnp.int32),
         back.reshape(owners * depth, width), place, moe_grad,
-        both(own_line, own_crossed, last_line, last_crossed, near_twin, far_twin), *attention,
+        pieces(own_line, pair_line, last_line) + pieces(own_crossed, pair_crossed, last_crossed), *attention,
     )
     return (moe_input_grad, query_grad, *finish(kept, lax.ppermute(sent, blk, backward)))
 

time: 225 us -> 266 us (1.18)
  waiting for transfers between devices: 105 us -> 149 us
  local copies, waits for them, and re-layouts: 19.1 us -> 16.4 us
    ppermute x4 -> x3, waiting for transfers between devices: 36 us -> 71 us  [local(): cross = lambda w: lax.ppermute(w, 'groups', swap)]
    all_gather x3 -> x2, waiting for transfers between devices: 17.5 us -> 32.1 us  [local(): line = lambda w: lax.all_gather(w, 'low', axis=0, tiled=False)]
    all_to_all x1, waiting for transfers between devices: 7.2 us -> 0.01 us  [local(): lax.all_to_all(rows.reshape(owners, depth, 2 * width), chips, 0, 0, tiled...]
    ppermute x1, waiting for transfers between devices: 12.7 us -> 19.1 us  [local(): w_last = lax.ppermute(w_far, 'near', swap)]
    all_to_all x1, starting transfers between devices: 6.35 us -> 10.7 us  [local(): lax.all_to_all(terms.reshape(owners, depth, width), chips, 0, 0, tiled=True)]
    ppermute x1, waiting for transfers between devices: 3.6 us -> 0.01 us  [local(): moved = lax.ppermute(w_last, 'low', swap)]
    unnamed x50 -> x44, local copies, waits for them, and re-layouts: 18.2 us -> 15.5 us
  transfers between devices with their start and end apart: 24 -> 22, of which waited for: 12 -> 9; matrix products, arithmetic and copies ran while one was open for 3% -> 2% of each run, Pallas kernels for 12% -> 10%
where the time goes in v17:
time: 266 us; the launch traced here: 262 us
  waiting for transfers between devices  149 us (56%)
  Pallas kernels  45.8 us (17%)
  starting transfers between devices  32.7 us (12%)
  local copies, waits for them, and re-layouts  16.4 us (6%)
  between operations  14.3 us (5%)
  other arithmetic  4.02 us (2%)
    ppermute x3, waiting for transfers between devices, local(): cross = lambda w: lax.ppermute(w, 'groups', swap)  71 us
    all_gather x2, waiting for transfers between devices, local(): line = lambda w: lax.all_gather(w, 'low', axis=0, tiled=False)  32.1 us
    ppermute x1, waiting for transfers between devices, local(): w_last = lax.ppermute(w_far, 'near', swap)  19.1 us
    pallas_call x1, Pallas kernels, tail(): pl.pallas_call(functools.partial(tail_kernel, (heads, tiles)), grid_spec=...  16.7 us
    unnamed x44, local copies, waits for them, and re-layouts  15.5 us
    ppermute x1, waiting for transfers between devices, local(): prev = lax.ppermute(jnp.concatenate([kv, seg_rows], axis=0), blk, onward)  15.5 us
    pallas_call x1, Pallas kernels, experts(): pl.pallas_call(functools.partial(expert_kernel, steps), grid=(steps + wid...  13.9 us
    all_to_all x1, starting transfers between devices, local(): lax.all_to_all(terms.reshape(owners, depth, width), chips, 0, 0, tiled=True)  10.7 us
  transfers between devices with their start and end apart: 22, of which 9 were waited for; matrix products, arithmetic and copies ran while one was open for 2% of the time, Pallas kernels for 10%

profile of v17, /device:TPU:13, one launch (start us, length us, event | category | flops | bytes accessed | tf_op | source)
XLA Modules:
  0.0 262.2 jit_solution(14315205437930797379)
XLA Ops:
  9.5 2.3 collective-permute-start.1
  16.4 1.6 copy-done.1
  18.1 3.1 %collective-permute-start.2 = (bf16[144,512]{1,0:T(8,128)(2,1)S(1)}, bf16[144,512]{1,0:T(8,128)(2,1)S(1)}, u32[]{:S(2)}, u32[]{:S(2)}) collective-permute-start(bf16[144,512]{1,0:T(8,128)(2,1)S(1)} %fusion.1), channel_id=1, source_target_pairs={{0,1},{1,2},{2,3},{3,4},{4,5},{5,6},{6,7},{7,8},{8,9},{9,10},{10,1... | collective-permute-start | bytes 442376 | tf_op jit(solution)/shard_map/ppermute | solution.py:422
  21.3 15.5 %collective-permute-done.2.prev_key_ref.prev_value_ref.prev_seg_ref = bf16[144,512]{1,0:T(8,128)(2,1)S(1)} collective-permute-done((bf16[144,512]{1,0:T(8,128)(2,1)S(1)}, bf16[144,512]{1,0:T(8,128)(2,1)S(1)}, u32[]{:S(2)}, u32[]{:S(2)}) %collective-permute-start.2) | collective-permute-done | bytes 147488 | tf_op jit(solution)/shard_map/ppermute | solution.py:422
  37.5 4.4 %all-to-all-start = ((bf16[8,48,4096]{2,1,0:T(8,128)(2,1)}), bf16[8,48,4096]{2,1,0:T(8,128)(2,1)}, u32[]{:S(2)}, u32[]{:S(2)}) async-start(bf16[8,48,4096]{2,1,0:T(8,128)(2,1)} %bitcast.21), calls=%async_computation | async-start | bytes 6291456 | tf_op jit(solution)/shard_map/all_to_all | solution.py:426
  42.0 2.2 pad_maximum_fusion
  44.2 2.1 collective-permute-start.3
  48.3 3.5 %attention_shares.1 = (bf16[2,2048,256]{2,1,0:T(8,128)(2,1)S(1)}, bf16[2,256,2048]{2,1,0:T(8,128)(2,1)S(1)}, bf16[2,2048,128]{2,1,0:T(8,128)(2,1)S(1)}, bf16[2,2...) custom-call(bf16[128,4096]{1,0:T(8,128)(2,1)S(1)} %copy-done.8, bf16[128,256]{1,0:T(8,128)(2,1)S(1)} %copy-done.10, ...), custom_call_target="tpu_custom_call" | custom-call | tf_op jit(solution)/shard_map/attention_shares/pallas_call | solution.py:201
  51.8 1.4 copy-done.2
  56.8 1.5 copy-done.6
  58.3 8.8 %prepare_weights.1 = (bf16[3,2048,512]{2,1,0:T(8,128)(2,1)}, bf16[3,2048,256]{2,1,0:T(8,128)(2,1)}, bf16[3,512,2048]{2,1,0:T(8,128)(2,1)}) custom-call(bf16[2048,384]{1,0:T(8,128)(2,1)S(1)} %copy-done.4, bf16[2048,384]{1,0:T(8,128)(2,1)S(1)} %copy-done.5, bf16[384,2048]{1,0:T(8,128)(2,1)S(1)} %copy-done.6, bf16[2048,384]{1,0:T(8,128)(2,1)} %collective-permute-done.3.refs_3_, ...), custom_call_target="tpu_custom_call" | custom-call | tf_op jit(solution)/shard_map/prepare_weights/pallas_call | solution.py:94
  67.1 32.1 %all-gather.7.cloned.1.call-done = bf16[4,128,2048]{2,1,0:T(8,128)(2,1)} async-done(((bf16[2,128,2048]{2,1,0:T(8,128)(2,1)}), bf16[4,128,2048]{2,1,0:T(8,128)(2,1)}) %all-gather.7.cloned.1.call-update) | async-done | bytes 2097168 | tf_op jit(solution)/shard_map/all_gather | solution.py:412
  100.9 19.1 %collective-permute-done.7 = bf16[128,2048]{1,0:T(8,128)(2,1)S(1)} collective-permute-done((bf16[128,2048]{1,0:T(8,128)(2,1)S(1)}, bf16[128,2048]{1,0:T(8,128)(2,1)S(1)}, u32[]{:S(2)}, u32[]{:S(2)}) %collective-permute-start.7) | collective-permute-done | bytes 524320 | tf_op jit(solution)/shard_map/ppermute | solution.py:428
  119.9 48.9 %collective-permute-done.6.refs_8_ = bf16[2,128,2048]{2,1,0:T(8,128)(2,1)} collective-permute-done((bf16[2,128,2048]{2,1,0:T(8,128)(2,1)}, bf16[2,128,2048]{2,1,0:T(8,128)(2,1)}, u32[]{:S(2)}, u32[]{:S(2)}) %collective-permute-start.6) | collective-permute-done | bytes 1048608 | tf_op jit(solution)/shard_map/ppermute | solution.py:413
  168.8 13.9 %expert_terms.1 = bf16[384,2048]{1,0:T(8,128)(2,1)} custom-call(bf16[384,4096]{1,0:T(8,128)(2,1)} %bitcast.13.rows_ref, bf16[3,2048,512]{2,1,0:T(8,128)(2,1)} %get-tuple-element.95.cols_ref, bf16[3,2048,256]{2,1,0:T(8,128)(2,1)} %get-tuple-element.96.down_ref, bf16[3,512,2048]{2,1,0:T(8,128)(2,1)} %get-tuple-element.97.back_ref), custom_call_target="tpu_custom_call" | custom-call | tf_op jit(solution)/shard_map/expert_terms/pallas_call | solution.py:145
  183.8 10.7 %all-to-all-start.1 = ((bf16[8,48,2048]{2,1,0:T(8,128)(2,1)}), bf16[8,48,2048]{2,1,0:T(8,128)(2,1)}, u32[]{:S(2)}, u32[]{:S(2)}) async-start(bf16[8,48,2048]{2,1,0:T(8,128)(2,1)} %bitcast.16), calls=%async_computation.1 | async-start | bytes 3145728 | tf_op jit(solution)/shard_map/all_to_all | solution.py:447
  194.5 2.2 collective-permute-start.10
  199.7 22.1 %collective-permute-done.15.refs_14_ = bf16[2,128,2048]{2,1,0:T(8,128)(2,1)} collective-permute-done((bf16[2,128,2048]{2,1,0:T(8,128)(2,1)}, bf16[2,128,2048]{2,1,0:T(8,128)(2,1)}, u32[]{:S(2)}, u32[]{:S(2)}) %collective-permute-start.15) | collective-permute-done | bytes 1048608 | tf_op jit(solution)/shard_map/ppermute | solution.py:413
  223.2 2.0 collective-permute-done.16.refs_15_
  225.2 3.7 %all-to-all-done.1 = bf16[8,48,2048]{2,1,0:T(8,128)(2,1)} async-done(((bf16[8,48,2048]{2,1,0:T(8,128)(2,1)}), bf16[8,48,2048]{2,1,0:T(8,128)(2,1)}, u32[]{:S(2)}, u32[]{:S(2)}) %all-to-all-start.1) | async-done | bytes 1572896 | tf_op jit(solution)/shard_map/all_to_all | solution.py:447
  228.9 16.7 %tail_attention.1 = (bf16[128,2048]{1,0:T(8,128)(2,1)}, bf16[128,4096]{1,0:T(8,128)(2,1)}, f32[2,128,256]{2,1,0:T(8,128)}, bf16[2,128,256]{2,1,0:T(8,128)(2,1)}) custom-call(s32[3]{0:T(128)} %pad_add_fusion.place_info, bf16[384,2048]{1,0:T(8,128)(2,1)} %bitcast.17.back_ref, bf16[128,384]{1,0:T(8,128)(2,1)} %copy-done.14, bf16[128,2048]{1,0:T(8,128)(2,1)} %grad_ref.3, ...), custom_call_target="tpu_custom_call" | custom-call | flops 2147483648 | bytes 23068672 | tf_op jit(solution)/shard_map/tail_attention/pallas_call | solution.py:323
  245.6 2.4 collective-permute-start.17
  248.1 5.0 %collective-permute-done.17.later_ref = bf16[2,128,256]{2,1,0:T(8,128)(2,1)S(1)} collective-permute-done((bf16[2,128,256]{2,1,0:T(8,128)(2,1)}, bf16[2,128,256]{2,1,0:T(8,128)(2,1)S(1)}, u32[]{:S(2)}, u32[]{:S(2)}) %collective-permute-start.17) | collective-permute-done | bytes 131104 | tf_op jit(solution)/shard_map/ppermute | solution.py:459
  253.7 1.7 finish.1
  (79 shorter events, 21.2 us)
Async XLA Ops:
  7.2 29.5 %all-gather.5.cloned.1.call-start = ((), (), s32[]{:S(2)}) async-start(), calls=%async_computation.2 | async-start | bytes 1572864 | tf_op jit(solution)/shard_map/all_gather | solution.py:412
  9.3 27.4 %collective-permute-start = (bf16[128,2048]{1,0:T(8,128)(2,1)}, bf16[128,2048]{1,0:T(8,128)(2,1)S(1)}, u32[]{:S(2)}, u32[]{:S(2)}) collective-permute-start(bf16[128,2048]{1,0:T(8,128)(2,1)} %constant_dynamic-slice_fusion), channel_id=1, source_target_pairs={{0,4},{4,0},{1,5},{5,1},{2,6},{6,2},{3,7},{7,3},{8,12},{12,8},{9,1... | collective-permute-start | bytes 1572872 | tf_op jit(solution)/shard_map/ppermute | solution.py:408
  9.5 27.2 %collective-permute-start.1 = (bf16[128,2048]{1,0:T(8,128)(2,1)}, bf16[128,2048]{1,0:T(8,128)(2,1)S(1)}, u32[]{:S(2)}, u32[]{:S(2)}) collective-permute-start(bf16[128,2048]{1,0:T(8,128)(2,1)} %constant_dynamic-slice_fusion), channel_id=1, source_target_pairs={{0,8},{8,0},{1,9},{9,1},{2,10},{10,2},{3,11},{11,3},{4,12},{12,4},... | collective-permute-start | bytes 1572872 | tf_op jit(solution)/shard_map/ppermute | solution.py:409
  18.1 18.7 %copy-start.14 = (bf16[128,384]{1,0:T(8,128)(2,1)}, bf16[128,384]{1,0:T(8,128)(2,1)S(1)}, u32[]{:S(2)}) copy-start(bf16[128,384]{1,0:T(8,128)(2,1)S(1)} %get-tuple-element.103.place_ref) | copy-start | bytes 294916
  18.1 18.6 %collective-permute-start.2 = (bf16[144,512]{1,0:T(8,128)(2,1)S(1)}, bf16[144,512]{1,0:T(8,128)(2,1)S(1)}, u32[]{:S(2)}, u32[]{:S(2)}) collective-permute-start(bf16[144,512]{1,0:T(8,128)(2,1)S(1)} %fusion.1), channel_id=1, source_target_pairs={{0,1},{1,2},{2,3},{3,4},{4,5},{5,6},{6,7},{7,8},{8,9},{9,10},{10,1... | collective-permute-start | bytes 442376 | tf_op jit(solution)/shard_map/ppermute | solution.py:422
  37.5 131.3 %all-to-all-start = ((bf16[8,48,4096]{2,1,0:T(8,128)(2,1)}), bf16[8,48,4096]{2,1,0:T(8,128)(2,1)}, u32[]{:S(2)}, u32[]{:S(2)}) async-start(bf16[8,48,4096]{2,1,0:T(8,128)(2,1)} %bitcast.21), calls=%async_computation | async-start | bytes 6291456 | tf_op jit(solution)/shard_map/all_to_all | solution.py:426
  41.9 57.3 %all-gather.7.cloned.1.call-start = ((), (), s32[]{:S(2)}) async-start(), calls=%async_computation.3 | async-start | bytes 3145728 | tf_op jit(solution)/shard_map/all_gather | solution.py:412
  44.2 12.5 %collective-permute-start.3 = (bf16[2048,384]{1,0:T(8,128)(2,1)S(1)}, bf16[2048,384]{1,0:T(8,128)(2,1)}, u32[]{:S(2)}, u32[]{:S(2)}) collective-permute-start(bf16[2048,384]{1,0:T(8,128)(2,1)S(1)} %copy-done.4), channel_id=1, source_target_pairs={{0,1},{1,0},{2,3},{3,2},{4,5},{5,4},{6,7},{7,6},{8,9},{9,8},{10,11... | collective-permute-start | bytes 4718600 | tf_op jit(solution)/shard_map/ppermute | solution.py:414
  46.3 10.5 %collective-permute-start.4 = (bf16[2048,384]{1,0:T(8,128)(2,1)}, bf16[2048,384]{1,0:T(8,128)(2,1)}, u32[]{:S(2)}, u32[]{:S(2)}) collective-permute-start(bf16[2048,384]{1,0:T(8,128)(2,1)} %refs_1_.1), channel_id=1, source_target_pairs={{0,1},{1,0},{2,3},{3,2},{4,5},{5,4},{6,7},{7,6},{8,9},{9,8},{10,11... | collective-permute-start | bytes 4718600 | tf_op jit(solution)/shard_map/ppermute | solution.py:414
  46.4 10.4 %collective-permute-start.5 = (bf16[384,2048]{1,0:T(8,128)(2,1)}, bf16[384,2048]{1,0:T(8,128)(2,1)}, u32[]{:S(2)}, u32[]{:S(2)}) collective-permute-start(bf16[384,2048]{1,0:T(8,128)(2,1)} %refs_2_.1), channel_id=1, source_target_pairs={{0,1},{1,0},{2,3},{3,2},{4,5},{5,4},{6,7},{7,6},{8,9},{9,8},{10,11... | collective-permute-start | bytes 4718600 | tf_op jit(solution)/shard_map/ppermute | solution.py:414
  99.3 84.6 %collective-permute-start.9 = (bf16[2,2,128,2048]{3,2,1,0:T(8,128)(2,1)}, bf16[2,2,128,2048]{3,2,1,0:T(8,128)(2,1)}, u32[]{:S(2)}, u32[]{:S(2)}) collective-permute-start(bf16[2,2,128,2048]{3,2,1,0:T(8,128)(2,1)} %bitcast.24), channel_id=1, source_target_pairs={{0,16},{16,0},{1,17},{17,1},{2,18},{18,2},{3,19},{19,3},{4,20},{20... | collective-permute-start | bytes 6291464 | tf_op jit(solution)/shard_map/ppermute | solution.py:413
  100.5 68.3 %collective-permute-start.6 = (bf16[2,128,2048]{2,1,0:T(8,128)(2,1)}, bf16[2,128,2048]{2,1,0:T(8,128)(2,1)}, u32[]{:S(2)}, u32[]{:S(2)}) collective-permute-start(bf16[2,128,2048]{2,1,0:T(8,128)(2,1)} %bitcast.28), channel_id=1, source_target_pairs={{0,16},{16,0},{1,17},{17,1},{2,18},{18,2},{3,19},{19,3},{4,20},{20... | collective-permute-start | bytes 3145736 | tf_op jit(solution)/shard_map/ppermute | solution.py:413
  100.7 19.2 %collective-permute-start.7 = (bf16[128,2048]{1,0:T(8,128)(2,1)S(1)}, bf16[128,2048]{1,0:T(8,128)(2,1)S(1)}, u32[]{:S(2)}, u32[]{:S(2)}) collective-permute-start(bf16[128,2048]{1,0:T(8,128)(2,1)S(1)} %collective-permute-done.1), channel_id=1, source_target_pairs={{0,4},{4,0},{1,5},{5,1},{2,6},{6,2},{3,7},{7,3},{8,12},{12,8},{9,1... | collective-permute-start | bytes 1572872 | tf_op jit(solution)/shard_map/ppermute | solution.py:428
  168.8 13.9 %collective-permute-start.8 = (bf16[128,2048]{1,0:T(8,128)(2,1)S(1)}, bf16[128,2048]{1,0:T(8,128)(2,1)S(1)}, u32[]{:S(2)}, u32[]{:S(2)}) collective-permute-start(bf16[128,2048]{1,0:T(8,128)(2,1)S(1)} %collective-permute-done.7), channel_id=1, source_target_pairs={{0,2},{2,0},{1,3},{3,1},{4,6},{6,4},{5,7},{7,5},{8,10},{10,8},{9,1... | collective-permute-start | bytes 1572872 | tf_op jit(solution)/shard_map/ppermute | solution.py:437
  183.8 14.0 %copy-start.18 = (bf16[4,128,2048]{2,1,0:T(8,128)(2,1)S(1)}, bf16[4,128,2048]{2,1,0:T(8,128)(2,1)}, u32[]{:S(2)}) copy-start(bf16[4,128,2048]{2,1,0:T(8,128)(2,1)} %all-gather.7.cloned.1.call-done) | copy-start | bytes 6291460
  183.8 45.1 %all-to-all-start.1 = ((bf16[8,48,2048]{2,1,0:T(8,128)(2,1)}), bf16[8,48,2048]{2,1,0:T(8,128)(2,1)}, u32[]{:S(2)}, u32[]{:S(2)}) async-start(bf16[8,48,2048]{2,1,0:T(8,128)(2,1)} %bitcast.16), calls=%async_computation.1 | async-start | bytes 3145728 | tf_op jit(solution)/shard_map/all_to_all | solution.py:447
  194.5 4.8 %collective-permute-start.10 = (bf16[2,128,2048]{2,1,0:T(8,128)(2,1)}, bf16[2,128,2048]{2,1,0:T(8,128)(2,1)}, u32[]{:S(2)}, u32[]{:S(2)}) collective-permute-start(bf16[2,128,2048]{2,1,0:T(8,128)(2,1)} %bitcast.29), channel_id=1, source_target_pairs={{0,1},{1,0},{2,3},{3,2},{4,5},{5,4},{6,7},{7,6},{8,9},{9,8},{10,11... | collective-permute-start | bytes 3145736 | tf_op jit(solution)/shard_map/ppermute | solution.py:414
  196.7 25.1 %collective-permute-start.15 = (bf16[2,128,2048]{2,1,0:T(8,128)(2,1)}, bf16[2,128,2048]{2,1,0:T(8,128)(2,1)}, u32[]{:S(2)}, u32[]{:S(2)}) collective-permute-start(bf16[2,128,2048]{2,1,0:T(8,128)(2,1)} %maximum_select_fusion.refs_6_), channel_id=1, source_target_pairs={{0,16},{16,0},{1,17},{17,1},{2,18},{18,2},{3,19},{19,3},{4,20},{20... | collective-permute-start | bytes 3145736 | tf_op jit(solution)/shard_map/ppermute | solution.py:413
  197.9 27.3 %collective-permute-start.11 = (bf16[2,2,128,2048]{3,2,1,0:T(8,128)(2,1)S(1)}, bf16[2,2,128,2048]{3,2,1,0:T(8,128)(2,1)}, u32[]{:S(2)}, u32[]{:S(2)}) collective-permute-start(bf16[2,2,128,2048]{3,2,1,0:T(8,128)(2,1)S(1)} %bitcast.27), channel_id=1, source_target_pairs={{0,1},{1,0},{2,3},{3,2},{4,5},{5,4},{6,7},{7,6},{8,9},{9,8},{10,11... | collective-permute-start | bytes 6291464 | tf_op jit(solution)/shard_map/ppermute | solution.py:414
  198.2 27.1 %collective-permute-start.14 = (bf16[2,2,128,2048]{3,2,1,0:T(8,128)(2,1)}, bf16[2,2,128,2048]{3,2,1,0:T(8,128)(2,1)}, u32[]{:S(2)}, u32[]{:S(2)}) collective-permute-start(bf16[2,2,128,2048]{3,2,1,0:T(8,128)(2,1)} %collective-permute-done.9.refs_10_.refs_12_), channel_id=1, source_target_pairs={{0,1},{1,0},{2,3},{3,2},{4,5},{5,4},{6,7},{7,6},{8,9},{9,8},{10,11... | collective-permute-start | bytes 6291464 | tf_op jit(solution)/shard_map/ppermute | solution.py:414
  198.4 24.9 %collective-permute-start.12 = (bf16[2,128,2048]{2,1,0:T(8,128)(2,1)}, bf16[2,128,2048]{2,1,0:T(8,128)(2,1)}, u32[]{:S(2)}, u32[]{:S(2)}) collective-permute-start(bf16[2,128,2048]{2,1,0:T(8,128)(2,1)} %maximum_select_fusion.refs_6_), channel_id=1, source_target_pairs={{0,1},{1,0},{2,3},{3,2},{4,5},{5,4},{6,7},{7,6},{8,9},{9,8},{10,11... | collective-permute-start | bytes 3145736 | tf_op jit(solution)/shard_map/ppermute | solution.py:414
  199.3 23.9 %collective-permute-start.13 = (bf16[2,128,2048]{2,1,0:T(8,128)(2,1)}, bf16[2,128,2048]{2,1,0:T(8,128)(2,1)}, u32[]{:S(2)}, u32[]{:S(2)}) collective-permute-start(bf16[2,128,2048]{2,1,0:T(8,128)(2,1)} %collective-permute-done.6.refs_8_), channel_id=1, source_target_pairs={{0,1},{1,0},{2,3},{3,2},{4,5},{5,4},{6,7},{7,6},{8,9},{9,8},{10,11... | collective-permute-start | bytes 3145736 | tf_op jit(solution)/shard_map/ppermute | solution.py:414
  221.8 3.4 %collective-permute-start.16 = (bf16[2,128,2048]{2,1,0:T(8,128)(2,1)}, bf16[2,128,2048]{2,1,0:T(8,128)(2,1)}, u32[]{:S(2)}, u32[]{:S(2)}) collective-permute-start(bf16[2,128,2048]{2,1,0:T(8,128)(2,1)} %collective-permute-done.15.refs_14_), channel_id=1, source_target_pairs={{0,1},{1,0},{2,3},{3,2},{4,5},{5,4},{6,7},{7,6},{8,9},{9,8},{10,11... | collective-permute-start | bytes 3145736 | tf_op jit(solution)/shard_map/ppermute | solution.py:414
  245.6 7.4 %collective-permute-start.17 = (bf16[2,128,256]{2,1,0:T(8,128)(2,1)}, bf16[2,128,256]{2,1,0:T(8,128)(2,1)S(1)}, u32[]{:S(2)}, u32[]{:S(2)}) collective-permute-start(bf16[2,128,256]{2,1,0:T(8,128)(2,1)} %get-tuple-element.117), channel_id=1, source_target_pairs={{1,0},{2,1},{3,2},{4,3},{5,4},{6,5},{7,6},{8,7},{9,8},{10,9},{11,1... | collective-permute-start | bytes 393224 | tf_op jit(solution)/shard_map/ppermute | solution.py:459
  (20 other events, 60.4 us)
Sparse Core Ops, SparseCore 0:
  10.2 23.0 all-gather.4
  44.9 54.3 all-gather.6

commit v18 on v17

--- a/solution.py
+++ b/solution.py
@@ -316,8 +316,8 @@
     paired = lambda turn, which: pl.BlockSpec(
         (spread, 1, size, tile), lambda i, info: (0, which, 0, turn(i))
     )
-    pieces_of = lambda turn: (
-        [single(turn)] * 2 + [paired(turn, 0)] * 2 + [paired(turn, 1)] * 2 + [single(turn)] * 2
+    pieces_of = lambda turn, first: (
+        [single(turn)] * 2 + [paired(turn, first)] * 2 + [paired(turn, first + 1)] * 2 + [single(turn)] * 2
     )
     kv = pl.BlockSpec((2, tokens, HD), lambda i, info: (0, 0, kv_group(i, info)))
     return pl.pallas_call(
@@ -326,7 +326,8 @@
             num_scalar_prefetch=1,
             grid=(steps + 1,),
             in_specs=[whole(back.shape), whole(place.shape), whole(moe_grad.shape)]
-            + [spec for turn in (own_tile, other_tile) for spec in pieces_of(turn)]
+            + pieces_of(own_tile, 0)
+            + pieces_of(other_tile, 2)
             + [
                 rows((heads * tokens, span)),
                 pl.BlockSpec(
@@ -424,12 +425,14 @@
     rows, w_near, w_far, own_line, prev = lax.optimization_barrier((rows, w_near, w_far, own_line, prev))
 
     rows_in = lax.all_to_all(rows.reshape(owners, depth, 2 * width), chips, 0, 0, tiled=True)
-    pair_line = line(jnp.stack([w_near, w_far]))
+    pair = jnp.stack([w_near, w_far])
+    pair_crossed = cross(pair)
+    four_lines = line(jnp.concatenate([pair, pair_crossed], axis=0))
+    own_line, pair_crossed = lax.optimization_barrier((own_line, pair_crossed))
+    own_crossed = cross(own_line)
     w_last = lax.ppermute(w_far, "near", swap)
     prepared = prepare_weights(own, other)
     attention = attention_shares(queries, key_heads, value_heads, prev, segs)
-    pair_line, prepared, attention = lax.optimization_barrier((pair_line, prepared, attention))
-    own_crossed, pair_crossed = cross(own_line), cross(pair_line)
     rows_in, prepared, attention, own_line, own_crossed, w_last = lax.optimization_barrier(
         (rows_in, prepared, attention, own_line, own_crossed, w_last)
     )
@@ -440,21 +443,22 @@
     else:
         last_line = line(w_last)
     terms = experts(rows_in.reshape(owners * depth, 2 * width), *prepared)
-    terms, own_line, own_crossed, last_line, pair_line, pair_crossed = lax.optimization_barrier(
-        (terms, own_line, own_crossed, last_line, pair_line, pair_crossed)
+    terms, own_line, own_crossed, last_line, four_lines = lax.optimization_barrier(
+        (terms, own_line, own_crossed, last_line, four_lines)
     )
     last_crossed = cross(last_line)
     back = lax.all_to_all(terms.reshape(owners, depth, width), chips, 0, 0, tiled=True)
 
-    def pieces(own_piece, pair_piece, last_piece):
-        pairs = [(piece, other_core(piece)) for piece in (own_piece, pair_piece, last_piece)]
-        return [*pairs[0], *pairs[1], *pairs[1], *pairs[2]]
+    four = (four_lines, other_core(four_lines))
+
+    def pieces(own_piece, last_piece):
+        return [own_piece, other_core(own_piece), *four, *four, last_piece, other_core(last_piece)]
 
     z = 2 * lax.axis_index("far") + lax.axis_index("near")
     moe_input_grad, query_grad, kept, sent = tail(
         jnp.stack([lax.axis_index("groups"), z, lax.axis_index("core")]).astype(jnp.int32),
         back.reshape(owners * depth, width), place, moe_grad,
-        pieces(own_line, pair_line, last_line) + pieces(own_crossed, pair_crossed, last_crossed), *attention,
+        pieces(own_line, last_line) + pieces(own_crossed, last_crossed), *attention,
     )
     return (moe_input_grad, query_grad, *finish(kept, lax.ppermute(sent, blk, backward)))
 

time: 266 us -> 226 us (0.85)
  waiting for transfers between devices: 149 us -> 109 us
  starting transfers between devices: 32.7 us -> 29.2 us
  local copies, waits for them, and re-layouts: 16.4 us -> 19.2 us
    ppermute x3, waiting for transfers between devices: 71 us -> 42.2 us  [local(): cross = lambda w: lax.ppermute(w, 'groups', swap)]
    all_gather x2, waiting for transfers between devices: 32.1 us -> 12 us  [local(): line = lambda w: lax.all_gather(w, 'low', axis=0, tiled=False)]
    ppermute x1, waiting for transfers between devices: 19.1 us -> 7.42 us  [local(): w_last = lax.ppermute(w_far, 'near', swap)]
    ppermute x1, waiting for transfers between devices: 0.01 us -> 11.5 us  [local(): moved = lax.ppermute(w_last, 'low', swap)]
    all_to_all x1, waiting for transfers between devices: 0.01 us -> 7.15 us  [local(): lax.all_to_all(rows.reshape(owners, depth, 2 * width), chips, 0, 0, tiled...]
    all_to_all x1, starting transfers between devices: 10.7 us -> 4.79 us  [local(): lax.all_to_all(terms.reshape(owners, depth, width), chips, 0, 0, tiled=True)]
    unnamed x44 -> x50, local copies, waits for them, and re-layouts: 15.5 us -> 18.2 us
    concatenate x0 -> x1, other arithmetic: none -> 2.66 us  [local(): four_lines = line(jnp.concatenate([pair, pair_crossed], axis=0))]
  transfers between devices with their start and end apart: 22 -> 21, of which waited for: 9 -> 10; matrix products, arithmetic and copies ran while one was open for 2% -> 3% of each run, Pallas kernels for 10% -> 12%
where the time goes in v18:
time: 226 us; the launch traced here: 223 us
  waiting for transfers between devices  109 us (48%)
  Pallas kernels  44.5 us (20%)
  starting transfers between devices  29.2 us (13%)
  local copies, waits for them, and re-layouts  19.2 us (8%)
  between operations  14.2 us (6%)
  other arithmetic  6.4 us (3%)
    ppermute x3, waiting for transfers between devices, local(): cross = lambda w: lax.ppermute(w, 'groups', swap)  42.2 us
    unnamed x50, local copies, waits for them, and re-layouts  18.2 us
    pallas_call x1, Pallas kernels, tail(): pl.pallas_call(functools.partial(tail_kernel, (heads, tiles)), grid_spec=...  16.8 us
    ppermute x1, waiting for transfers between devices, local(): prev = lax.ppermute(jnp.concatenate([kv, seg_rows], axis=0), blk, onward)  15.4 us
    pallas_call x1, Pallas kernels, experts(): pl.pallas_call(functools.partial(expert_kernel, steps), grid=(steps + wid...  12.6 us
    all_gather x2, waiting for transfers between devices, local(): line = lambda w: lax.all_gather(w, 'low', axis=0, tiled=False)  12 us
    ppermute x1, waiting for transfers between devices, local(): moved = lax.ppermute(w_last, 'low', swap)  11.5 us
    pallas_call x1, Pallas kernels, prepare_weights(): pl.pallas_call(weights_kernel, grid=(steps,), in_specs=[cols, cols, down]...  8.83 us
  transfers between devices with their start and end apart: 21, of which 10 were waited for; matrix products, arithmetic and copies ran while one was open for 3% of the time, Pallas kernels for 12%

profile of v18, /device:TPU:13, one launch (start us, length us, event | category | flops | bytes accessed | tf_op | source)
XLA Modules:
  0.0 222.5 jit_solution(4921176510517862733)
XLA Ops:
  9.5 2.3 %collective-permute-start.1 = (bf16[128,2048]{1,0:T(8,128)(2,1)}, bf16[128,2048]{1,0:T(8,128)(2,1)}, u32[]{:S(2)}, u32[]{:S(2)}) collective-permute-start(bf16[128,2048]{1,0:T(8,128)(2,1)} %constant_dynamic-slice_fusion), channel_id=1, source_target_pairs={{0,8},{8,0},{1,9},{9,1},{2,10},{10,2},{3,11},{11,3},{4,12},{12,4},... | collective-permute-start | bytes 1572872 | tf_op jit(solution)/shard_map/ppermute | solution.py:410
  16.4 1.6 copy-done.2
  18.1 3.2 %collective-permute-start.2 = (bf16[144,512]{1,0:T(8,128)(2,1)S(1)}, bf16[144,512]{1,0:T(8,128)(2,1)S(1)}, u32[]{:S(2)}, u32[]{:S(2)}) collective-permute-start(bf16[144,512]{1,0:T(8,128)(2,1)S(1)} %fusion.1), channel_id=1, source_target_pairs={{0,1},{1,2},{2,3},{3,4},{4,5},{5,6},{6,7},{7,8},{8,9},{9,10},{10,1... | collective-permute-start | bytes 442376 | tf_op jit(solution)/shard_map/ppermute | solution.py:423
  21.2 15.4 %collective-permute-done.2.prev_key_ref.prev_value_ref.prev_seg_ref = bf16[144,512]{1,0:T(8,128)(2,1)S(1)} collective-permute-done((bf16[144,512]{1,0:T(8,128)(2,1)S(1)}, bf16[144,512]{1,0:T(8,128)(2,1)S(1)}, u32[]{:S(2)}, u32[]{:S(2)}) %collective-permute-start.2) | collective-permute-done | bytes 147488 | tf_op jit(solution)/shard_map/ppermute | solution.py:423
  37.5 3.6 %all-to-all-start = ((bf16[8,48,4096]{2,1,0:T(8,128)(2,1)}), bf16[8,48,4096]{2,1,0:T(8,128)(2,1)S(1)}, u32[]{:S(2)}, u32[]{:S(2)}) async-start(bf16[8,48,4096]{2,1,0:T(8,128)(2,1)} %bitcast.22), calls=%async_computation | async-start | bytes 6291456 | tf_op jit(solution)/shard_map/all_to_all | solution.py:427
  43.8 20.6 %collective-permute-done.6 = bf16[2,128,2048]{2,1,0:T(8,128)(2,1)S(1)} collective-permute-done((bf16[2,128,2048]{2,1,0:T(8,128)(2,1)S(1)}, bf16[2,128,2048]{2,1,0:T(8,128)(2,1)S(1)}, u32[]{:S(2)}, u32[]{:S(2)}) %collective-permute-start.6) | collective-permute-done | bytes 1048608 | tf_op jit(solution)/shard_map/ppermute | solution.py:414
  64.4 2.7 %pad_maximum_fusion = bf16[4,128,2048]{2,1,0:T(8,128)(2,1)} fusion(bf16[2,128,2048]{2,1,0:T(8,128)(2,1)S(1)} %collective-permute-done.6, bf16[1,128,2048]{2,1,0:T(8,128)(2,1)} %bitcast.11, bf16[1,128,2048]{2,1,0:T(8,128)(2,1)S(1)} %bitcast.32), kind=kLoop, calls=%fused_computation | loop fusion | flops 2097152 | bytes 4194304 | tf_op jit(solution)/shard_map/concatenate | solution.py:430
  67.1 3.8 %collective-permute-start.3 = (bf16[2048,384]{1,0:T(8,128)(2,1)}, bf16[2048,384]{1,0:T(8,128)(2,1)}, u32[]{:S(2)}, u32[]{:S(2)}) collective-permute-start(bf16[2048,384]{1,0:T(8,128)(2,1)} %refs_0_.1), channel_id=1, source_target_pairs={{0,1},{1,0},{2,3},{3,2},{4,5},{5,4},{6,7},{7,6},{8,9},{9,8},{10,11... | collective-permute-start | bytes 4718600 | tf_op jit(solution)/shard_map/ppermute | solution.py:415
  74.4 3.5 %attention_shares.1 = (bf16[2,2048,256]{2,1,0:T(8,128)(2,1)S(1)}, bf16[2,256,2048]{2,1,0:T(8,128)(2,1)S(1)}, bf16[2,2048,128]{2,1,0:T(8,128)(2,1)S(1)}, bf16[2,2...) custom-call(bf16[128,4096]{1,0:T(8,128)(2,1)S(1)} %copy-done.9, bf16[128,256]{1,0:T(8,128)(2,1)S(1)} %copy-done.11, ...), custom_call_target="tpu_custom_call" | custom-call | tf_op jit(solution)/shard_map/attention_shares/pallas_call | solution.py:201
  86.0 8.8 %prepare_weights.1 = (bf16[3,2048,512]{2,1,0:T(8,128)(2,1)}, bf16[3,2048,256]{2,1,0:T(8,128)(2,1)}, bf16[3,512,2048]{2,1,0:T(8,128)(2,1)}) custom-call(bf16[2048,384]{1,0:T(8,128)(2,1)S(1)} %copy-done.5, bf16[2048,384]{1,0:T(8,128)(2,1)S(1)} %copy-done.6, bf16[384,2048]{1,0:T(8,128)(2,1)S(1)} %copy-done.7, bf16[2048,384]{1,0:T(8,128)(2,1)} %collective-permute-done.3.refs_3_, ...), custom_call_target="tpu_custom_call" | custom-call | tf_op jit(solution)/shard_map/prepare_weights/pallas_call | solution.py:94
  94.8 7.4 %collective-permute-done.8 = bf16[128,2048]{1,0:T(8,128)(2,1)} collective-permute-done((bf16[128,2048]{1,0:T(8,128)(2,1)}, bf16[128,2048]{1,0:T(8,128)(2,1)}, u32[]{:S(2)}, u32[]{:S(2)}) %collective-permute-start.8) | collective-permute-done | bytes 524320 | tf_op jit(solution)/shard_map/ppermute | solution.py:433
  102.2 7.2 %all-to-all-done = bf16[8,48,4096]{2,1,0:T(8,128)(2,1)S(1)} async-done(((bf16[8,48,4096]{2,1,0:T(8,128)(2,1)}), bf16[8,48,4096]{2,1,0:T(8,128)(2,1)S(1)}, u32[]{:S(2)}, u32[]{:S(2)}) %all-to-all-start) | async-done | bytes 3145760 | tf_op jit(solution)/shard_map/all_to_all | solution.py:427
  110.4 12.6 %expert_terms.1 = bf16[384,2048]{1,0:T(8,128)(2,1)} custom-call(bf16[384,4096]{1,0:T(8,128)(2,1)S(1)} %bitcast.21, bf16[3,2048,512]{2,1,0:T(8,128)(2,1)} %get-tuple-element.79.cols_ref, bf16[3,2048,256]{2,1,0:T(8,128)(2,1)} %get-tuple-element.80.down_ref, bf16[3,512,2048]{2,1,0:T(8,128)(2,1)} %get-tuple-element.81.back_ref), custom_call_target="tpu_custom_call" | custom-call | tf_op jit(solution)/shard_map/expert_terms/pallas_call | solution.py:145
  123.0 11.5 %collective-permute-done.9 = bf16[128,2048]{1,0:T(8,128)(2,1)} collective-permute-done((bf16[128,2048]{1,0:T(8,128)(2,1)}, bf16[128,2048]{1,0:T(8,128)(2,1)}, u32[]{:S(2)}, u32[]{:S(2)}) %collective-permute-start.9) | collective-permute-done | bytes 524320 | tf_op jit(solution)/shard_map/ppermute | solution.py:440
  134.5 1.7 maximum_select_fusion.refs_6_
  136.2 12.0 %all-gather.7.cloned.1.call-done = bf16[8,128,2048]{2,1,0:T(8,128)(2,1)} async-done(((bf16[4,128,2048]{2,1,0:T(8,128)(2,1)}), bf16[8,128,2048]{2,1,0:T(8,128)(2,1)}) %all-gather.7.cloned.1.call-update) | async-done | bytes 4194320 | tf_op jit(solution)/shard_map/all_gather | solution.py:413
  148.7 4.8 %all-to-all-start.1 = ((bf16[8,48,2048]{2,1,0:T(8,128)(2,1)}), bf16[8,48,2048]{2,1,0:T(8,128)(2,1)S(1)}, u32[]{:S(2)}, u32[]{:S(2)}) async-start(bf16[8,48,2048]{2,1,0:T(8,128)(2,1)} %bitcast.16), calls=%async_computation.1 | async-start | bytes 3145728 | tf_op jit(solution)/shard_map/all_to_all | solution.py:450
  156.1 21.6 %collective-permute-done.14.refs_14_ = bf16[2,128,2048]{2,1,0:T(8,128)(2,1)} collective-permute-done((bf16[2,128,2048]{2,1,0:T(8,128)(2,1)S(1)}, bf16[2,128,2048]{2,1,0:T(8,128)(2,1)}, u32[]{:S(2)}, u32[]{:S(2)}) %collective-permute-start.14) | collective-permute-done | bytes 1048608 | tf_op jit(solution)/shard_map/ppermute | solution.py:414
  179.8 1.9 collective-permute-done.15.refs_15_
  181.8 6.2 %all-to-all-done.1 = bf16[8,48,2048]{2,1,0:T(8,128)(2,1)S(1)} async-done(((bf16[8,48,2048]{2,1,0:T(8,128)(2,1)}), bf16[8,48,2048]{2,1,0:T(8,128)(2,1)S(1)}, u32[]{:S(2)}, u32[]{:S(2)}) %all-to-all-start.1) | async-done | bytes 1572896 | tf_op jit(solution)/shard_map/all_to_all | solution.py:450
  189.1 16.8 %tail_attention.1 = (bf16[128,2048]{1,0:T(8,128)(2,1)}, bf16[128,4096]{1,0:T(8,128)(2,1)}, f32[2,128,256]{2,1,0:T(8,128)}, bf16[2,128,256]{2,1,0:T(8,128)(2,1)}) custom-call(s32[3]{0:T(128)} %pad_add_fusion.place_info, bf16[384,2048]{1,0:T(8,128)(2,1)} %bitcast.30, bf16[128,384]{1,0:T(8,128)(2,1)} %copy-done.15, bf16[128,2048]{1,0:T(8,128)(2,1)} %grad_ref.3, ...), custom_call_target="tpu_custom_call" | custom-call | flops 2147483648 | bytes 23068672 | tf_op jit(solution)/shard_map/tail_attention/pallas_call | solution.py:323
  205.9 2.4 %collective-permute-start.16 = (bf16[2,128,256]{2,1,0:T(8,128)(2,1)}, bf16[2,128,256]{2,1,0:T(8,128)(2,1)S(1)}, u32[]{:S(2)}, u32[]{:S(2)}) collective-permute-start(bf16[2,128,256]{2,1,0:T(8,128)(2,1)} %get-tuple-element.99), channel_id=1, source_target_pairs={{1,0},{2,1},{3,2},{4,3},{5,4},{6,5},{7,6},{8,7},{9,8},{10,9},{11,1... | collective-permute-start | bytes 393224 | tf_op jit(solution)/shard_map/ppermute | solution.py:463
  208.3 5.0 %collective-permute-done.16.later_ref = bf16[2,128,256]{2,1,0:T(8,128)(2,1)S(1)} collective-permute-done((bf16[2,128,256]{2,1,0:T(8,128)(2,1)}, bf16[2,128,256]{2,1,0:T(8,128)(2,1)S(1)}, u32[]{:S(2)}, u32[]{:S(2)}) %collective-permute-start.16) | collective-permute-done | bytes 131104 | tf_op jit(solution)/shard_map/ppermute | solution.py:463
  214.0 1.7 finish.1
  (84 shorter events, 29.9 us)
Async XLA Ops:
  7.2 30.3 %all-gather.5.cloned.1.call-start = ((), (), s32[]{:S(2)}) async-start(), calls=%async_computation.2 | async-start | bytes 1572864 | tf_op jit(solution)/shard_map/all_gather | solution.py:413
  9.3 27.4 %collective-permute-start = (bf16[128,2048]{1,0:T(8,128)(2,1)}, bf16[128,2048]{1,0:T(8,128)(2,1)S(1)}, u32[]{:S(2)}, u32[]{:S(2)}) collective-permute-start(bf16[128,2048]{1,0:T(8,128)(2,1)} %constant_dynamic-slice_fusion), channel_id=1, source_target_pairs={{0,4},{4,0},{1,5},{5,1},{2,6},{6,2},{3,7},{7,3},{8,12},{12,8},{9,1... | collective-permute-start | bytes 1572872 | tf_op jit(solution)/shard_map/ppermute | solution.py:409
  9.5 28.0 %collective-permute-start.1 = (bf16[128,2048]{1,0:T(8,128)(2,1)}, bf16[128,2048]{1,0:T(8,128)(2,1)}, u32[]{:S(2)}, u32[]{:S(2)}) collective-permute-start(bf16[128,2048]{1,0:T(8,128)(2,1)} %constant_dynamic-slice_fusion), channel_id=1, source_target_pairs={{0,8},{8,0},{1,9},{9,1},{2,10},{10,2},{3,11},{11,3},{4,12},{12,4},... | collective-permute-start | bytes 1572872 | tf_op jit(solution)/shard_map/ppermute | solution.py:410
  18.1 18.6 %collective-permute-start.2 = (bf16[144,512]{1,0:T(8,128)(2,1)S(1)}, bf16[144,512]{1,0:T(8,128)(2,1)S(1)}, u32[]{:S(2)}, u32[]{:S(2)}) collective-permute-start(bf16[144,512]{1,0:T(8,128)(2,1)S(1)} %fusion.1), channel_id=1, source_target_pairs={{0,1},{1,2},{2,3},{3,4},{4,5},{5,6},{6,7},{7,8},{8,9},{9,10},{10,1... | collective-permute-start | bytes 442376 | tf_op jit(solution)/shard_map/ppermute | solution.py:423
  37.5 71.9 %all-to-all-start = ((bf16[8,48,4096]{2,1,0:T(8,128)(2,1)}), bf16[8,48,4096]{2,1,0:T(8,128)(2,1)S(1)}, u32[]{:S(2)}, u32[]{:S(2)}) async-start(bf16[8,48,4096]{2,1,0:T(8,128)(2,1)} %bitcast.22), calls=%async_computation | async-start | bytes 6291456 | tf_op jit(solution)/shard_map/all_to_all | solution.py:427
  41.1 107.1 %all-gather.7.cloned.1.call-start = ((), (), s32[]{:S(2)}) async-start(), calls=%async_computation.3 | async-start | bytes 6291456 | tf_op jit(solution)/shard_map/all_gather | solution.py:413
  41.2 23.3 %copy-start.22 = (bf16[128,2048]{1,0:T(8,128)(2,1)S(1)}, bf16[128,2048]{1,0:T(8,128)(2,1)}, u32[]{:S(2)}) copy-start(bf16[128,2048]{1,0:T(8,128)(2,1)} %copy-done.21) | copy-start | bytes 1572868
  42.5 21.9 %collective-permute-start.6 = (bf16[2,128,2048]{2,1,0:T(8,128)(2,1)S(1)}, bf16[2,128,2048]{2,1,0:T(8,128)(2,1)S(1)}, u32[]{:S(2)}, u32[]{:S(2)}) collective-permute-start(bf16[2,128,2048]{2,1,0:T(8,128)(2,1)S(1)} %pad_maximum_fusion.1), channel_id=1, source_target_pairs={{0,16},{16,0},{1,17},{17,1},{2,18},{18,2},{3,19},{19,3},{4,20},{20... | collective-permute-start | bytes 3145736 | tf_op jit(solution)/shard_map/ppermute | solution.py:414
  67.1 15.8 %collective-permute-start.3 = (bf16[2048,384]{1,0:T(8,128)(2,1)}, bf16[2048,384]{1,0:T(8,128)(2,1)}, u32[]{:S(2)}, u32[]{:S(2)}) collective-permute-start(bf16[2048,384]{1,0:T(8,128)(2,1)} %refs_0_.1), channel_id=1, source_target_pairs={{0,1},{1,0},{2,3},{3,2},{4,5},{5,4},{6,7},{7,6},{8,9},{9,8},{10,11... | collective-permute-start | bytes 4718600 | tf_op jit(solution)/shard_map/ppermute | solution.py:415
  70.9 12.0 %collective-permute-start.4 = (bf16[2048,384]{1,0:T(8,128)(2,1)}, bf16[2048,384]{1,0:T(8,128)(2,1)}, u32[]{:S(2)}, u32[]{:S(2)}) collective-permute-start(bf16[2048,384]{1,0:T(8,128)(2,1)} %refs_1_.1), channel_id=1, source_target_pairs={{0,1},{1,0},{2,3},{3,2},{4,5},{5,4},{6,7},{7,6},{8,9},{9,8},{10,11... | collective-permute-start | bytes 4718600 | tf_op jit(solution)/shard_map/ppermute | solution.py:415
  71.0 11.9 %collective-permute-start.5 = (bf16[384,2048]{1,0:T(8,128)(2,1)}, bf16[384,2048]{1,0:T(8,128)(2,1)}, u32[]{:S(2)}, u32[]{:S(2)}) collective-permute-start(bf16[384,2048]{1,0:T(8,128)(2,1)} %refs_2_.1), channel_id=1, source_target_pairs={{0,1},{1,0},{2,3},{3,2},{4,5},{5,4},{6,7},{7,6},{8,9},{9,8},{10,11... | collective-permute-start | bytes 4718600 | tf_op jit(solution)/shard_map/ppermute | solution.py:415
  71.4 30.8 %collective-permute-start.7 = (bf16[2,128,2048]{2,1,0:T(8,128)(2,1)}, bf16[2,128,2048]{2,1,0:T(8,128)(2,1)}, u32[]{:S(2)}, u32[]{:S(2)}) collective-permute-start(bf16[2,128,2048]{2,1,0:T(8,128)(2,1)} %bitcast.33), channel_id=1, source_target_pairs={{0,16},{16,0},{1,17},{17,1},{2,18},{18,2},{3,19},{19,3},{4,20},{20... | collective-permute-start | bytes 3145736 | tf_op jit(solution)/shard_map/ppermute | solution.py:414
  72.7 29.6 %collective-permute-start.8 = (bf16[128,2048]{1,0:T(8,128)(2,1)}, bf16[128,2048]{1,0:T(8,128)(2,1)}, u32[]{:S(2)}, u32[]{:S(2)}) collective-permute-start(bf16[128,2048]{1,0:T(8,128)(2,1)} %collective-permute-done.1), channel_id=1, source_target_pairs={{0,4},{4,0},{1,5},{5,1},{2,6},{6,2},{3,7},{7,3},{8,12},{12,8},{9,1... | collective-permute-start | bytes 1572872 | tf_op jit(solution)/shard_map/ppermute | solution.py:433
  109.4 25.1 %collective-permute-start.9 = (bf16[128,2048]{1,0:T(8,128)(2,1)}, bf16[128,2048]{1,0:T(8,128)(2,1)}, u32[]{:S(2)}, u32[]{:S(2)}) collective-permute-start(bf16[128,2048]{1,0:T(8,128)(2,1)} %collective-permute-done.8), channel_id=1, source_target_pairs={{0,2},{2,0},{1,3},{3,1},{4,6},{6,4},{5,7},{7,5},{8,10},{10,8},{9,1... | collective-permute-start | bytes 1572872 | tf_op jit(solution)/shard_map/ppermute | solution.py:440
  136.2 51.7 %copy-start.20 = (bf16[2,128,2048]{2,1,0:T(8,128)(2,1)}, bf16[2,128,2048]{2,1,0:T(8,128)(2,1)S(1)}, u32[]{:S(2)}) copy-start(bf16[2,128,2048]{2,1,0:T(8,128)(2,1)S(1)} %maximum_select_fusion.refs_6_) | copy-start | bytes 3145732
  148.2 39.7 %collective-permute-start.11 = (bf16[2,4,128,2048]{3,2,1,0:T(8,128)(2,1)}, bf16[2,4,128,2048]{3,2,1,0:T(8,128)(2,1)}, u32[]{:S(2)}, u32[]{:S(2)}) collective-permute-start(bf16[2,4,128,2048]{3,2,1,0:T(8,128)(2,1)} %bitcast.25), channel_id=1, source_target_pairs={{0,1},{1,0},{2,3},{3,2},{4,5},{5,4},{6,7},{7,6},{8,9},{9,8},{10,11... | collective-permute-start | bytes 12582920 | tf_op jit(solution)/shard_map/ppermute | solution.py:415
  148.7 39.3 %all-to-all-start.1 = ((bf16[8,48,2048]{2,1,0:T(8,128)(2,1)}), bf16[8,48,2048]{2,1,0:T(8,128)(2,1)S(1)}, u32[]{:S(2)}, u32[]{:S(2)}) async-start(bf16[8,48,2048]{2,1,0:T(8,128)(2,1)} %bitcast.16), calls=%async_computation.1 | async-start | bytes 3145728 | tf_op jit(solution)/shard_map/all_to_all | solution.py:450
  153.5 24.2 %collective-permute-start.14 = (bf16[2,128,2048]{2,1,0:T(8,128)(2,1)S(1)}, bf16[2,128,2048]{2,1,0:T(8,128)(2,1)}, u32[]{:S(2)}, u32[]{:S(2)}) collective-permute-start(bf16[2,128,2048]{2,1,0:T(8,128)(2,1)S(1)} %maximum_select_fusion.refs_6_), channel_id=1, source_target_pairs={{0,16},{16,0},{1,17},{17,1},{2,18},{18,2},{3,19},{19,3},{4,20},{20... | collective-permute-start | bytes 3145736 | tf_op jit(solution)/shard_map/ppermute | solution.py:414
  154.7 25.1 %collective-permute-start.12 = (bf16[2,128,2048]{2,1,0:T(8,128)(2,1)S(1)}, bf16[2,128,2048]{2,1,0:T(8,128)(2,1)}, u32[]{:S(2)}, u32[]{:S(2)}) collective-permute-start(bf16[2,128,2048]{2,1,0:T(8,128)(2,1)S(1)} %maximum_select_fusion.refs_6_), channel_id=1, source_target_pairs={{0,1},{1,0},{2,3},{3,2},{4,5},{5,4},{6,7},{7,6},{8,9},{9,8},{10,11... | collective-permute-start | bytes 3145736 | tf_op jit(solution)/shard_map/ppermute | solution.py:415
  155.6 24.2 %collective-permute-start.10 = (bf16[2,128,2048]{2,1,0:T(8,128)(2,1)}, bf16[2,128,2048]{2,1,0:T(8,128)(2,1)}, u32[]{:S(2)}, u32[]{:S(2)}) collective-permute-start(bf16[2,128,2048]{2,1,0:T(8,128)(2,1)} %bitcast.34), channel_id=1, source_target_pairs={{0,1},{1,0},{2,3},{3,2},{4,5},{5,4},{6,7},{7,6},{8,9},{9,8},{10,11... | collective-permute-start | bytes 3145736 | tf_op jit(solution)/shard_map/ppermute | solution.py:415
  155.6 24.2 %collective-permute-start.13 = (bf16[2,128,2048]{2,1,0:T(8,128)(2,1)}, bf16[2,128,2048]{2,1,0:T(8,128)(2,1)}, u32[]{:S(2)}, u32[]{:S(2)}) collective-permute-start(bf16[2,128,2048]{2,1,0:T(8,128)(2,1)} %collective-permute-done.7.refs_8_), channel_id=1, source_target_pairs={{0,1},{1,0},{2,3},{3,2},{4,5},{5,4},{6,7},{7,6},{8,9},{9,8},{10,11... | collective-permute-start | bytes 3145736 | tf_op jit(solution)/shard_map/ppermute | solution.py:415
  177.7 4.1 %collective-permute-start.15 = (bf16[2,128,2048]{2,1,0:T(8,128)(2,1)}, bf16[2,128,2048]{2,1,0:T(8,128)(2,1)}, u32[]{:S(2)}, u32[]{:S(2)}) collective-permute-start(bf16[2,128,2048]{2,1,0:T(8,128)(2,1)} %collective-permute-done.14.refs_14_), channel_id=1, source_target_pairs={{0,1},{1,0},{2,3},{3,2},{4,5},{5,4},{6,7},{7,6},{8,9},{9,8},{10,11... | collective-permute-start | bytes 3145736 | tf_op jit(solution)/shard_map/ppermute | solution.py:415
  189.1 26.5 %copy-start.1 = (bf16[128,4096]{1,0:T(8,128)(2,1)S(1)}, bf16[128,4096]{1,0:T(8,128)(2,1)}, u32[]{:S(2)}) copy-start(bf16[128,4096]{1,0:T(8,128)(2,1)} %param.21) | copy-start | bytes 3145732
  205.9 7.4 %collective-permute-start.16 = (bf16[2,128,256]{2,1,0:T(8,128)(2,1)}, bf16[2,128,256]{2,1,0:T(8,128)(2,1)S(1)}, u32[]{:S(2)}, u32[]{:S(2)}) collective-permute-start(bf16[2,128,256]{2,1,0:T(8,128)(2,1)} %get-tuple-element.99), channel_id=1, source_target_pairs={{1,0},{2,1},{3,2},{4,3},{5,4},{6,5},{7,6},{8,7},{9,8},{10,9},{11,1... | collective-permute-start | bytes 393224 | tf_op jit(solution)/shard_map/ppermute | solution.py:463
  (22 other events, 79.5 us)
Sparse Core Ops, SparseCore 0:
  10.2 23.0 all-gather.4
  67.2 80.9 all-gather.6

commit v19 on v16

--- a/solution.py
+++ b/solution.py
@@ -371,7 +371,7 @@
 def finish(kept, later):
     out = jax.ShapeDtypeStruct(kept.shape[1:], jnp.float32)
     return pl.pallas_call(
-        finish_kernel, out_shape=(out, out), compiler_params=params(60), cost_estimate=LIGHT, name="finish"
+        finish_kernel, out_shape=(out, out), compiler_params=params(16), cost_estimate=LIGHT, name="finish"
     )(kept, later)
 
 
@@ -440,10 +440,10 @@
     else:
         last_line = line(w_last)
     terms = experts(rows_in.reshape(owners * depth, 2 * width), *prepared)
-    terms, own_line, own_crossed, last_line, near_twin, far_twin = lax.optimization_barrier(
-        (terms, own_line, own_crossed, last_line, near_twin, far_twin)
-    )
-    last_crossed = cross(last_line)
+    terms, own_line, own_crossed, last_line, near_twin = lax.optimization_barrier(
+        (terms, own_line, own_crossed, last_line, near_twin)
+    )
+    last_crossed, far_twin = lax.optimization_barrier((cross(last_line), far_twin))
     back = lax.all_to_all(terms.reshape(owners, depth, width), chips, 0, 0, tiled=True)
     both = lambda *pieces: [w for piece in pieces for w in (piece, other_core(piece))]
 

time: 225 us -> 209 us (0.929)
  waiting for transfers between devices: 105 us -> 86.7 us
  starting transfers between devices: 31.7 us -> 34.9 us
    ppermute x4, waiting for transfers between devices: 36 us -> 21.1 us  [local(): cross = lambda w: lax.ppermute(w, 'groups', swap)]
    ppermute x1, waiting for transfers between devices: 12.7 us -> 5.54 us  [local(): w_last = lax.ppermute(w_far, 'near', swap)]
    ppermute x9, waiting for transfers between devices: 2.46 us -> 7.48 us  [local(): other_core = lambda w: lax.ppermute(w, 'core', swap)]
    all_to_all x1, waiting for transfers between devices: 5.14 us -> 1.68 us  [local(): lax.all_to_all(terms.reshape(owners, depth, width), chips, 0, 0, tiled=True)]
    unnamed x50 -> x48, local copies, waits for them, and re-layouts: 18.2 us -> 18.3 us
  transfers between devices with their start and end apart: 24 -> 24, of which waited for: 12 -> 11; matrix products, arithmetic and copies ran while one was open for 3% -> 3% of each run, Pallas kernels for 12% -> 13%
where the time goes in v19:
time: 209 us; the launch traced here: 205 us
  waiting for transfers between devices  86.7 us (41%)
  Pallas kernels  43.7 us (21%)
  starting transfers between devices  34.9 us (17%)
  local copies, waits for them, and re-layouts  19.3 us (9%)
  between operations  13.9 us (7%)
  other arithmetic  6.61 us (3%)
    ppermute x4, waiting for transfers between devices, local(): cross = lambda w: lax.ppermute(w, 'groups', swap)  21.1 us
    all_gather x3, waiting for transfers between devices, local(): line = lambda w: lax.all_gather(w, 'low', axis=0, tiled=False)  19.7 us
    unnamed x48, local copies, waits for them, and re-layouts  18.3 us
    pallas_call x1, Pallas kernels, tail(): pl.pallas_call(functools.partial(tail_kernel, (heads, tiles)), grid_spec=...  16.6 us
    ppermute x1, waiting for transfers between devices, local(): prev = lax.ppermute(jnp.concatenate([kv, seg_rows], axis=0), blk, onward)  15.4 us
    pallas_call x1, Pallas kernels, experts(): pl.pallas_call(functools.partial(expert_kernel, steps), grid=(steps + wid...  13 us
    ppermute x9, starting transfers between devices, local(): other_core = lambda w: lax.ppermute(w, 'core', swap)  9.62 us
    pallas_call x1, Pallas kernels, prepare_weights(): pl.pallas_call(weights_kernel, grid=(steps,), in_specs=[cols, cols, down]...  8.76 us
  transfers between devices with their start and end apart: 24, of which 11 were waited for; matrix products, arithmetic and copies ran while one was open for 3% of the time, Pallas kernels for 13%

profile of v19, /device:TPU:13, one launch (start us, length us, event | category | flops | bytes accessed | tf_op | source)
XLA Modules:
  0.0 205.1 jit_solution(16939906194582254366)
XLA Ops:
  9.5 2.3 %collective-permute-start.1 = (bf16[128,2048]{1,0:T(8,128)(2,1)}, bf16[128,2048]{1,0:T(8,128)(2,1)}, u32[]{:S(2)}, u32[]{:S(2)}) collective-permute-start(bf16[128,2048]{1,0:T(8,128)(2,1)} %constant_dynamic-slice_fusion), channel_id=1, source_target_pairs={{0,8},{8,0},{1,9},{9,1},{2,10},{10,2},{3,11},{11,3},{4,12},{12,4},... | collective-permute-start | bytes 1572872 | tf_op jit(solution)/shard_map/ppermute | solution.py:407
  18.1 3.2 %collective-permute-start.2 = (bf16[144,512]{1,0:T(8,128)(2,1)S(1)}, bf16[144,512]{1,0:T(8,128)(2,1)S(1)}, u32[]{:S(2)}, u32[]{:S(2)}) collective-permute-start(bf16[144,512]{1,0:T(8,128)(2,1)S(1)} %fusion.1), channel_id=1, source_target_pairs={{0,1},{1,2},{2,3},{3,4},{4,5},{5,6},{6,7},{7,8},{8,9},{9,10},{10,1... | collective-permute-start | bytes 442376 | tf_op jit(solution)/shard_map/ppermute | solution.py:420
  21.3 15.4 %collective-permute-done.2.prev_key_ref.prev_value_ref.prev_seg_ref = bf16[144,512]{1,0:T(8,128)(2,1)S(1)} collective-permute-done((bf16[144,512]{1,0:T(8,128)(2,1)S(1)}, bf16[144,512]{1,0:T(8,128)(2,1)S(1)}, u32[]{:S(2)}, u32[]{:S(2)}) %collective-permute-start.2) | collective-permute-done | bytes 147488 | tf_op jit(solution)/shard_map/ppermute | solution.py:420
  37.5 3.6 %all-to-all-start = ((bf16[8,48,4096]{2,1,0:T(8,128)(2,1)}), bf16[8,48,4096]{2,1,0:T(8,128)(2,1)S(1)}, u32[]{:S(2)}, u32[]{:S(2)}) async-start(bf16[8,48,4096]{2,1,0:T(8,128)(2,1)} %bitcast.25), calls=%async_computation | async-start | bytes 6291456 | tf_op jit(solution)/shard_map/all_to_all | solution.py:424
  42.4 9.7 %collective-permute-done.6 = bf16[128,2048]{1,0:T(8,128)(2,1)S(1)} collective-permute-done((bf16[128,2048]{1,0:T(8,128)(2,1)}, bf16[128,2048]{1,0:T(8,128)(2,1)S(1)}, u32[]{:S(2)}, u32[]{:S(2)}) %collective-permute-start.6) | collective-permute-done | bytes 524320 | tf_op jit(solution)/shard_map/ppermute | solution.py:411
  52.1 2.1 %pad_maximum_fusion = bf16[2,128,2048]{2,1,0:T(8,128)(2,1)} fusion(bf16[1,128,2048]{2,1,0:T(8,128)(2,1)S(1)} %bitcast.38, bf16[1,128,2048]{2,1,0:T(8,128)(2,1)} %bitcast.36), kind=kLoop, calls=%fused_computation.1 | loop fusion | flops 524288 | bytes 2097152 | tf_op jit(solution)/shard_map/stack | solution.py:426
  54.3 3.7 %collective-permute-start.3 = (bf16[2048,384]{1,0:T(8,128)(2,1)}, bf16[2048,384]{1,0:T(8,128)(2,1)}, u32[]{:S(2)}, u32[]{:S(2)}) collective-permute-start(bf16[2048,384]{1,0:T(8,128)(2,1)} %refs_0_.1), channel_id=1, source_target_pairs={{0,1},{1,0},{2,3},{3,2},{4,5},{5,4},{6,7},{7,6},{8,9},{9,8},{10,11... | collective-permute-start | bytes 4718600 | tf_op jit(solution)/shard_map/ppermute | solution.py:412
  60.0 11.5 %collective-permute-done.7 = bf16[128,2048]{1,0:T(8,128)(2,1)S(1)} collective-permute-done((bf16[128,2048]{1,0:T(8,128)(2,1)}, bf16[128,2048]{1,0:T(8,128)(2,1)S(1)}, u32[]{:S(2)}, u32[]{:S(2)}) %collective-permute-start.7) | collective-permute-done | bytes 524320 | tf_op jit(solution)/shard_map/ppermute | solution.py:411
  72.9 2.2 %pad_maximum_fusion.1 = bf16[2,128,2048]{2,1,0:T(8,128)(2,1)} fusion(bf16[1,128,2048]{2,1,0:T(8,128)(2,1)S(1)} %bitcast.37, bf16[1,128,2048]{2,1,0:T(8,128)(2,1)} %bitcast.18), kind=kLoop, calls=%fused_computation.2 | loop fusion | flops 524288 | bytes 2097152 | tf_op jit(solution)/shard_map/stack | solution.py:427
  76.6 3.5 %attention_shares.1 = (bf16[2,2048,256]{2,1,0:T(8,128)(2,1)S(1)}, bf16[2,256,2048]{2,1,0:T(8,128)(2,1)S(1)}, bf16[2,2048,128]{2,1,0:T(8,128)(2,1)S(1)}, bf16[2,2...) custom-call(bf16[128,4096]{1,0:T(8,128)(2,1)S(1)} %copy-done.8, bf16[128,256]{1,0:T(8,128)(2,1)S(1)} %copy-done.11, ...), custom_call_target="tpu_custom_call" | custom-call | tf_op jit(solution)/shard_map/attention_shares/pallas_call | solution.py:201
  87.9 8.8 %prepare_weights.1 = (bf16[3,2048,512]{2,1,0:T(8,128)(2,1)}, bf16[3,2048,256]{2,1,0:T(8,128)(2,1)}, bf16[3,512,2048]{2,1,0:T(8,128)(2,1)}) custom-call(bf16[2048,384]{1,0:T(8,128)(2,1)S(1)} %copy-done.5, bf16[2048,384]{1,0:T(8,128)(2,1)S(1)} %copy-done.6, bf16[384,2048]{1,0:T(8,128)(2,1)S(1)} %copy-done.7, bf16[2048,384]{1,0:T(8,128)(2,1)} %collective-permute-done.3.refs_3_, ...), custom_call_target="tpu_custom_call" | custom-call | tf_op jit(solution)/shard_map/prepare_weights/pallas_call | solution.py:94
  96.7 5.5 %collective-permute-done.9 = bf16[128,2048]{1,0:T(8,128)(2,1)} collective-permute-done((bf16[128,2048]{1,0:T(8,128)(2,1)}, bf16[128,2048]{1,0:T(8,128)(2,1)}, u32[]{:S(2)}, u32[]{:S(2)}) %collective-permute-start.9) | collective-permute-done | bytes 524320 | tf_op jit(solution)/shard_map/ppermute | solution.py:430
  102.2 7.2 %all-to-all-done = bf16[8,48,4096]{2,1,0:T(8,128)(2,1)S(1)} async-done(((bf16[8,48,4096]{2,1,0:T(8,128)(2,1)}), bf16[8,48,4096]{2,1,0:T(8,128)(2,1)S(1)}, u32[]{:S(2)}, u32[]{:S(2)}) %all-to-all-start) | async-done | bytes 3145760 | tf_op jit(solution)/shard_map/all_to_all | solution.py:424
  110.4 13.0 %expert_terms.1 = bf16[384,2048]{1,0:T(8,128)(2,1)} custom-call(bf16[384,4096]{1,0:T(8,128)(2,1)S(1)} %bitcast.24, bf16[3,2048,512]{2,1,0:T(8,128)(2,1)} %get-tuple-element.81.cols_ref, bf16[3,2048,256]{2,1,0:T(8,128)(2,1)} %get-tuple-element.82.down_ref, bf16[3,512,2048]{2,1,0:T(8,128)(2,1)} %get-tuple-element.83.back_ref), custom_call_target="tpu_custom_call" | custom-call | tf_op jit(solution)/shard_map/expert_terms/pallas_call | solution.py:145
  123.4 3.6 %collective-permute-done.10 = bf16[128,2048]{1,0:T(8,128)(2,1)} collective-permute-done((bf16[128,2048]{1,0:T(8,128)(2,1)}, bf16[128,2048]{1,0:T(8,128)(2,1)}, u32[]{:S(2)}, u32[]{:S(2)}) %collective-permute-start.10) | collective-permute-done | bytes 524320 | tf_op jit(solution)/shard_map/ppermute | solution.py:437
  127.0 1.7 maximum_select_fusion.refs_4_
  130.1 7.2 %all-to-all-start.1 = ((bf16[8,48,2048]{2,1,0:T(8,128)(2,1)}), bf16[8,48,2048]{2,1,0:T(8,128)(2,1)S(1)}, u32[]{:S(2)}, u32[]{:S(2)}) async-start(bf16[8,48,2048]{2,1,0:T(8,128)(2,1)} %bitcast.16), calls=%async_computation.1 | async-start | bytes 3145728 | tf_op jit(solution)/shard_map/all_to_all | solution.py:447
  137.3 4.1 %collective-permute-start.11 = (bf16[2,128,2048]{2,1,0:T(8,128)(2,1)}, bf16[2,128,2048]{2,1,0:T(8,128)(2,1)}, u32[]{:S(2)}, u32[]{:S(2)}) collective-permute-start(bf16[2,128,2048]{2,1,0:T(8,128)(2,1)} %bitcast.34), channel_id=1, source_target_pairs={{0,1},{1,0},{2,3},{3,2},{4,5},{5,4},{6,7},{7,6},{8,9},{9,8},{10,11... | collective-permute-start | bytes 3145736 | tf_op jit(solution)/shard_map/ppermute | solution.py:412
  141.3 19.6 %all-gather.11.cloned.1.call-done = bf16[4,128,2048]{2,1,0:T(8,128)(2,1)} async-done(((bf16[2,128,2048]{2,1,0:T(8,128)(2,1)}), bf16[4,128,2048]{2,1,0:T(8,128)(2,1)}) %all-gather.11.cloned.1.call-update) | async-done | bytes 2097168 | tf_op jit(solution)/shard_map/all_gather | solution.py:410
  162.6 6.0 %collective-permute-done.12.refs_3_ = bf16[2,128,2048]{2,1,0:T(8,128)(2,1)} collective-permute-done((bf16[2,128,2048]{2,1,0:T(8,128)(2,1)}, bf16[2,128,2048]{2,1,0:T(8,128)(2,1)}, u32[]{:S(2)}, u32[]{:S(2)}) %collective-permute-start.12) | collective-permute-done | bytes 1048608 | tf_op jit(solution)/shard_map/ppermute | solution.py:412
  170.1 1.7 all-to-all-done.1
  173.0 16.6 %tail_attention.1 = (bf16[128,2048]{1,0:T(8,128)(2,1)}, bf16[128,4096]{1,0:T(8,128)(2,1)}, f32[2,128,256]{2,1,0:T(8,128)}, bf16[2,128,256]{2,1,0:T(8,128)(2,1)}) custom-call(s32[3]{0:T(128)} %pad_add_fusion.place_info, bf16[384,2048]{1,0:T(8,128)(2,1)} %bitcast.28, bf16[128,384]{1,0:T(8,128)(2,1)} %copy-done.16, bf16[128,2048]{1,0:T(8,128)(2,1)} %grad_ref.3, ...), custom_call_target="tpu_custom_call" | custom-call | flops 2147483648 | bytes 23068672 | tf_op jit(solution)/shard_map/tail_attention/pallas_call | solution.py:320
  189.5 2.4 %collective-permute-start.18 = (bf16[2,128,256]{2,1,0:T(8,128)(2,1)}, bf16[2,128,256]{2,1,0:T(8,128)(2,1)S(1)}, u32[]{:S(2)}, u32[]{:S(2)}) collective-permute-start(bf16[2,128,256]{2,1,0:T(8,128)(2,1)} %get-tuple-element.103), channel_id=1, source_target_pairs={{1,0},{2,1},{3,2},{4,3},{5,4},{6,5},{7,6},{8,7},{9,8},{10,9},{11,1... | collective-permute-start | bytes 393224 | tf_op jit(solution)/shard_map/ppermute | solution.py:456
  192.0 5.0 %collective-permute-done.18.later_ref = bf16[2,128,256]{2,1,0:T(8,128)(2,1)S(1)} collective-permute-done((bf16[2,128,256]{2,1,0:T(8,128)(2,1)}, bf16[2,128,256]{2,1,0:T(8,128)(2,1)S(1)}, u32[]{:S(2)}, u32[]{:S(2)}) %collective-permute-start.18) | collective-permute-done | bytes 131104 | tf_op jit(solution)/shard_map/ppermute | solution.py:456
  (89 shorter events, 31.7 us)
Async XLA Ops:
  7.2 30.3 %all-gather.7.cloned.1.call-start = ((), (), s32[]{:S(2)}) async-start(), calls=%async_computation.2 | async-start | bytes 1572864 | tf_op jit(solution)/shard_map/all_gather | solution.py:410
  9.3 27.4 %collective-permute-start = (bf16[128,2048]{1,0:T(8,128)(2,1)}, bf16[128,2048]{1,0:T(8,128)(2,1)S(1)}, u32[]{:S(2)}, u32[]{:S(2)}) collective-permute-start(bf16[128,2048]{1,0:T(8,128)(2,1)} %constant_dynamic-slice_fusion), channel_id=1, source_target_pairs={{0,4},{4,0},{1,5},{5,1},{2,6},{6,2},{3,7},{7,3},{8,12},{12,8},{9,1... | collective-permute-start | bytes 1572872 | tf_op jit(solution)/shard_map/ppermute | solution.py:406
  9.5 28.0 %collective-permute-start.1 = (bf16[128,2048]{1,0:T(8,128)(2,1)}, bf16[128,2048]{1,0:T(8,128)(2,1)}, u32[]{:S(2)}, u32[]{:S(2)}) collective-permute-start(bf16[128,2048]{1,0:T(8,128)(2,1)} %constant_dynamic-slice_fusion), channel_id=1, source_target_pairs={{0,8},{8,0},{1,9},{9,1},{2,10},{10,2},{3,11},{11,3},{4,12},{12,4},... | collective-permute-start | bytes 1572872 | tf_op jit(solution)/shard_map/ppermute | solution.py:407
  18.1 18.6 %collective-permute-start.2 = (bf16[144,512]{1,0:T(8,128)(2,1)S(1)}, bf16[144,512]{1,0:T(8,128)(2,1)S(1)}, u32[]{:S(2)}, u32[]{:S(2)}) collective-permute-start(bf16[144,512]{1,0:T(8,128)(2,1)S(1)} %fusion.1), channel_id=1, source_target_pairs={{0,1},{1,2},{2,3},{3,4},{4,5},{5,6},{6,7},{7,8},{8,9},{9,10},{10,1... | collective-permute-start | bytes 442376 | tf_op jit(solution)/shard_map/ppermute | solution.py:420
  37.5 71.9 %all-to-all-start = ((bf16[8,48,4096]{2,1,0:T(8,128)(2,1)}), bf16[8,48,4096]{2,1,0:T(8,128)(2,1)S(1)}, u32[]{:S(2)}, u32[]{:S(2)}) async-start(bf16[8,48,4096]{2,1,0:T(8,128)(2,1)} %bitcast.25), calls=%async_computation | async-start | bytes 6291456 | tf_op jit(solution)/shard_map/all_to_all | solution.py:424
  41.1 87.6 %all-gather.9.cloned.1.call-start = ((), (), s32[]{:S(2)}) async-start(), calls=%async_computation.3 | async-start | bytes 3145728 | tf_op jit(solution)/shard_map/all_gather | solution.py:410
  41.2 10.9 %collective-permute-start.6 = (bf16[128,2048]{1,0:T(8,128)(2,1)}, bf16[128,2048]{1,0:T(8,128)(2,1)S(1)}, u32[]{:S(2)}, u32[]{:S(2)}) collective-permute-start(bf16[128,2048]{1,0:T(8,128)(2,1)} %copy-done.22), channel_id=1, source_target_pairs={{0,16},{16,0},{1,17},{17,1},{2,18},{18,2},{3,19},{19,3},{4,20},{20... | collective-permute-start | bytes 1572872 | tf_op jit(solution)/shard_map/ppermute | solution.py:411
  54.2 106.7 %all-gather.11.cloned.1.call-start = ((), (), s32[]{:S(2)}) async-start(), calls=%async_computation.4 | async-start | bytes 3145728 | tf_op jit(solution)/shard_map/all_gather | solution.py:410
  54.3 30.8 %collective-permute-start.3 = (bf16[2048,384]{1,0:T(8,128)(2,1)}, bf16[2048,384]{1,0:T(8,128)(2,1)}, u32[]{:S(2)}, u32[]{:S(2)}) collective-permute-start(bf16[2048,384]{1,0:T(8,128)(2,1)} %refs_0_.1), channel_id=1, source_target_pairs={{0,1},{1,0},{2,3},{3,2},{4,5},{5,4},{6,7},{7,6},{8,9},{9,8},{10,11... | collective-permute-start | bytes 4718600 | tf_op jit(solution)/shard_map/ppermute | solution.py:412
  58.0 27.0 %collective-permute-start.4 = (bf16[2048,384]{1,0:T(8,128)(2,1)}, bf16[2048,384]{1,0:T(8,128)(2,1)}, u32[]{:S(2)}, u32[]{:S(2)}) collective-permute-start(bf16[2048,384]{1,0:T(8,128)(2,1)} %refs_1_.1), channel_id=1, source_target_pairs={{0,1},{1,0},{2,3},{3,2},{4,5},{5,4},{6,7},{7,6},{8,9},{9,8},{10,11... | collective-permute-start | bytes 4718600 | tf_op jit(solution)/shard_map/ppermute | solution.py:412
  58.1 13.4 %collective-permute-start.7 = (bf16[128,2048]{1,0:T(8,128)(2,1)}, bf16[128,2048]{1,0:T(8,128)(2,1)S(1)}, u32[]{:S(2)}, u32[]{:S(2)}) collective-permute-start(bf16[128,2048]{1,0:T(8,128)(2,1)} %collective-permute-done.1), channel_id=1, source_target_pairs={{0,16},{16,0},{1,17},{17,1},{2,18},{18,2},{3,19},{19,3},{4,20},{20... | collective-permute-start | bytes 1572872 | tf_op jit(solution)/shard_map/ppermute | solution.py:411
  59.3 25.7 %collective-permute-start.5 = (bf16[384,2048]{1,0:T(8,128)(2,1)}, bf16[384,2048]{1,0:T(8,128)(2,1)}, u32[]{:S(2)}, u32[]{:S(2)}) collective-permute-start(bf16[384,2048]{1,0:T(8,128)(2,1)} %refs_2_.1), channel_id=1, source_target_pairs={{0,1},{1,0},{2,3},{3,2},{4,5},{5,4},{6,7},{7,6},{8,9},{9,8},{10,11... | collective-permute-start | bytes 4718600 | tf_op jit(solution)/shard_map/ppermute | solution.py:412
  71.5 30.7 %collective-permute-start.8 = (bf16[2,128,2048]{2,1,0:T(8,128)(2,1)}, bf16[2,128,2048]{2,1,0:T(8,128)(2,1)}, u32[]{:S(2)}, u32[]{:S(2)}) collective-permute-start(bf16[2,128,2048]{2,1,0:T(8,128)(2,1)} %bitcast.33), channel_id=1, source_target_pairs={{0,16},{16,0},{1,17},{17,1},{2,18},{18,2},{3,19},{19,3},{4,20},{20... | collective-permute-start | bytes 3145736 | tf_op jit(solution)/shard_map/ppermute | solution.py:411
  72.7 29.5 %collective-permute-start.9 = (bf16[128,2048]{1,0:T(8,128)(2,1)}, bf16[128,2048]{1,0:T(8,128)(2,1)}, u32[]{:S(2)}, u32[]{:S(2)}) collective-permute-start(bf16[128,2048]{1,0:T(8,128)(2,1)} %collective-permute-done.1), channel_id=1, source_target_pairs={{0,4},{4,0},{1,5},{5,1},{2,6},{6,2},{3,7},{7,3},{8,12},{12,8},{9,1... | collective-permute-start | bytes 1572872 | tf_op jit(solution)/shard_map/ppermute | solution.py:430
  109.4 17.6 %collective-permute-start.10 = (bf16[128,2048]{1,0:T(8,128)(2,1)}, bf16[128,2048]{1,0:T(8,128)(2,1)}, u32[]{:S(2)}, u32[]{:S(2)}) collective-permute-start(bf16[128,2048]{1,0:T(8,128)(2,1)} %collective-permute-done.9), channel_id=1, source_target_pairs={{0,2},{2,0},{1,3},{3,1},{4,6},{6,4},{5,7},{7,5},{8,10},{10,8},{9,1... | collective-permute-start | bytes 1572872 | tf_op jit(solution)/shard_map/ppermute | solution.py:437
  128.8 32.2 %collective-permute-start.14 = (bf16[2,128,2048]{2,1,0:T(8,128)(2,1)S(1)}, bf16[2,128,2048]{2,1,0:T(8,128)(2,1)}, u32[]{:S(2)}, u32[]{:S(2)}) collective-permute-start(bf16[2,128,2048]{2,1,0:T(8,128)(2,1)S(1)} %maximum_select_fusion.refs_4_), channel_id=1, source_target_pairs={{0,16},{16,0},{1,17},{17,1},{2,18},{18,2},{3,19},{19,3},{4,20},{20... | collective-permute-start | bytes 3145736 | tf_op jit(solution)/shard_map/ppermute | solution.py:411
  130.1 41.7 %all-to-all-start.1 = ((bf16[8,48,2048]{2,1,0:T(8,128)(2,1)}), bf16[8,48,2048]{2,1,0:T(8,128)(2,1)S(1)}, u32[]{:S(2)}, u32[]{:S(2)}) async-start(bf16[8,48,2048]{2,1,0:T(8,128)(2,1)} %bitcast.16), calls=%async_computation.1 | async-start | bytes 3145728 | tf_op jit(solution)/shard_map/all_to_all | solution.py:447
  137.3 24.7 %collective-permute-start.11 = (bf16[2,128,2048]{2,1,0:T(8,128)(2,1)}, bf16[2,128,2048]{2,1,0:T(8,128)(2,1)}, u32[]{:S(2)}, u32[]{:S(2)}) collective-permute-start(bf16[2,128,2048]{2,1,0:T(8,128)(2,1)} %bitcast.34), channel_id=1, source_target_pairs={{0,1},{1,0},{2,3},{3,2},{4,5},{5,4},{6,7},{7,6},{8,9},{9,8},{10,11... | collective-permute-start | bytes 3145736 | tf_op jit(solution)/shard_map/ppermute | solution.py:412
  141.3 28.7 %collective-permute-start.16 = (bf16[2,2,128,2048]{3,2,1,0:T(8,128)(2,1)}, bf16[2,2,128,2048]{3,2,1,0:T(8,128)(2,1)}, u32[]{:S(2)}, u32[]{:S(2)}) collective-permute-start(bf16[2,2,128,2048]{3,2,1,0:T(8,128)(2,1)} %bitcast.29), channel_id=1, source_target_pairs={{0,1},{1,0},{2,3},{3,2},{4,5},{5,4},{6,7},{7,6},{8,9},{9,8},{10,11... | collective-permute-start | bytes 6291464 | tf_op jit(solution)/shard_map/ppermute | solution.py:412
  161.0 10.8 %collective-permute-start.17 = (bf16[2,2,128,2048]{3,2,1,0:T(8,128)(2,1)}, bf16[2,2,128,2048]{3,2,1,0:T(8,128)(2,1)}, u32[]{:S(2)}, u32[]{:S(2)}) collective-permute-start(bf16[2,2,128,2048]{3,2,1,0:T(8,128)(2,1)} %bitcast.31), channel_id=1, source_target_pairs={{0,1},{1,0},{2,3},{3,2},{4,5},{5,4},{6,7},{7,6},{8,9},{9,8},{10,11... | collective-permute-start | bytes 6291464 | tf_op jit(solution)/shard_map/ppermute | solution.py:412
  161.4 7.1 %collective-permute-start.13 = (bf16[2,128,2048]{2,1,0:T(8,128)(2,1)S(1)}, bf16[2,128,2048]{2,1,0:T(8,128)(2,1)}, u32[]{:S(2)}, u32[]{:S(2)}) collective-permute-start(bf16[2,128,2048]{2,1,0:T(8,128)(2,1)S(1)} %maximum_select_fusion.refs_4_), channel_id=1, source_target_pairs={{0,1},{1,0},{2,3},{3,2},{4,5},{5,4},{6,7},{7,6},{8,9},{9,8},{10,11... | collective-permute-start | bytes 3145736 | tf_op jit(solution)/shard_map/ppermute | solution.py:412
  161.5 7.1 %collective-permute-start.12 = (bf16[2,128,2048]{2,1,0:T(8,128)(2,1)}, bf16[2,128,2048]{2,1,0:T(8,128)(2,1)}, u32[]{:S(2)}, u32[]{:S(2)}) collective-permute-start(bf16[2,128,2048]{2,1,0:T(8,128)(2,1)} %collective-permute-done.8.refs_2_), channel_id=1, source_target_pairs={{0,1},{1,0},{2,3},{3,2},{4,5},{5,4},{6,7},{7,6},{8,9},{9,8},{10,11... | collective-permute-start | bytes 3145736 | tf_op jit(solution)/shard_map/ppermute | solution.py:412
  162.0 8.1 %collective-permute-start.15 = (bf16[2,128,2048]{2,1,0:T(8,128)(2,1)}, bf16[2,128,2048]{2,1,0:T(8,128)(2,1)}, u32[]{:S(2)}, u32[]{:S(2)}) collective-permute-start(bf16[2,128,2048]{2,1,0:T(8,128)(2,1)} %collective-permute-done.14.refs_6_), channel_id=1, source_target_pairs={{0,1},{1,0},{2,3},{3,2},{4,5},{5,4},{6,7},{7,6},{8,9},{9,8},{10,11... | collective-permute-start | bytes 3145736 | tf_op jit(solution)/shard_map/ppermute | solution.py:412
  189.5 7.4 %collective-permute-start.18 = (bf16[2,128,256]{2,1,0:T(8,128)(2,1)}, bf16[2,128,256]{2,1,0:T(8,128)(2,1)S(1)}, u32[]{:S(2)}, u32[]{:S(2)}) collective-permute-start(bf16[2,128,256]{2,1,0:T(8,128)(2,1)} %get-tuple-element.103), channel_id=1, source_target_pairs={{1,0},{2,1},{3,2},{4,3},{5,4},{6,5},{7,6},{8,7},{9,8},{10,9},{11,1... | collective-permute-start | bytes 393224 | tf_op jit(solution)/shard_map/ppermute | solution.py:456
  (24 other events, 148.3 us)
Sparse Core Ops, SparseCore 0:
  10.2 23.0 all-gather.6
  54.4 51.7 all-gather.8
  107.7 53.2 all-gather.10

commit v20 on v19

--- a/solution.py
+++ b/solution.py
@@ -223,14 +223,14 @@
     plan, place_info, back_ref, place_ref, grad_ref, *refs
 ):
     heads, tiles = plan
-    own, last, twin, refs = refs[:4], refs[4:8], refs[8:12], refs[12:]
+    own, across, twin, refs = refs[:6], refs[6:12], refs[12:14], refs[14:]
     low_ref, turned_ref, q_ref, key_ref, value_ref, *refs = refs
     moe_ref, query_out, kept_out, sent_out, by_place, stream, held, sums = refs
     step = pl.program_id(0)
     tokens = query_out.shape[0]
     part_size = by_place.shape[2]
     size = own[0].shape[1]
-    mine, across = own[:2] + twin + last[:2], own[2:] + twin + last[2:]
+    mine, across = own[:4] + twin + own[4:], across[:4] + twin + across[4:]
     spread = part_size // size
     here, core = place_info[1], place_info[2]
 
@@ -323,8 +323,9 @@
             num_scalar_prefetch=1,
             grid=(steps + 1,),
             in_specs=[whole(back.shape), whole(place.shape), whole(moe_grad.shape)]
-            + ([piece(own_tile)] * 2 + [piece(other_tile)] * 2) * 2
-            + [twin] * 4
+            + [piece(own_tile)] * 6
+            + [piece(other_tile)] * 6
+            + [twin] * 2
             + [
                 rows((heads * tokens, span)),
                 pl.BlockSpec(
@@ -422,16 +423,19 @@
     rows, w_near, w_far, own_line, prev = lax.optimization_barrier((rows, w_near, w_far, own_line, prev))
 
     rows_in = lax.all_to_all(rows.reshape(owners, depth, 2 * width), chips, 0, 0, tiled=True)
-    near_crossed, far_crossed = cross(w_near), cross(w_far)
-    near_twin = line(jnp.stack([w_near, near_crossed]))
+    near_line = line(w_near)
+    far_crossed = cross(w_far)
     far_twin = line(jnp.stack([w_far, far_crossed]))
-    own_line, near_crossed, far_crossed = lax.optimization_barrier((own_line, near_crossed, far_crossed))
+    own_line, far_crossed = lax.optimization_barrier((own_line, far_crossed))
     own_crossed = cross(own_line)
+    near_crossed = cross(near_line)
     w_last = lax.ppermute(w_far, "near", swap)
     prepared = prepare_weights(own, other)
     attention = attention_shares(queries, key_heads, value_heads, prev, segs)
-    rows_in, prepared, attention, own_line, own_crossed, w_last = lax.optimization_barrier(
-        (rows_in, prepared, attention, own_line, own_crossed, w_last)
+    rows_in, prepared, attention, own_line, near_line, own_crossed, near_crossed, w_last = (
+        lax.optimization_barrier(
+            (rows_in, prepared, attention, own_line, near_line, own_crossed, near_crossed, w_last)
+        )
     )
     if low == 2:
         moved = lax.ppermute(w_last, "low", swap)
@@ -440,10 +444,10 @@
     else:
         last_line = line(w_last)
     terms = experts(rows_in.reshape(owners * depth, 2 * width), *prepared)
-    terms, own_line, own_crossed, last_line, near_twin = lax.optimization_barrier(
-        (terms, own_line, own_crossed, last_line, near_twin)
-    )
-    last_crossed, far_twin = lax.optimization_barrier((cross(last_line), far_twin))
+    terms, own_line, near_line, own_crossed, near_crossed, last_line, far_twin = lax.optimization_barrier(
+        (terms, own_line, near_line, own_crossed, near_crossed, last_line, far_twin)
+    )
+    last_crossed = cross(last_line)
     back = lax.all_to_all(terms.reshape(owners, depth, width), chips, 0, 0, tiled=True)
     both = lambda *pieces: [w for piece in pieces for w in (piece, other_core(piece))]
 
@@ -451,7 +455,7 @@
     moe_input_grad, query_grad, kept, sent = tail(
         jnp.stack([lax.axis_index("groups"), z, lax.axis_index("core")]).astype(jnp.int32),
         back.reshape(owners * depth, width), place, moe_grad,
-        both(own_line, own_crossed, last_line, last_crossed, near_twin, far_twin), *attention,
+        both(own_line, near_line, last_line, own_crossed, near_crossed, last_crossed, far_twin), *attention,
     )
     return (moe_input_grad, query_grad, *finish(kept, lax.ppermute(sent, blk, backward)))
 

time: 209 us -> 216 us (1.033)
  waiting for transfers between devices: 86.7 us -> 97.3 us
    ppermute x4, waiting for transfers between devices: 21.1 us -> 33.6 us  [local(): cross = lambda w: lax.ppermute(w, 'groups', swap)]
    all_to_all x1, waiting for transfers between devices: 7.21 us -> 0.01 us  [local(): lax.all_to_all(rows.reshape(owners, depth, 2 * width), chips, 0, 0, tiled...]
    ppermute x1, waiting for transfers between devices: 3.6 us -> 10.8 us  [local(): moved = lax.ppermute(w_last, 'low', swap)]
    ppermute x1, waiting for transfers between devices: 5.54 us -> 0.01 us  [local(): w_last = lax.ppermute(w_far, 'near', swap)]
    ppermute x9 -> x10, waiting for transfers between devices: 7.48 us -> 3.65 us  [local(): other_core = lambda w: lax.ppermute(w, 'core', swap)]
    all_gather x3, waiting for transfers between devices: 19.7 us -> 23.3 us  [local(): line = lambda w: lax.all_gather(w, 'low', axis=0, tiled=False)]
    all_to_all x1, waiting for transfers between devices: 1.68 us -> 4.83 us  [local(): lax.all_to_all(terms.reshape(owners, depth, width), chips, 0, 0, tiled=True)]
    ppermute x9 -> x10, starting transfers between devices: 9.62 us -> 8.32 us  [local(): other_core = lambda w: lax.ppermute(w, 'core', swap)]
  transfers between devices with their start and end apart: 24 -> 25, of which waited for: 11 -> 12; matrix products, arithmetic and copies ran while one was open for 3% -> 2% of each run, Pallas kernels for 13% -> 12%
where the time goes in v20:
time: 216 us; the launch traced here: 213 us
  waiting for transfers between devices  97.3 us (45%)
  Pallas kernels  43.7 us (20%)
  starting transfers between devices  33.8 us (16%)
  local copies, waits for them, and re-layouts  19.2 us (9%)
  between operations  14 us (6%)
  other arithmetic  4.64 us (2%)
    ppermute x4, waiting for transfers between devices, local(): cross = lambda w: lax.ppermute(w, 'groups', swap)  33.6 us
    all_gather x3, waiting for transfers between devices, local(): line = lambda w: lax.all_gather(w, 'low', axis=0, tiled=False)  23.3 us
    unnamed x52, local copies, waits for them, and re-layouts  18.3 us
    pallas_call x1, Pallas kernels, tail(): pl.pallas_call(functools.partial(tail_kernel, (heads, tiles)), grid_spec=...  16.7 us
    ppermute x1, waiting for transfers between devices, local(): prev = lax.ppermute(jnp.concatenate([kv, seg_rows], axis=0), blk, onward)  15.4 us
    pallas_call x1, Pallas kernels, experts(): pl.pallas_call(functools.partial(expert_kernel, steps), grid=(steps + wid...  12.6 us
    ppermute x1, waiting for transfers between devices, local(): moved = lax.ppermute(w_last, 'low', swap)  10.8 us
    pallas_call x1, Pallas kernels, prepare_weights(): pl.pallas_call(weights_kernel, grid=(steps,), in_specs=[cols, cols, down]...  8.99 us
  transfers between devices with their start and end apart: 25, of which 12 were waited for; matrix products, arithmetic and copies ran while one was open for 2% of the time, Pallas kernels for 12%

profile of v20, /device:TPU:13, one launch (start us, length us, event | category | flops | bytes accessed | tf_op | source)
XLA Modules:
  0.0 212.6 jit_solution(8212902262189095396)
XLA Ops:
  9.5 2.3 %collective-permute-start.1 = (bf16[128,2048]{1,0:T(8,128)(2,1)}, bf16[128,2048]{1,0:T(8,128)(2,1)S(1)}, u32[]{:S(2)}, u32[]{:S(2)}) collective-permute-start(bf16[128,2048]{1,0:T(8,128)(2,1)} %constant_dynamic-slice_fusion), channel_id=1, source_target_pairs={{0,8},{8,0},{1,9},{9,1},{2,10},{10,2},{3,11},{11,3},{4,12},{12,4},... | collective-permute-start | bytes 1572872 | tf_op jit(solution)/shard_map/ppermute | solution.py:408
  16.4 1.6 copy-done.2
  18.1 3.2 %collective-permute-start.2 = (bf16[144,512]{1,0:T(8,128)(2,1)S(1)}, bf16[144,512]{1,0:T(8,128)(2,1)S(1)}, u32[]{:S(2)}, u32[]{:S(2)}) collective-permute-start(bf16[144,512]{1,0:T(8,128)(2,1)S(1)} %fusion.1), channel_id=1, source_target_pairs={{0,1},{1,2},{2,3},{3,4},{4,5},{5,6},{6,7},{7,8},{8,9},{9,10},{10,1... | collective-permute-start | bytes 442376 | tf_op jit(solution)/shard_map/ppermute | solution.py:421
  21.3 15.4 %collective-permute-done.2.prev_key_ref.prev_value_ref.prev_seg_ref = bf16[144,512]{1,0:T(8,128)(2,1)S(1)} collective-permute-done((bf16[144,512]{1,0:T(8,128)(2,1)S(1)}, bf16[144,512]{1,0:T(8,128)(2,1)S(1)}, u32[]{:S(2)}, u32[]{:S(2)}) %collective-permute-start.2) | collective-permute-done | bytes 147488 | tf_op jit(solution)/shard_map/ppermute | solution.py:421
  37.5 3.6 %all-to-all-start = ((bf16[8,48,4096]{2,1,0:T(8,128)(2,1)}), bf16[8,48,4096]{2,1,0:T(8,128)(2,1)S(1)}, u32[]{:S(2)}, u32[]{:S(2)}) async-start(bf16[8,48,4096]{2,1,0:T(8,128)(2,1)} %bitcast.23), calls=%async_computation | async-start | bytes 6291456 | tf_op jit(solution)/shard_map/all_to_all | solution.py:425
  41.9 3.6 %collective-permute-start.3 = (bf16[2048,384]{1,0:T(8,128)(2,1)}, bf16[2048,384]{1,0:T(8,128)(2,1)}, u32[]{:S(2)}, u32[]{:S(2)}) collective-permute-start(bf16[2048,384]{1,0:T(8,128)(2,1)} %refs_0_.1), channel_id=1, source_target_pairs={{0,1},{1,0},{2,3},{3,2},{4,5},{5,4},{6,7},{7,6},{8,9},{9,8},{10,11... | collective-permute-start | bytes 4718600 | tf_op jit(solution)/shard_map/ppermute | solution.py:413
  47.3 12.1 %collective-permute-done.6 = bf16[128,2048]{1,0:T(8,128)(2,1)S(1)} collective-permute-done((bf16[128,2048]{1,0:T(8,128)(2,1)}, bf16[128,2048]{1,0:T(8,128)(2,1)S(1)}, u32[]{:S(2)}, u32[]{:S(2)}) %collective-permute-start.6) | collective-permute-done | bytes 524320 | tf_op jit(solution)/shard_map/ppermute | solution.py:412
  59.3 2.1 pad_maximum_fusion
  62.7 22.3 %all-gather.9.cloned.1.call-done = bf16[256,2048]{1,0:T(8,128)(2,1)} async-done(((bf16[128,2048]{1,0:T(8,128)(2,1)}), bf16[256,2048]{1,0:T(8,128)(2,1)}) %all-gather.9.cloned.1.call-update) | async-done | bytes 1048592 | tf_op jit(solution)/shard_map/all_gather | solution.py:411
  87.7 3.5 %attention_shares.1 = (bf16[2,2048,256]{2,1,0:T(8,128)(2,1)S(1)}, bf16[2,256,2048]{2,1,0:T(8,128)(2,1)S(1)}, bf16[2,2048,128]{2,1,0:T(8,128)(2,1)S(1)}, bf16[2,2...) custom-call(bf16[128,4096]{1,0:T(8,128)(2,1)S(1)} %copy-done.8, bf16[128,256]{1,0:T(8,128)(2,1)S(1)} %copy-done.11, ...), custom_call_target="tpu_custom_call" | custom-call | tf_op jit(solution)/shard_map/attention_shares/pallas_call | solution.py:201
  97.7 1.4 copy-done.7
  99.1 9.0 %prepare_weights.1 = (bf16[3,2048,512]{2,1,0:T(8,128)(2,1)}, bf16[3,2048,256]{2,1,0:T(8,128)(2,1)}, bf16[3,512,2048]{2,1,0:T(8,128)(2,1)}) custom-call(bf16[2048,384]{1,0:T(8,128)(2,1)S(1)} %copy-done.5, bf16[2048,384]{1,0:T(8,128)(2,1)S(1)} %copy-done.6, bf16[384,2048]{1,0:T(8,128)(2,1)S(1)} %copy-done.7, bf16[2048,384]{1,0:T(8,128)(2,1)} %collective-permute-done.3.refs_3_, ...), custom_call_target="tpu_custom_call" | custom-call | tf_op jit(solution)/shard_map/prepare_weights/pallas_call | solution.py:94
  108.1 1.5 collective-permute-done.8.refs_8_
  109.7 1.5 collective-permute-start.10
  111.2 12.6 %expert_terms.1 = bf16[384,2048]{1,0:T(8,128)(2,1)} custom-call(bf16[384,4096]{1,0:T(8,128)(2,1)S(1)} %bitcast.22, bf16[3,2048,512]{2,1,0:T(8,128)(2,1)} %get-tuple-element.83.cols_ref, bf16[3,2048,256]{2,1,0:T(8,128)(2,1)} %get-tuple-element.84.down_ref, bf16[3,512,2048]{2,1,0:T(8,128)(2,1)} %get-tuple-element.85.back_ref), custom_call_target="tpu_custom_call" | custom-call | tf_op jit(solution)/shard_map/expert_terms/pallas_call | solution.py:145
  123.8 10.8 %collective-permute-done.10 = bf16[128,2048]{1,0:T(8,128)(2,1)} collective-permute-done((bf16[128,2048]{1,0:T(8,128)(2,1)}, bf16[128,2048]{1,0:T(8,128)(2,1)}, u32[]{:S(2)}, u32[]{:S(2)}) %collective-permute-start.10) | collective-permute-done | bytes 524320 | tf_op jit(solution)/shard_map/ppermute | solution.py:441
  134.5 1.9 maximum_select_fusion.refs_4_
  137.4 7.2 %all-to-all-start.1 = ((bf16[8,48,2048]{2,1,0:T(8,128)(2,1)}), bf16[8,48,2048]{2,1,0:T(8,128)(2,1)S(1)}, u32[]{:S(2)}, u32[]{:S(2)}) async-start(bf16[8,48,2048]{2,1,0:T(8,128)(2,1)} %bitcast.17), calls=%async_computation.1 | async-start | bytes 3145728 | tf_op jit(solution)/shard_map/all_to_all | solution.py:451
  150.3 19.9 %collective-permute-done.16.refs_10_ = bf16[2,128,2048]{2,1,0:T(8,128)(2,1)} collective-permute-done((bf16[2,128,2048]{2,1,0:T(8,128)(2,1)S(1)}, bf16[2,128,2048]{2,1,0:T(8,128)(2,1)}, u32[]{:S(2)}, u32[]{:S(2)}) %collective-permute-start.16) | collective-permute-done | bytes 1048608 | tf_op jit(solution)/shard_map/ppermute | solution.py:412
  172.2 2.0 collective-permute-done.17.refs_11_
  174.2 4.8 %all-to-all-done.1 = bf16[8,48,2048]{2,1,0:T(8,128)(2,1)S(1)} async-done(((bf16[8,48,2048]{2,1,0:T(8,128)(2,1)}), bf16[8,48,2048]{2,1,0:T(8,128)(2,1)S(1)}, u32[]{:S(2)}, u32[]{:S(2)}) %all-to-all-start.1) | async-done | bytes 1572896 | tf_op jit(solution)/shard_map/all_to_all | solution.py:451
  180.2 16.7 %tail_attention.1 = (bf16[128,2048]{1,0:T(8,128)(2,1)}, bf16[128,4096]{1,0:T(8,128)(2,1)}, f32[2,128,256]{2,1,0:T(8,128)}, bf16[2,128,256]{2,1,0:T(8,128)(2,1)}) custom-call(s32[3]{0:T(128)} %pad_add_fusion.place_info, bf16[384,2048]{1,0:T(8,128)(2,1)} %bitcast.26, bf16[128,384]{1,0:T(8,128)(2,1)} %copy-done.16, bf16[128,2048]{1,0:T(8,128)(2,1)} %grad_ref.3, ...), custom_call_target="tpu_custom_call" | custom-call | flops 2147483648 | bytes 23068672 | tf_op jit(solution)/shard_map/tail_attention/pallas_call | solution.py:320
  197.0 2.4 %collective-permute-start.19 = (bf16[2,128,256]{2,1,0:T(8,128)(2,1)}, bf16[2,128,256]{2,1,0:T(8,128)(2,1)S(1)}, u32[]{:S(2)}, u32[]{:S(2)}) collective-permute-start(bf16[2,128,256]{2,1,0:T(8,128)(2,1)} %get-tuple-element.107), channel_id=1, source_target_pairs={{1,0},{2,1},{3,2},{4,3},{5,4},{6,5},{7,6},{8,7},{9,8},{10,9},{11,1... | collective-permute-start | bytes 393224 | tf_op jit(solution)/shard_map/ppermute | solution.py:460
  199.4 5.0 %collective-permute-done.19.later_ref = bf16[2,128,256]{2,1,0:T(8,128)(2,1)S(1)} collective-permute-done((bf16[2,128,256]{2,1,0:T(8,128)(2,1)}, bf16[2,128,256]{2,1,0:T(8,128)(2,1)S(1)}, u32[]{:S(2)}, u32[]{:S(2)}) %collective-permute-start.19) | collective-permute-done | bytes 131104 | tf_op jit(solution)/shard_map/ppermute | solution.py:460
  (94 shorter events, 32.0 us)
Async XLA Ops:
  7.2 29.5 %all-gather.7.cloned.1.call-start = ((), (), s32[]{:S(2)}) async-start(), calls=%async_computation.2 | async-start | bytes 1572864 | tf_op jit(solution)/shard_map/all_gather | solution.py:411
  9.3 27.4 %collective-permute-start = (bf16[128,2048]{1,0:T(8,128)(2,1)}, bf16[128,2048]{1,0:T(8,128)(2,1)}, u32[]{:S(2)}, u32[]{:S(2)}) collective-permute-start(bf16[128,2048]{1,0:T(8,128)(2,1)} %constant_dynamic-slice_fusion), channel_id=1, source_target_pairs={{0,4},{4,0},{1,5},{5,1},{2,6},{6,2},{3,7},{7,3},{8,12},{12,8},{9,1... | collective-permute-start | bytes 1572872 | tf_op jit(solution)/shard_map/ppermute | solution.py:407
  9.5 27.2 %collective-permute-start.1 = (bf16[128,2048]{1,0:T(8,128)(2,1)}, bf16[128,2048]{1,0:T(8,128)(2,1)S(1)}, u32[]{:S(2)}, u32[]{:S(2)}) collective-permute-start(bf16[128,2048]{1,0:T(8,128)(2,1)} %constant_dynamic-slice_fusion), channel_id=1, source_target_pairs={{0,8},{8,0},{1,9},{9,1},{2,10},{10,2},{3,11},{11,3},{4,12},{12,4},... | collective-permute-start | bytes 1572872 | tf_op jit(solution)/shard_map/ppermute | solution.py:408
  18.1 18.6 %collective-permute-start.2 = (bf16[144,512]{1,0:T(8,128)(2,1)S(1)}, bf16[144,512]{1,0:T(8,128)(2,1)S(1)}, u32[]{:S(2)}, u32[]{:S(2)}) collective-permute-start(bf16[144,512]{1,0:T(8,128)(2,1)S(1)} %fusion.1), channel_id=1, source_target_pairs={{0,1},{1,2},{2,3},{3,4},{4,5},{5,6},{6,7},{7,8},{8,9},{9,10},{10,1... | collective-permute-start | bytes 442376 | tf_op jit(solution)/shard_map/ppermute | solution.py:421
  37.5 72.2 %all-to-all-start = ((bf16[8,48,4096]{2,1,0:T(8,128)(2,1)}), bf16[8,48,4096]{2,1,0:T(8,128)(2,1)S(1)}, u32[]{:S(2)}, u32[]{:S(2)}) async-start(bf16[8,48,4096]{2,1,0:T(8,128)(2,1)} %bitcast.23), calls=%async_computation | async-start | bytes 6291456 | tf_op jit(solution)/shard_map/all_to_all | solution.py:425
  41.1 43.9 %all-gather.9.cloned.1.call-start = ((), (), s32[]{:S(2)}) async-start(), calls=%async_computation.3 | async-start | bytes 1572864 | tf_op jit(solution)/shard_map/all_gather | solution.py:411
  41.9 95.5 %all-gather.11.cloned.1.call-start = ((), (), s32[]{:S(2)}) async-start(), calls=%async_computation.4 | async-start | bytes 3145728 | tf_op jit(solution)/shard_map/all_gather | solution.py:411
  41.9 44.3 %collective-permute-start.3 = (bf16[2048,384]{1,0:T(8,128)(2,1)}, bf16[2048,384]{1,0:T(8,128)(2,1)}, u32[]{:S(2)}, u32[]{:S(2)}) collective-permute-start(bf16[2048,384]{1,0:T(8,128)(2,1)} %refs_0_.1), channel_id=1, source_target_pairs={{0,1},{1,0},{2,3},{3,2},{4,5},{5,4},{6,7},{7,6},{8,9},{9,8},{10,11... | collective-permute-start | bytes 4718600 | tf_op jit(solution)/shard_map/ppermute | solution.py:413
  45.5 13.8 %collective-permute-start.6 = (bf16[128,2048]{1,0:T(8,128)(2,1)}, bf16[128,2048]{1,0:T(8,128)(2,1)S(1)}, u32[]{:S(2)}, u32[]{:S(2)}) collective-permute-start(bf16[128,2048]{1,0:T(8,128)(2,1)} %copy-done.24), channel_id=1, source_target_pairs={{0,16},{16,0},{1,17},{17,1},{2,18},{18,2},{3,19},{19,3},{4,20},{20... | collective-permute-start | bytes 1572872 | tf_op jit(solution)/shard_map/ppermute | solution.py:412
  46.8 49.6 %collective-permute-start.4 = (bf16[2048,384]{1,0:T(8,128)(2,1)}, bf16[2048,384]{1,0:T(8,128)(2,1)}, u32[]{:S(2)}, u32[]{:S(2)}) collective-permute-start(bf16[2048,384]{1,0:T(8,128)(2,1)} %refs_1_.1), channel_id=1, source_target_pairs={{0,1},{1,0},{2,3},{3,2},{4,5},{5,4},{6,7},{7,6},{8,9},{9,8},{10,11... | collective-permute-start | bytes 4718600 | tf_op jit(solution)/shard_map/ppermute | solution.py:413
  47.1 49.2 %collective-permute-start.5 = (bf16[384,2048]{1,0:T(8,128)(2,1)}, bf16[384,2048]{1,0:T(8,128)(2,1)}, u32[]{:S(2)}, u32[]{:S(2)}) collective-permute-start(bf16[384,2048]{1,0:T(8,128)(2,1)} %refs_2_.1), channel_id=1, source_target_pairs={{0,1},{1,0},{2,3},{3,2},{4,5},{5,4},{6,7},{7,6},{8,9},{9,8},{10,11... | collective-permute-start | bytes 4718600 | tf_op jit(solution)/shard_map/ppermute | solution.py:413
  61.5 46.7 %collective-permute-start.7 = (bf16[2,128,2048]{2,1,0:T(8,128)(2,1)}, bf16[2,128,2048]{2,1,0:T(8,128)(2,1)}, u32[]{:S(2)}, u32[]{:S(2)}) collective-permute-start(bf16[2,128,2048]{2,1,0:T(8,128)(2,1)} %bitcast.29), channel_id=1, source_target_pairs={{0,16},{16,0},{1,17},{17,1},{2,18},{18,2},{3,19},{19,3},{4,20},{20... | collective-permute-start | bytes 3145736 | tf_op jit(solution)/shard_map/ppermute | solution.py:412
  85.1 24.6 %collective-permute-start.8 = (bf16[2,128,2048]{2,1,0:T(8,128)(2,1)}, bf16[2,128,2048]{2,1,0:T(8,128)(2,1)}, u32[]{:S(2)}, u32[]{:S(2)}) collective-permute-start(bf16[2,128,2048]{2,1,0:T(8,128)(2,1)} %bitcast.32), channel_id=1, source_target_pairs={{0,16},{16,0},{1,17},{17,1},{2,18},{18,2},{3,19},{19,3},{4,20},{20... | collective-permute-start | bytes 3145736 | tf_op jit(solution)/shard_map/ppermute | solution.py:412
  86.3 21.9 %collective-permute-start.9 = (bf16[128,2048]{1,0:T(8,128)(2,1)}, bf16[128,2048]{1,0:T(8,128)(2,1)}, u32[]{:S(2)}, u32[]{:S(2)}) collective-permute-start(bf16[128,2048]{1,0:T(8,128)(2,1)} %copy-done.24), channel_id=1, source_target_pairs={{0,4},{4,0},{1,5},{5,1},{2,6},{6,2},{3,7},{7,3},{8,12},{12,8},{9,1... | collective-permute-start | bytes 1572872 | tf_op jit(solution)/shard_map/ppermute | solution.py:432
  109.7 24.9 %collective-permute-start.10 = (bf16[128,2048]{1,0:T(8,128)(2,1)}, bf16[128,2048]{1,0:T(8,128)(2,1)}, u32[]{:S(2)}, u32[]{:S(2)}) collective-permute-start(bf16[128,2048]{1,0:T(8,128)(2,1)} %collective-permute-done.9), channel_id=1, source_target_pairs={{0,2},{2,0},{1,3},{3,1},{4,6},{6,4},{5,7},{7,5},{8,10},{10,8},{9,1... | collective-permute-start | bytes 1572872 | tf_op jit(solution)/shard_map/ppermute | solution.py:441
  137.4 41.7 %all-to-all-start.1 = ((bf16[8,48,2048]{2,1,0:T(8,128)(2,1)}), bf16[8,48,2048]{2,1,0:T(8,128)(2,1)S(1)}, u32[]{:S(2)}, u32[]{:S(2)}) async-start(bf16[8,48,2048]{2,1,0:T(8,128)(2,1)} %bitcast.17), calls=%async_computation.1 | async-start | bytes 3145728 | tf_op jit(solution)/shard_map/all_to_all | solution.py:451
  145.9 4.0 %collective-permute-start.12 = (bf16[2,128,2048]{2,1,0:T(8,128)(2,1)}, bf16[2,128,2048]{2,1,0:T(8,128)(2,1)S(1)}, u32[]{:S(2)}, u32[]{:S(2)}) collective-permute-start(bf16[2,128,2048]{2,1,0:T(8,128)(2,1)} %bitcast.33), channel_id=1, source_target_pairs={{0,1},{1,0},{2,3},{3,2},{4,5},{5,4},{6,7},{7,6},{8,9},{9,8},{10,11... | collective-permute-start | bytes 3145736 | tf_op jit(solution)/shard_map/ppermute | solution.py:413
  145.9 24.3 %collective-permute-start.16 = (bf16[2,128,2048]{2,1,0:T(8,128)(2,1)S(1)}, bf16[2,128,2048]{2,1,0:T(8,128)(2,1)}, u32[]{:S(2)}, u32[]{:S(2)}) collective-permute-start(bf16[2,128,2048]{2,1,0:T(8,128)(2,1)S(1)} %maximum_select_fusion.refs_4_), channel_id=1, source_target_pairs={{0,16},{16,0},{1,17},{17,1},{2,18},{18,2},{3,19},{19,3},{4,20},{20... | collective-permute-start | bytes 3145736 | tf_op jit(solution)/shard_map/ppermute | solution.py:412
  147.1 27.1 %collective-permute-start.18 = (bf16[2,2,128,2048]{3,2,1,0:T(8,128)(2,1)}, bf16[2,2,128,2048]{3,2,1,0:T(8,128)(2,1)}, u32[]{:S(2)}, u32[]{:S(2)}) collective-permute-start(bf16[2,2,128,2048]{3,2,1,0:T(8,128)(2,1)} %bitcast.27), channel_id=1, source_target_pairs={{0,1},{1,0},{2,3},{3,2},{4,5},{5,4},{6,7},{7,6},{8,9},{9,8},{10,11... | collective-permute-start | bytes 6291464 | tf_op jit(solution)/shard_map/ppermute | solution.py:413
  147.9 24.3 %collective-permute-start.13 = (bf16[2,128,2048]{2,1,0:T(8,128)(2,1)S(1)}, bf16[2,128,2048]{2,1,0:T(8,128)(2,1)}, u32[]{:S(2)}, u32[]{:S(2)}) collective-permute-start(bf16[2,128,2048]{2,1,0:T(8,128)(2,1)S(1)} %maximum_select_fusion.refs_4_), channel_id=1, source_target_pairs={{0,1},{1,0},{2,3},{3,2},{4,5},{5,4},{6,7},{7,6},{8,9},{9,8},{10,11... | collective-permute-start | bytes 3145736 | tf_op jit(solution)/shard_map/ppermute | solution.py:413
  148.4 23.8 %collective-permute-start.14 = (bf16[2,128,2048]{2,1,0:T(8,128)(2,1)}, bf16[2,128,2048]{2,1,0:T(8,128)(2,1)}, u32[]{:S(2)}, u32[]{:S(2)}) collective-permute-start(bf16[2,128,2048]{2,1,0:T(8,128)(2,1)} %collective-permute-done.7.refs_6_), channel_id=1, source_target_pairs={{0,1},{1,0},{2,3},{3,2},{4,5},{5,4},{6,7},{7,6},{8,9},{9,8},{10,11... | collective-permute-start | bytes 3145736 | tf_op jit(solution)/shard_map/ppermute | solution.py:413
  149.9 22.3 %collective-permute-start.15 = (bf16[2,128,2048]{2,1,0:T(8,128)(2,1)}, bf16[2,128,2048]{2,1,0:T(8,128)(2,1)}, u32[]{:S(2)}, u32[]{:S(2)}) collective-permute-start(bf16[2,128,2048]{2,1,0:T(8,128)(2,1)} %collective-permute-done.8.refs_8_), channel_id=1, source_target_pairs={{0,1},{1,0},{2,3},{3,2},{4,5},{5,4},{6,7},{7,6},{8,9},{9,8},{10,11... | collective-permute-start | bytes 3145736 | tf_op jit(solution)/shard_map/ppermute | solution.py:413
  170.2 4.0 %collective-permute-start.17 = (bf16[2,128,2048]{2,1,0:T(8,128)(2,1)}, bf16[2,128,2048]{2,1,0:T(8,128)(2,1)}, u32[]{:S(2)}, u32[]{:S(2)}) collective-permute-start(bf16[2,128,2048]{2,1,0:T(8,128)(2,1)} %collective-permute-done.16.refs_10_), channel_id=1, source_target_pairs={{0,1},{1,0},{2,3},{3,2},{4,5},{5,4},{6,7},{7,6},{8,9},{9,8},{10,11... | collective-permute-start | bytes 3145736 | tf_op jit(solution)/shard_map/ppermute | solution.py:413
  197.0 7.4 %collective-permute-start.19 = (bf16[2,128,256]{2,1,0:T(8,128)(2,1)}, bf16[2,128,256]{2,1,0:T(8,128)(2,1)S(1)}, u32[]{:S(2)}, u32[]{:S(2)}) collective-permute-start(bf16[2,128,256]{2,1,0:T(8,128)(2,1)} %get-tuple-element.107), channel_id=1, source_target_pairs={{1,0},{2,1},{3,2},{4,3},{5,4},{6,5},{7,6},{8,7},{9,8},{10,9},{11,1... | collective-permute-start | bytes 393224 | tf_op jit(solution)/shard_map/ppermute | solution.py:460
  (27 other events, 194.1 us)
Sparse Core Ops, SparseCore 0:
  10.2 23.0 all-gather.6
  43.5 41.4 all-gather.8
  87.2 50.1 all-gather.10

commit v21 on v19

--- a/solution.py
+++ b/solution.py
@@ -403,8 +403,8 @@
 
     share_cols = w_out.shape[1] // parts
     w_share = lax.dynamic_slice_in_dim(w_out, lax.axis_index("groups") * share_cols, share_cols, 1)
+    w_far = lax.ppermute(w_share, "far", swap)
     w_near = lax.ppermute(w_share, "near", swap)
-    w_far = lax.ppermute(w_share, "far", swap)
 
     rows, place = pick(routes, route_weight, moe_input, moe_grad, owners, depth)
     line = lambda w: lax.all_gather(w, "low", axis=0, tiled=False)
@@ -430,8 +430,8 @@
     w_last = lax.ppermute(w_far, "near", swap)
     prepared = prepare_weights(own, other)
     attention = attention_shares(queries, key_heads, value_heads, prev, segs)
-    rows_in, prepared, attention, own_line, own_crossed, w_last = lax.optimization_barrier(
-        (rows_in, prepared, attention, own_line, own_crossed, w_last)
+    rows_in, prepared, attention, own_line, own_crossed = lax.optimization_barrier(
+        (rows_in, prepared, attention, own_line, own_crossed)
     )
     if low == 2:
         moved = lax.ppermute(w_last, "low", swap)

time: 209 us -> 218 us (1.043)
  waiting for transfers between devices: 86.7 us -> 91.8 us
  starting transfers between devices: 34.9 us -> 37.1 us
    ppermute x1, waiting for transfers between devices: 5.54 us -> 26.5 us  [local(): w_last = lax.ppermute(w_far, 'near', swap)]
    all_gather x3, waiting for transfers between devices: 19.7 us -> 0.01 us  [local(): line = lambda w: lax.all_gather(w, 'low', axis=0, tiled=False)]
    ppermute x4, waiting for transfers between devices: 21.1 us -> 32.4 us  [local(): cross = lambda w: lax.ppermute(w, 'groups', swap)]
    all_to_all x1, waiting for transfers between devices: 7.21 us -> 0.01 us  [local(): lax.all_to_all(rows.reshape(owners, depth, 2 * width), chips, 0, 0, tiled...]
    ppermute x9, starting transfers between devices: 9.62 us -> 14.1 us  [local(): other_core = lambda w: lax.ppermute(w, 'core', swap)]
    all_to_all x1, waiting for transfers between devices: 1.68 us -> 5.57 us  [local(): lax.all_to_all(terms.reshape(owners, depth, width), chips, 0, 0, tiled=True)]
    ppermute x1, waiting for transfers between devices: 3.6 us -> 0.01 us  [local(): moved = lax.ppermute(w_last, 'low', swap)]
    all_to_all x1, starting transfers between devices: 7.21 us -> 5.02 us  [local(): lax.all_to_all(terms.reshape(owners, depth, width), chips, 0, 0, tiled=True)]
  transfers between devices with their start and end apart: 24 -> 24, of which waited for: 11 -> 9; matrix products, arithmetic and copies ran while one was open for 3% -> 4% of each run, Pallas kernels for 13% -> 12%
where the time goes in v21:
time: 218 us; the launch traced here: 214 us
  waiting for transfers between devices  91.8 us (42%)
  Pallas kernels  42.7 us (20%)
  starting transfers between devices  37.1 us (17%)
  local copies, waits for them, and re-layouts  20.5 us (9%)
  between operations  13.9 us (6%)
  other arithmetic  7.67 us (4%)
    ppermute x4, waiting for transfers between devices, local(): cross = lambda w: lax.ppermute(w, 'groups', swap)  32.4 us
    ppermute x1, waiting for transfers between devices, local(): w_last = lax.ppermute(w_far, 'near', swap)  26.5 us
    unnamed x50, local copies, waits for them, and re-layouts  19.6 us
    pallas_call x1, Pallas kernels, tail(): pl.pallas_call(functools.partial(tail_kernel, (heads, tiles)), grid_spec=...  16.6 us
    ppermute x1, waiting for transfers between devices, local(): prev = lax.ppermute(jnp.concatenate([kv, seg_rows], axis=0), blk, onward)  15.4 us
    ppermute x9, starting transfers between devices, local(): other_core = lambda w: lax.ppermute(w, 'core', swap)  14.1 us
    pallas_call x1, Pallas kernels, experts(): pl.pallas_call(functools.partial(expert_kernel, steps), grid=(steps + wid...  11.7 us
    pallas_call x1, Pallas kernels, prepare_weights(): pl.pallas_call(weights_kernel, grid=(steps,), in_specs=[cols, cols, down]...  8.98 us
  transfers between devices with their start and end apart: 24, of which 9 were waited for; matrix products, arithmetic and copies ran while one was open for 4% of the time, Pallas kernels for 12%

profile of v21, /device:TPU:13, one launch (start us, length us, event | category | flops | bytes accessed | tf_op | source)
XLA Modules:
  0.0 213.7 jit_solution(15693818125828261218)
XLA Ops:
  9.5 2.3 %collective-permute-start.1 = (bf16[128,2048]{1,0:T(8,128)(2,1)}, bf16[128,2048]{1,0:T(8,128)(2,1)}, u32[]{:S(2)}, u32[]{:S(2)}) collective-permute-start(bf16[128,2048]{1,0:T(8,128)(2,1)} %constant_dynamic-slice_fusion), channel_id=1, source_target_pairs={{0,8},{8,0},{1,9},{9,1},{2,10},{10,2},{3,11},{11,3},{4,12},{12,4},... | collective-permute-start | bytes 1572872 | tf_op jit(solution)/shard_map/ppermute | solution.py:406
  16.4 1.6 copy-done.3
  18.1 3.2 %collective-permute-start.2 = (bf16[144,512]{1,0:T(8,128)(2,1)S(1)}, bf16[144,512]{1,0:T(8,128)(2,1)S(1)}, u32[]{:S(2)}, u32[]{:S(2)}) collective-permute-start(bf16[144,512]{1,0:T(8,128)(2,1)S(1)} %fusion.1), channel_id=1, source_target_pairs={{0,1},{1,2},{2,3},{3,4},{4,5},{5,6},{6,7},{7,8},{8,9},{9,10},{10,1... | collective-permute-start | bytes 442376 | tf_op jit(solution)/shard_map/ppermute | solution.py:420
  21.3 15.4 %collective-permute-done.2.prev_key_ref.prev_value_ref.prev_seg_ref = bf16[144,512]{1,0:T(8,128)(2,1)S(1)} collective-permute-done((bf16[144,512]{1,0:T(8,128)(2,1)S(1)}, bf16[144,512]{1,0:T(8,128)(2,1)S(1)}, u32[]{:S(2)}, u32[]{:S(2)}) %collective-permute-start.2) | collective-permute-done | bytes 147488 | tf_op jit(solution)/shard_map/ppermute | solution.py:420
  37.5 3.6 %all-to-all-start = ((bf16[8,48,4096]{2,1,0:T(8,128)(2,1)}), bf16[8,48,4096]{2,1,0:T(8,128)(2,1)S(1)}, u32[]{:S(2)}, u32[]{:S(2)}) async-start(bf16[8,48,4096]{2,1,0:T(8,128)(2,1)} %bitcast.26), calls=%async_computation | async-start | bytes 6291456 | tf_op jit(solution)/shard_map/all_to_all | solution.py:424
  42.5 9.7 %collective-permute-done.6 = bf16[128,2048]{1,0:T(8,128)(2,1)S(1)} collective-permute-done((bf16[128,2048]{1,0:T(8,128)(2,1)}, bf16[128,2048]{1,0:T(8,128)(2,1)S(1)}, u32[]{:S(2)}, u32[]{:S(2)}) %collective-permute-start.6) | collective-permute-done | bytes 524320 | tf_op jit(solution)/shard_map/ppermute | solution.py:411
  52.1 2.1 pad_maximum_fusion
  54.3 3.7 %collective-permute-start.3 = (bf16[2048,384]{1,0:T(8,128)(2,1)}, bf16[2048,384]{1,0:T(8,128)(2,1)}, u32[]{:S(2)}, u32[]{:S(2)}) collective-permute-start(bf16[2048,384]{1,0:T(8,128)(2,1)} %refs_0_.1), channel_id=1, source_target_pairs={{0,1},{1,0},{2,3},{3,2},{4,5},{5,4},{6,7},{7,6},{8,9},{9,8},{10,11... | collective-permute-start | bytes 4718600 | tf_op jit(solution)/shard_map/ppermute | solution.py:412
  60.0 12.4 %collective-permute-done.7 = bf16[128,2048]{1,0:T(8,128)(2,1)S(1)} collective-permute-done((bf16[128,2048]{1,0:T(8,128)(2,1)}, bf16[128,2048]{1,0:T(8,128)(2,1)S(1)}, u32[]{:S(2)}, u32[]{:S(2)}) %collective-permute-start.7) | collective-permute-done | bytes 524320 | tf_op jit(solution)/shard_map/ppermute | solution.py:411
  73.6 2.1 pad_maximum_fusion.1
  75.7 26.5 %collective-permute-done.9 = bf16[128,2048]{1,0:T(8,128)(2,1)} collective-permute-done((bf16[128,2048]{1,0:T(8,128)(2,1)}, bf16[128,2048]{1,0:T(8,128)(2,1)}, u32[]{:S(2)}, u32[]{:S(2)}) %collective-permute-start.9) | collective-permute-done | bytes 524320 | tf_op jit(solution)/shard_map/ppermute | solution.py:430
  104.2 3.5 %attention_shares.1 = (bf16[2,2048,256]{2,1,0:T(8,128)(2,1)S(1)}, bf16[2,256,2048]{2,1,0:T(8,128)(2,1)S(1)}, bf16[2,2048,128]{2,1,0:T(8,128)(2,1)S(1)}, bf16[2,2...) custom-call(bf16[128,4096]{1,0:T(8,128)(2,1)S(1)} %copy-done.9, bf16[128,256]{1,0:T(8,128)(2,1)S(1)} %copy-done.12, ...), custom_call_target="tpu_custom_call" | custom-call | tf_op jit(solution)/shard_map/attention_shares/pallas_call | solution.py:201
  115.5 9.0 %prepare_weights.1 = (bf16[3,2048,512]{2,1,0:T(8,128)(2,1)}, bf16[3,2048,256]{2,1,0:T(8,128)(2,1)}, bf16[3,512,2048]{2,1,0:T(8,128)(2,1)}) custom-call(bf16[2048,384]{1,0:T(8,128)(2,1)S(1)} %copy-done.6, bf16[2048,384]{1,0:T(8,128)(2,1)S(1)} %copy-done.7, bf16[384,2048]{1,0:T(8,128)(2,1)S(1)} %copy-done.8, bf16[2048,384]{1,0:T(8,128)(2,1)} %collective-permute-done.3.refs_3_, ...), custom_call_target="tpu_custom_call" | custom-call | tf_op jit(solution)/shard_map/prepare_weights/pallas_call | solution.py:94
  124.5 2.8 %maximum_select_fusion.refs_4_ = bf16[2,128,2048]{2,1,0:T(8,128)(2,1)} fusion(bf16[1,128,2048]{2,1,0:T(8,128)(2,1)} %bitcast.12, bf16[1,128,2048]{2,1,0:T(8,128)(2,1)} %bitcast.11, pred[]{:T(512)S(6)} %eq.3), kind=kLoop, calls=%fused_computation | loop fusion | flops 1572864 | bytes 2097153 | tf_op jit(solution)/shard_map/jit(_where)/select_n | solution.py:439
  127.3 11.7 %expert_terms.1 = bf16[384,2048]{1,0:T(8,128)(2,1)S(1)} custom-call(bf16[384,4096]{1,0:T(8,128)(2,1)S(1)} %bitcast.24, bf16[3,2048,512]{2,1,0:T(8,128)(2,1)} %get-tuple-element.80.cols_ref, bf16[3,2048,256]{2,1,0:T(8,128)(2,1)} %get-tuple-element.81.down_ref, bf16[3,512,2048]{2,1,0:T(8,128)(2,1)} %get-tuple-element.82.back_ref), custom_call_target="tpu_custom_call" | custom-call | tf_op jit(solution)/shard_map/expert_terms/pallas_call | solution.py:145
  141.4 5.0 %all-to-all-start.1 = ((bf16[8,48,2048]{2,1,0:T(8,128)(2,1)}), bf16[8,48,2048]{2,1,0:T(8,128)(2,1)S(1)}, u32[]{:S(2)}, u32[]{:S(2)}) async-start(bf16[8,48,2048]{2,1,0:T(8,128)(2,1)} %bitcast.25), calls=%async_computation.1 | async-start | bytes 3145728 | tf_op jit(solution)/shard_map/all_to_all | solution.py:447
  146.4 4.7 %collective-permute-start.11 = (bf16[2,128,2048]{2,1,0:T(8,128)(2,1)}, bf16[2,128,2048]{2,1,0:T(8,128)(2,1)}, u32[]{:S(2)}, u32[]{:S(2)}) collective-permute-start(bf16[2,128,2048]{2,1,0:T(8,128)(2,1)} %bitcast.35), channel_id=1, source_target_pairs={{0,1},{1,0},{2,3},{3,2},{4,5},{5,4},{6,7},{7,6},{8,9},{9,8},{10,11... | collective-permute-start | bytes 3145736 | tf_op jit(solution)/shard_map/ppermute | solution.py:412
  151.1 10.4 %collective-permute-done.14.refs_6_ = bf16[2,128,2048]{2,1,0:T(8,128)(2,1)} collective-permute-done((bf16[2,128,2048]{2,1,0:T(8,128)(2,1)}, bf16[2,128,2048]{2,1,0:T(8,128)(2,1)}, u32[]{:S(2)}, u32[]{:S(2)}) %collective-permute-start.14) | collective-permute-done | bytes 1048608 | tf_op jit(solution)/shard_map/ppermute | solution.py:411
  161.5 4.6 %collective-permute-start.17 = (bf16[2,2,128,2048]{3,2,1,0:T(8,128)(2,1)}, bf16[2,2,128,2048]{3,2,1,0:T(8,128)(2,1)}, u32[]{:S(2)}, u32[]{:S(2)}) collective-permute-start(bf16[2,2,128,2048]{3,2,1,0:T(8,128)(2,1)} %bitcast.32), channel_id=1, source_target_pairs={{0,1},{1,0},{2,3},{3,2},{4,5},{5,4},{6,7},{7,6},{8,9},{9,8},{10,11... | collective-permute-start | bytes 6291464 | tf_op jit(solution)/shard_map/ppermute | solution.py:412
  167.3 5.9 %collective-permute-done.12.refs_3_ = bf16[2,128,2048]{2,1,0:T(8,128)(2,1)} collective-permute-done((bf16[2,128,2048]{2,1,0:T(8,128)(2,1)}, bf16[2,128,2048]{2,1,0:T(8,128)(2,1)}, u32[]{:S(2)}, u32[]{:S(2)}) %collective-permute-start.12) | collective-permute-done | bytes 1048608 | tf_op jit(solution)/shard_map/ppermute | solution.py:412
  174.7 5.6 %all-to-all-done.1 = bf16[8,48,2048]{2,1,0:T(8,128)(2,1)S(1)} async-done(((bf16[8,48,2048]{2,1,0:T(8,128)(2,1)}), bf16[8,48,2048]{2,1,0:T(8,128)(2,1)S(1)}, u32[]{:S(2)}, u32[]{:S(2)}) %all-to-all-start.1) | async-done | bytes 1572896 | tf_op jit(solution)/shard_map/all_to_all | solution.py:447
  181.5 16.6 %tail_attention.1 = (bf16[128,2048]{1,0:T(8,128)(2,1)}, bf16[128,4096]{1,0:T(8,128)(2,1)}, f32[2,128,256]{2,1,0:T(8,128)}, bf16[2,128,256]{2,1,0:T(8,128)(2,1)}) custom-call(s32[3]{0:T(128)} %pad_add_fusion.place_info, bf16[384,2048]{1,0:T(8,128)(2,1)} %bitcast.29, bf16[128,384]{1,0:T(8,128)(2,1)} %copy-done.17, bf16[128,2048]{1,0:T(8,128)(2,1)} %grad_ref.3, ...), custom_call_target="tpu_custom_call" | custom-call | flops 2147483648 | bytes 23068672 | tf_op jit(solution)/shard_map/tail_attention/pallas_call | solution.py:320
  198.1 3.0 %collective-permute-start.18 = (bf16[2,128,256]{2,1,0:T(8,128)(2,1)}, bf16[2,128,256]{2,1,0:T(8,128)(2,1)S(1)}, u32[]{:S(2)}, u32[]{:S(2)}) collective-permute-start(bf16[2,128,256]{2,1,0:T(8,128)(2,1)} %get-tuple-element.101), channel_id=1, source_target_pairs={{1,0},{2,1},{3,2},{4,3},{5,4},{6,5},{7,6},{8,7},{9,8},{10,9},{11,1... | collective-permute-start | bytes 393224 | tf_op jit(solution)/shard_map/ppermute | solution.py:456
  201.1 4.4 %collective-permute-done.18.later_ref = bf16[2,128,256]{2,1,0:T(8,128)(2,1)S(1)} collective-permute-done((bf16[2,128,256]{2,1,0:T(8,128)(2,1)}, bf16[2,128,256]{2,1,0:T(8,128)(2,1)S(1)}, u32[]{:S(2)}, u32[]{:S(2)}) %collective-permute-start.18) | collective-permute-done | bytes 131104 | tf_op jit(solution)/shard_map/ppermute | solution.py:456
  (91 shorter events, 29.9 us)
Async XLA Ops:
  7.2 30.3 %all-gather.7.cloned.1.call-start = ((), (), s32[]{:S(2)}) async-start(), calls=%async_computation.2 | async-start | bytes 1572864 | tf_op jit(solution)/shard_map/all_gather | solution.py:410
  9.3 27.4 %collective-permute-start = (bf16[128,2048]{1,0:T(8,128)(2,1)}, bf16[128,2048]{1,0:T(8,128)(2,1)S(1)}, u32[]{:S(2)}, u32[]{:S(2)}) collective-permute-start(bf16[128,2048]{1,0:T(8,128)(2,1)} %constant_dynamic-slice_fusion), channel_id=1, source_target_pairs={{0,4},{4,0},{1,5},{5,1},{2,6},{6,2},{3,7},{7,3},{8,12},{12,8},{9,1... | collective-permute-start | bytes 1572872 | tf_op jit(solution)/shard_map/ppermute | solution.py:407
  9.5 28.0 %collective-permute-start.1 = (bf16[128,2048]{1,0:T(8,128)(2,1)}, bf16[128,2048]{1,0:T(8,128)(2,1)}, u32[]{:S(2)}, u32[]{:S(2)}) collective-permute-start(bf16[128,2048]{1,0:T(8,128)(2,1)} %constant_dynamic-slice_fusion), channel_id=1, source_target_pairs={{0,8},{8,0},{1,9},{9,1},{2,10},{10,2},{3,11},{11,3},{4,12},{12,4},... | collective-permute-start | bytes 1572872 | tf_op jit(solution)/shard_map/ppermute | solution.py:406
  18.1 18.6 %collective-permute-start.2 = (bf16[144,512]{1,0:T(8,128)(2,1)S(1)}, bf16[144,512]{1,0:T(8,128)(2,1)S(1)}, u32[]{:S(2)}, u32[]{:S(2)}) collective-permute-start(bf16[144,512]{1,0:T(8,128)(2,1)S(1)} %fusion.1), channel_id=1, source_target_pairs={{0,1},{1,2},{2,3},{3,4},{4,5},{5,6},{6,7},{7,8},{8,9},{9,10},{10,1... | collective-permute-start | bytes 442376 | tf_op jit(solution)/shard_map/ppermute | solution.py:420
  37.5 89.7 %all-to-all-start = ((bf16[8,48,4096]{2,1,0:T(8,128)(2,1)}), bf16[8,48,4096]{2,1,0:T(8,128)(2,1)S(1)}, u32[]{:S(2)}, u32[]{:S(2)}) async-start(bf16[8,48,4096]{2,1,0:T(8,128)(2,1)} %bitcast.26), calls=%async_computation | async-start | bytes 6291456 | tf_op jit(solution)/shard_map/all_to_all | solution.py:424
  41.2 99.0 %all-gather.9.cloned.1.call-start = ((), (), s32[]{:S(2)}) async-start(), calls=%async_computation.3 | async-start | bytes 3145728 | tf_op jit(solution)/shard_map/all_gather | solution.py:410
  41.2 10.9 %collective-permute-start.6 = (bf16[128,2048]{1,0:T(8,128)(2,1)}, bf16[128,2048]{1,0:T(8,128)(2,1)S(1)}, u32[]{:S(2)}, u32[]{:S(2)}) collective-permute-start(bf16[128,2048]{1,0:T(8,128)(2,1)} %copy-done.23), channel_id=1, source_target_pairs={{0,16},{16,0},{1,17},{17,1},{2,18},{18,2},{3,19},{19,3},{4,20},{20... | collective-permute-start | bytes 1572872 | tf_op jit(solution)/shard_map/ppermute | solution.py:411
  54.3 96.9 %all-gather.11.cloned.1.call-start = ((), (), s32[]{:S(2)}) async-start(), calls=%async_computation.4 | async-start | bytes 3145728 | tf_op jit(solution)/shard_map/all_gather | solution.py:410
  54.3 58.4 %collective-permute-start.3 = (bf16[2048,384]{1,0:T(8,128)(2,1)}, bf16[2048,384]{1,0:T(8,128)(2,1)}, u32[]{:S(2)}, u32[]{:S(2)}) collective-permute-start(bf16[2048,384]{1,0:T(8,128)(2,1)} %refs_0_.1), channel_id=1, source_target_pairs={{0,1},{1,0},{2,3},{3,2},{4,5},{5,4},{6,7},{7,6},{8,9},{9,8},{10,11... | collective-permute-start | bytes 4718600 | tf_op jit(solution)/shard_map/ppermute | solution.py:412
  58.0 54.6 %collective-permute-start.4 = (bf16[2048,384]{1,0:T(8,128)(2,1)}, bf16[2048,384]{1,0:T(8,128)(2,1)}, u32[]{:S(2)}, u32[]{:S(2)}) collective-permute-start(bf16[2048,384]{1,0:T(8,128)(2,1)} %refs_1_.1), channel_id=1, source_target_pairs={{0,1},{1,0},{2,3},{3,2},{4,5},{5,4},{6,7},{7,6},{8,9},{9,8},{10,11... | collective-permute-start | bytes 4718600 | tf_op jit(solution)/shard_map/ppermute | solution.py:412
  58.1 54.6 %collective-permute-start.5 = (bf16[384,2048]{1,0:T(8,128)(2,1)}, bf16[384,2048]{1,0:T(8,128)(2,1)}, u32[]{:S(2)}, u32[]{:S(2)}) collective-permute-start(bf16[384,2048]{1,0:T(8,128)(2,1)} %refs_2_.1), channel_id=1, source_target_pairs={{0,1},{1,0},{2,3},{3,2},{4,5},{5,4},{6,7},{7,6},{8,9},{9,8},{10,11... | collective-permute-start | bytes 4718600 | tf_op jit(solution)/shard_map/ppermute | solution.py:412
  58.6 13.8 %collective-permute-start.7 = (bf16[128,2048]{1,0:T(8,128)(2,1)}, bf16[128,2048]{1,0:T(8,128)(2,1)S(1)}, u32[]{:S(2)}, u32[]{:S(2)}) collective-permute-start(bf16[128,2048]{1,0:T(8,128)(2,1)} %collective-permute-done.1), channel_id=1, source_target_pairs={{0,16},{16,0},{1,17},{17,1},{2,18},{18,2},{3,19},{19,3},{4,20},{20... | collective-permute-start | bytes 1572872 | tf_op jit(solution)/shard_map/ppermute | solution.py:411
  59.8 42.5 %collective-permute-start.9 = (bf16[128,2048]{1,0:T(8,128)(2,1)}, bf16[128,2048]{1,0:T(8,128)(2,1)}, u32[]{:S(2)}, u32[]{:S(2)}) collective-permute-start(bf16[128,2048]{1,0:T(8,128)(2,1)} %collective-permute-done.1), channel_id=1, source_target_pairs={{0,4},{4,0},{1,5},{5,1},{2,6},{6,2},{3,7},{7,3},{8,12},{12,8},{9,1... | collective-permute-start | bytes 1572872 | tf_op jit(solution)/shard_map/ppermute | solution.py:430
  72.4 54.9 %collective-permute-start.8 = (bf16[2,128,2048]{2,1,0:T(8,128)(2,1)}, bf16[2,128,2048]{2,1,0:T(8,128)(2,1)}, u32[]{:S(2)}, u32[]{:S(2)}) collective-permute-start(bf16[2,128,2048]{2,1,0:T(8,128)(2,1)} %bitcast.34), channel_id=1, source_target_pairs={{0,16},{16,0},{1,17},{17,1},{2,18},{18,2},{3,19},{19,3},{4,20},{20... | collective-permute-start | bytes 3145736 | tf_op jit(solution)/shard_map/ppermute | solution.py:411
  102.2 22.3 %collective-permute-start.10 = (bf16[128,2048]{1,0:T(8,128)(2,1)}, bf16[128,2048]{1,0:T(8,128)(2,1)}, u32[]{:S(2)}, u32[]{:S(2)}) collective-permute-start(bf16[128,2048]{1,0:T(8,128)(2,1)} %collective-permute-done.9), channel_id=1, source_target_pairs={{0,2},{2,0},{1,3},{3,1},{4,6},{6,4},{5,7},{7,5},{8,10},{10,8},{9,1... | collective-permute-start | bytes 1572872 | tf_op jit(solution)/shard_map/ppermute | solution.py:437
  140.2 21.3 %collective-permute-start.14 = (bf16[2,128,2048]{2,1,0:T(8,128)(2,1)}, bf16[2,128,2048]{2,1,0:T(8,128)(2,1)}, u32[]{:S(2)}, u32[]{:S(2)}) collective-permute-start(bf16[2,128,2048]{2,1,0:T(8,128)(2,1)} %maximum_select_fusion.refs_4_), channel_id=1, source_target_pairs={{0,16},{16,0},{1,17},{17,1},{2,18},{18,2},{3,19},{19,3},{4,20},{20... | collective-permute-start | bytes 3145736 | tf_op jit(solution)/shard_map/ppermute | solution.py:411
  141.4 38.9 %all-to-all-start.1 = ((bf16[8,48,2048]{2,1,0:T(8,128)(2,1)}), bf16[8,48,2048]{2,1,0:T(8,128)(2,1)S(1)}, u32[]{:S(2)}, u32[]{:S(2)}) async-start(bf16[8,48,2048]{2,1,0:T(8,128)(2,1)} %bitcast.25), calls=%async_computation.1 | async-start | bytes 3145728 | tf_op jit(solution)/shard_map/all_to_all | solution.py:447
  146.4 20.2 %collective-permute-start.11 = (bf16[2,128,2048]{2,1,0:T(8,128)(2,1)}, bf16[2,128,2048]{2,1,0:T(8,128)(2,1)}, u32[]{:S(2)}, u32[]{:S(2)}) collective-permute-start(bf16[2,128,2048]{2,1,0:T(8,128)(2,1)} %bitcast.35), channel_id=1, source_target_pairs={{0,1},{1,0},{2,3},{3,2},{4,5},{5,4},{6,7},{7,6},{8,9},{9,8},{10,11... | collective-permute-start | bytes 3145736 | tf_op jit(solution)/shard_map/ppermute | solution.py:412
  151.1 23.6 %collective-permute-start.16 = (bf16[2,2,128,2048]{3,2,1,0:T(8,128)(2,1)}, bf16[2,2,128,2048]{3,2,1,0:T(8,128)(2,1)}, u32[]{:S(2)}, u32[]{:S(2)}) collective-permute-start(bf16[2,2,128,2048]{3,2,1,0:T(8,128)(2,1)} %bitcast.30), channel_id=1, source_target_pairs={{0,1},{1,0},{2,3},{3,2},{4,5},{5,4},{6,7},{7,6},{8,9},{9,8},{10,11... | collective-permute-start | bytes 6291464 | tf_op jit(solution)/shard_map/ppermute | solution.py:412
  161.5 18.8 %collective-permute-start.17 = (bf16[2,2,128,2048]{3,2,1,0:T(8,128)(2,1)}, bf16[2,2,128,2048]{3,2,1,0:T(8,128)(2,1)}, u32[]{:S(2)}, u32[]{:S(2)}) collective-permute-start(bf16[2,2,128,2048]{3,2,1,0:T(8,128)(2,1)} %bitcast.32), channel_id=1, source_target_pairs={{0,1},{1,0},{2,3},{3,2},{4,5},{5,4},{6,7},{7,6},{8,9},{9,8},{10,11... | collective-permute-start | bytes 6291464 | tf_op jit(solution)/shard_map/ppermute | solution.py:412
  166.1 7.1 %collective-permute-start.13 = (bf16[2,128,2048]{2,1,0:T(8,128)(2,1)S(1)}, bf16[2,128,2048]{2,1,0:T(8,128)(2,1)}, u32[]{:S(2)}, u32[]{:S(2)}) collective-permute-start(bf16[2,128,2048]{2,1,0:T(8,128)(2,1)S(1)} %copy-done.22), channel_id=1, source_target_pairs={{0,1},{1,0},{2,3},{3,2},{4,5},{5,4},{6,7},{7,6},{8,9},{9,8},{10,11... | collective-permute-start | bytes 3145736 | tf_op jit(solution)/shard_map/ppermute | solution.py:412
  166.1 7.1 %collective-permute-start.12 = (bf16[2,128,2048]{2,1,0:T(8,128)(2,1)}, bf16[2,128,2048]{2,1,0:T(8,128)(2,1)}, u32[]{:S(2)}, u32[]{:S(2)}) collective-permute-start(bf16[2,128,2048]{2,1,0:T(8,128)(2,1)} %collective-permute-done.8.refs_2_), channel_id=1, source_target_pairs={{0,1},{1,0},{2,3},{3,2},{4,5},{5,4},{6,7},{7,6},{8,9},{9,8},{10,11... | collective-permute-start | bytes 3145736 | tf_op jit(solution)/shard_map/ppermute | solution.py:412
  166.6 8.1 %collective-permute-start.15 = (bf16[2,128,2048]{2,1,0:T(8,128)(2,1)}, bf16[2,128,2048]{2,1,0:T(8,128)(2,1)}, u32[]{:S(2)}, u32[]{:S(2)}) collective-permute-start(bf16[2,128,2048]{2,1,0:T(8,128)(2,1)} %collective-permute-done.14.refs_6_), channel_id=1, source_target_pairs={{0,1},{1,0},{2,3},{3,2},{4,5},{5,4},{6,7},{7,6},{8,9},{9,8},{10,11... | collective-permute-start | bytes 3145736 | tf_op jit(solution)/shard_map/ppermute | solution.py:412
  198.1 7.4 %collective-permute-start.18 = (bf16[2,128,256]{2,1,0:T(8,128)(2,1)}, bf16[2,128,256]{2,1,0:T(8,128)(2,1)S(1)}, u32[]{:S(2)}, u32[]{:S(2)}) collective-permute-start(bf16[2,128,256]{2,1,0:T(8,128)(2,1)} %get-tuple-element.101), channel_id=1, source_target_pairs={{1,0},{2,1},{3,2},{4,3},{5,4},{6,5},{7,6},{8,7},{9,8},{10,9},{11,1... | collective-permute-start | bytes 393224 | tf_op jit(solution)/shard_map/ppermute | solution.py:456
  (25 other events, 132.4 us)
Sparse Core Ops, SparseCore 0:
  10.2 23.0 all-gather.6
  54.4 53.1 all-gather.8
  109.2 33.2 all-gather.10

commit v22 on v21

--- a/solution.py
+++ b/solution.py
@@ -430,6 +430,7 @@
     w_last = lax.ppermute(w_far, "near", swap)
     prepared = prepare_weights(own, other)
     attention = attention_shares(queries, key_heads, value_heads, prev, segs)
+    w_last, prepared, attention = lax.optimization_barrier((w_last, prepared, attention))
     rows_in, prepared, attention, own_line, own_crossed = lax.optimization_barrier(
         (rows_in, prepared, attention, own_line, own_crossed)
     )

time: 218 us -> 210 us (0.963)
  starting transfers between devices: 37.1 us -> 31.6 us
    ppermute x1, waiting for transfers between devices: 26.5 us -> 4.89 us  [local(): w_last = lax.ppermute(w_far, 'near', swap)]
    ppermute x1, waiting for transfers between devices: 0.01 us -> 13.7 us  [local(): moved = lax.ppermute(w_last, 'low', swap)]
    all_gather x3, waiting for transfers between devices: 0.01 us -> 11.5 us  [local(): line = lambda w: lax.all_gather(w, 'low', axis=0, tiled=False)]
    ppermute x4, waiting for transfers between devices: 32.4 us -> 25.7 us  [local(): cross = lambda w: lax.ppermute(w, 'groups', swap)]
    ppermute x9, starting transfers between devices: 14.1 us -> 9.26 us  [local(): other_core = lambda w: lax.ppermute(w, 'core', swap)]
  transfers between devices with their start and end apart: 24 -> 24, of which waited for: 9 -> 11; matrix products, arithmetic and copies ran while one was open for 4% -> 4% of each run, Pallas kernels for 12% -> 12%
where the time goes in v22:
time: 210 us; the launch traced here: 207 us
  waiting for transfers between devices  89.9 us (43%)
  Pallas kernels  42.8 us (20%)
  starting transfers between devices  31.6 us (15%)
  local copies, waits for them, and re-layouts  20.5 us (10%)
  between operations  13.9 us (7%)
  other arithmetic  7.78 us (4%)
    ppermute x4, waiting for transfers between devices, local(): cross = lambda w: lax.ppermute(w, 'groups', swap)  25.7 us
    unnamed x50, local copies, waits for them, and re-layouts  19.6 us
    pallas_call x1, Pallas kernels, tail(): pl.pallas_call(functools.partial(tail_kernel, (heads, tiles)), grid_spec=...  16.6 us
    ppermute x1, waiting for transfers between devices, local(): prev = lax.ppermute(jnp.concatenate([kv, seg_rows], axis=0), blk, onward)  15.4 us
    ppermute x1, waiting for transfers between devices, local(): moved = lax.ppermute(w_last, 'low', swap)  13.7 us
    pallas_call x1, Pallas kernels, experts(): pl.pallas_call(functools.partial(expert_kernel, steps), grid=(steps + wid...  12 us
    all_gather x3, waiting for transfers between devices, local(): line = lambda w: lax.all_gather(w, 'low', axis=0, tiled=False)  11.5 us
    ppermute x9, starting transfers between devices, local(): other_core = lambda w: lax.ppermute(w, 'core', swap)  9.26 us
  transfers between devices with their start and end apart: 24, of which 11 were waited for; matrix products, arithmetic and copies ran while one was open for 4% of the time, Pallas kernels for 12%

profile of v22, /device:TPU:13, one launch (start us, length us, event | category | flops | bytes accessed | tf_op | source)
XLA Modules:
  0.0 206.6 jit_solution(6688038759402225337)
XLA Ops:
  9.5 2.3 %collective-permute-start.1 = (bf16[128,2048]{1,0:T(8,128)(2,1)}, bf16[128,2048]{1,0:T(8,128)(2,1)}, u32[]{:S(2)}, u32[]{:S(2)}) collective-permute-start(bf16[128,2048]{1,0:T(8,128)(2,1)} %constant_dynamic-slice_fusion), channel_id=1, source_target_pairs={{0,8},{8,0},{1,9},{9,1},{2,10},{10,2},{3,11},{11,3},{4,12},{12,4},... | collective-permute-start | bytes 1572872 | tf_op jit(solution)/shard_map/ppermute | solution.py:406
  18.1 3.2 %collective-permute-start.2 = (bf16[144,512]{1,0:T(8,128)(2,1)S(1)}, bf16[144,512]{1,0:T(8,128)(2,1)S(1)}, u32[]{:S(2)}, u32[]{:S(2)}) collective-permute-start(bf16[144,512]{1,0:T(8,128)(2,1)S(1)} %fusion.1), channel_id=1, source_target_pairs={{0,1},{1,2},{2,3},{3,4},{4,5},{5,6},{6,7},{7,8},{8,9},{9,10},{10,1... | collective-permute-start | bytes 442376 | tf_op jit(solution)/shard_map/ppermute | solution.py:420
  21.3 15.4 %collective-permute-done.2.prev_key_ref.prev_value_ref.prev_seg_ref = bf16[144,512]{1,0:T(8,128)(2,1)S(1)} collective-permute-done((bf16[144,512]{1,0:T(8,128)(2,1)S(1)}, bf16[144,512]{1,0:T(8,128)(2,1)S(1)}, u32[]{:S(2)}, u32[]{:S(2)}) %collective-permute-start.2) | collective-permute-done | bytes 147488 | tf_op jit(solution)/shard_map/ppermute | solution.py:420
  37.5 3.6 %all-to-all-start = ((bf16[8,48,4096]{2,1,0:T(8,128)(2,1)}), bf16[8,48,4096]{2,1,0:T(8,128)(2,1)S(1)}, u32[]{:S(2)}, u32[]{:S(2)}) async-start(bf16[8,48,4096]{2,1,0:T(8,128)(2,1)} %bitcast.26), calls=%async_computation | async-start | bytes 6291456 | tf_op jit(solution)/shard_map/all_to_all | solution.py:424
  42.5 9.7 %collective-permute-done.7 = bf16[128,2048]{1,0:T(8,128)(2,1)S(1)} collective-permute-done((bf16[128,2048]{1,0:T(8,128)(2,1)}, bf16[128,2048]{1,0:T(8,128)(2,1)S(1)}, u32[]{:S(2)}, u32[]{:S(2)}) %collective-permute-start.7) | collective-permute-done | bytes 524320 | tf_op jit(solution)/shard_map/ppermute | solution.py:411
  54.3 3.7 %collective-permute-start.4 = (bf16[2048,384]{1,0:T(8,128)(2,1)}, bf16[2048,384]{1,0:T(8,128)(2,1)}, u32[]{:S(2)}, u32[]{:S(2)}) collective-permute-start(bf16[2048,384]{1,0:T(8,128)(2,1)} %refs_0_.1), channel_id=1, source_target_pairs={{0,1},{1,0},{2,3},{3,2},{4,5},{5,4},{6,7},{7,6},{8,9},{9,8},{10,11... | collective-permute-start | bytes 4718600 | tf_op jit(solution)/shard_map/ppermute | solution.py:412
  60.0 12.4 %collective-permute-done.8 = bf16[128,2048]{1,0:T(8,128)(2,1)S(1)} collective-permute-done((bf16[128,2048]{1,0:T(8,128)(2,1)}, bf16[128,2048]{1,0:T(8,128)(2,1)S(1)}, u32[]{:S(2)}, u32[]{:S(2)}) %collective-permute-start.8) | collective-permute-done | bytes 524320 | tf_op jit(solution)/shard_map/ppermute | solution.py:411
  73.6 2.1 %pad_maximum_fusion.1 = bf16[2,128,2048]{2,1,0:T(8,128)(2,1)} fusion(bf16[1,128,2048]{2,1,0:T(8,128)(2,1)S(1)} %bitcast.38, bf16[1,128,2048]{2,1,0:T(8,128)(2,1)} %bitcast.18), kind=kLoop, calls=%fused_computation.2 | loop fusion | flops 524288 | bytes 2097152 | tf_op jit(solution)/shard_map/stack | solution.py:427
  77.2 3.5 %attention_shares.1 = (bf16[2,2048,256]{2,1,0:T(8,128)(2,1)S(1)}, bf16[2,256,2048]{2,1,0:T(8,128)(2,1)S(1)}, bf16[2,2048,128]{2,1,0:T(8,128)(2,1)S(1)}, bf16[2,2...) custom-call(bf16[128,4096]{1,0:T(8,128)(2,1)S(1)} %copy-done.9, bf16[128,256]{1,0:T(8,128)(2,1)S(1)} %copy-done.12, ...), custom_call_target="tpu_custom_call" | custom-call | tf_op jit(solution)/shard_map/attention_shares/pallas_call | solution.py:201
  88.6 8.8 %prepare_weights.1 = (bf16[3,2048,512]{2,1,0:T(8,128)(2,1)}, bf16[3,2048,256]{2,1,0:T(8,128)(2,1)}, bf16[3,512,2048]{2,1,0:T(8,128)(2,1)}) custom-call(bf16[2048,384]{1,0:T(8,128)(2,1)S(1)} %copy-done.6, bf16[2048,384]{1,0:T(8,128)(2,1)S(1)} %copy-done.7, bf16[384,2048]{1,0:T(8,128)(2,1)S(1)} %copy-done.8, bf16[2048,384]{1,0:T(8,128)(2,1)} %collective-permute-done.4.refs_3_, ...), custom_call_target="tpu_custom_call" | custom-call | tf_op jit(solution)/shard_map/prepare_weights/pallas_call | solution.py:94
  97.3 4.9 %collective-permute-done.3 = bf16[128,2048]{1,0:T(8,128)(2,1)} collective-permute-done((bf16[128,2048]{1,0:T(8,128)(2,1)}, bf16[128,2048]{1,0:T(8,128)(2,1)}, u32[]{:S(2)}, u32[]{:S(2)}) %collective-permute-start.3) | collective-permute-done | bytes 524320 | tf_op jit(solution)/shard_map/ppermute | solution.py:430
  102.7 13.7 %collective-permute-done.10 = bf16[128,2048]{1,0:T(8,128)(2,1)} collective-permute-done((bf16[128,2048]{1,0:T(8,128)(2,1)}, bf16[128,2048]{1,0:T(8,128)(2,1)}, u32[]{:S(2)}, u32[]{:S(2)}) %collective-permute-start.10) | collective-permute-done | bytes 524320 | tf_op jit(solution)/shard_map/ppermute | solution.py:438
  116.4 2.9 %maximum_select_fusion.refs_4_ = bf16[2,128,2048]{2,1,0:T(8,128)(2,1)} fusion(bf16[1,128,2048]{2,1,0:T(8,128)(2,1)} %bitcast.12, bf16[1,128,2048]{2,1,0:T(8,128)(2,1)} %bitcast.11, pred[]{:T(512)S(6)} %eq.3), kind=kLoop, calls=%fused_computation | loop fusion | flops 1572864 | bytes 2097153 | tf_op jit(solution)/shard_map/jit(_where)/select_n | solution.py:440
  119.3 12.0 %expert_terms.1 = bf16[384,2048]{1,0:T(8,128)(2,1)S(1)} custom-call(bf16[384,4096]{1,0:T(8,128)(2,1)S(1)} %bitcast.24, bf16[3,2048,512]{2,1,0:T(8,128)(2,1)} %get-tuple-element.97.cols_ref, bf16[3,2048,256]{2,1,0:T(8,128)(2,1)} %get-tuple-element.98.down_ref, bf16[3,512,2048]{2,1,0:T(8,128)(2,1)} %get-tuple-element.99.back_ref), custom_call_target="tpu_custom_call" | custom-call | tf_op jit(solution)/shard_map/expert_terms/pallas_call | solution.py:145
  133.7 5.0 %all-to-all-start.1 = ((bf16[8,48,2048]{2,1,0:T(8,128)(2,1)}), bf16[8,48,2048]{2,1,0:T(8,128)(2,1)S(1)}, u32[]{:S(2)}, u32[]{:S(2)}) async-start(bf16[8,48,2048]{2,1,0:T(8,128)(2,1)} %bitcast.25), calls=%async_computation.1 | async-start | bytes 3145728 | tf_op jit(solution)/shard_map/all_to_all | solution.py:448
  138.7 2.2 %collective-permute-start.11 = (bf16[2,128,2048]{2,1,0:T(8,128)(2,1)}, bf16[2,128,2048]{2,1,0:T(8,128)(2,1)}, u32[]{:S(2)}, u32[]{:S(2)}) collective-permute-start(bf16[2,128,2048]{2,1,0:T(8,128)(2,1)} %bitcast.35), channel_id=1, source_target_pairs={{0,1},{1,0},{2,3},{3,2},{4,5},{5,4},{6,7},{7,6},{8,9},{9,8},{10,11... | collective-permute-start | bytes 3145736 | tf_op jit(solution)/shard_map/ppermute | solution.py:412
  141.0 11.5 %all-gather.11.cloned.1.call-done = bf16[4,128,2048]{2,1,0:T(8,128)(2,1)} async-done(((bf16[2,128,2048]{2,1,0:T(8,128)(2,1)}), bf16[4,128,2048]{2,1,0:T(8,128)(2,1)}) %all-gather.11.cloned.1.call-update) | async-done | bytes 2097168 | tf_op jit(solution)/shard_map/all_gather | solution.py:410
  152.5 3.7 %collective-permute-done.14.refs_6_ = bf16[2,128,2048]{2,1,0:T(8,128)(2,1)} collective-permute-done((bf16[2,128,2048]{2,1,0:T(8,128)(2,1)}, bf16[2,128,2048]{2,1,0:T(8,128)(2,1)}, u32[]{:S(2)}, u32[]{:S(2)}) %collective-permute-start.14) | collective-permute-done | bytes 1048608 | tf_op jit(solution)/shard_map/ppermute | solution.py:411
  156.2 2.2 %collective-permute-start.17 = (bf16[2,2,128,2048]{3,2,1,0:T(8,128)(2,1)}, bf16[2,2,128,2048]{3,2,1,0:T(8,128)(2,1)}, u32[]{:S(2)}, u32[]{:S(2)}) collective-permute-start(bf16[2,2,128,2048]{3,2,1,0:T(8,128)(2,1)} %bitcast.32), channel_id=1, source_target_pairs={{0,1},{1,0},{2,3},{3,2},{4,5},{5,4},{6,7},{7,6},{8,9},{9,8},{10,11... | collective-permute-start | bytes 6291464 | tf_op jit(solution)/shard_map/ppermute | solution.py:412
  159.6 5.9 %collective-permute-done.12.refs_3_ = bf16[2,128,2048]{2,1,0:T(8,128)(2,1)} collective-permute-done((bf16[2,128,2048]{2,1,0:T(8,128)(2,1)}, bf16[2,128,2048]{2,1,0:T(8,128)(2,1)}, u32[]{:S(2)}, u32[]{:S(2)}) %collective-permute-start.12) | collective-permute-done | bytes 1048608 | tf_op jit(solution)/shard_map/ppermute | solution.py:412
  167.0 6.1 %all-to-all-done.1 = bf16[8,48,2048]{2,1,0:T(8,128)(2,1)S(1)} async-done(((bf16[8,48,2048]{2,1,0:T(8,128)(2,1)}), bf16[8,48,2048]{2,1,0:T(8,128)(2,1)S(1)}, u32[]{:S(2)}, u32[]{:S(2)}) %all-to-all-start.1) | async-done | bytes 1572896 | tf_op jit(solution)/shard_map/all_to_all | solution.py:448
  174.4 16.6 %tail_attention.1 = (bf16[128,2048]{1,0:T(8,128)(2,1)}, bf16[128,4096]{1,0:T(8,128)(2,1)}, f32[2,128,256]{2,1,0:T(8,128)}, bf16[2,128,256]{2,1,0:T(8,128)(2,1)}) custom-call(s32[3]{0:T(128)} %pad_add_fusion.place_info, bf16[384,2048]{1,0:T(8,128)(2,1)} %bitcast.29, bf16[128,384]{1,0:T(8,128)(2,1)} %copy-done.17, bf16[128,2048]{1,0:T(8,128)(2,1)} %grad_ref.3, ...), custom_call_target="tpu_custom_call" | custom-call | flops 2147483648 | bytes 23068672 | tf_op jit(solution)/shard_map/tail_attention/pallas_call | solution.py:320
  191.0 2.4 %collective-permute-start.18 = (bf16[2,128,256]{2,1,0:T(8,128)(2,1)}, bf16[2,128,256]{2,1,0:T(8,128)(2,1)S(1)}, u32[]{:S(2)}, u32[]{:S(2)}) collective-permute-start(bf16[2,128,256]{2,1,0:T(8,128)(2,1)} %get-tuple-element.119), channel_id=1, source_target_pairs={{1,0},{2,1},{3,2},{4,3},{5,4},{6,5},{7,6},{8,7},{9,8},{10,9},{11,1... | collective-permute-start | bytes 393224 | tf_op jit(solution)/shard_map/ppermute | solution.py:457
  193.4 5.0 %collective-permute-done.18.later_ref = bf16[2,128,256]{2,1,0:T(8,128)(2,1)S(1)} collective-permute-done((bf16[2,128,256]{2,1,0:T(8,128)(2,1)}, bf16[2,128,256]{2,1,0:T(8,128)(2,1)S(1)}, u32[]{:S(2)}, u32[]{:S(2)}) %collective-permute-start.18) | collective-permute-done | bytes 131104 | tf_op jit(solution)/shard_map/ppermute | solution.py:457
  (91 shorter events, 33.7 us)
Async XLA Ops:
  7.2 30.3 %all-gather.7.cloned.1.call-start = ((), (), s32[]{:S(2)}) async-start(), calls=%async_computation.2 | async-start | bytes 1572864 | tf_op jit(solution)/shard_map/all_gather | solution.py:410
  9.3 27.4 %collective-permute-start = (bf16[128,2048]{1,0:T(8,128)(2,1)}, bf16[128,2048]{1,0:T(8,128)(2,1)S(1)}, u32[]{:S(2)}, u32[]{:S(2)}) collective-permute-start(bf16[128,2048]{1,0:T(8,128)(2,1)} %constant_dynamic-slice_fusion), channel_id=1, source_target_pairs={{0,4},{4,0},{1,5},{5,1},{2,6},{6,2},{3,7},{7,3},{8,12},{12,8},{9,1... | collective-permute-start | bytes 1572872 | tf_op jit(solution)/shard_map/ppermute | solution.py:407
  9.5 28.0 %collective-permute-start.1 = (bf16[128,2048]{1,0:T(8,128)(2,1)}, bf16[128,2048]{1,0:T(8,128)(2,1)}, u32[]{:S(2)}, u32[]{:S(2)}) collective-permute-start(bf16[128,2048]{1,0:T(8,128)(2,1)} %constant_dynamic-slice_fusion), channel_id=1, source_target_pairs={{0,8},{8,0},{1,9},{9,1},{2,10},{10,2},{3,11},{11,3},{4,12},{12,4},... | collective-permute-start | bytes 1572872 | tf_op jit(solution)/shard_map/ppermute | solution.py:406
  18.1 18.6 %collective-permute-start.2 = (bf16[144,512]{1,0:T(8,128)(2,1)S(1)}, bf16[144,512]{1,0:T(8,128)(2,1)S(1)}, u32[]{:S(2)}, u32[]{:S(2)}) collective-permute-start(bf16[144,512]{1,0:T(8,128)(2,1)S(1)} %fusion.1), channel_id=1, source_target_pairs={{0,1},{1,2},{2,3},{3,4},{4,5},{5,6},{6,7},{7,8},{8,9},{9,10},{10,1... | collective-permute-start | bytes 442376 | tf_op jit(solution)/shard_map/ppermute | solution.py:420
  37.5 81.8 %all-to-all-start = ((bf16[8,48,4096]{2,1,0:T(8,128)(2,1)}), bf16[8,48,4096]{2,1,0:T(8,128)(2,1)S(1)}, u32[]{:S(2)}, u32[]{:S(2)}) async-start(bf16[8,48,4096]{2,1,0:T(8,128)(2,1)} %bitcast.26), calls=%async_computation | async-start | bytes 6291456 | tf_op jit(solution)/shard_map/all_to_all | solution.py:424
  41.2 91.4 %all-gather.9.cloned.1.call-start = ((), (), s32[]{:S(2)}) async-start(), calls=%async_computation.3 | async-start | bytes 3145728 | tf_op jit(solution)/shard_map/all_gather | solution.py:410
  41.2 10.9 %collective-permute-start.7 = (bf16[128,2048]{1,0:T(8,128)(2,1)}, bf16[128,2048]{1,0:T(8,128)(2,1)S(1)}, u32[]{:S(2)}, u32[]{:S(2)}) collective-permute-start(bf16[128,2048]{1,0:T(8,128)(2,1)} %copy-done.23), channel_id=1, source_target_pairs={{0,16},{16,0},{1,17},{17,1},{2,18},{18,2},{3,19},{19,3},{4,20},{20... | collective-permute-start | bytes 1572872 | tf_op jit(solution)/shard_map/ppermute | solution.py:411
  54.3 98.2 %all-gather.11.cloned.1.call-start = ((), (), s32[]{:S(2)}) async-start(), calls=%async_computation.4 | async-start | bytes 3145728 | tf_op jit(solution)/shard_map/all_gather | solution.py:410
  54.3 31.4 %collective-permute-start.4 = (bf16[2048,384]{1,0:T(8,128)(2,1)}, bf16[2048,384]{1,0:T(8,128)(2,1)}, u32[]{:S(2)}, u32[]{:S(2)}) collective-permute-start(bf16[2048,384]{1,0:T(8,128)(2,1)} %refs_0_.1), channel_id=1, source_target_pairs={{0,1},{1,0},{2,3},{3,2},{4,5},{5,4},{6,7},{7,6},{8,9},{9,8},{10,11... | collective-permute-start | bytes 4718600 | tf_op jit(solution)/shard_map/ppermute | solution.py:412
  58.0 27.7 %collective-permute-start.5 = (bf16[2048,384]{1,0:T(8,128)(2,1)}, bf16[2048,384]{1,0:T(8,128)(2,1)}, u32[]{:S(2)}, u32[]{:S(2)}) collective-permute-start(bf16[2048,384]{1,0:T(8,128)(2,1)} %refs_1_.1), channel_id=1, source_target_pairs={{0,1},{1,0},{2,3},{3,2},{4,5},{5,4},{6,7},{7,6},{8,9},{9,8},{10,11... | collective-permute-start | bytes 4718600 | tf_op jit(solution)/shard_map/ppermute | solution.py:412
  58.1 27.6 %collective-permute-start.6 = (bf16[384,2048]{1,0:T(8,128)(2,1)}, bf16[384,2048]{1,0:T(8,128)(2,1)}, u32[]{:S(2)}, u32[]{:S(2)}) collective-permute-start(bf16[384,2048]{1,0:T(8,128)(2,1)} %refs_2_.1), channel_id=1, source_target_pairs={{0,1},{1,0},{2,3},{3,2},{4,5},{5,4},{6,7},{7,6},{8,9},{9,8},{10,11... | collective-permute-start | bytes 4718600 | tf_op jit(solution)/shard_map/ppermute | solution.py:412
  58.6 13.8 %collective-permute-start.8 = (bf16[128,2048]{1,0:T(8,128)(2,1)}, bf16[128,2048]{1,0:T(8,128)(2,1)S(1)}, u32[]{:S(2)}, u32[]{:S(2)}) collective-permute-start(bf16[128,2048]{1,0:T(8,128)(2,1)} %collective-permute-done.1), channel_id=1, source_target_pairs={{0,16},{16,0},{1,17},{17,1},{2,18},{18,2},{3,19},{19,3},{4,20},{20... | collective-permute-start | bytes 1572872 | tf_op jit(solution)/shard_map/ppermute | solution.py:411
  59.8 42.5 %collective-permute-start.3 = (bf16[128,2048]{1,0:T(8,128)(2,1)}, bf16[128,2048]{1,0:T(8,128)(2,1)}, u32[]{:S(2)}, u32[]{:S(2)}) collective-permute-start(bf16[128,2048]{1,0:T(8,128)(2,1)} %collective-permute-done.1), channel_id=1, source_target_pairs={{0,4},{4,0},{1,5},{5,1},{2,6},{6,2},{3,7},{7,3},{8,12},{12,8},{9,1... | collective-permute-start | bytes 1572872 | tf_op jit(solution)/shard_map/ppermute | solution.py:430
  72.4 46.9 %collective-permute-start.9 = (bf16[2,128,2048]{2,1,0:T(8,128)(2,1)}, bf16[2,128,2048]{2,1,0:T(8,128)(2,1)}, u32[]{:S(2)}, u32[]{:S(2)}) collective-permute-start(bf16[2,128,2048]{2,1,0:T(8,128)(2,1)} %bitcast.34), channel_id=1, source_target_pairs={{0,16},{16,0},{1,17},{17,1},{2,18},{18,2},{3,19},{19,3},{4,20},{20... | collective-permute-start | bytes 3145736 | tf_op jit(solution)/shard_map/ppermute | solution.py:411
  102.2 14.2 %collective-permute-start.10 = (bf16[128,2048]{1,0:T(8,128)(2,1)}, bf16[128,2048]{1,0:T(8,128)(2,1)}, u32[]{:S(2)}, u32[]{:S(2)}) collective-permute-start(bf16[128,2048]{1,0:T(8,128)(2,1)} %collective-permute-done.3), channel_id=1, source_target_pairs={{0,2},{2,0},{1,3},{3,1},{4,6},{6,4},{5,7},{7,5},{8,10},{10,8},{9,1... | collective-permute-start | bytes 1572872 | tf_op jit(solution)/shard_map/ppermute | solution.py:438
  132.5 23.6 %collective-permute-start.14 = (bf16[2,128,2048]{2,1,0:T(8,128)(2,1)}, bf16[2,128,2048]{2,1,0:T(8,128)(2,1)}, u32[]{:S(2)}, u32[]{:S(2)}) collective-permute-start(bf16[2,128,2048]{2,1,0:T(8,128)(2,1)} %maximum_select_fusion.refs_4_), channel_id=1, source_target_pairs={{0,16},{16,0},{1,17},{17,1},{2,18},{18,2},{3,19},{19,3},{4,20},{20... | collective-permute-start | bytes 3145736 | tf_op jit(solution)/shard_map/ppermute | solution.py:411
  133.7 39.4 %all-to-all-start.1 = ((bf16[8,48,2048]{2,1,0:T(8,128)(2,1)}), bf16[8,48,2048]{2,1,0:T(8,128)(2,1)S(1)}, u32[]{:S(2)}, u32[]{:S(2)}) async-start(bf16[8,48,2048]{2,1,0:T(8,128)(2,1)} %bitcast.25), calls=%async_computation.1 | async-start | bytes 3145728 | tf_op jit(solution)/shard_map/all_to_all | solution.py:448
  138.7 20.2 %collective-permute-start.11 = (bf16[2,128,2048]{2,1,0:T(8,128)(2,1)}, bf16[2,128,2048]{2,1,0:T(8,128)(2,1)}, u32[]{:S(2)}, u32[]{:S(2)}) collective-permute-start(bf16[2,128,2048]{2,1,0:T(8,128)(2,1)} %bitcast.35), channel_id=1, source_target_pairs={{0,1},{1,0},{2,3},{3,2},{4,5},{5,4},{6,7},{7,6},{8,9},{9,8},{10,11... | collective-permute-start | bytes 3145736 | tf_op jit(solution)/shard_map/ppermute | solution.py:412
  141.0 26.1 %collective-permute-start.16 = (bf16[2,2,128,2048]{3,2,1,0:T(8,128)(2,1)}, bf16[2,2,128,2048]{3,2,1,0:T(8,128)(2,1)}, u32[]{:S(2)}, u32[]{:S(2)}) collective-permute-start(bf16[2,2,128,2048]{3,2,1,0:T(8,128)(2,1)} %bitcast.30), channel_id=1, source_target_pairs={{0,1},{1,0},{2,3},{3,2},{4,5},{5,4},{6,7},{7,6},{8,9},{9,8},{10,11... | collective-permute-start | bytes 6291464 | tf_op jit(solution)/shard_map/ppermute | solution.py:412
  156.2 17.0 %collective-permute-start.17 = (bf16[2,2,128,2048]{3,2,1,0:T(8,128)(2,1)}, bf16[2,2,128,2048]{3,2,1,0:T(8,128)(2,1)}, u32[]{:S(2)}, u32[]{:S(2)}) collective-permute-start(bf16[2,2,128,2048]{3,2,1,0:T(8,128)(2,1)} %bitcast.32), channel_id=1, source_target_pairs={{0,1},{1,0},{2,3},{3,2},{4,5},{5,4},{6,7},{7,6},{8,9},{9,8},{10,11... | collective-permute-start | bytes 6291464 | tf_op jit(solution)/shard_map/ppermute | solution.py:412
  158.4 7.1 %collective-permute-start.13 = (bf16[2,128,2048]{2,1,0:T(8,128)(2,1)S(1)}, bf16[2,128,2048]{2,1,0:T(8,128)(2,1)}, u32[]{:S(2)}, u32[]{:S(2)}) collective-permute-start(bf16[2,128,2048]{2,1,0:T(8,128)(2,1)S(1)} %copy-done.22), channel_id=1, source_target_pairs={{0,1},{1,0},{2,3},{3,2},{4,5},{5,4},{6,7},{7,6},{8,9},{9,8},{10,11... | collective-permute-start | bytes 3145736 | tf_op jit(solution)/shard_map/ppermute | solution.py:412
  158.4 7.1 %collective-permute-start.12 = (bf16[2,128,2048]{2,1,0:T(8,128)(2,1)}, bf16[2,128,2048]{2,1,0:T(8,128)(2,1)}, u32[]{:S(2)}, u32[]{:S(2)}) collective-permute-start(bf16[2,128,2048]{2,1,0:T(8,128)(2,1)} %collective-permute-done.9.refs_2_), channel_id=1, source_target_pairs={{0,1},{1,0},{2,3},{3,2},{4,5},{5,4},{6,7},{7,6},{8,9},{9,8},{10,11... | collective-permute-start | bytes 3145736 | tf_op jit(solution)/shard_map/ppermute | solution.py:412
  158.9 8.1 %collective-permute-start.15 = (bf16[2,128,2048]{2,1,0:T(8,128)(2,1)}, bf16[2,128,2048]{2,1,0:T(8,128)(2,1)}, u32[]{:S(2)}, u32[]{:S(2)}) collective-permute-start(bf16[2,128,2048]{2,1,0:T(8,128)(2,1)} %collective-permute-done.14.refs_6_), channel_id=1, source_target_pairs={{0,1},{1,0},{2,3},{3,2},{4,5},{5,4},{6,7},{7,6},{8,9},{9,8},{10,11... | collective-permute-start | bytes 3145736 | tf_op jit(solution)/shard_map/ppermute | solution.py:412
  191.0 7.4 %collective-permute-start.18 = (bf16[2,128,256]{2,1,0:T(8,128)(2,1)}, bf16[2,128,256]{2,1,0:T(8,128)(2,1)S(1)}, u32[]{:S(2)}, u32[]{:S(2)}) collective-permute-start(bf16[2,128,256]{2,1,0:T(8,128)(2,1)} %get-tuple-element.119), channel_id=1, source_target_pairs={{1,0},{2,1},{3,2},{4,3},{5,4},{6,5},{7,6},{8,7},{9,8},{10,9},{11,1... | collective-permute-start | bytes 393224 | tf_op jit(solution)/shard_map/ppermute | solution.py:457
  (25 other events, 132.4 us)
Sparse Core Ops, SparseCore 0:
  10.2 23.0 all-gather.6
  54.4 53.1 all-gather.8
  109.2 43.2 all-gather.10

commit v23 on v22

--- a/solution.py
+++ b/solution.py
@@ -434,16 +434,15 @@
     rows_in, prepared, attention, own_line, own_crossed = lax.optimization_barrier(
         (rows_in, prepared, attention, own_line, own_crossed)
     )
+    moved = lax.ppermute(w_last, "low", swap) if low == 2 else line(w_last)
+    terms = experts(rows_in.reshape(owners * depth, 2 * width), *prepared)
+    terms, own_line, own_crossed, w_last, moved, near_twin = lax.optimization_barrier(
+        (terms, own_line, own_crossed, w_last, moved, near_twin)
+    )
+    last_line = moved
     if low == 2:
-        moved = lax.ppermute(w_last, "low", swap)
         first = lax.axis_index("low") == 0
         last_line = jnp.where(first, jnp.stack([w_last, moved]), jnp.stack([moved, w_last]))
-    else:
-        last_line = line(w_last)
-    terms = experts(rows_in.reshape(owners * depth, 2 * width), *prepared)
-    terms, own_line, own_crossed, last_line, near_twin = lax.optimization_barrier(
-        (terms, own_line, own_crossed, last_line, near_twin)
-    )
     last_crossed, far_twin = lax.optimization_barrier((cross(last_line), far_twin))
     back = lax.all_to_all(terms.reshape(owners, depth, width), chips, 0, 0, tiled=True)
     both = lambda *pieces: [w for piece in pieces for w in (piece, other_core(piece))]

time: 210 us -> 204 us (0.971)
    all_gather x3, waiting for transfers between devices: 11.5 us -> 26.4 us  [local(): line = lambda w: lax.all_gather(w, 'low', axis=0, tiled=False)]
    ppermute x1, waiting for transfers between devices: 13.7 us -> 0.01 us  [local(): moved = lax.ppermute(w_last, 'low', swap) if low == 2 else line(w_last)]
    all_to_all x1, waiting for transfers between devices: 0.01 us -> 6.76 us  [local(): lax.all_to_all(rows.reshape(owners, depth, 2 * width), chips, 0, 0, tiled...]
    all_to_all x1, waiting for transfers between devices: 6.12 us -> 0.01 us  [local(): lax.all_to_all(terms.reshape(owners, depth, width), chips, 0, 0, tiled=True)]
    ppermute x4, waiting for transfers between devices: 25.7 us -> 22.2 us  [local(): cross = lambda w: lax.ppermute(w, 'groups', swap)]
    ppermute x9, starting transfers between devices: 9.26 us -> 6.74 us  [local(): other_core = lambda w: lax.ppermute(w, 'core', swap)]
    unnamed x50 -> x48, local copies, waits for them, and re-layouts: 19.6 us -> 18.3 us
  transfers between devices with their start and end apart: 24 -> 24, of which waited for: 11 -> 9; matrix products, arithmetic and copies ran while one was open for 4% -> 3% of each run, Pallas kernels for 12% -> 13%
where the time goes in v23:
time: 204 us; the launch traced here: 202 us
  waiting for transfers between devices  88.2 us (43%)
  Pallas kernels  43.6 us (21%)
  starting transfers between devices  30.5 us (15%)
  local copies, waits for them, and re-layouts  19.3 us (9%)
  between operations  14 us (7%)
  other arithmetic  6.61 us (3%)
    all_gather x3, waiting for transfers between devices, local(): line = lambda w: lax.all_gather(w, 'low', axis=0, tiled=False)  26.4 us
    ppermute x4, waiting for transfers between devices, local(): cross = lambda w: lax.ppermute(w, 'groups', swap)  22.2 us
    unnamed x48, local copies, waits for them, and re-layouts  18.3 us
    pallas_call x1, Pallas kernels, tail(): pl.pallas_call(functools.partial(tail_kernel, (heads, tiles)), grid_spec=...  16.6 us
    ppermute x1, waiting for transfers between devices, local(): prev = lax.ppermute(jnp.concatenate([kv, seg_rows], axis=0), blk, onward)  15.4 us
    pallas_call x1, Pallas kernels, experts(): pl.pallas_call(functools.partial(expert_kernel, steps), grid=(steps + wid...  12.9 us
    pallas_call x1, Pallas kernels, prepare_weights(): pl.pallas_call(weights_kernel, grid=(steps,), in_specs=[cols, cols, down]...  8.76 us
    ppermute x9, waiting for transfers between devices, local(): other_core = lambda w: lax.ppermute(w, 'core', swap)  7.53 us
  transfers between devices with their start and end apart: 24, of which 9 were waited for; matrix products, arithmetic and copies ran while one was open for 3% of the time, Pallas kernels for 13%

profile of v23, /device:TPU:13, one launch (start us, length us, event | category | flops | bytes accessed | tf_op | source)
XLA Modules:
  0.0 202.1 jit_solution(16533598813021825148)
XLA Ops:
  9.5 2.3 %collective-permute-start.1 = (bf16[128,2048]{1,0:T(8,128)(2,1)}, bf16[128,2048]{1,0:T(8,128)(2,1)}, u32[]{:S(2)}, u32[]{:S(2)}) collective-permute-start(bf16[128,2048]{1,0:T(8,128)(2,1)} %constant_dynamic-slice_fusion), channel_id=1, source_target_pairs={{0,8},{8,0},{1,9},{9,1},{2,10},{10,2},{3,11},{11,3},{4,12},{12,4},... | collective-permute-start | bytes 1572872 | tf_op jit(solution)/shard_map/ppermute | solution.py:406
  16.4 1.6 copy-done.2
  18.1 3.2 %collective-permute-start.2 = (bf16[144,512]{1,0:T(8,128)(2,1)S(1)}, bf16[144,512]{1,0:T(8,128)(2,1)S(1)}, u32[]{:S(2)}, u32[]{:S(2)}) collective-permute-start(bf16[144,512]{1,0:T(8,128)(2,1)S(1)} %fusion.1), channel_id=1, source_target_pairs={{0,1},{1,2},{2,3},{3,4},{4,5},{5,6},{6,7},{7,8},{8,9},{9,10},{10,1... | collective-permute-start | bytes 442376 | tf_op jit(solution)/shard_map/ppermute | solution.py:420
  21.3 15.4 %collective-permute-done.2.prev_key_ref.prev_value_ref.prev_seg_ref = bf16[144,512]{1,0:T(8,128)(2,1)S(1)} collective-permute-done((bf16[144,512]{1,0:T(8,128)(2,1)S(1)}, bf16[144,512]{1,0:T(8,128)(2,1)S(1)}, u32[]{:S(2)}, u32[]{:S(2)}) %collective-permute-start.2) | collective-permute-done | bytes 147488 | tf_op jit(solution)/shard_map/ppermute | solution.py:420
  37.5 3.6 %all-to-all-start = ((bf16[8,48,4096]{2,1,0:T(8,128)(2,1)}), bf16[8,48,4096]{2,1,0:T(8,128)(2,1)S(1)}, u32[]{:S(2)}, u32[]{:S(2)}) async-start(bf16[8,48,4096]{2,1,0:T(8,128)(2,1)} %bitcast.25), calls=%async_computation | async-start | bytes 6291456 | tf_op jit(solution)/shard_map/all_to_all | solution.py:424
  42.4 9.7 %collective-permute-done.7 = bf16[128,2048]{1,0:T(8,128)(2,1)S(1)} collective-permute-done((bf16[128,2048]{1,0:T(8,128)(2,1)}, bf16[128,2048]{1,0:T(8,128)(2,1)S(1)}, u32[]{:S(2)}, u32[]{:S(2)}) %collective-permute-start.7) | collective-permute-done | bytes 524320 | tf_op jit(solution)/shard_map/ppermute | solution.py:411
  52.1 2.1 %pad_maximum_fusion = bf16[2,128,2048]{2,1,0:T(8,128)(2,1)} fusion(bf16[1,128,2048]{2,1,0:T(8,128)(2,1)S(1)} %bitcast.38, bf16[1,128,2048]{2,1,0:T(8,128)(2,1)} %bitcast.36), kind=kLoop, calls=%fused_computation | loop fusion | flops 524288 | bytes 2097152 | tf_op jit(solution)/shard_map/stack | solution.py:426
  54.3 3.7 %collective-permute-start.4 = (bf16[2048,384]{1,0:T(8,128)(2,1)}, bf16[2048,384]{1,0:T(8,128)(2,1)}, u32[]{:S(2)}, u32[]{:S(2)}) collective-permute-start(bf16[2048,384]{1,0:T(8,128)(2,1)} %refs_0_.1), channel_id=1, source_target_pairs={{0,1},{1,0},{2,3},{3,2},{4,5},{5,4},{6,7},{7,6},{8,9},{9,8},{10,11... | collective-permute-start | bytes 4718600 | tf_op jit(solution)/shard_map/ppermute | solution.py:412
  59.8 12.6 %collective-permute-done.8 = bf16[128,2048]{1,0:T(8,128)(2,1)S(1)} collective-permute-done((bf16[128,2048]{1,0:T(8,128)(2,1)}, bf16[128,2048]{1,0:T(8,128)(2,1)S(1)}, u32[]{:S(2)}, u32[]{:S(2)}) %collective-permute-start.8) | collective-permute-done | bytes 524320 | tf_op jit(solution)/shard_map/ppermute | solution.py:411
  73.8 2.2 %pad_maximum_fusion.1 = bf16[2,128,2048]{2,1,0:T(8,128)(2,1)} fusion(bf16[1,128,2048]{2,1,0:T(8,128)(2,1)S(1)} %bitcast.37, bf16[1,128,2048]{2,1,0:T(8,128)(2,1)} %bitcast.18), kind=kLoop, calls=%fused_computation.2 | loop fusion | flops 524288 | bytes 2097152 | tf_op jit(solution)/shard_map/stack | solution.py:427
  77.4 3.5 %attention_shares.1 = (bf16[2,2048,256]{2,1,0:T(8,128)(2,1)S(1)}, bf16[2,256,2048]{2,1,0:T(8,128)(2,1)S(1)}, bf16[2,2048,128]{2,1,0:T(8,128)(2,1)S(1)}, bf16[2,2...) custom-call(bf16[128,4096]{1,0:T(8,128)(2,1)S(1)} %copy-done.8, bf16[128,256]{1,0:T(8,128)(2,1)S(1)} %copy-done.11, ...), custom_call_target="tpu_custom_call" | custom-call | tf_op jit(solution)/shard_map/attention_shares/pallas_call | solution.py:201
  87.3 1.4 copy-done.7
  88.7 8.8 %prepare_weights.1 = (bf16[3,2048,512]{2,1,0:T(8,128)(2,1)}, bf16[3,2048,256]{2,1,0:T(8,128)(2,1)}, bf16[3,512,2048]{2,1,0:T(8,128)(2,1)}) custom-call(bf16[2048,384]{1,0:T(8,128)(2,1)S(1)} %copy-done.5, bf16[2048,384]{1,0:T(8,128)(2,1)S(1)} %copy-done.6, bf16[384,2048]{1,0:T(8,128)(2,1)S(1)} %copy-done.7, bf16[2048,384]{1,0:T(8,128)(2,1)} %collective-permute-done.4.refs_3_, ...), custom_call_target="tpu_custom_call" | custom-call | tf_op jit(solution)/shard_map/prepare_weights/pallas_call | solution.py:94
  97.5 4.7 %collective-permute-done.3 = bf16[128,2048]{1,0:T(8,128)(2,1)} collective-permute-done((bf16[128,2048]{1,0:T(8,128)(2,1)}, bf16[128,2048]{1,0:T(8,128)(2,1)}, u32[]{:S(2)}, u32[]{:S(2)}) %collective-permute-start.3) | collective-permute-done | bytes 524320 | tf_op jit(solution)/shard_map/ppermute | solution.py:430
  102.7 6.8 %all-to-all-done = bf16[8,48,4096]{2,1,0:T(8,128)(2,1)S(1)} async-done(((bf16[8,48,4096]{2,1,0:T(8,128)(2,1)}), bf16[8,48,4096]{2,1,0:T(8,128)(2,1)S(1)}, u32[]{:S(2)}, u32[]{:S(2)}) %all-to-all-start) | async-done | bytes 3145760 | tf_op jit(solution)/shard_map/all_to_all | solution.py:424
  109.4 12.9 %expert_terms.1 = bf16[384,2048]{1,0:T(8,128)(2,1)} custom-call(bf16[384,4096]{1,0:T(8,128)(2,1)S(1)} %bitcast.24, bf16[3,2048,512]{2,1,0:T(8,128)(2,1)} %get-tuple-element.98.cols_ref, bf16[3,2048,256]{2,1,0:T(8,128)(2,1)} %get-tuple-element.99.down_ref, bf16[3,512,2048]{2,1,0:T(8,128)(2,1)} %get-tuple-element.100.back_ref), custom_call_target="tpu_custom_call" | custom-call | tf_op jit(solution)/shard_map/expert_terms/pallas_call | solution.py:145
  122.3 1.7 maximum_select_fusion.refs_4_
  125.3 6.3 %all-to-all-start.1 = ((bf16[8,48,2048]{2,1,0:T(8,128)(2,1)}), bf16[8,48,2048]{2,1,0:T(8,128)(2,1)S(1)}, u32[]{:S(2)}, u32[]{:S(2)}) async-start(bf16[8,48,2048]{2,1,0:T(8,128)(2,1)} %bitcast.14), calls=%async_computation.1 | async-start | bytes 3145728 | tf_op jit(solution)/shard_map/all_to_all | solution.py:447
  133.0 26.4 %all-gather.11.cloned.1.call-done = bf16[4,128,2048]{2,1,0:T(8,128)(2,1)} async-done(((bf16[2,128,2048]{2,1,0:T(8,128)(2,1)}), bf16[4,128,2048]{2,1,0:T(8,128)(2,1)}) %all-gather.11.cloned.1.call-update) | async-done | bytes 2097168 | tf_op jit(solution)/shard_map/all_gather | solution.py:410
  161.2 6.0 %collective-permute-done.12.refs_3_ = bf16[2,128,2048]{2,1,0:T(8,128)(2,1)} collective-permute-done((bf16[2,128,2048]{2,1,0:T(8,128)(2,1)}, bf16[2,128,2048]{2,1,0:T(8,128)(2,1)}, u32[]{:S(2)}, u32[]{:S(2)}) %collective-permute-start.12) | collective-permute-done | bytes 1048608 | tf_op jit(solution)/shard_map/ppermute | solution.py:412
  167.2 1.5 collective-permute-done.15.refs_7_
  169.9 16.6 %tail_attention.1 = (bf16[128,2048]{1,0:T(8,128)(2,1)}, bf16[128,4096]{1,0:T(8,128)(2,1)}, f32[2,128,256]{2,1,0:T(8,128)}, bf16[2,128,256]{2,1,0:T(8,128)(2,1)}) custom-call(s32[3]{0:T(128)} %pad_add_fusion.place_info, bf16[384,2048]{1,0:T(8,128)(2,1)} %bitcast.28, bf16[128,384]{1,0:T(8,128)(2,1)} %copy-done.16, bf16[128,2048]{1,0:T(8,128)(2,1)} %grad_ref.3, ...), custom_call_target="tpu_custom_call" | custom-call | flops 2147483648 | bytes 23068672 | tf_op jit(solution)/shard_map/tail_attention/pallas_call | solution.py:320
  186.5 2.3 %collective-permute-start.18 = (bf16[2,128,256]{2,1,0:T(8,128)(2,1)}, bf16[2,128,256]{2,1,0:T(8,128)(2,1)S(1)}, u32[]{:S(2)}, u32[]{:S(2)}) collective-permute-start(bf16[2,128,256]{2,1,0:T(8,128)(2,1)} %get-tuple-element.121), channel_id=1, source_target_pairs={{1,0},{2,1},{3,2},{4,3},{5,4},{6,5},{7,6},{8,7},{9,8},{10,9},{11,1... | collective-permute-start | bytes 393224 | tf_op jit(solution)/shard_map/ppermute | solution.py:456
  188.8 5.1 %collective-permute-done.18.later_ref = bf16[2,128,256]{2,1,0:T(8,128)(2,1)S(1)} collective-permute-done((bf16[2,128,256]{2,1,0:T(8,128)(2,1)}, bf16[2,128,256]{2,1,0:T(8,128)(2,1)S(1)}, u32[]{:S(2)}, u32[]{:S(2)}) %collective-permute-start.18) | collective-permute-done | bytes 131104 | tf_op jit(solution)/shard_map/ppermute | solution.py:456
  (89 shorter events, 27.7 us)
Async XLA Ops:
  7.2 30.3 %all-gather.7.cloned.1.call-start = ((), (), s32[]{:S(2)}) async-start(), calls=%async_computation.2 | async-start | bytes 1572864 | tf_op jit(solution)/shard_map/all_gather | solution.py:410
  9.3 27.4 %collective-permute-start = (bf16[128,2048]{1,0:T(8,128)(2,1)}, bf16[128,2048]{1,0:T(8,128)(2,1)S(1)}, u32[]{:S(2)}, u32[]{:S(2)}) collective-permute-start(bf16[128,2048]{1,0:T(8,128)(2,1)} %constant_dynamic-slice_fusion), channel_id=1, source_target_pairs={{0,4},{4,0},{1,5},{5,1},{2,6},{6,2},{3,7},{7,3},{8,12},{12,8},{9,1... | collective-permute-start | bytes 1572872 | tf_op jit(solution)/shard_map/ppermute | solution.py:407
  9.5 28.0 %collective-permute-start.1 = (bf16[128,2048]{1,0:T(8,128)(2,1)}, bf16[128,2048]{1,0:T(8,128)(2,1)}, u32[]{:S(2)}, u32[]{:S(2)}) collective-permute-start(bf16[128,2048]{1,0:T(8,128)(2,1)} %constant_dynamic-slice_fusion), channel_id=1, source_target_pairs={{0,8},{8,0},{1,9},{9,1},{2,10},{10,2},{3,11},{11,3},{4,12},{12,4},... | collective-permute-start | bytes 1572872 | tf_op jit(solution)/shard_map/ppermute | solution.py:406
  18.1 18.6 %collective-permute-start.2 = (bf16[144,512]{1,0:T(8,128)(2,1)S(1)}, bf16[144,512]{1,0:T(8,128)(2,1)S(1)}, u32[]{:S(2)}, u32[]{:S(2)}) collective-permute-start(bf16[144,512]{1,0:T(8,128)(2,1)S(1)} %fusion.1), channel_id=1, source_target_pairs={{0,1},{1,2},{2,3},{3,4},{4,5},{5,6},{6,7},{7,8},{8,9},{9,10},{10,1... | collective-permute-start | bytes 442376 | tf_op jit(solution)/shard_map/ppermute | solution.py:420
  37.5 71.9 %all-to-all-start = ((bf16[8,48,4096]{2,1,0:T(8,128)(2,1)}), bf16[8,48,4096]{2,1,0:T(8,128)(2,1)S(1)}, u32[]{:S(2)}, u32[]{:S(2)}) async-start(bf16[8,48,4096]{2,1,0:T(8,128)(2,1)} %bitcast.25), calls=%async_computation | async-start | bytes 6291456 | tf_op jit(solution)/shard_map/all_to_all | solution.py:424
  41.1 81.1 %all-gather.9.cloned.1.call-start = ((), (), s32[]{:S(2)}) async-start(), calls=%async_computation.3 | async-start | bytes 3145728 | tf_op jit(solution)/shard_map/all_gather | solution.py:410
  41.2 10.9 %collective-permute-start.7 = (bf16[128,2048]{1,0:T(8,128)(2,1)}, bf16[128,2048]{1,0:T(8,128)(2,1)S(1)}, u32[]{:S(2)}, u32[]{:S(2)}) collective-permute-start(bf16[128,2048]{1,0:T(8,128)(2,1)} %copy-done.22), channel_id=1, source_target_pairs={{0,16},{16,0},{1,17},{17,1},{2,18},{18,2},{3,19},{19,3},{4,20},{20... | collective-permute-start | bytes 1572872 | tf_op jit(solution)/shard_map/ppermute | solution.py:411
  54.2 105.1 %all-gather.11.cloned.1.call-start = ((), (), s32[]{:S(2)}) async-start(), calls=%async_computation.4 | async-start | bytes 3145728 | tf_op jit(solution)/shard_map/all_gather | solution.py:410
  54.3 31.6 %collective-permute-start.4 = (bf16[2048,384]{1,0:T(8,128)(2,1)}, bf16[2048,384]{1,0:T(8,128)(2,1)}, u32[]{:S(2)}, u32[]{:S(2)}) collective-permute-start(bf16[2048,384]{1,0:T(8,128)(2,1)} %refs_0_.1), channel_id=1, source_target_pairs={{0,1},{1,0},{2,3},{3,2},{4,5},{5,4},{6,7},{7,6},{8,9},{9,8},{10,11... | collective-permute-start | bytes 4718600 | tf_op jit(solution)/shard_map/ppermute | solution.py:412
  58.0 27.9 %collective-permute-start.5 = (bf16[2048,384]{1,0:T(8,128)(2,1)}, bf16[2048,384]{1,0:T(8,128)(2,1)}, u32[]{:S(2)}, u32[]{:S(2)}) collective-permute-start(bf16[2048,384]{1,0:T(8,128)(2,1)} %refs_1_.1), channel_id=1, source_target_pairs={{0,1},{1,0},{2,3},{3,2},{4,5},{5,4},{6,7},{7,6},{8,9},{9,8},{10,11... | collective-permute-start | bytes 4718600 | tf_op jit(solution)/shard_map/ppermute | solution.py:412
  58.1 27.8 %collective-permute-start.6 = (bf16[384,2048]{1,0:T(8,128)(2,1)}, bf16[384,2048]{1,0:T(8,128)(2,1)}, u32[]{:S(2)}, u32[]{:S(2)}) collective-permute-start(bf16[384,2048]{1,0:T(8,128)(2,1)} %refs_2_.1), channel_id=1, source_target_pairs={{0,1},{1,0},{2,3},{3,2},{4,5},{5,4},{6,7},{7,6},{8,9},{9,8},{10,11... | collective-permute-start | bytes 4718600 | tf_op jit(solution)/shard_map/ppermute | solution.py:412
  58.5 13.8 %collective-permute-start.8 = (bf16[128,2048]{1,0:T(8,128)(2,1)}, bf16[128,2048]{1,0:T(8,128)(2,1)S(1)}, u32[]{:S(2)}, u32[]{:S(2)}) collective-permute-start(bf16[128,2048]{1,0:T(8,128)(2,1)} %collective-permute-done.1), channel_id=1, source_target_pairs={{0,16},{16,0},{1,17},{17,1},{2,18},{18,2},{3,19},{19,3},{4,20},{20... | collective-permute-start | bytes 1572872 | tf_op jit(solution)/shard_map/ppermute | solution.py:411
  72.4 30.3 %collective-permute-start.9 = (bf16[2,128,2048]{2,1,0:T(8,128)(2,1)}, bf16[2,128,2048]{2,1,0:T(8,128)(2,1)}, u32[]{:S(2)}, u32[]{:S(2)}) collective-permute-start(bf16[2,128,2048]{2,1,0:T(8,128)(2,1)} %bitcast.33), channel_id=1, source_target_pairs={{0,16},{16,0},{1,17},{17,1},{2,18},{18,2},{3,19},{19,3},{4,20},{20... | collective-permute-start | bytes 3145736 | tf_op jit(solution)/shard_map/ppermute | solution.py:411
  73.6 28.6 %collective-permute-start.3 = (bf16[128,2048]{1,0:T(8,128)(2,1)}, bf16[128,2048]{1,0:T(8,128)(2,1)}, u32[]{:S(2)}, u32[]{:S(2)}) collective-permute-start(bf16[128,2048]{1,0:T(8,128)(2,1)} %collective-permute-done.1), channel_id=1, source_target_pairs={{0,4},{4,0},{1,5},{5,1},{2,6},{6,2},{3,7},{7,3},{8,12},{12,8},{9,1... | collective-permute-start | bytes 1572872 | tf_op jit(solution)/shard_map/ppermute | solution.py:430
  102.2 20.1 %collective-permute-start.10 = (bf16[128,2048]{1,0:T(8,128)(2,1)}, bf16[128,2048]{1,0:T(8,128)(2,1)}, u32[]{:S(2)}, u32[]{:S(2)}) collective-permute-start(bf16[128,2048]{1,0:T(8,128)(2,1)} %collective-permute-done.3), channel_id=1, source_target_pairs={{0,2},{2,0},{1,3},{3,1},{4,6},{6,4},{5,7},{7,5},{8,10},{10,8},{9,1... | collective-permute-start | bytes 1572872 | tf_op jit(solution)/shard_map/ppermute | solution.py:437
  124.0 35.3 %collective-permute-start.14 = (bf16[2,128,2048]{2,1,0:T(8,128)(2,1)S(1)}, bf16[2,128,2048]{2,1,0:T(8,128)(2,1)}, u32[]{:S(2)}, u32[]{:S(2)}) collective-permute-start(bf16[2,128,2048]{2,1,0:T(8,128)(2,1)S(1)} %maximum_select_fusion.refs_4_), channel_id=1, source_target_pairs={{0,16},{16,0},{1,17},{17,1},{2,18},{18,2},{3,19},{19,3},{4,20},{20... | collective-permute-start | bytes 3145736 | tf_op jit(solution)/shard_map/ppermute | solution.py:411
  125.3 43.4 %all-to-all-start.1 = ((bf16[8,48,2048]{2,1,0:T(8,128)(2,1)}), bf16[8,48,2048]{2,1,0:T(8,128)(2,1)S(1)}, u32[]{:S(2)}, u32[]{:S(2)}) async-start(bf16[8,48,2048]{2,1,0:T(8,128)(2,1)} %bitcast.14), calls=%async_computation.1 | async-start | bytes 3145728 | tf_op jit(solution)/shard_map/all_to_all | solution.py:447
  131.7 28.9 %collective-permute-start.11 = (bf16[2,128,2048]{2,1,0:T(8,128)(2,1)}, bf16[2,128,2048]{2,1,0:T(8,128)(2,1)}, u32[]{:S(2)}, u32[]{:S(2)}) collective-permute-start(bf16[2,128,2048]{2,1,0:T(8,128)(2,1)} %bitcast.34), channel_id=1, source_target_pairs={{0,1},{1,0},{2,3},{3,2},{4,5},{5,4},{6,7},{7,6},{8,9},{9,8},{10,11... | collective-permute-start | bytes 3145736 | tf_op jit(solution)/shard_map/ppermute | solution.py:412
  133.0 35.7 %collective-permute-start.16 = (bf16[2,2,128,2048]{3,2,1,0:T(8,128)(2,1)}, bf16[2,2,128,2048]{3,2,1,0:T(8,128)(2,1)}, u32[]{:S(2)}, u32[]{:S(2)}) collective-permute-start(bf16[2,2,128,2048]{3,2,1,0:T(8,128)(2,1)} %bitcast.29), channel_id=1, source_target_pairs={{0,1},{1,0},{2,3},{3,2},{4,5},{5,4},{6,7},{7,6},{8,9},{9,8},{10,11... | collective-permute-start | bytes 6291464 | tf_op jit(solution)/shard_map/ppermute | solution.py:412
  159.4 9.3 %collective-permute-start.17 = (bf16[2,2,128,2048]{3,2,1,0:T(8,128)(2,1)}, bf16[2,2,128,2048]{3,2,1,0:T(8,128)(2,1)}, u32[]{:S(2)}, u32[]{:S(2)}) collective-permute-start(bf16[2,2,128,2048]{3,2,1,0:T(8,128)(2,1)} %bitcast.31), channel_id=1, source_target_pairs={{0,1},{1,0},{2,3},{3,2},{4,5},{5,4},{6,7},{7,6},{8,9},{9,8},{10,11... | collective-permute-start | bytes 6291464 | tf_op jit(solution)/shard_map/ppermute | solution.py:412
  160.0 7.1 %collective-permute-start.13 = (bf16[2,128,2048]{2,1,0:T(8,128)(2,1)S(1)}, bf16[2,128,2048]{2,1,0:T(8,128)(2,1)}, u32[]{:S(2)}, u32[]{:S(2)}) collective-permute-start(bf16[2,128,2048]{2,1,0:T(8,128)(2,1)S(1)} %maximum_select_fusion.refs_4_), channel_id=1, source_target_pairs={{0,1},{1,0},{2,3},{3,2},{4,5},{5,4},{6,7},{7,6},{8,9},{9,8},{10,11... | collective-permute-start | bytes 3145736 | tf_op jit(solution)/shard_map/ppermute | solution.py:412
  160.0 7.1 %collective-permute-start.12 = (bf16[2,128,2048]{2,1,0:T(8,128)(2,1)}, bf16[2,128,2048]{2,1,0:T(8,128)(2,1)}, u32[]{:S(2)}, u32[]{:S(2)}) collective-permute-start(bf16[2,128,2048]{2,1,0:T(8,128)(2,1)} %collective-permute-done.9.refs_2_), channel_id=1, source_target_pairs={{0,1},{1,0},{2,3},{3,2},{4,5},{5,4},{6,7},{7,6},{8,9},{9,8},{10,11... | collective-permute-start | bytes 3145736 | tf_op jit(solution)/shard_map/ppermute | solution.py:412
  160.6 8.1 %collective-permute-start.15 = (bf16[2,128,2048]{2,1,0:T(8,128)(2,1)}, bf16[2,128,2048]{2,1,0:T(8,128)(2,1)}, u32[]{:S(2)}, u32[]{:S(2)}) collective-permute-start(bf16[2,128,2048]{2,1,0:T(8,128)(2,1)} %collective-permute-done.14.refs_6_), channel_id=1, source_target_pairs={{0,1},{1,0},{2,3},{3,2},{4,5},{5,4},{6,7},{7,6},{8,9},{9,8},{10,11... | collective-permute-start | bytes 3145736 | tf_op jit(solution)/shard_map/ppermute | solution.py:412
  186.5 7.4 %collective-permute-start.18 = (bf16[2,128,256]{2,1,0:T(8,128)(2,1)}, bf16[2,128,256]{2,1,0:T(8,128)(2,1)S(1)}, u32[]{:S(2)}, u32[]{:S(2)}) collective-permute-start(bf16[2,128,256]{2,1,0:T(8,128)(2,1)} %get-tuple-element.121), channel_id=1, source_target_pairs={{1,0},{2,1},{3,2},{4,3},{5,4},{6,5},{7,6},{8,7},{9,8},{10,9},{11,1... | collective-permute-start | bytes 393224 | tf_op jit(solution)/shard_map/ppermute | solution.py:456
  (24 other events, 149.9 us)
Sparse Core Ops, SparseCore 0:
  10.2 23.0 all-gather.6
  54.4 53.2 all-gather.8
  109.2 50.1 all-gather.10

commit v24 on v23

--- a/solution.py
+++ b/solution.py
@@ -419,7 +419,7 @@
     seg_rows = jnp.zeros((16, kv.shape[1]), jnp.bfloat16).at[0, :tokens].set(segs.astype(jnp.bfloat16))
     prev = lax.ppermute(jnp.concatenate([kv, seg_rows], axis=0), blk, onward)
     own_line = line(w_share)
-    rows, w_near, w_far, own_line, prev = lax.optimization_barrier((rows, w_near, w_far, own_line, prev))
+    rows, w_far, own_line, prev = lax.optimization_barrier((rows, w_far, own_line, prev))
 
     rows_in = lax.all_to_all(rows.reshape(owners, depth, 2 * width), chips, 0, 0, tiled=True)
     near_crossed, far_crossed = cross(w_near), cross(w_far)

time: 204 us -> 259 us (1.27)
  waiting for transfers between devices: 88.2 us -> 138 us
  starting transfers between devices: 30.5 us -> 34.4 us
    ppermute x1, waiting for transfers between devices: 0.01 us -> 62 us  [local(): w_near = lax.ppermute(w_share, 'near', swap)]
    all_gather x3, waiting for transfers between devices: 26.4 us -> 17.1 us  [local(): line = lambda w: lax.all_gather(w, 'low', axis=0, tiled=False)]
    all_to_all x1, waiting for transfers between devices: 6.76 us -> 0.01 us  [local(): lax.all_to_all(rows.reshape(owners, depth, 2 * width), chips, 0, 0, tiled...]
    ppermute x1, waiting for transfers between devices: 0.01 us -> 6.65 us  [local(): moved = lax.ppermute(w_last, 'low', swap) if low == 2 else line(w_last)]
    ppermute x1, waiting for transfers between devices: 4.69 us -> 0.01 us  [local(): w_last = lax.ppermute(w_far, 'near', swap)]
    ppermute x9, starting transfers between devices: 6.74 us -> 9.95 us  [local(): other_core = lambda w: lax.ppermute(w, 'core', swap)]
    unnamed x48 -> x46, local copies, waits for them, and re-layouts: 18.3 us -> 17.5 us
  transfers between devices with their start and end apart: 24 -> 24, of which waited for: 9 -> 10; matrix products, arithmetic and copies ran while one was open for 3% -> 2% of each run, Pallas kernels for 13% -> 10%
where the time goes in v24:
time: 259 us; the launch traced here: 255 us
  waiting for transfers between devices  138 us (53%)
  Pallas kernels  43.9 us (17%)
  starting transfers between devices  34.4 us (13%)
  local copies, waits for them, and re-layouts  18.5 us (7%)
  between operations  13.9 us (5%)
  other arithmetic  5.54 us (2%)
    ppermute x1, waiting for transfers between devices, local(): w_near = lax.ppermute(w_share, 'near', swap)  62 us
    ppermute x4, waiting for transfers between devices, local(): cross = lambda w: lax.ppermute(w, 'groups', swap)  22.5 us
    unnamed x46, local copies, waits for them, and re-layouts  17.5 us
    all_gather x3, waiting for transfers between devices, local(): line = lambda w: lax.all_gather(w, 'low', axis=0, tiled=False)  17.1 us
    pallas_call x1, Pallas kernels, tail(): pl.pallas_call(functools.partial(tail_kernel, (heads, tiles)), grid_spec=...  16.6 us
    ppermute x1, waiting for transfers between devices, local(): prev = lax.ppermute(jnp.concatenate([kv, seg_rows], axis=0), blk, onward)  16.4 us
    pallas_call x1, Pallas kernels, experts(): pl.pallas_call(functools.partial(expert_kernel, steps), grid=(steps + wid...  13.1 us
    ppermute x9, starting transfers between devices, local(): other_core = lambda w: lax.ppermute(w, 'core', swap)  9.95 us
  transfers between devices with their start and end apart: 24, of which 10 were waited for; matrix products, arithmetic and copies ran while one was open for 2% of the time, Pallas kernels for 10%

profile of v24, /device:TPU:13, one launch (start us, length us, event | category | flops | bytes accessed | tf_op | source)
XLA Modules:
  0.0 254.6 jit_solution(13068184904264604705)
XLA Ops:
  9.3 2.4 collective-permute-start
  16.3 1.7 copy-done.2
  18.0 1.9 collective-permute-start.1
  19.9 16.4 %collective-permute-done.1.prev_key_ref.prev_value_ref.prev_seg_ref = bf16[144,512]{1,0:T(8,128)(2,1)S(1)} collective-permute-done((bf16[144,512]{1,0:T(8,128)(2,1)S(1)}, bf16[144,512]{1,0:T(8,128)(2,1)S(1)}, u32[]{:S(2)}, u32[]{:S(2)}) %collective-permute-start.1) | collective-permute-done | bytes 147488 | tf_op jit(solution)/shard_map/ppermute | solution.py:420
  36.3 4.9 %all-to-all-start = ((bf16[8,48,4096]{2,1,0:T(8,128)(2,1)}), bf16[8,48,4096]{2,1,0:T(8,128)(2,1)S(1)}, u32[]{:S(2)}, u32[]{:S(2)}) async-start(bf16[8,48,4096]{2,1,0:T(8,128)(2,1)} %bitcast.25), calls=%async_computation | async-start | bytes 6291456 | tf_op jit(solution)/shard_map/all_to_all | solution.py:424
  41.5 62.0 %collective-permute-done.6 = bf16[128,2048]{1,0:T(8,128)(2,1)S(1)} collective-permute-done((bf16[128,2048]{1,0:T(8,128)(2,1)}, bf16[128,2048]{1,0:T(8,128)(2,1)S(1)}, u32[]{:S(2)}, u32[]{:S(2)}) %collective-permute-start.6) | collective-permute-done | bytes 524320 | tf_op jit(solution)/shard_map/ppermute | solution.py:407
  104.7 9.9 %collective-permute-done.7 = bf16[128,2048]{1,0:T(8,128)(2,1)S(1)} collective-permute-done((bf16[128,2048]{1,0:T(8,128)(2,1)S(1)}, bf16[128,2048]{1,0:T(8,128)(2,1)S(1)}, u32[]{:S(2)}, u32[]{:S(2)}) %collective-permute-start.7) | collective-permute-done | bytes 524320 | tf_op jit(solution)/shard_map/ppermute | solution.py:411
  115.7 3.2 %collective-permute-start.3 = (bf16[2048,384]{1,0:T(8,128)(2,1)}, bf16[2048,384]{1,0:T(8,128)(2,1)}, u32[]{:S(2)}, u32[]{:S(2)}) collective-permute-start(bf16[2048,384]{1,0:T(8,128)(2,1)} %refs_0_.1), channel_id=1, source_target_pairs={{0,1},{1,0},{2,3},{3,2},{4,5},{5,4},{6,7},{7,6},{8,9},{9,8},{10,11... | collective-permute-start | bytes 4718600 | tf_op jit(solution)/shard_map/ppermute | solution.py:412
  120.7 12.6 %collective-permute-done.8 = bf16[128,2048]{1,0:T(8,128)(2,1)S(1)} collective-permute-done((bf16[128,2048]{1,0:T(8,128)(2,1)}, bf16[128,2048]{1,0:T(8,128)(2,1)S(1)}, u32[]{:S(2)}, u32[]{:S(2)}) %collective-permute-start.8) | collective-permute-done | bytes 524320 | tf_op jit(solution)/shard_map/ppermute | solution.py:411
  134.5 2.2 pad_maximum_fusion.1
  138.2 3.5 %attention_shares.1 = (bf16[2,2048,256]{2,1,0:T(8,128)(2,1)S(1)}, bf16[2,256,2048]{2,1,0:T(8,128)(2,1)S(1)}, bf16[2,2048,128]{2,1,0:T(8,128)(2,1)S(1)}, bf16[2,2...) custom-call(bf16[128,4096]{1,0:T(8,128)(2,1)S(1)} %copy-done.8, bf16[128,256]{1,0:T(8,128)(2,1)S(1)} %copy-done.11, ...), custom_call_target="tpu_custom_call" | custom-call | tf_op jit(solution)/shard_map/attention_shares/pallas_call | solution.py:201
  149.5 8.8 %prepare_weights.1 = (bf16[3,2048,512]{2,1,0:T(8,128)(2,1)}, bf16[3,2048,256]{2,1,0:T(8,128)(2,1)}, bf16[3,512,2048]{2,1,0:T(8,128)(2,1)}) custom-call(bf16[2048,384]{1,0:T(8,128)(2,1)S(1)} %copy-done.5, bf16[2048,384]{1,0:T(8,128)(2,1)S(1)} %copy-done.6, bf16[384,2048]{1,0:T(8,128)(2,1)S(1)} %copy-done.7, bf16[2048,384]{1,0:T(8,128)(2,1)} %collective-permute-done.3.refs_3_, ...), custom_call_target="tpu_custom_call" | custom-call | tf_op jit(solution)/shard_map/prepare_weights/pallas_call | solution.py:94
  158.8 13.1 %expert_terms.1 = bf16[384,2048]{1,0:T(8,128)(2,1)} custom-call(bf16[384,4096]{1,0:T(8,128)(2,1)S(1)} %bitcast.24, bf16[3,2048,512]{2,1,0:T(8,128)(2,1)} %get-tuple-element.96.cols_ref, bf16[3,2048,256]{2,1,0:T(8,128)(2,1)} %get-tuple-element.97.down_ref, bf16[3,512,2048]{2,1,0:T(8,128)(2,1)} %get-tuple-element.98.back_ref), custom_call_target="tpu_custom_call" | custom-call | tf_op jit(solution)/shard_map/expert_terms/pallas_call | solution.py:145
  172.0 6.7 %collective-permute-done.10 = bf16[128,2048]{1,0:T(8,128)(2,1)} collective-permute-done((bf16[128,2048]{1,0:T(8,128)(2,1)}, bf16[128,2048]{1,0:T(8,128)(2,1)}, u32[]{:S(2)}, u32[]{:S(2)}) %collective-permute-start.10) | collective-permute-done | bytes 524320 | tf_op jit(solution)/shard_map/ppermute | solution.py:437
  178.6 1.7 maximum_select_fusion.refs_4_
  180.4 7.2 %all-to-all-start.1 = ((bf16[8,48,2048]{2,1,0:T(8,128)(2,1)}), bf16[8,48,2048]{2,1,0:T(8,128)(2,1)S(1)}, u32[]{:S(2)}, u32[]{:S(2)}) async-start(bf16[8,48,2048]{2,1,0:T(8,128)(2,1)} %bitcast.14), calls=%async_computation.1 | async-start | bytes 3145728 | tf_op jit(solution)/shard_map/all_to_all | solution.py:447
  187.6 5.2 %collective-permute-start.11 = (bf16[2,128,2048]{2,1,0:T(8,128)(2,1)}, bf16[2,128,2048]{2,1,0:T(8,128)(2,1)}, u32[]{:S(2)}, u32[]{:S(2)}) collective-permute-start(bf16[2,128,2048]{2,1,0:T(8,128)(2,1)} %bitcast.34), channel_id=1, source_target_pairs={{0,1},{1,0},{2,3},{3,2},{4,5},{5,4},{6,7},{7,6},{8,9},{9,8},{10,11... | collective-permute-start | bytes 3145736 | tf_op jit(solution)/shard_map/ppermute | solution.py:412
  192.8 17.1 %all-gather.11.cloned.1.call-done = bf16[4,128,2048]{2,1,0:T(8,128)(2,1)} async-done(((bf16[2,128,2048]{2,1,0:T(8,128)(2,1)}), bf16[4,128,2048]{2,1,0:T(8,128)(2,1)}) %all-gather.11.cloned.1.call-update) | async-done | bytes 2097168 | tf_op jit(solution)/shard_map/all_gather | solution.py:410
  211.5 6.0 %collective-permute-done.12.refs_3_ = bf16[2,128,2048]{2,1,0:T(8,128)(2,1)} collective-permute-done((bf16[2,128,2048]{2,1,0:T(8,128)(2,1)}, bf16[2,128,2048]{2,1,0:T(8,128)(2,1)}, u32[]{:S(2)}, u32[]{:S(2)}) %collective-permute-start.12) | collective-permute-done | bytes 1048608 | tf_op jit(solution)/shard_map/ppermute | solution.py:412
  217.4 1.5 collective-permute-done.15.refs_7_
  218.9 2.1 all-to-all-done.1
  222.2 16.6 %tail_attention.1 = (bf16[128,2048]{1,0:T(8,128)(2,1)}, bf16[128,4096]{1,0:T(8,128)(2,1)}, f32[2,128,256]{2,1,0:T(8,128)}, bf16[2,128,256]{2,1,0:T(8,128)(2,1)}) custom-call(s32[3]{0:T(128)} %pad_add_fusion.place_info, bf16[384,2048]{1,0:T(8,128)(2,1)} %bitcast.28, bf16[128,384]{1,0:T(8,128)(2,1)} %copy-done.16, bf16[128,2048]{1,0:T(8,128)(2,1)} %grad_ref.3, ...), custom_call_target="tpu_custom_call" | custom-call | flops 2147483648 | bytes 23068672 | tf_op jit(solution)/shard_map/tail_attention/pallas_call | solution.py:320
  238.8 3.5 %collective-permute-start.18 = (bf16[2,128,256]{2,1,0:T(8,128)(2,1)}, bf16[2,128,256]{2,1,0:T(8,128)(2,1)S(1)}, u32[]{:S(2)}, u32[]{:S(2)}) collective-permute-start(bf16[2,128,256]{2,1,0:T(8,128)(2,1)} %get-tuple-element.119), channel_id=1, source_target_pairs={{1,0},{2,1},{3,2},{4,3},{5,4},{6,5},{7,6},{8,7},{9,8},{10,9},{11,1... | collective-permute-start | bytes 393224 | tf_op jit(solution)/shard_map/ppermute | solution.py:456
  242.3 4.1 %collective-permute-done.18.later_ref = bf16[2,128,256]{2,1,0:T(8,128)(2,1)S(1)} collective-permute-done((bf16[2,128,256]{2,1,0:T(8,128)(2,1)}, bf16[2,128,256]{2,1,0:T(8,128)(2,1)S(1)}, u32[]{:S(2)}, u32[]{:S(2)}) %collective-permute-start.18) | collective-permute-done | bytes 131104 | tf_op jit(solution)/shard_map/ppermute | solution.py:456
  (87 shorter events, 26.6 us)
Async XLA Ops:
  7.2 29.1 %all-gather.7.cloned.1.call-start = ((), (), s32[]{:S(2)}) async-start(), calls=%async_computation.2 | async-start | bytes 1572864 | tf_op jit(solution)/shard_map/all_gather | solution.py:410
  9.3 27.0 %collective-permute-start = (bf16[128,2048]{1,0:T(8,128)(2,1)}, bf16[128,2048]{1,0:T(8,128)(2,1)}, u32[]{:S(2)}, u32[]{:S(2)}) collective-permute-start(bf16[128,2048]{1,0:T(8,128)(2,1)} %constant_dynamic-slice_fusion), channel_id=1, source_target_pairs={{0,8},{8,0},{1,9},{9,1},{2,10},{10,2},{3,11},{11,3},{4,12},{12,4},... | collective-permute-start | bytes 1572872 | tf_op jit(solution)/shard_map/ppermute | solution.py:406
  18.0 18.3 %collective-permute-start.1 = (bf16[144,512]{1,0:T(8,128)(2,1)S(1)}, bf16[144,512]{1,0:T(8,128)(2,1)S(1)}, u32[]{:S(2)}, u32[]{:S(2)}) collective-permute-start(bf16[144,512]{1,0:T(8,128)(2,1)S(1)} %fusion.1), channel_id=1, source_target_pairs={{0,1},{1,2},{2,3},{3,4},{4,5},{5,6},{6,7},{7,8},{8,9},{9,10},{10,1... | collective-permute-start | bytes 442376 | tf_op jit(solution)/shard_map/ppermute | solution.py:420
  36.3 122.5 %all-to-all-start = ((bf16[8,48,4096]{2,1,0:T(8,128)(2,1)}), bf16[8,48,4096]{2,1,0:T(8,128)(2,1)S(1)}, u32[]{:S(2)}, u32[]{:S(2)}) async-start(bf16[8,48,4096]{2,1,0:T(8,128)(2,1)} %bitcast.25), calls=%async_computation | async-start | bytes 6291456 | tf_op jit(solution)/shard_map/all_to_all | solution.py:424
  41.2 137.4 %all-gather.9.cloned.1.call-start = ((), (), s32[]{:S(2)}) async-start(), calls=%async_computation.3 | async-start | bytes 3145728 | tf_op jit(solution)/shard_map/all_gather | solution.py:410
  41.2 62.3 %collective-permute-start.6 = (bf16[128,2048]{1,0:T(8,128)(2,1)}, bf16[128,2048]{1,0:T(8,128)(2,1)S(1)}, u32[]{:S(2)}, u32[]{:S(2)}) collective-permute-start(bf16[128,2048]{1,0:T(8,128)(2,1)} %constant_dynamic-slice_fusion), channel_id=1, source_target_pairs={{0,4},{4,0},{1,5},{5,1},{2,6},{6,2},{3,7},{7,3},{8,12},{12,8},{9,1... | collective-permute-start | bytes 1572872 | tf_op jit(solution)/shard_map/ppermute | solution.py:407
  103.5 11.2 %collective-permute-start.7 = (bf16[128,2048]{1,0:T(8,128)(2,1)S(1)}, bf16[128,2048]{1,0:T(8,128)(2,1)S(1)}, u32[]{:S(2)}, u32[]{:S(2)}) collective-permute-start(bf16[128,2048]{1,0:T(8,128)(2,1)S(1)} %collective-permute-done.6), channel_id=1, source_target_pairs={{0,16},{16,0},{1,17},{17,1},{2,18},{18,2},{3,19},{19,3},{4,20},{20... | collective-permute-start | bytes 1572872 | tf_op jit(solution)/shard_map/ppermute | solution.py:411
  115.7 94.2 %all-gather.11.cloned.1.call-start = ((), (), s32[]{:S(2)}) async-start(), calls=%async_computation.4 | async-start | bytes 3145728 | tf_op jit(solution)/shard_map/all_gather | solution.py:410
  115.7 30.9 %collective-permute-start.3 = (bf16[2048,384]{1,0:T(8,128)(2,1)}, bf16[2048,384]{1,0:T(8,128)(2,1)}, u32[]{:S(2)}, u32[]{:S(2)}) collective-permute-start(bf16[2048,384]{1,0:T(8,128)(2,1)} %refs_0_.1), channel_id=1, source_target_pairs={{0,1},{1,0},{2,3},{3,2},{4,5},{5,4},{6,7},{7,6},{8,9},{9,8},{10,11... | collective-permute-start | bytes 4718600 | tf_op jit(solution)/shard_map/ppermute | solution.py:412
  119.0 27.7 %collective-permute-start.4 = (bf16[2048,384]{1,0:T(8,128)(2,1)}, bf16[2048,384]{1,0:T(8,128)(2,1)}, u32[]{:S(2)}, u32[]{:S(2)}) collective-permute-start(bf16[2048,384]{1,0:T(8,128)(2,1)} %refs_1_.1), channel_id=1, source_target_pairs={{0,1},{1,0},{2,3},{3,2},{4,5},{5,4},{6,7},{7,6},{8,9},{9,8},{10,11... | collective-permute-start | bytes 4718600 | tf_op jit(solution)/shard_map/ppermute | solution.py:412
  119.1 27.6 %collective-permute-start.5 = (bf16[384,2048]{1,0:T(8,128)(2,1)}, bf16[384,2048]{1,0:T(8,128)(2,1)}, u32[]{:S(2)}, u32[]{:S(2)}) collective-permute-start(bf16[384,2048]{1,0:T(8,128)(2,1)} %refs_2_.1), channel_id=1, source_target_pairs={{0,1},{1,0},{2,3},{3,2},{4,5},{5,4},{6,7},{7,6},{8,9},{9,8},{10,11... | collective-permute-start | bytes 4718600 | tf_op jit(solution)/shard_map/ppermute | solution.py:412
  119.5 13.8 %collective-permute-start.8 = (bf16[128,2048]{1,0:T(8,128)(2,1)}, bf16[128,2048]{1,0:T(8,128)(2,1)S(1)}, u32[]{:S(2)}, u32[]{:S(2)}) collective-permute-start(bf16[128,2048]{1,0:T(8,128)(2,1)} %collective-permute-done), channel_id=1, source_target_pairs={{0,16},{16,0},{1,17},{17,1},{2,18},{18,2},{3,19},{19,3},{4,20},{20... | collective-permute-start | bytes 1572872 | tf_op jit(solution)/shard_map/ppermute | solution.py:411
  133.3 25.5 %collective-permute-start.9 = (bf16[2,128,2048]{2,1,0:T(8,128)(2,1)}, bf16[2,128,2048]{2,1,0:T(8,128)(2,1)}, u32[]{:S(2)}, u32[]{:S(2)}) collective-permute-start(bf16[2,128,2048]{2,1,0:T(8,128)(2,1)} %bitcast.33), channel_id=1, source_target_pairs={{0,16},{16,0},{1,17},{17,1},{2,18},{18,2},{3,19},{19,3},{4,20},{20... | collective-permute-start | bytes 3145736 | tf_op jit(solution)/shard_map/ppermute | solution.py:411
  134.5 23.8 %collective-permute-start.2 = (bf16[128,2048]{1,0:T(8,128)(2,1)}, bf16[128,2048]{1,0:T(8,128)(2,1)}, u32[]{:S(2)}, u32[]{:S(2)}) collective-permute-start(bf16[128,2048]{1,0:T(8,128)(2,1)} %collective-permute-done), channel_id=1, source_target_pairs={{0,4},{4,0},{1,5},{5,1},{2,6},{6,2},{3,7},{7,3},{8,12},{12,8},{9,1... | collective-permute-start | bytes 1572872 | tf_op jit(solution)/shard_map/ppermute | solution.py:430
  158.3 20.3 %collective-permute-start.10 = (bf16[128,2048]{1,0:T(8,128)(2,1)}, bf16[128,2048]{1,0:T(8,128)(2,1)}, u32[]{:S(2)}, u32[]{:S(2)}) collective-permute-start(bf16[128,2048]{1,0:T(8,128)(2,1)} %collective-permute-done.2), channel_id=1, source_target_pairs={{0,2},{2,0},{1,3},{3,1},{4,6},{6,4},{5,7},{7,5},{8,10},{10,8},{9,1... | collective-permute-start | bytes 1572872 | tf_op jit(solution)/shard_map/ppermute | solution.py:437
  180.4 29.5 %collective-permute-start.14 = (bf16[2,128,2048]{2,1,0:T(8,128)(2,1)S(1)}, bf16[2,128,2048]{2,1,0:T(8,128)(2,1)}, u32[]{:S(2)}, u32[]{:S(2)}) collective-permute-start(bf16[2,128,2048]{2,1,0:T(8,128)(2,1)S(1)} %maximum_select_fusion.refs_4_), channel_id=1, source_target_pairs={{0,16},{16,0},{1,17},{17,1},{2,18},{18,2},{3,19},{19,3},{4,20},{20... | collective-permute-start | bytes 3145736 | tf_op jit(solution)/shard_map/ppermute | solution.py:411
  180.4 40.6 %all-to-all-start.1 = ((bf16[8,48,2048]{2,1,0:T(8,128)(2,1)}), bf16[8,48,2048]{2,1,0:T(8,128)(2,1)S(1)}, u32[]{:S(2)}, u32[]{:S(2)}) async-start(bf16[8,48,2048]{2,1,0:T(8,128)(2,1)} %bitcast.14), calls=%async_computation.1 | async-start | bytes 3145728 | tf_op jit(solution)/shard_map/all_to_all | solution.py:447
  187.6 23.2 %collective-permute-start.11 = (bf16[2,128,2048]{2,1,0:T(8,128)(2,1)}, bf16[2,128,2048]{2,1,0:T(8,128)(2,1)}, u32[]{:S(2)}, u32[]{:S(2)}) collective-permute-start(bf16[2,128,2048]{2,1,0:T(8,128)(2,1)} %bitcast.34), channel_id=1, source_target_pairs={{0,1},{1,0},{2,3},{3,2},{4,5},{5,4},{6,7},{7,6},{8,9},{9,8},{10,11... | collective-permute-start | bytes 3145736 | tf_op jit(solution)/shard_map/ppermute | solution.py:412
  192.8 26.2 %collective-permute-start.16 = (bf16[2,2,128,2048]{3,2,1,0:T(8,128)(2,1)}, bf16[2,2,128,2048]{3,2,1,0:T(8,128)(2,1)}, u32[]{:S(2)}, u32[]{:S(2)}) collective-permute-start(bf16[2,2,128,2048]{3,2,1,0:T(8,128)(2,1)} %bitcast.29), channel_id=1, source_target_pairs={{0,1},{1,0},{2,3},{3,2},{4,5},{5,4},{6,7},{7,6},{8,9},{9,8},{10,11... | collective-permute-start | bytes 6291464 | tf_op jit(solution)/shard_map/ppermute | solution.py:412
  209.9 11.2 %collective-permute-start.17 = (bf16[2,2,128,2048]{3,2,1,0:T(8,128)(2,1)}, bf16[2,2,128,2048]{3,2,1,0:T(8,128)(2,1)}, u32[]{:S(2)}, u32[]{:S(2)}) collective-permute-start(bf16[2,2,128,2048]{3,2,1,0:T(8,128)(2,1)} %bitcast.31), channel_id=1, source_target_pairs={{0,1},{1,0},{2,3},{3,2},{4,5},{5,4},{6,7},{7,6},{8,9},{9,8},{10,11... | collective-permute-start | bytes 6291464 | tf_op jit(solution)/shard_map/ppermute | solution.py:412
  210.3 7.1 %collective-permute-start.13 = (bf16[2,128,2048]{2,1,0:T(8,128)(2,1)S(1)}, bf16[2,128,2048]{2,1,0:T(8,128)(2,1)}, u32[]{:S(2)}, u32[]{:S(2)}) collective-permute-start(bf16[2,128,2048]{2,1,0:T(8,128)(2,1)S(1)} %maximum_select_fusion.refs_4_), channel_id=1, source_target_pairs={{0,1},{1,0},{2,3},{3,2},{4,5},{5,4},{6,7},{7,6},{8,9},{9,8},{10,11... | collective-permute-start | bytes 3145736 | tf_op jit(solution)/shard_map/ppermute | solution.py:412
  210.4 7.1 %collective-permute-start.12 = (bf16[2,128,2048]{2,1,0:T(8,128)(2,1)}, bf16[2,128,2048]{2,1,0:T(8,128)(2,1)}, u32[]{:S(2)}, u32[]{:S(2)}) collective-permute-start(bf16[2,128,2048]{2,1,0:T(8,128)(2,1)} %collective-permute-done.9.refs_2_), channel_id=1, source_target_pairs={{0,1},{1,0},{2,3},{3,2},{4,5},{5,4},{6,7},{7,6},{8,9},{9,8},{10,11... | collective-permute-start | bytes 3145736 | tf_op jit(solution)/shard_map/ppermute | solution.py:412
  210.8 8.1 %collective-permute-start.15 = (bf16[2,128,2048]{2,1,0:T(8,128)(2,1)}, bf16[2,128,2048]{2,1,0:T(8,128)(2,1)}, u32[]{:S(2)}, u32[]{:S(2)}) collective-permute-start(bf16[2,128,2048]{2,1,0:T(8,128)(2,1)} %collective-permute-done.14.refs_6_), channel_id=1, source_target_pairs={{0,1},{1,0},{2,3},{3,2},{4,5},{5,4},{6,7},{7,6},{8,9},{9,8},{10,11... | collective-permute-start | bytes 3145736 | tf_op jit(solution)/shard_map/ppermute | solution.py:412
  238.8 7.6 %collective-permute-start.18 = (bf16[2,128,256]{2,1,0:T(8,128)(2,1)}, bf16[2,128,256]{2,1,0:T(8,128)(2,1)S(1)}, u32[]{:S(2)}, u32[]{:S(2)}) collective-permute-start(bf16[2,128,256]{2,1,0:T(8,128)(2,1)} %get-tuple-element.119), channel_id=1, source_target_pairs={{1,0},{2,1},{3,2},{4,3},{5,4},{6,5},{7,6},{8,7},{9,8},{10,9},{11,1... | collective-permute-start | bytes 393224 | tf_op jit(solution)/shard_map/ppermute | solution.py:456
  (23 other events, 144.6 us)
Sparse Core Ops, SparseCore 0:
  10.2 23.0 all-gather.6
  115.8 35.1 all-gather.8
  152.5 57.2 all-gather.10

commit v25 on v23

--- a/solution.py
+++ b/solution.py
@@ -431,8 +431,9 @@
     prepared = prepare_weights(own, other)
     attention = attention_shares(queries, key_heads, value_heads, prev, segs)
     w_last, prepared, attention = lax.optimization_barrier((w_last, prepared, attention))
-    rows_in, prepared, attention, own_line, own_crossed = lax.optimization_barrier(
-        (rows_in, prepared, attention, own_line, own_crossed)
+    own_swapped = other_core(own_line)
+    rows_in, prepared, attention, own_line, own_swapped, own_crossed = lax.optimization_barrier(
+        (rows_in, prepared, attention, own_line, own_swapped, own_crossed)
     )
     moved = lax.ppermute(w_last, "low", swap) if low == 2 else line(w_last)
     terms = experts(rows_in.reshape(owners * depth, 2 * width), *prepared)
@@ -451,7 +452,7 @@
     moe_input_grad, query_grad, kept, sent = tail(
         jnp.stack([lax.axis_index("groups"), z, lax.axis_index("core")]).astype(jnp.int32),
         back.reshape(owners * depth, width), place, moe_grad,
-        both(own_line, own_crossed, last_line, last_crossed, near_twin, far_twin), *attention,
+        [own_line, own_swapped, *both(own_crossed, last_line, last_crossed, near_twin, far_twin)], *attention,
     )
     return (moe_input_grad, query_grad, *finish(kept, lax.ppermute(sent, blk, backward)))
 

time: 204 us -> 204 us (level)
  no operation moved by 1% of the time
where the time goes in v25:
time: 204 us; the launch traced here: 202 us
  waiting for transfers between devices  87.5 us (43%)
  Pallas kernels  43.6 us (21%)
  starting transfers between devices  31.2 us (15%)
  local copies, waits for them, and re-layouts  19.3 us (9%)
  between operations  13.9 us (7%)
  other arithmetic  6.59 us (3%)
    all_gather x3, waiting for transfers between devices, local(): line = lambda w: lax.all_gather(w, 'low', axis=0, tiled=False)  26.4 us
    ppermute x4, waiting for transfers between devices, local(): cross = lambda w: lax.ppermute(w, 'groups', swap)  22.2 us
    unnamed x48, local copies, waits for them, and re-layouts  18.3 us
    pallas_call x1, Pallas kernels, tail(): pl.pallas_call(functools.partial(tail_kernel, (heads, tiles)), grid_spec=...  16.6 us
    ppermute x1, waiting for transfers between devices, local(): prev = lax.ppermute(jnp.concatenate([kv, seg_rows], axis=0), blk, onward)  15.4 us
    pallas_call x1, Pallas kernels, experts(): pl.pallas_call(functools.partial(expert_kernel, steps), grid=(steps + wid...  12.9 us
    pallas_call x1, Pallas kernels, prepare_weights(): pl.pallas_call(weights_kernel, grid=(steps,), in_specs=[cols, cols, down]...  8.76 us
    ppermute x9, waiting for transfers between devices, local(): other_core = lambda w: lax.ppermute(w, 'core', swap)  7.53 us
  transfers between devices with their start and end apart: 24, of which 9 were waited for; matrix products, arithmetic and copies ran while one was open for 3% of the time, Pallas kernels for 13%

profile of v25, /device:TPU:13, one launch (start us, length us, event | category | flops | bytes accessed | tf_op | source)
XLA Modules:
  0.0 202.1 jit_solution(2871075231837833981)
XLA Ops:
  9.5 2.3 %collective-permute-start.1 = (bf16[128,2048]{1,0:T(8,128)(2,1)}, bf16[128,2048]{1,0:T(8,128)(2,1)}, u32[]{:S(2)}, u32[]{:S(2)}) collective-permute-start(bf16[128,2048]{1,0:T(8,128)(2,1)} %constant_dynamic-slice_fusion), channel_id=1, source_target_pairs={{0,8},{8,0},{1,9},{9,1},{2,10},{10,2},{3,11},{11,3},{4,12},{12,4},... | collective-permute-start | bytes 1572872 | tf_op jit(solution)/shard_map/ppermute | solution.py:406
  16.4 1.6 copy-done.2
  18.1 3.2 %collective-permute-start.2 = (bf16[144,512]{1,0:T(8,128)(2,1)S(1)}, bf16[144,512]{1,0:T(8,128)(2,1)S(1)}, u32[]{:S(2)}, u32[]{:S(2)}) collective-permute-start(bf16[144,512]{1,0:T(8,128)(2,1)S(1)} %fusion.1), channel_id=1, source_target_pairs={{0,1},{1,2},{2,3},{3,4},{4,5},{5,6},{6,7},{7,8},{8,9},{9,10},{10,1... | collective-permute-start | bytes 442376 | tf_op jit(solution)/shard_map/ppermute | solution.py:420
  21.3 15.4 %collective-permute-done.2.prev_key_ref.prev_value_ref.prev_seg_ref = bf16[144,512]{1,0:T(8,128)(2,1)S(1)} collective-permute-done((bf16[144,512]{1,0:T(8,128)(2,1)S(1)}, bf16[144,512]{1,0:T(8,128)(2,1)S(1)}, u32[]{:S(2)}, u32[]{:S(2)}) %collective-permute-start.2) | collective-permute-done | bytes 147488 | tf_op jit(solution)/shard_map/ppermute | solution.py:420
  37.5 3.6 %all-to-all-start = ((bf16[8,48,4096]{2,1,0:T(8,128)(2,1)}), bf16[8,48,4096]{2,1,0:T(8,128)(2,1)S(1)}, u32[]{:S(2)}, u32[]{:S(2)}) async-start(bf16[8,48,4096]{2,1,0:T(8,128)(2,1)} %bitcast.25), calls=%async_computation | async-start | bytes 6291456 | tf_op jit(solution)/shard_map/all_to_all | solution.py:424
  42.4 9.7 %collective-permute-done.7 = bf16[128,2048]{1,0:T(8,128)(2,1)S(1)} collective-permute-done((bf16[128,2048]{1,0:T(8,128)(2,1)}, bf16[128,2048]{1,0:T(8,128)(2,1)S(1)}, u32[]{:S(2)}, u32[]{:S(2)}) %collective-permute-start.7) | collective-permute-done | bytes 524320 | tf_op jit(solution)/shard_map/ppermute | solution.py:411
  52.1 2.1 %pad_maximum_fusion = bf16[2,128,2048]{2,1,0:T(8,128)(2,1)} fusion(bf16[1,128,2048]{2,1,0:T(8,128)(2,1)S(1)} %bitcast.38, bf16[1,128,2048]{2,1,0:T(8,128)(2,1)} %bitcast.36), kind=kLoop, calls=%fused_computation | loop fusion | flops 524288 | bytes 2097152 | tf_op jit(solution)/shard_map/stack | solution.py:426
  54.3 3.7 %collective-permute-start.4 = (bf16[2048,384]{1,0:T(8,128)(2,1)}, bf16[2048,384]{1,0:T(8,128)(2,1)}, u32[]{:S(2)}, u32[]{:S(2)}) collective-permute-start(bf16[2048,384]{1,0:T(8,128)(2,1)} %refs_0_.1), channel_id=1, source_target_pairs={{0,1},{1,0},{2,3},{3,2},{4,5},{5,4},{6,7},{7,6},{8,9},{9,8},{10,11... | collective-permute-start | bytes 4718600 | tf_op jit(solution)/shard_map/ppermute | solution.py:412
  59.8 12.6 %collective-permute-done.8 = bf16[128,2048]{1,0:T(8,128)(2,1)S(1)} collective-permute-done((bf16[128,2048]{1,0:T(8,128)(2,1)}, bf16[128,2048]{1,0:T(8,128)(2,1)S(1)}, u32[]{:S(2)}, u32[]{:S(2)}) %collective-permute-start.8) | collective-permute-done | bytes 524320 | tf_op jit(solution)/shard_map/ppermute | solution.py:411
  74.5 2.2 %pad_maximum_fusion.1 = bf16[2,128,2048]{2,1,0:T(8,128)(2,1)} fusion(bf16[1,128,2048]{2,1,0:T(8,128)(2,1)S(1)} %bitcast.37, bf16[1,128,2048]{2,1,0:T(8,128)(2,1)} %bitcast.18), kind=kLoop, calls=%fused_computation.2 | loop fusion | flops 524288 | bytes 2097152 | tf_op jit(solution)/shard_map/stack | solution.py:427
  78.2 3.5 %attention_shares.1 = (bf16[2,2048,256]{2,1,0:T(8,128)(2,1)S(1)}, bf16[2,256,2048]{2,1,0:T(8,128)(2,1)S(1)}, bf16[2,2048,128]{2,1,0:T(8,128)(2,1)S(1)}, bf16[2,2...) custom-call(bf16[128,4096]{1,0:T(8,128)(2,1)S(1)} %copy-done.8, bf16[128,256]{1,0:T(8,128)(2,1)S(1)} %copy-done.11, ...), custom_call_target="tpu_custom_call" | custom-call | tf_op jit(solution)/shard_map/attention_shares/pallas_call | solution.py:201
  88.1 1.4 copy-done.7
  89.5 8.8 %prepare_weights.1 = (bf16[3,2048,512]{2,1,0:T(8,128)(2,1)}, bf16[3,2048,256]{2,1,0:T(8,128)(2,1)}, bf16[3,512,2048]{2,1,0:T(8,128)(2,1)}) custom-call(bf16[2048,384]{1,0:T(8,128)(2,1)S(1)} %copy-done.5, bf16[2048,384]{1,0:T(8,128)(2,1)S(1)} %copy-done.6, bf16[384,2048]{1,0:T(8,128)(2,1)S(1)} %copy-done.7, bf16[2048,384]{1,0:T(8,128)(2,1)} %collective-permute-done.4.refs_3_, ...), custom_call_target="tpu_custom_call" | custom-call | tf_op jit(solution)/shard_map/prepare_weights/pallas_call | solution.py:94
  98.3 3.9 %collective-permute-done.3 = bf16[128,2048]{1,0:T(8,128)(2,1)} collective-permute-done((bf16[128,2048]{1,0:T(8,128)(2,1)}, bf16[128,2048]{1,0:T(8,128)(2,1)}, u32[]{:S(2)}, u32[]{:S(2)}) %collective-permute-start.3) | collective-permute-done | bytes 524320 | tf_op jit(solution)/shard_map/ppermute | solution.py:430
  102.7 6.8 %all-to-all-done = bf16[8,48,4096]{2,1,0:T(8,128)(2,1)S(1)} async-done(((bf16[8,48,4096]{2,1,0:T(8,128)(2,1)}), bf16[8,48,4096]{2,1,0:T(8,128)(2,1)S(1)}, u32[]{:S(2)}, u32[]{:S(2)}) %all-to-all-start) | async-done | bytes 3145760 | tf_op jit(solution)/shard_map/all_to_all | solution.py:424
  109.4 12.9 %expert_terms.1 = bf16[384,2048]{1,0:T(8,128)(2,1)} custom-call(bf16[384,4096]{1,0:T(8,128)(2,1)S(1)} %bitcast.24, bf16[3,2048,512]{2,1,0:T(8,128)(2,1)} %get-tuple-element.99.cols_ref, bf16[3,2048,256]{2,1,0:T(8,128)(2,1)} %get-tuple-element.100.down_ref, bf16[3,512,2048]{2,1,0:T(8,128)(2,1)} %get-tuple-element.101.back_ref), custom_call_target="tpu_custom_call" | custom-call | tf_op jit(solution)/shard_map/expert_terms/pallas_call | solution.py:145
  122.3 1.7 maximum_select_fusion.refs_4_
  125.3 6.3 %all-to-all-start.1 = ((bf16[8,48,2048]{2,1,0:T(8,128)(2,1)}), bf16[8,48,2048]{2,1,0:T(8,128)(2,1)S(1)}, u32[]{:S(2)}, u32[]{:S(2)}) async-start(bf16[8,48,2048]{2,1,0:T(8,128)(2,1)} %bitcast.14), calls=%async_computation.1 | async-start | bytes 3145728 | tf_op jit(solution)/shard_map/all_to_all | solution.py:448
  132.9 26.4 %all-gather.11.cloned.1.call-done = bf16[4,128,2048]{2,1,0:T(8,128)(2,1)} async-done(((bf16[2,128,2048]{2,1,0:T(8,128)(2,1)}), bf16[4,128,2048]{2,1,0:T(8,128)(2,1)}) %all-gather.11.cloned.1.call-update) | async-done | bytes 2097168 | tf_op jit(solution)/shard_map/all_gather | solution.py:410
  161.2 6.0 %collective-permute-done.12.refs_3_ = bf16[2,128,2048]{2,1,0:T(8,128)(2,1)} collective-permute-done((bf16[2,128,2048]{2,1,0:T(8,128)(2,1)}, bf16[2,128,2048]{2,1,0:T(8,128)(2,1)}, u32[]{:S(2)}, u32[]{:S(2)}) %collective-permute-start.12) | collective-permute-done | bytes 1048608 | tf_op jit(solution)/shard_map/ppermute | solution.py:412
  167.2 1.5 collective-permute-done.15.refs_7_
  169.9 16.6 %tail_attention.1 = (bf16[128,2048]{1,0:T(8,128)(2,1)}, bf16[128,4096]{1,0:T(8,128)(2,1)}, f32[2,128,256]{2,1,0:T(8,128)}, bf16[2,128,256]{2,1,0:T(8,128)(2,1)}) custom-call(s32[3]{0:T(128)} %pad_add_fusion.place_info, bf16[384,2048]{1,0:T(8,128)(2,1)} %bitcast.28, bf16[128,384]{1,0:T(8,128)(2,1)} %copy-done.16, bf16[128,2048]{1,0:T(8,128)(2,1)} %grad_ref.3, ...), custom_call_target="tpu_custom_call" | custom-call | flops 2147483648 | bytes 23068672 | tf_op jit(solution)/shard_map/tail_attention/pallas_call | solution.py:320
  186.5 2.3 %collective-permute-start.18 = (bf16[2,128,256]{2,1,0:T(8,128)(2,1)}, bf16[2,128,256]{2,1,0:T(8,128)(2,1)S(1)}, u32[]{:S(2)}, u32[]{:S(2)}) collective-permute-start(bf16[2,128,256]{2,1,0:T(8,128)(2,1)} %get-tuple-element.123), channel_id=1, source_target_pairs={{1,0},{2,1},{3,2},{4,3},{5,4},{6,5},{7,6},{8,7},{9,8},{10,9},{11,1... | collective-permute-start | bytes 393224 | tf_op jit(solution)/shard_map/ppermute | solution.py:457
  188.8 5.1 %collective-permute-done.18.later_ref = bf16[2,128,256]{2,1,0:T(8,128)(2,1)S(1)} collective-permute-done((bf16[2,128,256]{2,1,0:T(8,128)(2,1)}, bf16[2,128,256]{2,1,0:T(8,128)(2,1)S(1)}, u32[]{:S(2)}, u32[]{:S(2)}) %collective-permute-start.18) | collective-permute-done | bytes 131104 | tf_op jit(solution)/shard_map/ppermute | solution.py:457
  (89 shorter events, 28.5 us)
Async XLA Ops:
  7.2 30.3 %all-gather.7.cloned.1.call-start = ((), (), s32[]{:S(2)}) async-start(), calls=%async_computation.2 | async-start | bytes 1572864 | tf_op jit(solution)/shard_map/all_gather | solution.py:410
  9.3 27.4 %collective-permute-start = (bf16[128,2048]{1,0:T(8,128)(2,1)}, bf16[128,2048]{1,0:T(8,128)(2,1)S(1)}, u32[]{:S(2)}, u32[]{:S(2)}) collective-permute-start(bf16[128,2048]{1,0:T(8,128)(2,1)} %constant_dynamic-slice_fusion), channel_id=1, source_target_pairs={{0,4},{4,0},{1,5},{5,1},{2,6},{6,2},{3,7},{7,3},{8,12},{12,8},{9,1... | collective-permute-start | bytes 1572872 | tf_op jit(solution)/shard_map/ppermute | solution.py:407
  9.5 28.0 %collective-permute-start.1 = (bf16[128,2048]{1,0:T(8,128)(2,1)}, bf16[128,2048]{1,0:T(8,128)(2,1)}, u32[]{:S(2)}, u32[]{:S(2)}) collective-permute-start(bf16[128,2048]{1,0:T(8,128)(2,1)} %constant_dynamic-slice_fusion), channel_id=1, source_target_pairs={{0,8},{8,0},{1,9},{9,1},{2,10},{10,2},{3,11},{11,3},{4,12},{12,4},... | collective-permute-start | bytes 1572872 | tf_op jit(solution)/shard_map/ppermute | solution.py:406
  18.1 18.6 %collective-permute-start.2 = (bf16[144,512]{1,0:T(8,128)(2,1)S(1)}, bf16[144,512]{1,0:T(8,128)(2,1)S(1)}, u32[]{:S(2)}, u32[]{:S(2)}) collective-permute-start(bf16[144,512]{1,0:T(8,128)(2,1)S(1)} %fusion.1), channel_id=1, source_target_pairs={{0,1},{1,2},{2,3},{3,4},{4,5},{5,6},{6,7},{7,8},{8,9},{9,10},{10,1... | collective-permute-start | bytes 442376 | tf_op jit(solution)/shard_map/ppermute | solution.py:420
  37.5 71.9 %all-to-all-start = ((bf16[8,48,4096]{2,1,0:T(8,128)(2,1)}), bf16[8,48,4096]{2,1,0:T(8,128)(2,1)S(1)}, u32[]{:S(2)}, u32[]{:S(2)}) async-start(bf16[8,48,4096]{2,1,0:T(8,128)(2,1)} %bitcast.25), calls=%async_computation | async-start | bytes 6291456 | tf_op jit(solution)/shard_map/all_to_all | solution.py:424
  41.1 81.1 %all-gather.9.cloned.1.call-start = ((), (), s32[]{:S(2)}) async-start(), calls=%async_computation.3 | async-start | bytes 3145728 | tf_op jit(solution)/shard_map/all_gather | solution.py:410
  41.2 10.9 %collective-permute-start.7 = (bf16[128,2048]{1,0:T(8,128)(2,1)}, bf16[128,2048]{1,0:T(8,128)(2,1)S(1)}, u32[]{:S(2)}, u32[]{:S(2)}) collective-permute-start(bf16[128,2048]{1,0:T(8,128)(2,1)} %copy-done.22), channel_id=1, source_target_pairs={{0,16},{16,0},{1,17},{17,1},{2,18},{18,2},{3,19},{19,3},{4,20},{20... | collective-permute-start | bytes 1572872 | tf_op jit(solution)/shard_map/ppermute | solution.py:411
  54.2 105.1 %all-gather.11.cloned.1.call-start = ((), (), s32[]{:S(2)}) async-start(), calls=%async_computation.4 | async-start | bytes 3145728 | tf_op jit(solution)/shard_map/all_gather | solution.py:410
  54.3 20.0 %collective-permute-start.4 = (bf16[2048,384]{1,0:T(8,128)(2,1)}, bf16[2048,384]{1,0:T(8,128)(2,1)}, u32[]{:S(2)}, u32[]{:S(2)}) collective-permute-start(bf16[2048,384]{1,0:T(8,128)(2,1)} %refs_0_.1), channel_id=1, source_target_pairs={{0,1},{1,0},{2,3},{3,2},{4,5},{5,4},{6,7},{7,6},{8,9},{9,8},{10,11... | collective-permute-start | bytes 4718600 | tf_op jit(solution)/shard_map/ppermute | solution.py:412
  58.0 28.7 %collective-permute-start.5 = (bf16[2048,384]{1,0:T(8,128)(2,1)}, bf16[2048,384]{1,0:T(8,128)(2,1)}, u32[]{:S(2)}, u32[]{:S(2)}) collective-permute-start(bf16[2048,384]{1,0:T(8,128)(2,1)} %refs_1_.1), channel_id=1, source_target_pairs={{0,1},{1,0},{2,3},{3,2},{4,5},{5,4},{6,7},{7,6},{8,9},{9,8},{10,11... | collective-permute-start | bytes 4718600 | tf_op jit(solution)/shard_map/ppermute | solution.py:412
  58.1 28.6 %collective-permute-start.6 = (bf16[384,2048]{1,0:T(8,128)(2,1)}, bf16[384,2048]{1,0:T(8,128)(2,1)}, u32[]{:S(2)}, u32[]{:S(2)}) collective-permute-start(bf16[384,2048]{1,0:T(8,128)(2,1)} %refs_2_.1), channel_id=1, source_target_pairs={{0,1},{1,0},{2,3},{3,2},{4,5},{5,4},{6,7},{7,6},{8,9},{9,8},{10,11... | collective-permute-start | bytes 4718600 | tf_op jit(solution)/shard_map/ppermute | solution.py:412
  58.5 13.8 %collective-permute-start.8 = (bf16[128,2048]{1,0:T(8,128)(2,1)}, bf16[128,2048]{1,0:T(8,128)(2,1)S(1)}, u32[]{:S(2)}, u32[]{:S(2)}) collective-permute-start(bf16[128,2048]{1,0:T(8,128)(2,1)} %collective-permute-done.1), channel_id=1, source_target_pairs={{0,16},{16,0},{1,17},{17,1},{2,18},{18,2},{3,19},{19,3},{4,20},{20... | collective-permute-start | bytes 1572872 | tf_op jit(solution)/shard_map/ppermute | solution.py:411
  72.4 30.3 %collective-permute-start.9 = (bf16[2,128,2048]{2,1,0:T(8,128)(2,1)}, bf16[2,128,2048]{2,1,0:T(8,128)(2,1)}, u32[]{:S(2)}, u32[]{:S(2)}) collective-permute-start(bf16[2,128,2048]{2,1,0:T(8,128)(2,1)} %bitcast.33), channel_id=1, source_target_pairs={{0,1},{1,0},{2,3},{3,2},{4,5},{5,4},{6,7},{7,6},{8,9},{9,8},{10,11... | collective-permute-start | bytes 3145736 | tf_op jit(solution)/shard_map/ppermute | solution.py:412
  73.1 29.6 %collective-permute-start.10 = (bf16[2,128,2048]{2,1,0:T(8,128)(2,1)}, bf16[2,128,2048]{2,1,0:T(8,128)(2,1)}, u32[]{:S(2)}, u32[]{:S(2)}) collective-permute-start(bf16[2,128,2048]{2,1,0:T(8,128)(2,1)} %bitcast.34), channel_id=1, source_target_pairs={{0,16},{16,0},{1,17},{17,1},{2,18},{18,2},{3,19},{19,3},{4,20},{20... | collective-permute-start | bytes 3145736 | tf_op jit(solution)/shard_map/ppermute | solution.py:411
  74.3 27.9 %collective-permute-start.3 = (bf16[128,2048]{1,0:T(8,128)(2,1)}, bf16[128,2048]{1,0:T(8,128)(2,1)}, u32[]{:S(2)}, u32[]{:S(2)}) collective-permute-start(bf16[128,2048]{1,0:T(8,128)(2,1)} %collective-permute-done.1), channel_id=1, source_target_pairs={{0,4},{4,0},{1,5},{5,1},{2,6},{6,2},{3,7},{7,3},{8,12},{12,8},{9,1... | collective-permute-start | bytes 1572872 | tf_op jit(solution)/shard_map/ppermute | solution.py:430
  102.2 20.1 %collective-permute-start.11 = (bf16[128,2048]{1,0:T(8,128)(2,1)}, bf16[128,2048]{1,0:T(8,128)(2,1)}, u32[]{:S(2)}, u32[]{:S(2)}) collective-permute-start(bf16[128,2048]{1,0:T(8,128)(2,1)} %collective-permute-done.3), channel_id=1, source_target_pairs={{0,2},{2,0},{1,3},{3,1},{4,6},{6,4},{5,7},{7,5},{8,10},{10,8},{9,1... | collective-permute-start | bytes 1572872 | tf_op jit(solution)/shard_map/ppermute | solution.py:438
  124.0 35.4 %collective-permute-start.14 = (bf16[2,128,2048]{2,1,0:T(8,128)(2,1)S(1)}, bf16[2,128,2048]{2,1,0:T(8,128)(2,1)}, u32[]{:S(2)}, u32[]{:S(2)}) collective-permute-start(bf16[2,128,2048]{2,1,0:T(8,128)(2,1)S(1)} %maximum_select_fusion.refs_4_), channel_id=1, source_target_pairs={{0,16},{16,0},{1,17},{17,1},{2,18},{18,2},{3,19},{19,3},{4,20},{20... | collective-permute-start | bytes 3145736 | tf_op jit(solution)/shard_map/ppermute | solution.py:411
  125.3 43.4 %all-to-all-start.1 = ((bf16[8,48,2048]{2,1,0:T(8,128)(2,1)}), bf16[8,48,2048]{2,1,0:T(8,128)(2,1)S(1)}, u32[]{:S(2)}, u32[]{:S(2)}) async-start(bf16[8,48,2048]{2,1,0:T(8,128)(2,1)} %bitcast.14), calls=%async_computation.1 | async-start | bytes 3145728 | tf_op jit(solution)/shard_map/all_to_all | solution.py:448
  131.6 37.0 %collective-permute-start.16 = (bf16[2,2,128,2048]{3,2,1,0:T(8,128)(2,1)}, bf16[2,2,128,2048]{3,2,1,0:T(8,128)(2,1)}, u32[]{:S(2)}, u32[]{:S(2)}) collective-permute-start(bf16[2,2,128,2048]{3,2,1,0:T(8,128)(2,1)} %bitcast.29), channel_id=1, source_target_pairs={{0,1},{1,0},{2,3},{3,2},{4,5},{5,4},{6,7},{7,6},{8,9},{9,8},{10,11... | collective-permute-start | bytes 6291464 | tf_op jit(solution)/shard_map/ppermute | solution.py:412
  159.4 9.3 %collective-permute-start.17 = (bf16[2,2,128,2048]{3,2,1,0:T(8,128)(2,1)}, bf16[2,2,128,2048]{3,2,1,0:T(8,128)(2,1)}, u32[]{:S(2)}, u32[]{:S(2)}) collective-permute-start(bf16[2,2,128,2048]{3,2,1,0:T(8,128)(2,1)} %bitcast.31), channel_id=1, source_target_pairs={{0,1},{1,0},{2,3},{3,2},{4,5},{5,4},{6,7},{7,6},{8,9},{9,8},{10,11... | collective-permute-start | bytes 6291464 | tf_op jit(solution)/shard_map/ppermute | solution.py:412
  160.0 7.1 %collective-permute-start.13 = (bf16[2,128,2048]{2,1,0:T(8,128)(2,1)S(1)}, bf16[2,128,2048]{2,1,0:T(8,128)(2,1)}, u32[]{:S(2)}, u32[]{:S(2)}) collective-permute-start(bf16[2,128,2048]{2,1,0:T(8,128)(2,1)S(1)} %maximum_select_fusion.refs_4_), channel_id=1, source_target_pairs={{0,1},{1,0},{2,3},{3,2},{4,5},{5,4},{6,7},{7,6},{8,9},{9,8},{10,11... | collective-permute-start | bytes 3145736 | tf_op jit(solution)/shard_map/ppermute | solution.py:412
  160.0 7.1 %collective-permute-start.12 = (bf16[2,128,2048]{2,1,0:T(8,128)(2,1)}, bf16[2,128,2048]{2,1,0:T(8,128)(2,1)}, u32[]{:S(2)}, u32[]{:S(2)}) collective-permute-start(bf16[2,128,2048]{2,1,0:T(8,128)(2,1)} %collective-permute-done.10.refs_2_), channel_id=1, source_target_pairs={{0,1},{1,0},{2,3},{3,2},{4,5},{5,4},{6,7},{7,6},{8,9},{9,8},{10,11... | collective-permute-start | bytes 3145736 | tf_op jit(solution)/shard_map/ppermute | solution.py:412
  160.6 8.1 %collective-permute-start.15 = (bf16[2,128,2048]{2,1,0:T(8,128)(2,1)}, bf16[2,128,2048]{2,1,0:T(8,128)(2,1)}, u32[]{:S(2)}, u32[]{:S(2)}) collective-permute-start(bf16[2,128,2048]{2,1,0:T(8,128)(2,1)} %collective-permute-done.14.refs_6_), channel_id=1, source_target_pairs={{0,1},{1,0},{2,3},{3,2},{4,5},{5,4},{6,7},{7,6},{8,9},{9,8},{10,11... | collective-permute-start | bytes 3145736 | tf_op jit(solution)/shard_map/ppermute | solution.py:412
  186.5 7.4 %collective-permute-start.18 = (bf16[2,128,256]{2,1,0:T(8,128)(2,1)}, bf16[2,128,256]{2,1,0:T(8,128)(2,1)S(1)}, u32[]{:S(2)}, u32[]{:S(2)}) collective-permute-start(bf16[2,128,256]{2,1,0:T(8,128)(2,1)} %get-tuple-element.123), channel_id=1, source_target_pairs={{1,0},{2,1},{3,2},{4,3},{5,4},{6,5},{7,6},{8,7},{9,8},{10,9},{11,1... | collective-permute-start | bytes 393224 | tf_op jit(solution)/shard_map/ppermute | solution.py:457
  (24 other events, 150.0 us)
Sparse Core Ops, SparseCore 0:
  10.2 23.0 all-gather.6
  54.4 53.2 all-gather.8
  109.2 50.1 all-gather.10
